TPU v7x, 32 devices: a whole 2x2x4 slice. The times are simulated.
32 devices in a mesh: groups: 2 (over x), row: 8 (over z, y), col: 2 (over core).
Axes of the slice: x: 2, y: 2, z: 4, core: 2. Of those that a mesh axis runs over, the one named last changes fastest.
Arguments:
- snapshot: bfloat16 [2048, 32, 2048], P(('groups', 'row'), None, 'col'), parts along dimension 0, may hold values from -6 to 6
- mode2_factor: bfloat16 [4096, 64], P(('groups', 'col')), parts along dimension 0, may hold values from -0.125 to 0.125
- old_factor: bfloat16 [2048, 64], P(('groups', 'row')), parts along dimension 0, may hold values from -0.1875 to 0.1875
Outputs:
- new_factor: float32 [2048, 64], P(('groups', 'row', 'col')), parts along dimension 0
There are 2 independent parts, one for each index of `groups`. A program takes and returns all parts, laid end to end along the dimension named above; each array names one. Nothing has to cross between parts.
All inputs are finite; a program needn't handle non-finite values.
Results may differ from a plain program's by a relative error of at most 0.01.
Values may be sent and summed in bfloat16 or wider, within the bound.
No kernel may reach another device: no remote copies, remote signals or barrier semaphores. Data moves between devices by JAX's collectives and lax.ppermute only.
A program may use at most 64 MiB of HBM per device.

v0:
```python
import jax
import jax.numpy as jnp
from jax import lax
from jax.sharding import PartitionSpec as P


def finish(product_half, gram, total_rows):
    lower = jnp.linalg.cholesky(gram)
    solved = jax.scipy.linalg.solve_triangular(lower, product_half.T, lower=True)
    return solved.T * jnp.sqrt(jnp.float32(total_rows))


def per_device(snapshot, mode2_factor, old_factor):
    cells_one, fibers, cells_two = snapshot.shape
    rank = mode2_factor.shape[1]
    pairs = fibers // 2
    n_cols = lax.axis_size("col")
    total_rows = cells_one * lax.axis_size("row")
    half = cells_one // n_cols
    col_index = lax.axis_index("col")
    highest = lax.Precision.HIGHEST
    pair_count = pairs * cells_one // n_cols * lax.axis_size("col") // cells_one
    result = jnp.dot(
        snapshot.reshape(cells_one * 2 * pair_count, cells_two),
        mode2_factor,
        preferred_element_type=jnp.float32,
    )
    result = result.reshape(cells_one, pair_count, 2 * rank).transpose(1, 0, 2)
    core = lax.psum_scatter(
        result.reshape(pair_count * cells_one, 2 * rank).astype(jnp.bfloat16),
        "col",
        scatter_dimension=0,
        tiled=True,
    ).astype(jnp.float32)
    own_pairs = pairs // n_cols
    core_blocks = core.reshape(own_pairs, cells_one, 2 * rank)
    partial_proj = jnp.einsum(
        "ir,qic->rqc",
        old_factor.astype(jnp.float32),
        core_blocks,
        precision=highest,
        preferred_element_type=jnp.float32,
    )
    projected = lax.psum(partial_proj, "row").astype(jnp.bfloat16)
    partial_prod = jnp.einsum(
        "qic,rqc->ir",
        core_blocks,
        projected.astype(jnp.float32),
        precision=highest,
        preferred_element_type=jnp.float32,
    )
    product = lax.psum(partial_prod.astype(jnp.bfloat16), "col").astype(jnp.float32)
    local_gram = jnp.dot(product.T, product, precision=highest, preferred_element_type=jnp.float32)
    gram = lax.psum(local_gram, "row")
    product_half = lax.dynamic_slice_in_dim(product, col_index * half, half, 0)
    return finish(product_half, gram, total_rows)


def solution(mesh):
    return jax.shard_map(
        per_device,
        mesh=mesh,
        in_specs=(
            P(("groups", "row"), None, "col"),
            P(("groups", "col"), None),
            P(("groups", "row"), None),
        ),
        out_specs=P(("groups", "row", "col"), None),
        check_vma=False,
    )
```

profile of v0, /device:TPU:0, one launch (start us, length us, event | category | flops | bytes accessed | tf_op | source)
XLA Modules:
  0.0 125.6 jit_solution(7054464200559919380)
XLA Ops:
  6.5 0.0 copy-start
  6.5 0.0 reduce-scatter.2.cloned.1.call-start
  6.5 0.9 copy-done
  7.4 0.0 copy-start.1
  7.4 6.0 %convolution_convert_fusion = bf16[4096,64]{0,1:T(8,128)(2,1)S(1)} fusion(bf16[4096,1024]{1,0:T(8,128)(2,1)} %bitcast.29, bf16[1024,64]{0,1:T(8,128)(2,1)S(1)} %copy-done), kind=kOutput, calls=%fused_computation | convolution fusion | flops 537133056 | bytes 9043968 | tf_op jit(solution)/shard_map/dot_general | solution.py:23
  13.5 0.5 copy.9
  14.0 0.5 convert_element_type.23
  14.5 0.9 copy.10
  15.4 0.0 reduce-scatter.2.cloned.1.call-update
  15.4 10.8 %reduce-scatter.2.cloned.1.call-done = bf16[1024,128]{1,0:T(8,128)(2,1)} async-done(((bf16[2048,128]{1,0:T(8,128)(2,1)}), bf16[1024,128]{1,0:T(8,128)(2,1)}) %reduce-scatter.2.cloned.1.call-update) | async-done | bytes 262160 | tf_op jit(solution)/shard_map/reduce_scatter | solution.py:29
  26.2 0.0 copy-done.1
  26.2 1.1 convolution_bitcast_fusion
  27.3 40.7 %all-reduce.1 = bf16[64,8,128]{2,0,1:T(8,128)(2,1)S(1)} all-reduce(f32[64,8,128]{2,0,1:T(8,128)S(1)} %convolution_bitcast_fusion), channel_id=1, replica_groups=mesh['groups'=2,'row'=8,'col'=2] {'row'}, use_global_device_ids=true, to_apply=%region_1.0 | all-reduce | flops 65536 | bytes 393216 | tf_op jit(solution)/shard_map/psum | solution.py:44
  68.0 1.2 fusion
  69.2 3.4 %psum.22 = bf16[128,64]{0,1:T(8,128)(2,1)S(1)} all-reduce(bf16[128,64]{0,1:T(8,128)(2,1)S(1)} %fusion), channel_id=1, replica_groups=mesh['groups'=2,'row'=8,'col'=2] {'col'}, use_global_device_ids=true, to_apply=%region_2.0 | all-reduce | flops 8192 | bytes 32768 | tf_op jit(solution)/shard_map/psum | solution.py:52
  72.5 0.1 fusion.8
  72.7 33.0 %psum.23 = f32[64,64]{0,1:T(8,128)S(1)} all-reduce(f32[64,64]{0,1:T(8,128)S(1)} %fusion.8), channel_id=1, replica_groups=mesh['groups'=2,'row'=8,'col'=2] {'row'}, use_global_device_ids=true, to_apply=%region_3.0 | all-reduce | flops 4096 | bytes 32768 | tf_op jit(solution)/shard_map/psum | solution.py:54
  105.7 0.1 copy.12
  105.8 5.8 %cholesky.16 = f32[64,64]{1,0:T(8,128)S(1)} custom-call(f32[64,64]{1,0:T(8,128)S(1)} %fusion.4), custom_call_target="Cholesky" | custom-call | tf_op jit(solution)/shard_map/jit(cholesky)/cholesky | solution.py:8
  111.7 0.6 compare_reduce_fusion
  112.3 0.7 fusion.2
  113.0 4.9 %custom-call.7 = f32[1,64,64]{1,2,0:T(8,128)S(1)} custom-call(f32[1,64,64]{2,1,0:T(8,128)S(1)} %fusion.2), custom_call_target="InvertDiagBlocksLowerTriangular" | custom-call | tf_op jit(solution)/shard_map/jit(_solve_triangular)/triangular_solve | solution.py:9
  117.9 0.9 convolution_multiply_fusion
  (2 shorter events, 0.0 us)
Async XLA Ops:
  6.5 0.9 copy-start
  6.5 19.7 %reduce-scatter.2.cloned.1.call-start = ((), (), s32[]{:S(2)}) async-start(), calls=%async_computation.1 | async-start | bytes 786432 | tf_op jit(solution)/shard_map/reduce_scatter | solution.py:29
  7.4 18.8 %copy-start.1 = (bf16[128,64]{0,1:T(8,128)(2,1)S(1)}, bf16[128,64]{0,1:T(8,128)(2,1)}, u32[]{:S(2)}) copy-start(bf16[128,64]{0,1:T(8,128)(2,1)} %param.5) | copy-start | bytes 49156
Sparse Core Ops, SparseCore 0:
  15.5 10.6 reduce-scatter.1
where the time goes:
time: 126 us
  blocking collectives  77 us (61%)
  between operations  13.5 us (11%)
  other arithmetic  12.1 us (10%)
  waiting for transfers between devices  10.8 us (9%)
  matrix products  9.36 us (7%)
  local copies, waits for them, and re-layouts  2.88 us (2%)
    psum x1, blocking collectives, per_device(): projected = lax.psum(partial_proj, 'row').astype(jnp.bfloat16)  40.7 us
    psum x1, blocking collectives, per_device(): gram = lax.psum(local_gram, 'row')  33 us
    reduce_scatter x1, waiting for transfers between devices, per_device(): lax.psum_scatter(result.reshape(pair_count * cells_one, 2 * rank).astype(...  10.8 us
    another operation x3, other arithmetic, finish(): lower = jnp.linalg.cholesky(gram)  6.52 us
    dot_general x1, matrix products, per_device(): jnp.dot(snapshot.reshape(cells_one * 2 * pair_count, cells_two), mode2_fa...  6.05 us
    another operation x2, other arithmetic, finish(): jax.scipy.linalg.solve_triangular(lower, product_half.T, lower=True)  5.55 us
    psum x1, blocking collectives, per_device(): lax.psum(partial_prod.astype(jnp.bfloat16), 'col').astype(jnp.float32)  3.36 us
  transfers between devices with their start and end apart: 1, of which 1 were waited for; matrix products, arithmetic and copies ran while one was open for 0% of the time, Pallas kernels for 0%

commit v1 on v0

v1 whole, which is shorter than its diff:
```python
import functools

import jax
import jax.numpy as jnp
from jax import lax
from jax.experimental import pallas as pl
from jax.experimental.pallas import tpu as pltpu
from jax.sharding import PartitionSpec as P

F32 = jnp.float32
BF16 = jnp.bfloat16
LANES = 128


def dot_f32(a, b, dims, precision=None):
    return lax.dot_general(a, b, (dims, ((), ())), precision=precision, preferred_element_type=F32)


def contract_kernel(fibers, rank, snapshot_ref, mode2_ref, send_ref, own_ref, wide_ref, core_ref):
    cells, _, depth = snapshot_ref.shape
    reps = LANES // rank

    @pl.when(pl.program_id(0) == 0)
    def _():
        wide_ref[...] = jnp.concatenate([mode2_ref[...]] * reps, axis=1)

    core_ref[...] = dot_f32(
        snapshot_ref[...].reshape(cells * fibers, depth), wide_ref[...], ((1,), (0,))
    )
    lane = lax.broadcasted_iota(jnp.int32, (cells, LANES), 1)
    first = lax.axis_index("col") == 0
    half = fibers // 2

    def columns(start):
        part = core_ref[pl.ds(start, cells, stride=fibers), :]
        for r in range(1, reps):
            other = core_ref[pl.ds(start + r, cells, stride=fibers), :]
            part = jnp.where(lane < r * rank, part, other)
        return part

    for block in range(half // reps):
        low = columns(block * reps)
        high = columns(half + block * reps)
        where = slice(block * LANES, (block + 1) * LANES)
        own_ref[:, where] = jnp.where(first, low, high).astype(BF16)
        send_ref[:, where] = jnp.where(first, high, low).astype(BF16)


def contract(snapshot, mode2):
    cells, fibers, depth = snapshot.shape
    rank = mode2.shape[1]
    step = 16
    width = fibers // 2 * rank
    out = jax.ShapeDtypeStruct((cells, width), BF16)
    return pl.pallas_call(
        functools.partial(contract_kernel, fibers, rank),
        grid=(cells // step,),
        in_specs=[
            pl.BlockSpec((step, fibers, depth), lambda i: (i, 0, 0)),
            pl.BlockSpec((depth, rank), lambda i: (0, 0)),
        ],
        out_specs=[pl.BlockSpec((step, width), lambda i: (i, 0))] * 2,
        out_shape=[out, out],
        scratch_shapes=[
            pltpu.VMEM((depth, LANES), BF16),
            pltpu.VMEM((step * fibers, LANES), F32),
        ],
        compiler_params=pltpu.CompilerParams(vmem_limit_bytes=32 * 2**20),
        name="contract",
    )(snapshot, mode2)


def project_kernel(own_ref, got_ref, factor_ref, out_ref):
    rank = factor_ref.shape[1]
    factor = factor_ref[...]
    total = dot_f32(factor, own_ref[...], ((0,), (0,))) + dot_f32(factor, got_ref[...], ((0,), (0,)))
    for block in range(total.shape[1] // LANES):
        out_ref[pl.ds(block * rank, rank), :] = total[:, block * LANES:(block + 1) * LANES].astype(BF16)


def project(own, got, factor):
    rank = factor.shape[1]
    rows = rank * own.shape[1] // LANES
    return pl.pallas_call(
        project_kernel,
        out_shape=jax.ShapeDtypeStruct((rows, LANES), BF16),
        name="project",
    )(own, got, factor)


def reduce_kernel(parts_ref, out_ref):
    total = jnp.sum(parts_ref[...].astype(F32), axis=0).astype(BF16)
    out_ref[...] = jnp.broadcast_to(total[None], out_ref.shape)


def reduce_parts(parts):
    return pl.pallas_call(
        reduce_kernel,
        out_shape=jax.ShapeDtypeStruct(parts.shape, BF16),
        name="reduce_parts",
    )(parts)


def product_kernel(own_ref, got_ref, projected_ref, out_ref):
    cells, width = own_ref.shape
    rank = projected_ref.shape[0] // (width // LANES)
    total = jnp.zeros((cells, rank), F32)
    for block in range(width // LANES):
        where = slice(block * LANES, (block + 1) * LANES)
        projected = projected_ref[pl.ds(block * rank, rank), :]
        total += dot_f32(own_ref[:, where], projected, ((1,), (1,)))
        total += dot_f32(got_ref[:, where], projected, ((1,), (1,)))
    half = cells // 2
    both = jnp.concatenate([total[:half], total[half:]], axis=1).astype(BF16)
    out_ref[...] = jnp.broadcast_to(both[None], out_ref.shape)


def product_terms(own, got, projected, copies):
    cells = own.shape[0]
    return pl.pallas_call(
        product_kernel,
        out_shape=jax.ShapeDtypeStruct((copies, cells // 2, LANES), BF16),
        name="product_terms",
    )(own, got, projected)


def finish_kernel(n_rows, n_cols, parts_ref, out_ref, prod_ref):
    half = parts_ref.shape[1]
    rank = LANES // 2
    highest = lax.Precision.HIGHEST
    for row in range(n_rows):
        total = parts_ref[row * n_cols].astype(F32)
        for col in range(1, n_cols):
            total += parts_ref[row * n_cols + col].astype(F32)
        prod_ref[pl.ds(row * half, half), :] = total
    prod = prod_ref[...]
    wide = dot_f32(prod, prod, ((0,), (0,)), highest)
    gram = wide[:rank, :rank] + wide[rank:, rank:]
    eye = (
        lax.broadcasted_iota(jnp.int32, (rank, rank), 0)
        == lax.broadcasted_iota(jnp.int32, (rank, rank), 1)
    ).astype(F32)
    both = jnp.concatenate([gram, eye], axis=1)
    row_index = lax.broadcasted_iota(jnp.int32, (rank, 1), 0)
    pivots = jnp.zeros((rank, 1), F32)
    for k in range(rank):
        pivot = both[k:k + 1, k:k + 1]
        pivots = jnp.where(row_index == k, pivot, pivots)
        factor = jnp.where(row_index > k, both[:, k:k + 1] / pivot, 0.0)
        both = both - factor * both[k:k + 1, :]
    total_rows = n_rows * half * 2
    inverse = both[:, rank:] * (lax.rsqrt(pivots) * (total_rows ** 0.5))
    row = lax.axis_index("row")
    mine = prod_ref[pl.ds(pl.multiple_of(row * half, half), half), :]
    mine = jnp.where(lax.axis_index("col") == 0, mine[:, :rank], mine[:, rank:])
    out_ref[...] = dot_f32(mine, inverse, ((1,), (1,)), highest)


def finish(parts, n_rows, n_cols):
    half = parts.shape[1]
    return pl.pallas_call(
        functools.partial(finish_kernel, n_rows, n_cols),
        out_shape=jax.ShapeDtypeStruct((half, LANES // 2), F32),
        scratch_shapes=[pltpu.VMEM((n_rows * half, LANES), F32)],
        name="finish",
    )(parts)


def per_device(snapshot, mode2_factor, old_factor):
    n_rows, n_cols = lax.axis_size("row"), lax.axis_size("col")
    send, own = contract(snapshot, mode2_factor)
    got = lax.ppermute(send, "col", [(c, (c + 1) % n_cols) for c in range(n_cols)])
    partial = project(own, got, old_factor)
    parts = lax.all_to_all(partial.reshape(n_rows, -1, LANES), "row", 0, 0, tiled=True)
    chunks = lax.all_to_all(reduce_parts(parts), "row", 0, 0, tiled=True)
    terms = product_terms(own, got, chunks.reshape(-1, LANES), n_rows * n_cols)
    gathered = lax.all_to_all(terms, ("row", "col"), 0, 0, tiled=True)
    return finish(gathered, n_rows, n_cols)


def solution(mesh):
    return jax.shard_map(
        per_device,
        mesh=mesh,
        in_specs=(
            P(("groups", "row"), None, "col"),
            P(("groups", "col"), None),
            P(("groups", "row"), None),
        ),
        out_specs=P(("groups", "row", "col"), None),
        check_vma=False,
    )
```

time: 126 us -> 66.3 us (0.53)
  blocking collectives: 77 us -> 40.2 us
  Pallas kernels: 0 us -> 18.1 us
  between operations: 13.5 us -> 0.04 us
  other arithmetic: 12.1 us -> 0 us
  waiting for transfers between devices: 10.8 us -> 0.44 us
  matrix products: 9.36 us -> 0 us
  local copies, waits for them, and re-layouts: 2.88 us -> 6.57 us
    psum x3 -> x0, blocking collectives: 77 us -> none  [the longest x1 40.7 us: per_device(): projected = lax.psum(partial_proj, 'row').astype(jnp.bfloat16)]
    all_to_all x0 -> x3, blocking collectives: none -> 40.2 us  [the longest x1 14.6 us: per_device(): lax.all_to_all(partial.reshape(n_rows, -1, LANES), 'row', 0, 0, tiled=True)]
    pallas_call x0 -> x5, Pallas kernels: none -> 18.1 us  [the longest x1 8.05 us: finish(): pl.pallas_call(functools.partial(finish_kernel, n_rows, n_cols), out_shap...]
    another operation x5 -> x0, other arithmetic: 12.1 us -> none  [the longest x3 6.52 us: finish(): lower = jnp.linalg.cholesky(gram)]
    reduce_scatter x1 -> x0, waiting for transfers between devices: 10.8 us -> none  [per_device(): lax.psum_scatter(result.reshape(pair_count * cells_one, 2 * rank).astype(...]
    dot_general x4 -> x0, matrix products: 8.45 us -> none  [the longest x1 6.05 us: per_device(): jnp.dot(snapshot.reshape(cells_one * 2 * pair_count, cells_two), mode2_fa...]
    unnamed x4 -> x10, local copies, waits for them, and re-layouts: 0.91 us -> 6.57 us
    convert_element_type x3 -> x0, local copies, waits for them, and re-layouts: 1.89 us -> none  [per_device(): result.reshape(pair_count * cells_one, 2 * rank).astype(jnp.bfloat16)]
  transfers between devices with their start and end apart: 1 -> 1, of which waited for: 1 -> 1; matrix products, arithmetic and copies ran while one was open for 0% -> 1% of each run, Pallas kernels for 0% -> 0%
where the time goes in v1:
time: 66.3 us; the launch traced here: 65.8 us
  blocking collectives  40.2 us (61%)
  Pallas kernels  18.1 us (27%)
  local copies, waits for them, and re-layouts  6.57 us (10%)
    all_to_all x1, blocking collectives, per_device(): lax.all_to_all(partial.reshape(n_rows, -1, LANES), 'row', 0, 0, tiled=True)  14.6 us
    all_to_all x1, blocking collectives, per_device(): gathered = lax.all_to_all(terms, ('row', 'col'), 0, 0, tiled=True)  14.2 us
    all_to_all x1, blocking collectives, per_device(): chunks = lax.all_to_all(reduce_parts(parts), 'row', 0, 0, tiled=True)  11.3 us
    pallas_call x1, Pallas kernels, finish(): pl.pallas_call(functools.partial(finish_kernel, n_rows, n_cols), out_shap...  8.05 us
    unnamed x10, local copies, waits for them, and re-layouts  6.57 us
    pallas_call x1, Pallas kernels, contract(): pl.pallas_call(functools.partial(contract_kernel, fibers, rank), grid=(ce...  4.4 us
    pallas_call x1, Pallas kernels, product_terms(): pl.pallas_call(product_kernel, out_shape=jax.ShapeDtypeStruct((copies, ce...  2.13 us
    pallas_call x1, Pallas kernels, project(): pl.pallas_call(project_kernel, out_shape=jax.ShapeDtypeStruct((rows, LANE...  1.93 us
  transfers between devices with their start and end apart: 1, of which 1 were waited for; matrix products, arithmetic and copies ran while one was open for 1% of the time, Pallas kernels for 0%

profile of v1, /device:TPU:0, one launch (start us, length us, event | category | flops | bytes accessed | tf_op | source)
XLA Modules:
  0.0 65.8 jit_solution(15118703853996148535)
XLA Ops:
  0.0 0.0 copy-start.3
  0.0 1.1 %copy.4.mode2_ref = bf16[1024,64]{1,0:T(8,128)(2,1)S(1)} copy(bf16[1024,64]{0,1:T(8,128)(2,1)} %param.4) | data formatting | bytes 262144 | tf_op args[1]
  1.1 0.0 copy-start
  1.1 3.4 %copy-done = bf16[128,32,1024]{2,1,0:T(8,128)(2,1)S(1)} copy-done((bf16[128,32,1024]{2,1,0:T(8,128)(2,1)S(1)}, bf16[128,32,1024]{2,1,0:T(8,128)(2,1)}, u32[]{:S(2)}) %copy-start) | copy-done | bytes 8388632
  4.5 4.4 %contract.1 = (bf16[128,1024]{1,0:T(8,128)(2,1)S(1)}, bf16[128,1024]{1,0:T(8,128)(2,1)S(1)}) custom-call(bf16[128,32,1024]{2,1,0:T(8,128)(2,1)S(1)} %copy-done, bf16[1024,64]{1,0:T(8,128)(2,1)S(1)} %copy.4.mode2_ref), custom_call_target="tpu_custom_call" | custom-call | tf_op jit(solution)/shard_map/contract/pallas_call | solution.py:55
  8.9 0.0 copy-start.1
  8.9 0.7 %copy-done.1 = bf16[128,1024]{1,0:T(8,128)(2,1)} copy-done((bf16[128,1024]{1,0:T(8,128)(2,1)}, bf16[128,1024]{1,0:T(8,128)(2,1)S(1)}, u32[]{:S(2)}) %copy-start.1) | copy-done | bytes 262168
  9.6 0.5 collective-permute-start
  10.0 0.0 copy-done.3
  10.0 0.7 %copy.5.factor_ref = bf16[128,64]{1,0:T(8,128)(2,1)} copy(bf16[128,64]{0,1:T(8,128)(2,1)S(1)} %copy-done.3) | data formatting | bytes 32768 | tf_op args[2]
  10.8 0.4 collective-permute-done.got_ref
  11.2 0.0 copy-start.2
  11.2 0.7 %copy-done.2 = bf16[128,1024]{1,0:T(8,128)(2,1)} copy-done((bf16[128,1024]{1,0:T(8,128)(2,1)}, bf16[128,1024]{1,0:T(8,128)(2,1)S(1)}, u32[]{:S(2)}) %copy-start.2) | copy-done | bytes 262168
  11.9 1.9 %project.1 = bf16[512,128]{1,0:T(8,128)(2,1)} custom-call(bf16[128,1024]{1,0:T(8,128)(2,1)} %copy-done.1, bf16[128,1024]{1,0:T(8,128)(2,1)} %copy-done.2, bf16[128,64]{1,0:T(8,128)(2,1)} %copy.5.factor_ref), custom_call_target="tpu_custom_call" | custom-call | tf_op jit(solution)/shard_map/project/pallas_call | solution.py:84
  13.8 14.6 %all_to_all.15.parts_ref = bf16[8,64,128]{2,1,0:T(8,128)(2,1)} all-to-all(bf16[8,64,128]{2,1,0:T(8,128)(2,1)} %bitcast.3), channel_id=1, replica_groups=mesh['groups'=2,'row'=8,'col'=2] {'row'}, dimensions={0} | all-to-all | bytes 262144 | tf_op jit(solution)/shard_map/all_to_all | solution.py:174
  28.5 1.6 %reduce_parts.1 = bf16[8,64,128]{2,1,0:T(8,128)(2,1)} custom-call(bf16[8,64,128]{2,1,0:T(8,128)(2,1)} %all_to_all.15.parts_ref), custom_call_target="tpu_custom_call" | custom-call | tf_op jit(solution)/shard_map/reduce_parts/pallas_call | solution.py:97
  30.0 11.3 %all_to_all.16 = bf16[8,64,128]{2,1,0:T(8,128)(2,1)} all-to-all(bf16[8,64,128]{2,1,0:T(8,128)(2,1)} %reduce_parts.1), channel_id=1, replica_groups=mesh['groups'=2,'row'=8,'col'=2] {'row'}, dimensions={0} | all-to-all | bytes 262144 | tf_op jit(solution)/shard_map/all_to_all | solution.py:175
  41.4 2.1 %product_terms.1 = bf16[16,64,128]{2,1,0:T(8,128)(2,1)} custom-call(bf16[128,1024]{1,0:T(8,128)(2,1)} %copy-done.1, bf16[128,1024]{1,0:T(8,128)(2,1)} %copy-done.2, bf16[512,128]{1,0:T(8,128)(2,1)} %bitcast.2), custom_call_target="tpu_custom_call" | custom-call | tf_op jit(solution)/shard_map/product_terms/pallas_call | solution.py:120
  43.5 14.2 %all_to_all.17.parts_ref = bf16[16,64,128]{2,1,0:T(8,128)(2,1)} all-to-all(bf16[16,64,128]{2,1,0:T(8,128)(2,1)} %product_terms.1), channel_id=1, replica_groups=mesh['groups'=2,'row'=8,'col'=2] {'row','col'}, dimensions={0} | all-to-all | bytes 524288 | tf_op jit(solution)/shard_map/all_to_all | solution.py:177
  57.7 8.0 %finish.1 = f32[64,64]{1,0:T(8,128)} custom-call(bf16[16,64,128]{2,1,0:T(8,128)(2,1)} %all_to_all.17.parts_ref), custom_call_target="tpu_custom_call" | custom-call | tf_op jit(solution)/shard_map/finish/pallas_call | solution.py:161
Async XLA Ops:
  0.0 10.0 %copy-start.3 = (bf16[128,64]{0,1:T(8,128)(2,1)S(1)}, bf16[128,64]{0,1:T(8,128)(2,1)}, u32[]{:S(2)}) copy-start(bf16[128,64]{0,1:T(8,128)(2,1)} %param.5) | copy-start | bytes 49156
  1.1 3.4 %copy-start = (bf16[128,32,1024]{2,1,0:T(8,128)(2,1)S(1)}, bf16[128,32,1024]{2,1,0:T(8,128)(2,1)}, u32[]{:S(2)}) copy-start(bf16[128,32,1024]{2,1,0:T(8,128)(2,1)} %snapshot_ref.1) | copy-start | bytes 25165828
  8.9 0.7 %copy-start.1 = (bf16[128,1024]{1,0:T(8,128)(2,1)}, bf16[128,1024]{1,0:T(8,128)(2,1)S(1)}, u32[]{:S(2)}) copy-start(bf16[128,1024]{1,0:T(8,128)(2,1)S(1)} %get-tuple-element.7.own_ref) | copy-start | bytes 786436
  9.6 1.6 %collective-permute-start = (bf16[128,1024]{1,0:T(8,128)(2,1)S(1)}, bf16[128,1024]{1,0:T(8,128)(2,1)S(1)}, u32[]{:S(2)}, u32[]{:S(2)}) collective-permute-start(bf16[128,1024]{1,0:T(8,128)(2,1)S(1)} %get-tuple-element.8), channel_id=1, source_target_pairs={{0,1},{1,0},{2,3},{3,2},{4,5},{5,4},{6,7},{7,6},{8,9},{9,8},{10,11... | collective-permute-start | bytes 786440 | tf_op jit(solution)/shard_map/ppermute | solution.py:172
  11.2 0.7 %copy-start.2 = (bf16[128,1024]{1,0:T(8,128)(2,1)}, bf16[128,1024]{1,0:T(8,128)(2,1)S(1)}, u32[]{:S(2)}) copy-start(bf16[128,1024]{1,0:T(8,128)(2,1)S(1)} %collective-permute-done.got_ref) | copy-start | bytes 786436

commit v2 on v1

v2 whole, which is shorter than its diff:
```python
import functools

import jax
import jax.numpy as jnp
from jax import lax
from jax.experimental import pallas as pl
from jax.experimental.pallas import tpu as pltpu
from jax.sharding import PartitionSpec as P

F32 = jnp.float32
BF16 = jnp.bfloat16
LANES = 128
MIB = 2**20


def dot_f32(a, b, dims, precision=None):
    return lax.dot_general(a, b, (dims, ((), ())), precision=precision, preferred_element_type=F32)


def params(mib):
    return pltpu.CompilerParams(vmem_limit_bytes=mib * MIB)


def contract_kernel(step, snapshot_ref, mode2_ref, send_ref, own_ref, slab_ref, core_ref, sems):
    cells, fibers, depth = snapshot_ref.shape
    rank = mode2_ref.shape[0]
    reps = LANES // rank
    half = fibers // 2
    chunks = cells // step

    def copy(chunk):
        where = pl.ds(chunk * step, step)
        return pltpu.make_async_copy(snapshot_ref.at[where], slab_ref.at[where], sems.at[chunk])

    for chunk in range(chunks):
        copy(chunk).start()
    wide = jnp.concatenate([mode2_ref[...]] * reps, axis=0).T
    lane = lax.broadcasted_iota(jnp.int32, (step, LANES), 1)
    first = lax.axis_index("col") == 0

    for chunk in range(chunks):
        copy(chunk).wait()
        core = core_ref.at[chunk % 2]
        rows = pl.ds(chunk * step, step)
        core[...] = dot_f32(slab_ref[rows].reshape(step * fibers, depth), wide, ((1,), (0,)))

        def columns(start):
            part = core[pl.ds(start, step, stride=fibers), :]
            for r in range(1, reps):
                other = core[pl.ds(start + r, step, stride=fibers), :]
                part = jnp.where(lane < r * rank, part, other)
            return part

        for block in range(half // reps):
            low = columns(block * reps)
            high = columns(half + block * reps)
            where = slice(block * LANES, (block + 1) * LANES)
            own_ref[rows, where] = jnp.where(first, low, high).astype(BF16)
            send_ref[rows, where] = jnp.where(first, high, low).astype(BF16)


def contract(snapshot, mode2_t):
    cells, fibers, depth = snapshot.shape
    rank = mode2_t.shape[0]
    step = 16
    out = jax.ShapeDtypeStruct((cells, fibers // 2 * rank), BF16)
    return pl.pallas_call(
        functools.partial(contract_kernel, step),
        in_specs=[
            pl.BlockSpec(memory_space=pltpu.HBM),
            pl.BlockSpec(memory_space=pltpu.VMEM),
        ],
        out_shape=[out, out],
        scratch_shapes=[
            pltpu.VMEM(snapshot.shape, BF16),
            pltpu.VMEM((2, step * fibers, LANES), F32),
            pltpu.SemaphoreType.DMA((cells // step,)),
        ],
        compiler_params=params(16),
        name="contract",
    )(snapshot, mode2_t)


def project_kernel(n_rows, own_ref, got_ref, factor_ref, *refs):
    outs, scratch_ref = refs[:-1], refs[-1]
    rank = factor_ref.shape[0]
    factor = factor_ref[...]
    total = dot_f32(factor, own_ref[...], ((1,), (0,))) + dot_f32(factor, got_ref[...], ((1,), (0,)))
    for block in range(total.shape[1] // LANES):
        scratch_ref[pl.ds(block * rank, rank), :] = total[:, block * LANES:(block + 1) * LANES]
    row = lax.axis_index("row")
    size = outs[0].shape[0]
    for m, out in enumerate(outs):
        piece = lax.rem(row + m, n_rows)
        out[...] = scratch_ref[pl.ds(pl.multiple_of(piece * size, size), size), :].astype(BF16)


def project(own, got, factor_t, n_rows):
    rank = factor_t.shape[0]
    rows = rank * own.shape[1] // LANES
    return pl.pallas_call(
        functools.partial(project_kernel, n_rows),
        out_shape=[jax.ShapeDtypeStruct((rows // n_rows, LANES), BF16)] * n_rows,
        scratch_shapes=[pltpu.VMEM((rows, LANES), F32)],
        compiler_params=params(4),
        name="project",
    )(own, got, factor_t)


def reduce_kernel(*refs):
    total = refs[0][...].astype(F32)
    for ref in refs[1:-1]:
        total += ref[...].astype(F32)
    refs[-1][...] = total.astype(BF16)


def reduce_parts(parts):
    return pl.pallas_call(
        reduce_kernel,
        out_shape=jax.ShapeDtypeStruct(parts[0].shape, BF16),
        compiler_params=params(4),
        name="reduce_parts",
    )(*parts)


def product_kernel(n_rows, own_ref, got_ref, *refs):
    pieces, out_ref, scratch_ref = refs[:-2], refs[-2], refs[-1]
    cells, width = own_ref.shape
    rank = scratch_ref.shape[0] // (width // LANES)
    row = lax.axis_index("row")
    size = pieces[0].shape[0]
    for m, ref in enumerate(pieces):
        piece = lax.rem(row - m + n_rows, n_rows)
        scratch_ref[pl.ds(pl.multiple_of(piece * size, size), size), :] = ref[...].astype(F32)
    total = jnp.zeros((cells, rank), F32)
    for block in range(width // LANES):
        where = slice(block * LANES, (block + 1) * LANES)
        projected = scratch_ref[pl.ds(block * rank, rank), :].astype(BF16)
        total += dot_f32(own_ref[:, where], projected, ((1,), (1,)))
        total += dot_f32(got_ref[:, where], projected, ((1,), (1,)))
    half = cells // 2
    out_ref[...] = jnp.concatenate([total[:half], total[half:]], axis=1).astype(BF16)


def product_terms(own, got, pieces):
    cells = own.shape[0]
    rows = len(pieces) * pieces[0].shape[0]
    return pl.pallas_call(
        functools.partial(product_kernel, len(pieces)),
        out_shape=jax.ShapeDtypeStruct((cells // 2, LANES), BF16),
        scratch_shapes=[pltpu.VMEM((rows, LANES), F32)],
        compiler_params=params(4),
        name="product_terms",
    )(own, got, *pieces)


def finish_kernel(n_rows, n_cols, *refs):
    terms, out_ref, prod_ref = refs[:-2], refs[-2], refs[-1]
    half = terms[0].shape[0]
    rank = LANES // 2
    highest = lax.Precision.HIGHEST
    col = lax.axis_index("col")
    for step in range(n_rows):
        total = terms[step * n_cols][...].astype(F32)
        for m in range(1, n_cols):
            total += terms[step * n_cols + m][...].astype(F32)
        prod_ref[pl.ds(step * half, half), :] = total
    prod = prod_ref[...]
    wide = dot_f32(prod, prod, ((0,), (0,)), highest)
    gram = wide[:rank, :rank] + wide[rank:, rank:]
    eye = (
        lax.broadcasted_iota(jnp.int32, (rank, rank), 0)
        == lax.broadcasted_iota(jnp.int32, (rank, rank), 1)
    ).astype(F32)
    both = jnp.concatenate([gram, eye], axis=1)
    row_index = lax.broadcasted_iota(jnp.int32, (rank, 1), 0)
    pivots = jnp.zeros((rank, 1), F32)
    for k in range(rank):
        pivot = both[k:k + 1, k:k + 1]
        pivots = jnp.where(row_index == k, pivot, pivots)
        factor = jnp.where(row_index > k, both[:, k:k + 1] / pivot, 0.0)
        both = both - factor * both[k:k + 1, :]
    total_rows = n_rows * half * 2
    inverse = both[:, rank:] * (lax.rsqrt(pivots) * (total_rows ** 0.5))
    mine = prod_ref[pl.ds(0, half), :]
    mine = jnp.where(col == 0, mine[:, :rank], mine[:, rank:])
    out_ref[...] = dot_f32(mine, inverse, ((1,), (1,)), highest)


def finish(terms, n_rows, n_cols):
    half = terms[0].shape[0]
    return pl.pallas_call(
        functools.partial(finish_kernel, n_rows, n_cols),
        out_shape=jax.ShapeDtypeStruct((half, LANES // 2), F32),
        scratch_shapes=[pltpu.VMEM((n_rows * half, LANES), F32)],
        compiler_params=params(16),
        name="finish",
    )(*terms)


def per_device(snapshot, mode2_factor, old_factor):
    n_rows, n_cols = lax.axis_size("row"), lax.axis_size("col")

    def shift(x, row_by, col_by):
        if row_by == 0 and col_by == 0:
            return x
        pairs = [
            (r * n_cols + c, (r + row_by) % n_rows * n_cols + (c + col_by) % n_cols)
            for r in range(n_rows)
            for c in range(n_cols)
        ]
        return lax.ppermute(x, ("row", "col"), pairs)

    send, own = contract(snapshot, mode2_factor.T)
    got = shift(send, 0, 1)
    pieces = project(own, got, old_factor.T, n_rows)
    mine = reduce_parts([shift(piece, m, 0) for m, piece in enumerate(pieces)])
    projected = [shift(mine, m, 0) for m in range(n_rows)]
    term = product_terms(own, got, projected)
    terms = [shift(term, r, c) for r in range(n_rows) for c in range(n_cols)]
    return finish(terms, n_rows, n_cols)


def solution(mesh):
    return jax.shard_map(
        per_device,
        mesh=mesh,
        in_specs=(
            P(("groups", "row"), None, "col"),
            P(("groups", "col"), None),
            P(("groups", "row"), None),
        ),
        out_specs=P(("groups", "row", "col"), None),
        check_vma=False,
    )
```

time: 66.3 us -> 75 us (1.13)
  starting transfers between devices: 0.45 us -> 43.1 us
  blocking collectives: 40.2 us -> 0 us
  waiting for transfers between devices: 0.44 us -> 12.7 us
  Pallas kernels: 18.1 us -> 14.7 us
  local copies, waits for them, and re-layouts: 6.57 us -> 4.29 us
    ppermute x1 -> x30, starting transfers between devices: 0.45 us -> 43.1 us  [shift(): return lax.ppermute(x, ('row', 'col'), pairs)]
    all_to_all x3 -> x0, blocking collectives: 40.2 us -> none  [the longest x1 14.6 us: per_device(): lax.all_to_all(partial.reshape(n_rows, -1, LANES), 'row', 0, 0, tiled=True)]
    ppermute x1 -> x30, waiting for transfers between devices: 0.44 us -> 12.7 us  [shift(): return lax.ppermute(x, ('row', 'col'), pairs)]
    pallas_call x4, Pallas kernels: 10 us -> 7.54 us  [the longest x1 6.91 us: contract(): pl.pallas_call(functools.partial(contract_kernel, step), in_specs=[pl.Blo...]
    unnamed x10 -> x6, local copies, waits for them, and re-layouts: 6.57 us -> 4.29 us
    pallas_call x1, Pallas kernels: 8.05 us -> 7.11 us  [finish(): pl.pallas_call(functools.partial(finish_kernel, n_rows, n_cols), out_shap...]
  transfers between devices with their start and end apart: 1 -> 30, of which waited for: 1 -> 10; matrix products, arithmetic and copies ran while one was open for 1% -> 0% of each run, Pallas kernels for 0% -> 0%
where the time goes in v2:
time: 75 us; the launch traced here: 74.8 us
  starting transfers between devices  43.1 us (57%)
  Pallas kernels  14.7 us (20%)
  waiting for transfers between devices  12.7 us (17%)
  local copies, waits for them, and re-layouts  4.29 us (6%)
    ppermute x30, starting transfers between devices, shift(): return lax.ppermute(x, ('row', 'col'), pairs)  43.1 us
    ppermute x30, waiting for transfers between devices, shift(): return lax.ppermute(x, ('row', 'col'), pairs)  12.7 us
    pallas_call x1, Pallas kernels, finish(): pl.pallas_call(functools.partial(finish_kernel, n_rows, n_cols), out_shap...  7.11 us
    pallas_call x1, Pallas kernels, contract(): pl.pallas_call(functools.partial(contract_kernel, step), in_specs=[pl.Blo...  6.91 us
    unnamed x6, local copies, waits for them, and re-layouts  4.29 us
  transfers between devices with their start and end apart: 30, of which 10 were waited for; matrix products, arithmetic and copies ran while one was open for 0% of the time, Pallas kernels for 0%

profile of v2, /device:TPU:0, one launch (start us, length us, event | category | flops | bytes accessed | tf_op | source)
XLA Modules:
  0.0 74.8 jit_solution(6910850890065472309)
XLA Ops:
  0.0 3.4 %copy-done = bf16[128,32,1024]{2,1,0:T(8,128)(2,1)S(1)} copy-done((bf16[128,32,1024]{2,1,0:T(8,128)(2,1)S(1)}, bf16[128,32,1024]{2,1,0:T(8,128)(2,1)}, u32[]{:S(2)}) %copy-start) | copy-done | bytes 8388632
  3.4 0.9 %copy-done.1 = bf16[1024,64]{0,1:T(8,128)(2,1)S(1)} copy-done((bf16[1024,64]{0,1:T(8,128)(2,1)S(1)}, bf16[1024,64]{0,1:T(8,128)(2,1)}, u32[]{:S(2)}) %copy-start.1) | copy-done | bytes 131096
  4.3 6.9 %contract.1 = (bf16[128,1024]{1,0:T(8,128)(2,1)S(1)}, bf16[128,1024]{1,0:T(8,128)(2,1)S(1)}) custom-call(bf16[128,32,1024]{2,1,0:T(8,128)(2,1)S(1)} %copy-done, bf16[64,1024]{1,0:T(8,128)(2,1)S(1)} %bitcast.2), custom_call_target="tpu_custom_call" | custom-call | tf_op jit(solution)/shard_map/contract/pallas_call | solution.py:67
  11.2 0.5 collective-permute-start
  11.7 1.2 %collective-permute-done.got_ref = bf16[128,1024]{1,0:T(8,128)(2,1)S(1)} collective-permute-done((bf16[128,1024]{1,0:T(8,128)(2,1)S(1)}, bf16[128,1024]{1,0:T(8,128)(2,1)S(1)}, u32[]{:S(2)}, u32[]{:S(2)}) %collective-permute-start) | collective-permute-done | bytes 262176 | tf_op jit(solution)/shard_map/ppermute | solution.py:212
  12.9 0.2 project.1
  13.1 2.9 %collective-permute-start.1 = (bf16[64,128]{1,0:T(8,128)(2,1)S(1)}, bf16[64,128]{1,0:T(8,128)(2,1)S(1)}, u32[]{:S(2)}, u32[]{:S(2)}) collective-permute-start(bf16[64,128]{1,0:T(8,128)(2,1)S(1)} %get-tuple-element.18), channel_id=1, source_target_pairs={{0,2},{1,3},{2,4},{3,5},{4,6},{5,7},{6,8},{7,9},{8,10},{9,11},{10,... | collective-permute-start | bytes 49160 | tf_op jit(solution)/shard_map/ppermute | solution.py:212
  16.1 1.6 %collective-permute-start.2 = (bf16[64,128]{1,0:T(8,128)(2,1)S(1)}, bf16[64,128]{1,0:T(8,128)(2,1)S(1)}, u32[]{:S(2)}, u32[]{:S(2)}) collective-permute-start(bf16[64,128]{1,0:T(8,128)(2,1)S(1)} %get-tuple-element.19), channel_id=1, source_target_pairs={{0,4},{1,5},{2,6},{3,7},{4,8},{5,9},{6,10},{7,11},{8,12},{9,13},{1... | collective-permute-start | bytes 49160 | tf_op jit(solution)/shard_map/ppermute | solution.py:212
  17.6 2.5 %collective-permute-start.3 = (bf16[64,128]{1,0:T(8,128)(2,1)S(1)}, bf16[64,128]{1,0:T(8,128)(2,1)S(1)}, u32[]{:S(2)}, u32[]{:S(2)}) collective-permute-start(bf16[64,128]{1,0:T(8,128)(2,1)S(1)} %get-tuple-element.20), channel_id=1, source_target_pairs={{0,6},{1,7},{2,8},{3,9},{4,10},{5,11},{6,12},{7,13},{8,14},{9,15},... | collective-permute-start | bytes 49160 | tf_op jit(solution)/shard_map/ppermute | solution.py:212
  20.2 1.2 %collective-permute-start.4 = (bf16[64,128]{1,0:T(8,128)(2,1)S(1)}, bf16[64,128]{1,0:T(8,128)(2,1)S(1)}, u32[]{:S(2)}, u32[]{:S(2)}) collective-permute-start(bf16[64,128]{1,0:T(8,128)(2,1)S(1)} %get-tuple-element.21), channel_id=1, source_target_pairs={{0,8},{1,9},{2,10},{3,11},{4,12},{5,13},{6,14},{7,15},{8,0},{9,1},... | collective-permute-start | bytes 49160 | tf_op jit(solution)/shard_map/ppermute | solution.py:212
  21.4 2.7 %collective-permute-start.5 = (bf16[64,128]{1,0:T(8,128)(2,1)S(1)}, bf16[64,128]{1,0:T(8,128)(2,1)S(1)}, u32[]{:S(2)}, u32[]{:S(2)}) collective-permute-start(bf16[64,128]{1,0:T(8,128)(2,1)S(1)} %get-tuple-element.22), channel_id=1, source_target_pairs={{0,10},{1,11},{2,12},{3,13},{4,14},{5,15},{6,0},{7,1},{8,2},{9,3},... | collective-permute-start | bytes 49160 | tf_op jit(solution)/shard_map/ppermute | solution.py:212
  24.1 0.0 collective-permute-done.1.refs_1_
  24.1 1.3 %collective-permute-start.6 = (bf16[64,128]{1,0:T(8,128)(2,1)S(1)}, bf16[64,128]{1,0:T(8,128)(2,1)S(1)}, u32[]{:S(2)}, u32[]{:S(2)}) collective-permute-start(bf16[64,128]{1,0:T(8,128)(2,1)S(1)} %get-tuple-element.23), channel_id=1, source_target_pairs={{0,12},{1,13},{2,14},{3,15},{4,0},{5,1},{6,2},{7,3},{8,4},{9,5},{1... | collective-permute-start | bytes 49160 | tf_op jit(solution)/shard_map/ppermute | solution.py:212
  25.4 0.0 collective-permute-done.2.refs_2_
  25.4 1.4 %collective-permute-start.7 = (bf16[64,128]{1,0:T(8,128)(2,1)S(1)}, bf16[64,128]{1,0:T(8,128)(2,1)S(1)}, u32[]{:S(2)}, u32[]{:S(2)}) collective-permute-start(bf16[64,128]{1,0:T(8,128)(2,1)S(1)} %get-tuple-element.24), channel_id=1, source_target_pairs={{0,14},{1,15},{2,0},{3,1},{4,2},{5,3},{6,4},{7,5},{8,6},{9,7},{10,... | collective-permute-start | bytes 49160 | tf_op jit(solution)/shard_map/ppermute | solution.py:212
  26.8 0.0 collective-permute-done.3.refs_3_
  26.8 0.0 collective-permute-done.4.refs_4_
  26.8 0.0 collective-permute-done.5.refs_5_
  26.8 1.0 %collective-permute-done.6.refs_6_ = bf16[64,128]{1,0:T(8,128)(2,1)S(1)} collective-permute-done((bf16[64,128]{1,0:T(8,128)(2,1)S(1)}, bf16[64,128]{1,0:T(8,128)(2,1)S(1)}, u32[]{:S(2)}, u32[]{:S(2)}) %collective-permute-start.6) | collective-permute-done | bytes 16416 | tf_op jit(solution)/shard_map/ppermute | solution.py:212
  27.8 1.4 %collective-permute-done.7.refs_7_ = bf16[64,128]{1,0:T(8,128)(2,1)S(1)} collective-permute-done((bf16[64,128]{1,0:T(8,128)(2,1)S(1)}, bf16[64,128]{1,0:T(8,128)(2,1)S(1)}, u32[]{:S(2)}, u32[]{:S(2)}) %collective-permute-start.7) | collective-permute-done | bytes 16416 | tf_op jit(solution)/shard_map/ppermute | solution.py:212
  29.2 4.1 %collective-permute-start.14 = (bf16[64,128]{1,0:T(8,128)(2,1)S(1)}, bf16[64,128]{1,0:T(8,128)(2,1)S(1)}, u32[]{:S(2)}, u32[]{:S(2)}) collective-permute-start(bf16[64,128]{1,0:T(8,128)(2,1)S(1)} %reduce_parts.1.refs_0_), channel_id=1, source_target_pairs={{0,14},{1,15},{2,0},{3,1},{4,2},{5,3},{6,4},{7,5},{8,6},{9,7},{10,... | collective-permute-start | bytes 49160 | tf_op jit(solution)/shard_map/ppermute | solution.py:212
  33.3 0.0 collective-permute-start.13
  33.3 0.0 collective-permute-start.12
  33.3 3.0 %collective-permute-start.11 = (bf16[64,128]{1,0:T(8,128)(2,1)S(1)}, bf16[64,128]{1,0:T(8,128)(2,1)S(1)}, u32[]{:S(2)}, u32[]{:S(2)}) collective-permute-start(bf16[64,128]{1,0:T(8,128)(2,1)S(1)} %reduce_parts.1.refs_0_), channel_id=1, source_target_pairs={{0,8},{1,9},{2,10},{3,11},{4,12},{5,13},{6,14},{7,15},{8,0},{9,1},... | collective-permute-start | bytes 49160 | tf_op jit(solution)/shard_map/ppermute | solution.py:212
  36.3 0.3 collective-permute-start.10
  36.6 0.0 collective-permute-done.14.refs_7_
  36.6 1.7 %collective-permute-start.9 = (bf16[64,128]{1,0:T(8,128)(2,1)S(1)}, bf16[64,128]{1,0:T(8,128)(2,1)S(1)}, u32[]{:S(2)}, u32[]{:S(2)}) collective-permute-start(bf16[64,128]{1,0:T(8,128)(2,1)S(1)} %reduce_parts.1.refs_0_), channel_id=1, source_target_pairs={{0,4},{1,5},{2,6},{3,7},{4,8},{5,9},{6,10},{7,11},{8,12},{9,13},{1... | collective-permute-start | bytes 49160 | tf_op jit(solution)/shard_map/ppermute | solution.py:212
  38.3 0.0 collective-permute-done.13.refs_6_
  38.3 1.5 %collective-permute-start.8 = (bf16[64,128]{1,0:T(8,128)(2,1)S(1)}, bf16[64,128]{1,0:T(8,128)(2,1)S(1)}, u32[]{:S(2)}, u32[]{:S(2)}) collective-permute-start(bf16[64,128]{1,0:T(8,128)(2,1)S(1)} %reduce_parts.1.refs_0_), channel_id=1, source_target_pairs={{0,2},{1,3},{2,4},{3,5},{4,6},{5,7},{6,8},{7,9},{8,10},{9,11},{10,... | collective-permute-start | bytes 49160 | tf_op jit(solution)/shard_map/ppermute | solution.py:212
  39.8 0.0 collective-permute-done.12.refs_5_
  39.8 0.0 collective-permute-done.11.refs_4_
  39.8 2.1 %collective-permute-done.10.refs_3_ = bf16[64,128]{1,0:T(8,128)(2,1)S(1)} collective-permute-done((bf16[64,128]{1,0:T(8,128)(2,1)S(1)}, bf16[64,128]{1,0:T(8,128)(2,1)S(1)}, u32[]{:S(2)}, u32[]{:S(2)}) %collective-permute-start.10) | collective-permute-done | bytes 16416 | tf_op jit(solution)/shard_map/ppermute | solution.py:212
  41.9 1.6 %collective-permute-done.9.refs_2_ = bf16[64,128]{1,0:T(8,128)(2,1)S(1)} collective-permute-done((bf16[64,128]{1,0:T(8,128)(2,1)S(1)}, bf16[64,128]{1,0:T(8,128)(2,1)S(1)}, u32[]{:S(2)}, u32[]{:S(2)}) %collective-permute-start.9) | collective-permute-done | bytes 16416 | tf_op jit(solution)/shard_map/ppermute | solution.py:212
  43.4 1.3 %collective-permute-done.8.refs_1_ = bf16[64,128]{1,0:T(8,128)(2,1)S(1)} collective-permute-done((bf16[64,128]{1,0:T(8,128)(2,1)S(1)}, bf16[64,128]{1,0:T(8,128)(2,1)S(1)}, u32[]{:S(2)}, u32[]{:S(2)}) %collective-permute-start.8) | collective-permute-done | bytes 16416 | tf_op jit(solution)/shard_map/ppermute | solution.py:212
  44.7 0.4 product_terms.1.refs_0_
  45.1 0.0 collective-permute-start.29
  45.2 0.6 collective-permute-start.28
  45.8 3.8 %collective-permute-start.27 = (bf16[64,128]{1,0:T(8,128)(2,1)S(1)}, bf16[64,128]{1,0:T(8,128)(2,1)S(1)}, u32[]{:S(2)}, u32[]{:S(2)}) collective-permute-start(bf16[64,128]{1,0:T(8,128)(2,1)S(1)} %product_terms.1.refs_0_), channel_id=1, source_target_pairs={{0,13},{1,12},{2,15},{3,14},{4,1},{5,0},{6,3},{7,2},{8,5},{9,4},{1... | collective-permute-start | bytes 49160 | tf_op jit(solution)/shard_map/ppermute | solution.py:212
  49.5 0.0 collective-permute-start.26
  49.5 0.1 collective-permute-start.25
  49.6 0.0 collective-permute-done.29.refs_15_
  49.6 2.1 %collective-permute-start.24 = (bf16[64,128]{1,0:T(8,128)(2,1)S(1)}, bf16[64,128]{1,0:T(8,128)(2,1)S(1)}, u32[]{:S(2)}, u32[]{:S(2)}) collective-permute-start(bf16[64,128]{1,0:T(8,128)(2,1)S(1)} %product_terms.1.refs_0_), channel_id=1, source_target_pairs={{0,10},{1,11},{2,12},{3,13},{4,14},{5,15},{6,0},{7,1},{8,2},{9,3},... | collective-permute-start | bytes 49160 | tf_op jit(solution)/shard_map/ppermute | solution.py:212
  51.7 0.0 collective-permute-done.28.refs_14_
  51.7 2.6 %collective-permute-start.23 = (bf16[64,128]{1,0:T(8,128)(2,1)S(1)}, bf16[64,128]{1,0:T(8,128)(2,1)S(1)}, u32[]{:S(2)}, u32[]{:S(2)}) collective-permute-start(bf16[64,128]{1,0:T(8,128)(2,1)S(1)} %product_terms.1.refs_0_), channel_id=1, source_target_pairs={{0,9},{1,8},{2,11},{3,10},{4,13},{5,12},{6,15},{7,14},{8,1},{9,0},... | collective-permute-start | bytes 49160 | tf_op jit(solution)/shard_map/ppermute | solution.py:212
  54.3 0.0 collective-permute-done.27.refs_13_
  54.3 2.0 %collective-permute-start.22 = (bf16[64,128]{1,0:T(8,128)(2,1)S(1)}, bf16[64,128]{1,0:T(8,128)(2,1)S(1)}, u32[]{:S(2)}, u32[]{:S(2)}) collective-permute-start(bf16[64,128]{1,0:T(8,128)(2,1)S(1)} %product_terms.1.refs_0_), channel_id=1, source_target_pairs={{0,8},{1,9},{2,10},{3,11},{4,12},{5,13},{6,14},{7,15},{8,0},{9,1},... | collective-permute-start | bytes 49160 | tf_op jit(solution)/shard_map/ppermute | solution.py:212
  56.3 0.0 collective-permute-done.26.refs_12_
  56.3 0.0 collective-permute-start.21
  56.3 0.0 collective-permute-done.25.refs_11_
  56.3 2.1 %collective-permute-start.20 = (bf16[64,128]{1,0:T(8,128)(2,1)S(1)}, bf16[64,128]{1,0:T(8,128)(2,1)S(1)}, u32[]{:S(2)}, u32[]{:S(2)}) collective-permute-start(bf16[64,128]{1,0:T(8,128)(2,1)S(1)} %product_terms.1.refs_0_), channel_id=1, source_target_pairs={{0,6},{1,7},{2,8},{3,9},{4,10},{5,11},{6,12},{7,13},{8,14},{9,15},... | collective-permute-start | bytes 49160 | tf_op jit(solution)/shard_map/ppermute | solution.py:212
  58.4 0.0 collective-permute-done.24.refs_10_
  58.4 1.7 %collective-permute-start.19 = (bf16[64,128]{1,0:T(8,128)(2,1)S(1)}, bf16[64,128]{1,0:T(8,128)(2,1)S(1)}, u32[]{:S(2)}, u32[]{:S(2)}) collective-permute-start(bf16[64,128]{1,0:T(8,128)(2,1)S(1)} %product_terms.1.refs_0_), channel_id=1, source_target_pairs={{0,5},{1,4},{2,7},{3,6},{4,9},{5,8},{6,11},{7,10},{8,13},{9,12},{1... | collective-permute-start | bytes 49160 | tf_op jit(solution)/shard_map/ppermute | solution.py:212
  60.1 0.0 collective-permute-done.23.refs_9_
  60.2 0.1 collective-permute-start.18
  60.2 0.0 collective-permute-done.22.refs_8_
  60.2 0.7 collective-permute-start.17
  61.0 0.3 collective-permute-done.21.refs_7_
  61.3 1.6 %collective-permute-start.16 = (bf16[64,128]{1,0:T(8,128)(2,1)S(1)}, bf16[64,128]{1,0:T(8,128)(2,1)S(1)}, u32[]{:S(2)}, u32[]{:S(2)}) collective-permute-start(bf16[64,128]{1,0:T(8,128)(2,1)S(1)} %product_terms.1.refs_0_), channel_id=1, source_target_pairs={{0,2},{1,3},{2,4},{3,5},{4,6},{5,7},{6,8},{7,9},{8,10},{9,11},{10,... | collective-permute-start | bytes 49160 | tf_op jit(solution)/shard_map/ppermute | solution.py:212
  62.9 0.0 collective-permute-done.20.refs_6_
  62.9 0.9 %collective-permute-start.15 = (bf16[64,128]{1,0:T(8,128)(2,1)S(1)}, bf16[64,128]{1,0:T(8,128)(2,1)S(1)}, u32[]{:S(2)}, u32[]{:S(2)}) collective-permute-start(bf16[64,128]{1,0:T(8,128)(2,1)S(1)} %product_terms.1.refs_0_), channel_id=1, source_target_pairs={{0,1},{1,0},{2,3},{3,2},{4,5},{5,4},{6,7},{7,6},{8,9},{9,8},{10,11... | collective-permute-start | bytes 49160 | tf_op jit(solution)/shard_map/ppermute | solution.py:212
  63.8 1.9 %collective-permute-done.18.refs_4_ = bf16[64,128]{1,0:T(8,128)(2,1)S(1)} collective-permute-done((bf16[64,128]{1,0:T(8,128)(2,1)S(1)}, bf16[64,128]{1,0:T(8,128)(2,1)S(1)}, u32[]{:S(2)}, u32[]{:S(2)}) %collective-permute-start.18) | collective-permute-done | bytes 16416 | tf_op jit(solution)/shard_map/ppermute | solution.py:212
  65.7 0.5 collective-permute-done.17.refs_3_
  66.2 1.5 %collective-permute-done.16.refs_2_ = bf16[64,128]{1,0:T(8,128)(2,1)S(1)} collective-permute-done((bf16[64,128]{1,0:T(8,128)(2,1)S(1)}, bf16[64,128]{1,0:T(8,128)(2,1)S(1)}, u32[]{:S(2)}, u32[]{:S(2)}) %collective-permute-start.16) | collective-permute-done | bytes 16416 | tf_op jit(solution)/shard_map/ppermute | solution.py:212
  67.7 7.1 %finish.1 = f32[64,64]{1,0:T(8,128)} custom-call(bf16[64,128]{1,0:T(8,128)(2,1)S(1)} %product_terms.1.refs_0_, bf16[64,128]{1,0:T(8,128)(2,1)S(1)} %collective-permute-done.15.refs_1_, bf16[64,128]{1,0:T(8,128)(2,1)S(1)} %collective-permute-done.16.refs_2_, bf16[64,128]{1,0:T(8,128)(2,1)S(1)} %collective-permute-done.17.refs_3_, ...), custom_call_target="tpu_custom_call" | custom-call | tf_op jit(solution)/shard_map/finish/pallas_call | solution.py:192
  (7 shorter events, 0.0 us)
Async XLA Ops:
  0.0 3.4 %copy-start = (bf16[128,32,1024]{2,1,0:T(8,128)(2,1)S(1)}, bf16[128,32,1024]{2,1,0:T(8,128)(2,1)}, u32[]{:S(2)}) copy-start(bf16[128,32,1024]{2,1,0:T(8,128)(2,1)} %snapshot_ref.1) | copy-start | bytes 25165828
  3.4 0.9 %copy-start.1 = (bf16[1024,64]{0,1:T(8,128)(2,1)S(1)}, bf16[1024,64]{0,1:T(8,128)(2,1)}, u32[]{:S(2)}) copy-start(bf16[1024,64]{0,1:T(8,128)(2,1)} %param.4) | copy-start | bytes 393220
  4.3 8.6 %copy-start.2 = (bf16[128,64]{0,1:T(8,128)(2,1)S(1)}, bf16[128,64]{0,1:T(8,128)(2,1)}, u32[]{:S(2)}) copy-start(bf16[128,64]{0,1:T(8,128)(2,1)} %param.5) | copy-start | bytes 49156
  11.2 1.7 %collective-permute-start = (bf16[128,1024]{1,0:T(8,128)(2,1)S(1)}, bf16[128,1024]{1,0:T(8,128)(2,1)S(1)}, u32[]{:S(2)}, u32[]{:S(2)}) collective-permute-start(bf16[128,1024]{1,0:T(8,128)(2,1)S(1)} %get-tuple-element.16), channel_id=1, source_target_pairs={{0,1},{1,0},{2,3},{3,2},{4,5},{5,4},{6,7},{7,6},{8,9},{9,8},{10,11... | collective-permute-start | bytes 786440 | tf_op jit(solution)/shard_map/ppermute | solution.py:212
  13.1 10.9 %collective-permute-start.1 = (bf16[64,128]{1,0:T(8,128)(2,1)S(1)}, bf16[64,128]{1,0:T(8,128)(2,1)S(1)}, u32[]{:S(2)}, u32[]{:S(2)}) collective-permute-start(bf16[64,128]{1,0:T(8,128)(2,1)S(1)} %get-tuple-element.18), channel_id=1, source_target_pairs={{0,2},{1,3},{2,4},{3,5},{4,6},{5,7},{6,8},{7,9},{8,10},{9,11},{10,... | collective-permute-start | bytes 49160 | tf_op jit(solution)/shard_map/ppermute | solution.py:212
  16.1 9.3 %collective-permute-start.2 = (bf16[64,128]{1,0:T(8,128)(2,1)S(1)}, bf16[64,128]{1,0:T(8,128)(2,1)S(1)}, u32[]{:S(2)}, u32[]{:S(2)}) collective-permute-start(bf16[64,128]{1,0:T(8,128)(2,1)S(1)} %get-tuple-element.19), channel_id=1, source_target_pairs={{0,4},{1,5},{2,6},{3,7},{4,8},{5,9},{6,10},{7,11},{8,12},{9,13},{1... | collective-permute-start | bytes 49160 | tf_op jit(solution)/shard_map/ppermute | solution.py:212
  17.6 9.2 %collective-permute-start.3 = (bf16[64,128]{1,0:T(8,128)(2,1)S(1)}, bf16[64,128]{1,0:T(8,128)(2,1)S(1)}, u32[]{:S(2)}, u32[]{:S(2)}) collective-permute-start(bf16[64,128]{1,0:T(8,128)(2,1)S(1)} %get-tuple-element.20), channel_id=1, source_target_pairs={{0,6},{1,7},{2,8},{3,9},{4,10},{5,11},{6,12},{7,13},{8,14},{9,15},... | collective-permute-start | bytes 49160 | tf_op jit(solution)/shard_map/ppermute | solution.py:212
  20.2 6.6 %collective-permute-start.4 = (bf16[64,128]{1,0:T(8,128)(2,1)S(1)}, bf16[64,128]{1,0:T(8,128)(2,1)S(1)}, u32[]{:S(2)}, u32[]{:S(2)}) collective-permute-start(bf16[64,128]{1,0:T(8,128)(2,1)S(1)} %get-tuple-element.21), channel_id=1, source_target_pairs={{0,8},{1,9},{2,10},{3,11},{4,12},{5,13},{6,14},{7,15},{8,0},{9,1},... | collective-permute-start | bytes 49160 | tf_op jit(solution)/shard_map/ppermute | solution.py:212
  21.4 5.4 %collective-permute-start.5 = (bf16[64,128]{1,0:T(8,128)(2,1)S(1)}, bf16[64,128]{1,0:T(8,128)(2,1)S(1)}, u32[]{:S(2)}, u32[]{:S(2)}) collective-permute-start(bf16[64,128]{1,0:T(8,128)(2,1)S(1)} %get-tuple-element.22), channel_id=1, source_target_pairs={{0,10},{1,11},{2,12},{3,13},{4,14},{5,15},{6,0},{7,1},{8,2},{9,3},... | collective-permute-start | bytes 49160 | tf_op jit(solution)/shard_map/ppermute | solution.py:212
  24.1 3.7 %collective-permute-start.6 = (bf16[64,128]{1,0:T(8,128)(2,1)S(1)}, bf16[64,128]{1,0:T(8,128)(2,1)S(1)}, u32[]{:S(2)}, u32[]{:S(2)}) collective-permute-start(bf16[64,128]{1,0:T(8,128)(2,1)S(1)} %get-tuple-element.23), channel_id=1, source_target_pairs={{0,12},{1,13},{2,14},{3,15},{4,0},{5,1},{6,2},{7,3},{8,4},{9,5},{1... | collective-permute-start | bytes 49160 | tf_op jit(solution)/shard_map/ppermute | solution.py:212
  25.4 3.8 %collective-permute-start.7 = (bf16[64,128]{1,0:T(8,128)(2,1)S(1)}, bf16[64,128]{1,0:T(8,128)(2,1)S(1)}, u32[]{:S(2)}, u32[]{:S(2)}) collective-permute-start(bf16[64,128]{1,0:T(8,128)(2,1)S(1)} %get-tuple-element.24), channel_id=1, source_target_pairs={{0,14},{1,15},{2,0},{3,1},{4,2},{5,3},{6,4},{7,5},{8,6},{9,7},{10,... | collective-permute-start | bytes 49160 | tf_op jit(solution)/shard_map/ppermute | solution.py:212
  29.2 7.4 %collective-permute-start.14 = (bf16[64,128]{1,0:T(8,128)(2,1)S(1)}, bf16[64,128]{1,0:T(8,128)(2,1)S(1)}, u32[]{:S(2)}, u32[]{:S(2)}) collective-permute-start(bf16[64,128]{1,0:T(8,128)(2,1)S(1)} %reduce_parts.1.refs_0_), channel_id=1, source_target_pairs={{0,14},{1,15},{2,0},{3,1},{4,2},{5,3},{6,4},{7,5},{8,6},{9,7},{10,... | collective-permute-start | bytes 49160 | tf_op jit(solution)/shard_map/ppermute | solution.py:212
  33.3 5.0 %collective-permute-start.13 = (bf16[64,128]{1,0:T(8,128)(2,1)S(1)}, bf16[64,128]{1,0:T(8,128)(2,1)S(1)}, u32[]{:S(2)}, u32[]{:S(2)}) collective-permute-start(bf16[64,128]{1,0:T(8,128)(2,1)S(1)} %reduce_parts.1.refs_0_), channel_id=1, source_target_pairs={{0,12},{1,13},{2,14},{3,15},{4,0},{5,1},{6,2},{7,3},{8,4},{9,5},{1... | collective-permute-start | bytes 49160 | tf_op jit(solution)/shard_map/ppermute | solution.py:212
  33.3 6.4 %collective-permute-start.12 = (bf16[64,128]{1,0:T(8,128)(2,1)S(1)}, bf16[64,128]{1,0:T(8,128)(2,1)S(1)}, u32[]{:S(2)}, u32[]{:S(2)}) collective-permute-start(bf16[64,128]{1,0:T(8,128)(2,1)S(1)} %reduce_parts.1.refs_0_), channel_id=1, source_target_pairs={{0,10},{1,11},{2,12},{3,13},{4,14},{5,15},{6,0},{7,1},{8,2},{9,3},... | collective-permute-start | bytes 49160 | tf_op jit(solution)/shard_map/ppermute | solution.py:212
  33.3 6.4 %collective-permute-start.11 = (bf16[64,128]{1,0:T(8,128)(2,1)S(1)}, bf16[64,128]{1,0:T(8,128)(2,1)S(1)}, u32[]{:S(2)}, u32[]{:S(2)}) collective-permute-start(bf16[64,128]{1,0:T(8,128)(2,1)S(1)} %reduce_parts.1.refs_0_), channel_id=1, source_target_pairs={{0,8},{1,9},{2,10},{3,11},{4,12},{5,13},{6,14},{7,15},{8,0},{9,1},... | collective-permute-start | bytes 49160 | tf_op jit(solution)/shard_map/ppermute | solution.py:212
  36.3 5.5 %collective-permute-start.10 = (bf16[64,128]{1,0:T(8,128)(2,1)S(1)}, bf16[64,128]{1,0:T(8,128)(2,1)S(1)}, u32[]{:S(2)}, u32[]{:S(2)}) collective-permute-start(bf16[64,128]{1,0:T(8,128)(2,1)S(1)} %reduce_parts.1.refs_0_), channel_id=1, source_target_pairs={{0,6},{1,7},{2,8},{3,9},{4,10},{5,11},{6,12},{7,13},{8,14},{9,15},... | collective-permute-start | bytes 49160 | tf_op jit(solution)/shard_map/ppermute | solution.py:212
  36.6 6.8 %collective-permute-start.9 = (bf16[64,128]{1,0:T(8,128)(2,1)S(1)}, bf16[64,128]{1,0:T(8,128)(2,1)S(1)}, u32[]{:S(2)}, u32[]{:S(2)}) collective-permute-start(bf16[64,128]{1,0:T(8,128)(2,1)S(1)} %reduce_parts.1.refs_0_), channel_id=1, source_target_pairs={{0,4},{1,5},{2,6},{3,7},{4,8},{5,9},{6,10},{7,11},{8,12},{9,13},{1... | collective-permute-start | bytes 49160 | tf_op jit(solution)/shard_map/ppermute | solution.py:212
  38.3 6.4 %collective-permute-start.8 = (bf16[64,128]{1,0:T(8,128)(2,1)S(1)}, bf16[64,128]{1,0:T(8,128)(2,1)S(1)}, u32[]{:S(2)}, u32[]{:S(2)}) collective-permute-start(bf16[64,128]{1,0:T(8,128)(2,1)S(1)} %reduce_parts.1.refs_0_), channel_id=1, source_target_pairs={{0,2},{1,3},{2,4},{3,5},{4,6},{5,7},{6,8},{7,9},{8,10},{9,11},{10,... | collective-permute-start | bytes 49160 | tf_op jit(solution)/shard_map/ppermute | solution.py:212
  45.1 4.5 %collective-permute-start.29 = (bf16[64,128]{1,0:T(8,128)(2,1)S(1)}, bf16[64,128]{1,0:T(8,128)(2,1)S(1)}, u32[]{:S(2)}, u32[]{:S(2)}) collective-permute-start(bf16[64,128]{1,0:T(8,128)(2,1)S(1)} %product_terms.1.refs_0_), channel_id=1, source_target_pairs={{0,15},{1,14},{2,1},{3,0},{4,3},{5,2},{6,5},{7,4},{8,7},{9,6},{10,... | collective-permute-start | bytes 49160 | tf_op jit(solution)/shard_map/ppermute | solution.py:212
  45.2 6.6 %collective-permute-start.28 = (bf16[64,128]{1,0:T(8,128)(2,1)S(1)}, bf16[64,128]{1,0:T(8,128)(2,1)S(1)}, u32[]{:S(2)}, u32[]{:S(2)}) collective-permute-start(bf16[64,128]{1,0:T(8,128)(2,1)S(1)} %product_terms.1.refs_0_), channel_id=1, source_target_pairs={{0,14},{1,15},{2,0},{3,1},{4,2},{5,3},{6,4},{7,5},{8,6},{9,7},{10,... | collective-permute-start | bytes 49160 | tf_op jit(solution)/shard_map/ppermute | solution.py:212
  45.8 8.5 %collective-permute-start.27 = (bf16[64,128]{1,0:T(8,128)(2,1)S(1)}, bf16[64,128]{1,0:T(8,128)(2,1)S(1)}, u32[]{:S(2)}, u32[]{:S(2)}) collective-permute-start(bf16[64,128]{1,0:T(8,128)(2,1)S(1)} %product_terms.1.refs_0_), channel_id=1, source_target_pairs={{0,13},{1,12},{2,15},{3,14},{4,1},{5,0},{6,3},{7,2},{8,5},{9,4},{1... | collective-permute-start | bytes 49160 | tf_op jit(solution)/shard_map/ppermute | solution.py:212
  49.5 6.8 %collective-permute-start.26 = (bf16[64,128]{1,0:T(8,128)(2,1)S(1)}, bf16[64,128]{1,0:T(8,128)(2,1)S(1)}, u32[]{:S(2)}, u32[]{:S(2)}) collective-permute-start(bf16[64,128]{1,0:T(8,128)(2,1)S(1)} %product_terms.1.refs_0_), channel_id=1, source_target_pairs={{0,12},{1,13},{2,14},{3,15},{4,0},{5,1},{6,2},{7,3},{8,4},{9,5},{1... | collective-permute-start | bytes 49160 | tf_op jit(solution)/shard_map/ppermute | solution.py:212
  49.5 6.8 %collective-permute-start.25 = (bf16[64,128]{1,0:T(8,128)(2,1)S(1)}, bf16[64,128]{1,0:T(8,128)(2,1)S(1)}, u32[]{:S(2)}, u32[]{:S(2)}) collective-permute-start(bf16[64,128]{1,0:T(8,128)(2,1)S(1)} %product_terms.1.refs_0_), channel_id=1, source_target_pairs={{0,11},{1,10},{2,13},{3,12},{4,15},{5,14},{6,1},{7,0},{8,3},{9,2},... | collective-permute-start | bytes 49160 | tf_op jit(solution)/shard_map/ppermute | solution.py:212
  49.6 8.8 %collective-permute-start.24 = (bf16[64,128]{1,0:T(8,128)(2,1)S(1)}, bf16[64,128]{1,0:T(8,128)(2,1)S(1)}, u32[]{:S(2)}, u32[]{:S(2)}) collective-permute-start(bf16[64,128]{1,0:T(8,128)(2,1)S(1)} %product_terms.1.refs_0_), channel_id=1, source_target_pairs={{0,10},{1,11},{2,12},{3,13},{4,14},{5,15},{6,0},{7,1},{8,2},{9,3},... | collective-permute-start | bytes 49160 | tf_op jit(solution)/shard_map/ppermute | solution.py:212
  51.7 8.4 %collective-permute-start.23 = (bf16[64,128]{1,0:T(8,128)(2,1)S(1)}, bf16[64,128]{1,0:T(8,128)(2,1)S(1)}, u32[]{:S(2)}, u32[]{:S(2)}) collective-permute-start(bf16[64,128]{1,0:T(8,128)(2,1)S(1)} %product_terms.1.refs_0_), channel_id=1, source_target_pairs={{0,9},{1,8},{2,11},{3,10},{4,13},{5,12},{6,15},{7,14},{8,1},{9,0},... | collective-permute-start | bytes 49160 | tf_op jit(solution)/shard_map/ppermute | solution.py:212
  54.3 5.9 %collective-permute-start.22 = (bf16[64,128]{1,0:T(8,128)(2,1)S(1)}, bf16[64,128]{1,0:T(8,128)(2,1)S(1)}, u32[]{:S(2)}, u32[]{:S(2)}) collective-permute-start(bf16[64,128]{1,0:T(8,128)(2,1)S(1)} %product_terms.1.refs_0_), channel_id=1, source_target_pairs={{0,8},{1,9},{2,10},{3,11},{4,12},{5,13},{6,14},{7,15},{8,0},{9,1},... | collective-permute-start | bytes 49160 | tf_op jit(solution)/shard_map/ppermute | solution.py:212
  56.3 5.0 %collective-permute-start.21 = (bf16[64,128]{1,0:T(8,128)(2,1)S(1)}, bf16[64,128]{1,0:T(8,128)(2,1)S(1)}, u32[]{:S(2)}, u32[]{:S(2)}) collective-permute-start(bf16[64,128]{1,0:T(8,128)(2,1)S(1)} %product_terms.1.refs_0_), channel_id=1, source_target_pairs={{0,7},{1,6},{2,9},{3,8},{4,11},{5,10},{6,13},{7,12},{8,15},{9,14},... | collective-permute-start | bytes 49160 | tf_op jit(solution)/shard_map/ppermute | solution.py:212
  56.3 6.6 %collective-permute-start.20 = (bf16[64,128]{1,0:T(8,128)(2,1)S(1)}, bf16[64,128]{1,0:T(8,128)(2,1)S(1)}, u32[]{:S(2)}, u32[]{:S(2)}) collective-permute-start(bf16[64,128]{1,0:T(8,128)(2,1)S(1)} %product_terms.1.refs_0_), channel_id=1, source_target_pairs={{0,6},{1,7},{2,8},{3,9},{4,10},{5,11},{6,12},{7,13},{8,14},{9,15},... | collective-permute-start | bytes 49160 | tf_op jit(solution)/shard_map/ppermute | solution.py:212
  58.4 5.4 %collective-permute-start.19 = (bf16[64,128]{1,0:T(8,128)(2,1)S(1)}, bf16[64,128]{1,0:T(8,128)(2,1)S(1)}, u32[]{:S(2)}, u32[]{:S(2)}) collective-permute-start(bf16[64,128]{1,0:T(8,128)(2,1)S(1)} %product_terms.1.refs_0_), channel_id=1, source_target_pairs={{0,5},{1,4},{2,7},{3,6},{4,9},{5,8},{6,11},{7,10},{8,13},{9,12},{1... | collective-permute-start | bytes 49160 | tf_op jit(solution)/shard_map/ppermute | solution.py:212
  60.2 5.5 %collective-permute-start.18 = (bf16[64,128]{1,0:T(8,128)(2,1)S(1)}, bf16[64,128]{1,0:T(8,128)(2,1)S(1)}, u32[]{:S(2)}, u32[]{:S(2)}) collective-permute-start(bf16[64,128]{1,0:T(8,128)(2,1)S(1)} %product_terms.1.refs_0_), channel_id=1, source_target_pairs={{0,4},{1,5},{2,6},{3,7},{4,8},{5,9},{6,10},{7,11},{8,12},{9,13},{1... | collective-permute-start | bytes 49160 | tf_op jit(solution)/shard_map/ppermute | solution.py:212
  60.2 6.0 %collective-permute-start.17 = (bf16[64,128]{1,0:T(8,128)(2,1)S(1)}, bf16[64,128]{1,0:T(8,128)(2,1)S(1)}, u32[]{:S(2)}, u32[]{:S(2)}) collective-permute-start(bf16[64,128]{1,0:T(8,128)(2,1)S(1)} %product_terms.1.refs_0_), channel_id=1, source_target_pairs={{0,3},{1,2},{2,5},{3,4},{4,7},{5,6},{6,9},{7,8},{8,11},{9,10},{10,... | collective-permute-start | bytes 49160 | tf_op jit(solution)/shard_map/ppermute | solution.py:212
  61.3 6.4 %collective-permute-start.16 = (bf16[64,128]{1,0:T(8,128)(2,1)S(1)}, bf16[64,128]{1,0:T(8,128)(2,1)S(1)}, u32[]{:S(2)}, u32[]{:S(2)}) collective-permute-start(bf16[64,128]{1,0:T(8,128)(2,1)S(1)} %product_terms.1.refs_0_), channel_id=1, source_target_pairs={{0,2},{1,3},{2,4},{3,5},{4,6},{5,7},{6,8},{7,9},{8,10},{9,11},{10,... | collective-permute-start | bytes 49160 | tf_op jit(solution)/shard_map/ppermute | solution.py:212
  62.9 4.8 %collective-permute-start.15 = (bf16[64,128]{1,0:T(8,128)(2,1)S(1)}, bf16[64,128]{1,0:T(8,128)(2,1)S(1)}, u32[]{:S(2)}, u32[]{:S(2)}) collective-permute-start(bf16[64,128]{1,0:T(8,128)(2,1)S(1)} %product_terms.1.refs_0_), channel_id=1, source_target_pairs={{0,1},{1,0},{2,3},{3,2},{4,5},{5,4},{6,7},{7,6},{8,9},{9,8},{10,11... | collective-permute-start | bytes 49160 | tf_op jit(solution)/shard_map/ppermute | solution.py:212

commit v3 on v2

v3 whole, which is shorter than its diff:
```python
import functools

import jax
import jax.numpy as jnp
from jax import lax
from jax.experimental import pallas as pl
from jax.experimental.pallas import tpu as pltpu
from jax.sharding import PartitionSpec as P

F32 = jnp.float32
BF16 = jnp.bfloat16
LANES = 128
MIB = 2**20


def dot_f32(a, b, dims, precision=None):
    return lax.dot_general(a, b, (dims, ((), ())), precision=precision, preferred_element_type=F32)


def params(mib):
    return pltpu.CompilerParams(vmem_limit_bytes=mib * MIB)


def contract_kernel(step, snapshot_ref, mode2_ref, send_ref, own_ref, slab_ref, core_ref, sems):
    cells, fibers, depth = snapshot_ref.shape
    rank = mode2_ref.shape[0]
    reps = LANES // rank
    half = fibers // 2
    chunks = cells // step

    def copy(chunk):
        where = pl.ds(chunk * step, step)
        return pltpu.make_async_copy(snapshot_ref.at[where], slab_ref.at[where], sems.at[chunk])

    for chunk in range(chunks):
        copy(chunk).start()
    wide = jnp.concatenate([mode2_ref[...]] * reps, axis=0).T
    lane = lax.broadcasted_iota(jnp.int32, (step, LANES), 1)
    first = lax.axis_index("col") == 0

    for chunk in range(chunks):
        copy(chunk).wait()
        core = core_ref.at[chunk % 2]
        rows = pl.ds(chunk * step, step)
        core[...] = dot_f32(slab_ref[rows].reshape(step * fibers, depth), wide, ((1,), (0,)))

        def columns(start):
            part = core[pl.ds(start, step, stride=fibers), :]
            for r in range(1, reps):
                other = core[pl.ds(start + r, step, stride=fibers), :]
                part = jnp.where(lane < r * rank, part, other)
            return part

        for block in range(half // reps):
            low = columns(block * reps)
            high = columns(half + block * reps)
            where = slice(block * LANES, (block + 1) * LANES)
            own_ref[rows, where] = jnp.where(first, low, high).astype(BF16)
            send_ref[rows, where] = jnp.where(first, high, low).astype(BF16)


def contract(snapshot, mode2_t):
    cells, fibers, depth = snapshot.shape
    rank = mode2_t.shape[0]
    step = 16
    out = jax.ShapeDtypeStruct((cells, fibers // 2 * rank), BF16)
    return pl.pallas_call(
        functools.partial(contract_kernel, step),
        in_specs=[
            pl.BlockSpec(memory_space=pltpu.HBM),
            pl.BlockSpec(memory_space=pltpu.VMEM),
        ],
        out_shape=[out, out],
        scratch_shapes=[
            pltpu.VMEM(snapshot.shape, BF16),
            pltpu.VMEM((2, step * fibers, LANES), F32),
            pltpu.SemaphoreType.DMA((cells // step,)),
        ],
        compiler_params=params(57),
        name="contract",
    )(snapshot, mode2_t)


def add_to(*refs):
    total = refs[0][...].astype(F32)
    for ref in refs[1:]:
        total += ref[...].astype(F32)
    return total


def project_kernel(own_ref, got_ref, factor_ref, keep_ref, send_ref):
    rank = factor_ref.shape[0]
    factor = factor_ref[...]
    total = dot_f32(factor, own_ref[...], ((1,), (0,))) + dot_f32(factor, got_ref[...], ((1,), (0,)))
    even = lax.rem(lax.axis_index("row"), 2) == 0
    blocks = total.shape[1] // LANES // 2
    for block in range(blocks):
        low = total[:, block * LANES:(block + 1) * LANES]
        high = total[:, (block + blocks) * LANES:(block + blocks + 1) * LANES]
        rows = pl.ds(block * rank, rank)
        keep_ref[rows, :] = jnp.where(even, low, high)
        send_ref[rows, :] = jnp.where(even, high, low).astype(BF16)


def project(own, got, factor_t):
    rank = factor_t.shape[0]
    shape = (rank * own.shape[1] // LANES // 2, LANES)
    return pl.pallas_call(
        project_kernel,
        out_shape=[jax.ShapeDtypeStruct(shape, F32), jax.ShapeDtypeStruct(shape, BF16)],
        compiler_params=params(4),
        name="project",
    )(own, got, factor_t)


def add_kernel(mine_ref, got_ref, out_ref):
    out_ref[...] = add_to(mine_ref, got_ref).astype(out_ref.dtype)


def add(mine, got):
    return pl.pallas_call(
        add_kernel,
        out_shape=jax.ShapeDtypeStruct(got.shape, got.dtype),
        compiler_params=params(4),
        name="add",
    )(mine, got)


def product_kernel(own_ref, got_ref, mine_ref, other_ref, out_ref):
    cells, width = own_ref.shape
    blocks = width // LANES // 2
    rank = mine_ref.shape[0] // blocks
    even = lax.rem(lax.axis_index("row"), 2) == 0
    total = jnp.zeros((cells, rank), F32)
    for block in range(blocks):
        rows = pl.ds(block * rank, rank)
        mine, other = mine_ref[rows, :], other_ref[rows, :]
        low = jnp.where(even, mine, other)
        high = jnp.where(even, other, mine)
        for at, projected in ((block, low), (block + blocks, high)):
            where = slice(at * LANES, (at + 1) * LANES)
            total += dot_f32(own_ref[:, where], projected, ((1,), (1,)))
            total += dot_f32(got_ref[:, where], projected, ((1,), (1,)))
    half = cells // 2
    out_ref[...] = jnp.concatenate([total[:half], total[half:]], axis=1).astype(BF16)


def product_terms(own, got, mine, other):
    return pl.pallas_call(
        product_kernel,
        out_shape=jax.ShapeDtypeStruct((own.shape[0] // 2, LANES), BF16),
        compiler_params=params(4),
        name="product_terms",
    )(own, got, mine, other)


def gram_kernel(term_ref, got_ref, out_ref):
    product = add_to(term_ref, got_ref)
    rank = LANES // 2
    wide = dot_f32(product, product, ((0,), (0,)), lax.Precision.HIGHEST)
    gram = wide[:rank, :rank] + wide[rank:, rank:]
    out_ref[...] = jnp.concatenate([gram[:rank // 2], gram[rank // 2:]], axis=1)


def local_gram(term, got):
    return pl.pallas_call(
        gram_kernel,
        out_shape=jax.ShapeDtypeStruct((LANES // 4, LANES), F32),
        compiler_params=params(4),
        name="local_gram",
    )(term, got)


def finish_kernel(total_rows, term_ref, got_term_ref, gram_ref, got_gram_ref, out_ref):
    rank = LANES // 2
    packed = gram_ref[...] + got_gram_ref[...]
    gram = jnp.concatenate([packed[:, :rank], packed[:, rank:]], axis=0)
    eye = (
        lax.broadcasted_iota(jnp.int32, (rank, rank), 0)
        == lax.broadcasted_iota(jnp.int32, (rank, rank), 1)
    ).astype(F32)
    both = jnp.concatenate([gram, eye], axis=1)
    row_index = lax.broadcasted_iota(jnp.int32, (rank, 1), 0)
    pivots = jnp.zeros((rank, 1), F32)
    for k in range(rank):
        pivot = both[k:k + 1, k:k + 1]
        pivots = jnp.where(row_index == k, pivot, pivots)
        factor = jnp.where(row_index > k, both[:, k:k + 1] / pivot, 0.0)
        both = both - factor * both[k:k + 1, :]
    inverse = both[:, rank:] * (lax.rsqrt(pivots) * (total_rows ** 0.5))
    product = add_to(term_ref, got_term_ref)
    mine = jnp.where(lax.axis_index("col") == 0, product[:, :rank], product[:, rank:])
    out_ref[...] = dot_f32(mine, inverse, ((1,), (1,)), lax.Precision.HIGHEST)


def finish(total_rows, term, got_term, gram, got_gram):
    return pl.pallas_call(
        functools.partial(finish_kernel, total_rows),
        out_shape=jax.ShapeDtypeStruct((term.shape[0], LANES // 2), F32),
        compiler_params=params(4),
        name="finish",
    )(term, got_term, gram, got_gram)


def swap(x, axis, mask):
    return lax.ppermute(x, axis, [(d, d ^ mask) for d in range(lax.axis_size(axis))])


def per_device(snapshot, mode2_factor, old_factor):
    n_rows = lax.axis_size("row")
    masks = [1 << bit for bit in range(n_rows.bit_length() - 1)]
    total_rows = snapshot.shape[0] * n_rows

    send, own = contract(snapshot, mode2_factor.T)
    got = swap(send, "col", 1)

    keep, send = project(own, got, old_factor.T)
    mine = add(keep, swap(send, "row", masks[0]))
    for mask in masks[1:]:
        mine = add(mine, swap(mine, "row", mask))
    other = swap(mine, "row", masks[0])

    term = product_terms(own, got, mine, other)
    got_term = swap(term, "col", 1)
    gram = local_gram(term, got_term)
    for mask in masks[:-1]:
        gram = add(gram, swap(gram, "row", mask))
    return finish(total_rows, term, got_term, gram, swap(gram, "row", masks[-1]))


def solution(mesh):
    return jax.shard_map(
        per_device,
        mesh=mesh,
        in_specs=(
            P(("groups", "row"), None, "col"),
            P(("groups", "col"), None),
            P(("groups", "row"), None),
        ),
        out_specs=P(("groups", "row", "col"), None),
        check_vma=False,
    )
```

time: 75 us -> 53.7 us (0.72)
  starting transfers between devices: 43.1 us -> 17.3 us
  waiting for transfers between devices: 12.7 us -> 17.4 us
  local copies, waits for them, and re-layouts: 4.29 us -> 1.9 us
  Pallas kernels: 14.7 us -> 16.9 us
    ppermute x30 -> x9, starting transfers between devices: 43.1 us -> 17.3 us  [swap(): lax.ppermute(x, axis, [(d, d ^ mask) for d in range(lax.axis_size(axis))])]
    ppermute x30 -> x9, waiting for transfers between devices: 12.7 us -> 17.4 us  [swap(): lax.ppermute(x, axis, [(d, d ^ mask) for d in range(lax.axis_size(axis))])]
    unnamed x6, local copies, waits for them, and re-layouts: 4.29 us -> 1.9 us
    pallas_call x1, Pallas kernels: 6.91 us -> 9.28 us  [contract(): pl.pallas_call(functools.partial(contract_kernel, step), in_specs=[pl.Blo...]
    pallas_call x4 -> x9, Pallas kernels: 7.74 us -> 7.65 us  [the longest x1 6.62 us: finish(): pl.pallas_call(functools.partial(finish_kernel, total_rows), out_shape=ja...]
  transfers between devices with their start and end apart: 30 -> 9, of which waited for: 10 -> 9; matrix products, arithmetic and copies ran while one was open for 0% -> 0% of each run, Pallas kernels for 0% -> 0%
where the time goes in v3:
time: 53.7 us; the launch traced here: 53.5 us
  waiting for transfers between devices  17.4 us (32%)
  starting transfers between devices  17.3 us (32%)
  Pallas kernels  16.9 us (31%)
  local copies, waits for them, and re-layouts  1.9 us (4%)
    ppermute x9, waiting for transfers between devices, swap(): lax.ppermute(x, axis, [(d, d ^ mask) for d in range(lax.axis_size(axis))])  17.4 us
    ppermute x9, starting transfers between devices, swap(): lax.ppermute(x, axis, [(d, d ^ mask) for d in range(lax.axis_size(axis))])  17.3 us
    pallas_call x1, Pallas kernels, contract(): pl.pallas_call(functools.partial(contract_kernel, step), in_specs=[pl.Blo...  9.28 us
    pallas_call x1, Pallas kernels, finish(): pl.pallas_call(functools.partial(finish_kernel, total_rows), out_shape=ja...  6.62 us
    unnamed x6, local copies, waits for them, and re-layouts  1.9 us
  transfers between devices with their start and end apart: 9, of which 9 were waited for; matrix products, arithmetic and copies ran while one was open for 0% of the time, Pallas kernels for 0%

profile of v3, /device:TPU:0, one launch (start us, length us, event | category | flops | bytes accessed | tf_op | source)
XLA Modules:
  0.0 53.5 jit_solution(1736393469958310606)
XLA Ops:
  0.0 0.0 copy-start.2
  0.0 9.3 %contract.1 = (bf16[128,1024]{1,0:T(8,128)(2,1)}, bf16[128,1024]{1,0:T(8,128)(2,1)}) custom-call(bf16[128,32,1024]{2,1,0:T(8,128)(2,1)} %snapshot_ref.1, bf16[64,1024]{1,0:T(8,128)(2,1)} %bitcast.3), custom_call_target="tpu_custom_call" | custom-call | tf_op jit(solution)/shard_map/contract/pallas_call | solution.py:67
  9.3 0.5 collective-permute-start
  9.8 1.4 %collective-permute-done.got_ref = bf16[128,1024]{1,0:T(8,128)(2,1)S(1)} collective-permute-done((bf16[128,1024]{1,0:T(8,128)(2,1)}, bf16[128,1024]{1,0:T(8,128)(2,1)S(1)}, u32[]{:S(2)}, u32[]{:S(2)}) %collective-permute-start) | collective-permute-done | bytes 262176 | tf_op jit(solution)/shard_map/ppermute | solution.py:206
  11.2 0.0 copy-done.2
  11.2 0.0 copy-start
  11.2 0.9 %copy-done = bf16[128,1024]{1,0:T(8,128)(2,1)S(1)} copy-done((bf16[128,1024]{1,0:T(8,128)(2,1)S(1)}, bf16[128,1024]{1,0:T(8,128)(2,1)}, u32[]{:S(2)}) %copy-start) | copy-done | bytes 262168
  12.1 0.2 project.1
  12.4 3.0 %collective-permute-start.1 = (bf16[256,128]{1,0:T(8,128)(2,1)S(1)}, bf16[256,128]{1,0:T(8,128)(2,1)S(1)}, u32[]{:S(2)}, u32[]{:S(2)}) collective-permute-start(bf16[256,128]{1,0:T(8,128)(2,1)S(1)} %get-tuple-element.12), channel_id=1, source_target_pairs={{0,2},{2,0},{4,6},{6,4},{8,10},{10,8},{12,14},{14,12},{1,3},{3,1},... | collective-permute-start | bytes 196616 | tf_op jit(solution)/shard_map/ppermute | solution.py:206
  15.3 2.4 %collective-permute-done.1.got_ref = bf16[256,128]{1,0:T(8,128)(2,1)S(1)} collective-permute-done((bf16[256,128]{1,0:T(8,128)(2,1)S(1)}, bf16[256,128]{1,0:T(8,128)(2,1)S(1)}, u32[]{:S(2)}, u32[]{:S(2)}) %collective-permute-start.1) | collective-permute-done | bytes 65568 | tf_op jit(solution)/shard_map/ppermute | solution.py:206
  17.7 2.0 %collective-permute-start.2 = (bf16[256,128]{1,0:T(8,128)(2,1)S(1)}, bf16[256,128]{1,0:T(8,128)(2,1)S(1)}, u32[]{:S(2)}, u32[]{:S(2)}) collective-permute-start(bf16[256,128]{1,0:T(8,128)(2,1)S(1)} %add.5.mine_ref), channel_id=1, source_target_pairs={{0,4},{2,6},{4,0},{6,2},{8,12},{10,14},{12,8},{14,10},{1,5},{3,7},... | collective-permute-start | bytes 196616 | tf_op jit(solution)/shard_map/ppermute | solution.py:206
  19.7 2.3 %collective-permute-done.2.got_ref = bf16[256,128]{1,0:T(8,128)(2,1)S(1)} collective-permute-done((bf16[256,128]{1,0:T(8,128)(2,1)S(1)}, bf16[256,128]{1,0:T(8,128)(2,1)S(1)}, u32[]{:S(2)}, u32[]{:S(2)}) %collective-permute-start.2) | collective-permute-done | bytes 65568 | tf_op jit(solution)/shard_map/ppermute | solution.py:206
  22.1 3.0 %collective-permute-start.3 = (bf16[256,128]{1,0:T(8,128)(2,1)S(1)}, bf16[256,128]{1,0:T(8,128)(2,1)S(1)}, u32[]{:S(2)}, u32[]{:S(2)}) collective-permute-start(bf16[256,128]{1,0:T(8,128)(2,1)S(1)} %add.6.mine_ref), channel_id=1, source_target_pairs={{0,8},{2,10},{4,12},{6,14},{8,0},{10,2},{12,4},{14,6},{1,9},{3,11}... | collective-permute-start | bytes 196616 | tf_op jit(solution)/shard_map/ppermute | solution.py:206
  25.1 2.2 %collective-permute-done.3.got_ref = bf16[256,128]{1,0:T(8,128)(2,1)S(1)} collective-permute-done((bf16[256,128]{1,0:T(8,128)(2,1)S(1)}, bf16[256,128]{1,0:T(8,128)(2,1)S(1)}, u32[]{:S(2)}, u32[]{:S(2)}) %collective-permute-start.3) | collective-permute-done | bytes 65568 | tf_op jit(solution)/shard_map/ppermute | solution.py:206
  27.4 1.9 %collective-permute-start.4 = (bf16[256,128]{1,0:T(8,128)(2,1)S(1)}, bf16[256,128]{1,0:T(8,128)(2,1)S(1)}, u32[]{:S(2)}, u32[]{:S(2)}) collective-permute-start(bf16[256,128]{1,0:T(8,128)(2,1)S(1)} %add.7.mine_ref), channel_id=1, source_target_pairs={{0,2},{2,0},{4,6},{6,4},{8,10},{10,8},{12,14},{14,12},{1,3},{3,1},... | collective-permute-start | bytes 196616 | tf_op jit(solution)/shard_map/ppermute | solution.py:206
  29.3 2.4 %collective-permute-done.4.other_ref = bf16[256,128]{1,0:T(8,128)(2,1)S(1)} collective-permute-done((bf16[256,128]{1,0:T(8,128)(2,1)S(1)}, bf16[256,128]{1,0:T(8,128)(2,1)S(1)}, u32[]{:S(2)}, u32[]{:S(2)}) %collective-permute-start.4) | collective-permute-done | bytes 65568 | tf_op jit(solution)/shard_map/ppermute | solution.py:206
  31.7 0.0 copy-start.1
  31.7 0.9 %copy-done.1 = bf16[128,1024]{1,0:T(8,128)(2,1)S(1)} copy-done((bf16[128,1024]{1,0:T(8,128)(2,1)S(1)}, bf16[128,1024]{1,0:T(8,128)(2,1)}, u32[]{:S(2)}) %copy-start.1) | copy-done | bytes 262168
  32.6 0.4 product_terms.1.term_ref
  33.0 0.1 collective-permute-start.5
  33.1 1.2 %collective-permute-done.5.got_ref.got_term_ref = bf16[64,128]{1,0:T(8,128)(2,1)S(1)} collective-permute-done((bf16[64,128]{1,0:T(8,128)(2,1)S(1)}, bf16[64,128]{1,0:T(8,128)(2,1)S(1)}, u32[]{:S(2)}, u32[]{:S(2)}) %collective-permute-start.5) | collective-permute-done | bytes 16416 | tf_op jit(solution)/shard_map/ppermute | solution.py:206
  34.2 0.4 local_gram.1.mine_ref
  34.6 1.9 %collective-permute-start.6 = (f32[32,128]{1,0:T(8,128)S(1)}, f32[32,128]{1,0:T(8,128)S(1)}, u32[]{:S(2)}, u32[]{:S(2)}) collective-permute-start(f32[32,128]{1,0:T(8,128)S(1)} %local_gram.1.mine_ref), channel_id=1, source_target_pairs={{0,2},{2,0},{4,6},{6,4},{8,10},{10,8},{12,14},{14,12},{1,3},{3,1},... | collective-permute-start | bytes 49160 | tf_op jit(solution)/shard_map/ppermute | solution.py:206
  36.5 1.9 %collective-permute-done.6.got_ref = f32[32,128]{1,0:T(8,128)S(1)} collective-permute-done((f32[32,128]{1,0:T(8,128)S(1)}, f32[32,128]{1,0:T(8,128)S(1)}, u32[]{:S(2)}, u32[]{:S(2)}) %collective-permute-start.6) | collective-permute-done | bytes 16416 | tf_op jit(solution)/shard_map/ppermute | solution.py:206
  38.4 1.9 %collective-permute-start.7 = (f32[32,128]{1,0:T(8,128)S(1)}, f32[32,128]{1,0:T(8,128)S(1)}, u32[]{:S(2)}, u32[]{:S(2)}) collective-permute-start(f32[32,128]{1,0:T(8,128)S(1)} %add.8.mine_ref), channel_id=1, source_target_pairs={{0,4},{2,6},{4,0},{6,2},{8,12},{10,14},{12,8},{14,10},{1,5},{3,7},... | collective-permute-start | bytes 49160 | tf_op jit(solution)/shard_map/ppermute | solution.py:206
  40.3 1.8 %collective-permute-done.7.got_ref = f32[32,128]{1,0:T(8,128)S(1)} collective-permute-done((f32[32,128]{1,0:T(8,128)S(1)}, f32[32,128]{1,0:T(8,128)S(1)}, u32[]{:S(2)}, u32[]{:S(2)}) %collective-permute-start.7) | collective-permute-done | bytes 16416 | tf_op jit(solution)/shard_map/ppermute | solution.py:206
  42.1 3.1 %collective-permute-start.8 = (f32[32,128]{1,0:T(8,128)S(1)}, f32[32,128]{1,0:T(8,128)S(1)}, u32[]{:S(2)}, u32[]{:S(2)}) collective-permute-start(f32[32,128]{1,0:T(8,128)S(1)} %add.9.gram_ref), channel_id=1, source_target_pairs={{0,8},{2,10},{4,12},{6,14},{8,0},{10,2},{12,4},{14,6},{1,9},{3,11}... | collective-permute-start | bytes 49160 | tf_op jit(solution)/shard_map/ppermute | solution.py:206
  45.2 1.7 %collective-permute-done.8.got_gram_ref = f32[32,128]{1,0:T(8,128)S(1)} collective-permute-done((f32[32,128]{1,0:T(8,128)S(1)}, f32[32,128]{1,0:T(8,128)S(1)}, u32[]{:S(2)}, u32[]{:S(2)}) %collective-permute-start.8) | collective-permute-done | bytes 16416 | tf_op jit(solution)/shard_map/ppermute | solution.py:206
  46.9 6.6 %finish.1 = f32[64,64]{1,0:T(8,128)} custom-call(bf16[64,128]{1,0:T(8,128)(2,1)S(1)} %product_terms.1.term_ref, bf16[64,128]{1,0:T(8,128)(2,1)S(1)} %collective-permute-done.5.got_ref.got_term_ref, f32[32,128]{1,0:T(8,128)S(1)} %add.9.gram_ref, f32[32,128]{1,0:T(8,128)S(1)} %collective-permute-done.8.got_gram_ref), custom_call_target="tpu_custom_call" | custom-call | tf_op jit(solution)/shard_map/finish/pallas_call | solution.py:197
  (5 shorter events, 0.1 us)
Async XLA Ops:
  0.0 11.2 %copy-start.2 = (bf16[128,64]{0,1:T(8,128)(2,1)S(1)}, bf16[128,64]{0,1:T(8,128)(2,1)}, u32[]{:S(2)}) copy-start(bf16[128,64]{0,1:T(8,128)(2,1)} %param.5) | copy-start | bytes 49156
  9.3 1.9 %collective-permute-start = (bf16[128,1024]{1,0:T(8,128)(2,1)}, bf16[128,1024]{1,0:T(8,128)(2,1)S(1)}, u32[]{:S(2)}, u32[]{:S(2)}) collective-permute-start(bf16[128,1024]{1,0:T(8,128)(2,1)} %get-tuple-element.10), channel_id=1, source_target_pairs={{0,1},{1,0},{2,3},{3,2},{4,5},{5,4},{6,7},{7,6},{8,9},{9,8},{10,11... | collective-permute-start | bytes 786440 | tf_op jit(solution)/shard_map/ppermute | solution.py:206
  11.2 1.0 %copy-start = (bf16[128,1024]{1,0:T(8,128)(2,1)S(1)}, bf16[128,1024]{1,0:T(8,128)(2,1)}, u32[]{:S(2)}) copy-start(bf16[128,1024]{1,0:T(8,128)(2,1)} %get-tuple-element.9.own_ref) | copy-start | bytes 786436
  12.4 5.3 %collective-permute-start.1 = (bf16[256,128]{1,0:T(8,128)(2,1)S(1)}, bf16[256,128]{1,0:T(8,128)(2,1)S(1)}, u32[]{:S(2)}, u32[]{:S(2)}) collective-permute-start(bf16[256,128]{1,0:T(8,128)(2,1)S(1)} %get-tuple-element.12), channel_id=1, source_target_pairs={{0,2},{2,0},{4,6},{6,4},{8,10},{10,8},{12,14},{14,12},{1,3},{3,1},... | collective-permute-start | bytes 196616 | tf_op jit(solution)/shard_map/ppermute | solution.py:206
  17.7 4.3 %collective-permute-start.2 = (bf16[256,128]{1,0:T(8,128)(2,1)S(1)}, bf16[256,128]{1,0:T(8,128)(2,1)S(1)}, u32[]{:S(2)}, u32[]{:S(2)}) collective-permute-start(bf16[256,128]{1,0:T(8,128)(2,1)S(1)} %add.5.mine_ref), channel_id=1, source_target_pairs={{0,4},{2,6},{4,0},{6,2},{8,12},{10,14},{12,8},{14,10},{1,5},{3,7},... | collective-permute-start | bytes 196616 | tf_op jit(solution)/shard_map/ppermute | solution.py:206
  22.1 5.3 %collective-permute-start.3 = (bf16[256,128]{1,0:T(8,128)(2,1)S(1)}, bf16[256,128]{1,0:T(8,128)(2,1)S(1)}, u32[]{:S(2)}, u32[]{:S(2)}) collective-permute-start(bf16[256,128]{1,0:T(8,128)(2,1)S(1)} %add.6.mine_ref), channel_id=1, source_target_pairs={{0,8},{2,10},{4,12},{6,14},{8,0},{10,2},{12,4},{14,6},{1,9},{3,11}... | collective-permute-start | bytes 196616 | tf_op jit(solution)/shard_map/ppermute | solution.py:206
  27.4 4.3 %collective-permute-start.4 = (bf16[256,128]{1,0:T(8,128)(2,1)S(1)}, bf16[256,128]{1,0:T(8,128)(2,1)S(1)}, u32[]{:S(2)}, u32[]{:S(2)}) collective-permute-start(bf16[256,128]{1,0:T(8,128)(2,1)S(1)} %add.7.mine_ref), channel_id=1, source_target_pairs={{0,2},{2,0},{4,6},{6,4},{8,10},{10,8},{12,14},{14,12},{1,3},{3,1},... | collective-permute-start | bytes 196616 | tf_op jit(solution)/shard_map/ppermute | solution.py:206
  31.7 1.0 %copy-start.1 = (bf16[128,1024]{1,0:T(8,128)(2,1)S(1)}, bf16[128,1024]{1,0:T(8,128)(2,1)}, u32[]{:S(2)}) copy-start(bf16[128,1024]{1,0:T(8,128)(2,1)} %get-tuple-element.9.own_ref) | copy-start | bytes 786436
  33.0 1.2 %collective-permute-start.5 = (bf16[64,128]{1,0:T(8,128)(2,1)S(1)}, bf16[64,128]{1,0:T(8,128)(2,1)S(1)}, u32[]{:S(2)}, u32[]{:S(2)}) collective-permute-start(bf16[64,128]{1,0:T(8,128)(2,1)S(1)} %product_terms.1.term_ref), channel_id=1, source_target_pairs={{0,1},{1,0},{2,3},{3,2},{4,5},{5,4},{6,7},{7,6},{8,9},{9,8},{10,11... | collective-permute-start | bytes 49160 | tf_op jit(solution)/shard_map/ppermute | solution.py:206
  34.6 3.8 %collective-permute-start.6 = (f32[32,128]{1,0:T(8,128)S(1)}, f32[32,128]{1,0:T(8,128)S(1)}, u32[]{:S(2)}, u32[]{:S(2)}) collective-permute-start(f32[32,128]{1,0:T(8,128)S(1)} %local_gram.1.mine_ref), channel_id=1, source_target_pairs={{0,2},{2,0},{4,6},{6,4},{8,10},{10,8},{12,14},{14,12},{1,3},{3,1},... | collective-permute-start | bytes 49160 | tf_op jit(solution)/shard_map/ppermute | solution.py:206
  38.4 3.7 %collective-permute-start.7 = (f32[32,128]{1,0:T(8,128)S(1)}, f32[32,128]{1,0:T(8,128)S(1)}, u32[]{:S(2)}, u32[]{:S(2)}) collective-permute-start(f32[32,128]{1,0:T(8,128)S(1)} %add.8.mine_ref), channel_id=1, source_target_pairs={{0,4},{2,6},{4,0},{6,2},{8,12},{10,14},{12,8},{14,10},{1,5},{3,7},... | collective-permute-start | bytes 49160 | tf_op jit(solution)/shard_map/ppermute | solution.py:206
  42.1 4.8 %collective-permute-start.8 = (f32[32,128]{1,0:T(8,128)S(1)}, f32[32,128]{1,0:T(8,128)S(1)}, u32[]{:S(2)}, u32[]{:S(2)}) collective-permute-start(f32[32,128]{1,0:T(8,128)S(1)} %add.9.gram_ref), channel_id=1, source_target_pairs={{0,8},{2,10},{4,12},{6,14},{8,0},{10,2},{12,4},{14,6},{1,9},{3,11}... | collective-permute-start | bytes 49160 | tf_op jit(solution)/shard_map/ppermute | solution.py:206

commit v4 on v3

v4 whole, which is shorter than its diff:
```python
import functools

import jax
import jax.numpy as jnp
from jax import lax
from jax.experimental import pallas as pl
from jax.experimental.pallas import tpu as pltpu
from jax.sharding import PartitionSpec as P

F32 = jnp.float32
BF16 = jnp.bfloat16
LANES = 128
MIB = 2**20


def dot_f32(a, b, dims, precision=None):
    return lax.dot_general(a, b, (dims, ((), ())), precision=precision, preferred_element_type=F32)


def params(mib):
    return pltpu.CompilerParams(vmem_limit_bytes=mib * MIB)


def contract_kernel(
    step, ahead, snapshot_ref, mode2_ref, factor_ref, core_ref, projected_ref,
    slab_ref, wide_ref, even_ref, odd_ref, sems,
):
    cells, fibers, depth = snapshot_ref.shape
    rank = mode2_ref.shape[0]
    reps = LANES // rank
    chunks = cells // step
    flat = (even_ref, odd_ref)

    def copy(chunk):
        where = pl.ds(chunk * step, step)
        return pltpu.make_async_copy(snapshot_ref.at[where], slab_ref.at[where], sems.at[chunk])

    for chunk in range(ahead):
        copy(chunk).start()
    wide_ref[...] = jnp.concatenate([mode2_ref[...]] * reps, axis=0).T
    lane = lax.broadcasted_iota(jnp.int32, (step, LANES), 1)

    def multiply(chunk):
        x = slab_ref[pl.ds(chunk * step, step)].reshape(step * fibers, depth)
        flat[chunk % 2][...] = dot_f32(x, wide_ref[...], ((1,), (0,)))

    def spread(chunk):
        source = flat[chunk % 2]
        for block in range(fibers // reps):
            part = source[pl.ds(block * reps, step, stride=fibers), :]
            for r in range(1, reps):
                other = source[pl.ds(block * reps + r, step, stride=fibers), :]
                part = jnp.where(lane < r * rank, part, other)
            where = slice(block * LANES, (block + 1) * LANES)
            core_ref[pl.ds(chunk * step, step), where] = part.astype(BF16)

    for chunk in range(chunks):
        copy(chunk).wait()
        if chunk + ahead < chunks:
            copy(chunk + ahead).start()
        multiply(chunk)
        if chunk:
            spread(chunk - 1)
    spread(chunks - 1)

    total = dot_f32(factor_ref[...], core_ref[...], ((1,), (0,)))
    for block in range(total.shape[1] // LANES):
        where = slice(block * LANES, (block + 1) * LANES)
        projected_ref[pl.ds(block * rank, rank), :] = total[:, where].astype(BF16)


def contract(snapshot, mode2_t, factor_t):
    cells, fibers, depth = snapshot.shape
    rank = mode2_t.shape[0]
    step = 16
    width = fibers * rank
    return pl.pallas_call(
        functools.partial(contract_kernel, step, 3),
        in_specs=[
            pl.BlockSpec(memory_space=pltpu.HBM),
            pl.BlockSpec(memory_space=pltpu.VMEM),
            pl.BlockSpec(memory_space=pltpu.VMEM),
        ],
        out_shape=[
            jax.ShapeDtypeStruct((cells, width), BF16),
            jax.ShapeDtypeStruct((rank * width // LANES, LANES), BF16),
        ],
        scratch_shapes=[
            pltpu.VMEM(snapshot.shape, BF16),
            pltpu.VMEM((depth, LANES), BF16),
            pltpu.VMEM((step * fibers, LANES), F32),
            pltpu.VMEM((step * fibers, LANES), F32),
            pltpu.SemaphoreType.DMA((cells // step,)),
        ],
        compiler_params=params(57),
        name="contract",
    )(snapshot, mode2_t, factor_t)


def add_kernel(mine_ref, got_ref, out_ref):
    total = mine_ref[...].astype(F32) + got_ref[...].astype(F32)
    out_ref[...] = total.astype(out_ref.dtype)


def add(mine, got):
    return pl.pallas_call(
        add_kernel,
        out_shape=jax.ShapeDtypeStruct(got.shape, got.dtype),
        compiler_params=params(4),
        name="add",
    )(mine, got)


def halves_kernel(mine_ref, got_ref, low_ref, high_ref):
    half = low_ref.shape[0]
    for out, start in ((low_ref, 0), (high_ref, half)):
        rows = pl.ds(start, half)
        out[...] = (mine_ref[rows, :].astype(F32) + got_ref[rows, :].astype(F32)).astype(BF16)


def add_in_halves(mine, got):
    out = jax.ShapeDtypeStruct((mine.shape[0] // 2, LANES), BF16)
    return pl.pallas_call(
        halves_kernel, out_shape=[out, out], compiler_params=params(4), name="add_in_halves"
    )(mine, got)


def product_kernel(own_ref, got_ref, low_ref, high_ref, product_ref, gram_ref):
    cells, width = own_ref.shape
    blocks = width // LANES // 2
    rank = low_ref.shape[0] // blocks
    total = jnp.zeros((cells, rank), F32)
    for start, ref in ((0, low_ref), (blocks, high_ref)):
        for block in range(blocks):
            projected = ref[pl.ds(block * rank, rank), :]
            where = slice((start + block) * LANES, (start + block + 1) * LANES)
            total += dot_f32(own_ref[:, where], projected, ((1,), (1,)))
            total += dot_f32(got_ref[:, where], projected, ((1,), (1,)))
    half = cells // 2
    product_ref[...] = jnp.concatenate([total[:half], total[half:]], axis=1)
    gram = dot_f32(total, total, ((0,), (0,)), lax.Precision.HIGHEST)
    gram_ref[...] = jnp.concatenate([gram[:rank // 2], gram[rank // 2:]], axis=1)


def product_and_gram(own, got, low, high):
    return pl.pallas_call(
        product_kernel,
        out_shape=[
            jax.ShapeDtypeStruct((own.shape[0] // 2, LANES), F32),
            jax.ShapeDtypeStruct((LANES // 4, LANES), F32),
        ],
        compiler_params=params(8),
        name="product_and_gram",
    )(own, got, low, high)


def finish_kernel(total_rows, mine_ref, got_ref, gram_ref, got_gram_ref, out_ref):
    rank = LANES // 2
    hub = lax.axis_index("col") == 1
    packed = jnp.where(hub, gram_ref[...], got_gram_ref[...])
    gram = jnp.concatenate([packed[:, :rank], packed[:, rank:]], axis=0)
    eye = (
        lax.broadcasted_iota(jnp.int32, (rank, rank), 0)
        == lax.broadcasted_iota(jnp.int32, (rank, rank), 1)
    ).astype(F32)
    both = jnp.concatenate([gram, eye], axis=1)
    row_index = lax.broadcasted_iota(jnp.int32, (rank, 1), 0)
    pivots = jnp.zeros((rank, 1), F32)
    for k in range(rank):
        pivot = both[k:k + 1, k:k + 1]
        pivots = jnp.where(row_index == k, pivot, pivots)
        factor = jnp.where(row_index > k, both[:, k:k + 1] / pivot, 0.0)
        both = both - factor * both[k:k + 1, :]
    inverse = both[:, rank:] * (lax.rsqrt(pivots) * (total_rows ** 0.5))
    mine = jnp.where(hub, mine_ref[:, rank:], got_ref[:, :rank])
    out_ref[...] = dot_f32(mine, inverse, ((1,), (1,)), lax.Precision.HIGHEST)


def finish(total_rows, mine, got, gram, got_gram):
    return pl.pallas_call(
        functools.partial(finish_kernel, total_rows),
        out_shape=jax.ShapeDtypeStruct((mine.shape[0], LANES // 2), F32),
        compiler_params=params(4),
        name="finish",
    )(mine, got, gram, got_gram)


def per_device(snapshot, mode2_factor, old_factor):
    n_rows, n_cols = lax.axis_size("row"), lax.axis_size("col")
    masks = [1 << bit for bit in range(n_rows.bit_length() - 1)]
    total_rows = snapshot.shape[0] * n_rows

    def to_hub(x):
        return lax.ppermute(x, "col", [(0, 1)])

    def from_hub(x):
        return lax.ppermute(x, "col", [(1, 0)])

    def swap(x, mask):
        pairs = [(r * n_cols + 1, (r ^ mask) * n_cols + 1) for r in range(n_rows)]
        return lax.ppermute(x, ("row", "col"), pairs)

    core, projected = contract(snapshot, mode2_factor.T, old_factor.T)
    got_projected = to_hub(projected)
    got_core = to_hub(core)
    low, high = add_in_halves(projected, got_projected)
    for mask, turned in zip(masks, masks[1:] + masks[:1]):
        got_low, got_high = swap(low, mask), swap(high, turned)
        low, high = add(low, got_low), add(high, got_high)

    product, gram = product_and_gram(core, got_core, low, high)
    got_product = from_hub(product)
    for mask in masks:
        gram = add(gram, swap(gram, mask))
    return finish(total_rows, product, got_product, gram, from_hub(gram))


def solution(mesh):
    return jax.shard_map(
        per_device,
        mesh=mesh,
        in_specs=(
            P(("groups", "row"), None, "col"),
            P(("groups", "col"), None),
            P(("groups", "row"), None),
        ),
        out_specs=P(("groups", "row", "col"), None),
        check_vma=False,
    )
```

time: 53.7 us -> 63.7 us (1.19)
  waiting for transfers between devices: 17.4 us -> 31.3 us
  starting transfers between devices: 17.3 us -> 12.3 us
    ppermute x9 -> x13, waiting for transfers between devices: 17.4 us -> 31.3 us  [the longest x2 31.2 us: from_hub(): return lax.ppermute(x, 'col', [(1, 0)])]
    ppermute x9 -> x13, starting transfers between devices: 17.3 us -> 12.3 us  [the longest x9 6.05 us: swap(): return lax.ppermute(x, ('row', 'col'), pairs)]
    pallas_call x4 -> x3, Pallas kernels: 10.2 us -> 10.5 us  [the longest x1 9.7 us: contract(): pl.pallas_call(functools.partial(contract_kernel, step, 3), in_specs=[pl....]
    unnamed x6 -> x4, local copies, waits for them, and re-layouts: 1.9 us -> 1.98 us
  transfers between devices with their start and end apart: 9 -> 13, of which waited for: 9 -> 2; matrix products, arithmetic and copies ran while one was open for 0% -> 0% of each run, Pallas kernels for 0% -> 0%
where the time goes in v4:
time: 63.7 us; the launch traced here: 63.2 us
  waiting for transfers between devices  31.3 us (49%)
  Pallas kernels  17.3 us (27%)
  starting transfers between devices  12.3 us (19%)
  local copies, waits for them, and re-layouts  1.98 us (3%)
    ppermute x2, waiting for transfers between devices, from_hub(): return lax.ppermute(x, 'col', [(1, 0)])  31.2 us
    pallas_call x1, Pallas kernels, contract(): pl.pallas_call(functools.partial(contract_kernel, step, 3), in_specs=[pl....  9.7 us
    pallas_call x1, Pallas kernels, finish(): pl.pallas_call(functools.partial(finish_kernel, total_rows), out_shape=ja...  6.61 us
    ppermute x9, starting transfers between devices, swap(): return lax.ppermute(x, ('row', 'col'), pairs)  6.05 us
    ppermute x2, starting transfers between devices, to_hub(): return lax.ppermute(x, 'col', [(0, 1)])  3.69 us
    ppermute x2, starting transfers between devices, from_hub(): return lax.ppermute(x, 'col', [(1, 0)])  2.58 us
    unnamed x4, local copies, waits for them, and re-layouts  1.98 us
  transfers between devices with their start and end apart: 13, of which 2 were waited for; matrix products, arithmetic and copies ran while one was open for 0% of the time, Pallas kernels for 0%

profile of v4, /device:TPU:0, one launch (start us, length us, event | category | flops | bytes accessed | tf_op | source)
XLA Modules:
  0.0 63.2 jit_solution(3889336670345374062)
XLA Ops:
  0.0 9.7 %contract.1 = (bf16[128,2048]{1,0:T(8,128)(2,1)}, bf16[1024,128]{1,0:T(8,128)(2,1)}) custom-call(bf16[128,32,1024]{2,1,0:T(8,128)(2,1)} %snapshot_ref.1, bf16[64,1024]{1,0:T(8,128)(2,1)} %bitcast.2, bf16[64,128]{1,0:T(8,128)(2,1)} %bitcast.3), custom_call_target="tpu_custom_call" | custom-call | tf_op jit(solution)/shard_map/contract/pallas_call | solution.py:77
  9.7 2.4 %collective-permute-start.1 = (bf16[1024,128]{1,0:T(8,128)(2,1)}, bf16[1024,128]{1,0:T(8,128)(2,1)S(1)}, u32[]{:S(2)}, u32[]{:S(2)}) collective-permute-start(bf16[1024,128]{1,0:T(8,128)(2,1)} %get-tuple-element.12.mine_ref), channel_id=1, source_target_pairs={{0,1},{2,3},{4,5},{6,7},{8,9},{10,11},{12,13},{14,15},{16,17},{18,... | collective-permute-start | bytes 786440 | tf_op jit(solution)/shard_map/ppermute | solution.py:194
  12.1 1.3 %collective-permute-start = (bf16[128,2048]{1,0:T(8,128)(2,1)}, bf16[128,2048]{1,0:T(8,128)(2,1)S(1)}, u32[]{:S(2)}, u32[]{:S(2)}) collective-permute-start(bf16[128,2048]{1,0:T(8,128)(2,1)} %get-tuple-element.11.own_ref), channel_id=1, source_target_pairs={{0,1},{2,3},{4,5},{6,7},{8,9},{10,11},{12,13},{14,15},{16,17},{18,... | collective-permute-start | bytes 1572872 | tf_op jit(solution)/shard_map/ppermute | solution.py:194
  13.4 0.0 collective-permute-done.1.got_ref
  13.4 0.0 copy-start.1
  13.4 0.9 %copy-done.1 = bf16[1024,128]{1,0:T(8,128)(2,1)S(1)} copy-done((bf16[1024,128]{1,0:T(8,128)(2,1)S(1)}, bf16[1024,128]{1,0:T(8,128)(2,1)}, u32[]{:S(2)}) %copy-start.1) | copy-done | bytes 262168
  14.4 0.1 add_in_halves.1
  14.4 0.7 %collective-permute-start.2 = (bf16[512,128]{1,0:T(8,128)(2,1)S(1)}, bf16[512,128]{1,0:T(8,128)(2,1)S(1)}, u32[]{:S(2)}, u32[]{:S(2)}) collective-permute-start(bf16[512,128]{1,0:T(8,128)(2,1)S(1)} %get-tuple-element.13.mine_ref), channel_id=1, source_target_pairs={{1,3},{3,1},{5,7},{7,5},{9,11},{11,9},{13,15},{15,13},{17,19},{19,... | collective-permute-start | bytes 393224 | tf_op jit(solution)/shard_map/ppermute | solution.py:201
  15.1 0.7 %collective-permute-start.5 = (bf16[512,128]{1,0:T(8,128)(2,1)S(1)}, bf16[512,128]{1,0:T(8,128)(2,1)S(1)}, u32[]{:S(2)}, u32[]{:S(2)}) collective-permute-start(bf16[512,128]{1,0:T(8,128)(2,1)S(1)} %get-tuple-element.14.mine_ref), channel_id=1, source_target_pairs={{1,5},{3,7},{5,1},{7,3},{9,13},{11,15},{13,9},{15,11},{17,21},{19,... | collective-permute-start | bytes 393224 | tf_op jit(solution)/shard_map/ppermute | solution.py:201
  15.8 0.0 collective-permute-done.2.got_ref
  15.9 0.7 %collective-permute-start.3 = (bf16[512,128]{1,0:T(8,128)(2,1)S(1)}, bf16[512,128]{1,0:T(8,128)(2,1)S(1)}, u32[]{:S(2)}, u32[]{:S(2)}) collective-permute-start(bf16[512,128]{1,0:T(8,128)(2,1)S(1)} %add.9.mine_ref), channel_id=1, source_target_pairs={{1,5},{3,7},{5,1},{7,3},{9,13},{11,15},{13,9},{15,11},{17,21},{19,... | collective-permute-start | bytes 393224 | tf_op jit(solution)/shard_map/ppermute | solution.py:201
  16.5 0.0 collective-permute-done.5.got_ref
  16.6 0.7 %collective-permute-start.6 = (bf16[512,128]{1,0:T(8,128)(2,1)S(1)}, bf16[512,128]{1,0:T(8,128)(2,1)S(1)}, u32[]{:S(2)}, u32[]{:S(2)}) collective-permute-start(bf16[512,128]{1,0:T(8,128)(2,1)S(1)} %add.12.mine_ref), channel_id=1, source_target_pairs={{1,9},{3,11},{5,13},{7,15},{9,1},{11,3},{13,5},{15,7},{17,25},{19,... | collective-permute-start | bytes 393224 | tf_op jit(solution)/shard_map/ppermute | solution.py:201
  17.3 0.0 collective-permute-done.3.got_ref
  17.3 0.7 %collective-permute-start.4 = (bf16[512,128]{1,0:T(8,128)(2,1)S(1)}, bf16[512,128]{1,0:T(8,128)(2,1)S(1)}, u32[]{:S(2)}, u32[]{:S(2)}) collective-permute-start(bf16[512,128]{1,0:T(8,128)(2,1)S(1)} %add.10.mine_ref), channel_id=1, source_target_pairs={{1,9},{3,11},{5,13},{7,15},{9,1},{11,3},{13,5},{15,7},{17,25},{19,... | collective-permute-start | bytes 393224 | tf_op jit(solution)/shard_map/ppermute | solution.py:201
  18.0 0.0 collective-permute-done.6.got_ref
  18.0 0.7 %collective-permute-start.7 = (bf16[512,128]{1,0:T(8,128)(2,1)S(1)}, bf16[512,128]{1,0:T(8,128)(2,1)S(1)}, u32[]{:S(2)}, u32[]{:S(2)}) collective-permute-start(bf16[512,128]{1,0:T(8,128)(2,1)S(1)} %add.13.mine_ref), channel_id=1, source_target_pairs={{1,3},{3,1},{5,7},{7,5},{9,11},{11,9},{13,15},{15,13},{17,19},{19,... | collective-permute-start | bytes 393224 | tf_op jit(solution)/shard_map/ppermute | solution.py:201
  18.7 0.0 collective-permute-done.4.got_ref
  18.8 0.0 collective-permute-done.7.got_ref
  18.8 0.0 collective-permute-done.got_ref
  18.8 0.0 copy-start
  18.8 1.0 %copy-done = bf16[128,2048]{1,0:T(8,128)(2,1)S(1)} copy-done((bf16[128,2048]{1,0:T(8,128)(2,1)S(1)}, bf16[128,2048]{1,0:T(8,128)(2,1)}, u32[]{:S(2)}) %copy-start) | copy-done | bytes 524312
  19.9 0.7 %product_and_gram.1 = (f32[64,128]{1,0:T(8,128)S(1)}, f32[32,128]{1,0:T(8,128)S(1)}) custom-call(bf16[128,2048]{1,0:T(8,128)(2,1)S(1)} %copy-done, bf16[128,2048]{1,0:T(8,128)(2,1)S(1)} %collective-permute-done.got_ref, bf16[512,128]{1,0:T(8,128)(2,1)S(1)} %add.11.low_ref, bf16[512,128]{1,0:T(8,128)(2,1)S(1)} %add.14.high_ref), custom_call_target="tpu_custom_call" | custom-call | tf_op jit(solution)/shard_map/product_and_gram/pallas_call | solution.py:146
  20.6 0.7 %collective-permute-start.9 = (f32[32,128]{1,0:T(8,128)S(1)}, f32[32,128]{1,0:T(8,128)S(1)}, u32[]{:S(2)}, u32[]{:S(2)}) collective-permute-start(f32[32,128]{1,0:T(8,128)S(1)} %get-tuple-element.16.mine_ref), channel_id=1, source_target_pairs={{1,3},{3,1},{5,7},{7,5},{9,11},{11,9},{13,15},{15,13},{17,19},{19,... | collective-permute-start | bytes 49160 | tf_op jit(solution)/shard_map/ppermute | solution.py:201
  21.3 0.0 collective-permute-done.9.got_ref
  21.4 0.7 %collective-permute-start.10 = (f32[32,128]{1,0:T(8,128)S(1)}, f32[32,128]{1,0:T(8,128)S(1)}, u32[]{:S(2)}, u32[]{:S(2)}) collective-permute-start(f32[32,128]{1,0:T(8,128)S(1)} %add.15.mine_ref), channel_id=1, source_target_pairs={{1,5},{3,7},{5,1},{7,3},{9,13},{11,15},{13,9},{15,11},{17,21},{19,... | collective-permute-start | bytes 49160 | tf_op jit(solution)/shard_map/ppermute | solution.py:201
  22.0 0.0 collective-permute-done.10.got_ref
  22.1 0.7 %collective-permute-start.11 = (f32[32,128]{1,0:T(8,128)S(1)}, f32[32,128]{1,0:T(8,128)S(1)}, u32[]{:S(2)}, u32[]{:S(2)}) collective-permute-start(f32[32,128]{1,0:T(8,128)S(1)} %add.16.mine_ref), channel_id=1, source_target_pairs={{1,9},{3,11},{5,13},{7,15},{9,1},{11,3},{13,5},{15,7},{17,25},{19,... | collective-permute-start | bytes 49160 | tf_op jit(solution)/shard_map/ppermute | solution.py:201
  22.7 1.3 %collective-permute-start.8 = (f32[64,128]{1,0:T(8,128)S(1)}, f32[64,128]{1,0:T(8,128)S(1)}, u32[]{:S(2)}, u32[]{:S(2)}) collective-permute-start(f32[64,128]{1,0:T(8,128)S(1)} %get-tuple-element.15.mine_ref), channel_id=1, source_target_pairs={{1,0},{3,2},{5,4},{7,6},{9,8},{11,10},{13,12},{15,14},{17,16},{19,... | collective-permute-start | bytes 98312 | tf_op jit(solution)/shard_map/ppermute | solution.py:197
  24.0 0.0 collective-permute-done.11.got_ref
  24.1 1.3 %collective-permute-start.12 = (f32[32,128]{1,0:T(8,128)S(1)}, f32[32,128]{1,0:T(8,128)S(1)}, u32[]{:S(2)}, u32[]{:S(2)}) collective-permute-start(f32[32,128]{1,0:T(8,128)S(1)} %add.17.gram_ref), channel_id=1, source_target_pairs={{1,0},{3,2},{5,4},{7,6},{9,8},{11,10},{13,12},{15,14},{17,16},{19,... | collective-permute-start | bytes 49160 | tf_op jit(solution)/shard_map/ppermute | solution.py:197
  25.4 29.8 %collective-permute-done.8.got_ref = f32[64,128]{1,0:T(8,128)S(1)} collective-permute-done((f32[64,128]{1,0:T(8,128)S(1)}, f32[64,128]{1,0:T(8,128)S(1)}, u32[]{:S(2)}, u32[]{:S(2)}) %collective-permute-start.8) | collective-permute-done | bytes 32800 | tf_op jit(solution)/shard_map/ppermute | solution.py:197
  55.2 1.4 %collective-permute-done.12.got_gram_ref = f32[32,128]{1,0:T(8,128)S(1)} collective-permute-done((f32[32,128]{1,0:T(8,128)S(1)}, f32[32,128]{1,0:T(8,128)S(1)}, u32[]{:S(2)}, u32[]{:S(2)}) %collective-permute-start.12) | collective-permute-done | bytes 16416 | tf_op jit(solution)/shard_map/ppermute | solution.py:197
  56.6 6.6 %finish.1 = f32[64,64]{1,0:T(8,128)} custom-call(f32[64,128]{1,0:T(8,128)S(1)} %get-tuple-element.15.mine_ref, f32[64,128]{1,0:T(8,128)S(1)} %collective-permute-done.8.got_ref, f32[32,128]{1,0:T(8,128)S(1)} %add.17.gram_ref, f32[32,128]{1,0:T(8,128)S(1)} %collective-permute-done.12.got_gram_ref), custom_call_target="tpu_custom_call" | custom-call | tf_op jit(solution)/shard_map/finish/pallas_call | solution.py:180
  (9 shorter events, 0.2 us)
Async XLA Ops:
  9.7 3.7 %collective-permute-start.1 = (bf16[1024,128]{1,0:T(8,128)(2,1)}, bf16[1024,128]{1,0:T(8,128)(2,1)S(1)}, u32[]{:S(2)}, u32[]{:S(2)}) collective-permute-start(bf16[1024,128]{1,0:T(8,128)(2,1)} %get-tuple-element.12.mine_ref), channel_id=1, source_target_pairs={{0,1},{2,3},{4,5},{6,7},{8,9},{10,11},{12,13},{14,15},{16,17},{18,... | collective-permute-start | bytes 786440 | tf_op jit(solution)/shard_map/ppermute | solution.py:194
  12.1 6.7 %collective-permute-start = (bf16[128,2048]{1,0:T(8,128)(2,1)}, bf16[128,2048]{1,0:T(8,128)(2,1)S(1)}, u32[]{:S(2)}, u32[]{:S(2)}) collective-permute-start(bf16[128,2048]{1,0:T(8,128)(2,1)} %get-tuple-element.11.own_ref), channel_id=1, source_target_pairs={{0,1},{2,3},{4,5},{6,7},{8,9},{10,11},{12,13},{14,15},{16,17},{18,... | collective-permute-start | bytes 1572872 | tf_op jit(solution)/shard_map/ppermute | solution.py:194
  13.4 1.0 %copy-start.1 = (bf16[1024,128]{1,0:T(8,128)(2,1)S(1)}, bf16[1024,128]{1,0:T(8,128)(2,1)}, u32[]{:S(2)}) copy-start(bf16[1024,128]{1,0:T(8,128)(2,1)} %get-tuple-element.12.mine_ref) | copy-start | bytes 786436
  14.4 1.4 %collective-permute-start.2 = (bf16[512,128]{1,0:T(8,128)(2,1)S(1)}, bf16[512,128]{1,0:T(8,128)(2,1)S(1)}, u32[]{:S(2)}, u32[]{:S(2)}) collective-permute-start(bf16[512,128]{1,0:T(8,128)(2,1)S(1)} %get-tuple-element.13.mine_ref), channel_id=1, source_target_pairs={{1,3},{3,1},{5,7},{7,5},{9,11},{11,9},{13,15},{15,13},{17,19},{19,... | collective-permute-start | bytes 393224 | tf_op jit(solution)/shard_map/ppermute | solution.py:201
  15.1 1.4 %collective-permute-start.5 = (bf16[512,128]{1,0:T(8,128)(2,1)S(1)}, bf16[512,128]{1,0:T(8,128)(2,1)S(1)}, u32[]{:S(2)}, u32[]{:S(2)}) collective-permute-start(bf16[512,128]{1,0:T(8,128)(2,1)S(1)} %get-tuple-element.14.mine_ref), channel_id=1, source_target_pairs={{1,5},{3,7},{5,1},{7,3},{9,13},{11,15},{13,9},{15,11},{17,21},{19,... | collective-permute-start | bytes 393224 | tf_op jit(solution)/shard_map/ppermute | solution.py:201
  15.9 1.4 %collective-permute-start.3 = (bf16[512,128]{1,0:T(8,128)(2,1)S(1)}, bf16[512,128]{1,0:T(8,128)(2,1)S(1)}, u32[]{:S(2)}, u32[]{:S(2)}) collective-permute-start(bf16[512,128]{1,0:T(8,128)(2,1)S(1)} %add.9.mine_ref), channel_id=1, source_target_pairs={{1,5},{3,7},{5,1},{7,3},{9,13},{11,15},{13,9},{15,11},{17,21},{19,... | collective-permute-start | bytes 393224 | tf_op jit(solution)/shard_map/ppermute | solution.py:201
  16.6 1.4 %collective-permute-start.6 = (bf16[512,128]{1,0:T(8,128)(2,1)S(1)}, bf16[512,128]{1,0:T(8,128)(2,1)S(1)}, u32[]{:S(2)}, u32[]{:S(2)}) collective-permute-start(bf16[512,128]{1,0:T(8,128)(2,1)S(1)} %add.12.mine_ref), channel_id=1, source_target_pairs={{1,9},{3,11},{5,13},{7,15},{9,1},{11,3},{13,5},{15,7},{17,25},{19,... | collective-permute-start | bytes 393224 | tf_op jit(solution)/shard_map/ppermute | solution.py:201
  17.3 1.4 %collective-permute-start.4 = (bf16[512,128]{1,0:T(8,128)(2,1)S(1)}, bf16[512,128]{1,0:T(8,128)(2,1)S(1)}, u32[]{:S(2)}, u32[]{:S(2)}) collective-permute-start(bf16[512,128]{1,0:T(8,128)(2,1)S(1)} %add.10.mine_ref), channel_id=1, source_target_pairs={{1,9},{3,11},{5,13},{7,15},{9,1},{11,3},{13,5},{15,7},{17,25},{19,... | collective-permute-start | bytes 393224 | tf_op jit(solution)/shard_map/ppermute | solution.py:201
  18.0 0.7 %collective-permute-start.7 = (bf16[512,128]{1,0:T(8,128)(2,1)S(1)}, bf16[512,128]{1,0:T(8,128)(2,1)S(1)}, u32[]{:S(2)}, u32[]{:S(2)}) collective-permute-start(bf16[512,128]{1,0:T(8,128)(2,1)S(1)} %add.13.mine_ref), channel_id=1, source_target_pairs={{1,3},{3,1},{5,7},{7,5},{9,11},{11,9},{13,15},{15,13},{17,19},{19,... | collective-permute-start | bytes 393224 | tf_op jit(solution)/shard_map/ppermute | solution.py:201
  18.8 1.0 %copy-start = (bf16[128,2048]{1,0:T(8,128)(2,1)S(1)}, bf16[128,2048]{1,0:T(8,128)(2,1)}, u32[]{:S(2)}) copy-start(bf16[128,2048]{1,0:T(8,128)(2,1)} %get-tuple-element.11.own_ref) | copy-start | bytes 1572868
  20.6 0.7 %collective-permute-start.9 = (f32[32,128]{1,0:T(8,128)S(1)}, f32[32,128]{1,0:T(8,128)S(1)}, u32[]{:S(2)}, u32[]{:S(2)}) collective-permute-start(f32[32,128]{1,0:T(8,128)S(1)} %get-tuple-element.16.mine_ref), channel_id=1, source_target_pairs={{1,3},{3,1},{5,7},{7,5},{9,11},{11,9},{13,15},{15,13},{17,19},{19,... | collective-permute-start | bytes 49160 | tf_op jit(solution)/shard_map/ppermute | solution.py:201
  21.4 0.7 %collective-permute-start.10 = (f32[32,128]{1,0:T(8,128)S(1)}, f32[32,128]{1,0:T(8,128)S(1)}, u32[]{:S(2)}, u32[]{:S(2)}) collective-permute-start(f32[32,128]{1,0:T(8,128)S(1)} %add.15.mine_ref), channel_id=1, source_target_pairs={{1,5},{3,7},{5,1},{7,3},{9,13},{11,15},{13,9},{15,11},{17,21},{19,... | collective-permute-start | bytes 49160 | tf_op jit(solution)/shard_map/ppermute | solution.py:201
  22.1 2.0 %collective-permute-start.11 = (f32[32,128]{1,0:T(8,128)S(1)}, f32[32,128]{1,0:T(8,128)S(1)}, u32[]{:S(2)}, u32[]{:S(2)}) collective-permute-start(f32[32,128]{1,0:T(8,128)S(1)} %add.16.mine_ref), channel_id=1, source_target_pairs={{1,9},{3,11},{5,13},{7,15},{9,1},{11,3},{13,5},{15,7},{17,25},{19,... | collective-permute-start | bytes 49160 | tf_op jit(solution)/shard_map/ppermute | solution.py:201
  22.7 32.5 %collective-permute-start.8 = (f32[64,128]{1,0:T(8,128)S(1)}, f32[64,128]{1,0:T(8,128)S(1)}, u32[]{:S(2)}, u32[]{:S(2)}) collective-permute-start(f32[64,128]{1,0:T(8,128)S(1)} %get-tuple-element.15.mine_ref), channel_id=1, source_target_pairs={{1,0},{3,2},{5,4},{7,6},{9,8},{11,10},{13,12},{15,14},{17,16},{19,... | collective-permute-start | bytes 98312 | tf_op jit(solution)/shard_map/ppermute | solution.py:197
  24.1 32.5 %collective-permute-start.12 = (f32[32,128]{1,0:T(8,128)S(1)}, f32[32,128]{1,0:T(8,128)S(1)}, u32[]{:S(2)}, u32[]{:S(2)}) collective-permute-start(f32[32,128]{1,0:T(8,128)S(1)} %add.17.gram_ref), channel_id=1, source_target_pairs={{1,0},{3,2},{5,4},{7,6},{9,8},{11,10},{13,12},{15,14},{17,16},{19,... | collective-permute-start | bytes 49160 | tf_op jit(solution)/shard_map/ppermute | solution.py:197

commit v5 on v4

--- a/solution.py
+++ b/solution.py
@@ -29,7 +29,6 @@
     rank = mode2_ref.shape[0]
     reps = LANES // rank
     chunks = cells // step
-    flat = (even_ref, odd_ref)
 
     def copy(chunk):
         where = pl.ds(chunk * step, step)
@@ -40,28 +39,34 @@
     wide_ref[...] = jnp.concatenate([mode2_ref[...]] * reps, axis=0).T
     lane = lax.broadcasted_iota(jnp.int32, (step, LANES), 1)
 
-    def multiply(chunk):
+    def multiply(chunk, flat_ref):
+        copy(chunk).wait()
+
+        @pl.when(chunk + ahead < chunks)
+        def _():
+            copy(chunk + ahead).start()
+
         x = slab_ref[pl.ds(chunk * step, step)].reshape(step * fibers, depth)
-        flat[chunk % 2][...] = dot_f32(x, wide_ref[...], ((1,), (0,)))
-
-    def spread(chunk):
-        source = flat[chunk % 2]
+        flat_ref[...] = dot_f32(x, wide_ref[...], ((1,), (0,)))
+
+    def spread(chunk, flat_ref):
+        rows = pl.ds(pl.multiple_of(chunk * step, step), step)
         for block in range(fibers // reps):
-            part = source[pl.ds(block * reps, step, stride=fibers), :]
+            part = flat_ref[pl.ds(block * reps, step, stride=fibers), :]
             for r in range(1, reps):
-                other = source[pl.ds(block * reps + r, step, stride=fibers), :]
+                other = flat_ref[pl.ds(block * reps + r, step, stride=fibers), :]
                 part = jnp.where(lane < r * rank, part, other)
-            where = slice(block * LANES, (block + 1) * LANES)
-            core_ref[pl.ds(chunk * step, step), where] = part.astype(BF16)
-
-    for chunk in range(chunks):
-        copy(chunk).wait()
-        if chunk + ahead < chunks:
-            copy(chunk + ahead).start()
-        multiply(chunk)
-        if chunk:
-            spread(chunk - 1)
-    spread(chunks - 1)
+            core_ref[rows, block * LANES:(block + 1) * LANES] = part.astype(BF16)
+
+    def two_chunks(pair, _):
+        multiply(2 * pair, even_ref)
+        spread(jnp.maximum(2 * pair - 1, 0), odd_ref)
+        multiply(2 * pair + 1, odd_ref)
+        spread(2 * pair, even_ref)
+        return _
+
+    lax.fori_loop(0, chunks // 2, two_chunks, 0)
+    spread(chunks - 1, odd_ref)
 
     total = dot_f32(factor_ref[...], core_ref[...], ((1,), (0,)))
     for block in range(total.shape[1] // LANES):
@@ -190,29 +195,30 @@
     masks = [1 << bit for bit in range(n_rows.bit_length() - 1)]
     total_rows = snapshot.shape[0] * n_rows
 
-    def to_hub(x):
-        return lax.ppermute(x, "col", [(0, 1)])
-
-    def from_hub(x):
-        return lax.ppermute(x, "col", [(1, 0)])
+    def in_chip(x):
+        return lax.ppermute(x, "col", [(c, (c + 1) % n_cols) for c in range(n_cols)])
 
     def swap(x, mask):
-        pairs = [(r * n_cols + 1, (r ^ mask) * n_cols + 1) for r in range(n_rows)]
+        pairs = [
+            (r * n_cols + c, (r ^ (mask if c else 0)) * n_cols + c)
+            for r in range(n_rows)
+            for c in range(n_cols)
+        ]
         return lax.ppermute(x, ("row", "col"), pairs)
 
     core, projected = contract(snapshot, mode2_factor.T, old_factor.T)
-    got_projected = to_hub(projected)
-    got_core = to_hub(core)
+    got_projected = in_chip(projected)
+    got_core = in_chip(core)
     low, high = add_in_halves(projected, got_projected)
     for mask, turned in zip(masks, masks[1:] + masks[:1]):
         got_low, got_high = swap(low, mask), swap(high, turned)
         low, high = add(low, got_low), add(high, got_high)
 
     product, gram = product_and_gram(core, got_core, low, high)
-    got_product = from_hub(product)
+    got_product = in_chip(product)
     for mask in masks:
         gram = add(gram, swap(gram, mask))
-    return finish(total_rows, product, got_product, gram, from_hub(gram))
+    return finish(total_rows, product, got_product, gram, in_chip(gram))
 
 
 def solution(mesh):

time: 63.7 us -> 61.2 us (0.961)
  waiting for transfers between devices: 31.3 us -> 2.16 us
  starting transfers between devices: 12.3 us -> 38.9 us
    ppermute x4, waiting for transfers between devices: 31.3 us -> 2.14 us  [in_chip(): lax.ppermute(x, 'col', [(c, (c + 1) % n_cols) for c in range(n_cols)])]
    ppermute x4, starting transfers between devices: 6.28 us -> 32.8 us  [in_chip(): lax.ppermute(x, 'col', [(c, (c + 1) % n_cols) for c in range(n_cols)])]
where the time goes in v5:
time: 61.2 us; the launch traced here: 60.8 us
  starting transfers between devices  38.9 us (64%)
  Pallas kernels  17.5 us (29%)
  waiting for transfers between devices  2.16 us (4%)
  local copies, waits for them, and re-layouts  1.98 us (3%)
    ppermute x4, starting transfers between devices, in_chip(): lax.ppermute(x, 'col', [(c, (c + 1) % n_cols) for c in range(n_cols)])  32.8 us
    pallas_call x1, Pallas kernels, contract(): pl.pallas_call(functools.partial(contract_kernel, step, 3), in_specs=[pl....  9.9 us
    pallas_call x1, Pallas kernels, finish(): pl.pallas_call(functools.partial(finish_kernel, total_rows), out_shape=ja...  6.61 us
    ppermute x9, starting transfers between devices, swap(): return lax.ppermute(x, ('row', 'col'), pairs)  6.05 us
    ppermute x4, waiting for transfers between devices, in_chip(): lax.ppermute(x, 'col', [(c, (c + 1) % n_cols) for c in range(n_cols)])  2.14 us
    unnamed x4, local copies, waits for them, and re-layouts  1.98 us
  transfers between devices with their start and end apart: 13, of which 2 were waited for; matrix products, arithmetic and copies ran while one was open for 0% of the time, Pallas kernels for 0%

profile of v5, /device:TPU:0, one launch (start us, length us, event | category | flops | bytes accessed | tf_op | source)
XLA Modules:
  0.0 60.8 jit_solution(10652782868816192719)
XLA Ops:
  0.0 9.9 %contract.1 = (bf16[128,2048]{1,0:T(8,128)(2,1)}, bf16[1024,128]{1,0:T(8,128)(2,1)}) custom-call(bf16[128,32,1024]{2,1,0:T(8,128)(2,1)} %snapshot_ref.1, bf16[64,1024]{1,0:T(8,128)(2,1)} %bitcast.2, bf16[64,128]{1,0:T(8,128)(2,1)} %bitcast.3), custom_call_target="tpu_custom_call" | custom-call | tf_op jit(solution)/shard_map/contract/pallas_call | solution.py:82
  9.9 0.5 collective-permute-start.1
  10.4 0.1 collective-permute-start
  10.5 1.3 %collective-permute-done.1.got_ref = bf16[1024,128]{1,0:T(8,128)(2,1)S(1)} collective-permute-done((bf16[1024,128]{1,0:T(8,128)(2,1)}, bf16[1024,128]{1,0:T(8,128)(2,1)S(1)}, u32[]{:S(2)}, u32[]{:S(2)}) %collective-permute-start.1) | collective-permute-done | bytes 262176 | tf_op jit(solution)/shard_map/ppermute | solution.py:199
  11.8 0.0 copy-start.1
  11.8 0.9 %copy-done.1 = bf16[1024,128]{1,0:T(8,128)(2,1)S(1)} copy-done((bf16[1024,128]{1,0:T(8,128)(2,1)S(1)}, bf16[1024,128]{1,0:T(8,128)(2,1)}, u32[]{:S(2)}) %copy-start.1) | copy-done | bytes 262168
  12.7 0.1 add_in_halves.1
  12.8 0.7 %collective-permute-start.2 = (bf16[512,128]{1,0:T(8,128)(2,1)S(1)}, bf16[512,128]{1,0:T(8,128)(2,1)S(1)}, u32[]{:S(2)}, u32[]{:S(2)}) collective-permute-start(bf16[512,128]{1,0:T(8,128)(2,1)S(1)} %get-tuple-element.13.mine_ref), channel_id=1, source_target_pairs={{0,0},{1,3},{2,2},{3,1},{4,4},{5,7},{6,6},{7,5},{8,8},{9,11},{10,1... | collective-permute-start | bytes 393224 | tf_op jit(solution)/shard_map/ppermute | solution.py:207
  13.5 0.7 %collective-permute-start.5 = (bf16[512,128]{1,0:T(8,128)(2,1)S(1)}, bf16[512,128]{1,0:T(8,128)(2,1)S(1)}, u32[]{:S(2)}, u32[]{:S(2)}) collective-permute-start(bf16[512,128]{1,0:T(8,128)(2,1)S(1)} %get-tuple-element.14.mine_ref), channel_id=1, source_target_pairs={{0,0},{1,5},{2,2},{3,7},{4,4},{5,1},{6,6},{7,3},{8,8},{9,13},{10,1... | collective-permute-start | bytes 393224 | tf_op jit(solution)/shard_map/ppermute | solution.py:207
  14.2 0.0 collective-permute-done.2.got_ref
  14.2 0.7 %collective-permute-start.3 = (bf16[512,128]{1,0:T(8,128)(2,1)S(1)}, bf16[512,128]{1,0:T(8,128)(2,1)S(1)}, u32[]{:S(2)}, u32[]{:S(2)}) collective-permute-start(bf16[512,128]{1,0:T(8,128)(2,1)S(1)} %add.9.mine_ref), channel_id=1, source_target_pairs={{0,0},{1,5},{2,2},{3,7},{4,4},{5,1},{6,6},{7,3},{8,8},{9,13},{10,1... | collective-permute-start | bytes 393224 | tf_op jit(solution)/shard_map/ppermute | solution.py:207
  14.9 0.0 collective-permute-done.5.got_ref
  14.9 0.7 %collective-permute-start.6 = (bf16[512,128]{1,0:T(8,128)(2,1)S(1)}, bf16[512,128]{1,0:T(8,128)(2,1)S(1)}, u32[]{:S(2)}, u32[]{:S(2)}) collective-permute-start(bf16[512,128]{1,0:T(8,128)(2,1)S(1)} %add.12.mine_ref), channel_id=1, source_target_pairs={{0,0},{1,9},{2,2},{3,11},{4,4},{5,13},{6,6},{7,15},{8,8},{9,1},{10... | collective-permute-start | bytes 393224 | tf_op jit(solution)/shard_map/ppermute | solution.py:207
  15.6 0.0 collective-permute-done.3.got_ref
  15.7 0.7 %collective-permute-start.4 = (bf16[512,128]{1,0:T(8,128)(2,1)S(1)}, bf16[512,128]{1,0:T(8,128)(2,1)S(1)}, u32[]{:S(2)}, u32[]{:S(2)}) collective-permute-start(bf16[512,128]{1,0:T(8,128)(2,1)S(1)} %add.10.mine_ref), channel_id=1, source_target_pairs={{0,0},{1,9},{2,2},{3,11},{4,4},{5,13},{6,6},{7,15},{8,8},{9,1},{10... | collective-permute-start | bytes 393224 | tf_op jit(solution)/shard_map/ppermute | solution.py:207
  16.4 0.0 collective-permute-done.6.got_ref
  16.4 0.7 %collective-permute-start.7 = (bf16[512,128]{1,0:T(8,128)(2,1)S(1)}, bf16[512,128]{1,0:T(8,128)(2,1)S(1)}, u32[]{:S(2)}, u32[]{:S(2)}) collective-permute-start(bf16[512,128]{1,0:T(8,128)(2,1)S(1)} %add.13.mine_ref), channel_id=1, source_target_pairs={{0,0},{1,3},{2,2},{3,1},{4,4},{5,7},{6,6},{7,5},{8,8},{9,11},{10,1... | collective-permute-start | bytes 393224 | tf_op jit(solution)/shard_map/ppermute | solution.py:207
  17.1 0.0 collective-permute-done.4.got_ref
  17.1 0.0 collective-permute-done.7.got_ref
  17.2 0.0 collective-permute-done.got_ref
  17.2 0.0 copy-start
  17.2 1.0 %copy-done = bf16[128,2048]{1,0:T(8,128)(2,1)S(1)} copy-done((bf16[128,2048]{1,0:T(8,128)(2,1)S(1)}, bf16[128,2048]{1,0:T(8,128)(2,1)}, u32[]{:S(2)}) %copy-start) | copy-done | bytes 524312
  18.2 0.7 %product_and_gram.1 = (f32[64,128]{1,0:T(8,128)S(1)}, f32[32,128]{1,0:T(8,128)S(1)}) custom-call(bf16[128,2048]{1,0:T(8,128)(2,1)S(1)} %copy-done, bf16[128,2048]{1,0:T(8,128)(2,1)S(1)} %collective-permute-done.got_ref, bf16[512,128]{1,0:T(8,128)(2,1)S(1)} %add.11.low_ref, bf16[512,128]{1,0:T(8,128)(2,1)S(1)} %add.14.high_ref), custom_call_target="tpu_custom_call" | custom-call | tf_op jit(solution)/shard_map/product_and_gram/pallas_call | solution.py:151
  19.0 0.7 %collective-permute-start.9 = (f32[32,128]{1,0:T(8,128)S(1)}, f32[32,128]{1,0:T(8,128)S(1)}, u32[]{:S(2)}, u32[]{:S(2)}) collective-permute-start(f32[32,128]{1,0:T(8,128)S(1)} %get-tuple-element.16.mine_ref), channel_id=1, source_target_pairs={{0,0},{1,3},{2,2},{3,1},{4,4},{5,7},{6,6},{7,5},{8,8},{9,11},{10,1... | collective-permute-start | bytes 49160 | tf_op jit(solution)/shard_map/ppermute | solution.py:207
  19.7 0.0 collective-permute-done.9.got_ref
  19.7 0.7 %collective-permute-start.10 = (f32[32,128]{1,0:T(8,128)S(1)}, f32[32,128]{1,0:T(8,128)S(1)}, u32[]{:S(2)}, u32[]{:S(2)}) collective-permute-start(f32[32,128]{1,0:T(8,128)S(1)} %add.15.mine_ref), channel_id=1, source_target_pairs={{0,0},{1,5},{2,2},{3,7},{4,4},{5,1},{6,6},{7,3},{8,8},{9,13},{10,1... | collective-permute-start | bytes 49160 | tf_op jit(solution)/shard_map/ppermute | solution.py:207
  20.4 0.0 collective-permute-done.10.got_ref
  20.4 0.7 %collective-permute-start.11 = (f32[32,128]{1,0:T(8,128)S(1)}, f32[32,128]{1,0:T(8,128)S(1)}, u32[]{:S(2)}, u32[]{:S(2)}) collective-permute-start(f32[32,128]{1,0:T(8,128)S(1)} %add.16.mine_ref), channel_id=1, source_target_pairs={{0,0},{1,9},{2,2},{3,11},{4,4},{5,13},{6,6},{7,15},{8,8},{9,1},{10... | collective-permute-start | bytes 49160 | tf_op jit(solution)/shard_map/ppermute | solution.py:207
  21.1 30.9 %collective-permute-start.8 = (f32[64,128]{1,0:T(8,128)S(1)}, f32[64,128]{1,0:T(8,128)S(1)}, u32[]{:S(2)}, u32[]{:S(2)}) collective-permute-start(f32[64,128]{1,0:T(8,128)S(1)} %get-tuple-element.15.mine_ref), channel_id=1, source_target_pairs={{0,1},{1,0},{2,3},{3,2},{4,5},{5,4},{6,7},{7,6},{8,9},{9,8},{10,11... | collective-permute-start | bytes 98312 | tf_op jit(solution)/shard_map/ppermute | solution.py:199
  52.0 0.0 collective-permute-done.11.got_ref
  52.0 1.4 %collective-permute-start.12 = (f32[32,128]{1,0:T(8,128)S(1)}, f32[32,128]{1,0:T(8,128)S(1)}, u32[]{:S(2)}, u32[]{:S(2)}) collective-permute-start(f32[32,128]{1,0:T(8,128)S(1)} %add.17.gram_ref), channel_id=1, source_target_pairs={{0,1},{1,0},{2,3},{3,2},{4,5},{5,4},{6,7},{7,6},{8,9},{9,8},{10,11... | collective-permute-start | bytes 49160 | tf_op jit(solution)/shard_map/ppermute | solution.py:199
  53.3 0.0 collective-permute-done.8.got_ref
  53.3 0.8 %collective-permute-done.12.got_gram_ref = f32[32,128]{1,0:T(8,128)S(1)} collective-permute-done((f32[32,128]{1,0:T(8,128)S(1)}, f32[32,128]{1,0:T(8,128)S(1)}, u32[]{:S(2)}, u32[]{:S(2)}) %collective-permute-start.12) | collective-permute-done | bytes 16416 | tf_op jit(solution)/shard_map/ppermute | solution.py:199
  54.2 6.6 %finish.1 = f32[64,64]{1,0:T(8,128)} custom-call(f32[64,128]{1,0:T(8,128)S(1)} %get-tuple-element.15.mine_ref, f32[64,128]{1,0:T(8,128)S(1)} %collective-permute-done.8.got_ref, f32[32,128]{1,0:T(8,128)S(1)} %add.17.gram_ref, f32[32,128]{1,0:T(8,128)S(1)} %collective-permute-done.12.got_gram_ref), custom_call_target="tpu_custom_call" | custom-call | tf_op jit(solution)/shard_map/finish/pallas_call | solution.py:185
  (9 shorter events, 0.2 us)
Async XLA Ops:
  9.9 1.9 %collective-permute-start.1 = (bf16[1024,128]{1,0:T(8,128)(2,1)}, bf16[1024,128]{1,0:T(8,128)(2,1)S(1)}, u32[]{:S(2)}, u32[]{:S(2)}) collective-permute-start(bf16[1024,128]{1,0:T(8,128)(2,1)} %get-tuple-element.12.mine_ref), channel_id=1, source_target_pairs={{0,1},{1,0},{2,3},{3,2},{4,5},{5,4},{6,7},{7,6},{8,9},{9,8},{10,11... | collective-permute-start | bytes 786440 | tf_op jit(solution)/shard_map/ppermute | solution.py:199
  10.4 6.8 %collective-permute-start = (bf16[128,2048]{1,0:T(8,128)(2,1)}, bf16[128,2048]{1,0:T(8,128)(2,1)S(1)}, u32[]{:S(2)}, u32[]{:S(2)}) collective-permute-start(bf16[128,2048]{1,0:T(8,128)(2,1)} %get-tuple-element.11.own_ref), channel_id=1, source_target_pairs={{0,1},{1,0},{2,3},{3,2},{4,5},{5,4},{6,7},{7,6},{8,9},{9,8},{10,11... | collective-permute-start | bytes 1572872 | tf_op jit(solution)/shard_map/ppermute | solution.py:199
  11.8 0.9 %copy-start.1 = (bf16[1024,128]{1,0:T(8,128)(2,1)S(1)}, bf16[1024,128]{1,0:T(8,128)(2,1)}, u32[]{:S(2)}) copy-start(bf16[1024,128]{1,0:T(8,128)(2,1)} %get-tuple-element.12.mine_ref) | copy-start | bytes 786436
  12.8 1.4 %collective-permute-start.2 = (bf16[512,128]{1,0:T(8,128)(2,1)S(1)}, bf16[512,128]{1,0:T(8,128)(2,1)S(1)}, u32[]{:S(2)}, u32[]{:S(2)}) collective-permute-start(bf16[512,128]{1,0:T(8,128)(2,1)S(1)} %get-tuple-element.13.mine_ref), channel_id=1, source_target_pairs={{0,0},{1,3},{2,2},{3,1},{4,4},{5,7},{6,6},{7,5},{8,8},{9,11},{10,1... | collective-permute-start | bytes 393224 | tf_op jit(solution)/shard_map/ppermute | solution.py:207
  13.5 1.4 %collective-permute-start.5 = (bf16[512,128]{1,0:T(8,128)(2,1)S(1)}, bf16[512,128]{1,0:T(8,128)(2,1)S(1)}, u32[]{:S(2)}, u32[]{:S(2)}) collective-permute-start(bf16[512,128]{1,0:T(8,128)(2,1)S(1)} %get-tuple-element.14.mine_ref), channel_id=1, source_target_pairs={{0,0},{1,5},{2,2},{3,7},{4,4},{5,1},{6,6},{7,3},{8,8},{9,13},{10,1... | collective-permute-start | bytes 393224 | tf_op jit(solution)/shard_map/ppermute | solution.py:207
  14.2 1.4 %collective-permute-start.3 = (bf16[512,128]{1,0:T(8,128)(2,1)S(1)}, bf16[512,128]{1,0:T(8,128)(2,1)S(1)}, u32[]{:S(2)}, u32[]{:S(2)}) collective-permute-start(bf16[512,128]{1,0:T(8,128)(2,1)S(1)} %add.9.mine_ref), channel_id=1, source_target_pairs={{0,0},{1,5},{2,2},{3,7},{4,4},{5,1},{6,6},{7,3},{8,8},{9,13},{10,1... | collective-permute-start | bytes 393224 | tf_op jit(solution)/shard_map/ppermute | solution.py:207
  14.9 1.4 %collective-permute-start.6 = (bf16[512,128]{1,0:T(8,128)(2,1)S(1)}, bf16[512,128]{1,0:T(8,128)(2,1)S(1)}, u32[]{:S(2)}, u32[]{:S(2)}) collective-permute-start(bf16[512,128]{1,0:T(8,128)(2,1)S(1)} %add.12.mine_ref), channel_id=1, source_target_pairs={{0,0},{1,9},{2,2},{3,11},{4,4},{5,13},{6,6},{7,15},{8,8},{9,1},{10... | collective-permute-start | bytes 393224 | tf_op jit(solution)/shard_map/ppermute | solution.py:207
  15.7 1.4 %collective-permute-start.4 = (bf16[512,128]{1,0:T(8,128)(2,1)S(1)}, bf16[512,128]{1,0:T(8,128)(2,1)S(1)}, u32[]{:S(2)}, u32[]{:S(2)}) collective-permute-start(bf16[512,128]{1,0:T(8,128)(2,1)S(1)} %add.10.mine_ref), channel_id=1, source_target_pairs={{0,0},{1,9},{2,2},{3,11},{4,4},{5,13},{6,6},{7,15},{8,8},{9,1},{10... | collective-permute-start | bytes 393224 | tf_op jit(solution)/shard_map/ppermute | solution.py:207
  16.4 0.7 %collective-permute-start.7 = (bf16[512,128]{1,0:T(8,128)(2,1)S(1)}, bf16[512,128]{1,0:T(8,128)(2,1)S(1)}, u32[]{:S(2)}, u32[]{:S(2)}) collective-permute-start(bf16[512,128]{1,0:T(8,128)(2,1)S(1)} %add.13.mine_ref), channel_id=1, source_target_pairs={{0,0},{1,3},{2,2},{3,1},{4,4},{5,7},{6,6},{7,5},{8,8},{9,11},{10,1... | collective-permute-start | bytes 393224 | tf_op jit(solution)/shard_map/ppermute | solution.py:207
  17.2 1.0 %copy-start = (bf16[128,2048]{1,0:T(8,128)(2,1)S(1)}, bf16[128,2048]{1,0:T(8,128)(2,1)}, u32[]{:S(2)}) copy-start(bf16[128,2048]{1,0:T(8,128)(2,1)} %get-tuple-element.11.own_ref) | copy-start | bytes 1572868
  19.0 0.7 %collective-permute-start.9 = (f32[32,128]{1,0:T(8,128)S(1)}, f32[32,128]{1,0:T(8,128)S(1)}, u32[]{:S(2)}, u32[]{:S(2)}) collective-permute-start(f32[32,128]{1,0:T(8,128)S(1)} %get-tuple-element.16.mine_ref), channel_id=1, source_target_pairs={{0,0},{1,3},{2,2},{3,1},{4,4},{5,7},{6,6},{7,5},{8,8},{9,11},{10,1... | collective-permute-start | bytes 49160 | tf_op jit(solution)/shard_map/ppermute | solution.py:207
  19.7 0.7 %collective-permute-start.10 = (f32[32,128]{1,0:T(8,128)S(1)}, f32[32,128]{1,0:T(8,128)S(1)}, u32[]{:S(2)}, u32[]{:S(2)}) collective-permute-start(f32[32,128]{1,0:T(8,128)S(1)} %add.15.mine_ref), channel_id=1, source_target_pairs={{0,0},{1,5},{2,2},{3,7},{4,4},{5,1},{6,6},{7,3},{8,8},{9,13},{10,1... | collective-permute-start | bytes 49160 | tf_op jit(solution)/shard_map/ppermute | solution.py:207
  20.4 31.5 %collective-permute-start.11 = (f32[32,128]{1,0:T(8,128)S(1)}, f32[32,128]{1,0:T(8,128)S(1)}, u32[]{:S(2)}, u32[]{:S(2)}) collective-permute-start(f32[32,128]{1,0:T(8,128)S(1)} %add.16.mine_ref), channel_id=1, source_target_pairs={{0,0},{1,9},{2,2},{3,11},{4,4},{5,13},{6,6},{7,15},{8,8},{9,1},{10... | collective-permute-start | bytes 49160 | tf_op jit(solution)/shard_map/ppermute | solution.py:207
  21.1 32.2 %collective-permute-start.8 = (f32[64,128]{1,0:T(8,128)S(1)}, f32[64,128]{1,0:T(8,128)S(1)}, u32[]{:S(2)}, u32[]{:S(2)}) collective-permute-start(f32[64,128]{1,0:T(8,128)S(1)} %get-tuple-element.15.mine_ref), channel_id=1, source_target_pairs={{0,1},{1,0},{2,3},{3,2},{4,5},{5,4},{6,7},{7,6},{8,9},{9,8},{10,11... | collective-permute-start | bytes 98312 | tf_op jit(solution)/shard_map/ppermute | solution.py:199
  52.0 2.2 %collective-permute-start.12 = (f32[32,128]{1,0:T(8,128)S(1)}, f32[32,128]{1,0:T(8,128)S(1)}, u32[]{:S(2)}, u32[]{:S(2)}) collective-permute-start(f32[32,128]{1,0:T(8,128)S(1)} %add.17.gram_ref), channel_id=1, source_target_pairs={{0,1},{1,0},{2,3},{3,2},{4,5},{5,4},{6,7},{7,6},{8,9},{9,8},{10,11... | collective-permute-start | bytes 49160 | tf_op jit(solution)/shard_map/ppermute | solution.py:199

commit v6 on v3

--- a/solution.py
+++ b/solution.py
@@ -21,42 +21,63 @@
     return pltpu.CompilerParams(vmem_limit_bytes=mib * MIB)
 
 
-def contract_kernel(step, snapshot_ref, mode2_ref, send_ref, own_ref, slab_ref, core_ref, sems):
+def own_half():
+    row = lax.axis_index("row")
+    half = lax.axis_index("col")
+    for bit in range(lax.axis_size("row").bit_length() - 1):
+        half += lax.rem(lax.div(row, 1 << bit), 2)
+    return lax.rem(half, 2)
+
+
+def contract_kernel(
+    step, parts, snapshot_ref, mode2_ref, send_ref, own_ref,
+    slab_ref, wide_ref, even_ref, odd_ref, sems,
+):
     cells, fibers, depth = snapshot_ref.shape
     rank = mode2_ref.shape[0]
     reps = LANES // rank
     half = fibers // 2
     chunks = cells // step
 
-    def copy(chunk):
-        where = pl.ds(chunk * step, step)
+    def copy(start, size, chunk):
+        where = pl.ds(start, size)
         return pltpu.make_async_copy(snapshot_ref.at[where], slab_ref.at[where], sems.at[chunk])
 
-    for chunk in range(chunks):
-        copy(chunk).start()
-    wide = jnp.concatenate([mode2_ref[...]] * reps, axis=0).T
+    def start(piece, _):
+        size = step // parts
+        copy(piece * size, size, piece // parts).start()
+        return _
+
+    lax.fori_loop(0, chunks * parts, start, 0)
+    wide_ref[...] = jnp.concatenate([mode2_ref[...]] * reps, axis=0).T
     lane = lax.broadcasted_iota(jnp.int32, (step, LANES), 1)
-    first = lax.axis_index("col") == 0
-
-    for chunk in range(chunks):
-        copy(chunk).wait()
-        core = core_ref.at[chunk % 2]
-        rows = pl.ds(chunk * step, step)
-        core[...] = dot_f32(slab_ref[rows].reshape(step * fibers, depth), wide, ((1,), (0,)))
-
-        def columns(start):
-            part = core[pl.ds(start, step, stride=fibers), :]
-            for r in range(1, reps):
-                other = core[pl.ds(start + r, step, stride=fibers), :]
-                part = jnp.where(lane < r * rank, part, other)
-            return part
-
-        for block in range(half // reps):
-            low = columns(block * reps)
-            high = columns(half + block * reps)
-            where = slice(block * LANES, (block + 1) * LANES)
-            own_ref[rows, where] = jnp.where(first, low, high).astype(BF16)
-            send_ref[rows, where] = jnp.where(first, high, low).astype(BF16)
+    own_start = own_half() * half
+    send_start = half - own_start
+
+    def multiply(chunk, flat_ref):
+        copy(chunk * step, step, chunk).wait()
+        x = slab_ref[pl.ds(chunk * step, step)].reshape(step * fibers, depth)
+        flat_ref[...] = dot_f32(x, wide_ref[...], ((1,), (0,)))
+
+    def spread(chunk, flat_ref):
+        rows = pl.ds(pl.multiple_of(chunk * step, step), step)
+        for base, out_ref in ((own_start, own_ref), (send_start, send_ref)):
+            for block in range(half // reps):
+                part = flat_ref[pl.ds(base + block * reps, step, stride=fibers), :]
+                for r in range(1, reps):
+                    other = flat_ref[pl.ds(base + block * reps + r, step, stride=fibers), :]
+                    part = jnp.where(lane < r * rank, part, other)
+                out_ref[rows, block * LANES:(block + 1) * LANES] = part.astype(BF16)
+
+    def two_chunks(pair, _):
+        multiply(2 * pair, even_ref)
+        spread(jnp.maximum(2 * pair - 1, 0), odd_ref)
+        multiply(2 * pair + 1, odd_ref)
+        spread(2 * pair, even_ref)
+        return _
+
+    lax.fori_loop(0, chunks // 2, two_chunks, 0)
+    spread(chunks - 1, odd_ref)
 
 
 def contract(snapshot, mode2_t):
@@ -65,7 +86,7 @@
     step = 16
     out = jax.ShapeDtypeStruct((cells, fibers // 2 * rank), BF16)
     return pl.pallas_call(
-        functools.partial(contract_kernel, step),
+        functools.partial(contract_kernel, step, 4),
         in_specs=[
             pl.BlockSpec(memory_space=pltpu.HBM),
             pl.BlockSpec(memory_space=pltpu.VMEM),
@@ -73,10 +94,12 @@
         out_shape=[out, out],
         scratch_shapes=[
             pltpu.VMEM(snapshot.shape, BF16),
-            pltpu.VMEM((2, step * fibers, LANES), F32),
+            pltpu.VMEM((depth, LANES), BF16),
+            pltpu.VMEM((step * fibers, LANES), F32),
+            pltpu.VMEM((step * fibers, LANES), F32),
             pltpu.SemaphoreType.DMA((cells // step,)),
         ],
-        compiler_params=params(57),
+        compiler_params=params(50),
         name="contract",
     )(snapshot, mode2_t)
 
@@ -202,30 +225,34 @@
     )(term, got_term, gram, got_gram)
 
 
-def swap(x, axis, mask):
-    return lax.ppermute(x, axis, [(d, d ^ mask) for d in range(lax.axis_size(axis))])
-
-
 def per_device(snapshot, mode2_factor, old_factor):
-    n_rows = lax.axis_size("row")
+    n_rows, n_cols = lax.axis_size("row"), lax.axis_size("col")
     masks = [1 << bit for bit in range(n_rows.bit_length() - 1)]
     total_rows = snapshot.shape[0] * n_rows
 
+    def swap(x, mask):
+        pairs = [
+            (r * n_cols + c, (r ^ mask) * n_cols + (c + 1) % n_cols)
+            for r in range(n_rows)
+            for c in range(n_cols)
+        ]
+        return lax.ppermute(x, ("row", "col"), pairs)
+
     send, own = contract(snapshot, mode2_factor.T)
-    got = swap(send, "col", 1)
+    got = swap(send, 0)
 
     keep, send = project(own, got, old_factor.T)
-    mine = add(keep, swap(send, "row", masks[0]))
+    mine = add(keep, swap(send, masks[0]))
     for mask in masks[1:]:
-        mine = add(mine, swap(mine, "row", mask))
-    other = swap(mine, "row", masks[0])
+        mine = add(mine, swap(mine, mask))
+    other = swap(mine, masks[0])
 
     term = product_terms(own, got, mine, other)
-    got_term = swap(term, "col", 1)
+    got_term = swap(term, 0)
     gram = local_gram(term, got_term)
     for mask in masks[:-1]:
-        gram = add(gram, swap(gram, "row", mask))
-    return finish(total_rows, term, got_term, gram, swap(gram, "row", masks[-1]))
+        gram = add(gram, swap(gram, mask))
+    return finish(total_rows, term, got_term, gram, swap(gram, masks[-1]))
 
 
 def solution(mesh):

time: 53.7 us -> 50.5 us (0.940)
  waiting for transfers between devices: 17.4 us -> 15.2 us
  local copies, waits for them, and re-layouts: 1.9 us -> 0.91 us
  starting transfers between devices: 17.3 us -> 18.1 us
  Pallas kernels: 16.9 us -> 16.1 us
    ppermute x9, waiting for transfers between devices: 17.4 us -> 15.2 us  [swap(): return lax.ppermute(x, ('row', 'col'), pairs)]
    unnamed x6 -> x4, local copies, waits for them, and re-layouts: 1.9 us -> 0.91 us
    ppermute x9, starting transfers between devices: 17.3 us -> 18.1 us  [swap(): return lax.ppermute(x, ('row', 'col'), pairs)]
    pallas_call x1, Pallas kernels: 9.28 us -> 8.49 us  [contract(): pl.pallas_call(functools.partial(contract_kernel, step, 4), in_specs=[pl....]
where the time goes in v6:
time: 50.5 us; the launch traced here: 50.4 us
  starting transfers between devices  18.1 us (36%)
  Pallas kernels  16.1 us (32%)
  waiting for transfers between devices  15.2 us (30%)
  local copies, waits for them, and re-layouts  0.91 us (2%)
    ppermute x9, starting transfers between devices, swap(): return lax.ppermute(x, ('row', 'col'), pairs)  18.1 us
    ppermute x9, waiting for transfers between devices, swap(): return lax.ppermute(x, ('row', 'col'), pairs)  15.2 us
    pallas_call x1, Pallas kernels, contract(): pl.pallas_call(functools.partial(contract_kernel, step, 4), in_specs=[pl....  8.49 us
    pallas_call x1, Pallas kernels, finish(): pl.pallas_call(functools.partial(finish_kernel, total_rows), out_shape=ja...  6.61 us
  transfers between devices with their start and end apart: 9, of which 9 were waited for; matrix products, arithmetic and copies ran while one was open for 0% of the time, Pallas kernels for 0%

profile of v6, /device:TPU:0, one launch (start us, length us, event | category | flops | bytes accessed | tf_op | source)
XLA Modules:
  0.0 50.4 jit_solution(15218885608106600465)
XLA Ops:
  0.0 0.0 copy-start
  0.0 0.9 %copy-done = bf16[1024,64]{0,1:T(8,128)(2,1)S(1)} copy-done((bf16[1024,64]{0,1:T(8,128)(2,1)S(1)}, bf16[1024,64]{0,1:T(8,128)(2,1)}, u32[]{:S(2)}) %copy-start) | copy-done | bytes 131096
  0.9 0.0 copy-start.1
  0.9 8.5 %contract.1 = (bf16[128,1024]{1,0:T(8,128)(2,1)S(1)}, bf16[128,1024]{1,0:T(8,128)(2,1)S(1)}) custom-call(bf16[128,32,1024]{2,1,0:T(8,128)(2,1)} %snapshot_ref.1, bf16[64,1024]{1,0:T(8,128)(2,1)S(1)} %bitcast.2), custom_call_target="tpu_custom_call" | custom-call | tf_op jit(solution)/shard_map/contract/pallas_call | solution.py:88
  9.4 0.5 %collective-permute-start = (bf16[128,1024]{1,0:T(8,128)(2,1)S(1)}, bf16[128,1024]{1,0:T(8,128)(2,1)S(1)}, u32[]{:S(2)}, u32[]{:S(2)}) collective-permute-start(bf16[128,1024]{1,0:T(8,128)(2,1)S(1)} %get-tuple-element.10), channel_id=1, source_target_pairs={{0,1},{1,0},{2,3},{3,2},{4,5},{5,4},{6,7},{7,6},{8,9},{9,8},{10,11... | collective-permute-start | bytes 786440 | tf_op jit(solution)/shard_map/ppermute | solution.py:239
  9.9 1.2 %collective-permute-done.got_ref = bf16[128,1024]{1,0:T(8,128)(2,1)S(1)} collective-permute-done((bf16[128,1024]{1,0:T(8,128)(2,1)S(1)}, bf16[128,1024]{1,0:T(8,128)(2,1)S(1)}, u32[]{:S(2)}, u32[]{:S(2)}) %collective-permute-start) | collective-permute-done | bytes 262176 | tf_op jit(solution)/shard_map/ppermute | solution.py:239
  11.1 0.0 copy-done.1
  11.1 0.2 project.1
  11.3 2.7 %collective-permute-start.1 = (bf16[256,128]{1,0:T(8,128)(2,1)S(1)}, bf16[256,128]{1,0:T(8,128)(2,1)S(1)}, u32[]{:S(2)}, u32[]{:S(2)}) collective-permute-start(bf16[256,128]{1,0:T(8,128)(2,1)S(1)} %get-tuple-element.12), channel_id=1, source_target_pairs={{0,3},{1,2},{2,1},{3,0},{4,7},{5,6},{6,5},{7,4},{8,11},{9,10},{10,... | collective-permute-start | bytes 196616 | tf_op jit(solution)/shard_map/ppermute | solution.py:239
  14.0 2.2 %collective-permute-done.1.got_ref = bf16[256,128]{1,0:T(8,128)(2,1)S(1)} collective-permute-done((bf16[256,128]{1,0:T(8,128)(2,1)S(1)}, bf16[256,128]{1,0:T(8,128)(2,1)S(1)}, u32[]{:S(2)}, u32[]{:S(2)}) %collective-permute-start.1) | collective-permute-done | bytes 65568 | tf_op jit(solution)/shard_map/ppermute | solution.py:239
  16.2 2.0 %collective-permute-start.2 = (bf16[256,128]{1,0:T(8,128)(2,1)S(1)}, bf16[256,128]{1,0:T(8,128)(2,1)S(1)}, u32[]{:S(2)}, u32[]{:S(2)}) collective-permute-start(bf16[256,128]{1,0:T(8,128)(2,1)S(1)} %add.5.mine_ref), channel_id=1, source_target_pairs={{0,5},{1,4},{2,7},{3,6},{4,1},{5,0},{6,3},{7,2},{8,13},{9,12},{10,... | collective-permute-start | bytes 196616 | tf_op jit(solution)/shard_map/ppermute | solution.py:239
  18.2 2.2 %collective-permute-done.2.got_ref = bf16[256,128]{1,0:T(8,128)(2,1)S(1)} collective-permute-done((bf16[256,128]{1,0:T(8,128)(2,1)S(1)}, bf16[256,128]{1,0:T(8,128)(2,1)S(1)}, u32[]{:S(2)}, u32[]{:S(2)}) %collective-permute-start.2) | collective-permute-done | bytes 65568 | tf_op jit(solution)/shard_map/ppermute | solution.py:239
  20.4 3.0 %collective-permute-start.3 = (bf16[256,128]{1,0:T(8,128)(2,1)S(1)}, bf16[256,128]{1,0:T(8,128)(2,1)S(1)}, u32[]{:S(2)}, u32[]{:S(2)}) collective-permute-start(bf16[256,128]{1,0:T(8,128)(2,1)S(1)} %add.6.mine_ref), channel_id=1, source_target_pairs={{0,9},{1,8},{2,11},{3,10},{4,13},{5,12},{6,15},{7,14},{8,1},{9,0},... | collective-permute-start | bytes 196616 | tf_op jit(solution)/shard_map/ppermute | solution.py:239
  23.4 2.2 %collective-permute-done.3.got_ref = bf16[256,128]{1,0:T(8,128)(2,1)S(1)} collective-permute-done((bf16[256,128]{1,0:T(8,128)(2,1)S(1)}, bf16[256,128]{1,0:T(8,128)(2,1)S(1)}, u32[]{:S(2)}, u32[]{:S(2)}) %collective-permute-start.3) | collective-permute-done | bytes 65568 | tf_op jit(solution)/shard_map/ppermute | solution.py:239
  25.6 3.2 %collective-permute-start.4 = (bf16[256,128]{1,0:T(8,128)(2,1)S(1)}, bf16[256,128]{1,0:T(8,128)(2,1)S(1)}, u32[]{:S(2)}, u32[]{:S(2)}) collective-permute-start(bf16[256,128]{1,0:T(8,128)(2,1)S(1)} %add.7.mine_ref), channel_id=1, source_target_pairs={{0,3},{1,2},{2,1},{3,0},{4,7},{5,6},{6,5},{7,4},{8,11},{9,10},{10,... | collective-permute-start | bytes 196616 | tf_op jit(solution)/shard_map/ppermute | solution.py:239
  28.8 2.0 %collective-permute-done.4.other_ref = bf16[256,128]{1,0:T(8,128)(2,1)S(1)} collective-permute-done((bf16[256,128]{1,0:T(8,128)(2,1)S(1)}, bf16[256,128]{1,0:T(8,128)(2,1)S(1)}, u32[]{:S(2)}, u32[]{:S(2)}) %collective-permute-start.4) | collective-permute-done | bytes 65568 | tf_op jit(solution)/shard_map/ppermute | solution.py:239
  30.7 0.4 product_terms.1.term_ref
  31.1 0.1 collective-permute-start.5
  31.2 1.2 %collective-permute-done.5.got_ref.got_term_ref = bf16[64,128]{1,0:T(8,128)(2,1)S(1)} collective-permute-done((bf16[64,128]{1,0:T(8,128)(2,1)S(1)}, bf16[64,128]{1,0:T(8,128)(2,1)S(1)}, u32[]{:S(2)}, u32[]{:S(2)}) %collective-permute-start.5) | collective-permute-done | bytes 16416 | tf_op jit(solution)/shard_map/ppermute | solution.py:239
  32.3 0.4 local_gram.1.mine_ref
  32.7 1.8 %collective-permute-start.6 = (f32[32,128]{1,0:T(8,128)S(1)}, f32[32,128]{1,0:T(8,128)S(1)}, u32[]{:S(2)}, u32[]{:S(2)}) collective-permute-start(f32[32,128]{1,0:T(8,128)S(1)} %local_gram.1.mine_ref), channel_id=1, source_target_pairs={{0,3},{1,2},{2,1},{3,0},{4,7},{5,6},{6,5},{7,4},{8,11},{9,10},{10,... | collective-permute-start | bytes 49160 | tf_op jit(solution)/shard_map/ppermute | solution.py:239
  34.5 1.4 %collective-permute-done.6.got_ref = f32[32,128]{1,0:T(8,128)S(1)} collective-permute-done((f32[32,128]{1,0:T(8,128)S(1)}, f32[32,128]{1,0:T(8,128)S(1)}, u32[]{:S(2)}, u32[]{:S(2)}) %collective-permute-start.6) | collective-permute-done | bytes 16416 | tf_op jit(solution)/shard_map/ppermute | solution.py:239
  35.9 1.7 %collective-permute-start.7 = (f32[32,128]{1,0:T(8,128)S(1)}, f32[32,128]{1,0:T(8,128)S(1)}, u32[]{:S(2)}, u32[]{:S(2)}) collective-permute-start(f32[32,128]{1,0:T(8,128)S(1)} %add.8.mine_ref), channel_id=1, source_target_pairs={{0,5},{1,4},{2,7},{3,6},{4,1},{5,0},{6,3},{7,2},{8,13},{9,12},{10,... | collective-permute-start | bytes 49160 | tf_op jit(solution)/shard_map/ppermute | solution.py:239
  37.6 1.5 %collective-permute-done.7.got_ref = f32[32,128]{1,0:T(8,128)S(1)} collective-permute-done((f32[32,128]{1,0:T(8,128)S(1)}, f32[32,128]{1,0:T(8,128)S(1)}, u32[]{:S(2)}, u32[]{:S(2)}) %collective-permute-start.7) | collective-permute-done | bytes 16416 | tf_op jit(solution)/shard_map/ppermute | solution.py:239
  39.1 3.2 %collective-permute-start.8 = (f32[32,128]{1,0:T(8,128)S(1)}, f32[32,128]{1,0:T(8,128)S(1)}, u32[]{:S(2)}, u32[]{:S(2)}) collective-permute-start(f32[32,128]{1,0:T(8,128)S(1)} %add.9.gram_ref), channel_id=1, source_target_pairs={{0,9},{1,8},{2,11},{3,10},{4,13},{5,12},{6,15},{7,14},{8,1},{9,0},... | collective-permute-start | bytes 49160 | tf_op jit(solution)/shard_map/ppermute | solution.py:239
  42.3 1.4 %collective-permute-done.8.got_gram_ref = f32[32,128]{1,0:T(8,128)S(1)} collective-permute-done((f32[32,128]{1,0:T(8,128)S(1)}, f32[32,128]{1,0:T(8,128)S(1)}, u32[]{:S(2)}, u32[]{:S(2)}) %collective-permute-start.8) | collective-permute-done | bytes 16416 | tf_op jit(solution)/shard_map/ppermute | solution.py:239
  43.7 6.6 %finish.1 = f32[64,64]{1,0:T(8,128)} custom-call(bf16[64,128]{1,0:T(8,128)(2,1)S(1)} %product_terms.1.term_ref, bf16[64,128]{1,0:T(8,128)(2,1)S(1)} %collective-permute-done.5.got_ref.got_term_ref, f32[32,128]{1,0:T(8,128)S(1)} %add.9.gram_ref, f32[32,128]{1,0:T(8,128)S(1)} %collective-permute-done.8.got_gram_ref), custom_call_target="tpu_custom_call" | custom-call | tf_op jit(solution)/shard_map/finish/pallas_call | solution.py:220
  (5 shorter events, 0.1 us)
Async XLA Ops:
  0.0 0.9 %copy-start = (bf16[1024,64]{0,1:T(8,128)(2,1)S(1)}, bf16[1024,64]{0,1:T(8,128)(2,1)}, u32[]{:S(2)}) copy-start(bf16[1024,64]{0,1:T(8,128)(2,1)} %param.4) | copy-start | bytes 393220
  0.9 10.2 %copy-start.1 = (bf16[128,64]{0,1:T(8,128)(2,1)S(1)}, bf16[128,64]{0,1:T(8,128)(2,1)}, u32[]{:S(2)}) copy-start(bf16[128,64]{0,1:T(8,128)(2,1)} %param.5) | copy-start | bytes 49156
  9.4 1.7 %collective-permute-start = (bf16[128,1024]{1,0:T(8,128)(2,1)S(1)}, bf16[128,1024]{1,0:T(8,128)(2,1)S(1)}, u32[]{:S(2)}, u32[]{:S(2)}) collective-permute-start(bf16[128,1024]{1,0:T(8,128)(2,1)S(1)} %get-tuple-element.10), channel_id=1, source_target_pairs={{0,1},{1,0},{2,3},{3,2},{4,5},{5,4},{6,7},{7,6},{8,9},{9,8},{10,11... | collective-permute-start | bytes 786440 | tf_op jit(solution)/shard_map/ppermute | solution.py:239
  11.3 4.9 %collective-permute-start.1 = (bf16[256,128]{1,0:T(8,128)(2,1)S(1)}, bf16[256,128]{1,0:T(8,128)(2,1)S(1)}, u32[]{:S(2)}, u32[]{:S(2)}) collective-permute-start(bf16[256,128]{1,0:T(8,128)(2,1)S(1)} %get-tuple-element.12), channel_id=1, source_target_pairs={{0,3},{1,2},{2,1},{3,0},{4,7},{5,6},{6,5},{7,4},{8,11},{9,10},{10,... | collective-permute-start | bytes 196616 | tf_op jit(solution)/shard_map/ppermute | solution.py:239
  16.2 4.2 %collective-permute-start.2 = (bf16[256,128]{1,0:T(8,128)(2,1)S(1)}, bf16[256,128]{1,0:T(8,128)(2,1)S(1)}, u32[]{:S(2)}, u32[]{:S(2)}) collective-permute-start(bf16[256,128]{1,0:T(8,128)(2,1)S(1)} %add.5.mine_ref), channel_id=1, source_target_pairs={{0,5},{1,4},{2,7},{3,6},{4,1},{5,0},{6,3},{7,2},{8,13},{9,12},{10,... | collective-permute-start | bytes 196616 | tf_op jit(solution)/shard_map/ppermute | solution.py:239
  20.4 5.2 %collective-permute-start.3 = (bf16[256,128]{1,0:T(8,128)(2,1)S(1)}, bf16[256,128]{1,0:T(8,128)(2,1)S(1)}, u32[]{:S(2)}, u32[]{:S(2)}) collective-permute-start(bf16[256,128]{1,0:T(8,128)(2,1)S(1)} %add.6.mine_ref), channel_id=1, source_target_pairs={{0,9},{1,8},{2,11},{3,10},{4,13},{5,12},{6,15},{7,14},{8,1},{9,0},... | collective-permute-start | bytes 196616 | tf_op jit(solution)/shard_map/ppermute | solution.py:239
  25.6 5.1 %collective-permute-start.4 = (bf16[256,128]{1,0:T(8,128)(2,1)S(1)}, bf16[256,128]{1,0:T(8,128)(2,1)S(1)}, u32[]{:S(2)}, u32[]{:S(2)}) collective-permute-start(bf16[256,128]{1,0:T(8,128)(2,1)S(1)} %add.7.mine_ref), channel_id=1, source_target_pairs={{0,3},{1,2},{2,1},{3,0},{4,7},{5,6},{6,5},{7,4},{8,11},{9,10},{10,... | collective-permute-start | bytes 196616 | tf_op jit(solution)/shard_map/ppermute | solution.py:239
  31.1 1.2 %collective-permute-start.5 = (bf16[64,128]{1,0:T(8,128)(2,1)S(1)}, bf16[64,128]{1,0:T(8,128)(2,1)S(1)}, u32[]{:S(2)}, u32[]{:S(2)}) collective-permute-start(bf16[64,128]{1,0:T(8,128)(2,1)S(1)} %product_terms.1.term_ref), channel_id=1, source_target_pairs={{0,1},{1,0},{2,3},{3,2},{4,5},{5,4},{6,7},{7,6},{8,9},{9,8},{10,11... | collective-permute-start | bytes 49160 | tf_op jit(solution)/shard_map/ppermute | solution.py:239
  32.7 3.2 %collective-permute-start.6 = (f32[32,128]{1,0:T(8,128)S(1)}, f32[32,128]{1,0:T(8,128)S(1)}, u32[]{:S(2)}, u32[]{:S(2)}) collective-permute-start(f32[32,128]{1,0:T(8,128)S(1)} %local_gram.1.mine_ref), channel_id=1, source_target_pairs={{0,3},{1,2},{2,1},{3,0},{4,7},{5,6},{6,5},{7,4},{8,11},{9,10},{10,... | collective-permute-start | bytes 49160 | tf_op jit(solution)/shard_map/ppermute | solution.py:239
  35.9 3.2 %collective-permute-start.7 = (f32[32,128]{1,0:T(8,128)S(1)}, f32[32,128]{1,0:T(8,128)S(1)}, u32[]{:S(2)}, u32[]{:S(2)}) collective-permute-start(f32[32,128]{1,0:T(8,128)S(1)} %add.8.mine_ref), channel_id=1, source_target_pairs={{0,5},{1,4},{2,7},{3,6},{4,1},{5,0},{6,3},{7,2},{8,13},{9,12},{10,... | collective-permute-start | bytes 49160 | tf_op jit(solution)/shard_map/ppermute | solution.py:239
  39.1 4.6 %collective-permute-start.8 = (f32[32,128]{1,0:T(8,128)S(1)}, f32[32,128]{1,0:T(8,128)S(1)}, u32[]{:S(2)}, u32[]{:S(2)}) collective-permute-start(f32[32,128]{1,0:T(8,128)S(1)} %add.9.gram_ref), channel_id=1, source_target_pairs={{0,9},{1,8},{2,11},{3,10},{4,13},{5,12},{6,15},{7,14},{8,1},{9,0},... | collective-permute-start | bytes 49160 | tf_op jit(solution)/shard_map/ppermute | solution.py:239

commit v7 on v6

--- a/solution.py
+++ b/solution.py
@@ -49,7 +49,7 @@
         return _
 
     lax.fori_loop(0, chunks * parts, start, 0)
-    wide_ref[...] = jnp.concatenate([mode2_ref[...]] * reps, axis=0).T
+    wide_ref[...] = jnp.concatenate([mode2_ref[...]] * reps, axis=0)
     lane = lax.broadcasted_iota(jnp.int32, (step, LANES), 1)
     own_start = own_half() * half
     send_start = half - own_start
@@ -57,7 +57,7 @@
     def multiply(chunk, flat_ref):
         copy(chunk * step, step, chunk).wait()
         x = slab_ref[pl.ds(chunk * step, step)].reshape(step * fibers, depth)
-        flat_ref[...] = dot_f32(x, wide_ref[...], ((1,), (0,)))
+        flat_ref[...] = dot_f32(x, wide_ref[...], ((1,), (1,)))
 
     def spread(chunk, flat_ref):
         rows = pl.ds(pl.multiple_of(chunk * step, step), step)
@@ -94,7 +94,7 @@
         out_shape=[out, out],
         scratch_shapes=[
             pltpu.VMEM(snapshot.shape, BF16),
-            pltpu.VMEM((depth, LANES), BF16),
+            pltpu.VMEM((LANES, depth), BF16),
             pltpu.VMEM((step * fibers, LANES), F32),
             pltpu.VMEM((step * fibers, LANES), F32),
             pltpu.SemaphoreType.DMA((cells // step,)),
@@ -178,6 +178,67 @@
 
 
 def gram_kernel(term_ref, got_ref, out_ref):
+    product = add_to(term_ref, got_ref)
+    rank = LANES // 2
+    wide = dot_f32(product, product, ((0,), (0,)), lax.Precision.HIGHEST)
+    gram = wide[:rank, :rank] + wide[rank:, rank:]
+    out_ref[...] = jnp.concatenate([gram[:rank // 2], gram[rank // 2:]], axis=1)
+
+
+def local_gram(term, got):
+    return pl.pallas_call(
+        gram_kernel,
+        out_shape=jax.ShapeDtypeStruct((LANES // 4, LANES), F32),
+        compiler_params=params(4),
+        name="local_gram",
+    )(term, got)
+
+
+def eliminate(gram):
+    rank = gram.shape[0]
+    tile = 8
+    count = rank // tile
+    wide = 2 * rank
+    sublane = lax.broadcasted_iota(jnp.int32, (tile, wide), 0)
+    lane = lax.broadcasted_iota(jnp.int32, (tile, wide), 1)
+    full = lambda x: jnp.broadcast_to(x, (tile, wide))
+    both = []
+    for v in range(count):
+        mine = gram[v * tile:(v + 1) * tile]
+        both.append(jnp.where(lane < rank, jnp.concatenate([mine, mine], axis=1),
+                              (lane - rank == sublane + v * tile).astype(F32)))
+    pivots = []
+    for p in range(count):
+        cols = [
+            {v: full(both[v][:, p * tile + j:p * tile + j + 1]) for v in range(p, count)}
+            for j in range(tile)
+        ]
+        found = jnp.ones((tile, wide), F32)
+        for j in range(tile):
+            pivot = full(cols[j][p][j:j + 1])
+            found = jnp.where(sublane == j, pivot, found)
+            inverse = 1.0 / pivot
+            row = full(both[p][j:j + 1]) * inverse
+            heads = {k: full(cols[k][p][j:j + 1]) * inverse for k in range(j + 1, tile)}
+            for v in range(p, count):
+                factor = cols[j][v]
+                if v == p:
+                    factor = jnp.where(sublane > j, factor, 0.0)
+                for k, head in heads.items():
+                    cols[k][v] = cols[k][v] - factor * head
+                both[v] = both[v] - factor * row
+        pivots.append(found)
+    return both, pivots
+
+
+def finish_kernel(total_rows, term_ref, got_term_ref, gram_ref, got_gram_ref, out_ref):
+    rank = LANES // 2
+    packed = gram_ref[...] + got_gram_ref[...]
+    gram = jnp.concatenate([packed[:, :rank], packed[:, rank:]], axis=0)
+    both, pivots = eliminate(gram)
+    scale = total_rows ** 0.5
+    inverse = jnp.concatenate([b * (lax.rsqrt(p) * scale) for b, p in zip(both, pivots)], axis=0)
+    inverse = inverse[:, rank:]
     product = add_to(term_ref, got_ref)
     rank = LANES // 2
     wide = dot_f32(product, product, ((0,), (0,)), lax.Precision.HIGHEST)

time: 50.5 us -> 50.3 us (level)
  no operation moved by 1% of the time
where the time goes in v7:
time: 50.3 us; the launch traced here: 50.2 us
  starting transfers between devices  17.9 us (36%)
  Pallas kernels  15.9 us (32%)
  waiting for transfers between devices  15.5 us (31%)
  local copies, waits for them, and re-layouts  0.91 us (2%)
    ppermute x9, starting transfers between devices, swap(): return lax.ppermute(x, ('row', 'col'), pairs)  17.9 us
    ppermute x9, waiting for transfers between devices, swap(): return lax.ppermute(x, ('row', 'col'), pairs)  15.5 us
    pallas_call x1, Pallas kernels, contract(): pl.pallas_call(functools.partial(contract_kernel, step, 4), in_specs=[pl....  8.22 us
    pallas_call x1, Pallas kernels, finish(): pl.pallas_call(functools.partial(finish_kernel, total_rows), out_shape=ja...  6.61 us
  transfers between devices with their start and end apart: 9, of which 9 were waited for; matrix products, arithmetic and copies ran while one was open for 0% of the time, Pallas kernels for 0%

profile of v7, /device:TPU:0, one launch (start us, length us, event | category | flops | bytes accessed | tf_op | source)
XLA Modules:
  0.0 50.2 jit_solution(4892437348105363285)
XLA Ops:
  0.0 0.0 copy-start
  0.0 0.9 %copy-done = bf16[1024,64]{0,1:T(8,128)(2,1)S(1)} copy-done((bf16[1024,64]{0,1:T(8,128)(2,1)S(1)}, bf16[1024,64]{0,1:T(8,128)(2,1)}, u32[]{:S(2)}) %copy-start) | copy-done | bytes 131096
  0.9 0.0 copy-start.1
  0.9 8.2 %contract.1 = (bf16[128,1024]{1,0:T(8,128)(2,1)S(1)}, bf16[128,1024]{1,0:T(8,128)(2,1)S(1)}) custom-call(bf16[128,32,1024]{2,1,0:T(8,128)(2,1)} %snapshot_ref.1, bf16[64,1024]{1,0:T(8,128)(2,1)S(1)} %bitcast.2), custom_call_target="tpu_custom_call" | custom-call | tf_op jit(solution)/shard_map/contract/pallas_call | solution.py:88
  9.1 0.6 %collective-permute-start = (bf16[128,1024]{1,0:T(8,128)(2,1)S(1)}, bf16[128,1024]{1,0:T(8,128)(2,1)S(1)}, u32[]{:S(2)}, u32[]{:S(2)}) collective-permute-start(bf16[128,1024]{1,0:T(8,128)(2,1)S(1)} %get-tuple-element.10), channel_id=1, source_target_pairs={{0,1},{1,0},{2,3},{3,2},{4,5},{5,4},{6,7},{7,6},{8,9},{9,8},{10,11... | collective-permute-start | bytes 786440 | tf_op jit(solution)/shard_map/ppermute | solution.py:300
  9.7 1.2 %collective-permute-done.got_ref = bf16[128,1024]{1,0:T(8,128)(2,1)S(1)} collective-permute-done((bf16[128,1024]{1,0:T(8,128)(2,1)S(1)}, bf16[128,1024]{1,0:T(8,128)(2,1)S(1)}, u32[]{:S(2)}, u32[]{:S(2)}) %collective-permute-start) | collective-permute-done | bytes 262176 | tf_op jit(solution)/shard_map/ppermute | solution.py:300
  10.9 0.0 copy-done.1
  10.9 0.2 project.1
  11.1 2.7 %collective-permute-start.1 = (bf16[256,128]{1,0:T(8,128)(2,1)S(1)}, bf16[256,128]{1,0:T(8,128)(2,1)S(1)}, u32[]{:S(2)}, u32[]{:S(2)}) collective-permute-start(bf16[256,128]{1,0:T(8,128)(2,1)S(1)} %get-tuple-element.12), channel_id=1, source_target_pairs={{0,3},{1,2},{2,1},{3,0},{4,7},{5,6},{6,5},{7,4},{8,11},{9,10},{10,... | collective-permute-start | bytes 196616 | tf_op jit(solution)/shard_map/ppermute | solution.py:300
  13.8 2.2 %collective-permute-done.1.got_ref = bf16[256,128]{1,0:T(8,128)(2,1)S(1)} collective-permute-done((bf16[256,128]{1,0:T(8,128)(2,1)S(1)}, bf16[256,128]{1,0:T(8,128)(2,1)S(1)}, u32[]{:S(2)}, u32[]{:S(2)}) %collective-permute-start.1) | collective-permute-done | bytes 65568 | tf_op jit(solution)/shard_map/ppermute | solution.py:300
  16.0 2.0 %collective-permute-start.2 = (bf16[256,128]{1,0:T(8,128)(2,1)S(1)}, bf16[256,128]{1,0:T(8,128)(2,1)S(1)}, u32[]{:S(2)}, u32[]{:S(2)}) collective-permute-start(bf16[256,128]{1,0:T(8,128)(2,1)S(1)} %add.5.mine_ref), channel_id=1, source_target_pairs={{0,5},{1,4},{2,7},{3,6},{4,1},{5,0},{6,3},{7,2},{8,13},{9,12},{10,... | collective-permute-start | bytes 196616 | tf_op jit(solution)/shard_map/ppermute | solution.py:300
  18.0 2.2 %collective-permute-done.2.got_ref = bf16[256,128]{1,0:T(8,128)(2,1)S(1)} collective-permute-done((bf16[256,128]{1,0:T(8,128)(2,1)S(1)}, bf16[256,128]{1,0:T(8,128)(2,1)S(1)}, u32[]{:S(2)}, u32[]{:S(2)}) %collective-permute-start.2) | collective-permute-done | bytes 65568 | tf_op jit(solution)/shard_map/ppermute | solution.py:300
  20.2 3.0 %collective-permute-start.3 = (bf16[256,128]{1,0:T(8,128)(2,1)S(1)}, bf16[256,128]{1,0:T(8,128)(2,1)S(1)}, u32[]{:S(2)}, u32[]{:S(2)}) collective-permute-start(bf16[256,128]{1,0:T(8,128)(2,1)S(1)} %add.6.mine_ref), channel_id=1, source_target_pairs={{0,9},{1,8},{2,11},{3,10},{4,13},{5,12},{6,15},{7,14},{8,1},{9,0},... | collective-permute-start | bytes 196616 | tf_op jit(solution)/shard_map/ppermute | solution.py:300
  23.2 2.2 %collective-permute-done.3.got_ref = bf16[256,128]{1,0:T(8,128)(2,1)S(1)} collective-permute-done((bf16[256,128]{1,0:T(8,128)(2,1)S(1)}, bf16[256,128]{1,0:T(8,128)(2,1)S(1)}, u32[]{:S(2)}, u32[]{:S(2)}) %collective-permute-start.3) | collective-permute-done | bytes 65568 | tf_op jit(solution)/shard_map/ppermute | solution.py:300
  25.4 3.2 %collective-permute-start.4 = (bf16[256,128]{1,0:T(8,128)(2,1)S(1)}, bf16[256,128]{1,0:T(8,128)(2,1)S(1)}, u32[]{:S(2)}, u32[]{:S(2)}) collective-permute-start(bf16[256,128]{1,0:T(8,128)(2,1)S(1)} %add.7.mine_ref), channel_id=1, source_target_pairs={{0,3},{1,2},{2,1},{3,0},{4,7},{5,6},{6,5},{7,4},{8,11},{9,10},{10,... | collective-permute-start | bytes 196616 | tf_op jit(solution)/shard_map/ppermute | solution.py:300
  28.6 2.2 %collective-permute-done.4.other_ref = bf16[256,128]{1,0:T(8,128)(2,1)S(1)} collective-permute-done((bf16[256,128]{1,0:T(8,128)(2,1)S(1)}, bf16[256,128]{1,0:T(8,128)(2,1)S(1)}, u32[]{:S(2)}, u32[]{:S(2)}) %collective-permute-start.4) | collective-permute-done | bytes 65568 | tf_op jit(solution)/shard_map/ppermute | solution.py:300
  30.8 0.4 product_terms.1.term_ref
  31.1 0.4 collective-permute-start.5
  31.5 0.9 %collective-permute-done.5.got_ref.got_term_ref = bf16[64,128]{1,0:T(8,128)(2,1)S(1)} collective-permute-done((bf16[64,128]{1,0:T(8,128)(2,1)S(1)}, bf16[64,128]{1,0:T(8,128)(2,1)S(1)}, u32[]{:S(2)}, u32[]{:S(2)}) %collective-permute-start.5) | collective-permute-done | bytes 16416 | tf_op jit(solution)/shard_map/ppermute | solution.py:300
  32.4 0.4 local_gram.1.mine_ref
  32.8 1.9 %collective-permute-start.6 = (f32[32,128]{1,0:T(8,128)S(1)}, f32[32,128]{1,0:T(8,128)S(1)}, u32[]{:S(2)}, u32[]{:S(2)}) collective-permute-start(f32[32,128]{1,0:T(8,128)S(1)} %local_gram.1.mine_ref), channel_id=1, source_target_pairs={{0,3},{1,2},{2,1},{3,0},{4,7},{5,6},{6,5},{7,4},{8,11},{9,10},{10,... | collective-permute-start | bytes 49160 | tf_op jit(solution)/shard_map/ppermute | solution.py:300
  34.7 1.4 %collective-permute-done.6.got_ref = f32[32,128]{1,0:T(8,128)S(1)} collective-permute-done((f32[32,128]{1,0:T(8,128)S(1)}, f32[32,128]{1,0:T(8,128)S(1)}, u32[]{:S(2)}, u32[]{:S(2)}) %collective-permute-start.6) | collective-permute-done | bytes 16416 | tf_op jit(solution)/shard_map/ppermute | solution.py:300
  36.1 1.3 %collective-permute-start.7 = (f32[32,128]{1,0:T(8,128)S(1)}, f32[32,128]{1,0:T(8,128)S(1)}, u32[]{:S(2)}, u32[]{:S(2)}) collective-permute-start(f32[32,128]{1,0:T(8,128)S(1)} %add.8.mine_ref), channel_id=1, source_target_pairs={{0,5},{1,4},{2,7},{3,6},{4,1},{5,0},{6,3},{7,2},{8,13},{9,12},{10,... | collective-permute-start | bytes 49160 | tf_op jit(solution)/shard_map/ppermute | solution.py:300
  37.4 1.9 %collective-permute-done.7.got_ref = f32[32,128]{1,0:T(8,128)S(1)} collective-permute-done((f32[32,128]{1,0:T(8,128)S(1)}, f32[32,128]{1,0:T(8,128)S(1)}, u32[]{:S(2)}, u32[]{:S(2)}) %collective-permute-start.7) | collective-permute-done | bytes 16416 | tf_op jit(solution)/shard_map/ppermute | solution.py:300
  39.3 2.8 %collective-permute-start.8 = (f32[32,128]{1,0:T(8,128)S(1)}, f32[32,128]{1,0:T(8,128)S(1)}, u32[]{:S(2)}, u32[]{:S(2)}) collective-permute-start(f32[32,128]{1,0:T(8,128)S(1)} %add.9.gram_ref), channel_id=1, source_target_pairs={{0,9},{1,8},{2,11},{3,10},{4,13},{5,12},{6,15},{7,14},{8,1},{9,0},... | collective-permute-start | bytes 49160 | tf_op jit(solution)/shard_map/ppermute | solution.py:300
  42.1 1.4 %collective-permute-done.8.got_gram_ref = f32[32,128]{1,0:T(8,128)S(1)} collective-permute-done((f32[32,128]{1,0:T(8,128)S(1)}, f32[32,128]{1,0:T(8,128)S(1)}, u32[]{:S(2)}, u32[]{:S(2)}) %collective-permute-start.8) | collective-permute-done | bytes 16416 | tf_op jit(solution)/shard_map/ppermute | solution.py:300
  43.5 6.6 %finish.1 = f32[64,64]{1,0:T(8,128)} custom-call(bf16[64,128]{1,0:T(8,128)(2,1)S(1)} %product_terms.1.term_ref, bf16[64,128]{1,0:T(8,128)(2,1)S(1)} %collective-permute-done.5.got_ref.got_term_ref, f32[32,128]{1,0:T(8,128)S(1)} %add.9.gram_ref, f32[32,128]{1,0:T(8,128)S(1)} %collective-permute-done.8.got_gram_ref), custom_call_target="tpu_custom_call" | custom-call | tf_op jit(solution)/shard_map/finish/pallas_call | solution.py:281
  (5 shorter events, 0.1 us)
Async XLA Ops:
  0.0 0.9 %copy-start = (bf16[1024,64]{0,1:T(8,128)(2,1)S(1)}, bf16[1024,64]{0,1:T(8,128)(2,1)}, u32[]{:S(2)}) copy-start(bf16[1024,64]{0,1:T(8,128)(2,1)} %param.4) | copy-start | bytes 393220
  0.9 10.0 %copy-start.1 = (bf16[128,64]{0,1:T(8,128)(2,1)S(1)}, bf16[128,64]{0,1:T(8,128)(2,1)}, u32[]{:S(2)}) copy-start(bf16[128,64]{0,1:T(8,128)(2,1)} %param.5) | copy-start | bytes 49156
  9.1 1.7 %collective-permute-start = (bf16[128,1024]{1,0:T(8,128)(2,1)S(1)}, bf16[128,1024]{1,0:T(8,128)(2,1)S(1)}, u32[]{:S(2)}, u32[]{:S(2)}) collective-permute-start(bf16[128,1024]{1,0:T(8,128)(2,1)S(1)} %get-tuple-element.10), channel_id=1, source_target_pairs={{0,1},{1,0},{2,3},{3,2},{4,5},{5,4},{6,7},{7,6},{8,9},{9,8},{10,11... | collective-permute-start | bytes 786440 | tf_op jit(solution)/shard_map/ppermute | solution.py:300
  11.1 4.9 %collective-permute-start.1 = (bf16[256,128]{1,0:T(8,128)(2,1)S(1)}, bf16[256,128]{1,0:T(8,128)(2,1)S(1)}, u32[]{:S(2)}, u32[]{:S(2)}) collective-permute-start(bf16[256,128]{1,0:T(8,128)(2,1)S(1)} %get-tuple-element.12), channel_id=1, source_target_pairs={{0,3},{1,2},{2,1},{3,0},{4,7},{5,6},{6,5},{7,4},{8,11},{9,10},{10,... | collective-permute-start | bytes 196616 | tf_op jit(solution)/shard_map/ppermute | solution.py:300
  16.0 4.2 %collective-permute-start.2 = (bf16[256,128]{1,0:T(8,128)(2,1)S(1)}, bf16[256,128]{1,0:T(8,128)(2,1)S(1)}, u32[]{:S(2)}, u32[]{:S(2)}) collective-permute-start(bf16[256,128]{1,0:T(8,128)(2,1)S(1)} %add.5.mine_ref), channel_id=1, source_target_pairs={{0,5},{1,4},{2,7},{3,6},{4,1},{5,0},{6,3},{7,2},{8,13},{9,12},{10,... | collective-permute-start | bytes 196616 | tf_op jit(solution)/shard_map/ppermute | solution.py:300
  20.2 5.2 %collective-permute-start.3 = (bf16[256,128]{1,0:T(8,128)(2,1)S(1)}, bf16[256,128]{1,0:T(8,128)(2,1)S(1)}, u32[]{:S(2)}, u32[]{:S(2)}) collective-permute-start(bf16[256,128]{1,0:T(8,128)(2,1)S(1)} %add.6.mine_ref), channel_id=1, source_target_pairs={{0,9},{1,8},{2,11},{3,10},{4,13},{5,12},{6,15},{7,14},{8,1},{9,0},... | collective-permute-start | bytes 196616 | tf_op jit(solution)/shard_map/ppermute | solution.py:300
  25.4 5.4 %collective-permute-start.4 = (bf16[256,128]{1,0:T(8,128)(2,1)S(1)}, bf16[256,128]{1,0:T(8,128)(2,1)S(1)}, u32[]{:S(2)}, u32[]{:S(2)}) collective-permute-start(bf16[256,128]{1,0:T(8,128)(2,1)S(1)} %add.7.mine_ref), channel_id=1, source_target_pairs={{0,3},{1,2},{2,1},{3,0},{4,7},{5,6},{6,5},{7,4},{8,11},{9,10},{10,... | collective-permute-start | bytes 196616 | tf_op jit(solution)/shard_map/ppermute | solution.py:300
  31.1 1.2 %collective-permute-start.5 = (bf16[64,128]{1,0:T(8,128)(2,1)S(1)}, bf16[64,128]{1,0:T(8,128)(2,1)S(1)}, u32[]{:S(2)}, u32[]{:S(2)}) collective-permute-start(bf16[64,128]{1,0:T(8,128)(2,1)S(1)} %product_terms.1.term_ref), channel_id=1, source_target_pairs={{0,1},{1,0},{2,3},{3,2},{4,5},{5,4},{6,7},{7,6},{8,9},{9,8},{10,11... | collective-permute-start | bytes 49160 | tf_op jit(solution)/shard_map/ppermute | solution.py:300
  32.8 3.4 %collective-permute-start.6 = (f32[32,128]{1,0:T(8,128)S(1)}, f32[32,128]{1,0:T(8,128)S(1)}, u32[]{:S(2)}, u32[]{:S(2)}) collective-permute-start(f32[32,128]{1,0:T(8,128)S(1)} %local_gram.1.mine_ref), channel_id=1, source_target_pairs={{0,3},{1,2},{2,1},{3,0},{4,7},{5,6},{6,5},{7,4},{8,11},{9,10},{10,... | collective-permute-start | bytes 49160 | tf_op jit(solution)/shard_map/ppermute | solution.py:300
  36.1 3.2 %collective-permute-start.7 = (f32[32,128]{1,0:T(8,128)S(1)}, f32[32,128]{1,0:T(8,128)S(1)}, u32[]{:S(2)}, u32[]{:S(2)}) collective-permute-start(f32[32,128]{1,0:T(8,128)S(1)} %add.8.mine_ref), channel_id=1, source_target_pairs={{0,5},{1,4},{2,7},{3,6},{4,1},{5,0},{6,3},{7,2},{8,13},{9,12},{10,... | collective-permute-start | bytes 49160 | tf_op jit(solution)/shard_map/ppermute | solution.py:300
  39.3 4.2 %collective-permute-start.8 = (f32[32,128]{1,0:T(8,128)S(1)}, f32[32,128]{1,0:T(8,128)S(1)}, u32[]{:S(2)}, u32[]{:S(2)}) collective-permute-start(f32[32,128]{1,0:T(8,128)S(1)} %add.9.gram_ref), channel_id=1, source_target_pairs={{0,9},{1,8},{2,11},{3,10},{4,13},{5,12},{6,15},{7,14},{8,1},{9,0},... | collective-permute-start | bytes 49160 | tf_op jit(solution)/shard_map/ppermute | solution.py:300

commit v8 on v7

--- a/solution.py
+++ b/solution.py
@@ -30,7 +30,7 @@
 
 
 def contract_kernel(
-    step, parts, snapshot_ref, mode2_ref, send_ref, own_ref,
+    step, parts, ahead, snapshot_ref, mode2_ref, send_ref, own_ref,
     slab_ref, wide_ref, even_ref, odd_ref, sems,
 ):
     cells, fibers, depth = snapshot_ref.shape
@@ -43,12 +43,13 @@
         where = pl.ds(start, size)
         return pltpu.make_async_copy(snapshot_ref.at[where], slab_ref.at[where], sems.at[chunk])
 
-    def start(piece, _):
+    def start(chunk):
         size = step // parts
-        copy(piece * size, size, piece // parts).start()
-        return _
-
-    lax.fori_loop(0, chunks * parts, start, 0)
+        for part in range(parts):
+            copy(chunk * step + part * size, size, chunk).start()
+
+    for chunk in range(ahead):
+        start(chunk)
     wide_ref[...] = jnp.concatenate([mode2_ref[...]] * reps, axis=0)
     lane = lax.broadcasted_iota(jnp.int32, (step, LANES), 1)
     own_start = own_half() * half
@@ -56,6 +57,11 @@
 
     def multiply(chunk, flat_ref):
         copy(chunk * step, step, chunk).wait()
+
+        @pl.when(chunk + ahead < chunks)
+        def _():
+            start(chunk + ahead)
+
         x = slab_ref[pl.ds(chunk * step, step)].reshape(step * fibers, depth)
         flat_ref[...] = dot_f32(x, wide_ref[...], ((1,), (1,)))
 
@@ -86,7 +92,7 @@
     step = 16
     out = jax.ShapeDtypeStruct((cells, fibers // 2 * rank), BF16)
     return pl.pallas_call(
-        functools.partial(contract_kernel, step, 4),
+        functools.partial(contract_kernel, step, 8, 2),
         in_specs=[
             pl.BlockSpec(memory_space=pltpu.HBM),
             pl.BlockSpec(memory_space=pltpu.VMEM),
@@ -192,6 +198,13 @@
         compiler_params=params(4),
         name="local_gram",
     )(term, got)
+
+
+def reciprocal(x):
+    guess = pl.reciprocal(x, approx=True, full_range=False)
+    for _ in range(2):
+        guess = guess * (2.0 - x * guess)
+    return guess
 
 
 def eliminate(gram):
@@ -213,20 +226,25 @@
             {v: full(both[v][:, p * tile + j:p * tile + j + 1]) for v in range(p, count)}
             for j in range(tile)
         ]
-        found = jnp.ones((tile, wide), F32)
+        rows = [full(both[p][j:j + 1]) for j in range(tile)]
+        block = [[full(cols[k][p][j:j + 1]) for k in range(j + 1)] for j in range(tile)]
+        found, kept = block[0][0], rows[0]
         for j in range(tile):
-            pivot = full(cols[j][p][j:j + 1])
-            found = jnp.where(sublane == j, pivot, found)
-            inverse = 1.0 / pivot
-            row = full(both[p][j:j + 1]) * inverse
-            heads = {k: full(cols[k][p][j:j + 1]) * inverse for k in range(j + 1, tile)}
-            for v in range(p, count):
-                factor = cols[j][v]
-                if v == p:
-                    factor = jnp.where(sublane > j, factor, 0.0)
-                for k, head in heads.items():
-                    cols[k][v] = cols[k][v] - factor * head
-                both[v] = both[v] - factor * row
+            if j:
+                found = jnp.where(sublane == j, block[j][j], found)
+                kept = jnp.where(sublane == j, rows[j], kept)
+            inverse = reciprocal(block[j][j])
+            scaled = {i: block[i][j] * inverse for i in range(j + 1, tile)}
+            for i, factor in scaled.items():
+                for k in range(j + 1, i + 1):
+                    block[i][k] = block[i][k] - factor * block[k][j]
+                rows[i] = rows[i] - factor * rows[j]
+            row = rows[j] * inverse
+            for v in range(p + 1, count):
+                for i, factor in scaled.items():
+                    cols[i][v] = cols[i][v] - factor * cols[j][v]
+                both[v] = both[v] - cols[j][v] * row
+        both[p] = kept
         pivots.append(found)
     return both, pivots
 

time: 50.3 us -> 50.6 us (level)
  no operation moved by 1% of the time
where the time goes in v8:
time: 50.6 us; the launch traced here: 50.5 us
  starting transfers between devices  18.1 us (36%)
  Pallas kernels  16.2 us (32%)
  waiting for transfers between devices  15.2 us (30%)
  local copies, waits for them, and re-layouts  0.91 us (2%)
    ppermute x9, starting transfers between devices, swap(): return lax.ppermute(x, ('row', 'col'), pairs)  18.1 us
    ppermute x9, waiting for transfers between devices, swap(): return lax.ppermute(x, ('row', 'col'), pairs)  15.2 us
    pallas_call x1, Pallas kernels, contract(): pl.pallas_call(functools.partial(contract_kernel, step, 8, 2), in_specs=[...  8.57 us
    pallas_call x1, Pallas kernels, finish(): pl.pallas_call(functools.partial(finish_kernel, total_rows), out_shape=ja...  6.61 us
  transfers between devices with their start and end apart: 9, of which 9 were waited for; matrix products, arithmetic and copies ran while one was open for 0% of the time, Pallas kernels for 0%

profile of v8, /device:TPU:0, one launch (start us, length us, event | category | flops | bytes accessed | tf_op | source)
XLA Modules:
  0.0 50.5 jit_solution(11889762233264022412)
XLA Ops:
  0.0 0.0 copy-start
  0.0 0.9 %copy-done = bf16[1024,64]{0,1:T(8,128)(2,1)S(1)} copy-done((bf16[1024,64]{0,1:T(8,128)(2,1)S(1)}, bf16[1024,64]{0,1:T(8,128)(2,1)}, u32[]{:S(2)}) %copy-start) | copy-done | bytes 131096
  0.9 0.0 copy-start.1
  0.9 8.6 %contract.1 = (bf16[128,1024]{1,0:T(8,128)(2,1)S(1)}, bf16[128,1024]{1,0:T(8,128)(2,1)S(1)}) custom-call(bf16[128,32,1024]{2,1,0:T(8,128)(2,1)} %snapshot_ref.1, bf16[64,1024]{1,0:T(8,128)(2,1)S(1)} %bitcast.2), custom_call_target="tpu_custom_call" | custom-call | tf_op jit(solution)/shard_map/contract/pallas_call | solution.py:94
  9.5 0.6 %collective-permute-start = (bf16[128,1024]{1,0:T(8,128)(2,1)S(1)}, bf16[128,1024]{1,0:T(8,128)(2,1)S(1)}, u32[]{:S(2)}, u32[]{:S(2)}) collective-permute-start(bf16[128,1024]{1,0:T(8,128)(2,1)S(1)} %get-tuple-element.10), channel_id=1, source_target_pairs={{0,1},{1,0},{2,3},{3,2},{4,5},{5,4},{6,7},{7,6},{8,9},{9,8},{10,11... | collective-permute-start | bytes 786440 | tf_op jit(solution)/shard_map/ppermute | solution.py:318
  10.0 1.2 %collective-permute-done.got_ref = bf16[128,1024]{1,0:T(8,128)(2,1)S(1)} collective-permute-done((bf16[128,1024]{1,0:T(8,128)(2,1)S(1)}, bf16[128,1024]{1,0:T(8,128)(2,1)S(1)}, u32[]{:S(2)}, u32[]{:S(2)}) %collective-permute-start) | collective-permute-done | bytes 262176 | tf_op jit(solution)/shard_map/ppermute | solution.py:318
  11.2 0.0 copy-done.1
  11.2 0.2 project.1
  11.4 2.7 %collective-permute-start.1 = (bf16[256,128]{1,0:T(8,128)(2,1)S(1)}, bf16[256,128]{1,0:T(8,128)(2,1)S(1)}, u32[]{:S(2)}, u32[]{:S(2)}) collective-permute-start(bf16[256,128]{1,0:T(8,128)(2,1)S(1)} %get-tuple-element.12), channel_id=1, source_target_pairs={{0,3},{1,2},{2,1},{3,0},{4,7},{5,6},{6,5},{7,4},{8,11},{9,10},{10,... | collective-permute-start | bytes 196616 | tf_op jit(solution)/shard_map/ppermute | solution.py:318
  14.1 2.2 %collective-permute-done.1.got_ref = bf16[256,128]{1,0:T(8,128)(2,1)S(1)} collective-permute-done((bf16[256,128]{1,0:T(8,128)(2,1)S(1)}, bf16[256,128]{1,0:T(8,128)(2,1)S(1)}, u32[]{:S(2)}, u32[]{:S(2)}) %collective-permute-start.1) | collective-permute-done | bytes 65568 | tf_op jit(solution)/shard_map/ppermute | solution.py:318
  16.3 2.0 %collective-permute-start.2 = (bf16[256,128]{1,0:T(8,128)(2,1)S(1)}, bf16[256,128]{1,0:T(8,128)(2,1)S(1)}, u32[]{:S(2)}, u32[]{:S(2)}) collective-permute-start(bf16[256,128]{1,0:T(8,128)(2,1)S(1)} %add.5.mine_ref), channel_id=1, source_target_pairs={{0,5},{1,4},{2,7},{3,6},{4,1},{5,0},{6,3},{7,2},{8,13},{9,12},{10,... | collective-permute-start | bytes 196616 | tf_op jit(solution)/shard_map/ppermute | solution.py:318
  18.3 2.2 %collective-permute-done.2.got_ref = bf16[256,128]{1,0:T(8,128)(2,1)S(1)} collective-permute-done((bf16[256,128]{1,0:T(8,128)(2,1)S(1)}, bf16[256,128]{1,0:T(8,128)(2,1)S(1)}, u32[]{:S(2)}, u32[]{:S(2)}) %collective-permute-start.2) | collective-permute-done | bytes 65568 | tf_op jit(solution)/shard_map/ppermute | solution.py:318
  20.5 3.0 %collective-permute-start.3 = (bf16[256,128]{1,0:T(8,128)(2,1)S(1)}, bf16[256,128]{1,0:T(8,128)(2,1)S(1)}, u32[]{:S(2)}, u32[]{:S(2)}) collective-permute-start(bf16[256,128]{1,0:T(8,128)(2,1)S(1)} %add.6.mine_ref), channel_id=1, source_target_pairs={{0,9},{1,8},{2,11},{3,10},{4,13},{5,12},{6,15},{7,14},{8,1},{9,0},... | collective-permute-start | bytes 196616 | tf_op jit(solution)/shard_map/ppermute | solution.py:318
  23.5 2.2 %collective-permute-done.3.got_ref = bf16[256,128]{1,0:T(8,128)(2,1)S(1)} collective-permute-done((bf16[256,128]{1,0:T(8,128)(2,1)S(1)}, bf16[256,128]{1,0:T(8,128)(2,1)S(1)}, u32[]{:S(2)}, u32[]{:S(2)}) %collective-permute-start.3) | collective-permute-done | bytes 65568 | tf_op jit(solution)/shard_map/ppermute | solution.py:318
  25.7 3.2 %collective-permute-start.4 = (bf16[256,128]{1,0:T(8,128)(2,1)S(1)}, bf16[256,128]{1,0:T(8,128)(2,1)S(1)}, u32[]{:S(2)}, u32[]{:S(2)}) collective-permute-start(bf16[256,128]{1,0:T(8,128)(2,1)S(1)} %add.7.mine_ref), channel_id=1, source_target_pairs={{0,3},{1,2},{2,1},{3,0},{4,7},{5,6},{6,5},{7,4},{8,11},{9,10},{10,... | collective-permute-start | bytes 196616 | tf_op jit(solution)/shard_map/ppermute | solution.py:318
  28.9 2.0 %collective-permute-done.4.other_ref = bf16[256,128]{1,0:T(8,128)(2,1)S(1)} collective-permute-done((bf16[256,128]{1,0:T(8,128)(2,1)S(1)}, bf16[256,128]{1,0:T(8,128)(2,1)S(1)}, u32[]{:S(2)}, u32[]{:S(2)}) %collective-permute-start.4) | collective-permute-done | bytes 65568 | tf_op jit(solution)/shard_map/ppermute | solution.py:318
  30.9 0.4 product_terms.1.term_ref
  31.2 0.1 collective-permute-start.5
  31.3 1.2 %collective-permute-done.5.got_ref.got_term_ref = bf16[64,128]{1,0:T(8,128)(2,1)S(1)} collective-permute-done((bf16[64,128]{1,0:T(8,128)(2,1)S(1)}, bf16[64,128]{1,0:T(8,128)(2,1)S(1)}, u32[]{:S(2)}, u32[]{:S(2)}) %collective-permute-start.5) | collective-permute-done | bytes 16416 | tf_op jit(solution)/shard_map/ppermute | solution.py:318
  32.5 0.4 local_gram.1.mine_ref
  32.9 1.8 %collective-permute-start.6 = (f32[32,128]{1,0:T(8,128)S(1)}, f32[32,128]{1,0:T(8,128)S(1)}, u32[]{:S(2)}, u32[]{:S(2)}) collective-permute-start(f32[32,128]{1,0:T(8,128)S(1)} %local_gram.1.mine_ref), channel_id=1, source_target_pairs={{0,3},{1,2},{2,1},{3,0},{4,7},{5,6},{6,5},{7,4},{8,11},{9,10},{10,... | collective-permute-start | bytes 49160 | tf_op jit(solution)/shard_map/ppermute | solution.py:318
  34.6 1.4 %collective-permute-done.6.got_ref = f32[32,128]{1,0:T(8,128)S(1)} collective-permute-done((f32[32,128]{1,0:T(8,128)S(1)}, f32[32,128]{1,0:T(8,128)S(1)}, u32[]{:S(2)}, u32[]{:S(2)}) %collective-permute-start.6) | collective-permute-done | bytes 16416 | tf_op jit(solution)/shard_map/ppermute | solution.py:318
  36.1 1.7 %collective-permute-start.7 = (f32[32,128]{1,0:T(8,128)S(1)}, f32[32,128]{1,0:T(8,128)S(1)}, u32[]{:S(2)}, u32[]{:S(2)}) collective-permute-start(f32[32,128]{1,0:T(8,128)S(1)} %add.8.mine_ref), channel_id=1, source_target_pairs={{0,5},{1,4},{2,7},{3,6},{4,1},{5,0},{6,3},{7,2},{8,13},{9,12},{10,... | collective-permute-start | bytes 49160 | tf_op jit(solution)/shard_map/ppermute | solution.py:318
  37.8 1.5 %collective-permute-done.7.got_ref = f32[32,128]{1,0:T(8,128)S(1)} collective-permute-done((f32[32,128]{1,0:T(8,128)S(1)}, f32[32,128]{1,0:T(8,128)S(1)}, u32[]{:S(2)}, u32[]{:S(2)}) %collective-permute-start.7) | collective-permute-done | bytes 16416 | tf_op jit(solution)/shard_map/ppermute | solution.py:318
  39.3 3.2 %collective-permute-start.8 = (f32[32,128]{1,0:T(8,128)S(1)}, f32[32,128]{1,0:T(8,128)S(1)}, u32[]{:S(2)}, u32[]{:S(2)}) collective-permute-start(f32[32,128]{1,0:T(8,128)S(1)} %add.9.gram_ref), channel_id=1, source_target_pairs={{0,9},{1,8},{2,11},{3,10},{4,13},{5,12},{6,15},{7,14},{8,1},{9,0},... | collective-permute-start | bytes 49160 | tf_op jit(solution)/shard_map/ppermute | solution.py:318
  42.4 1.4 %collective-permute-done.8.got_gram_ref = f32[32,128]{1,0:T(8,128)S(1)} collective-permute-done((f32[32,128]{1,0:T(8,128)S(1)}, f32[32,128]{1,0:T(8,128)S(1)}, u32[]{:S(2)}, u32[]{:S(2)}) %collective-permute-start.8) | collective-permute-done | bytes 16416 | tf_op jit(solution)/shard_map/ppermute | solution.py:318
  43.9 6.6 %finish.1 = f32[64,64]{1,0:T(8,128)} custom-call(bf16[64,128]{1,0:T(8,128)(2,1)S(1)} %product_terms.1.term_ref, bf16[64,128]{1,0:T(8,128)(2,1)S(1)} %collective-permute-done.5.got_ref.got_term_ref, f32[32,128]{1,0:T(8,128)S(1)} %add.9.gram_ref, f32[32,128]{1,0:T(8,128)S(1)} %collective-permute-done.8.got_gram_ref), custom_call_target="tpu_custom_call" | custom-call | tf_op jit(solution)/shard_map/finish/pallas_call | solution.py:299
  (5 shorter events, 0.1 us)
Async XLA Ops:
  0.0 0.9 %copy-start = (bf16[1024,64]{0,1:T(8,128)(2,1)S(1)}, bf16[1024,64]{0,1:T(8,128)(2,1)}, u32[]{:S(2)}) copy-start(bf16[1024,64]{0,1:T(8,128)(2,1)} %param.4) | copy-start | bytes 393220
  0.9 10.3 %copy-start.1 = (bf16[128,64]{0,1:T(8,128)(2,1)S(1)}, bf16[128,64]{0,1:T(8,128)(2,1)}, u32[]{:S(2)}) copy-start(bf16[128,64]{0,1:T(8,128)(2,1)} %param.5) | copy-start | bytes 49156
  9.5 1.7 %collective-permute-start = (bf16[128,1024]{1,0:T(8,128)(2,1)S(1)}, bf16[128,1024]{1,0:T(8,128)(2,1)S(1)}, u32[]{:S(2)}, u32[]{:S(2)}) collective-permute-start(bf16[128,1024]{1,0:T(8,128)(2,1)S(1)} %get-tuple-element.10), channel_id=1, source_target_pairs={{0,1},{1,0},{2,3},{3,2},{4,5},{5,4},{6,7},{7,6},{8,9},{9,8},{10,11... | collective-permute-start | bytes 786440 | tf_op jit(solution)/shard_map/ppermute | solution.py:318
  11.4 4.9 %collective-permute-start.1 = (bf16[256,128]{1,0:T(8,128)(2,1)S(1)}, bf16[256,128]{1,0:T(8,128)(2,1)S(1)}, u32[]{:S(2)}, u32[]{:S(2)}) collective-permute-start(bf16[256,128]{1,0:T(8,128)(2,1)S(1)} %get-tuple-element.12), channel_id=1, source_target_pairs={{0,3},{1,2},{2,1},{3,0},{4,7},{5,6},{6,5},{7,4},{8,11},{9,10},{10,... | collective-permute-start | bytes 196616 | tf_op jit(solution)/shard_map/ppermute | solution.py:318
  16.3 4.2 %collective-permute-start.2 = (bf16[256,128]{1,0:T(8,128)(2,1)S(1)}, bf16[256,128]{1,0:T(8,128)(2,1)S(1)}, u32[]{:S(2)}, u32[]{:S(2)}) collective-permute-start(bf16[256,128]{1,0:T(8,128)(2,1)S(1)} %add.5.mine_ref), channel_id=1, source_target_pairs={{0,5},{1,4},{2,7},{3,6},{4,1},{5,0},{6,3},{7,2},{8,13},{9,12},{10,... | collective-permute-start | bytes 196616 | tf_op jit(solution)/shard_map/ppermute | solution.py:318
  20.5 5.2 %collective-permute-start.3 = (bf16[256,128]{1,0:T(8,128)(2,1)S(1)}, bf16[256,128]{1,0:T(8,128)(2,1)S(1)}, u32[]{:S(2)}, u32[]{:S(2)}) collective-permute-start(bf16[256,128]{1,0:T(8,128)(2,1)S(1)} %add.6.mine_ref), channel_id=1, source_target_pairs={{0,9},{1,8},{2,11},{3,10},{4,13},{5,12},{6,15},{7,14},{8,1},{9,0},... | collective-permute-start | bytes 196616 | tf_op jit(solution)/shard_map/ppermute | solution.py:318
  25.7 5.2 %collective-permute-start.4 = (bf16[256,128]{1,0:T(8,128)(2,1)S(1)}, bf16[256,128]{1,0:T(8,128)(2,1)S(1)}, u32[]{:S(2)}, u32[]{:S(2)}) collective-permute-start(bf16[256,128]{1,0:T(8,128)(2,1)S(1)} %add.7.mine_ref), channel_id=1, source_target_pairs={{0,3},{1,2},{2,1},{3,0},{4,7},{5,6},{6,5},{7,4},{8,11},{9,10},{10,... | collective-permute-start | bytes 196616 | tf_op jit(solution)/shard_map/ppermute | solution.py:318
  31.2 1.2 %collective-permute-start.5 = (bf16[64,128]{1,0:T(8,128)(2,1)S(1)}, bf16[64,128]{1,0:T(8,128)(2,1)S(1)}, u32[]{:S(2)}, u32[]{:S(2)}) collective-permute-start(bf16[64,128]{1,0:T(8,128)(2,1)S(1)} %product_terms.1.term_ref), channel_id=1, source_target_pairs={{0,1},{1,0},{2,3},{3,2},{4,5},{5,4},{6,7},{7,6},{8,9},{9,8},{10,11... | collective-permute-start | bytes 49160 | tf_op jit(solution)/shard_map/ppermute | solution.py:318
  32.9 3.2 %collective-permute-start.6 = (f32[32,128]{1,0:T(8,128)S(1)}, f32[32,128]{1,0:T(8,128)S(1)}, u32[]{:S(2)}, u32[]{:S(2)}) collective-permute-start(f32[32,128]{1,0:T(8,128)S(1)} %local_gram.1.mine_ref), channel_id=1, source_target_pairs={{0,3},{1,2},{2,1},{3,0},{4,7},{5,6},{6,5},{7,4},{8,11},{9,10},{10,... | collective-permute-start | bytes 49160 | tf_op jit(solution)/shard_map/ppermute | solution.py:318
  36.1 3.2 %collective-permute-start.7 = (f32[32,128]{1,0:T(8,128)S(1)}, f32[32,128]{1,0:T(8,128)S(1)}, u32[]{:S(2)}, u32[]{:S(2)}) collective-permute-start(f32[32,128]{1,0:T(8,128)S(1)} %add.8.mine_ref), channel_id=1, source_target_pairs={{0,5},{1,4},{2,7},{3,6},{4,1},{5,0},{6,3},{7,2},{8,13},{9,12},{10,... | collective-permute-start | bytes 49160 | tf_op jit(solution)/shard_map/ppermute | solution.py:318
  39.3 4.6 %collective-permute-start.8 = (f32[32,128]{1,0:T(8,128)S(1)}, f32[32,128]{1,0:T(8,128)S(1)}, u32[]{:S(2)}, u32[]{:S(2)}) collective-permute-start(f32[32,128]{1,0:T(8,128)S(1)} %add.9.gram_ref), channel_id=1, source_target_pairs={{0,9},{1,8},{2,11},{3,10},{4,13},{5,12},{6,15},{7,14},{8,1},{9,0},... | collective-permute-start | bytes 49160 | tf_op jit(solution)/shard_map/ppermute | solution.py:318

commit v9 on v8

--- a/solution.py
+++ b/solution.py
@@ -30,39 +30,28 @@
 
 
 def contract_kernel(
-    step, parts, ahead, snapshot_ref, mode2_ref, send_ref, own_ref,
+    step, fibers, snapshot_ref, mode2_ref, send_ref, own_ref,
     slab_ref, wide_ref, even_ref, odd_ref, sems,
 ):
-    cells, fibers, depth = snapshot_ref.shape
-    rank = mode2_ref.shape[0]
+    rank, depth = mode2_ref.shape
     reps = LANES // rank
     half = fibers // 2
-    chunks = cells // step
-
-    def copy(start, size, chunk):
-        where = pl.ds(start, size)
+    chunks = snapshot_ref.shape[0] // (step * fibers)
+
+    def copy(chunk):
+        where = pl.ds(chunk * step * fibers, step * fibers)
         return pltpu.make_async_copy(snapshot_ref.at[where], slab_ref.at[where], sems.at[chunk])
 
-    def start(chunk):
-        size = step // parts
-        for part in range(parts):
-            copy(chunk * step + part * size, size, chunk).start()
-
-    for chunk in range(ahead):
-        start(chunk)
+    for chunk in range(chunks):
+        copy(chunk).start(priority=chunk % 2)
     wide_ref[...] = jnp.concatenate([mode2_ref[...]] * reps, axis=0)
     lane = lax.broadcasted_iota(jnp.int32, (step, LANES), 1)
     own_start = own_half() * half
     send_start = half - own_start
 
     def multiply(chunk, flat_ref):
-        copy(chunk * step, step, chunk).wait()
-
-        @pl.when(chunk + ahead < chunks)
-        def _():
-            start(chunk + ahead)
-
-        x = slab_ref[pl.ds(chunk * step, step)].reshape(step * fibers, depth)
+        copy(chunk).wait()
+        x = slab_ref[pl.ds(chunk * step * fibers, step * fibers), :]
         flat_ref[...] = dot_f32(x, wide_ref[...], ((1,), (1,)))
 
     def spread(chunk, flat_ref):
@@ -92,14 +81,14 @@
     step = 16
     out = jax.ShapeDtypeStruct((cells, fibers // 2 * rank), BF16)
     return pl.pallas_call(
-        functools.partial(contract_kernel, step, 8, 2),
+        functools.partial(contract_kernel, step, fibers),
         in_specs=[
             pl.BlockSpec(memory_space=pltpu.HBM),
             pl.BlockSpec(memory_space=pltpu.VMEM),
         ],
         out_shape=[out, out],
         scratch_shapes=[
-            pltpu.VMEM(snapshot.shape, BF16),
+            pltpu.VMEM((cells * fibers, depth), BF16),
             pltpu.VMEM((LANES, depth), BF16),
             pltpu.VMEM((step * fibers, LANES), F32),
             pltpu.VMEM((step * fibers, LANES), F32),
@@ -107,7 +96,7 @@
         ],
         compiler_params=params(50),
         name="contract",
-    )(snapshot, mode2_t)
+    )(snapshot.reshape(cells * fibers, depth), mode2_t)
 
 
 def add_to(*refs):
@@ -257,39 +246,6 @@
     scale = total_rows ** 0.5
     inverse = jnp.concatenate([b * (lax.rsqrt(p) * scale) for b, p in zip(both, pivots)], axis=0)
     inverse = inverse[:, rank:]
-    product = add_to(term_ref, got_ref)
-    rank = LANES // 2
-    wide = dot_f32(product, product, ((0,), (0,)), lax.Precision.HIGHEST)
-    gram = wide[:rank, :rank] + wide[rank:, rank:]
-    out_ref[...] = jnp.concatenate([gram[:rank // 2], gram[rank // 2:]], axis=1)
-
-
-def local_gram(term, got):
-    return pl.pallas_call(
-        gram_kernel,
-        out_shape=jax.ShapeDtypeStruct((LANES // 4, LANES), F32),
-        compiler_params=params(4),
-        name="local_gram",
-    )(term, got)
-
-
-def finish_kernel(total_rows, term_ref, got_term_ref, gram_ref, got_gram_ref, out_ref):
-    rank = LANES // 2
-    packed = gram_ref[...] + got_gram_ref[...]
-    gram = jnp.concatenate([packed[:, :rank], packed[:, rank:]], axis=0)
-    eye = (
-        lax.broadcasted_iota(jnp.int32, (rank, rank), 0)
-        == lax.broadcasted_iota(jnp.int32, (rank, rank), 1)
-    ).astype(F32)
-    both = jnp.concatenate([gram, eye], axis=1)
-    row_index = lax.broadcasted_iota(jnp.int32, (rank, 1), 0)
-    pivots = jnp.zeros((rank, 1), F32)
-    for k in range(rank):
-        pivot = both[k:k + 1, k:k + 1]
-        pivots = jnp.where(row_index == k, pivot, pivots)
-        factor = jnp.where(row_index > k, both[:, k:k + 1] / pivot, 0.0)
-        both = both - factor * both[k:k + 1, :]
-    inverse = both[:, rank:] * (lax.rsqrt(pivots) * (total_rows ** 0.5))
     product = add_to(term_ref, got_term_ref)
     mine = jnp.where(lax.axis_index("col") == 0, product[:, :rank], product[:, rank:])
     out_ref[...] = dot_f32(mine, inverse, ((1,), (1,)), lax.Precision.HIGHEST)

time: 50.6 us -> 47.4 us (0.937)
  Pallas kernels: 16.2 us -> 13 us
    pallas_call x1, Pallas kernels: 6.61 us -> 3.29 us  [finish(): pl.pallas_call(functools.partial(finish_kernel, total_rows), out_shape=ja...]
where the time goes in v9:
time: 47.4 us; the launch traced here: 47.3 us
  starting transfers between devices  18.2 us (38%)
  waiting for transfers between devices  15.1 us (32%)
  Pallas kernels  13 us (27%)
  local copies, waits for them, and re-layouts  0.91 us (2%)
    ppermute x9, starting transfers between devices, swap(): return lax.ppermute(x, ('row', 'col'), pairs)  18.2 us
    ppermute x9, waiting for transfers between devices, swap(): return lax.ppermute(x, ('row', 'col'), pairs)  15.1 us
    pallas_call x1, Pallas kernels, contract(): pl.pallas_call(functools.partial(contract_kernel, step, fibers), in_specs...  8.69 us
    pallas_call x1, Pallas kernels, finish(): pl.pallas_call(functools.partial(finish_kernel, total_rows), out_shape=ja...  3.29 us
  transfers between devices with their start and end apart: 9, of which 9 were waited for; matrix products, arithmetic and copies ran while one was open for 0% of the time, Pallas kernels for 0%

profile of v9, /device:TPU:0, one launch (start us, length us, event | category | flops | bytes accessed | tf_op | source)
XLA Modules:
  0.0 47.3 jit_solution(18145624640600282411)
XLA Ops:
  0.0 0.0 copy-start
  0.0 0.9 %copy-done = bf16[1024,64]{0,1:T(8,128)(2,1)S(1)} copy-done((bf16[1024,64]{0,1:T(8,128)(2,1)S(1)}, bf16[1024,64]{0,1:T(8,128)(2,1)}, u32[]{:S(2)}) %copy-start) | copy-done | bytes 131096
  0.9 0.0 copy-start.1
  0.9 8.7 %contract.1 = (bf16[128,1024]{1,0:T(8,128)(2,1)S(1)}, bf16[128,1024]{1,0:T(8,128)(2,1)S(1)}) custom-call(bf16[4096,1024]{1,0:T(8,128)(2,1)} %bitcast.5, bf16[64,1024]{1,0:T(8,128)(2,1)S(1)} %bitcast.3), custom_call_target="tpu_custom_call" | custom-call | tf_op jit(solution)/shard_map/contract/pallas_call | solution.py:83
  9.6 0.6 %collective-permute-start = (bf16[128,1024]{1,0:T(8,128)(2,1)S(1)}, bf16[128,1024]{1,0:T(8,128)(2,1)S(1)}, u32[]{:S(2)}, u32[]{:S(2)}) collective-permute-start(bf16[128,1024]{1,0:T(8,128)(2,1)S(1)} %get-tuple-element.10), channel_id=1, source_target_pairs={{0,1},{1,0},{2,3},{3,2},{4,5},{5,4},{6,7},{7,6},{8,9},{9,8},{10,11... | collective-permute-start | bytes 786440 | tf_op jit(solution)/shard_map/ppermute | solution.py:274
  10.2 1.2 %collective-permute-done.got_ref = bf16[128,1024]{1,0:T(8,128)(2,1)S(1)} collective-permute-done((bf16[128,1024]{1,0:T(8,128)(2,1)S(1)}, bf16[128,1024]{1,0:T(8,128)(2,1)S(1)}, u32[]{:S(2)}, u32[]{:S(2)}) %collective-permute-start) | collective-permute-done | bytes 262176 | tf_op jit(solution)/shard_map/ppermute | solution.py:274
  11.3 0.0 copy-done.1
  11.3 0.2 project.1
  11.6 2.7 %collective-permute-start.1 = (bf16[256,128]{1,0:T(8,128)(2,1)S(1)}, bf16[256,128]{1,0:T(8,128)(2,1)S(1)}, u32[]{:S(2)}, u32[]{:S(2)}) collective-permute-start(bf16[256,128]{1,0:T(8,128)(2,1)S(1)} %get-tuple-element.12), channel_id=1, source_target_pairs={{0,3},{1,2},{2,1},{3,0},{4,7},{5,6},{6,5},{7,4},{8,11},{9,10},{10,... | collective-permute-start | bytes 196616 | tf_op jit(solution)/shard_map/ppermute | solution.py:274
  14.3 2.2 %collective-permute-done.1.got_ref = bf16[256,128]{1,0:T(8,128)(2,1)S(1)} collective-permute-done((bf16[256,128]{1,0:T(8,128)(2,1)S(1)}, bf16[256,128]{1,0:T(8,128)(2,1)S(1)}, u32[]{:S(2)}, u32[]{:S(2)}) %collective-permute-start.1) | collective-permute-done | bytes 65568 | tf_op jit(solution)/shard_map/ppermute | solution.py:274
  16.5 2.0 %collective-permute-start.2 = (bf16[256,128]{1,0:T(8,128)(2,1)S(1)}, bf16[256,128]{1,0:T(8,128)(2,1)S(1)}, u32[]{:S(2)}, u32[]{:S(2)}) collective-permute-start(bf16[256,128]{1,0:T(8,128)(2,1)S(1)} %add.5.mine_ref), channel_id=1, source_target_pairs={{0,5},{1,4},{2,7},{3,6},{4,1},{5,0},{6,3},{7,2},{8,13},{9,12},{10,... | collective-permute-start | bytes 196616 | tf_op jit(solution)/shard_map/ppermute | solution.py:274
  18.5 2.2 %collective-permute-done.2.got_ref = bf16[256,128]{1,0:T(8,128)(2,1)S(1)} collective-permute-done((bf16[256,128]{1,0:T(8,128)(2,1)S(1)}, bf16[256,128]{1,0:T(8,128)(2,1)S(1)}, u32[]{:S(2)}, u32[]{:S(2)}) %collective-permute-start.2) | collective-permute-done | bytes 65568 | tf_op jit(solution)/shard_map/ppermute | solution.py:274
  20.7 3.0 %collective-permute-start.3 = (bf16[256,128]{1,0:T(8,128)(2,1)S(1)}, bf16[256,128]{1,0:T(8,128)(2,1)S(1)}, u32[]{:S(2)}, u32[]{:S(2)}) collective-permute-start(bf16[256,128]{1,0:T(8,128)(2,1)S(1)} %add.6.mine_ref), channel_id=1, source_target_pairs={{0,9},{1,8},{2,11},{3,10},{4,13},{5,12},{6,15},{7,14},{8,1},{9,0},... | collective-permute-start | bytes 196616 | tf_op jit(solution)/shard_map/ppermute | solution.py:274
  23.7 2.2 %collective-permute-done.3.got_ref = bf16[256,128]{1,0:T(8,128)(2,1)S(1)} collective-permute-done((bf16[256,128]{1,0:T(8,128)(2,1)S(1)}, bf16[256,128]{1,0:T(8,128)(2,1)S(1)}, u32[]{:S(2)}, u32[]{:S(2)}) %collective-permute-start.3) | collective-permute-done | bytes 65568 | tf_op jit(solution)/shard_map/ppermute | solution.py:274
  25.9 3.2 %collective-permute-start.4 = (bf16[256,128]{1,0:T(8,128)(2,1)S(1)}, bf16[256,128]{1,0:T(8,128)(2,1)S(1)}, u32[]{:S(2)}, u32[]{:S(2)}) collective-permute-start(bf16[256,128]{1,0:T(8,128)(2,1)S(1)} %add.7.mine_ref), channel_id=1, source_target_pairs={{0,3},{1,2},{2,1},{3,0},{4,7},{5,6},{6,5},{7,4},{8,11},{9,10},{10,... | collective-permute-start | bytes 196616 | tf_op jit(solution)/shard_map/ppermute | solution.py:274
  29.0 2.0 %collective-permute-done.4.other_ref = bf16[256,128]{1,0:T(8,128)(2,1)S(1)} collective-permute-done((bf16[256,128]{1,0:T(8,128)(2,1)S(1)}, bf16[256,128]{1,0:T(8,128)(2,1)S(1)}, u32[]{:S(2)}, u32[]{:S(2)}) %collective-permute-start.4) | collective-permute-done | bytes 65568 | tf_op jit(solution)/shard_map/ppermute | solution.py:274
  31.0 0.4 product_terms.1.term_ref
  31.4 0.1 collective-permute-start.5
  31.4 1.2 %collective-permute-done.5.got_ref.got_term_ref = bf16[64,128]{1,0:T(8,128)(2,1)S(1)} collective-permute-done((bf16[64,128]{1,0:T(8,128)(2,1)S(1)}, bf16[64,128]{1,0:T(8,128)(2,1)S(1)}, u32[]{:S(2)}, u32[]{:S(2)}) %collective-permute-start.5) | collective-permute-done | bytes 16416 | tf_op jit(solution)/shard_map/ppermute | solution.py:274
  32.6 0.4 local_gram.1.mine_ref
  33.0 1.8 %collective-permute-start.6 = (f32[32,128]{1,0:T(8,128)S(1)}, f32[32,128]{1,0:T(8,128)S(1)}, u32[]{:S(2)}, u32[]{:S(2)}) collective-permute-start(f32[32,128]{1,0:T(8,128)S(1)} %local_gram.1.mine_ref), channel_id=1, source_target_pairs={{0,3},{1,2},{2,1},{3,0},{4,7},{5,6},{6,5},{7,4},{8,11},{9,10},{10,... | collective-permute-start | bytes 49160 | tf_op jit(solution)/shard_map/ppermute | solution.py:274
  34.7 1.4 %collective-permute-done.6.got_ref = f32[32,128]{1,0:T(8,128)S(1)} collective-permute-done((f32[32,128]{1,0:T(8,128)S(1)}, f32[32,128]{1,0:T(8,128)S(1)}, u32[]{:S(2)}, u32[]{:S(2)}) %collective-permute-start.6) | collective-permute-done | bytes 16416 | tf_op jit(solution)/shard_map/ppermute | solution.py:274
  36.2 1.7 %collective-permute-start.7 = (f32[32,128]{1,0:T(8,128)S(1)}, f32[32,128]{1,0:T(8,128)S(1)}, u32[]{:S(2)}, u32[]{:S(2)}) collective-permute-start(f32[32,128]{1,0:T(8,128)S(1)} %add.8.mine_ref), channel_id=1, source_target_pairs={{0,5},{1,4},{2,7},{3,6},{4,1},{5,0},{6,3},{7,2},{8,13},{9,12},{10,... | collective-permute-start | bytes 49160 | tf_op jit(solution)/shard_map/ppermute | solution.py:274
  37.9 1.5 %collective-permute-done.7.got_ref = f32[32,128]{1,0:T(8,128)S(1)} collective-permute-done((f32[32,128]{1,0:T(8,128)S(1)}, f32[32,128]{1,0:T(8,128)S(1)}, u32[]{:S(2)}, u32[]{:S(2)}) %collective-permute-start.7) | collective-permute-done | bytes 16416 | tf_op jit(solution)/shard_map/ppermute | solution.py:274
  39.4 3.2 %collective-permute-start.8 = (f32[32,128]{1,0:T(8,128)S(1)}, f32[32,128]{1,0:T(8,128)S(1)}, u32[]{:S(2)}, u32[]{:S(2)}) collective-permute-start(f32[32,128]{1,0:T(8,128)S(1)} %add.9.gram_ref), channel_id=1, source_target_pairs={{0,9},{1,8},{2,11},{3,10},{4,13},{5,12},{6,15},{7,14},{8,1},{9,0},... | collective-permute-start | bytes 49160 | tf_op jit(solution)/shard_map/ppermute | solution.py:274
  42.6 1.4 %collective-permute-done.8.got_gram_ref = f32[32,128]{1,0:T(8,128)S(1)} collective-permute-done((f32[32,128]{1,0:T(8,128)S(1)}, f32[32,128]{1,0:T(8,128)S(1)}, u32[]{:S(2)}, u32[]{:S(2)}) %collective-permute-start.8) | collective-permute-done | bytes 16416 | tf_op jit(solution)/shard_map/ppermute | solution.py:274
  44.0 3.3 %finish.1 = f32[64,64]{1,0:T(8,128)} custom-call(bf16[64,128]{1,0:T(8,128)(2,1)S(1)} %product_terms.1.term_ref, bf16[64,128]{1,0:T(8,128)(2,1)S(1)} %collective-permute-done.5.got_ref.got_term_ref, f32[32,128]{1,0:T(8,128)S(1)} %add.9.gram_ref, f32[32,128]{1,0:T(8,128)S(1)} %collective-permute-done.8.got_gram_ref), custom_call_target="tpu_custom_call" | custom-call | tf_op jit(solution)/shard_map/finish/pallas_call | solution.py:255
  (5 shorter events, 0.1 us)
Async XLA Ops:
  0.0 0.9 %copy-start = (bf16[1024,64]{0,1:T(8,128)(2,1)S(1)}, bf16[1024,64]{0,1:T(8,128)(2,1)}, u32[]{:S(2)}) copy-start(bf16[1024,64]{0,1:T(8,128)(2,1)} %param.4) | copy-start | bytes 393220
  0.9 10.4 %copy-start.1 = (bf16[128,64]{0,1:T(8,128)(2,1)S(1)}, bf16[128,64]{0,1:T(8,128)(2,1)}, u32[]{:S(2)}) copy-start(bf16[128,64]{0,1:T(8,128)(2,1)} %param.5) | copy-start | bytes 49156
  9.6 1.7 %collective-permute-start = (bf16[128,1024]{1,0:T(8,128)(2,1)S(1)}, bf16[128,1024]{1,0:T(8,128)(2,1)S(1)}, u32[]{:S(2)}, u32[]{:S(2)}) collective-permute-start(bf16[128,1024]{1,0:T(8,128)(2,1)S(1)} %get-tuple-element.10), channel_id=1, source_target_pairs={{0,1},{1,0},{2,3},{3,2},{4,5},{5,4},{6,7},{7,6},{8,9},{9,8},{10,11... | collective-permute-start | bytes 786440 | tf_op jit(solution)/shard_map/ppermute | solution.py:274
  11.6 4.9 %collective-permute-start.1 = (bf16[256,128]{1,0:T(8,128)(2,1)S(1)}, bf16[256,128]{1,0:T(8,128)(2,1)S(1)}, u32[]{:S(2)}, u32[]{:S(2)}) collective-permute-start(bf16[256,128]{1,0:T(8,128)(2,1)S(1)} %get-tuple-element.12), channel_id=1, source_target_pairs={{0,3},{1,2},{2,1},{3,0},{4,7},{5,6},{6,5},{7,4},{8,11},{9,10},{10,... | collective-permute-start | bytes 196616 | tf_op jit(solution)/shard_map/ppermute | solution.py:274
  16.5 4.2 %collective-permute-start.2 = (bf16[256,128]{1,0:T(8,128)(2,1)S(1)}, bf16[256,128]{1,0:T(8,128)(2,1)S(1)}, u32[]{:S(2)}, u32[]{:S(2)}) collective-permute-start(bf16[256,128]{1,0:T(8,128)(2,1)S(1)} %add.5.mine_ref), channel_id=1, source_target_pairs={{0,5},{1,4},{2,7},{3,6},{4,1},{5,0},{6,3},{7,2},{8,13},{9,12},{10,... | collective-permute-start | bytes 196616 | tf_op jit(solution)/shard_map/ppermute | solution.py:274
  20.7 5.2 %collective-permute-start.3 = (bf16[256,128]{1,0:T(8,128)(2,1)S(1)}, bf16[256,128]{1,0:T(8,128)(2,1)S(1)}, u32[]{:S(2)}, u32[]{:S(2)}) collective-permute-start(bf16[256,128]{1,0:T(8,128)(2,1)S(1)} %add.6.mine_ref), channel_id=1, source_target_pairs={{0,9},{1,8},{2,11},{3,10},{4,13},{5,12},{6,15},{7,14},{8,1},{9,0},... | collective-permute-start | bytes 196616 | tf_op jit(solution)/shard_map/ppermute | solution.py:274
  25.9 5.1 %collective-permute-start.4 = (bf16[256,128]{1,0:T(8,128)(2,1)S(1)}, bf16[256,128]{1,0:T(8,128)(2,1)S(1)}, u32[]{:S(2)}, u32[]{:S(2)}) collective-permute-start(bf16[256,128]{1,0:T(8,128)(2,1)S(1)} %add.7.mine_ref), channel_id=1, source_target_pairs={{0,3},{1,2},{2,1},{3,0},{4,7},{5,6},{6,5},{7,4},{8,11},{9,10},{10,... | collective-permute-start | bytes 196616 | tf_op jit(solution)/shard_map/ppermute | solution.py:274
  31.4 1.2 %collective-permute-start.5 = (bf16[64,128]{1,0:T(8,128)(2,1)S(1)}, bf16[64,128]{1,0:T(8,128)(2,1)S(1)}, u32[]{:S(2)}, u32[]{:S(2)}) collective-permute-start(bf16[64,128]{1,0:T(8,128)(2,1)S(1)} %product_terms.1.term_ref), channel_id=1, source_target_pairs={{0,1},{1,0},{2,3},{3,2},{4,5},{5,4},{6,7},{7,6},{8,9},{9,8},{10,11... | collective-permute-start | bytes 49160 | tf_op jit(solution)/shard_map/ppermute | solution.py:274
  33.0 3.2 %collective-permute-start.6 = (f32[32,128]{1,0:T(8,128)S(1)}, f32[32,128]{1,0:T(8,128)S(1)}, u32[]{:S(2)}, u32[]{:S(2)}) collective-permute-start(f32[32,128]{1,0:T(8,128)S(1)} %local_gram.1.mine_ref), channel_id=1, source_target_pairs={{0,3},{1,2},{2,1},{3,0},{4,7},{5,6},{6,5},{7,4},{8,11},{9,10},{10,... | collective-permute-start | bytes 49160 | tf_op jit(solution)/shard_map/ppermute | solution.py:274
  36.2 3.2 %collective-permute-start.7 = (f32[32,128]{1,0:T(8,128)S(1)}, f32[32,128]{1,0:T(8,128)S(1)}, u32[]{:S(2)}, u32[]{:S(2)}) collective-permute-start(f32[32,128]{1,0:T(8,128)S(1)} %add.8.mine_ref), channel_id=1, source_target_pairs={{0,5},{1,4},{2,7},{3,6},{4,1},{5,0},{6,3},{7,2},{8,13},{9,12},{10,... | collective-permute-start | bytes 49160 | tf_op jit(solution)/shard_map/ppermute | solution.py:274
  39.4 4.6 %collective-permute-start.8 = (f32[32,128]{1,0:T(8,128)S(1)}, f32[32,128]{1,0:T(8,128)S(1)}, u32[]{:S(2)}, u32[]{:S(2)}) collective-permute-start(f32[32,128]{1,0:T(8,128)S(1)} %add.9.gram_ref), channel_id=1, source_target_pairs={{0,9},{1,8},{2,11},{3,10},{4,13},{5,12},{6,15},{7,14},{8,1},{9,0},... | collective-permute-start | bytes 49160 | tf_op jit(solution)/shard_map/ppermute | solution.py:274

commit v10 on v9

--- a/solution.py
+++ b/solution.py
@@ -31,27 +31,20 @@
 
 def contract_kernel(
     step, fibers, snapshot_ref, mode2_ref, send_ref, own_ref,
-    slab_ref, wide_ref, even_ref, odd_ref, sems,
+    wide_ref, even_ref, odd_ref,
 ):
     rank, depth = mode2_ref.shape
     reps = LANES // rank
     half = fibers // 2
     chunks = snapshot_ref.shape[0] // (step * fibers)
 
-    def copy(chunk):
-        where = pl.ds(chunk * step * fibers, step * fibers)
-        return pltpu.make_async_copy(snapshot_ref.at[where], slab_ref.at[where], sems.at[chunk])
-
-    for chunk in range(chunks):
-        copy(chunk).start(priority=chunk % 2)
     wide_ref[...] = jnp.concatenate([mode2_ref[...]] * reps, axis=0)
     lane = lax.broadcasted_iota(jnp.int32, (step, LANES), 1)
     own_start = own_half() * half
     send_start = half - own_start
 
     def multiply(chunk, flat_ref):
-        copy(chunk).wait()
-        x = slab_ref[pl.ds(chunk * step * fibers, step * fibers), :]
+        x = snapshot_ref[pl.ds(chunk * step * fibers, step * fibers), :]
         flat_ref[...] = dot_f32(x, wide_ref[...], ((1,), (1,)))
 
     def spread(chunk, flat_ref):
@@ -83,18 +76,16 @@
     return pl.pallas_call(
         functools.partial(contract_kernel, step, fibers),
         in_specs=[
-            pl.BlockSpec(memory_space=pltpu.HBM),
+            pl.BlockSpec(memory_space=pltpu.VMEM),
             pl.BlockSpec(memory_space=pltpu.VMEM),
         ],
         out_shape=[out, out],
         scratch_shapes=[
-            pltpu.VMEM((cells * fibers, depth), BF16),
             pltpu.VMEM((LANES, depth), BF16),
             pltpu.VMEM((step * fibers, LANES), F32),
             pltpu.VMEM((step * fibers, LANES), F32),
-            pltpu.SemaphoreType.DMA((cells // step,)),
         ],
-        compiler_params=params(50),
+        compiler_params=params(24),
         name="contract",
     )(snapshot.reshape(cells * fibers, depth), mode2_t)
 

time: 47.4 us -> 46.3 us (0.977)
  Pallas kernels: 13 us -> 8.62 us
  local copies, waits for them, and re-layouts: 0.91 us -> 4.29 us
    pallas_call x1, Pallas kernels: 8.69 us -> 4.3 us  [contract(): pl.pallas_call(functools.partial(contract_kernel, step, fibers), in_specs...]
    unnamed x4 -> x6, local copies, waits for them, and re-layouts: 0.91 us -> 4.29 us
where the time goes in v10:
time: 46.3 us; the launch traced here: 46.1 us
  starting transfers between devices  18 us (39%)
  waiting for transfers between devices  15.2 us (33%)
  Pallas kernels  8.62 us (19%)
  local copies, waits for them, and re-layouts  4.29 us (9%)
    ppermute x9, starting transfers between devices, swap(): return lax.ppermute(x, ('row', 'col'), pairs)  18 us
    ppermute x9, waiting for transfers between devices, swap(): return lax.ppermute(x, ('row', 'col'), pairs)  15.2 us
    pallas_call x1, Pallas kernels, contract(): pl.pallas_call(functools.partial(contract_kernel, step, fibers), in_specs...  4.3 us
    unnamed x6, local copies, waits for them, and re-layouts  4.29 us
    pallas_call x1, Pallas kernels, finish(): pl.pallas_call(functools.partial(finish_kernel, total_rows), out_shape=ja...  3.29 us
  transfers between devices with their start and end apart: 9, of which 9 were waited for; matrix products, arithmetic and copies ran while one was open for 0% of the time, Pallas kernels for 0%

profile of v10, /device:TPU:0, one launch (start us, length us, event | category | flops | bytes accessed | tf_op | source)
XLA Modules:
  0.0 46.1 jit_solution(16733468951006607717)
XLA Ops:
  0.0 0.0 copy-start
  0.0 3.4 %copy-done = bf16[128,32,1024]{2,1,0:T(8,128)(2,1)S(1)} copy-done((bf16[128,32,1024]{2,1,0:T(8,128)(2,1)S(1)}, bf16[128,32,1024]{2,1,0:T(8,128)(2,1)}, u32[]{:S(2)}) %copy-start) | copy-done | bytes 8388632
  3.4 0.0 copy-start.1
  3.4 0.9 %copy-done.1 = bf16[1024,64]{0,1:T(8,128)(2,1)S(1)} copy-done((bf16[1024,64]{0,1:T(8,128)(2,1)S(1)}, bf16[1024,64]{0,1:T(8,128)(2,1)}, u32[]{:S(2)}) %copy-start.1) | copy-done | bytes 131096
  4.3 0.0 copy-start.2
  4.3 4.3 %contract.1 = (bf16[128,1024]{1,0:T(8,128)(2,1)S(1)}, bf16[128,1024]{1,0:T(8,128)(2,1)S(1)}) custom-call(bf16[4096,1024]{1,0:T(8,128)(2,1)S(1)} %bitcast.3, bf16[64,1024]{1,0:T(8,128)(2,1)S(1)} %bitcast.4), custom_call_target="tpu_custom_call" | custom-call | tf_op jit(solution)/shard_map/contract/pallas_call | solution.py:76
  8.6 0.5 collective-permute-start
  9.1 1.2 %collective-permute-done.got_ref = bf16[128,1024]{1,0:T(8,128)(2,1)S(1)} collective-permute-done((bf16[128,1024]{1,0:T(8,128)(2,1)S(1)}, bf16[128,1024]{1,0:T(8,128)(2,1)S(1)}, u32[]{:S(2)}, u32[]{:S(2)}) %collective-permute-start) | collective-permute-done | bytes 262176 | tf_op jit(solution)/shard_map/ppermute | solution.py:265
  10.2 0.0 copy-done.2
  10.2 0.2 project.1
  10.4 2.7 %collective-permute-start.1 = (bf16[256,128]{1,0:T(8,128)(2,1)S(1)}, bf16[256,128]{1,0:T(8,128)(2,1)S(1)}, u32[]{:S(2)}, u32[]{:S(2)}) collective-permute-start(bf16[256,128]{1,0:T(8,128)(2,1)S(1)} %get-tuple-element.12), channel_id=1, source_target_pairs={{0,3},{1,2},{2,1},{3,0},{4,7},{5,6},{6,5},{7,4},{8,11},{9,10},{10,... | collective-permute-start | bytes 196616 | tf_op jit(solution)/shard_map/ppermute | solution.py:265
  13.1 2.2 %collective-permute-done.1.got_ref = bf16[256,128]{1,0:T(8,128)(2,1)S(1)} collective-permute-done((bf16[256,128]{1,0:T(8,128)(2,1)S(1)}, bf16[256,128]{1,0:T(8,128)(2,1)S(1)}, u32[]{:S(2)}, u32[]{:S(2)}) %collective-permute-start.1) | collective-permute-done | bytes 65568 | tf_op jit(solution)/shard_map/ppermute | solution.py:265
  15.3 2.0 %collective-permute-start.2 = (bf16[256,128]{1,0:T(8,128)(2,1)S(1)}, bf16[256,128]{1,0:T(8,128)(2,1)S(1)}, u32[]{:S(2)}, u32[]{:S(2)}) collective-permute-start(bf16[256,128]{1,0:T(8,128)(2,1)S(1)} %add.5.mine_ref), channel_id=1, source_target_pairs={{0,5},{1,4},{2,7},{3,6},{4,1},{5,0},{6,3},{7,2},{8,13},{9,12},{10,... | collective-permute-start | bytes 196616 | tf_op jit(solution)/shard_map/ppermute | solution.py:265
  17.3 2.2 %collective-permute-done.2.got_ref = bf16[256,128]{1,0:T(8,128)(2,1)S(1)} collective-permute-done((bf16[256,128]{1,0:T(8,128)(2,1)S(1)}, bf16[256,128]{1,0:T(8,128)(2,1)S(1)}, u32[]{:S(2)}, u32[]{:S(2)}) %collective-permute-start.2) | collective-permute-done | bytes 65568 | tf_op jit(solution)/shard_map/ppermute | solution.py:265
  19.5 3.0 %collective-permute-start.3 = (bf16[256,128]{1,0:T(8,128)(2,1)S(1)}, bf16[256,128]{1,0:T(8,128)(2,1)S(1)}, u32[]{:S(2)}, u32[]{:S(2)}) collective-permute-start(bf16[256,128]{1,0:T(8,128)(2,1)S(1)} %add.6.mine_ref), channel_id=1, source_target_pairs={{0,9},{1,8},{2,11},{3,10},{4,13},{5,12},{6,15},{7,14},{8,1},{9,0},... | collective-permute-start | bytes 196616 | tf_op jit(solution)/shard_map/ppermute | solution.py:265
  22.5 2.2 %collective-permute-done.3.got_ref = bf16[256,128]{1,0:T(8,128)(2,1)S(1)} collective-permute-done((bf16[256,128]{1,0:T(8,128)(2,1)S(1)}, bf16[256,128]{1,0:T(8,128)(2,1)S(1)}, u32[]{:S(2)}, u32[]{:S(2)}) %collective-permute-start.3) | collective-permute-done | bytes 65568 | tf_op jit(solution)/shard_map/ppermute | solution.py:265
  24.7 3.2 %collective-permute-start.4 = (bf16[256,128]{1,0:T(8,128)(2,1)S(1)}, bf16[256,128]{1,0:T(8,128)(2,1)S(1)}, u32[]{:S(2)}, u32[]{:S(2)}) collective-permute-start(bf16[256,128]{1,0:T(8,128)(2,1)S(1)} %add.7.mine_ref), channel_id=1, source_target_pairs={{0,3},{1,2},{2,1},{3,0},{4,7},{5,6},{6,5},{7,4},{8,11},{9,10},{10,... | collective-permute-start | bytes 196616 | tf_op jit(solution)/shard_map/ppermute | solution.py:265
  27.9 2.0 %collective-permute-done.4.other_ref = bf16[256,128]{1,0:T(8,128)(2,1)S(1)} collective-permute-done((bf16[256,128]{1,0:T(8,128)(2,1)S(1)}, bf16[256,128]{1,0:T(8,128)(2,1)S(1)}, u32[]{:S(2)}, u32[]{:S(2)}) %collective-permute-start.4) | collective-permute-done | bytes 65568 | tf_op jit(solution)/shard_map/ppermute | solution.py:265
  29.9 0.4 product_terms.1.term_ref
  30.2 0.1 collective-permute-start.5
  30.3 1.2 %collective-permute-done.5.got_ref.got_term_ref = bf16[64,128]{1,0:T(8,128)(2,1)S(1)} collective-permute-done((bf16[64,128]{1,0:T(8,128)(2,1)S(1)}, bf16[64,128]{1,0:T(8,128)(2,1)S(1)}, u32[]{:S(2)}, u32[]{:S(2)}) %collective-permute-start.5) | collective-permute-done | bytes 16416 | tf_op jit(solution)/shard_map/ppermute | solution.py:265
  31.5 0.4 local_gram.1.mine_ref
  31.9 1.8 %collective-permute-start.6 = (f32[32,128]{1,0:T(8,128)S(1)}, f32[32,128]{1,0:T(8,128)S(1)}, u32[]{:S(2)}, u32[]{:S(2)}) collective-permute-start(f32[32,128]{1,0:T(8,128)S(1)} %local_gram.1.mine_ref), channel_id=1, source_target_pairs={{0,3},{1,2},{2,1},{3,0},{4,7},{5,6},{6,5},{7,4},{8,11},{9,10},{10,... | collective-permute-start | bytes 49160 | tf_op jit(solution)/shard_map/ppermute | solution.py:265
  33.6 1.4 %collective-permute-done.6.got_ref = f32[32,128]{1,0:T(8,128)S(1)} collective-permute-done((f32[32,128]{1,0:T(8,128)S(1)}, f32[32,128]{1,0:T(8,128)S(1)}, u32[]{:S(2)}, u32[]{:S(2)}) %collective-permute-start.6) | collective-permute-done | bytes 16416 | tf_op jit(solution)/shard_map/ppermute | solution.py:265
  35.1 1.7 %collective-permute-start.7 = (f32[32,128]{1,0:T(8,128)S(1)}, f32[32,128]{1,0:T(8,128)S(1)}, u32[]{:S(2)}, u32[]{:S(2)}) collective-permute-start(f32[32,128]{1,0:T(8,128)S(1)} %add.8.mine_ref), channel_id=1, source_target_pairs={{0,5},{1,4},{2,7},{3,6},{4,1},{5,0},{6,3},{7,2},{8,13},{9,12},{10,... | collective-permute-start | bytes 49160 | tf_op jit(solution)/shard_map/ppermute | solution.py:265
  36.8 1.5 %collective-permute-done.7.got_ref = f32[32,128]{1,0:T(8,128)S(1)} collective-permute-done((f32[32,128]{1,0:T(8,128)S(1)}, f32[32,128]{1,0:T(8,128)S(1)}, u32[]{:S(2)}, u32[]{:S(2)}) %collective-permute-start.7) | collective-permute-done | bytes 16416 | tf_op jit(solution)/shard_map/ppermute | solution.py:265
  38.2 3.2 %collective-permute-start.8 = (f32[32,128]{1,0:T(8,128)S(1)}, f32[32,128]{1,0:T(8,128)S(1)}, u32[]{:S(2)}, u32[]{:S(2)}) collective-permute-start(f32[32,128]{1,0:T(8,128)S(1)} %add.9.gram_ref), channel_id=1, source_target_pairs={{0,9},{1,8},{2,11},{3,10},{4,13},{5,12},{6,15},{7,14},{8,1},{9,0},... | collective-permute-start | bytes 49160 | tf_op jit(solution)/shard_map/ppermute | solution.py:265
  41.4 1.4 %collective-permute-done.8.got_gram_ref = f32[32,128]{1,0:T(8,128)S(1)} collective-permute-done((f32[32,128]{1,0:T(8,128)S(1)}, f32[32,128]{1,0:T(8,128)S(1)}, u32[]{:S(2)}, u32[]{:S(2)}) %collective-permute-start.8) | collective-permute-done | bytes 16416 | tf_op jit(solution)/shard_map/ppermute | solution.py:265
  42.9 3.3 %finish.1 = f32[64,64]{1,0:T(8,128)} custom-call(bf16[64,128]{1,0:T(8,128)(2,1)S(1)} %product_terms.1.term_ref, bf16[64,128]{1,0:T(8,128)(2,1)S(1)} %collective-permute-done.5.got_ref.got_term_ref, f32[32,128]{1,0:T(8,128)S(1)} %add.9.gram_ref, f32[32,128]{1,0:T(8,128)S(1)} %collective-permute-done.8.got_gram_ref), custom_call_target="tpu_custom_call" | custom-call | tf_op jit(solution)/shard_map/finish/pallas_call | solution.py:246
  (5 shorter events, 0.1 us)
Async XLA Ops:
  0.0 3.4 %copy-start = (bf16[128,32,1024]{2,1,0:T(8,128)(2,1)S(1)}, bf16[128,32,1024]{2,1,0:T(8,128)(2,1)}, u32[]{:S(2)}) copy-start(bf16[128,32,1024]{2,1,0:T(8,128)(2,1)} %param.3) | copy-start | bytes 25165828
  3.4 0.9 %copy-start.1 = (bf16[1024,64]{0,1:T(8,128)(2,1)S(1)}, bf16[1024,64]{0,1:T(8,128)(2,1)}, u32[]{:S(2)}) copy-start(bf16[1024,64]{0,1:T(8,128)(2,1)} %param.4) | copy-start | bytes 393220
  4.3 5.9 %copy-start.2 = (bf16[128,64]{0,1:T(8,128)(2,1)S(1)}, bf16[128,64]{0,1:T(8,128)(2,1)}, u32[]{:S(2)}) copy-start(bf16[128,64]{0,1:T(8,128)(2,1)} %param.5) | copy-start | bytes 49156
  8.6 1.6 %collective-permute-start = (bf16[128,1024]{1,0:T(8,128)(2,1)S(1)}, bf16[128,1024]{1,0:T(8,128)(2,1)S(1)}, u32[]{:S(2)}, u32[]{:S(2)}) collective-permute-start(bf16[128,1024]{1,0:T(8,128)(2,1)S(1)} %get-tuple-element.10), channel_id=1, source_target_pairs={{0,1},{1,0},{2,3},{3,2},{4,5},{5,4},{6,7},{7,6},{8,9},{9,8},{10,11... | collective-permute-start | bytes 786440 | tf_op jit(solution)/shard_map/ppermute | solution.py:265
  10.4 4.9 %collective-permute-start.1 = (bf16[256,128]{1,0:T(8,128)(2,1)S(1)}, bf16[256,128]{1,0:T(8,128)(2,1)S(1)}, u32[]{:S(2)}, u32[]{:S(2)}) collective-permute-start(bf16[256,128]{1,0:T(8,128)(2,1)S(1)} %get-tuple-element.12), channel_id=1, source_target_pairs={{0,3},{1,2},{2,1},{3,0},{4,7},{5,6},{6,5},{7,4},{8,11},{9,10},{10,... | collective-permute-start | bytes 196616 | tf_op jit(solution)/shard_map/ppermute | solution.py:265
  15.3 4.2 %collective-permute-start.2 = (bf16[256,128]{1,0:T(8,128)(2,1)S(1)}, bf16[256,128]{1,0:T(8,128)(2,1)S(1)}, u32[]{:S(2)}, u32[]{:S(2)}) collective-permute-start(bf16[256,128]{1,0:T(8,128)(2,1)S(1)} %add.5.mine_ref), channel_id=1, source_target_pairs={{0,5},{1,4},{2,7},{3,6},{4,1},{5,0},{6,3},{7,2},{8,13},{9,12},{10,... | collective-permute-start | bytes 196616 | tf_op jit(solution)/shard_map/ppermute | solution.py:265
  19.5 5.2 %collective-permute-start.3 = (bf16[256,128]{1,0:T(8,128)(2,1)S(1)}, bf16[256,128]{1,0:T(8,128)(2,1)S(1)}, u32[]{:S(2)}, u32[]{:S(2)}) collective-permute-start(bf16[256,128]{1,0:T(8,128)(2,1)S(1)} %add.6.mine_ref), channel_id=1, source_target_pairs={{0,9},{1,8},{2,11},{3,10},{4,13},{5,12},{6,15},{7,14},{8,1},{9,0},... | collective-permute-start | bytes 196616 | tf_op jit(solution)/shard_map/ppermute | solution.py:265
  24.7 5.1 %collective-permute-start.4 = (bf16[256,128]{1,0:T(8,128)(2,1)S(1)}, bf16[256,128]{1,0:T(8,128)(2,1)S(1)}, u32[]{:S(2)}, u32[]{:S(2)}) collective-permute-start(bf16[256,128]{1,0:T(8,128)(2,1)S(1)} %add.7.mine_ref), channel_id=1, source_target_pairs={{0,3},{1,2},{2,1},{3,0},{4,7},{5,6},{6,5},{7,4},{8,11},{9,10},{10,... | collective-permute-start | bytes 196616 | tf_op jit(solution)/shard_map/ppermute | solution.py:265
  30.2 1.2 %collective-permute-start.5 = (bf16[64,128]{1,0:T(8,128)(2,1)S(1)}, bf16[64,128]{1,0:T(8,128)(2,1)S(1)}, u32[]{:S(2)}, u32[]{:S(2)}) collective-permute-start(bf16[64,128]{1,0:T(8,128)(2,1)S(1)} %product_terms.1.term_ref), channel_id=1, source_target_pairs={{0,1},{1,0},{2,3},{3,2},{4,5},{5,4},{6,7},{7,6},{8,9},{9,8},{10,11... | collective-permute-start | bytes 49160 | tf_op jit(solution)/shard_map/ppermute | solution.py:265
  31.9 3.2 %collective-permute-start.6 = (f32[32,128]{1,0:T(8,128)S(1)}, f32[32,128]{1,0:T(8,128)S(1)}, u32[]{:S(2)}, u32[]{:S(2)}) collective-permute-start(f32[32,128]{1,0:T(8,128)S(1)} %local_gram.1.mine_ref), channel_id=1, source_target_pairs={{0,3},{1,2},{2,1},{3,0},{4,7},{5,6},{6,5},{7,4},{8,11},{9,10},{10,... | collective-permute-start | bytes 49160 | tf_op jit(solution)/shard_map/ppermute | solution.py:265
  35.1 3.2 %collective-permute-start.7 = (f32[32,128]{1,0:T(8,128)S(1)}, f32[32,128]{1,0:T(8,128)S(1)}, u32[]{:S(2)}, u32[]{:S(2)}) collective-permute-start(f32[32,128]{1,0:T(8,128)S(1)} %add.8.mine_ref), channel_id=1, source_target_pairs={{0,5},{1,4},{2,7},{3,6},{4,1},{5,0},{6,3},{7,2},{8,13},{9,12},{10,... | collective-permute-start | bytes 49160 | tf_op jit(solution)/shard_map/ppermute | solution.py:265
  38.2 4.6 %collective-permute-start.8 = (f32[32,128]{1,0:T(8,128)S(1)}, f32[32,128]{1,0:T(8,128)S(1)}, u32[]{:S(2)}, u32[]{:S(2)}) collective-permute-start(f32[32,128]{1,0:T(8,128)S(1)} %add.9.gram_ref), channel_id=1, source_target_pairs={{0,9},{1,8},{2,11},{3,10},{4,13},{5,12},{6,15},{7,14},{8,1},{9,0},... | collective-permute-start | bytes 49160 | tf_op jit(solution)/shard_map/ppermute | solution.py:265

commit v11 on v10

--- a/solution.py
+++ b/solution.py
@@ -29,33 +29,45 @@
     return lax.rem(half, 2)
 
 
-def contract_kernel(
-    step, fibers, snapshot_ref, mode2_ref, send_ref, own_ref,
-    wide_ref, even_ref, odd_ref,
-):
+def contract_kernel(step, fibers, snapshot_ref, mode2_ref, send_ref, own_ref, even_ref, odd_ref):
     rank, depth = mode2_ref.shape
+    tile = 8
     reps = LANES // rank
-    half = fibers // 2
+    block = tile * fibers
+    blocks = step // tile
+    out_rows = block // reps
     chunks = snapshot_ref.shape[0] // (step * fibers)
-
-    wide_ref[...] = jnp.concatenate([mode2_ref[...]] * reps, axis=0)
-    lane = lax.broadcasted_iota(jnp.int32, (step, LANES), 1)
-    own_start = own_half() * half
-    send_start = half - own_start
+    wide = jnp.concatenate([mode2_ref[...]] * reps, axis=0)
+    lane = lax.broadcasted_iota(jnp.int32, (block, LANES), 1)
+    to = lax.broadcasted_iota(jnp.int32, (out_rows, reps * block), 0)
+    at = lax.broadcasted_iota(jnp.int32, (out_rows, reps * block), 1)
+    cell = lax.div(lax.rem(at, block), fibers)
+    fiber = lax.rem(at, fibers)
+    wanted = lax.div(to, tile) * reps + lax.div(at, block)
+    order = ((lax.rem(to, tile) == cell) & (wanted == fiber)).astype(F32).astype(BF16)
+    first = own_half() == 0
+    pairs = fibers // reps
 
     def multiply(chunk, flat_ref):
         x = snapshot_ref[pl.ds(chunk * step * fibers, step * fibers), :]
-        flat_ref[...] = dot_f32(x, wide_ref[...], ((1,), (1,)))
+        flat_ref[...] = dot_f32(x, wide, ((1,), (1,))).astype(BF16)
 
     def spread(chunk, flat_ref):
         rows = pl.ds(pl.multiple_of(chunk * step, step), step)
-        for base, out_ref in ((own_start, own_ref), (send_start, send_ref)):
-            for block in range(half // reps):
-                part = flat_ref[pl.ds(base + block * reps, step, stride=fibers), :]
-                for r in range(1, reps):
-                    other = flat_ref[pl.ds(base + block * reps + r, step, stride=fibers), :]
-                    part = jnp.where(lane < r * rank, part, other)
-                out_ref[rows, block * LANES:(block + 1) * LANES] = part.astype(BF16)
+        spreads = []
+        for b in range(blocks):
+            flat = flat_ref[pl.ds(b * block, block), :].astype(F32)
+            groups = [
+                jnp.where(lax.div(lane, rank) == r, flat, 0.0).astype(BF16) for r in range(reps)
+            ]
+            spreads.append(dot_f32(order, jnp.concatenate(groups, axis=0), ((1,), (0,))))
+        for p in range(pairs // 2):
+            low = jnp.concatenate([x[p * tile:(p + 1) * tile] for x in spreads], axis=0)
+            q = p + pairs // 2
+            high = jnp.concatenate([x[q * tile:(q + 1) * tile] for x in spreads], axis=0)
+            where = slice(p * LANES, (p + 1) * LANES)
+            own_ref[rows, where] = jnp.where(first, low, high).astype(BF16)
+            send_ref[rows, where] = jnp.where(first, high, low).astype(BF16)
 
     def two_chunks(pair, _):
         multiply(2 * pair, even_ref)
@@ -80,11 +92,7 @@
             pl.BlockSpec(memory_space=pltpu.VMEM),
         ],
         out_shape=[out, out],
-        scratch_shapes=[
-            pltpu.VMEM((LANES, depth), BF16),
-            pltpu.VMEM((step * fibers, LANES), F32),
-            pltpu.VMEM((step * fibers, LANES), F32),
-        ],
+        scratch_shapes=[pltpu.VMEM((step * fibers, LANES), BF16)] * 2,
         compiler_params=params(24),
         name="contract",
     )(snapshot.reshape(cells * fibers, depth), mode2_t)

time: 46.3 us -> 46 us (level)
  no operation moved by 1% of the time
where the time goes in v11:
time: 46 us; the launch traced here: 45.9 us
  starting transfers between devices  18.1 us (39%)
  waiting for transfers between devices  15.2 us (33%)
  Pallas kernels  8.29 us (18%)
  local copies, waits for them, and re-layouts  4.29 us (9%)
    ppermute x9, starting transfers between devices, swap(): return lax.ppermute(x, ('row', 'col'), pairs)  18.1 us
    ppermute x9, waiting for transfers between devices, swap(): return lax.ppermute(x, ('row', 'col'), pairs)  15.2 us
    unnamed x6, local copies, waits for them, and re-layouts  4.29 us
    pallas_call x1, Pallas kernels, contract(): pl.pallas_call(functools.partial(contract_kernel, step, fibers), in_specs...  3.96 us
    pallas_call x1, Pallas kernels, finish(): pl.pallas_call(functools.partial(finish_kernel, total_rows), out_shape=ja...  3.29 us
  transfers between devices with their start and end apart: 9, of which 9 were waited for; matrix products, arithmetic and copies ran while one was open for 0% of the time, Pallas kernels for 0%

profile of v11, /device:TPU:0, one launch (start us, length us, event | category | flops | bytes accessed | tf_op | source)
XLA Modules:
  0.0 45.9 jit_solution(15453226015822433920)
XLA Ops:
  0.0 0.0 copy-start
  0.0 3.4 %copy-done = bf16[128,32,1024]{2,1,0:T(8,128)(2,1)S(1)} copy-done((bf16[128,32,1024]{2,1,0:T(8,128)(2,1)S(1)}, bf16[128,32,1024]{2,1,0:T(8,128)(2,1)}, u32[]{:S(2)}) %copy-start) | copy-done | bytes 8388632
  3.4 0.0 copy-start.1
  3.4 0.9 %copy-done.1 = bf16[1024,64]{0,1:T(8,128)(2,1)S(1)} copy-done((bf16[1024,64]{0,1:T(8,128)(2,1)S(1)}, bf16[1024,64]{0,1:T(8,128)(2,1)}, u32[]{:S(2)}) %copy-start.1) | copy-done | bytes 131096
  4.3 0.0 copy-start.2
  4.3 4.0 %contract.1 = (bf16[128,1024]{1,0:T(8,128)(2,1)S(1)}, bf16[128,1024]{1,0:T(8,128)(2,1)S(1)}) custom-call(bf16[4096,1024]{1,0:T(8,128)(2,1)S(1)} %bitcast.3, bf16[64,1024]{1,0:T(8,128)(2,1)S(1)} %bitcast.4), custom_call_target="tpu_custom_call" | custom-call | tf_op jit(solution)/shard_map/contract/pallas_call | solution.py:88
  8.3 0.5 %collective-permute-start = (bf16[128,1024]{1,0:T(8,128)(2,1)S(1)}, bf16[128,1024]{1,0:T(8,128)(2,1)S(1)}, u32[]{:S(2)}, u32[]{:S(2)}) collective-permute-start(bf16[128,1024]{1,0:T(8,128)(2,1)S(1)} %get-tuple-element.10), channel_id=1, source_target_pairs={{0,1},{1,0},{2,3},{3,2},{4,5},{5,4},{6,7},{7,6},{8,9},{9,8},{10,11... | collective-permute-start | bytes 786440 | tf_op jit(solution)/shard_map/ppermute | solution.py:273
  8.8 1.2 %collective-permute-done.got_ref = bf16[128,1024]{1,0:T(8,128)(2,1)S(1)} collective-permute-done((bf16[128,1024]{1,0:T(8,128)(2,1)S(1)}, bf16[128,1024]{1,0:T(8,128)(2,1)S(1)}, u32[]{:S(2)}, u32[]{:S(2)}) %collective-permute-start) | collective-permute-done | bytes 262176 | tf_op jit(solution)/shard_map/ppermute | solution.py:273
  9.9 0.0 copy-done.2
  9.9 0.2 project.1
  10.2 2.7 %collective-permute-start.1 = (bf16[256,128]{1,0:T(8,128)(2,1)S(1)}, bf16[256,128]{1,0:T(8,128)(2,1)S(1)}, u32[]{:S(2)}, u32[]{:S(2)}) collective-permute-start(bf16[256,128]{1,0:T(8,128)(2,1)S(1)} %get-tuple-element.12), channel_id=1, source_target_pairs={{0,3},{1,2},{2,1},{3,0},{4,7},{5,6},{6,5},{7,4},{8,11},{9,10},{10,... | collective-permute-start | bytes 196616 | tf_op jit(solution)/shard_map/ppermute | solution.py:273
  12.9 2.2 %collective-permute-done.1.got_ref = bf16[256,128]{1,0:T(8,128)(2,1)S(1)} collective-permute-done((bf16[256,128]{1,0:T(8,128)(2,1)S(1)}, bf16[256,128]{1,0:T(8,128)(2,1)S(1)}, u32[]{:S(2)}, u32[]{:S(2)}) %collective-permute-start.1) | collective-permute-done | bytes 65568 | tf_op jit(solution)/shard_map/ppermute | solution.py:273
  15.0 2.0 %collective-permute-start.2 = (bf16[256,128]{1,0:T(8,128)(2,1)S(1)}, bf16[256,128]{1,0:T(8,128)(2,1)S(1)}, u32[]{:S(2)}, u32[]{:S(2)}) collective-permute-start(bf16[256,128]{1,0:T(8,128)(2,1)S(1)} %add.5.mine_ref), channel_id=1, source_target_pairs={{0,5},{1,4},{2,7},{3,6},{4,1},{5,0},{6,3},{7,2},{8,13},{9,12},{10,... | collective-permute-start | bytes 196616 | tf_op jit(solution)/shard_map/ppermute | solution.py:273
  17.1 2.2 %collective-permute-done.2.got_ref = bf16[256,128]{1,0:T(8,128)(2,1)S(1)} collective-permute-done((bf16[256,128]{1,0:T(8,128)(2,1)S(1)}, bf16[256,128]{1,0:T(8,128)(2,1)S(1)}, u32[]{:S(2)}, u32[]{:S(2)}) %collective-permute-start.2) | collective-permute-done | bytes 65568 | tf_op jit(solution)/shard_map/ppermute | solution.py:273
  19.3 3.0 %collective-permute-start.3 = (bf16[256,128]{1,0:T(8,128)(2,1)S(1)}, bf16[256,128]{1,0:T(8,128)(2,1)S(1)}, u32[]{:S(2)}, u32[]{:S(2)}) collective-permute-start(bf16[256,128]{1,0:T(8,128)(2,1)S(1)} %add.6.mine_ref), channel_id=1, source_target_pairs={{0,9},{1,8},{2,11},{3,10},{4,13},{5,12},{6,15},{7,14},{8,1},{9,0},... | collective-permute-start | bytes 196616 | tf_op jit(solution)/shard_map/ppermute | solution.py:273
  22.2 2.2 %collective-permute-done.3.got_ref = bf16[256,128]{1,0:T(8,128)(2,1)S(1)} collective-permute-done((bf16[256,128]{1,0:T(8,128)(2,1)S(1)}, bf16[256,128]{1,0:T(8,128)(2,1)S(1)}, u32[]{:S(2)}, u32[]{:S(2)}) %collective-permute-start.3) | collective-permute-done | bytes 65568 | tf_op jit(solution)/shard_map/ppermute | solution.py:273
  24.4 3.2 %collective-permute-start.4 = (bf16[256,128]{1,0:T(8,128)(2,1)S(1)}, bf16[256,128]{1,0:T(8,128)(2,1)S(1)}, u32[]{:S(2)}, u32[]{:S(2)}) collective-permute-start(bf16[256,128]{1,0:T(8,128)(2,1)S(1)} %add.7.mine_ref), channel_id=1, source_target_pairs={{0,3},{1,2},{2,1},{3,0},{4,7},{5,6},{6,5},{7,4},{8,11},{9,10},{10,... | collective-permute-start | bytes 196616 | tf_op jit(solution)/shard_map/ppermute | solution.py:273
  27.6 2.0 %collective-permute-done.4.other_ref = bf16[256,128]{1,0:T(8,128)(2,1)S(1)} collective-permute-done((bf16[256,128]{1,0:T(8,128)(2,1)S(1)}, bf16[256,128]{1,0:T(8,128)(2,1)S(1)}, u32[]{:S(2)}, u32[]{:S(2)}) %collective-permute-start.4) | collective-permute-done | bytes 65568 | tf_op jit(solution)/shard_map/ppermute | solution.py:273
  29.6 0.4 product_terms.1.term_ref
  30.0 0.1 collective-permute-start.5
  30.0 1.2 %collective-permute-done.5.got_ref.got_term_ref = bf16[64,128]{1,0:T(8,128)(2,1)S(1)} collective-permute-done((bf16[64,128]{1,0:T(8,128)(2,1)S(1)}, bf16[64,128]{1,0:T(8,128)(2,1)S(1)}, u32[]{:S(2)}, u32[]{:S(2)}) %collective-permute-start.5) | collective-permute-done | bytes 16416 | tf_op jit(solution)/shard_map/ppermute | solution.py:273
  31.2 0.4 local_gram.1.mine_ref
  31.6 1.8 %collective-permute-start.6 = (f32[32,128]{1,0:T(8,128)S(1)}, f32[32,128]{1,0:T(8,128)S(1)}, u32[]{:S(2)}, u32[]{:S(2)}) collective-permute-start(f32[32,128]{1,0:T(8,128)S(1)} %local_gram.1.mine_ref), channel_id=1, source_target_pairs={{0,3},{1,2},{2,1},{3,0},{4,7},{5,6},{6,5},{7,4},{8,11},{9,10},{10,... | collective-permute-start | bytes 49160 | tf_op jit(solution)/shard_map/ppermute | solution.py:273
  33.4 1.4 %collective-permute-done.6.got_ref = f32[32,128]{1,0:T(8,128)S(1)} collective-permute-done((f32[32,128]{1,0:T(8,128)S(1)}, f32[32,128]{1,0:T(8,128)S(1)}, u32[]{:S(2)}, u32[]{:S(2)}) %collective-permute-start.6) | collective-permute-done | bytes 16416 | tf_op jit(solution)/shard_map/ppermute | solution.py:273
  34.8 1.7 %collective-permute-start.7 = (f32[32,128]{1,0:T(8,128)S(1)}, f32[32,128]{1,0:T(8,128)S(1)}, u32[]{:S(2)}, u32[]{:S(2)}) collective-permute-start(f32[32,128]{1,0:T(8,128)S(1)} %add.8.mine_ref), channel_id=1, source_target_pairs={{0,5},{1,4},{2,7},{3,6},{4,1},{5,0},{6,3},{7,2},{8,13},{9,12},{10,... | collective-permute-start | bytes 49160 | tf_op jit(solution)/shard_map/ppermute | solution.py:273
  36.5 1.5 %collective-permute-done.7.got_ref = f32[32,128]{1,0:T(8,128)S(1)} collective-permute-done((f32[32,128]{1,0:T(8,128)S(1)}, f32[32,128]{1,0:T(8,128)S(1)}, u32[]{:S(2)}, u32[]{:S(2)}) %collective-permute-start.7) | collective-permute-done | bytes 16416 | tf_op jit(solution)/shard_map/ppermute | solution.py:273
  38.0 3.2 %collective-permute-start.8 = (f32[32,128]{1,0:T(8,128)S(1)}, f32[32,128]{1,0:T(8,128)S(1)}, u32[]{:S(2)}, u32[]{:S(2)}) collective-permute-start(f32[32,128]{1,0:T(8,128)S(1)} %add.9.gram_ref), channel_id=1, source_target_pairs={{0,9},{1,8},{2,11},{3,10},{4,13},{5,12},{6,15},{7,14},{8,1},{9,0},... | collective-permute-start | bytes 49160 | tf_op jit(solution)/shard_map/ppermute | solution.py:273
  41.1 1.4 %collective-permute-done.8.got_gram_ref = f32[32,128]{1,0:T(8,128)S(1)} collective-permute-done((f32[32,128]{1,0:T(8,128)S(1)}, f32[32,128]{1,0:T(8,128)S(1)}, u32[]{:S(2)}, u32[]{:S(2)}) %collective-permute-start.8) | collective-permute-done | bytes 16416 | tf_op jit(solution)/shard_map/ppermute | solution.py:273
  42.6 3.3 %finish.1 = f32[64,64]{1,0:T(8,128)} custom-call(bf16[64,128]{1,0:T(8,128)(2,1)S(1)} %product_terms.1.term_ref, bf16[64,128]{1,0:T(8,128)(2,1)S(1)} %collective-permute-done.5.got_ref.got_term_ref, f32[32,128]{1,0:T(8,128)S(1)} %add.9.gram_ref, f32[32,128]{1,0:T(8,128)S(1)} %collective-permute-done.8.got_gram_ref), custom_call_target="tpu_custom_call" | custom-call | tf_op jit(solution)/shard_map/finish/pallas_call | solution.py:254
  (5 shorter events, 0.1 us)
Async XLA Ops:
  0.0 3.4 %copy-start = (bf16[128,32,1024]{2,1,0:T(8,128)(2,1)S(1)}, bf16[128,32,1024]{2,1,0:T(8,128)(2,1)}, u32[]{:S(2)}) copy-start(bf16[128,32,1024]{2,1,0:T(8,128)(2,1)} %param.3) | copy-start | bytes 25165828
  3.4 0.9 %copy-start.1 = (bf16[1024,64]{0,1:T(8,128)(2,1)S(1)}, bf16[1024,64]{0,1:T(8,128)(2,1)}, u32[]{:S(2)}) copy-start(bf16[1024,64]{0,1:T(8,128)(2,1)} %param.4) | copy-start | bytes 393220
  4.3 5.6 %copy-start.2 = (bf16[128,64]{0,1:T(8,128)(2,1)S(1)}, bf16[128,64]{0,1:T(8,128)(2,1)}, u32[]{:S(2)}) copy-start(bf16[128,64]{0,1:T(8,128)(2,1)} %param.5) | copy-start | bytes 49156
  8.3 1.7 %collective-permute-start = (bf16[128,1024]{1,0:T(8,128)(2,1)S(1)}, bf16[128,1024]{1,0:T(8,128)(2,1)S(1)}, u32[]{:S(2)}, u32[]{:S(2)}) collective-permute-start(bf16[128,1024]{1,0:T(8,128)(2,1)S(1)} %get-tuple-element.10), channel_id=1, source_target_pairs={{0,1},{1,0},{2,3},{3,2},{4,5},{5,4},{6,7},{7,6},{8,9},{9,8},{10,11... | collective-permute-start | bytes 786440 | tf_op jit(solution)/shard_map/ppermute | solution.py:273
  10.2 4.9 %collective-permute-start.1 = (bf16[256,128]{1,0:T(8,128)(2,1)S(1)}, bf16[256,128]{1,0:T(8,128)(2,1)S(1)}, u32[]{:S(2)}, u32[]{:S(2)}) collective-permute-start(bf16[256,128]{1,0:T(8,128)(2,1)S(1)} %get-tuple-element.12), channel_id=1, source_target_pairs={{0,3},{1,2},{2,1},{3,0},{4,7},{5,6},{6,5},{7,4},{8,11},{9,10},{10,... | collective-permute-start | bytes 196616 | tf_op jit(solution)/shard_map/ppermute | solution.py:273
  15.0 4.2 %collective-permute-start.2 = (bf16[256,128]{1,0:T(8,128)(2,1)S(1)}, bf16[256,128]{1,0:T(8,128)(2,1)S(1)}, u32[]{:S(2)}, u32[]{:S(2)}) collective-permute-start(bf16[256,128]{1,0:T(8,128)(2,1)S(1)} %add.5.mine_ref), channel_id=1, source_target_pairs={{0,5},{1,4},{2,7},{3,6},{4,1},{5,0},{6,3},{7,2},{8,13},{9,12},{10,... | collective-permute-start | bytes 196616 | tf_op jit(solution)/shard_map/ppermute | solution.py:273
  19.3 5.2 %collective-permute-start.3 = (bf16[256,128]{1,0:T(8,128)(2,1)S(1)}, bf16[256,128]{1,0:T(8,128)(2,1)S(1)}, u32[]{:S(2)}, u32[]{:S(2)}) collective-permute-start(bf16[256,128]{1,0:T(8,128)(2,1)S(1)} %add.6.mine_ref), channel_id=1, source_target_pairs={{0,9},{1,8},{2,11},{3,10},{4,13},{5,12},{6,15},{7,14},{8,1},{9,0},... | collective-permute-start | bytes 196616 | tf_op jit(solution)/shard_map/ppermute | solution.py:273
  24.4 5.2 %collective-permute-start.4 = (bf16[256,128]{1,0:T(8,128)(2,1)S(1)}, bf16[256,128]{1,0:T(8,128)(2,1)S(1)}, u32[]{:S(2)}, u32[]{:S(2)}) collective-permute-start(bf16[256,128]{1,0:T(8,128)(2,1)S(1)} %add.7.mine_ref), channel_id=1, source_target_pairs={{0,3},{1,2},{2,1},{3,0},{4,7},{5,6},{6,5},{7,4},{8,11},{9,10},{10,... | collective-permute-start | bytes 196616 | tf_op jit(solution)/shard_map/ppermute | solution.py:273
  30.0 1.2 %collective-permute-start.5 = (bf16[64,128]{1,0:T(8,128)(2,1)S(1)}, bf16[64,128]{1,0:T(8,128)(2,1)S(1)}, u32[]{:S(2)}, u32[]{:S(2)}) collective-permute-start(bf16[64,128]{1,0:T(8,128)(2,1)S(1)} %product_terms.1.term_ref), channel_id=1, source_target_pairs={{0,1},{1,0},{2,3},{3,2},{4,5},{5,4},{6,7},{7,6},{8,9},{9,8},{10,11... | collective-permute-start | bytes 49160 | tf_op jit(solution)/shard_map/ppermute | solution.py:273
  31.6 3.2 %collective-permute-start.6 = (f32[32,128]{1,0:T(8,128)S(1)}, f32[32,128]{1,0:T(8,128)S(1)}, u32[]{:S(2)}, u32[]{:S(2)}) collective-permute-start(f32[32,128]{1,0:T(8,128)S(1)} %local_gram.1.mine_ref), channel_id=1, source_target_pairs={{0,3},{1,2},{2,1},{3,0},{4,7},{5,6},{6,5},{7,4},{8,11},{9,10},{10,... | collective-permute-start | bytes 49160 | tf_op jit(solution)/shard_map/ppermute | solution.py:273
  34.8 3.2 %collective-permute-start.7 = (f32[32,128]{1,0:T(8,128)S(1)}, f32[32,128]{1,0:T(8,128)S(1)}, u32[]{:S(2)}, u32[]{:S(2)}) collective-permute-start(f32[32,128]{1,0:T(8,128)S(1)} %add.8.mine_ref), channel_id=1, source_target_pairs={{0,5},{1,4},{2,7},{3,6},{4,1},{5,0},{6,3},{7,2},{8,13},{9,12},{10,... | collective-permute-start | bytes 49160 | tf_op jit(solution)/shard_map/ppermute | solution.py:273
  38.0 4.6 %collective-permute-start.8 = (f32[32,128]{1,0:T(8,128)S(1)}, f32[32,128]{1,0:T(8,128)S(1)}, u32[]{:S(2)}, u32[]{:S(2)}) collective-permute-start(f32[32,128]{1,0:T(8,128)S(1)} %add.9.gram_ref), channel_id=1, source_target_pairs={{0,9},{1,8},{2,11},{3,10},{4,13},{5,12},{6,15},{7,14},{8,1},{9,0},... | collective-permute-start | bytes 49160 | tf_op jit(solution)/shard_map/ppermute | solution.py:273

commit v12 on v11

--- a/solution.py
+++ b/solution.py
@@ -29,7 +29,9 @@
     return lax.rem(half, 2)
 
 
-def contract_kernel(step, fibers, snapshot_ref, mode2_ref, send_ref, own_ref, even_ref, odd_ref):
+def contract_kernel(
+    step, fibers, ahead, snapshot_ref, mode2_ref, send_ref, own_ref, slab_ref, even_ref, odd_ref, sems
+):
     rank, depth = mode2_ref.shape
     tile = 8
     reps = LANES // rank
@@ -37,6 +39,13 @@
     blocks = step // tile
     out_rows = block // reps
     chunks = snapshot_ref.shape[0] // (step * fibers)
+
+    def copy(chunk):
+        where = pl.ds(chunk * step * fibers, step * fibers)
+        return pltpu.make_async_copy(snapshot_ref.at[where], slab_ref.at[where], sems.at[chunk])
+
+    for chunk in range(ahead):
+        copy(chunk).start()
     wide = jnp.concatenate([mode2_ref[...]] * reps, axis=0)
     lane = lax.broadcasted_iota(jnp.int32, (block, LANES), 1)
     to = lax.broadcasted_iota(jnp.int32, (out_rows, reps * block), 0)
@@ -49,8 +58,16 @@
     pairs = fibers // reps
 
     def multiply(chunk, flat_ref):
-        x = snapshot_ref[pl.ds(chunk * step * fibers, step * fibers), :]
-        flat_ref[...] = dot_f32(x, wide, ((1,), (1,))).astype(BF16)
+        copy(chunk).wait()
+
+        @pl.when(chunk + ahead < chunks)
+        def _():
+            copy(chunk + ahead).start()
+
+        rows = pl.ds(chunk * step * fibers, step * fibers)
+        low = dot_f32(slab_ref[rows, :depth // 2], wide[:, :depth // 2], ((1,), (1,)))
+        high = dot_f32(slab_ref[rows, depth // 2:], wide[:, depth // 2:], ((1,), (1,)))
+        flat_ref[...] = (low + high).astype(BF16)
 
     def spread(chunk, flat_ref):
         rows = pl.ds(pl.multiple_of(chunk * step, step), step)
@@ -86,14 +103,19 @@
     step = 16
     out = jax.ShapeDtypeStruct((cells, fibers // 2 * rank), BF16)
     return pl.pallas_call(
-        functools.partial(contract_kernel, step, fibers),
+        functools.partial(contract_kernel, step, fibers, 3),
         in_specs=[
-            pl.BlockSpec(memory_space=pltpu.VMEM),
+            pl.BlockSpec(memory_space=pltpu.HBM),
             pl.BlockSpec(memory_space=pltpu.VMEM),
         ],
         out_shape=[out, out],
-        scratch_shapes=[pltpu.VMEM((step * fibers, LANES), BF16)] * 2,
-        compiler_params=params(24),
+        scratch_shapes=[
+            pltpu.VMEM((cells * fibers, depth), BF16),
+            pltpu.VMEM((step * fibers, LANES), BF16),
+            pltpu.VMEM((step * fibers, LANES), BF16),
+            pltpu.SemaphoreType.DMA((cells // step,)),
+        ],
+        compiler_params=params(50),
         name="contract",
     )(snapshot.reshape(cells * fibers, depth), mode2_t)
 

time: 46 us -> 45.8 us (level)
  local copies, waits for them, and re-layouts: 4.29 us -> 0.91 us
  Pallas kernels: 8.29 us -> 11.4 us
    unnamed x6 -> x4, local copies, waits for them, and re-layouts: 4.29 us -> 0.91 us
    pallas_call x1, Pallas kernels: 3.96 us -> 7.12 us  [contract(): pl.pallas_call(functools.partial(contract_kernel, step, fibers, 3), in_sp...]
where the time goes in v12:
time: 45.8 us; the launch traced here: 45.7 us
  starting transfers between devices  18.1 us (40%)
  waiting for transfers between devices  15.2 us (33%)
  Pallas kernels  11.4 us (25%)
  local copies, waits for them, and re-layouts  0.91 us (2%)
    ppermute x9, starting transfers between devices, swap(): return lax.ppermute(x, ('row', 'col'), pairs)  18.1 us
    ppermute x9, waiting for transfers between devices, swap(): return lax.ppermute(x, ('row', 'col'), pairs)  15.2 us
    pallas_call x1, Pallas kernels, contract(): pl.pallas_call(functools.partial(contract_kernel, step, fibers, 3), in_sp...  7.12 us
    pallas_call x1, Pallas kernels, finish(): pl.pallas_call(functools.partial(finish_kernel, total_rows), out_shape=ja...  3.29 us
  transfers between devices with their start and end apart: 9, of which 9 were waited for; matrix products, arithmetic and copies ran while one was open for 0% of the time, Pallas kernels for 0%

profile of v12, /device:TPU:0, one launch (start us, length us, event | category | flops | bytes accessed | tf_op | source)
XLA Modules:
  0.0 45.7 jit_solution(2748818037213693067)
XLA Ops:
  0.0 0.0 copy-start
  0.0 0.9 %copy-done = bf16[1024,64]{0,1:T(8,128)(2,1)S(1)} copy-done((bf16[1024,64]{0,1:T(8,128)(2,1)S(1)}, bf16[1024,64]{0,1:T(8,128)(2,1)}, u32[]{:S(2)}) %copy-start) | copy-done | bytes 131096
  0.9 0.0 copy-start.1
  0.9 7.1 %contract.1 = (bf16[128,1024]{1,0:T(8,128)(2,1)S(1)}, bf16[128,1024]{1,0:T(8,128)(2,1)S(1)}) custom-call(bf16[4096,1024]{1,0:T(8,128)(2,1)} %bitcast.5, bf16[64,1024]{1,0:T(8,128)(2,1)S(1)} %bitcast.3), custom_call_target="tpu_custom_call" | custom-call | tf_op jit(solution)/shard_map/contract/pallas_call | solution.py:105
  8.0 0.5 %collective-permute-start = (bf16[128,1024]{1,0:T(8,128)(2,1)S(1)}, bf16[128,1024]{1,0:T(8,128)(2,1)S(1)}, u32[]{:S(2)}, u32[]{:S(2)}) collective-permute-start(bf16[128,1024]{1,0:T(8,128)(2,1)S(1)} %get-tuple-element.10), channel_id=1, source_target_pairs={{0,1},{1,0},{2,3},{3,2},{4,5},{5,4},{6,7},{7,6},{8,9},{9,8},{10,11... | collective-permute-start | bytes 786440 | tf_op jit(solution)/shard_map/ppermute | solution.py:295
  8.6 1.2 %collective-permute-done.got_ref = bf16[128,1024]{1,0:T(8,128)(2,1)S(1)} collective-permute-done((bf16[128,1024]{1,0:T(8,128)(2,1)S(1)}, bf16[128,1024]{1,0:T(8,128)(2,1)S(1)}, u32[]{:S(2)}, u32[]{:S(2)}) %collective-permute-start) | collective-permute-done | bytes 262176 | tf_op jit(solution)/shard_map/ppermute | solution.py:295
  9.7 0.0 copy-done.1
  9.7 0.2 project.1
  9.9 2.7 %collective-permute-start.1 = (bf16[256,128]{1,0:T(8,128)(2,1)S(1)}, bf16[256,128]{1,0:T(8,128)(2,1)S(1)}, u32[]{:S(2)}, u32[]{:S(2)}) collective-permute-start(bf16[256,128]{1,0:T(8,128)(2,1)S(1)} %get-tuple-element.12), channel_id=1, source_target_pairs={{0,3},{1,2},{2,1},{3,0},{4,7},{5,6},{6,5},{7,4},{8,11},{9,10},{10,... | collective-permute-start | bytes 196616 | tf_op jit(solution)/shard_map/ppermute | solution.py:295
  12.6 2.2 %collective-permute-done.1.got_ref = bf16[256,128]{1,0:T(8,128)(2,1)S(1)} collective-permute-done((bf16[256,128]{1,0:T(8,128)(2,1)S(1)}, bf16[256,128]{1,0:T(8,128)(2,1)S(1)}, u32[]{:S(2)}, u32[]{:S(2)}) %collective-permute-start.1) | collective-permute-done | bytes 65568 | tf_op jit(solution)/shard_map/ppermute | solution.py:295
  14.8 2.0 %collective-permute-start.2 = (bf16[256,128]{1,0:T(8,128)(2,1)S(1)}, bf16[256,128]{1,0:T(8,128)(2,1)S(1)}, u32[]{:S(2)}, u32[]{:S(2)}) collective-permute-start(bf16[256,128]{1,0:T(8,128)(2,1)S(1)} %add.5.mine_ref), channel_id=1, source_target_pairs={{0,5},{1,4},{2,7},{3,6},{4,1},{5,0},{6,3},{7,2},{8,13},{9,12},{10,... | collective-permute-start | bytes 196616 | tf_op jit(solution)/shard_map/ppermute | solution.py:295
  16.9 2.2 %collective-permute-done.2.got_ref = bf16[256,128]{1,0:T(8,128)(2,1)S(1)} collective-permute-done((bf16[256,128]{1,0:T(8,128)(2,1)S(1)}, bf16[256,128]{1,0:T(8,128)(2,1)S(1)}, u32[]{:S(2)}, u32[]{:S(2)}) %collective-permute-start.2) | collective-permute-done | bytes 65568 | tf_op jit(solution)/shard_map/ppermute | solution.py:295
  19.0 3.0 %collective-permute-start.3 = (bf16[256,128]{1,0:T(8,128)(2,1)S(1)}, bf16[256,128]{1,0:T(8,128)(2,1)S(1)}, u32[]{:S(2)}, u32[]{:S(2)}) collective-permute-start(bf16[256,128]{1,0:T(8,128)(2,1)S(1)} %add.6.mine_ref), channel_id=1, source_target_pairs={{0,9},{1,8},{2,11},{3,10},{4,13},{5,12},{6,15},{7,14},{8,1},{9,0},... | collective-permute-start | bytes 196616 | tf_op jit(solution)/shard_map/ppermute | solution.py:295
  22.0 2.2 %collective-permute-done.3.got_ref = bf16[256,128]{1,0:T(8,128)(2,1)S(1)} collective-permute-done((bf16[256,128]{1,0:T(8,128)(2,1)S(1)}, bf16[256,128]{1,0:T(8,128)(2,1)S(1)}, u32[]{:S(2)}, u32[]{:S(2)}) %collective-permute-start.3) | collective-permute-done | bytes 65568 | tf_op jit(solution)/shard_map/ppermute | solution.py:295
  24.2 3.2 %collective-permute-start.4 = (bf16[256,128]{1,0:T(8,128)(2,1)S(1)}, bf16[256,128]{1,0:T(8,128)(2,1)S(1)}, u32[]{:S(2)}, u32[]{:S(2)}) collective-permute-start(bf16[256,128]{1,0:T(8,128)(2,1)S(1)} %add.7.mine_ref), channel_id=1, source_target_pairs={{0,3},{1,2},{2,1},{3,0},{4,7},{5,6},{6,5},{7,4},{8,11},{9,10},{10,... | collective-permute-start | bytes 196616 | tf_op jit(solution)/shard_map/ppermute | solution.py:295
  27.4 2.0 %collective-permute-done.4.other_ref = bf16[256,128]{1,0:T(8,128)(2,1)S(1)} collective-permute-done((bf16[256,128]{1,0:T(8,128)(2,1)S(1)}, bf16[256,128]{1,0:T(8,128)(2,1)S(1)}, u32[]{:S(2)}, u32[]{:S(2)}) %collective-permute-start.4) | collective-permute-done | bytes 65568 | tf_op jit(solution)/shard_map/ppermute | solution.py:295
  29.4 0.4 product_terms.1.term_ref
  29.7 0.1 collective-permute-start.5
  29.8 1.2 %collective-permute-done.5.got_ref.got_term_ref = bf16[64,128]{1,0:T(8,128)(2,1)S(1)} collective-permute-done((bf16[64,128]{1,0:T(8,128)(2,1)S(1)}, bf16[64,128]{1,0:T(8,128)(2,1)S(1)}, u32[]{:S(2)}, u32[]{:S(2)}) %collective-permute-start.5) | collective-permute-done | bytes 16416 | tf_op jit(solution)/shard_map/ppermute | solution.py:295
  31.0 0.4 local_gram.1.mine_ref
  31.4 1.8 %collective-permute-start.6 = (f32[32,128]{1,0:T(8,128)S(1)}, f32[32,128]{1,0:T(8,128)S(1)}, u32[]{:S(2)}, u32[]{:S(2)}) collective-permute-start(f32[32,128]{1,0:T(8,128)S(1)} %local_gram.1.mine_ref), channel_id=1, source_target_pairs={{0,3},{1,2},{2,1},{3,0},{4,7},{5,6},{6,5},{7,4},{8,11},{9,10},{10,... | collective-permute-start | bytes 49160 | tf_op jit(solution)/shard_map/ppermute | solution.py:295
  33.1 1.4 %collective-permute-done.6.got_ref = f32[32,128]{1,0:T(8,128)S(1)} collective-permute-done((f32[32,128]{1,0:T(8,128)S(1)}, f32[32,128]{1,0:T(8,128)S(1)}, u32[]{:S(2)}, u32[]{:S(2)}) %collective-permute-start.6) | collective-permute-done | bytes 16416 | tf_op jit(solution)/shard_map/ppermute | solution.py:295
  34.6 1.7 %collective-permute-start.7 = (f32[32,128]{1,0:T(8,128)S(1)}, f32[32,128]{1,0:T(8,128)S(1)}, u32[]{:S(2)}, u32[]{:S(2)}) collective-permute-start(f32[32,128]{1,0:T(8,128)S(1)} %add.8.mine_ref), channel_id=1, source_target_pairs={{0,5},{1,4},{2,7},{3,6},{4,1},{5,0},{6,3},{7,2},{8,13},{9,12},{10,... | collective-permute-start | bytes 49160 | tf_op jit(solution)/shard_map/ppermute | solution.py:295
  36.3 1.5 %collective-permute-done.7.got_ref = f32[32,128]{1,0:T(8,128)S(1)} collective-permute-done((f32[32,128]{1,0:T(8,128)S(1)}, f32[32,128]{1,0:T(8,128)S(1)}, u32[]{:S(2)}, u32[]{:S(2)}) %collective-permute-start.7) | collective-permute-done | bytes 16416 | tf_op jit(solution)/shard_map/ppermute | solution.py:295
  37.8 3.2 %collective-permute-start.8 = (f32[32,128]{1,0:T(8,128)S(1)}, f32[32,128]{1,0:T(8,128)S(1)}, u32[]{:S(2)}, u32[]{:S(2)}) collective-permute-start(f32[32,128]{1,0:T(8,128)S(1)} %add.9.gram_ref), channel_id=1, source_target_pairs={{0,9},{1,8},{2,11},{3,10},{4,13},{5,12},{6,15},{7,14},{8,1},{9,0},... | collective-permute-start | bytes 49160 | tf_op jit(solution)/shard_map/ppermute | solution.py:295
  40.9 1.4 %collective-permute-done.8.got_gram_ref = f32[32,128]{1,0:T(8,128)S(1)} collective-permute-done((f32[32,128]{1,0:T(8,128)S(1)}, f32[32,128]{1,0:T(8,128)S(1)}, u32[]{:S(2)}, u32[]{:S(2)}) %collective-permute-start.8) | collective-permute-done | bytes 16416 | tf_op jit(solution)/shard_map/ppermute | solution.py:295
  42.4 3.3 %finish.1 = f32[64,64]{1,0:T(8,128)} custom-call(bf16[64,128]{1,0:T(8,128)(2,1)S(1)} %product_terms.1.term_ref, bf16[64,128]{1,0:T(8,128)(2,1)S(1)} %collective-permute-done.5.got_ref.got_term_ref, f32[32,128]{1,0:T(8,128)S(1)} %add.9.gram_ref, f32[32,128]{1,0:T(8,128)S(1)} %collective-permute-done.8.got_gram_ref), custom_call_target="tpu_custom_call" | custom-call | tf_op jit(solution)/shard_map/finish/pallas_call | solution.py:276
  (5 shorter events, 0.1 us)
Async XLA Ops:
  0.0 0.9 %copy-start = (bf16[1024,64]{0,1:T(8,128)(2,1)S(1)}, bf16[1024,64]{0,1:T(8,128)(2,1)}, u32[]{:S(2)}) copy-start(bf16[1024,64]{0,1:T(8,128)(2,1)} %param.4) | copy-start | bytes 393220
  0.9 8.8 %copy-start.1 = (bf16[128,64]{0,1:T(8,128)(2,1)S(1)}, bf16[128,64]{0,1:T(8,128)(2,1)}, u32[]{:S(2)}) copy-start(bf16[128,64]{0,1:T(8,128)(2,1)} %param.5) | copy-start | bytes 49156
  8.0 1.7 %collective-permute-start = (bf16[128,1024]{1,0:T(8,128)(2,1)S(1)}, bf16[128,1024]{1,0:T(8,128)(2,1)S(1)}, u32[]{:S(2)}, u32[]{:S(2)}) collective-permute-start(bf16[128,1024]{1,0:T(8,128)(2,1)S(1)} %get-tuple-element.10), channel_id=1, source_target_pairs={{0,1},{1,0},{2,3},{3,2},{4,5},{5,4},{6,7},{7,6},{8,9},{9,8},{10,11... | collective-permute-start | bytes 786440 | tf_op jit(solution)/shard_map/ppermute | solution.py:295
  9.9 4.9 %collective-permute-start.1 = (bf16[256,128]{1,0:T(8,128)(2,1)S(1)}, bf16[256,128]{1,0:T(8,128)(2,1)S(1)}, u32[]{:S(2)}, u32[]{:S(2)}) collective-permute-start(bf16[256,128]{1,0:T(8,128)(2,1)S(1)} %get-tuple-element.12), channel_id=1, source_target_pairs={{0,3},{1,2},{2,1},{3,0},{4,7},{5,6},{6,5},{7,4},{8,11},{9,10},{10,... | collective-permute-start | bytes 196616 | tf_op jit(solution)/shard_map/ppermute | solution.py:295
  14.8 4.2 %collective-permute-start.2 = (bf16[256,128]{1,0:T(8,128)(2,1)S(1)}, bf16[256,128]{1,0:T(8,128)(2,1)S(1)}, u32[]{:S(2)}, u32[]{:S(2)}) collective-permute-start(bf16[256,128]{1,0:T(8,128)(2,1)S(1)} %add.5.mine_ref), channel_id=1, source_target_pairs={{0,5},{1,4},{2,7},{3,6},{4,1},{5,0},{6,3},{7,2},{8,13},{9,12},{10,... | collective-permute-start | bytes 196616 | tf_op jit(solution)/shard_map/ppermute | solution.py:295
  19.0 5.2 %collective-permute-start.3 = (bf16[256,128]{1,0:T(8,128)(2,1)S(1)}, bf16[256,128]{1,0:T(8,128)(2,1)S(1)}, u32[]{:S(2)}, u32[]{:S(2)}) collective-permute-start(bf16[256,128]{1,0:T(8,128)(2,1)S(1)} %add.6.mine_ref), channel_id=1, source_target_pairs={{0,9},{1,8},{2,11},{3,10},{4,13},{5,12},{6,15},{7,14},{8,1},{9,0},... | collective-permute-start | bytes 196616 | tf_op jit(solution)/shard_map/ppermute | solution.py:295
  24.2 5.1 %collective-permute-start.4 = (bf16[256,128]{1,0:T(8,128)(2,1)S(1)}, bf16[256,128]{1,0:T(8,128)(2,1)S(1)}, u32[]{:S(2)}, u32[]{:S(2)}) collective-permute-start(bf16[256,128]{1,0:T(8,128)(2,1)S(1)} %add.7.mine_ref), channel_id=1, source_target_pairs={{0,3},{1,2},{2,1},{3,0},{4,7},{5,6},{6,5},{7,4},{8,11},{9,10},{10,... | collective-permute-start | bytes 196616 | tf_op jit(solution)/shard_map/ppermute | solution.py:295
  29.7 1.2 %collective-permute-start.5 = (bf16[64,128]{1,0:T(8,128)(2,1)S(1)}, bf16[64,128]{1,0:T(8,128)(2,1)S(1)}, u32[]{:S(2)}, u32[]{:S(2)}) collective-permute-start(bf16[64,128]{1,0:T(8,128)(2,1)S(1)} %product_terms.1.term_ref), channel_id=1, source_target_pairs={{0,1},{1,0},{2,3},{3,2},{4,5},{5,4},{6,7},{7,6},{8,9},{9,8},{10,11... | collective-permute-start | bytes 49160 | tf_op jit(solution)/shard_map/ppermute | solution.py:295
  31.4 3.2 %collective-permute-start.6 = (f32[32,128]{1,0:T(8,128)S(1)}, f32[32,128]{1,0:T(8,128)S(1)}, u32[]{:S(2)}, u32[]{:S(2)}) collective-permute-start(f32[32,128]{1,0:T(8,128)S(1)} %local_gram.1.mine_ref), channel_id=1, source_target_pairs={{0,3},{1,2},{2,1},{3,0},{4,7},{5,6},{6,5},{7,4},{8,11},{9,10},{10,... | collective-permute-start | bytes 49160 | tf_op jit(solution)/shard_map/ppermute | solution.py:295
  34.6 3.2 %collective-permute-start.7 = (f32[32,128]{1,0:T(8,128)S(1)}, f32[32,128]{1,0:T(8,128)S(1)}, u32[]{:S(2)}, u32[]{:S(2)}) collective-permute-start(f32[32,128]{1,0:T(8,128)S(1)} %add.8.mine_ref), channel_id=1, source_target_pairs={{0,5},{1,4},{2,7},{3,6},{4,1},{5,0},{6,3},{7,2},{8,13},{9,12},{10,... | collective-permute-start | bytes 49160 | tf_op jit(solution)/shard_map/ppermute | solution.py:295
  37.8 4.6 %collective-permute-start.8 = (f32[32,128]{1,0:T(8,128)S(1)}, f32[32,128]{1,0:T(8,128)S(1)}, u32[]{:S(2)}, u32[]{:S(2)}) collective-permute-start(f32[32,128]{1,0:T(8,128)S(1)} %add.9.gram_ref), channel_id=1, source_target_pairs={{0,9},{1,8},{2,11},{3,10},{4,13},{5,12},{6,15},{7,14},{8,1},{9,0},... | collective-permute-start | bytes 49160 | tf_op jit(solution)/shard_map/ppermute | solution.py:295

commit v13 on v12

--- a/solution.py
+++ b/solution.py
@@ -120,40 +120,51 @@
     )(snapshot.reshape(cells * fibers, depth), mode2_t)
 
 
-def add_to(*refs):
-    total = refs[0][...].astype(F32)
-    for ref in refs[1:]:
-        total += ref[...].astype(F32)
-    return total
-
-
-def project_kernel(own_ref, got_ref, factor_ref, keep_ref, send_ref):
+def is_even():
+    return lax.rem(lax.axis_index("row"), 2) == 0
+
+
+def project_kernel(own_ref, got_ref, factor_ref, keep_ref, send_ref, mine_ref, give_ref):
     rank = factor_ref.shape[0]
-    factor = factor_ref[...]
-    total = dot_f32(factor, own_ref[...], ((1,), (0,))) + dot_f32(factor, got_ref[...], ((1,), (0,)))
-    even = lax.rem(lax.axis_index("row"), 2) == 0
-    blocks = total.shape[1] // LANES // 2
-    for block in range(blocks):
-        low = total[:, block * LANES:(block + 1) * LANES]
-        high = total[:, (block + blocks) * LANES:(block + blocks + 1) * LANES]
+    width = mine_ref.shape[1]
+    even = is_even()
+    halves = []
+    for start in (0, width):
+        where = slice(start, start + width)
+        halves.append(own_ref[:, where].astype(F32) + got_ref[:, where].astype(F32))
+    mine = jnp.where(even, halves[0], halves[1]).astype(BF16)
+    give = jnp.where(even, halves[1], halves[0]).astype(BF16)
+    mine_ref[...] = mine
+    give_ref[...] = give
+    keep = dot_f32(factor_ref[...], mine, ((1,), (0,)))
+    send = dot_f32(factor_ref[...], give, ((1,), (0,)))
+    for block in range(width // LANES):
+        where = slice(block * LANES, (block + 1) * LANES)
         rows = pl.ds(block * rank, rank)
-        keep_ref[rows, :] = jnp.where(even, low, high)
-        send_ref[rows, :] = jnp.where(even, high, low).astype(BF16)
+        keep_ref[rows, :] = keep[:, where]
+        send_ref[rows, :] = send[:, where].astype(BF16)
 
 
 def project(own, got, factor_t):
-    rank = factor_t.shape[0]
-    shape = (rank * own.shape[1] // LANES // 2, LANES)
+    cells, width = own.shape
+    rows = factor_t.shape[0] * width // LANES // 2
+    columns = jax.ShapeDtypeStruct((cells, width // 2), BF16)
     return pl.pallas_call(
         project_kernel,
-        out_shape=[jax.ShapeDtypeStruct(shape, F32), jax.ShapeDtypeStruct(shape, BF16)],
-        compiler_params=params(4),
+        out_shape=[
+            jax.ShapeDtypeStruct((rows, LANES), F32),
+            jax.ShapeDtypeStruct((rows, LANES), BF16),
+            columns,
+            columns,
+        ],
+        compiler_params=params(8),
         name="project",
     )(own, got, factor_t)
 
 
 def add_kernel(mine_ref, got_ref, out_ref):
-    out_ref[...] = add_to(mine_ref, got_ref).astype(out_ref.dtype)
+    total = mine_ref[...].astype(F32) + got_ref[...].astype(F32)
+    out_ref[...] = total.astype(out_ref.dtype)
 
 
 def add(mine, got):
@@ -165,36 +176,38 @@
     )(mine, got)
 
 
-def product_kernel(own_ref, got_ref, mine_ref, other_ref, out_ref):
-    cells, width = own_ref.shape
-    blocks = width // LANES // 2
-    rank = mine_ref.shape[0] // blocks
-    even = lax.rem(lax.axis_index("row"), 2) == 0
-    total = jnp.zeros((cells, rank), F32)
-    for block in range(blocks):
-        rows = pl.ds(block * rank, rank)
-        mine, other = mine_ref[rows, :], other_ref[rows, :]
-        low = jnp.where(even, mine, other)
-        high = jnp.where(even, other, mine)
-        for at, projected in ((block, low), (block + blocks, high)):
-            where = slice(at * LANES, (at + 1) * LANES)
-            total += dot_f32(own_ref[:, where], projected, ((1,), (1,)))
-            total += dot_f32(got_ref[:, where], projected, ((1,), (1,)))
-    half = cells // 2
-    out_ref[...] = jnp.concatenate([total[:half], total[half:]], axis=1).astype(BF16)
-
-
-def product_terms(own, got, mine, other):
+def product_kernel(mine_ref, got_ref, projected_ref, out_ref):
+    blocks = mine_ref.shape[1] // LANES
+    rank = projected_ref.shape[0] // blocks
+    terms = []
+    for ref in (mine_ref, got_ref):
+        total = jnp.zeros((ref.shape[0], rank), F32)
+        for block in range(blocks):
+            projected = projected_ref[pl.ds(block * rank, rank), :]
+            where = slice(block * LANES, (block + 1) * LANES)
+            total += dot_f32(ref[:, where], projected, ((1,), (1,)))
+        terms.append(total)
+    even = is_even()
+    low = jnp.where(even, terms[0], terms[1])
+    high = jnp.where(even, terms[1], terms[0])
+    out_ref[...] = jnp.concatenate([low, high], axis=1).astype(BF16)
+
+
+def product_terms(mine, got, projected):
     return pl.pallas_call(
         product_kernel,
-        out_shape=jax.ShapeDtypeStruct((own.shape[0] // 2, LANES), BF16),
+        out_shape=jax.ShapeDtypeStruct((mine.shape[0], LANES), BF16),
         compiler_params=params(4),
         name="product_terms",
-    )(own, got, mine, other)
+    )(mine, got, projected)
+
+
+def pair_product(term_ref, got_ref):
+    return term_ref[...].astype(F32) + got_ref[...].astype(F32)
 
 
 def gram_kernel(term_ref, got_ref, out_ref):
-    product = add_to(term_ref, got_ref)
+    product = pair_product(term_ref, got_ref)
     rank = LANES // 2
     wide = dot_f32(product, product, ((0,), (0,)), lax.Precision.HIGHEST)
     gram = wide[:rank, :rank] + wide[rank:, rank:]
@@ -267,15 +280,17 @@
     scale = total_rows ** 0.5
     inverse = jnp.concatenate([b * (lax.rsqrt(p) * scale) for b, p in zip(both, pivots)], axis=0)
     inverse = inverse[:, rank:]
-    product = add_to(term_ref, got_term_ref)
-    mine = jnp.where(lax.axis_index("col") == 0, product[:, :rank], product[:, rank:])
+    half = term_ref.shape[0] // 2
+    product = pair_product(term_ref, got_term_ref)
+    product = jnp.where(lax.axis_index("col") == 0, product[:half], product[half:])
+    mine = jnp.where(is_even(), product[:, :rank], product[:, rank:])
     out_ref[...] = dot_f32(mine, inverse, ((1,), (1,)), lax.Precision.HIGHEST)
 
 
 def finish(total_rows, term, got_term, gram, got_gram):
     return pl.pallas_call(
         functools.partial(finish_kernel, total_rows),
-        out_shape=jax.ShapeDtypeStruct((term.shape[0], LANES // 2), F32),
+        out_shape=jax.ShapeDtypeStruct((term.shape[0] // 2, LANES // 2), F32),
         compiler_params=params(4),
         name="finish",
     )(term, got_term, gram, got_gram)
@@ -297,16 +312,17 @@
     send, own = contract(snapshot, mode2_factor.T)
     got = swap(send, 0)
 
-    keep, send = project(own, got, old_factor.T)
+    keep, send, columns, give = project(own, got, old_factor.T)
     mine = add(keep, swap(send, masks[0]))
+    got_columns = swap(give, masks[0])
     for mask in masks[1:]:
         mine = add(mine, swap(mine, mask))
-    other = swap(mine, masks[0])
-
-    term = product_terms(own, got, mine, other)
-    got_term = swap(term, 0)
+
+    term = product_terms(columns, got_columns, mine)
+    term = add(term, swap(term, 0))
+    got_term = swap(term, masks[0])
     gram = local_gram(term, got_term)
-    for mask in masks[:-1]:
+    for mask in masks[1:-1]:
         gram = add(gram, swap(gram, mask))
     return finish(total_rows, term, got_term, gram, swap(gram, masks[-1]))
 

time: 45.8 us -> 42.2 us (0.921)
  starting transfers between devices: 18.1 us -> 14.4 us
    ppermute x9, starting transfers between devices: 18.1 us -> 14.4 us  [swap(): return lax.ppermute(x, ('row', 'col'), pairs)]
  transfers between devices with their start and end apart: 9 -> 9, of which waited for: 9 -> 8; matrix products, arithmetic and copies ran while one was open for 0% -> 0% of each run, Pallas kernels for 0% -> 0%
where the time goes in v13:
time: 42.2 us; the launch traced here: 42.1 us
  waiting for transfers between devices  15.3 us (36%)
  starting transfers between devices  14.4 us (34%)
  Pallas kernels  11.4 us (27%)
  local copies, waits for them, and re-layouts  0.91 us (2%)
    ppermute x9, waiting for transfers between devices, swap(): return lax.ppermute(x, ('row', 'col'), pairs)  15.3 us
    ppermute x9, starting transfers between devices, swap(): return lax.ppermute(x, ('row', 'col'), pairs)  14.4 us
    pallas_call x1, Pallas kernels, contract(): pl.pallas_call(functools.partial(contract_kernel, step, fibers, 3), in_sp...  7.12 us
    pallas_call x1, Pallas kernels, finish(): pl.pallas_call(functools.partial(finish_kernel, total_rows), out_shape=ja...  3.29 us
    unnamed x4, local copies, waits for them, and re-layouts  0.91 us
  transfers between devices with their start and end apart: 9, of which 8 were waited for; matrix products, arithmetic and copies ran while one was open for 0% of the time, Pallas kernels for 0%

profile of v13, /device:TPU:0, one launch (start us, length us, event | category | flops | bytes accessed | tf_op | source)
XLA Modules:
  0.0 42.1 jit_solution(13113143905392686150)
XLA Ops:
  0.0 0.0 copy-start
  0.0 0.9 %copy-done = bf16[1024,64]{0,1:T(8,128)(2,1)S(1)} copy-done((bf16[1024,64]{0,1:T(8,128)(2,1)S(1)}, bf16[1024,64]{0,1:T(8,128)(2,1)}, u32[]{:S(2)}) %copy-start) | copy-done | bytes 131096
  0.9 0.0 copy-start.1
  0.9 7.1 %contract.1 = (bf16[128,1024]{1,0:T(8,128)(2,1)S(1)}, bf16[128,1024]{1,0:T(8,128)(2,1)S(1)}) custom-call(bf16[4096,1024]{1,0:T(8,128)(2,1)} %bitcast.5, bf16[64,1024]{1,0:T(8,128)(2,1)S(1)} %bitcast.3), custom_call_target="tpu_custom_call" | custom-call | tf_op jit(solution)/shard_map/contract/pallas_call | solution.py:105
  8.0 0.5 %collective-permute-start = (bf16[128,1024]{1,0:T(8,128)(2,1)S(1)}, bf16[128,1024]{1,0:T(8,128)(2,1)S(1)}, u32[]{:S(2)}, u32[]{:S(2)}) collective-permute-start(bf16[128,1024]{1,0:T(8,128)(2,1)S(1)} %get-tuple-element.12), channel_id=1, source_target_pairs={{0,1},{1,0},{2,3},{3,2},{4,5},{5,4},{6,7},{7,6},{8,9},{9,8},{10,11... | collective-permute-start | bytes 786440 | tf_op jit(solution)/shard_map/ppermute | solution.py:310
  8.6 1.2 %collective-permute-done.got_ref = bf16[128,1024]{1,0:T(8,128)(2,1)S(1)} collective-permute-done((bf16[128,1024]{1,0:T(8,128)(2,1)S(1)}, bf16[128,1024]{1,0:T(8,128)(2,1)S(1)}, u32[]{:S(2)}, u32[]{:S(2)}) %collective-permute-start) | collective-permute-done | bytes 262176 | tf_op jit(solution)/shard_map/ppermute | solution.py:310
  9.7 0.0 copy-done.1
  9.7 0.2 project.1
  10.0 2.7 %collective-permute-start.2 = (bf16[256,128]{1,0:T(8,128)(2,1)S(1)}, bf16[256,128]{1,0:T(8,128)(2,1)S(1)}, u32[]{:S(2)}, u32[]{:S(2)}) collective-permute-start(bf16[256,128]{1,0:T(8,128)(2,1)S(1)} %get-tuple-element.16), channel_id=1, source_target_pairs={{0,3},{1,2},{2,1},{3,0},{4,7},{5,6},{6,5},{7,4},{8,11},{9,10},{10,... | collective-permute-start | bytes 196616 | tf_op jit(solution)/shard_map/ppermute | solution.py:310
  12.6 2.2 %collective-permute-done.2.got_ref = bf16[256,128]{1,0:T(8,128)(2,1)S(1)} collective-permute-done((bf16[256,128]{1,0:T(8,128)(2,1)S(1)}, bf16[256,128]{1,0:T(8,128)(2,1)S(1)}, u32[]{:S(2)}, u32[]{:S(2)}) %collective-permute-start.2) | collective-permute-done | bytes 65568 | tf_op jit(solution)/shard_map/ppermute | solution.py:310
  14.8 2.0 %collective-permute-start.3 = (bf16[256,128]{1,0:T(8,128)(2,1)S(1)}, bf16[256,128]{1,0:T(8,128)(2,1)S(1)}, u32[]{:S(2)}, u32[]{:S(2)}) collective-permute-start(bf16[256,128]{1,0:T(8,128)(2,1)S(1)} %add.5.mine_ref), channel_id=1, source_target_pairs={{0,5},{1,4},{2,7},{3,6},{4,1},{5,0},{6,3},{7,2},{8,13},{9,12},{10,... | collective-permute-start | bytes 196616 | tf_op jit(solution)/shard_map/ppermute | solution.py:310
  16.9 1.5 %collective-permute-start.1 = (bf16[128,512]{1,0:T(8,128)(2,1)S(1)}, bf16[128,512]{1,0:T(8,128)(2,1)S(1)}, u32[]{:S(2)}, u32[]{:S(2)}) collective-permute-start(bf16[128,512]{1,0:T(8,128)(2,1)S(1)} %get-tuple-element.14), channel_id=1, source_target_pairs={{0,3},{1,2},{2,1},{3,0},{4,7},{5,6},{6,5},{7,4},{8,11},{9,10},{10,... | collective-permute-start | bytes 393224 | tf_op jit(solution)/shard_map/ppermute | solution.py:310
  18.4 0.7 %collective-permute-done.3.got_ref = bf16[256,128]{1,0:T(8,128)(2,1)S(1)} collective-permute-done((bf16[256,128]{1,0:T(8,128)(2,1)S(1)}, bf16[256,128]{1,0:T(8,128)(2,1)S(1)}, u32[]{:S(2)}, u32[]{:S(2)}) %collective-permute-start.3) | collective-permute-done | bytes 65568 | tf_op jit(solution)/shard_map/ppermute | solution.py:310
  19.1 3.3 %collective-permute-start.4 = (bf16[256,128]{1,0:T(8,128)(2,1)S(1)}, bf16[256,128]{1,0:T(8,128)(2,1)S(1)}, u32[]{:S(2)}, u32[]{:S(2)}) collective-permute-start(bf16[256,128]{1,0:T(8,128)(2,1)S(1)} %add.6.mine_ref), channel_id=1, source_target_pairs={{0,9},{1,8},{2,11},{3,10},{4,13},{5,12},{6,15},{7,14},{8,1},{9,0},... | collective-permute-start | bytes 196616 | tf_op jit(solution)/shard_map/ppermute | solution.py:310
  22.3 3.8 %collective-permute-done.4.got_ref = bf16[256,128]{1,0:T(8,128)(2,1)S(1)} collective-permute-done((bf16[256,128]{1,0:T(8,128)(2,1)S(1)}, bf16[256,128]{1,0:T(8,128)(2,1)S(1)}, u32[]{:S(2)}, u32[]{:S(2)}) %collective-permute-start.4) | collective-permute-done | bytes 65568 | tf_op jit(solution)/shard_map/ppermute | solution.py:310
  26.2 0.0 collective-permute-done.1.got_ref
  26.2 0.3 product_terms.1.mine_ref
  26.5 0.2 collective-permute-start.5
  26.6 1.1 %collective-permute-done.5.got_ref = bf16[128,128]{1,0:T(8,128)(2,1)S(1)} collective-permute-done((bf16[128,128]{1,0:T(8,128)(2,1)S(1)}, bf16[128,128]{1,0:T(8,128)(2,1)S(1)}, u32[]{:S(2)}, u32[]{:S(2)}) %collective-permute-start.5) | collective-permute-done | bytes 32800 | tf_op jit(solution)/shard_map/ppermute | solution.py:310
  27.7 1.3 %collective-permute-start.6 = (bf16[128,128]{1,0:T(8,128)(2,1)S(1)}, bf16[128,128]{1,0:T(8,128)(2,1)S(1)}, u32[]{:S(2)}, u32[]{:S(2)}) collective-permute-start(bf16[128,128]{1,0:T(8,128)(2,1)S(1)} %add.8.term_ref), channel_id=1, source_target_pairs={{0,3},{1,2},{2,1},{3,0},{4,7},{5,6},{6,5},{7,4},{8,11},{9,10},{10,... | collective-permute-start | bytes 98312 | tf_op jit(solution)/shard_map/ppermute | solution.py:310
  29.0 2.1 %collective-permute-done.6.got_ref.got_term_ref = bf16[128,128]{1,0:T(8,128)(2,1)S(1)} collective-permute-done((bf16[128,128]{1,0:T(8,128)(2,1)S(1)}, bf16[128,128]{1,0:T(8,128)(2,1)S(1)}, u32[]{:S(2)}, u32[]{:S(2)}) %collective-permute-start.6) | collective-permute-done | bytes 32800 | tf_op jit(solution)/shard_map/ppermute | solution.py:310
  31.2 0.4 local_gram.1.mine_ref
  31.6 0.7 %collective-permute-start.7 = (f32[32,128]{1,0:T(8,128)S(1)}, f32[32,128]{1,0:T(8,128)S(1)}, u32[]{:S(2)}, u32[]{:S(2)}) collective-permute-start(f32[32,128]{1,0:T(8,128)S(1)} %local_gram.1.mine_ref), channel_id=1, source_target_pairs={{0,5},{1,4},{2,7},{3,6},{4,1},{5,0},{6,3},{7,2},{8,13},{9,12},{10,... | collective-permute-start | bytes 49160 | tf_op jit(solution)/shard_map/ppermute | solution.py:310
  32.3 2.4 %collective-permute-done.7.got_ref = f32[32,128]{1,0:T(8,128)S(1)} collective-permute-done((f32[32,128]{1,0:T(8,128)S(1)}, f32[32,128]{1,0:T(8,128)S(1)}, u32[]{:S(2)}, u32[]{:S(2)}) %collective-permute-start.7) | collective-permute-done | bytes 16416 | tf_op jit(solution)/shard_map/ppermute | solution.py:310
  34.7 2.2 %collective-permute-start.8 = (f32[32,128]{1,0:T(8,128)S(1)}, f32[32,128]{1,0:T(8,128)S(1)}, u32[]{:S(2)}, u32[]{:S(2)}) collective-permute-start(f32[32,128]{1,0:T(8,128)S(1)} %add.9.gram_ref), channel_id=1, source_target_pairs={{0,9},{1,8},{2,11},{3,10},{4,13},{5,12},{6,15},{7,14},{8,1},{9,0},... | collective-permute-start | bytes 49160 | tf_op jit(solution)/shard_map/ppermute | solution.py:310
  37.0 1.8 %collective-permute-done.8.got_gram_ref = f32[32,128]{1,0:T(8,128)S(1)} collective-permute-done((f32[32,128]{1,0:T(8,128)S(1)}, f32[32,128]{1,0:T(8,128)S(1)}, u32[]{:S(2)}, u32[]{:S(2)}) %collective-permute-start.8) | collective-permute-done | bytes 16416 | tf_op jit(solution)/shard_map/ppermute | solution.py:310
  38.8 3.3 %finish.1 = f32[64,64]{1,0:T(8,128)} custom-call(bf16[128,128]{1,0:T(8,128)(2,1)S(1)} %add.8.term_ref, bf16[128,128]{1,0:T(8,128)(2,1)S(1)} %collective-permute-done.6.got_ref.got_term_ref, f32[32,128]{1,0:T(8,128)S(1)} %add.9.gram_ref, f32[32,128]{1,0:T(8,128)S(1)} %collective-permute-done.8.got_gram_ref), custom_call_target="tpu_custom_call" | custom-call | tf_op jit(solution)/shard_map/finish/pallas_call | solution.py:291
  (5 shorter events, 0.1 us)
Async XLA Ops:
  0.0 0.9 %copy-start = (bf16[1024,64]{0,1:T(8,128)(2,1)S(1)}, bf16[1024,64]{0,1:T(8,128)(2,1)}, u32[]{:S(2)}) copy-start(bf16[1024,64]{0,1:T(8,128)(2,1)} %param.4) | copy-start | bytes 393220
  0.9 8.8 %copy-start.1 = (bf16[128,64]{0,1:T(8,128)(2,1)S(1)}, bf16[128,64]{0,1:T(8,128)(2,1)}, u32[]{:S(2)}) copy-start(bf16[128,64]{0,1:T(8,128)(2,1)} %param.5) | copy-start | bytes 49156
  8.0 1.7 %collective-permute-start = (bf16[128,1024]{1,0:T(8,128)(2,1)S(1)}, bf16[128,1024]{1,0:T(8,128)(2,1)S(1)}, u32[]{:S(2)}, u32[]{:S(2)}) collective-permute-start(bf16[128,1024]{1,0:T(8,128)(2,1)S(1)} %get-tuple-element.12), channel_id=1, source_target_pairs={{0,1},{1,0},{2,3},{3,2},{4,5},{5,4},{6,7},{7,6},{8,9},{9,8},{10,11... | collective-permute-start | bytes 786440 | tf_op jit(solution)/shard_map/ppermute | solution.py:310
  10.0 4.9 %collective-permute-start.2 = (bf16[256,128]{1,0:T(8,128)(2,1)S(1)}, bf16[256,128]{1,0:T(8,128)(2,1)S(1)}, u32[]{:S(2)}, u32[]{:S(2)}) collective-permute-start(bf16[256,128]{1,0:T(8,128)(2,1)S(1)} %get-tuple-element.16), channel_id=1, source_target_pairs={{0,3},{1,2},{2,1},{3,0},{4,7},{5,6},{6,5},{7,4},{8,11},{9,10},{10,... | collective-permute-start | bytes 196616 | tf_op jit(solution)/shard_map/ppermute | solution.py:310
  14.8 4.2 %collective-permute-start.3 = (bf16[256,128]{1,0:T(8,128)(2,1)S(1)}, bf16[256,128]{1,0:T(8,128)(2,1)S(1)}, u32[]{:S(2)}, u32[]{:S(2)}) collective-permute-start(bf16[256,128]{1,0:T(8,128)(2,1)S(1)} %add.5.mine_ref), channel_id=1, source_target_pairs={{0,5},{1,4},{2,7},{3,6},{4,1},{5,0},{6,3},{7,2},{8,13},{9,12},{10,... | collective-permute-start | bytes 196616 | tf_op jit(solution)/shard_map/ppermute | solution.py:310
  16.9 9.3 %collective-permute-start.1 = (bf16[128,512]{1,0:T(8,128)(2,1)S(1)}, bf16[128,512]{1,0:T(8,128)(2,1)S(1)}, u32[]{:S(2)}, u32[]{:S(2)}) collective-permute-start(bf16[128,512]{1,0:T(8,128)(2,1)S(1)} %get-tuple-element.14), channel_id=1, source_target_pairs={{0,3},{1,2},{2,1},{3,0},{4,7},{5,6},{6,5},{7,4},{8,11},{9,10},{10,... | collective-permute-start | bytes 393224 | tf_op jit(solution)/shard_map/ppermute | solution.py:310
  19.1 7.1 %collective-permute-start.4 = (bf16[256,128]{1,0:T(8,128)(2,1)S(1)}, bf16[256,128]{1,0:T(8,128)(2,1)S(1)}, u32[]{:S(2)}, u32[]{:S(2)}) collective-permute-start(bf16[256,128]{1,0:T(8,128)(2,1)S(1)} %add.6.mine_ref), channel_id=1, source_target_pairs={{0,9},{1,8},{2,11},{3,10},{4,13},{5,12},{6,15},{7,14},{8,1},{9,0},... | collective-permute-start | bytes 196616 | tf_op jit(solution)/shard_map/ppermute | solution.py:310
  26.5 1.3 %collective-permute-start.5 = (bf16[128,128]{1,0:T(8,128)(2,1)S(1)}, bf16[128,128]{1,0:T(8,128)(2,1)S(1)}, u32[]{:S(2)}, u32[]{:S(2)}) collective-permute-start(bf16[128,128]{1,0:T(8,128)(2,1)S(1)} %product_terms.1.mine_ref), channel_id=1, source_target_pairs={{0,1},{1,0},{2,3},{3,2},{4,5},{5,4},{6,7},{7,6},{8,9},{9,8},{10,11... | collective-permute-start | bytes 98312 | tf_op jit(solution)/shard_map/ppermute | solution.py:310
  27.7 3.4 %collective-permute-start.6 = (bf16[128,128]{1,0:T(8,128)(2,1)S(1)}, bf16[128,128]{1,0:T(8,128)(2,1)S(1)}, u32[]{:S(2)}, u32[]{:S(2)}) collective-permute-start(bf16[128,128]{1,0:T(8,128)(2,1)S(1)} %add.8.term_ref), channel_id=1, source_target_pairs={{0,3},{1,2},{2,1},{3,0},{4,7},{5,6},{6,5},{7,4},{8,11},{9,10},{10,... | collective-permute-start | bytes 98312 | tf_op jit(solution)/shard_map/ppermute | solution.py:310
  31.6 3.2 %collective-permute-start.7 = (f32[32,128]{1,0:T(8,128)S(1)}, f32[32,128]{1,0:T(8,128)S(1)}, u32[]{:S(2)}, u32[]{:S(2)}) collective-permute-start(f32[32,128]{1,0:T(8,128)S(1)} %local_gram.1.mine_ref), channel_id=1, source_target_pairs={{0,5},{1,4},{2,7},{3,6},{4,1},{5,0},{6,3},{7,2},{8,13},{9,12},{10,... | collective-permute-start | bytes 49160 | tf_op jit(solution)/shard_map/ppermute | solution.py:310
  34.7 4.1 %collective-permute-start.8 = (f32[32,128]{1,0:T(8,128)S(1)}, f32[32,128]{1,0:T(8,128)S(1)}, u32[]{:S(2)}, u32[]{:S(2)}) collective-permute-start(f32[32,128]{1,0:T(8,128)S(1)} %add.9.gram_ref), channel_id=1, source_target_pairs={{0,9},{1,8},{2,11},{3,10},{4,13},{5,12},{6,15},{7,14},{8,1},{9,0},... | collective-permute-start | bytes 49160 | tf_op jit(solution)/shard_map/ppermute | solution.py:310

commit v14 on v13

--- a/solution.py
+++ b/solution.py
@@ -29,62 +29,68 @@
     return lax.rem(half, 2)
 
 
-def contract_kernel(
-    step, fibers, ahead, snapshot_ref, mode2_ref, send_ref, own_ref, slab_ref, even_ref, odd_ref, sems
-):
-    rank, depth = mode2_ref.shape
-    tile = 8
+TILE = 8
+
+
+def prepare_kernel(fibers, mode2_ref, wide_ref, order_ref):
+    rank = mode2_ref.shape[0]
     reps = LANES // rank
-    block = tile * fibers
-    blocks = step // tile
-    out_rows = block // reps
-    chunks = snapshot_ref.shape[0] // (step * fibers)
-
-    def copy(chunk):
-        where = pl.ds(chunk * step * fibers, step * fibers)
-        return pltpu.make_async_copy(snapshot_ref.at[where], slab_ref.at[where], sems.at[chunk])
-
-    for chunk in range(ahead):
-        copy(chunk).start()
-    wide = jnp.concatenate([mode2_ref[...]] * reps, axis=0)
+    wide_ref[...] = jnp.concatenate([mode2_ref[...]] * reps, axis=0)
+    block = TILE * fibers
+    to = lax.broadcasted_iota(jnp.int32, order_ref.shape, 0)
+    at = lax.broadcasted_iota(jnp.int32, order_ref.shape, 1)
+    cell = lax.div(lax.rem(at, block), fibers)
+    wanted = lax.div(to, TILE) * reps + lax.div(at, block)
+    same = (lax.rem(to, TILE) == cell) & (wanted == lax.rem(at, fibers))
+    order_ref[...] = same.astype(F32).astype(BF16)
+
+
+def prepare(mode2_t, fibers):
+    rank, depth = mode2_t.shape
+    reps = LANES // rank
+    block = TILE * fibers
+    return pl.pallas_call(
+        functools.partial(prepare_kernel, fibers),
+        out_shape=[
+            jax.ShapeDtypeStruct((LANES, depth), BF16),
+            jax.ShapeDtypeStruct((block // reps, block * reps), BF16),
+        ],
+        compiler_params=params(4),
+        cost_estimate=pl.CostEstimate(flops=0, bytes_accessed=2**24, transcendentals=0),
+        name="prepare",
+    )(mode2_t)
+
+
+def contract_kernel(step, own, snapshot_ref, wide_ref, order_ref, core_ref, even_ref, odd_ref):
+    cells, fibers, depth = snapshot_ref.shape
+    half = fibers // 2
+    block = TILE * half
+    reps = order_ref.shape[1] // block
+    rank = LANES // reps
+    chunks = cells // step
     lane = lax.broadcasted_iota(jnp.int32, (block, LANES), 1)
-    to = lax.broadcasted_iota(jnp.int32, (out_rows, reps * block), 0)
-    at = lax.broadcasted_iota(jnp.int32, (out_rows, reps * block), 1)
-    cell = lax.div(lax.rem(at, block), fibers)
-    fiber = lax.rem(at, fibers)
-    wanted = lax.div(to, tile) * reps + lax.div(at, block)
-    order = ((lax.rem(to, tile) == cell) & (wanted == fiber)).astype(F32).astype(BF16)
-    first = own_half() == 0
-    pairs = fibers // reps
+    start = own_half() if own else 1 - own_half()
+    start = pl.multiple_of(start * half, half)
 
     def multiply(chunk, flat_ref):
-        copy(chunk).wait()
-
-        @pl.when(chunk + ahead < chunks)
-        def _():
-            copy(chunk + ahead).start()
-
-        rows = pl.ds(chunk * step * fibers, step * fibers)
-        low = dot_f32(slab_ref[rows, :depth // 2], wide[:, :depth // 2], ((1,), (1,)))
-        high = dot_f32(slab_ref[rows, depth // 2:], wide[:, depth // 2:], ((1,), (1,)))
+        x = snapshot_ref[pl.ds(chunk * step, step), pl.ds(start, half), :]
+        x = x.reshape(step * half, depth)
+        low = dot_f32(x[:, :depth // 2], wide_ref[:, :depth // 2], ((1,), (1,)))
+        high = dot_f32(x[:, depth // 2:], wide_ref[:, depth // 2:], ((1,), (1,)))
         flat_ref[...] = (low + high).astype(BF16)
 
     def spread(chunk, flat_ref):
         rows = pl.ds(pl.multiple_of(chunk * step, step), step)
         spreads = []
-        for b in range(blocks):
+        for b in range(step // TILE):
             flat = flat_ref[pl.ds(b * block, block), :].astype(F32)
             groups = [
                 jnp.where(lax.div(lane, rank) == r, flat, 0.0).astype(BF16) for r in range(reps)
             ]
-            spreads.append(dot_f32(order, jnp.concatenate(groups, axis=0), ((1,), (0,))))
-        for p in range(pairs // 2):
-            low = jnp.concatenate([x[p * tile:(p + 1) * tile] for x in spreads], axis=0)
-            q = p + pairs // 2
-            high = jnp.concatenate([x[q * tile:(q + 1) * tile] for x in spreads], axis=0)
-            where = slice(p * LANES, (p + 1) * LANES)
-            own_ref[rows, where] = jnp.where(first, low, high).astype(BF16)
-            send_ref[rows, where] = jnp.where(first, high, low).astype(BF16)
+            spreads.append(dot_f32(order_ref[...], jnp.concatenate(groups, axis=0), ((1,), (0,))))
+        for p in range(half // reps):
+            part = jnp.concatenate([x[p * TILE:(p + 1) * TILE] for x in spreads], axis=0)
+            core_ref[rows, p * LANES:(p + 1) * LANES] = part.astype(BF16)
 
     def two_chunks(pair, _):
         multiply(2 * pair, even_ref)
@@ -97,27 +103,17 @@
     spread(chunks - 1, odd_ref)
 
 
-def contract(snapshot, mode2_t):
+def contract(snapshot, wide, order, own):
     cells, fibers, depth = snapshot.shape
-    rank = mode2_t.shape[0]
-    step = 16
-    out = jax.ShapeDtypeStruct((cells, fibers // 2 * rank), BF16)
-    return pl.pallas_call(
-        functools.partial(contract_kernel, step, fibers, 3),
-        in_specs=[
-            pl.BlockSpec(memory_space=pltpu.HBM),
-            pl.BlockSpec(memory_space=pltpu.VMEM),
-        ],
-        out_shape=[out, out],
-        scratch_shapes=[
-            pltpu.VMEM((cells * fibers, depth), BF16),
-            pltpu.VMEM((step * fibers, LANES), BF16),
-            pltpu.VMEM((step * fibers, LANES), BF16),
-            pltpu.SemaphoreType.DMA((cells // step,)),
-        ],
-        compiler_params=params(50),
-        name="contract",
-    )(snapshot.reshape(cells * fibers, depth), mode2_t)
+    step = 32
+    reps = order.shape[1] // (TILE * fibers // 2)
+    return pl.pallas_call(
+        functools.partial(contract_kernel, step, own),
+        out_shape=jax.ShapeDtypeStruct((cells, fibers // 2 // reps * LANES), BF16),
+        scratch_shapes=[pltpu.VMEM((step * fibers // 2, LANES), BF16)] * 2,
+        compiler_params=params(24),
+        name="contract_own" if own else "contract_send",
+    )(snapshot, wide, order)
 
 
 def is_even():
@@ -162,18 +158,20 @@
     )(own, got, factor_t)
 
 
-def add_kernel(mine_ref, got_ref, out_ref):
+def add_kernel(mine_ref, got_ref, *refs):
     total = mine_ref[...].astype(F32) + got_ref[...].astype(F32)
-    out_ref[...] = total.astype(out_ref.dtype)
-
-
-def add(mine, got):
+    refs[-1][...] = total.astype(refs[-1].dtype)
+
+
+def add(mine, got, *after):
+    whole = pl.BlockSpec(memory_space=pltpu.VMEM)
     return pl.pallas_call(
         add_kernel,
+        in_specs=[whole, whole] + [pl.BlockSpec(memory_space=pl.ANY)] * len(after),
         out_shape=jax.ShapeDtypeStruct(got.shape, got.dtype),
         compiler_params=params(4),
         name="add",
-    )(mine, got)
+    )(mine, got, *after)
 
 
 def product_kernel(mine_ref, got_ref, projected_ref, out_ref):
@@ -309,14 +307,16 @@
         ]
         return lax.ppermute(x, ("row", "col"), pairs)
 
-    send, own = contract(snapshot, mode2_factor.T)
-    got = swap(send, 0)
+    wide, order = prepare(mode2_factor.T, snapshot.shape[1] // 2)
+    got = swap(contract(snapshot, wide, order, False), 0)
+    own = contract(snapshot, wide, order, True)
 
     keep, send, columns, give = project(own, got, old_factor.T)
     mine = add(keep, swap(send, masks[0]))
     got_columns = swap(give, masks[0])
-    for mask in masks[1:]:
-        mine = add(mine, swap(mine, mask))
+    for step, mask in enumerate(masks[1:]):
+        after = [got_columns] if step == 0 else []
+        mine = add(mine, swap(mine, mask), *after)
 
     term = product_terms(columns, got_columns, mine)
     term = add(term, swap(term, 0))

time: 42.2 us -> 40.9 us (0.969)
  local copies, waits for them, and re-layouts: 0.91 us -> 4.28 us
  Pallas kernels: 11.4 us -> 8.12 us
  starting transfers between devices: 14.4 us -> 11.6 us
  waiting for transfers between devices: 15.3 us -> 16.6 us
    unnamed x4 -> x6, local copies, waits for them, and re-layouts: 0.91 us -> 4.28 us
    pallas_call x6 -> x8, Pallas kernels: 7.18 us -> 3.91 us  [the longest x2 3.82 us: contract(): pl.pallas_call(functools.partial(contract_kernel, step, own), out_shape=j...]
    ppermute x9, starting transfers between devices: 14.4 us -> 11.6 us  [swap(): return lax.ppermute(x, ('row', 'col'), pairs)]
    ppermute x9, waiting for transfers between devices: 15.3 us -> 16.6 us  [swap(): return lax.ppermute(x, ('row', 'col'), pairs)]
  transfers between devices with their start and end apart: 9 -> 9, of which waited for: 8 -> 8; matrix products, arithmetic and copies ran while one was open for 0% -> 0% of each run, Pallas kernels for 0% -> 5%
where the time goes in v14:
time: 40.9 us; the launch traced here: 40.7 us
  waiting for transfers between devices  16.6 us (41%)
  starting transfers between devices  11.6 us (28%)
  Pallas kernels  8.12 us (20%)
  local copies, waits for them, and re-layouts  4.28 us (10%)
    ppermute x9, waiting for transfers between devices, swap(): return lax.ppermute(x, ('row', 'col'), pairs)  16.6 us
    ppermute x9, starting transfers between devices, swap(): return lax.ppermute(x, ('row', 'col'), pairs)  11.6 us
    unnamed x6, local copies, waits for them, and re-layouts  4.28 us
    pallas_call x2, Pallas kernels, contract(): pl.pallas_call(functools.partial(contract_kernel, step, own), out_shape=j...  3.82 us
    pallas_call x1, Pallas kernels, finish(): pl.pallas_call(functools.partial(finish_kernel, total_rows), out_shape=ja...  3.29 us
  transfers between devices with their start and end apart: 9, of which 8 were waited for; matrix products, arithmetic and copies ran while one was open for 0% of the time, Pallas kernels for 5%

profile of v14, /device:TPU:0, one launch (start us, length us, event | category | flops | bytes accessed | tf_op | source)
XLA Modules:
  0.0 40.7 jit_solution(4953435433963150655)
XLA Ops:
  0.0 0.0 copy-start.1
  0.0 0.9 %copy-done.1 = bf16[1024,64]{0,1:T(8,128)(2,1)S(1)} copy-done((bf16[1024,64]{0,1:T(8,128)(2,1)S(1)}, bf16[1024,64]{0,1:T(8,128)(2,1)}, u32[]{:S(2)}) %copy-start.1) | copy-done | bytes 131096
  0.9 0.0 copy-start
  0.9 3.4 %copy-done = bf16[128,32,1024]{2,1,0:T(8,128)(2,1)S(1)} copy-done((bf16[128,32,1024]{2,1,0:T(8,128)(2,1)S(1)}, bf16[128,32,1024]{2,1,0:T(8,128)(2,1)}, u32[]{:S(2)}) %copy-start) | copy-done | bytes 8388632
  4.3 0.0 copy-start.2
  4.3 1.9 %contract_send.1 = bf16[128,1024]{1,0:T(8,128)(2,1)S(1)} custom-call(bf16[128,32,1024]{2,1,0:T(8,128)(2,1)S(1)} %copy-done, bf16[128,1024]{1,0:T(8,128)(2,1)S(1)} %get-tuple-element.11.wide_ref, bf16[64,256]{1,0:T(8,128)(2,1)S(1)} %get-tuple-element.12.order_ref), custom_call_target="tpu_custom_call" | custom-call | tf_op jit(solution)/shard_map/contract_send/pallas_call | solution.py:110
  6.2 0.5 %collective-permute-start = (bf16[128,1024]{1,0:T(8,128)(2,1)S(1)}, bf16[128,1024]{1,0:T(8,128)(2,1)S(1)}, u32[]{:S(2)}, u32[]{:S(2)}) collective-permute-start(bf16[128,1024]{1,0:T(8,128)(2,1)S(1)} %contract_send.1), channel_id=1, source_target_pairs={{0,1},{1,0},{2,3},{3,2},{4,5},{5,4},{6,7},{7,6},{8,9},{9,8},{10,11... | collective-permute-start | bytes 786440 | tf_op jit(solution)/shard_map/ppermute | solution.py:308
  6.7 1.9 %contract_own.1.own_ref = bf16[128,1024]{1,0:T(8,128)(2,1)S(1)} custom-call(bf16[128,32,1024]{2,1,0:T(8,128)(2,1)S(1)} %copy-done, bf16[128,1024]{1,0:T(8,128)(2,1)S(1)} %get-tuple-element.11.wide_ref, bf16[64,256]{1,0:T(8,128)(2,1)S(1)} %get-tuple-element.12.order_ref), custom_call_target="tpu_custom_call" | custom-call | tf_op jit(solution)/shard_map/contract_own/pallas_call | solution.py:110
  8.7 0.0 collective-permute-done.got_ref
  8.7 0.0 copy-done.2
  8.7 0.2 project.1
  8.9 2.7 %collective-permute-start.2 = (bf16[256,128]{1,0:T(8,128)(2,1)S(1)}, bf16[256,128]{1,0:T(8,128)(2,1)S(1)}, u32[]{:S(2)}, u32[]{:S(2)}) collective-permute-start(bf16[256,128]{1,0:T(8,128)(2,1)S(1)} %get-tuple-element.16), channel_id=1, source_target_pairs={{0,3},{1,2},{2,1},{3,0},{4,7},{5,6},{6,5},{7,4},{8,11},{9,10},{10,... | collective-permute-start | bytes 196616 | tf_op jit(solution)/shard_map/ppermute | solution.py:308
  11.7 0.0 collective-permute-start.1
  11.7 2.4 %collective-permute-done.2.got_ref = bf16[256,128]{1,0:T(8,128)(2,1)S(1)} collective-permute-done((bf16[256,128]{1,0:T(8,128)(2,1)S(1)}, bf16[256,128]{1,0:T(8,128)(2,1)S(1)}, u32[]{:S(2)}, u32[]{:S(2)}) %collective-permute-start.2) | collective-permute-done | bytes 65568 | tf_op jit(solution)/shard_map/ppermute | solution.py:308
  14.1 1.4 %collective-permute-start.3 = (bf16[256,128]{1,0:T(8,128)(2,1)S(1)}, bf16[256,128]{1,0:T(8,128)(2,1)S(1)}, u32[]{:S(2)}, u32[]{:S(2)}) collective-permute-start(bf16[256,128]{1,0:T(8,128)(2,1)S(1)} %add.5.mine_ref), channel_id=1, source_target_pairs={{0,5},{1,4},{2,7},{3,6},{4,1},{5,0},{6,3},{7,2},{8,13},{9,12},{10,... | collective-permute-start | bytes 196616 | tf_op jit(solution)/shard_map/ppermute | solution.py:308
  15.5 1.8 %collective-permute-done.1.refs_0_.got_ref = bf16[128,512]{1,0:T(8,128)(2,1)S(1)} collective-permute-done((bf16[128,512]{1,0:T(8,128)(2,1)S(1)}, bf16[128,512]{1,0:T(8,128)(2,1)S(1)}, u32[]{:S(2)}, u32[]{:S(2)}) %collective-permute-start.1) | collective-permute-done | bytes 131104 | tf_op jit(solution)/shard_map/ppermute | solution.py:308
  17.3 1.0 %collective-permute-done.3.got_ref = bf16[256,128]{1,0:T(8,128)(2,1)S(1)} collective-permute-done((bf16[256,128]{1,0:T(8,128)(2,1)S(1)}, bf16[256,128]{1,0:T(8,128)(2,1)S(1)}, u32[]{:S(2)}, u32[]{:S(2)}) %collective-permute-start.3) | collective-permute-done | bytes 65568 | tf_op jit(solution)/shard_map/ppermute | solution.py:308
  18.3 2.3 %collective-permute-start.4 = (bf16[256,128]{1,0:T(8,128)(2,1)S(1)}, bf16[256,128]{1,0:T(8,128)(2,1)S(1)}, u32[]{:S(2)}, u32[]{:S(2)}) collective-permute-start(bf16[256,128]{1,0:T(8,128)(2,1)S(1)} %add.6.mine_ref), channel_id=1, source_target_pairs={{0,9},{1,8},{2,11},{3,10},{4,13},{5,12},{6,15},{7,14},{8,1},{9,0},... | collective-permute-start | bytes 196616 | tf_op jit(solution)/shard_map/ppermute | solution.py:308
  20.7 4.1 %collective-permute-done.4.got_ref = bf16[256,128]{1,0:T(8,128)(2,1)S(1)} collective-permute-done((bf16[256,128]{1,0:T(8,128)(2,1)S(1)}, bf16[256,128]{1,0:T(8,128)(2,1)S(1)}, u32[]{:S(2)}, u32[]{:S(2)}) %collective-permute-start.4) | collective-permute-done | bytes 65568 | tf_op jit(solution)/shard_map/ppermute | solution.py:308
  24.8 0.3 product_terms.1.mine_ref
  25.1 0.2 collective-permute-start.5
  25.3 1.1 %collective-permute-done.5.got_ref = bf16[128,128]{1,0:T(8,128)(2,1)S(1)} collective-permute-done((bf16[128,128]{1,0:T(8,128)(2,1)S(1)}, bf16[128,128]{1,0:T(8,128)(2,1)S(1)}, u32[]{:S(2)}, u32[]{:S(2)}) %collective-permute-start.5) | collective-permute-done | bytes 32800 | tf_op jit(solution)/shard_map/ppermute | solution.py:308
  26.4 1.5 %collective-permute-start.6 = (bf16[128,128]{1,0:T(8,128)(2,1)S(1)}, bf16[128,128]{1,0:T(8,128)(2,1)S(1)}, u32[]{:S(2)}, u32[]{:S(2)}) collective-permute-start(bf16[128,128]{1,0:T(8,128)(2,1)S(1)} %add.8.term_ref), channel_id=1, source_target_pairs={{0,3},{1,2},{2,1},{3,0},{4,7},{5,6},{6,5},{7,4},{8,11},{9,10},{10,... | collective-permute-start | bytes 98312 | tf_op jit(solution)/shard_map/ppermute | solution.py:308
  27.9 2.0 %collective-permute-done.6.got_ref.got_term_ref = bf16[128,128]{1,0:T(8,128)(2,1)S(1)} collective-permute-done((bf16[128,128]{1,0:T(8,128)(2,1)S(1)}, bf16[128,128]{1,0:T(8,128)(2,1)S(1)}, u32[]{:S(2)}, u32[]{:S(2)}) %collective-permute-start.6) | collective-permute-done | bytes 32800 | tf_op jit(solution)/shard_map/ppermute | solution.py:308
  29.8 0.4 local_gram.1.mine_ref
  30.2 0.7 %collective-permute-start.7 = (f32[32,128]{1,0:T(8,128)S(1)}, f32[32,128]{1,0:T(8,128)S(1)}, u32[]{:S(2)}, u32[]{:S(2)}) collective-permute-start(f32[32,128]{1,0:T(8,128)S(1)} %local_gram.1.mine_ref), channel_id=1, source_target_pairs={{0,5},{1,4},{2,7},{3,6},{4,1},{5,0},{6,3},{7,2},{8,13},{9,12},{10,... | collective-permute-start | bytes 49160 | tf_op jit(solution)/shard_map/ppermute | solution.py:308
  30.9 2.4 %collective-permute-done.7.got_ref = f32[32,128]{1,0:T(8,128)S(1)} collective-permute-done((f32[32,128]{1,0:T(8,128)S(1)}, f32[32,128]{1,0:T(8,128)S(1)}, u32[]{:S(2)}, u32[]{:S(2)}) %collective-permute-start.7) | collective-permute-done | bytes 16416 | tf_op jit(solution)/shard_map/ppermute | solution.py:308
  33.4 2.3 %collective-permute-start.8 = (f32[32,128]{1,0:T(8,128)S(1)}, f32[32,128]{1,0:T(8,128)S(1)}, u32[]{:S(2)}, u32[]{:S(2)}) collective-permute-start(f32[32,128]{1,0:T(8,128)S(1)} %add.9.gram_ref), channel_id=1, source_target_pairs={{0,9},{1,8},{2,11},{3,10},{4,13},{5,12},{6,15},{7,14},{8,1},{9,0},... | collective-permute-start | bytes 49160 | tf_op jit(solution)/shard_map/ppermute | solution.py:308
  35.6 1.8 %collective-permute-done.8.got_gram_ref = f32[32,128]{1,0:T(8,128)S(1)} collective-permute-done((f32[32,128]{1,0:T(8,128)S(1)}, f32[32,128]{1,0:T(8,128)S(1)}, u32[]{:S(2)}, u32[]{:S(2)}) %collective-permute-start.8) | collective-permute-done | bytes 16416 | tf_op jit(solution)/shard_map/ppermute | solution.py:308
  37.5 3.3 %finish.1 = f32[64,64]{1,0:T(8,128)} custom-call(bf16[128,128]{1,0:T(8,128)(2,1)S(1)} %add.8.term_ref, bf16[128,128]{1,0:T(8,128)(2,1)S(1)} %collective-permute-done.6.got_ref.got_term_ref, f32[32,128]{1,0:T(8,128)S(1)} %add.9.gram_ref, f32[32,128]{1,0:T(8,128)S(1)} %collective-permute-done.8.got_gram_ref), custom_call_target="tpu_custom_call" | custom-call | tf_op jit(solution)/shard_map/finish/pallas_call | solution.py:289
  (6 shorter events, 0.1 us)
Async XLA Ops:
  0.0 0.9 %copy-start.1 = (bf16[1024,64]{0,1:T(8,128)(2,1)S(1)}, bf16[1024,64]{0,1:T(8,128)(2,1)}, u32[]{:S(2)}) copy-start(bf16[1024,64]{0,1:T(8,128)(2,1)} %param.4) | copy-start | bytes 393220
  0.9 3.4 %copy-start = (bf16[128,32,1024]{2,1,0:T(8,128)(2,1)S(1)}, bf16[128,32,1024]{2,1,0:T(8,128)(2,1)}, u32[]{:S(2)}) copy-start(bf16[128,32,1024]{2,1,0:T(8,128)(2,1)} %snapshot_ref.3) | copy-start | bytes 25165828
  4.3 4.4 %copy-start.2 = (bf16[128,64]{0,1:T(8,128)(2,1)S(1)}, bf16[128,64]{0,1:T(8,128)(2,1)}, u32[]{:S(2)}) copy-start(bf16[128,64]{0,1:T(8,128)(2,1)} %param.5) | copy-start | bytes 49156
  6.2 2.4 %collective-permute-start = (bf16[128,1024]{1,0:T(8,128)(2,1)S(1)}, bf16[128,1024]{1,0:T(8,128)(2,1)S(1)}, u32[]{:S(2)}, u32[]{:S(2)}) collective-permute-start(bf16[128,1024]{1,0:T(8,128)(2,1)S(1)} %contract_send.1), channel_id=1, source_target_pairs={{0,1},{1,0},{2,3},{3,2},{4,5},{5,4},{6,7},{7,6},{8,9},{9,8},{10,11... | collective-permute-start | bytes 786440 | tf_op jit(solution)/shard_map/ppermute | solution.py:308
  8.9 5.2 %collective-permute-start.2 = (bf16[256,128]{1,0:T(8,128)(2,1)S(1)}, bf16[256,128]{1,0:T(8,128)(2,1)S(1)}, u32[]{:S(2)}, u32[]{:S(2)}) collective-permute-start(bf16[256,128]{1,0:T(8,128)(2,1)S(1)} %get-tuple-element.16), channel_id=1, source_target_pairs={{0,3},{1,2},{2,1},{3,0},{4,7},{5,6},{6,5},{7,4},{8,11},{9,10},{10,... | collective-permute-start | bytes 196616 | tf_op jit(solution)/shard_map/ppermute | solution.py:308
  11.7 5.6 %collective-permute-start.1 = (bf16[128,512]{1,0:T(8,128)(2,1)S(1)}, bf16[128,512]{1,0:T(8,128)(2,1)S(1)}, u32[]{:S(2)}, u32[]{:S(2)}) collective-permute-start(bf16[128,512]{1,0:T(8,128)(2,1)S(1)} %get-tuple-element.14), channel_id=1, source_target_pairs={{0,3},{1,2},{2,1},{3,0},{4,7},{5,6},{6,5},{7,4},{8,11},{9,10},{10,... | collective-permute-start | bytes 393224 | tf_op jit(solution)/shard_map/ppermute | solution.py:308
  14.1 4.2 %collective-permute-start.3 = (bf16[256,128]{1,0:T(8,128)(2,1)S(1)}, bf16[256,128]{1,0:T(8,128)(2,1)S(1)}, u32[]{:S(2)}, u32[]{:S(2)}) collective-permute-start(bf16[256,128]{1,0:T(8,128)(2,1)S(1)} %add.5.mine_ref), channel_id=1, source_target_pairs={{0,5},{1,4},{2,7},{3,6},{4,1},{5,0},{6,3},{7,2},{8,13},{9,12},{10,... | collective-permute-start | bytes 196616 | tf_op jit(solution)/shard_map/ppermute | solution.py:308
  18.3 6.5 %collective-permute-start.4 = (bf16[256,128]{1,0:T(8,128)(2,1)S(1)}, bf16[256,128]{1,0:T(8,128)(2,1)S(1)}, u32[]{:S(2)}, u32[]{:S(2)}) collective-permute-start(bf16[256,128]{1,0:T(8,128)(2,1)S(1)} %add.6.mine_ref), channel_id=1, source_target_pairs={{0,9},{1,8},{2,11},{3,10},{4,13},{5,12},{6,15},{7,14},{8,1},{9,0},... | collective-permute-start | bytes 196616 | tf_op jit(solution)/shard_map/ppermute | solution.py:308
  25.1 1.3 %collective-permute-start.5 = (bf16[128,128]{1,0:T(8,128)(2,1)S(1)}, bf16[128,128]{1,0:T(8,128)(2,1)S(1)}, u32[]{:S(2)}, u32[]{:S(2)}) collective-permute-start(bf16[128,128]{1,0:T(8,128)(2,1)S(1)} %product_terms.1.mine_ref), channel_id=1, source_target_pairs={{0,1},{1,0},{2,3},{3,2},{4,5},{5,4},{6,7},{7,6},{8,9},{9,8},{10,11... | collective-permute-start | bytes 98312 | tf_op jit(solution)/shard_map/ppermute | solution.py:308
  26.4 3.4 %collective-permute-start.6 = (bf16[128,128]{1,0:T(8,128)(2,1)S(1)}, bf16[128,128]{1,0:T(8,128)(2,1)S(1)}, u32[]{:S(2)}, u32[]{:S(2)}) collective-permute-start(bf16[128,128]{1,0:T(8,128)(2,1)S(1)} %add.8.term_ref), channel_id=1, source_target_pairs={{0,3},{1,2},{2,1},{3,0},{4,7},{5,6},{6,5},{7,4},{8,11},{9,10},{10,... | collective-permute-start | bytes 98312 | tf_op jit(solution)/shard_map/ppermute | solution.py:308
  30.2 3.2 %collective-permute-start.7 = (f32[32,128]{1,0:T(8,128)S(1)}, f32[32,128]{1,0:T(8,128)S(1)}, u32[]{:S(2)}, u32[]{:S(2)}) collective-permute-start(f32[32,128]{1,0:T(8,128)S(1)} %local_gram.1.mine_ref), channel_id=1, source_target_pairs={{0,5},{1,4},{2,7},{3,6},{4,1},{5,0},{6,3},{7,2},{8,13},{9,12},{10,... | collective-permute-start | bytes 49160 | tf_op jit(solution)/shard_map/ppermute | solution.py:308
  33.4 4.1 %collective-permute-start.8 = (f32[32,128]{1,0:T(8,128)S(1)}, f32[32,128]{1,0:T(8,128)S(1)}, u32[]{:S(2)}, u32[]{:S(2)}) collective-permute-start(f32[32,128]{1,0:T(8,128)S(1)} %add.9.gram_ref), channel_id=1, source_target_pairs={{0,9},{1,8},{2,11},{3,10},{4,13},{5,12},{6,15},{7,14},{8,1},{9,0},... | collective-permute-start | bytes 49160 | tf_op jit(solution)/shard_map/ppermute | solution.py:308

commit v15 on v14

--- a/solution.py
+++ b/solution.py
@@ -32,62 +32,39 @@
 TILE = 8
 
 
-def prepare_kernel(fibers, mode2_ref, wide_ref, order_ref):
+def contract_kernel(step, own, snapshot_ref, mode2_ref, core_ref, even_ref, odd_ref):
+    cells, fibers, depth = snapshot_ref.shape
     rank = mode2_ref.shape[0]
+    half = fibers // 2
     reps = LANES // rank
-    wide_ref[...] = jnp.concatenate([mode2_ref[...]] * reps, axis=0)
-    block = TILE * fibers
-    to = lax.broadcasted_iota(jnp.int32, order_ref.shape, 0)
-    at = lax.broadcasted_iota(jnp.int32, order_ref.shape, 1)
-    cell = lax.div(lax.rem(at, block), fibers)
-    wanted = lax.div(to, TILE) * reps + lax.div(at, block)
-    same = (lax.rem(to, TILE) == cell) & (wanted == lax.rem(at, fibers))
-    order_ref[...] = same.astype(F32).astype(BF16)
-
-
-def prepare(mode2_t, fibers):
-    rank, depth = mode2_t.shape
-    reps = LANES // rank
-    block = TILE * fibers
-    return pl.pallas_call(
-        functools.partial(prepare_kernel, fibers),
-        out_shape=[
-            jax.ShapeDtypeStruct((LANES, depth), BF16),
-            jax.ShapeDtypeStruct((block // reps, block * reps), BF16),
-        ],
-        compiler_params=params(4),
-        cost_estimate=pl.CostEstimate(flops=0, bytes_accessed=2**24, transcendentals=0),
-        name="prepare",
-    )(mode2_t)
-
-
-def contract_kernel(step, own, snapshot_ref, wide_ref, order_ref, core_ref, even_ref, odd_ref):
-    cells, fibers, depth = snapshot_ref.shape
-    half = fibers // 2
     block = TILE * half
-    reps = order_ref.shape[1] // block
-    rank = LANES // reps
     chunks = cells // step
-    lane = lax.broadcasted_iota(jnp.int32, (block, LANES), 1)
     start = own_half() if own else 1 - own_half()
     start = pl.multiple_of(start * half, half)
+    shape = (block // reps, block * reps)
+    to = lax.broadcasted_iota(jnp.int32, shape, 0)
+    at = lax.broadcasted_iota(jnp.int32, shape, 1)
+    cell = lax.div(lax.rem(at, block), half)
+    wanted = lax.div(to, TILE) * reps + lax.div(at, block)
+    same = (lax.rem(to, TILE) == cell) & (wanted == lax.rem(at, half))
+    order = same.astype(F32).astype(BF16)
 
     def multiply(chunk, flat_ref):
         x = snapshot_ref[pl.ds(chunk * step, step), pl.ds(start, half), :]
         x = x.reshape(step * half, depth)
-        low = dot_f32(x[:, :depth // 2], wide_ref[:, :depth // 2], ((1,), (1,)))
-        high = dot_f32(x[:, depth // 2:], wide_ref[:, depth // 2:], ((1,), (1,)))
-        flat_ref[...] = (low + high).astype(BF16)
+        flat_ref[...] = dot_f32(mode2_ref[...], x, ((1,), (1,))).astype(BF16)
 
     def spread(chunk, flat_ref):
         rows = pl.ds(pl.multiple_of(chunk * step, step), step)
         spreads = []
         for b in range(step // TILE):
-            flat = flat_ref[pl.ds(b * block, block), :].astype(F32)
+            flat = flat_ref[:, b * block:(b + 1) * block]
+            none = jnp.zeros_like(flat)
             groups = [
-                jnp.where(lax.div(lane, rank) == r, flat, 0.0).astype(BF16) for r in range(reps)
+                jnp.concatenate([flat if k == r else none for k in range(reps)], axis=1)
+                for r in range(reps)
             ]
-            spreads.append(dot_f32(order_ref[...], jnp.concatenate(groups, axis=0), ((1,), (0,))))
+            spreads.append(dot_f32(order, jnp.concatenate(groups, axis=0), ((1,), (1,))))
         for p in range(half // reps):
             part = jnp.concatenate([x[p * TILE:(p + 1) * TILE] for x in spreads], axis=0)
             core_ref[rows, p * LANES:(p + 1) * LANES] = part.astype(BF16)
@@ -103,17 +80,17 @@
     spread(chunks - 1, odd_ref)
 
 
-def contract(snapshot, wide, order, own):
+def contract(snapshot, mode2_t, own):
     cells, fibers, depth = snapshot.shape
+    rank = mode2_t.shape[0]
     step = 32
-    reps = order.shape[1] // (TILE * fibers // 2)
     return pl.pallas_call(
         functools.partial(contract_kernel, step, own),
-        out_shape=jax.ShapeDtypeStruct((cells, fibers // 2 // reps * LANES), BF16),
-        scratch_shapes=[pltpu.VMEM((step * fibers // 2, LANES), BF16)] * 2,
+        out_shape=jax.ShapeDtypeStruct((cells, fibers // 2 * rank), BF16),
+        scratch_shapes=[pltpu.VMEM((rank, step * fibers // 2), BF16)] * 2,
         compiler_params=params(24),
         name="contract_own" if own else "contract_send",
-    )(snapshot, wide, order)
+    )(snapshot, mode2_t)
 
 
 def is_even():
@@ -174,14 +151,32 @@
     )(mine, got, *after)
 
 
-def product_kernel(mine_ref, got_ref, projected_ref, out_ref):
-    blocks = mine_ref.shape[1] // LANES
-    rank = projected_ref.shape[0] // blocks
+def halves_kernel(mine_ref, got_ref, low_ref, high_ref):
+    size = low_ref.shape[0]
+    for start, ref in ((0, low_ref), (size, high_ref)):
+        rows = pl.ds(start, size)
+        ref[...] = (mine_ref[rows, :] + got_ref[rows, :].astype(F32)).astype(BF16)
+
+
+def add_in_halves(mine, got):
+    out = jax.ShapeDtypeStruct((got.shape[0] // 2, LANES), BF16)
+    return pl.pallas_call(
+        halves_kernel,
+        out_shape=[out, out],
+        compiler_params=params(4),
+        name="add_in_halves",
+    )(mine, got)
+
+
+def product_kernel(mine_ref, got_ref, low_ref, high_ref, out_ref):
+    blocks = mine_ref.shape[1] // LANES // 2
+    rank = low_ref.shape[0] // blocks
     terms = []
     for ref in (mine_ref, got_ref):
         total = jnp.zeros((ref.shape[0], rank), F32)
-        for block in range(blocks):
-            projected = projected_ref[pl.ds(block * rank, rank), :]
+        for block in range(2 * blocks):
+            half_ref = low_ref if block < blocks else high_ref
+            projected = half_ref[pl.ds(block % blocks * rank, rank), :]
             where = slice(block * LANES, (block + 1) * LANES)
             total += dot_f32(ref[:, where], projected, ((1,), (1,)))
         terms.append(total)
@@ -191,13 +186,13 @@
     out_ref[...] = jnp.concatenate([low, high], axis=1).astype(BF16)
 
 
-def product_terms(mine, got, projected):
+def product_terms(mine, got, low, high):
     return pl.pallas_call(
         product_kernel,
         out_shape=jax.ShapeDtypeStruct((mine.shape[0], LANES), BF16),
         compiler_params=params(4),
         name="product_terms",
-    )(mine, got, projected)
+    )(mine, got, low, high)
 
 
 def pair_product(term_ref, got_ref):
@@ -307,18 +302,20 @@
         ]
         return lax.ppermute(x, ("row", "col"), pairs)
 
-    wide, order = prepare(mode2_factor.T, snapshot.shape[1] // 2)
-    got = swap(contract(snapshot, wide, order, False), 0)
-    own = contract(snapshot, wide, order, True)
+    mode2_t = mode2_factor.T
+    got = swap(contract(snapshot, mode2_t, False), 0)
+    own = contract(snapshot, mode2_t, True)
 
     keep, send, columns, give = project(own, got, old_factor.T)
-    mine = add(keep, swap(send, masks[0]))
+    low, high = add_in_halves(keep, swap(send, masks[0]))
     got_columns = swap(give, masks[0])
-    for step, mask in enumerate(masks[1:]):
-        after = [got_columns] if step == 0 else []
-        mine = add(mine, swap(mine, mask), *after)
-
-    term = product_terms(columns, got_columns, mine)
+    others = masks[1:]
+    for step, (mask, turned) in enumerate(zip(others, others[1:] + others[:1])):
+        after = [got_columns] if step == 1 else []
+        got_low, got_high = swap(low, mask), swap(high, turned)
+        low, high = add(low, got_low), add(high, got_high, *after)
+
+    term = product_terms(columns, got_columns, low, high)
     term = add(term, swap(term, 0))
     got_term = swap(term, masks[0])
     gram = local_gram(term, got_term)

time: 40.9 us -> 41 us (level)
  waiting for transfers between devices: 16.6 us -> 11.9 us
  starting transfers between devices: 11.6 us -> 16.1 us
    ppermute x9 -> x11, waiting for transfers between devices: 16.6 us -> 11.9 us  [swap(): return lax.ppermute(x, ('row', 'col'), pairs)]
    ppermute x9 -> x11, starting transfers between devices: 11.6 us -> 16.1 us  [swap(): return lax.ppermute(x, ('row', 'col'), pairs)]
  transfers between devices with their start and end apart: 9 -> 11, of which waited for: 8 -> 7; matrix products, arithmetic and copies ran while one was open for 0% -> 0% of each run, Pallas kernels for 5% -> 5%
where the time goes in v15:
time: 41 us; the launch traced here: 40.8 us
  starting transfers between devices  16.1 us (39%)
  waiting for transfers between devices  11.9 us (29%)
  Pallas kernels  8.44 us (21%)
  local copies, waits for them, and re-layouts  4.29 us (10%)
    ppermute x11, starting transfers between devices, swap(): return lax.ppermute(x, ('row', 'col'), pairs)  16.1 us
    ppermute x11, waiting for transfers between devices, swap(): return lax.ppermute(x, ('row', 'col'), pairs)  11.9 us
    unnamed x6, local copies, waits for them, and re-layouts  4.29 us
    pallas_call x2, Pallas kernels, contract(): pl.pallas_call(functools.partial(contract_kernel, step, own), out_shape=j...  4.16 us
    pallas_call x1, Pallas kernels, finish(): pl.pallas_call(functools.partial(finish_kernel, total_rows), out_shape=ja...  3.29 us
  transfers between devices with their start and end apart: 11, of which 7 were waited for; matrix products, arithmetic and copies ran while one was open for 0% of the time, Pallas kernels for 5%

profile of v15, /device:TPU:0, one launch (start us, length us, event | category | flops | bytes accessed | tf_op | source)
XLA Modules:
  0.0 40.8 jit_solution(11901482538821864819)
XLA Ops:
  0.0 0.0 copy-start
  0.0 3.4 %copy-done = bf16[128,32,1024]{2,1,0:T(8,128)(2,1)S(1)} copy-done((bf16[128,32,1024]{2,1,0:T(8,128)(2,1)S(1)}, bf16[128,32,1024]{2,1,0:T(8,128)(2,1)}, u32[]{:S(2)}) %copy-start) | copy-done | bytes 8388632
  3.4 0.0 copy-start.1
  3.4 0.9 %copy-done.1 = bf16[1024,64]{0,1:T(8,128)(2,1)S(1)} copy-done((bf16[1024,64]{0,1:T(8,128)(2,1)S(1)}, bf16[1024,64]{0,1:T(8,128)(2,1)}, u32[]{:S(2)}) %copy-start.1) | copy-done | bytes 131096
  4.3 0.0 copy-start.2
  4.3 2.1 %contract_send.1 = bf16[128,1024]{1,0:T(8,128)(2,1)S(1)} custom-call(bf16[128,32,1024]{2,1,0:T(8,128)(2,1)S(1)} %copy-done, bf16[64,1024]{1,0:T(8,128)(2,1)S(1)} %bitcast.2), custom_call_target="tpu_custom_call" | custom-call | tf_op jit(solution)/shard_map/contract_send/pallas_call | solution.py:87
  6.4 0.5 %collective-permute-start = (bf16[128,1024]{1,0:T(8,128)(2,1)S(1)}, bf16[128,1024]{1,0:T(8,128)(2,1)S(1)}, u32[]{:S(2)}, u32[]{:S(2)}) collective-permute-start(bf16[128,1024]{1,0:T(8,128)(2,1)S(1)} %contract_send.1), channel_id=1, source_target_pairs={{0,1},{1,0},{2,3},{3,2},{4,5},{5,4},{6,7},{7,6},{8,9},{9,8},{10,11... | collective-permute-start | bytes 786440 | tf_op jit(solution)/shard_map/ppermute | solution.py:303
  6.9 2.1 %contract_own.1.own_ref = bf16[128,1024]{1,0:T(8,128)(2,1)S(1)} custom-call(bf16[128,32,1024]{2,1,0:T(8,128)(2,1)S(1)} %copy-done, bf16[64,1024]{1,0:T(8,128)(2,1)S(1)} %bitcast.3), custom_call_target="tpu_custom_call" | custom-call | tf_op jit(solution)/shard_map/contract_own/pallas_call | solution.py:87
  9.0 0.0 collective-permute-done.got_ref
  9.0 0.0 copy-done.2
  9.0 0.2 project.1
  9.3 2.7 %collective-permute-start.2 = (bf16[256,128]{1,0:T(8,128)(2,1)S(1)}, bf16[256,128]{1,0:T(8,128)(2,1)S(1)}, u32[]{:S(2)}, u32[]{:S(2)}) collective-permute-start(bf16[256,128]{1,0:T(8,128)(2,1)S(1)} %get-tuple-element.14), channel_id=1, source_target_pairs={{0,3},{1,2},{2,1},{3,0},{4,7},{5,6},{6,5},{7,4},{8,11},{9,10},{10,... | collective-permute-start | bytes 196616 | tf_op jit(solution)/shard_map/ppermute | solution.py:303
  12.0 0.1 collective-permute-start.1
  12.0 2.4 %collective-permute-done.2.got_ref = bf16[256,128]{1,0:T(8,128)(2,1)S(1)} collective-permute-done((bf16[256,128]{1,0:T(8,128)(2,1)S(1)}, bf16[256,128]{1,0:T(8,128)(2,1)S(1)}, u32[]{:S(2)}, u32[]{:S(2)}) %collective-permute-start.2) | collective-permute-done | bytes 65568 | tf_op jit(solution)/shard_map/ppermute | solution.py:303
  14.4 1.4 %collective-permute-start.3 = (bf16[128,128]{1,0:T(8,128)(2,1)S(1)}, bf16[128,128]{1,0:T(8,128)(2,1)S(1)}, u32[]{:S(2)}, u32[]{:S(2)}) collective-permute-start(bf16[128,128]{1,0:T(8,128)(2,1)S(1)} %get-tuple-element.15.mine_ref), channel_id=1, source_target_pairs={{0,5},{1,4},{2,7},{3,6},{4,1},{5,0},{6,3},{7,2},{8,13},{9,12},{10,... | collective-permute-start | bytes 98312 | tf_op jit(solution)/shard_map/ppermute | solution.py:303
  15.8 2.5 %collective-permute-start.5 = (bf16[128,128]{1,0:T(8,128)(2,1)S(1)}, bf16[128,128]{1,0:T(8,128)(2,1)S(1)}, u32[]{:S(2)}, u32[]{:S(2)}) collective-permute-start(bf16[128,128]{1,0:T(8,128)(2,1)S(1)} %get-tuple-element.16.mine_ref), channel_id=1, source_target_pairs={{0,9},{1,8},{2,11},{3,10},{4,13},{5,12},{6,15},{7,14},{8,1},{9,0},... | collective-permute-start | bytes 98312 | tf_op jit(solution)/shard_map/ppermute | solution.py:303
  18.3 0.0 collective-permute-done.3.got_ref
  18.4 2.2 %collective-permute-start.4 = (bf16[128,128]{1,0:T(8,128)(2,1)S(1)}, bf16[128,128]{1,0:T(8,128)(2,1)S(1)}, u32[]{:S(2)}, u32[]{:S(2)}) collective-permute-start(bf16[128,128]{1,0:T(8,128)(2,1)S(1)} %add.6.mine_ref), channel_id=1, source_target_pairs={{0,9},{1,8},{2,11},{3,10},{4,13},{5,12},{6,15},{7,14},{8,1},{9,0},... | collective-permute-start | bytes 98312 | tf_op jit(solution)/shard_map/ppermute | solution.py:303
  20.6 0.0 collective-permute-done.5.got_ref
  20.6 1.3 %collective-permute-start.6 = (bf16[128,128]{1,0:T(8,128)(2,1)S(1)}, bf16[128,128]{1,0:T(8,128)(2,1)S(1)}, u32[]{:S(2)}, u32[]{:S(2)}) collective-permute-start(bf16[128,128]{1,0:T(8,128)(2,1)S(1)} %add.8.mine_ref), channel_id=1, source_target_pairs={{0,5},{1,4},{2,7},{3,6},{4,1},{5,0},{6,3},{7,2},{8,13},{9,12},{10,... | collective-permute-start | bytes 98312 | tf_op jit(solution)/shard_map/ppermute | solution.py:303
  21.9 0.8 %collective-permute-done.4.got_ref = bf16[128,128]{1,0:T(8,128)(2,1)S(1)} collective-permute-done((bf16[128,128]{1,0:T(8,128)(2,1)S(1)}, bf16[128,128]{1,0:T(8,128)(2,1)S(1)}, u32[]{:S(2)}, u32[]{:S(2)}) %collective-permute-start.4) | collective-permute-done | bytes 32800 | tf_op jit(solution)/shard_map/ppermute | solution.py:303
  22.7 1.4 %collective-permute-done.6.got_ref = bf16[128,128]{1,0:T(8,128)(2,1)S(1)} collective-permute-done((bf16[128,128]{1,0:T(8,128)(2,1)S(1)}, bf16[128,128]{1,0:T(8,128)(2,1)S(1)}, u32[]{:S(2)}, u32[]{:S(2)}) %collective-permute-start.6) | collective-permute-done | bytes 32800 | tf_op jit(solution)/shard_map/ppermute | solution.py:303
  24.1 0.0 collective-permute-done.1.refs_0_.got_ref
  24.1 0.3 product_terms.1.mine_ref
  24.4 0.3 collective-permute-start.7
  24.7 0.9 %collective-permute-done.7.got_ref = bf16[128,128]{1,0:T(8,128)(2,1)S(1)} collective-permute-done((bf16[128,128]{1,0:T(8,128)(2,1)S(1)}, bf16[128,128]{1,0:T(8,128)(2,1)S(1)}, u32[]{:S(2)}, u32[]{:S(2)}) %collective-permute-start.7) | collective-permute-done | bytes 32800 | tf_op jit(solution)/shard_map/ppermute | solution.py:303
  25.7 2.6 %collective-permute-start.8 = (bf16[128,128]{1,0:T(8,128)(2,1)S(1)}, bf16[128,128]{1,0:T(8,128)(2,1)S(1)}, u32[]{:S(2)}, u32[]{:S(2)}) collective-permute-start(bf16[128,128]{1,0:T(8,128)(2,1)S(1)} %add.10.term_ref), channel_id=1, source_target_pairs={{0,3},{1,2},{2,1},{3,0},{4,7},{5,6},{6,5},{7,4},{8,11},{9,10},{10,... | collective-permute-start | bytes 98312 | tf_op jit(solution)/shard_map/ppermute | solution.py:303
  28.3 1.6 %collective-permute-done.8.got_ref.got_term_ref = bf16[128,128]{1,0:T(8,128)(2,1)S(1)} collective-permute-done((bf16[128,128]{1,0:T(8,128)(2,1)S(1)}, bf16[128,128]{1,0:T(8,128)(2,1)S(1)}, u32[]{:S(2)}, u32[]{:S(2)}) %collective-permute-start.8) | collective-permute-done | bytes 32800 | tf_op jit(solution)/shard_map/ppermute | solution.py:303
  29.9 0.4 local_gram.1.mine_ref
  30.3 0.8 %collective-permute-start.9 = (f32[32,128]{1,0:T(8,128)S(1)}, f32[32,128]{1,0:T(8,128)S(1)}, u32[]{:S(2)}, u32[]{:S(2)}) collective-permute-start(f32[32,128]{1,0:T(8,128)S(1)} %local_gram.1.mine_ref), channel_id=1, source_target_pairs={{0,5},{1,4},{2,7},{3,6},{4,1},{5,0},{6,3},{7,2},{8,13},{9,12},{10,... | collective-permute-start | bytes 49160 | tf_op jit(solution)/shard_map/ppermute | solution.py:303
  31.1 2.3 %collective-permute-done.9.got_ref = f32[32,128]{1,0:T(8,128)S(1)} collective-permute-done((f32[32,128]{1,0:T(8,128)S(1)}, f32[32,128]{1,0:T(8,128)S(1)}, u32[]{:S(2)}, u32[]{:S(2)}) %collective-permute-start.9) | collective-permute-done | bytes 16416 | tf_op jit(solution)/shard_map/ppermute | solution.py:303
  33.5 1.6 %collective-permute-start.10 = (f32[32,128]{1,0:T(8,128)S(1)}, f32[32,128]{1,0:T(8,128)S(1)}, u32[]{:S(2)}, u32[]{:S(2)}) collective-permute-start(f32[32,128]{1,0:T(8,128)S(1)} %add.11.gram_ref), channel_id=1, source_target_pairs={{0,9},{1,8},{2,11},{3,10},{4,13},{5,12},{6,15},{7,14},{8,1},{9,0},... | collective-permute-start | bytes 49160 | tf_op jit(solution)/shard_map/ppermute | solution.py:303
  35.1 2.5 %collective-permute-done.10.got_gram_ref = f32[32,128]{1,0:T(8,128)S(1)} collective-permute-done((f32[32,128]{1,0:T(8,128)S(1)}, f32[32,128]{1,0:T(8,128)S(1)}, u32[]{:S(2)}, u32[]{:S(2)}) %collective-permute-start.10) | collective-permute-done | bytes 16416 | tf_op jit(solution)/shard_map/ppermute | solution.py:303
  37.5 3.3 %finish.1 = f32[64,64]{1,0:T(8,128)} custom-call(bf16[128,128]{1,0:T(8,128)(2,1)S(1)} %add.10.term_ref, bf16[128,128]{1,0:T(8,128)(2,1)S(1)} %collective-permute-done.8.got_ref.got_term_ref, f32[32,128]{1,0:T(8,128)S(1)} %add.11.gram_ref, f32[32,128]{1,0:T(8,128)S(1)} %collective-permute-done.10.got_gram_ref), custom_call_target="tpu_custom_call" | custom-call | tf_op jit(solution)/shard_map/finish/pallas_call | solution.py:284
  (7 shorter events, 0.1 us)
Async XLA Ops:
  0.0 3.4 %copy-start = (bf16[128,32,1024]{2,1,0:T(8,128)(2,1)S(1)}, bf16[128,32,1024]{2,1,0:T(8,128)(2,1)}, u32[]{:S(2)}) copy-start(bf16[128,32,1024]{2,1,0:T(8,128)(2,1)} %snapshot_ref.3) | copy-start | bytes 25165828
  3.4 0.9 %copy-start.1 = (bf16[1024,64]{0,1:T(8,128)(2,1)S(1)}, bf16[1024,64]{0,1:T(8,128)(2,1)}, u32[]{:S(2)}) copy-start(bf16[1024,64]{0,1:T(8,128)(2,1)} %param.4) | copy-start | bytes 393220
  4.3 4.7 %copy-start.2 = (bf16[128,64]{0,1:T(8,128)(2,1)S(1)}, bf16[128,64]{0,1:T(8,128)(2,1)}, u32[]{:S(2)}) copy-start(bf16[128,64]{0,1:T(8,128)(2,1)} %param.5) | copy-start | bytes 49156
  6.4 2.6 %collective-permute-start = (bf16[128,1024]{1,0:T(8,128)(2,1)S(1)}, bf16[128,1024]{1,0:T(8,128)(2,1)S(1)}, u32[]{:S(2)}, u32[]{:S(2)}) collective-permute-start(bf16[128,1024]{1,0:T(8,128)(2,1)S(1)} %contract_send.1), channel_id=1, source_target_pairs={{0,1},{1,0},{2,3},{3,2},{4,5},{5,4},{6,7},{7,6},{8,9},{9,8},{10,11... | collective-permute-start | bytes 786440 | tf_op jit(solution)/shard_map/ppermute | solution.py:303
  9.3 5.1 %collective-permute-start.2 = (bf16[256,128]{1,0:T(8,128)(2,1)S(1)}, bf16[256,128]{1,0:T(8,128)(2,1)S(1)}, u32[]{:S(2)}, u32[]{:S(2)}) collective-permute-start(bf16[256,128]{1,0:T(8,128)(2,1)S(1)} %get-tuple-element.14), channel_id=1, source_target_pairs={{0,3},{1,2},{2,1},{3,0},{4,7},{5,6},{6,5},{7,4},{8,11},{9,10},{10,... | collective-permute-start | bytes 196616 | tf_op jit(solution)/shard_map/ppermute | solution.py:303
  12.0 12.1 %collective-permute-start.1 = (bf16[128,512]{1,0:T(8,128)(2,1)S(1)}, bf16[128,512]{1,0:T(8,128)(2,1)S(1)}, u32[]{:S(2)}, u32[]{:S(2)}) collective-permute-start(bf16[128,512]{1,0:T(8,128)(2,1)S(1)} %get-tuple-element.12), channel_id=1, source_target_pairs={{0,3},{1,2},{2,1},{3,0},{4,7},{5,6},{6,5},{7,4},{8,11},{9,10},{10,... | collective-permute-start | bytes 393224 | tf_op jit(solution)/shard_map/ppermute | solution.py:303
  14.4 3.9 %collective-permute-start.3 = (bf16[128,128]{1,0:T(8,128)(2,1)S(1)}, bf16[128,128]{1,0:T(8,128)(2,1)S(1)}, u32[]{:S(2)}, u32[]{:S(2)}) collective-permute-start(bf16[128,128]{1,0:T(8,128)(2,1)S(1)} %get-tuple-element.15.mine_ref), channel_id=1, source_target_pairs={{0,5},{1,4},{2,7},{3,6},{4,1},{5,0},{6,3},{7,2},{8,13},{9,12},{10,... | collective-permute-start | bytes 98312 | tf_op jit(solution)/shard_map/ppermute | solution.py:303
  15.8 4.8 %collective-permute-start.5 = (bf16[128,128]{1,0:T(8,128)(2,1)S(1)}, bf16[128,128]{1,0:T(8,128)(2,1)S(1)}, u32[]{:S(2)}, u32[]{:S(2)}) collective-permute-start(bf16[128,128]{1,0:T(8,128)(2,1)S(1)} %get-tuple-element.16.mine_ref), channel_id=1, source_target_pairs={{0,9},{1,8},{2,11},{3,10},{4,13},{5,12},{6,15},{7,14},{8,1},{9,0},... | collective-permute-start | bytes 98312 | tf_op jit(solution)/shard_map/ppermute | solution.py:303
  18.4 4.3 %collective-permute-start.4 = (bf16[128,128]{1,0:T(8,128)(2,1)S(1)}, bf16[128,128]{1,0:T(8,128)(2,1)S(1)}, u32[]{:S(2)}, u32[]{:S(2)}) collective-permute-start(bf16[128,128]{1,0:T(8,128)(2,1)S(1)} %add.6.mine_ref), channel_id=1, source_target_pairs={{0,9},{1,8},{2,11},{3,10},{4,13},{5,12},{6,15},{7,14},{8,1},{9,0},... | collective-permute-start | bytes 98312 | tf_op jit(solution)/shard_map/ppermute | solution.py:303
  20.6 3.5 %collective-permute-start.6 = (bf16[128,128]{1,0:T(8,128)(2,1)S(1)}, bf16[128,128]{1,0:T(8,128)(2,1)S(1)}, u32[]{:S(2)}, u32[]{:S(2)}) collective-permute-start(bf16[128,128]{1,0:T(8,128)(2,1)S(1)} %add.8.mine_ref), channel_id=1, source_target_pairs={{0,5},{1,4},{2,7},{3,6},{4,1},{5,0},{6,3},{7,2},{8,13},{9,12},{10,... | collective-permute-start | bytes 98312 | tf_op jit(solution)/shard_map/ppermute | solution.py:303
  24.4 1.3 %collective-permute-start.7 = (bf16[128,128]{1,0:T(8,128)(2,1)S(1)}, bf16[128,128]{1,0:T(8,128)(2,1)S(1)}, u32[]{:S(2)}, u32[]{:S(2)}) collective-permute-start(bf16[128,128]{1,0:T(8,128)(2,1)S(1)} %product_terms.1.mine_ref), channel_id=1, source_target_pairs={{0,1},{1,0},{2,3},{3,2},{4,5},{5,4},{6,7},{7,6},{8,9},{9,8},{10,11... | collective-permute-start | bytes 98312 | tf_op jit(solution)/shard_map/ppermute | solution.py:303
  25.7 4.2 %collective-permute-start.8 = (bf16[128,128]{1,0:T(8,128)(2,1)S(1)}, bf16[128,128]{1,0:T(8,128)(2,1)S(1)}, u32[]{:S(2)}, u32[]{:S(2)}) collective-permute-start(bf16[128,128]{1,0:T(8,128)(2,1)S(1)} %add.10.term_ref), channel_id=1, source_target_pairs={{0,3},{1,2},{2,1},{3,0},{4,7},{5,6},{6,5},{7,4},{8,11},{9,10},{10,... | collective-permute-start | bytes 98312 | tf_op jit(solution)/shard_map/ppermute | solution.py:303
  30.3 3.2 %collective-permute-start.9 = (f32[32,128]{1,0:T(8,128)S(1)}, f32[32,128]{1,0:T(8,128)S(1)}, u32[]{:S(2)}, u32[]{:S(2)}) collective-permute-start(f32[32,128]{1,0:T(8,128)S(1)} %local_gram.1.mine_ref), channel_id=1, source_target_pairs={{0,5},{1,4},{2,7},{3,6},{4,1},{5,0},{6,3},{7,2},{8,13},{9,12},{10,... | collective-permute-start | bytes 49160 | tf_op jit(solution)/shard_map/ppermute | solution.py:303
  33.5 4.1 %collective-permute-start.10 = (f32[32,128]{1,0:T(8,128)S(1)}, f32[32,128]{1,0:T(8,128)S(1)}, u32[]{:S(2)}, u32[]{:S(2)}) collective-permute-start(f32[32,128]{1,0:T(8,128)S(1)} %add.11.gram_ref), channel_id=1, source_target_pairs={{0,9},{1,8},{2,11},{3,10},{4,13},{5,12},{6,15},{7,14},{8,1},{9,0},... | collective-permute-start | bytes 49160 | tf_op jit(solution)/shard_map/ppermute | solution.py:303

commit v16 on v15

--- a/solution.py
+++ b/solution.py
@@ -32,39 +32,41 @@
 TILE = 8
 
 
-def contract_kernel(step, own, snapshot_ref, mode2_ref, core_ref, even_ref, odd_ref):
-    cells, fibers, depth = snapshot_ref.shape
-    rank = mode2_ref.shape[0]
-    half = fibers // 2
-    reps = LANES // rank
+def fill_order(order_ref, half):
     block = TILE * half
-    chunks = cells // step
-    start = own_half() if own else 1 - own_half()
-    start = pl.multiple_of(start * half, half)
-    shape = (block // reps, block * reps)
-    to = lax.broadcasted_iota(jnp.int32, shape, 0)
-    at = lax.broadcasted_iota(jnp.int32, shape, 1)
+    reps = order_ref.shape[1] // block
+    to = lax.broadcasted_iota(jnp.int32, order_ref.shape, 0)
+    at = lax.broadcasted_iota(jnp.int32, order_ref.shape, 1)
     cell = lax.div(lax.rem(at, block), half)
     wanted = lax.div(to, TILE) * reps + lax.div(at, block)
     same = (lax.rem(to, TILE) == cell) & (wanted == lax.rem(at, half))
-    order = same.astype(F32).astype(BF16)
+    order_ref[...] = same.astype(F32).astype(BF16)
+
+
+def contract_loop(step, slab_ref, wide_ref, order_ref, core_ref, even_ref, odd_ref, ready):
+    cells, half, depth = slab_ref.shape
+    block = TILE * half
+    reps = order_ref.shape[1] // block
+    rank = LANES // reps
+    chunks = cells // step
+    lane = lax.broadcasted_iota(jnp.int32, (block, LANES), 1)
 
     def multiply(chunk, flat_ref):
-        x = snapshot_ref[pl.ds(chunk * step, step), pl.ds(start, half), :]
-        x = x.reshape(step * half, depth)
-        flat_ref[...] = dot_f32(mode2_ref[...], x, ((1,), (1,))).astype(BF16)
+        ready(chunk)
+        x = slab_ref[pl.ds(chunk * step, step)].reshape(step * half, depth)
+        low = dot_f32(x[:, :depth // 2], wide_ref[:, :depth // 2], ((1,), (1,)))
+        high = dot_f32(x[:, depth // 2:], wide_ref[:, depth // 2:], ((1,), (1,)))
+        flat_ref[...] = (low + high).astype(BF16)
 
     def spread(chunk, flat_ref):
         rows = pl.ds(pl.multiple_of(chunk * step, step), step)
         spreads = []
         for b in range(step // TILE):
-            flat = flat_ref[:, b * block:(b + 1) * block]
-            none = jnp.zeros_like(flat)
+            flat = flat_ref[pl.ds(b * block, block), :].astype(F32)
             groups = [
-                jnp.concatenate([flat if k == r else none for k in range(reps)], axis=1)
-                for r in range(reps)
+                jnp.where(lax.div(lane, rank) == r, flat, 0.0).astype(BF16) for r in range(reps)
             ]
-            spreads.append(dot_f32(order, jnp.concatenate(groups, axis=0), ((1,), (1,))))
+            spreads.append(dot_f32(order_ref[...], jnp.concatenate(groups, axis=0), ((1,), (0,))))
         for p in range(half // reps):
             part = jnp.concatenate([x[p * TILE:(p + 1) * TILE] for x in spreads], axis=0)
             core_ref[rows, p * LANES:(p + 1) * LANES] = part.astype(BF16)
@@ -80,17 +82,109 @@
     spread(chunks - 1, odd_ref)
 
 
-def contract(snapshot, mode2_t, own):
+STEP = 32
+
+
+def send_kernel(
+    snapshot_ref, mode2_ref, core_ref, kept_ref, wide_ref, order_ref,
+    slab_ref, small_ref, even_ref, odd_ref, sems, kept_sem, small_sem,
+):
+    cells, half, _ = slab_ref.shape
+    rank = mode2_ref.shape[0]
+    chunks = cells // STEP
+    keep_start = pl.multiple_of(own_half() * half, half)
+    send_start = pl.multiple_of((1 - own_half()) * half, half)
+
+    def send_copy(start, size, chunk):
+        where = pl.ds(start, size)
+        return pltpu.make_async_copy(
+            snapshot_ref.at[where, pl.ds(send_start, half)], slab_ref.at[where], sems.at[chunk]
+        )
+
+    def kept_copy(start, size):
+        where = pl.ds(start, size)
+        return pltpu.make_async_copy(
+            snapshot_ref.at[where, pl.ds(keep_start, half)], kept_ref.at[where], kept_sem
+        )
+
+    def start_send(chunk, parts):
+        size = STEP // parts
+        for part in range(parts):
+            send_copy(chunk * STEP + part * size, size, chunk).start()
+
+    def start_kept(chunk):
+        for part in range(2):
+            kept_copy(chunk * STEP + part * (STEP // 2), STEP // 2).start()
+
+    small = pltpu.make_async_copy(mode2_ref, small_ref, small_sem)
+    small.start()
+    start_send(0, 4)
+    for chunk in range(1, chunks - 1):
+        start_send(chunk, 2)
+    fill_order(order_ref, half)
+    small.wait()
+    wide_ref[...] = jnp.concatenate([small_ref[...]] * (LANES // rank), axis=0)
+
+    def ready(chunk):
+        send_copy(chunk * STEP, STEP, chunk).wait()
+        for now in range(chunks):
+
+            @pl.when(chunk == now)
+            def _():
+                if now == 0:
+                    start_send(chunks - 1, 2)
+                start_kept(now)
+
+    contract_loop(STEP, slab_ref, wide_ref, order_ref, core_ref, even_ref, odd_ref, ready)
+    kept_copy(0, cells).wait()
+
+
+def contract_send(snapshot, mode2_t):
     cells, fibers, depth = snapshot.shape
     rank = mode2_t.shape[0]
-    step = 32
-    return pl.pallas_call(
-        functools.partial(contract_kernel, step, own),
-        out_shape=jax.ShapeDtypeStruct((cells, fibers // 2 * rank), BF16),
-        scratch_shapes=[pltpu.VMEM((rank, step * fibers // 2), BF16)] * 2,
+    half = fibers // 2
+    reps = LANES // rank
+    block = TILE * half
+    any_space = pl.BlockSpec(memory_space=pltpu.HBM)
+    return pl.pallas_call(
+        send_kernel,
+        in_specs=[any_space, any_space],
+        out_shape=[
+            jax.ShapeDtypeStruct((cells, half * rank), BF16),
+            jax.ShapeDtypeStruct((cells, half, depth), BF16),
+            jax.ShapeDtypeStruct((LANES, depth), BF16),
+            jax.ShapeDtypeStruct((block // reps, block * reps), BF16),
+        ],
+        scratch_shapes=[
+            pltpu.VMEM((cells, half, depth), BF16),
+            pltpu.VMEM((rank, depth), BF16),
+            pltpu.VMEM((STEP * half, LANES), BF16),
+            pltpu.VMEM((STEP * half, LANES), BF16),
+            pltpu.SemaphoreType.DMA((cells // STEP,)),
+            pltpu.SemaphoreType.DMA,
+            pltpu.SemaphoreType.DMA,
+        ],
+        compiler_params=params(47),
+        name="contract_send",
+    )(snapshot, mode2_t)
+
+
+def own_kernel(slab_ref, wide_ref, order_ref, core_ref, even_ref, odd_ref):
+    contract_loop(
+        STEP, slab_ref, wide_ref, order_ref, core_ref, even_ref, odd_ref, lambda chunk: None
+    )
+
+
+def contract_own(slab, wide, order):
+    cells, half, _ = slab.shape
+    reps = order.shape[1] // (TILE * half)
+    return pl.pallas_call(
+        own_kernel,
+        out_shape=jax.ShapeDtypeStruct((cells, half // reps * LANES), BF16),
+        scratch_shapes=[pltpu.VMEM((STEP * half, LANES), BF16)] * 2,
         compiler_params=params(24),
-        name="contract_own" if own else "contract_send",
-    )(snapshot, mode2_t)
+        name="contract_own",
+    )(slab, wide, order)
 
 
 def is_even():
@@ -302,9 +396,9 @@
         ]
         return lax.ppermute(x, ("row", "col"), pairs)
 
-    mode2_t = mode2_factor.T
-    got = swap(contract(snapshot, mode2_t, False), 0)
-    own = contract(snapshot, mode2_t, True)
+    send, kept, wide, order = contract_send(snapshot, mode2_factor.T)
+    got = swap(send, 0)
+    own = contract_own(kept, wide, order)
 
     keep, send, columns, give = project(own, got, old_factor.T)
     low, high = add_in_halves(keep, swap(send, masks[0]))

time: 41 us -> 40.6 us (level)
  local copies, waits for them, and re-layouts: 4.29 us -> 0.91 us
  Pallas kernels: 8.44 us -> 11.5 us
    unnamed x6 -> x4, local copies, waits for them, and re-layouts: 4.29 us -> 0.91 us
    pallas_call x2, Pallas kernels: 4.16 us -> 7.2 us  [the longest x1 5.28 us: contract_send(): pl.pallas_call(send_kernel, in_specs=[any_space, any_space], out_shape=[j...]
where the time goes in v16:
time: 40.6 us; the launch traced here: 40.5 us
  starting transfers between devices  16.1 us (40%)
  waiting for transfers between devices  11.9 us (29%)
  Pallas kernels  11.5 us (28%)
  local copies, waits for them, and re-layouts  0.91 us (2%)
    ppermute x11, starting transfers between devices, swap(): return lax.ppermute(x, ('row', 'col'), pairs)  16.1 us
    ppermute x11, waiting for transfers between devices, swap(): return lax.ppermute(x, ('row', 'col'), pairs)  11.9 us
    pallas_call x1, Pallas kernels, contract_send(): pl.pallas_call(send_kernel, in_specs=[any_space, any_space], out_shape=[j...  5.28 us
    pallas_call x1, Pallas kernels, finish(): pl.pallas_call(functools.partial(finish_kernel, total_rows), out_shape=ja...  3.29 us
    pallas_call x1, Pallas kernels, contract_own(): pl.pallas_call(own_kernel, out_shape=jax.ShapeDtypeStruct((cells, half //...  1.91 us
    unnamed x4, local copies, waits for them, and re-layouts  0.91 us
  transfers between devices with their start and end apart: 11, of which 7 were waited for; matrix products, arithmetic and copies ran while one was open for 0% of the time, Pallas kernels for 5%

profile of v16, /device:TPU:0, one launch (start us, length us, event | category | flops | bytes accessed | tf_op | source)
XLA Modules:
  0.0 40.5 jit_solution(2485265423419728294)
XLA Ops:
  0.0 0.0 copy-start
  0.0 0.9 %copy-done = bf16[1024,64]{0,1:T(8,128)(2,1)S(1)} copy-done((bf16[1024,64]{0,1:T(8,128)(2,1)S(1)}, bf16[1024,64]{0,1:T(8,128)(2,1)}, u32[]{:S(2)}) %copy-start) | copy-done | bytes 131096
  0.9 0.0 copy-start.1
  0.9 5.3 %contract_send.1 = (bf16[128,1024]{1,0:T(8,128)(2,1)S(1)}, bf16[128,16,1024]{2,1,0:T(8,128)(2,1)S(1)}, bf16[128,1024]{1,0:T(8,128)(2,1)S(1)}, bf16[64,256]{1,0:T(8,128)(2,1)S(1)}) custom-call(bf16[128,32,1024]{2,1,0:T(8,128)(2,1)} %snapshot_ref.1, bf16[64,1024]{1,0:T(8,128)(2,1)S(1)} %bitcast.2), custom_call_target="tpu_custom_call" | custom-call | tf_op jit(solution)/shard_map/contract_send/pallas_call | solution.py:149
  6.2 0.5 %collective-permute-start = (bf16[128,1024]{1,0:T(8,128)(2,1)S(1)}, bf16[128,1024]{1,0:T(8,128)(2,1)S(1)}, u32[]{:S(2)}, u32[]{:S(2)}) collective-permute-start(bf16[128,1024]{1,0:T(8,128)(2,1)S(1)} %get-tuple-element.18), channel_id=1, source_target_pairs={{0,1},{1,0},{2,3},{3,2},{4,5},{5,4},{6,7},{7,6},{8,9},{9,8},{10,11... | collective-permute-start | bytes 786440 | tf_op jit(solution)/shard_map/ppermute | solution.py:397
  6.7 1.9 %contract_own.1.own_ref = bf16[128,1024]{1,0:T(8,128)(2,1)S(1)} custom-call(bf16[128,16,1024]{2,1,0:T(8,128)(2,1)S(1)} %get-tuple-element.15.slab_ref, bf16[128,1024]{1,0:T(8,128)(2,1)S(1)} %get-tuple-element.16.wide_ref, bf16[64,256]{1,0:T(8,128)(2,1)S(1)} %get-tuple-element.17.order_ref), custom_call_target="tpu_custom_call" | custom-call | tf_op jit(solution)/shard_map/contract_own/pallas_call | solution.py:181
  8.6 0.0 collective-permute-done.got_ref
  8.6 0.0 copy-done.1
  8.7 0.2 project.1
  8.9 2.7 %collective-permute-start.2 = (bf16[256,128]{1,0:T(8,128)(2,1)S(1)}, bf16[256,128]{1,0:T(8,128)(2,1)S(1)}, u32[]{:S(2)}, u32[]{:S(2)}) collective-permute-start(bf16[256,128]{1,0:T(8,128)(2,1)S(1)} %get-tuple-element.22), channel_id=1, source_target_pairs={{0,3},{1,2},{2,1},{3,0},{4,7},{5,6},{6,5},{7,4},{8,11},{9,10},{10,... | collective-permute-start | bytes 196616 | tf_op jit(solution)/shard_map/ppermute | solution.py:397
  11.6 0.1 collective-permute-start.1
  11.7 2.4 %collective-permute-done.2.got_ref = bf16[256,128]{1,0:T(8,128)(2,1)S(1)} collective-permute-done((bf16[256,128]{1,0:T(8,128)(2,1)S(1)}, bf16[256,128]{1,0:T(8,128)(2,1)S(1)}, u32[]{:S(2)}, u32[]{:S(2)}) %collective-permute-start.2) | collective-permute-done | bytes 65568 | tf_op jit(solution)/shard_map/ppermute | solution.py:397
  14.1 1.4 %collective-permute-start.3 = (bf16[128,128]{1,0:T(8,128)(2,1)S(1)}, bf16[128,128]{1,0:T(8,128)(2,1)S(1)}, u32[]{:S(2)}, u32[]{:S(2)}) collective-permute-start(bf16[128,128]{1,0:T(8,128)(2,1)S(1)} %get-tuple-element.23.mine_ref), channel_id=1, source_target_pairs={{0,5},{1,4},{2,7},{3,6},{4,1},{5,0},{6,3},{7,2},{8,13},{9,12},{10,... | collective-permute-start | bytes 98312 | tf_op jit(solution)/shard_map/ppermute | solution.py:397
  15.4 2.5 %collective-permute-start.5 = (bf16[128,128]{1,0:T(8,128)(2,1)S(1)}, bf16[128,128]{1,0:T(8,128)(2,1)S(1)}, u32[]{:S(2)}, u32[]{:S(2)}) collective-permute-start(bf16[128,128]{1,0:T(8,128)(2,1)S(1)} %get-tuple-element.24.mine_ref), channel_id=1, source_target_pairs={{0,9},{1,8},{2,11},{3,10},{4,13},{5,12},{6,15},{7,14},{8,1},{9,0},... | collective-permute-start | bytes 98312 | tf_op jit(solution)/shard_map/ppermute | solution.py:397
  18.0 0.0 collective-permute-done.3.got_ref
  18.0 2.2 %collective-permute-start.4 = (bf16[128,128]{1,0:T(8,128)(2,1)S(1)}, bf16[128,128]{1,0:T(8,128)(2,1)S(1)}, u32[]{:S(2)}, u32[]{:S(2)}) collective-permute-start(bf16[128,128]{1,0:T(8,128)(2,1)S(1)} %add.6.mine_ref), channel_id=1, source_target_pairs={{0,9},{1,8},{2,11},{3,10},{4,13},{5,12},{6,15},{7,14},{8,1},{9,0},... | collective-permute-start | bytes 98312 | tf_op jit(solution)/shard_map/ppermute | solution.py:397
  20.2 0.0 collective-permute-done.5.got_ref
  20.2 1.3 %collective-permute-start.6 = (bf16[128,128]{1,0:T(8,128)(2,1)S(1)}, bf16[128,128]{1,0:T(8,128)(2,1)S(1)}, u32[]{:S(2)}, u32[]{:S(2)}) collective-permute-start(bf16[128,128]{1,0:T(8,128)(2,1)S(1)} %add.8.mine_ref), channel_id=1, source_target_pairs={{0,5},{1,4},{2,7},{3,6},{4,1},{5,0},{6,3},{7,2},{8,13},{9,12},{10,... | collective-permute-start | bytes 98312 | tf_op jit(solution)/shard_map/ppermute | solution.py:397
  21.5 0.8 %collective-permute-done.4.got_ref = bf16[128,128]{1,0:T(8,128)(2,1)S(1)} collective-permute-done((bf16[128,128]{1,0:T(8,128)(2,1)S(1)}, bf16[128,128]{1,0:T(8,128)(2,1)S(1)}, u32[]{:S(2)}, u32[]{:S(2)}) %collective-permute-start.4) | collective-permute-done | bytes 32800 | tf_op jit(solution)/shard_map/ppermute | solution.py:397
  22.3 1.4 %collective-permute-done.6.got_ref = bf16[128,128]{1,0:T(8,128)(2,1)S(1)} collective-permute-done((bf16[128,128]{1,0:T(8,128)(2,1)S(1)}, bf16[128,128]{1,0:T(8,128)(2,1)S(1)}, u32[]{:S(2)}, u32[]{:S(2)}) %collective-permute-start.6) | collective-permute-done | bytes 32800 | tf_op jit(solution)/shard_map/ppermute | solution.py:397
  23.7 0.0 collective-permute-done.1.refs_0_.got_ref
  23.7 0.3 product_terms.1.mine_ref
  24.0 0.3 collective-permute-start.7
  24.4 0.9 %collective-permute-done.7.got_ref = bf16[128,128]{1,0:T(8,128)(2,1)S(1)} collective-permute-done((bf16[128,128]{1,0:T(8,128)(2,1)S(1)}, bf16[128,128]{1,0:T(8,128)(2,1)S(1)}, u32[]{:S(2)}, u32[]{:S(2)}) %collective-permute-start.7) | collective-permute-done | bytes 32800 | tf_op jit(solution)/shard_map/ppermute | solution.py:397
  25.3 2.6 %collective-permute-start.8 = (bf16[128,128]{1,0:T(8,128)(2,1)S(1)}, bf16[128,128]{1,0:T(8,128)(2,1)S(1)}, u32[]{:S(2)}, u32[]{:S(2)}) collective-permute-start(bf16[128,128]{1,0:T(8,128)(2,1)S(1)} %add.10.term_ref), channel_id=1, source_target_pairs={{0,3},{1,2},{2,1},{3,0},{4,7},{5,6},{6,5},{7,4},{8,11},{9,10},{10,... | collective-permute-start | bytes 98312 | tf_op jit(solution)/shard_map/ppermute | solution.py:397
  27.9 1.6 %collective-permute-done.8.got_ref.got_term_ref = bf16[128,128]{1,0:T(8,128)(2,1)S(1)} collective-permute-done((bf16[128,128]{1,0:T(8,128)(2,1)S(1)}, bf16[128,128]{1,0:T(8,128)(2,1)S(1)}, u32[]{:S(2)}, u32[]{:S(2)}) %collective-permute-start.8) | collective-permute-done | bytes 32800 | tf_op jit(solution)/shard_map/ppermute | solution.py:397
  29.5 0.4 local_gram.1.mine_ref
  29.9 0.9 %collective-permute-start.9 = (f32[32,128]{1,0:T(8,128)S(1)}, f32[32,128]{1,0:T(8,128)S(1)}, u32[]{:S(2)}, u32[]{:S(2)}) collective-permute-start(f32[32,128]{1,0:T(8,128)S(1)} %local_gram.1.mine_ref), channel_id=1, source_target_pairs={{0,5},{1,4},{2,7},{3,6},{4,1},{5,0},{6,3},{7,2},{8,13},{9,12},{10,... | collective-permute-start | bytes 49160 | tf_op jit(solution)/shard_map/ppermute | solution.py:397
  30.8 2.3 %collective-permute-done.9.got_ref = f32[32,128]{1,0:T(8,128)S(1)} collective-permute-done((f32[32,128]{1,0:T(8,128)S(1)}, f32[32,128]{1,0:T(8,128)S(1)}, u32[]{:S(2)}, u32[]{:S(2)}) %collective-permute-start.9) | collective-permute-done | bytes 16416 | tf_op jit(solution)/shard_map/ppermute | solution.py:397
  33.1 1.6 %collective-permute-start.10 = (f32[32,128]{1,0:T(8,128)S(1)}, f32[32,128]{1,0:T(8,128)S(1)}, u32[]{:S(2)}, u32[]{:S(2)}) collective-permute-start(f32[32,128]{1,0:T(8,128)S(1)} %add.11.gram_ref), channel_id=1, source_target_pairs={{0,9},{1,8},{2,11},{3,10},{4,13},{5,12},{6,15},{7,14},{8,1},{9,0},... | collective-permute-start | bytes 49160 | tf_op jit(solution)/shard_map/ppermute | solution.py:397
  34.7 2.5 %collective-permute-done.10.got_gram_ref = f32[32,128]{1,0:T(8,128)S(1)} collective-permute-done((f32[32,128]{1,0:T(8,128)S(1)}, f32[32,128]{1,0:T(8,128)S(1)}, u32[]{:S(2)}, u32[]{:S(2)}) %collective-permute-start.10) | collective-permute-done | bytes 16416 | tf_op jit(solution)/shard_map/ppermute | solution.py:397
  37.2 3.3 %finish.1 = f32[64,64]{1,0:T(8,128)} custom-call(bf16[128,128]{1,0:T(8,128)(2,1)S(1)} %add.10.term_ref, bf16[128,128]{1,0:T(8,128)(2,1)S(1)} %collective-permute-done.8.got_ref.got_term_ref, f32[32,128]{1,0:T(8,128)S(1)} %add.11.gram_ref, f32[32,128]{1,0:T(8,128)S(1)} %collective-permute-done.10.got_gram_ref), custom_call_target="tpu_custom_call" | custom-call | tf_op jit(solution)/shard_map/finish/pallas_call | solution.py:378
  (7 shorter events, 0.1 us)
Async XLA Ops:
  0.0 0.9 %copy-start = (bf16[1024,64]{0,1:T(8,128)(2,1)S(1)}, bf16[1024,64]{0,1:T(8,128)(2,1)}, u32[]{:S(2)}) copy-start(bf16[1024,64]{0,1:T(8,128)(2,1)} %param.4) | copy-start | bytes 393220
  0.9 7.7 %copy-start.1 = (bf16[128,64]{0,1:T(8,128)(2,1)S(1)}, bf16[128,64]{0,1:T(8,128)(2,1)}, u32[]{:S(2)}) copy-start(bf16[128,64]{0,1:T(8,128)(2,1)} %param.5) | copy-start | bytes 49156
  6.2 2.4 %collective-permute-start = (bf16[128,1024]{1,0:T(8,128)(2,1)S(1)}, bf16[128,1024]{1,0:T(8,128)(2,1)S(1)}, u32[]{:S(2)}, u32[]{:S(2)}) collective-permute-start(bf16[128,1024]{1,0:T(8,128)(2,1)S(1)} %get-tuple-element.18), channel_id=1, source_target_pairs={{0,1},{1,0},{2,3},{3,2},{4,5},{5,4},{6,7},{7,6},{8,9},{9,8},{10,11... | collective-permute-start | bytes 786440 | tf_op jit(solution)/shard_map/ppermute | solution.py:397
  8.9 5.1 %collective-permute-start.2 = (bf16[256,128]{1,0:T(8,128)(2,1)S(1)}, bf16[256,128]{1,0:T(8,128)(2,1)S(1)}, u32[]{:S(2)}, u32[]{:S(2)}) collective-permute-start(bf16[256,128]{1,0:T(8,128)(2,1)S(1)} %get-tuple-element.22), channel_id=1, source_target_pairs={{0,3},{1,2},{2,1},{3,0},{4,7},{5,6},{6,5},{7,4},{8,11},{9,10},{10,... | collective-permute-start | bytes 196616 | tf_op jit(solution)/shard_map/ppermute | solution.py:397
  11.6 12.1 %collective-permute-start.1 = (bf16[128,512]{1,0:T(8,128)(2,1)S(1)}, bf16[128,512]{1,0:T(8,128)(2,1)S(1)}, u32[]{:S(2)}, u32[]{:S(2)}) collective-permute-start(bf16[128,512]{1,0:T(8,128)(2,1)S(1)} %get-tuple-element.20), channel_id=1, source_target_pairs={{0,3},{1,2},{2,1},{3,0},{4,7},{5,6},{6,5},{7,4},{8,11},{9,10},{10,... | collective-permute-start | bytes 393224 | tf_op jit(solution)/shard_map/ppermute | solution.py:397
  14.1 3.9 %collective-permute-start.3 = (bf16[128,128]{1,0:T(8,128)(2,1)S(1)}, bf16[128,128]{1,0:T(8,128)(2,1)S(1)}, u32[]{:S(2)}, u32[]{:S(2)}) collective-permute-start(bf16[128,128]{1,0:T(8,128)(2,1)S(1)} %get-tuple-element.23.mine_ref), channel_id=1, source_target_pairs={{0,5},{1,4},{2,7},{3,6},{4,1},{5,0},{6,3},{7,2},{8,13},{9,12},{10,... | collective-permute-start | bytes 98312 | tf_op jit(solution)/shard_map/ppermute | solution.py:397
  15.4 4.8 %collective-permute-start.5 = (bf16[128,128]{1,0:T(8,128)(2,1)S(1)}, bf16[128,128]{1,0:T(8,128)(2,1)S(1)}, u32[]{:S(2)}, u32[]{:S(2)}) collective-permute-start(bf16[128,128]{1,0:T(8,128)(2,1)S(1)} %get-tuple-element.24.mine_ref), channel_id=1, source_target_pairs={{0,9},{1,8},{2,11},{3,10},{4,13},{5,12},{6,15},{7,14},{8,1},{9,0},... | collective-permute-start | bytes 98312 | tf_op jit(solution)/shard_map/ppermute | solution.py:397
  18.0 4.3 %collective-permute-start.4 = (bf16[128,128]{1,0:T(8,128)(2,1)S(1)}, bf16[128,128]{1,0:T(8,128)(2,1)S(1)}, u32[]{:S(2)}, u32[]{:S(2)}) collective-permute-start(bf16[128,128]{1,0:T(8,128)(2,1)S(1)} %add.6.mine_ref), channel_id=1, source_target_pairs={{0,9},{1,8},{2,11},{3,10},{4,13},{5,12},{6,15},{7,14},{8,1},{9,0},... | collective-permute-start | bytes 98312 | tf_op jit(solution)/shard_map/ppermute | solution.py:397
  20.2 3.5 %collective-permute-start.6 = (bf16[128,128]{1,0:T(8,128)(2,1)S(1)}, bf16[128,128]{1,0:T(8,128)(2,1)S(1)}, u32[]{:S(2)}, u32[]{:S(2)}) collective-permute-start(bf16[128,128]{1,0:T(8,128)(2,1)S(1)} %add.8.mine_ref), channel_id=1, source_target_pairs={{0,5},{1,4},{2,7},{3,6},{4,1},{5,0},{6,3},{7,2},{8,13},{9,12},{10,... | collective-permute-start | bytes 98312 | tf_op jit(solution)/shard_map/ppermute | solution.py:397
  24.0 1.3 %collective-permute-start.7 = (bf16[128,128]{1,0:T(8,128)(2,1)S(1)}, bf16[128,128]{1,0:T(8,128)(2,1)S(1)}, u32[]{:S(2)}, u32[]{:S(2)}) collective-permute-start(bf16[128,128]{1,0:T(8,128)(2,1)S(1)} %product_terms.1.mine_ref), channel_id=1, source_target_pairs={{0,1},{1,0},{2,3},{3,2},{4,5},{5,4},{6,7},{7,6},{8,9},{9,8},{10,11... | collective-permute-start | bytes 98312 | tf_op jit(solution)/shard_map/ppermute | solution.py:397
  25.3 4.2 %collective-permute-start.8 = (bf16[128,128]{1,0:T(8,128)(2,1)S(1)}, bf16[128,128]{1,0:T(8,128)(2,1)S(1)}, u32[]{:S(2)}, u32[]{:S(2)}) collective-permute-start(bf16[128,128]{1,0:T(8,128)(2,1)S(1)} %add.10.term_ref), channel_id=1, source_target_pairs={{0,3},{1,2},{2,1},{3,0},{4,7},{5,6},{6,5},{7,4},{8,11},{9,10},{10,... | collective-permute-start | bytes 98312 | tf_op jit(solution)/shard_map/ppermute | solution.py:397
  29.9 3.2 %collective-permute-start.9 = (f32[32,128]{1,0:T(8,128)S(1)}, f32[32,128]{1,0:T(8,128)S(1)}, u32[]{:S(2)}, u32[]{:S(2)}) collective-permute-start(f32[32,128]{1,0:T(8,128)S(1)} %local_gram.1.mine_ref), channel_id=1, source_target_pairs={{0,5},{1,4},{2,7},{3,6},{4,1},{5,0},{6,3},{7,2},{8,13},{9,12},{10,... | collective-permute-start | bytes 49160 | tf_op jit(solution)/shard_map/ppermute | solution.py:397
  33.1 4.1 %collective-permute-start.10 = (f32[32,128]{1,0:T(8,128)S(1)}, f32[32,128]{1,0:T(8,128)S(1)}, u32[]{:S(2)}, u32[]{:S(2)}) collective-permute-start(f32[32,128]{1,0:T(8,128)S(1)} %add.11.gram_ref), channel_id=1, source_target_pairs={{0,9},{1,8},{2,11},{3,10},{4,13},{5,12},{6,15},{7,14},{8,1},{9,0},... | collective-permute-start | bytes 49160 | tf_op jit(solution)/shard_map/ppermute | solution.py:397

commit v17 on v14

--- a/solution.py
+++ b/solution.py
@@ -174,30 +174,48 @@
     )(mine, got, *after)
 
 
-def product_kernel(mine_ref, got_ref, projected_ref, out_ref):
-    blocks = mine_ref.shape[1] // LANES
-    rank = projected_ref.shape[0] // blocks
-    terms = []
-    for ref in (mine_ref, got_ref):
-        total = jnp.zeros((ref.shape[0], rank), F32)
-        for block in range(blocks):
-            projected = projected_ref[pl.ds(block * rank, rank), :]
-            where = slice(block * LANES, (block + 1) * LANES)
-            total += dot_f32(ref[:, where], projected, ((1,), (1,)))
-        terms.append(total)
+def halves_kernel(mine_ref, got_ref, low_ref, high_ref):
+    size = low_ref.shape[0]
+    for start, ref in ((0, low_ref), (size, high_ref)):
+        rows = pl.ds(start, size)
+        ref[...] = (mine_ref[rows, :] + got_ref[rows, :].astype(F32)).astype(BF16)
+
+
+def add_in_halves(mine, got):
+    out = jax.ShapeDtypeStruct((got.shape[0] // 2, LANES), BF16)
+    return pl.pallas_call(
+        halves_kernel,
+        out_shape=[out, out],
+        compiler_params=params(4),
+        name="add_in_halves",
+    )(mine, got)
+
+
+def product_kernel(mine_ref, got_ref, low_ref, high_ref, out_ref):
+    blocks = mine_ref.shape[1] // LANES // 2
+    rank = low_ref.shape[0] // blocks
+    projected = jnp.concatenate(
+        [
+            ref[pl.ds(block * rank, rank), :]
+            for ref in (low_ref, high_ref)
+            for block in range(blocks)
+        ],
+        axis=1,
+    )
+    terms = [dot_f32(ref[...], projected, ((1,), (1,))) for ref in (mine_ref, got_ref)]
     even = is_even()
     low = jnp.where(even, terms[0], terms[1])
     high = jnp.where(even, terms[1], terms[0])
     out_ref[...] = jnp.concatenate([low, high], axis=1).astype(BF16)
 
 
-def product_terms(mine, got, projected):
+def product_terms(mine, got, low, high):
     return pl.pallas_call(
         product_kernel,
         out_shape=jax.ShapeDtypeStruct((mine.shape[0], LANES), BF16),
         compiler_params=params(4),
         name="product_terms",
-    )(mine, got, projected)
+    )(mine, got, low, high)
 
 
 def pair_product(term_ref, got_ref):
@@ -207,7 +225,7 @@
 def gram_kernel(term_ref, got_ref, out_ref):
     product = pair_product(term_ref, got_ref)
     rank = LANES // 2
-    wide = dot_f32(product, product, ((0,), (0,)), lax.Precision.HIGHEST)
+    wide = dot_parts(product, product, 0)
     gram = wide[:rank, :rank] + wide[rank:, rank:]
     out_ref[...] = jnp.concatenate([gram[:rank // 2], gram[rank // 2:]], axis=1)
 
@@ -221,11 +239,16 @@
     )(term, got)
 
 
-def reciprocal(x):
-    guess = pl.reciprocal(x, approx=True, full_range=False)
-    for _ in range(2):
-        guess = guess * (2.0 - x * guess)
-    return guess
+def parts(x):
+    high = x.astype(BF16)
+    return high, (x - high.astype(F32)).astype(BF16)
+
+
+def dot_parts(a, b, axis):
+    (ah, al), (bh, bl) = parts(a), parts(b)
+    left = jnp.concatenate([ah, ah, al], axis=axis)
+    right = jnp.concatenate([bh, bl, bh], axis=axis)
+    return dot_f32(left, right, ((axis,), (axis,)))
 
 
 def eliminate(gram):
@@ -254,7 +277,7 @@
             if j:
                 found = jnp.where(sublane == j, block[j][j], found)
                 kept = jnp.where(sublane == j, rows[j], kept)
-            inverse = reciprocal(block[j][j])
+            inverse = pl.reciprocal(block[j][j], approx=True, full_range=False)
             scaled = {i: block[i][j] * inverse for i in range(j + 1, tile)}
             for i, factor in scaled.items():
                 for k in range(j + 1, i + 1):
@@ -282,7 +305,7 @@
     product = pair_product(term_ref, got_term_ref)
     product = jnp.where(lax.axis_index("col") == 0, product[:half], product[half:])
     mine = jnp.where(is_even(), product[:, :rank], product[:, rank:])
-    out_ref[...] = dot_f32(mine, inverse, ((1,), (1,)), lax.Precision.HIGHEST)
+    out_ref[...] = dot_parts(mine, inverse, 1)
 
 
 def finish(total_rows, term, got_term, gram, got_gram):
@@ -312,13 +335,15 @@
     own = contract(snapshot, wide, order, True)
 
     keep, send, columns, give = project(own, got, old_factor.T)
-    mine = add(keep, swap(send, masks[0]))
+    low, high = add_in_halves(keep, swap(send, masks[0]))
     got_columns = swap(give, masks[0])
-    for step, mask in enumerate(masks[1:]):
-        after = [got_columns] if step == 0 else []
-        mine = add(mine, swap(mine, mask), *after)
-
-    term = product_terms(columns, got_columns, mine)
+    others = masks[1:]
+    for step, (mask, turned) in enumerate(zip(others, others[1:] + others[:1])):
+        after = [got_columns] if step == 1 else []
+        got_low, got_high = swap(low, mask), swap(high, turned)
+        low, high = add(low, got_low), add(high, got_high, *after)
+
+    term = product_terms(columns, got_columns, low, high)
     term = add(term, swap(term, 0))
     got_term = swap(term, masks[0])
     gram = local_gram(term, got_term)

time: 40.9 us -> 40.1 us (0.980)
  waiting for transfers between devices: 16.6 us -> 11.9 us
  starting transfers between devices: 11.6 us -> 16.1 us
  Pallas kernels: 8.12 us -> 7.53 us
    ppermute x9 -> x11, waiting for transfers between devices: 16.6 us -> 11.9 us  [swap(): return lax.ppermute(x, ('row', 'col'), pairs)]
    ppermute x9 -> x11, starting transfers between devices: 11.6 us -> 16.1 us  [swap(): return lax.ppermute(x, ('row', 'col'), pairs)]
    pallas_call x1, Pallas kernels: 3.29 us -> 2.76 us  [finish(): pl.pallas_call(functools.partial(finish_kernel, total_rows), out_shape=ja...]
  transfers between devices with their start and end apart: 9 -> 11, of which waited for: 8 -> 7; matrix products, arithmetic and copies ran while one was open for 0% -> 0% of each run, Pallas kernels for 5% -> 5%
where the time goes in v17:
time: 40.1 us; the launch traced here: 39.9 us
  starting transfers between devices  16.1 us (40%)
  waiting for transfers between devices  11.9 us (30%)
  Pallas kernels  7.53 us (19%)
  local copies, waits for them, and re-layouts  4.28 us (11%)
    ppermute x11, starting transfers between devices, swap(): return lax.ppermute(x, ('row', 'col'), pairs)  16.1 us
    ppermute x11, waiting for transfers between devices, swap(): return lax.ppermute(x, ('row', 'col'), pairs)  11.9 us
    unnamed x6, local copies, waits for them, and re-layouts  4.28 us
    pallas_call x2, Pallas kernels, contract(): pl.pallas_call(functools.partial(contract_kernel, step, own), out_shape=j...  3.82 us
    pallas_call x1, Pallas kernels, finish(): pl.pallas_call(functools.partial(finish_kernel, total_rows), out_shape=ja...  2.76 us
  transfers between devices with their start and end apart: 11, of which 7 were waited for; matrix products, arithmetic and copies ran while one was open for 0% of the time, Pallas kernels for 5%

profile of v17, /device:TPU:0, one launch (start us, length us, event | category | flops | bytes accessed | tf_op | source)
XLA Modules:
  0.0 39.9 jit_solution(10767069120499370466)
XLA Ops:
  0.0 0.0 copy-start.1
  0.0 0.9 %copy-done.1 = bf16[1024,64]{0,1:T(8,128)(2,1)S(1)} copy-done((bf16[1024,64]{0,1:T(8,128)(2,1)S(1)}, bf16[1024,64]{0,1:T(8,128)(2,1)}, u32[]{:S(2)}) %copy-start.1) | copy-done | bytes 131096
  0.9 0.0 copy-start
  0.9 3.4 %copy-done = bf16[128,32,1024]{2,1,0:T(8,128)(2,1)S(1)} copy-done((bf16[128,32,1024]{2,1,0:T(8,128)(2,1)S(1)}, bf16[128,32,1024]{2,1,0:T(8,128)(2,1)}, u32[]{:S(2)}) %copy-start) | copy-done | bytes 8388632
  4.3 0.0 copy-start.2
  4.3 1.9 %contract_send.1 = bf16[128,1024]{1,0:T(8,128)(2,1)S(1)} custom-call(bf16[128,32,1024]{2,1,0:T(8,128)(2,1)S(1)} %copy-done, bf16[128,1024]{1,0:T(8,128)(2,1)S(1)} %get-tuple-element.13.wide_ref, bf16[64,256]{1,0:T(8,128)(2,1)S(1)} %get-tuple-element.14.order_ref), custom_call_target="tpu_custom_call" | custom-call | tf_op jit(solution)/shard_map/contract_send/pallas_call | solution.py:110
  6.2 0.5 %collective-permute-start = (bf16[128,1024]{1,0:T(8,128)(2,1)S(1)}, bf16[128,1024]{1,0:T(8,128)(2,1)S(1)}, u32[]{:S(2)}, u32[]{:S(2)}) collective-permute-start(bf16[128,1024]{1,0:T(8,128)(2,1)S(1)} %contract_send.1), channel_id=1, source_target_pairs={{0,1},{1,0},{2,3},{3,2},{4,5},{5,4},{6,7},{7,6},{8,9},{9,8},{10,11... | collective-permute-start | bytes 786440 | tf_op jit(solution)/shard_map/ppermute | solution.py:331
  6.7 1.9 %contract_own.1.own_ref = bf16[128,1024]{1,0:T(8,128)(2,1)S(1)} custom-call(bf16[128,32,1024]{2,1,0:T(8,128)(2,1)S(1)} %copy-done, bf16[128,1024]{1,0:T(8,128)(2,1)S(1)} %get-tuple-element.13.wide_ref, bf16[64,256]{1,0:T(8,128)(2,1)S(1)} %get-tuple-element.14.order_ref), custom_call_target="tpu_custom_call" | custom-call | tf_op jit(solution)/shard_map/contract_own/pallas_call | solution.py:110
  8.7 0.0 collective-permute-done.got_ref
  8.7 0.0 copy-done.2
  8.7 0.2 project.1
  8.9 2.7 %collective-permute-start.2 = (bf16[256,128]{1,0:T(8,128)(2,1)S(1)}, bf16[256,128]{1,0:T(8,128)(2,1)S(1)}, u32[]{:S(2)}, u32[]{:S(2)}) collective-permute-start(bf16[256,128]{1,0:T(8,128)(2,1)S(1)} %get-tuple-element.18), channel_id=1, source_target_pairs={{0,3},{1,2},{2,1},{3,0},{4,7},{5,6},{6,5},{7,4},{8,11},{9,10},{10,... | collective-permute-start | bytes 196616 | tf_op jit(solution)/shard_map/ppermute | solution.py:331
  11.7 0.0 collective-permute-start.1
  11.7 2.4 %collective-permute-done.2.got_ref = bf16[256,128]{1,0:T(8,128)(2,1)S(1)} collective-permute-done((bf16[256,128]{1,0:T(8,128)(2,1)S(1)}, bf16[256,128]{1,0:T(8,128)(2,1)S(1)}, u32[]{:S(2)}, u32[]{:S(2)}) %collective-permute-start.2) | collective-permute-done | bytes 65568 | tf_op jit(solution)/shard_map/ppermute | solution.py:331
  14.1 1.4 %collective-permute-start.3 = (bf16[128,128]{1,0:T(8,128)(2,1)S(1)}, bf16[128,128]{1,0:T(8,128)(2,1)S(1)}, u32[]{:S(2)}, u32[]{:S(2)}) collective-permute-start(bf16[128,128]{1,0:T(8,128)(2,1)S(1)} %get-tuple-element.19.mine_ref), channel_id=1, source_target_pairs={{0,5},{1,4},{2,7},{3,6},{4,1},{5,0},{6,3},{7,2},{8,13},{9,12},{10,... | collective-permute-start | bytes 98312 | tf_op jit(solution)/shard_map/ppermute | solution.py:331
  15.5 2.5 %collective-permute-start.5 = (bf16[128,128]{1,0:T(8,128)(2,1)S(1)}, bf16[128,128]{1,0:T(8,128)(2,1)S(1)}, u32[]{:S(2)}, u32[]{:S(2)}) collective-permute-start(bf16[128,128]{1,0:T(8,128)(2,1)S(1)} %get-tuple-element.20.mine_ref), channel_id=1, source_target_pairs={{0,9},{1,8},{2,11},{3,10},{4,13},{5,12},{6,15},{7,14},{8,1},{9,0},... | collective-permute-start | bytes 98312 | tf_op jit(solution)/shard_map/ppermute | solution.py:331
  18.0 0.0 collective-permute-done.3.got_ref
  18.0 2.1 %collective-permute-start.4 = (bf16[128,128]{1,0:T(8,128)(2,1)S(1)}, bf16[128,128]{1,0:T(8,128)(2,1)S(1)}, u32[]{:S(2)}, u32[]{:S(2)}) collective-permute-start(bf16[128,128]{1,0:T(8,128)(2,1)S(1)} %add.6.mine_ref), channel_id=1, source_target_pairs={{0,9},{1,8},{2,11},{3,10},{4,13},{5,12},{6,15},{7,14},{8,1},{9,0},... | collective-permute-start | bytes 98312 | tf_op jit(solution)/shard_map/ppermute | solution.py:331
  20.2 0.0 collective-permute-done.5.got_ref
  20.2 1.3 %collective-permute-start.6 = (bf16[128,128]{1,0:T(8,128)(2,1)S(1)}, bf16[128,128]{1,0:T(8,128)(2,1)S(1)}, u32[]{:S(2)}, u32[]{:S(2)}) collective-permute-start(bf16[128,128]{1,0:T(8,128)(2,1)S(1)} %add.8.mine_ref), channel_id=1, source_target_pairs={{0,5},{1,4},{2,7},{3,6},{4,1},{5,0},{6,3},{7,2},{8,13},{9,12},{10,... | collective-permute-start | bytes 98312 | tf_op jit(solution)/shard_map/ppermute | solution.py:331
  21.5 0.8 %collective-permute-done.4.got_ref = bf16[128,128]{1,0:T(8,128)(2,1)S(1)} collective-permute-done((bf16[128,128]{1,0:T(8,128)(2,1)S(1)}, bf16[128,128]{1,0:T(8,128)(2,1)S(1)}, u32[]{:S(2)}, u32[]{:S(2)}) %collective-permute-start.4) | collective-permute-done | bytes 32800 | tf_op jit(solution)/shard_map/ppermute | solution.py:331
  22.4 1.4 %collective-permute-done.6.got_ref = bf16[128,128]{1,0:T(8,128)(2,1)S(1)} collective-permute-done((bf16[128,128]{1,0:T(8,128)(2,1)S(1)}, bf16[128,128]{1,0:T(8,128)(2,1)S(1)}, u32[]{:S(2)}, u32[]{:S(2)}) %collective-permute-start.6) | collective-permute-done | bytes 32800 | tf_op jit(solution)/shard_map/ppermute | solution.py:331
  23.8 0.0 collective-permute-done.1.refs_0_.got_ref
  23.8 0.3 product_terms.1.mine_ref
  24.1 0.4 collective-permute-start.7
  24.4 0.9 %collective-permute-done.7.got_ref = bf16[128,128]{1,0:T(8,128)(2,1)S(1)} collective-permute-done((bf16[128,128]{1,0:T(8,128)(2,1)S(1)}, bf16[128,128]{1,0:T(8,128)(2,1)S(1)}, u32[]{:S(2)}, u32[]{:S(2)}) %collective-permute-start.7) | collective-permute-done | bytes 32800 | tf_op jit(solution)/shard_map/ppermute | solution.py:331
  25.3 2.6 %collective-permute-start.8 = (bf16[128,128]{1,0:T(8,128)(2,1)S(1)}, bf16[128,128]{1,0:T(8,128)(2,1)S(1)}, u32[]{:S(2)}, u32[]{:S(2)}) collective-permute-start(bf16[128,128]{1,0:T(8,128)(2,1)S(1)} %add.10.term_ref), channel_id=1, source_target_pairs={{0,3},{1,2},{2,1},{3,0},{4,7},{5,6},{6,5},{7,4},{8,11},{9,10},{10,... | collective-permute-start | bytes 98312 | tf_op jit(solution)/shard_map/ppermute | solution.py:331
  28.0 1.6 %collective-permute-done.8.got_ref.got_term_ref = bf16[128,128]{1,0:T(8,128)(2,1)S(1)} collective-permute-done((bf16[128,128]{1,0:T(8,128)(2,1)S(1)}, bf16[128,128]{1,0:T(8,128)(2,1)S(1)}, u32[]{:S(2)}, u32[]{:S(2)}) %collective-permute-start.8) | collective-permute-done | bytes 32800 | tf_op jit(solution)/shard_map/ppermute | solution.py:331
  29.6 0.3 local_gram.1.mine_ref
  29.9 0.8 %collective-permute-start.9 = (f32[32,128]{1,0:T(8,128)S(1)}, f32[32,128]{1,0:T(8,128)S(1)}, u32[]{:S(2)}, u32[]{:S(2)}) collective-permute-start(f32[32,128]{1,0:T(8,128)S(1)} %local_gram.1.mine_ref), channel_id=1, source_target_pairs={{0,5},{1,4},{2,7},{3,6},{4,1},{5,0},{6,3},{7,2},{8,13},{9,12},{10,... | collective-permute-start | bytes 49160 | tf_op jit(solution)/shard_map/ppermute | solution.py:331
  30.8 2.3 %collective-permute-done.9.got_ref = f32[32,128]{1,0:T(8,128)S(1)} collective-permute-done((f32[32,128]{1,0:T(8,128)S(1)}, f32[32,128]{1,0:T(8,128)S(1)}, u32[]{:S(2)}, u32[]{:S(2)}) %collective-permute-start.9) | collective-permute-done | bytes 16416 | tf_op jit(solution)/shard_map/ppermute | solution.py:331
  33.1 1.6 %collective-permute-start.10 = (f32[32,128]{1,0:T(8,128)S(1)}, f32[32,128]{1,0:T(8,128)S(1)}, u32[]{:S(2)}, u32[]{:S(2)}) collective-permute-start(f32[32,128]{1,0:T(8,128)S(1)} %add.11.gram_ref), channel_id=1, source_target_pairs={{0,9},{1,8},{2,11},{3,10},{4,13},{5,12},{6,15},{7,14},{8,1},{9,0},... | collective-permute-start | bytes 49160 | tf_op jit(solution)/shard_map/ppermute | solution.py:331
  34.7 2.5 %collective-permute-done.10.got_gram_ref = f32[32,128]{1,0:T(8,128)S(1)} collective-permute-done((f32[32,128]{1,0:T(8,128)S(1)}, f32[32,128]{1,0:T(8,128)S(1)}, u32[]{:S(2)}, u32[]{:S(2)}) %collective-permute-start.10) | collective-permute-done | bytes 16416 | tf_op jit(solution)/shard_map/ppermute | solution.py:331
  37.2 2.8 %finish.1 = f32[64,64]{1,0:T(8,128)} custom-call(bf16[128,128]{1,0:T(8,128)(2,1)S(1)} %add.10.term_ref, bf16[128,128]{1,0:T(8,128)(2,1)S(1)} %collective-permute-done.8.got_ref.got_term_ref, f32[32,128]{1,0:T(8,128)S(1)} %add.11.gram_ref, f32[32,128]{1,0:T(8,128)S(1)} %collective-permute-done.10.got_gram_ref), custom_call_target="tpu_custom_call" | custom-call | tf_op jit(solution)/shard_map/finish/pallas_call | solution.py:312
  (8 shorter events, 0.1 us)
Async XLA Ops:
  0.0 0.9 %copy-start.1 = (bf16[1024,64]{0,1:T(8,128)(2,1)S(1)}, bf16[1024,64]{0,1:T(8,128)(2,1)}, u32[]{:S(2)}) copy-start(bf16[1024,64]{0,1:T(8,128)(2,1)} %param.4) | copy-start | bytes 393220
  0.9 3.4 %copy-start = (bf16[128,32,1024]{2,1,0:T(8,128)(2,1)S(1)}, bf16[128,32,1024]{2,1,0:T(8,128)(2,1)}, u32[]{:S(2)}) copy-start(bf16[128,32,1024]{2,1,0:T(8,128)(2,1)} %snapshot_ref.3) | copy-start | bytes 25165828
  4.3 4.4 %copy-start.2 = (bf16[128,64]{0,1:T(8,128)(2,1)S(1)}, bf16[128,64]{0,1:T(8,128)(2,1)}, u32[]{:S(2)}) copy-start(bf16[128,64]{0,1:T(8,128)(2,1)} %param.5) | copy-start | bytes 49156
  6.2 2.4 %collective-permute-start = (bf16[128,1024]{1,0:T(8,128)(2,1)S(1)}, bf16[128,1024]{1,0:T(8,128)(2,1)S(1)}, u32[]{:S(2)}, u32[]{:S(2)}) collective-permute-start(bf16[128,1024]{1,0:T(8,128)(2,1)S(1)} %contract_send.1), channel_id=1, source_target_pairs={{0,1},{1,0},{2,3},{3,2},{4,5},{5,4},{6,7},{7,6},{8,9},{9,8},{10,11... | collective-permute-start | bytes 786440 | tf_op jit(solution)/shard_map/ppermute | solution.py:331
  8.9 5.2 %collective-permute-start.2 = (bf16[256,128]{1,0:T(8,128)(2,1)S(1)}, bf16[256,128]{1,0:T(8,128)(2,1)S(1)}, u32[]{:S(2)}, u32[]{:S(2)}) collective-permute-start(bf16[256,128]{1,0:T(8,128)(2,1)S(1)} %get-tuple-element.18), channel_id=1, source_target_pairs={{0,3},{1,2},{2,1},{3,0},{4,7},{5,6},{6,5},{7,4},{8,11},{9,10},{10,... | collective-permute-start | bytes 196616 | tf_op jit(solution)/shard_map/ppermute | solution.py:331
  11.7 12.1 %collective-permute-start.1 = (bf16[128,512]{1,0:T(8,128)(2,1)S(1)}, bf16[128,512]{1,0:T(8,128)(2,1)S(1)}, u32[]{:S(2)}, u32[]{:S(2)}) collective-permute-start(bf16[128,512]{1,0:T(8,128)(2,1)S(1)} %get-tuple-element.16), channel_id=1, source_target_pairs={{0,3},{1,2},{2,1},{3,0},{4,7},{5,6},{6,5},{7,4},{8,11},{9,10},{10,... | collective-permute-start | bytes 393224 | tf_op jit(solution)/shard_map/ppermute | solution.py:331
  14.1 3.9 %collective-permute-start.3 = (bf16[128,128]{1,0:T(8,128)(2,1)S(1)}, bf16[128,128]{1,0:T(8,128)(2,1)S(1)}, u32[]{:S(2)}, u32[]{:S(2)}) collective-permute-start(bf16[128,128]{1,0:T(8,128)(2,1)S(1)} %get-tuple-element.19.mine_ref), channel_id=1, source_target_pairs={{0,5},{1,4},{2,7},{3,6},{4,1},{5,0},{6,3},{7,2},{8,13},{9,12},{10,... | collective-permute-start | bytes 98312 | tf_op jit(solution)/shard_map/ppermute | solution.py:331
  15.5 4.7 %collective-permute-start.5 = (bf16[128,128]{1,0:T(8,128)(2,1)S(1)}, bf16[128,128]{1,0:T(8,128)(2,1)S(1)}, u32[]{:S(2)}, u32[]{:S(2)}) collective-permute-start(bf16[128,128]{1,0:T(8,128)(2,1)S(1)} %get-tuple-element.20.mine_ref), channel_id=1, source_target_pairs={{0,9},{1,8},{2,11},{3,10},{4,13},{5,12},{6,15},{7,14},{8,1},{9,0},... | collective-permute-start | bytes 98312 | tf_op jit(solution)/shard_map/ppermute | solution.py:331
  18.0 4.3 %collective-permute-start.4 = (bf16[128,128]{1,0:T(8,128)(2,1)S(1)}, bf16[128,128]{1,0:T(8,128)(2,1)S(1)}, u32[]{:S(2)}, u32[]{:S(2)}) collective-permute-start(bf16[128,128]{1,0:T(8,128)(2,1)S(1)} %add.6.mine_ref), channel_id=1, source_target_pairs={{0,9},{1,8},{2,11},{3,10},{4,13},{5,12},{6,15},{7,14},{8,1},{9,0},... | collective-permute-start | bytes 98312 | tf_op jit(solution)/shard_map/ppermute | solution.py:331
  20.2 3.5 %collective-permute-start.6 = (bf16[128,128]{1,0:T(8,128)(2,1)S(1)}, bf16[128,128]{1,0:T(8,128)(2,1)S(1)}, u32[]{:S(2)}, u32[]{:S(2)}) collective-permute-start(bf16[128,128]{1,0:T(8,128)(2,1)S(1)} %add.8.mine_ref), channel_id=1, source_target_pairs={{0,5},{1,4},{2,7},{3,6},{4,1},{5,0},{6,3},{7,2},{8,13},{9,12},{10,... | collective-permute-start | bytes 98312 | tf_op jit(solution)/shard_map/ppermute | solution.py:331
  24.1 1.3 %collective-permute-start.7 = (bf16[128,128]{1,0:T(8,128)(2,1)S(1)}, bf16[128,128]{1,0:T(8,128)(2,1)S(1)}, u32[]{:S(2)}, u32[]{:S(2)}) collective-permute-start(bf16[128,128]{1,0:T(8,128)(2,1)S(1)} %product_terms.1.mine_ref), channel_id=1, source_target_pairs={{0,1},{1,0},{2,3},{3,2},{4,5},{5,4},{6,7},{7,6},{8,9},{9,8},{10,11... | collective-permute-start | bytes 98312 | tf_op jit(solution)/shard_map/ppermute | solution.py:331
  25.3 4.2 %collective-permute-start.8 = (bf16[128,128]{1,0:T(8,128)(2,1)S(1)}, bf16[128,128]{1,0:T(8,128)(2,1)S(1)}, u32[]{:S(2)}, u32[]{:S(2)}) collective-permute-start(bf16[128,128]{1,0:T(8,128)(2,1)S(1)} %add.10.term_ref), channel_id=1, source_target_pairs={{0,3},{1,2},{2,1},{3,0},{4,7},{5,6},{6,5},{7,4},{8,11},{9,10},{10,... | collective-permute-start | bytes 98312 | tf_op jit(solution)/shard_map/ppermute | solution.py:331
  29.9 3.2 %collective-permute-start.9 = (f32[32,128]{1,0:T(8,128)S(1)}, f32[32,128]{1,0:T(8,128)S(1)}, u32[]{:S(2)}, u32[]{:S(2)}) collective-permute-start(f32[32,128]{1,0:T(8,128)S(1)} %local_gram.1.mine_ref), channel_id=1, source_target_pairs={{0,5},{1,4},{2,7},{3,6},{4,1},{5,0},{6,3},{7,2},{8,13},{9,12},{10,... | collective-permute-start | bytes 49160 | tf_op jit(solution)/shard_map/ppermute | solution.py:331
  33.1 4.1 %collective-permute-start.10 = (f32[32,128]{1,0:T(8,128)S(1)}, f32[32,128]{1,0:T(8,128)S(1)}, u32[]{:S(2)}, u32[]{:S(2)}) collective-permute-start(f32[32,128]{1,0:T(8,128)S(1)} %add.11.gram_ref), channel_id=1, source_target_pairs={{0,9},{1,8},{2,11},{3,10},{4,13},{5,12},{6,15},{7,14},{8,1},{9,0},... | collective-permute-start | bytes 49160 | tf_op jit(solution)/shard_map/ppermute | solution.py:331

commit v18 on v17

--- a/solution.py
+++ b/solution.py
@@ -32,88 +32,157 @@
 TILE = 8
 
 
-def prepare_kernel(fibers, mode2_ref, wide_ref, order_ref):
-    rank = mode2_ref.shape[0]
-    reps = LANES // rank
-    wide_ref[...] = jnp.concatenate([mode2_ref[...]] * reps, axis=0)
-    block = TILE * fibers
+def fill_order(order_ref, half):
+    block = TILE * half
     to = lax.broadcasted_iota(jnp.int32, order_ref.shape, 0)
     at = lax.broadcasted_iota(jnp.int32, order_ref.shape, 1)
-    cell = lax.div(lax.rem(at, block), fibers)
-    wanted = lax.div(to, TILE) * reps + lax.div(at, block)
-    same = (lax.rem(to, TILE) == cell) & (wanted == lax.rem(at, fibers))
+    cell = lax.div(lax.rem(at, block), half)
+    wanted = lax.div(to, TILE) * (order_ref.shape[1] // block) + lax.div(at, block)
+    same = (lax.rem(to, TILE) == cell) & (wanted == lax.rem(at, half))
     order_ref[...] = same.astype(F32).astype(BF16)
 
 
-def prepare(mode2_t, fibers):
-    rank, depth = mode2_t.shape
+def multiply(slab, wide_ref, flat_ref):
+    cells, half, depth = slab.shape
+    x = slab.reshape(cells * half, depth)
+    low = dot_f32(x[:, :depth // 2], wide_ref[:, :depth // 2], ((1,), (1,)))
+    high = dot_f32(x[:, depth // 2:], wide_ref[:, depth // 2:], ((1,), (1,)))
+    flat_ref[...] = (low + high).astype(BF16)
+
+
+def spread(half, flat_ref, order_ref, core_ref, start):
+    block = TILE * half
+    reps = order_ref.shape[1] // block
+    step = flat_ref.shape[0] // half
+    group = lax.div(lax.broadcasted_iota(jnp.int32, (block, LANES), 1), LANES // reps)
+    spreads = []
+    for b in range(step // TILE):
+        flat = flat_ref[pl.ds(b * block, block), :].astype(F32)
+        groups = [jnp.where(group == r, flat, 0.0).astype(BF16) for r in range(reps)]
+        spreads.append(dot_f32(order_ref[...], jnp.concatenate(groups, axis=0), ((1,), (0,))))
+    for p in range(half // reps):
+        part = jnp.concatenate([x[p * TILE:(p + 1) * TILE] for x in spreads], axis=0)
+        core_ref[pl.ds(start, step), p * LANES:(p + 1) * LANES] = part.astype(BF16)
+
+
+STEP = 32
+
+
+def slab_copies(snapshot_ref, first, slab_ref, half_index, sem):
+    half = slab_ref.shape[1]
+    fibers = pl.ds(pl.multiple_of(half_index * half, half), half)
+
+    def copy(start, size):
+        return pltpu.make_async_copy(
+            snapshot_ref.at[pl.ds(start, size), fibers],
+            slab_ref.at[pl.ds(start - first, size)],
+            sem,
+        )
+
+    def start(begin, size, count):
+        for part in range(count):
+            copy(begin + part * (size // count), size // count).start()
+
+    return start, lambda begin, size: copy(begin, size).wait()
+
+
+def send_kernel(
+    snapshot_ref, mode2_ref, core_ref, kept_ref, wide_ref, order_ref,
+    slab_ref, small_ref, even_ref, odd_ref, sems, kept_sem, small_sem,
+):
+    cells, half, _ = slab_ref.shape
+    rank = mode2_ref.shape[0]
+    chunks = cells // STEP
+    kept = kept_ref.shape[0]
+    flat = (even_ref, odd_ref)
+    sends = [
+        slab_copies(snapshot_ref, 0, slab_ref, 1 - own_half(), sems.at[chunk])
+        for chunk in range(chunks)
+    ]
+    start_kept, wait_kept = slab_copies(snapshot_ref, 0, kept_ref, own_half(), kept_sem)
+
+    small = pltpu.make_async_copy(mode2_ref, small_ref, small_sem)
+    small.start()
+    for chunk in range(min(3, chunks)):
+        sends[chunk][0](chunk * STEP, STEP, 2 if chunk else 4)
+    fill_order(order_ref, half)
+    small.wait()
+    wide_ref[...] = jnp.concatenate([small_ref[...]] * (LANES // rank), axis=0)
+    for chunk in range(chunks):
+        sends[chunk][1](chunk * STEP, STEP)
+        if chunk + 3 < chunks:
+            sends[chunk + 3][0]((chunk + 3) * STEP, STEP, 2)
+        if chunk * STEP < kept:
+            start_kept(chunk * STEP, STEP, 2)
+        multiply(slab_ref[pl.ds(chunk * STEP, STEP)], wide_ref, flat[chunk % 2])
+        if chunk:
+            spread(half, flat[(chunk - 1) % 2], order_ref, core_ref, (chunk - 1) * STEP)
+    spread(half, flat[(chunks - 1) % 2], order_ref, core_ref, (chunks - 1) * STEP)
+    wait_kept(0, kept)
+
+
+def contract_send(snapshot, mode2_t):
+    cells, fibers, depth = snapshot.shape
+    rank = mode2_t.shape[0]
+    half = fibers // 2
     reps = LANES // rank
-    block = TILE * fibers
-    return pl.pallas_call(
-        functools.partial(prepare_kernel, fibers),
+    block = TILE * half
+    pinned = pl.BlockSpec(memory_space=pltpu.HBM)
+    return pl.pallas_call(
+        send_kernel,
+        in_specs=[pinned, pinned],
         out_shape=[
+            jax.ShapeDtypeStruct((cells, half * rank), BF16),
+            jax.ShapeDtypeStruct((cells // 2, half, depth), BF16),
             jax.ShapeDtypeStruct((LANES, depth), BF16),
             jax.ShapeDtypeStruct((block // reps, block * reps), BF16),
         ],
-        compiler_params=params(4),
-        cost_estimate=pl.CostEstimate(flops=0, bytes_accessed=2**24, transcendentals=0),
-        name="prepare",
-    )(mode2_t)
-
-
-def contract_kernel(step, own, snapshot_ref, wide_ref, order_ref, core_ref, even_ref, odd_ref):
-    cells, fibers, depth = snapshot_ref.shape
-    half = fibers // 2
-    block = TILE * half
-    reps = order_ref.shape[1] // block
-    rank = LANES // reps
-    chunks = cells // step
-    lane = lax.broadcasted_iota(jnp.int32, (block, LANES), 1)
-    start = own_half() if own else 1 - own_half()
-    start = pl.multiple_of(start * half, half)
-
-    def multiply(chunk, flat_ref):
-        x = snapshot_ref[pl.ds(chunk * step, step), pl.ds(start, half), :]
-        x = x.reshape(step * half, depth)
-        low = dot_f32(x[:, :depth // 2], wide_ref[:, :depth // 2], ((1,), (1,)))
-        high = dot_f32(x[:, depth // 2:], wide_ref[:, depth // 2:], ((1,), (1,)))
-        flat_ref[...] = (low + high).astype(BF16)
-
-    def spread(chunk, flat_ref):
-        rows = pl.ds(pl.multiple_of(chunk * step, step), step)
-        spreads = []
-        for b in range(step // TILE):
-            flat = flat_ref[pl.ds(b * block, block), :].astype(F32)
-            groups = [
-                jnp.where(lax.div(lane, rank) == r, flat, 0.0).astype(BF16) for r in range(reps)
-            ]
-            spreads.append(dot_f32(order_ref[...], jnp.concatenate(groups, axis=0), ((1,), (0,))))
-        for p in range(half // reps):
-            part = jnp.concatenate([x[p * TILE:(p + 1) * TILE] for x in spreads], axis=0)
-            core_ref[rows, p * LANES:(p + 1) * LANES] = part.astype(BF16)
-
-    def two_chunks(pair, _):
-        multiply(2 * pair, even_ref)
-        spread(jnp.maximum(2 * pair - 1, 0), odd_ref)
-        multiply(2 * pair + 1, odd_ref)
-        spread(2 * pair, even_ref)
-        return _
-
-    lax.fori_loop(0, chunks // 2, two_chunks, 0)
-    spread(chunks - 1, odd_ref)
-
-
-def contract(snapshot, wide, order, own):
-    cells, fibers, depth = snapshot.shape
-    step = 32
-    reps = order.shape[1] // (TILE * fibers // 2)
-    return pl.pallas_call(
-        functools.partial(contract_kernel, step, own),
-        out_shape=jax.ShapeDtypeStruct((cells, fibers // 2 // reps * LANES), BF16),
-        scratch_shapes=[pltpu.VMEM((step * fibers // 2, LANES), BF16)] * 2,
+        scratch_shapes=[
+            pltpu.VMEM((cells, half, depth), BF16),
+            pltpu.VMEM((rank, depth), BF16),
+            pltpu.VMEM((STEP * half, LANES), BF16),
+            pltpu.VMEM((STEP * half, LANES), BF16),
+            pltpu.SemaphoreType.DMA((cells // STEP,)),
+            pltpu.SemaphoreType.DMA,
+            pltpu.SemaphoreType.DMA,
+        ],
         compiler_params=params(24),
-        name="contract_own" if own else "contract_send",
-    )(snapshot, wide, order)
+        name="contract_send",
+    )(snapshot, mode2_t)
+
+
+def own_kernel(
+    kept_ref, snapshot_ref, wide_ref, order_ref, core_ref, rest_ref, even_ref, odd_ref, sem
+):
+    kept, half, _ = kept_ref.shape
+    rest = rest_ref.shape[0]
+    start, wait = slab_copies(snapshot_ref, kept, rest_ref, own_half(), sem)
+    start(kept, rest, 4)
+    multiply(kept_ref[...], wide_ref, even_ref)
+    wait(kept, rest)
+    multiply(rest_ref[...], wide_ref, odd_ref)
+    spread(half, even_ref, order_ref, core_ref, 0)
+    spread(half, odd_ref, order_ref, core_ref, kept)
+
+
+def contract_own(kept, snapshot, wide, order):
+    cells = snapshot.shape[0]
+    rows, half, depth = kept.shape
+    reps = order.shape[1] // (TILE * half)
+    whole = pl.BlockSpec(memory_space=pltpu.VMEM)
+    return pl.pallas_call(
+        own_kernel,
+        in_specs=[whole, pl.BlockSpec(memory_space=pltpu.HBM), whole, whole],
+        out_shape=jax.ShapeDtypeStruct((cells, half // reps * LANES), BF16),
+        scratch_shapes=[
+            pltpu.VMEM((cells - rows, half, depth), BF16),
+            pltpu.VMEM((rows * half, LANES), BF16),
+            pltpu.VMEM(((cells - rows) * half, LANES), BF16),
+            pltpu.SemaphoreType.DMA,
+        ],
+        compiler_params=params(24),
+        name="contract_own",
+    )(kept, snapshot, wide, order)
 
 
 def is_even():
@@ -330,9 +399,11 @@
         ]
         return lax.ppermute(x, ("row", "col"), pairs)
 
-    wide, order = prepare(mode2_factor.T, snapshot.shape[1] // 2)
-    got = swap(contract(snapshot, wide, order, False), 0)
-    own = contract(snapshot, wide, order, True)
+    snapshot = pltpu.with_memory_space_constraint(snapshot, pltpu.HBM)
+    mode2_t = pltpu.with_memory_space_constraint(mode2_factor.T, pltpu.HBM)
+    send, kept, wide, order = contract_send(snapshot, mode2_t)
+    got = swap(send, 0)
+    own = contract_own(kept, snapshot, wide, order)
 
     keep, send, columns, give = project(own, got, old_factor.T)
     low, high = add_in_halves(keep, swap(send, masks[0]))

time: 40.1 us -> 40.3 us (level)
  Pallas kernels: 7.53 us -> 12.1 us
  local copies, waits for them, and re-layouts: 4.28 us -> 0.01 us
    pallas_call x3 -> x2, Pallas kernels: 3.84 us -> 8.38 us  [the longest x1 4.31 us: contract_send(): pl.pallas_call(send_kernel, in_specs=[pinned, pinned], out_shape=[jax.Sha...]
    unnamed x6 -> x2, local copies, waits for them, and re-layouts: 4.28 us -> 0.01 us
  transfers between devices with their start and end apart: 11 -> 11, of which waited for: 7 -> 7; matrix products, arithmetic and copies ran while one was open for 0% -> 0% of each run, Pallas kernels for 5% -> 10%
where the time goes in v18:
time: 40.3 us; the launch traced here: 40.2 us
  starting transfers between devices  16.1 us (40%)
  Pallas kernels  12.1 us (30%)
  waiting for transfers between devices  12 us (30%)
    ppermute x11, starting transfers between devices, swap(): return lax.ppermute(x, ('row', 'col'), pairs)  16.1 us
    ppermute x11, waiting for transfers between devices, swap(): return lax.ppermute(x, ('row', 'col'), pairs)  12 us
    pallas_call x1, Pallas kernels, contract_send(): pl.pallas_call(send_kernel, in_specs=[pinned, pinned], out_shape=[jax.Sha...  4.31 us
    pallas_call x1, Pallas kernels, contract_own(): pl.pallas_call(own_kernel, in_specs=[whole, pl.BlockSpec(memory_space=plt...  4.07 us
    pallas_call x1, Pallas kernels, finish(): pl.pallas_call(functools.partial(finish_kernel, total_rows), out_shape=ja...  2.76 us
  transfers between devices with their start and end apart: 11, of which 7 were waited for; matrix products, arithmetic and copies ran while one was open for 0% of the time, Pallas kernels for 10%

profile of v18, /device:TPU:0, one launch (start us, length us, event | category | flops | bytes accessed | tf_op | source)
XLA Modules:
  0.0 40.2 jit_solution(13071204110452828137)
XLA Ops:
  0.0 0.0 copy-start
  0.0 4.3 %contract_send.1 = (bf16[128,1024]{1,0:T(8,128)(2,1)S(1)}, bf16[64,16,1024]{2,1,0:T(8,128)(2,1)S(1)}, bf16[128,1024]{1,0:T(8,128)(2,1)S(1)}, bf16[64,256]{1,0:T(8,128)(2,1)S(1)}) custom-call(bf16[128,32,1024]{2,1,0:T(8,128)(2,1)} %snapshot_ref.3, bf16[64,1024]{1,0:T(8,128)(2,1)} %bitcast.3), custom_call_target="tpu_custom_call" | custom-call | tf_op jit(solution)/shard_map/contract_send/pallas_call | solution.py:131
  4.3 0.5 %collective-permute-start = (bf16[128,1024]{1,0:T(8,128)(2,1)S(1)}, bf16[128,1024]{1,0:T(8,128)(2,1)S(1)}, u32[]{:S(2)}, u32[]{:S(2)}) collective-permute-start(bf16[128,1024]{1,0:T(8,128)(2,1)S(1)} %get-tuple-element.18), channel_id=1, source_target_pairs={{0,1},{1,0},{2,3},{3,2},{4,5},{5,4},{6,7},{7,6},{8,9},{9,8},{10,11... | collective-permute-start | bytes 786440 | tf_op jit(solution)/shard_map/ppermute | solution.py:400
  4.8 4.1 %contract_own.1.own_ref = bf16[128,1024]{1,0:T(8,128)(2,1)S(1)} custom-call(bf16[64,16,1024]{2,1,0:T(8,128)(2,1)S(1)} %get-tuple-element.15.kept_ref, bf16[128,32,1024]{2,1,0:T(8,128)(2,1)} %snapshot_ref.3, bf16[128,1024]{1,0:T(8,128)(2,1)S(1)} %get-tuple-element.16.wide_ref, bf16[64,256]{1,0:T(8,128)(2,1)S(1)} %get-tuple-element.17.order_ref), custom_call_target="tpu_custom_call" | custom-call | tf_op jit(solution)/shard_map/contract_own/pallas_call | solution.py:173
  8.9 0.0 collective-permute-done.got_ref
  8.9 0.0 copy-done
  8.9 0.2 project.1
  9.2 2.7 %collective-permute-start.2 = (bf16[256,128]{1,0:T(8,128)(2,1)S(1)}, bf16[256,128]{1,0:T(8,128)(2,1)S(1)}, u32[]{:S(2)}, u32[]{:S(2)}) collective-permute-start(bf16[256,128]{1,0:T(8,128)(2,1)S(1)} %get-tuple-element.22), channel_id=1, source_target_pairs={{0,3},{1,2},{2,1},{3,0},{4,7},{5,6},{6,5},{7,4},{8,11},{9,10},{10,... | collective-permute-start | bytes 196616 | tf_op jit(solution)/shard_map/ppermute | solution.py:400
  11.9 0.1 collective-permute-start.1
  12.0 2.4 %collective-permute-done.2.got_ref = bf16[256,128]{1,0:T(8,128)(2,1)S(1)} collective-permute-done((bf16[256,128]{1,0:T(8,128)(2,1)S(1)}, bf16[256,128]{1,0:T(8,128)(2,1)S(1)}, u32[]{:S(2)}, u32[]{:S(2)}) %collective-permute-start.2) | collective-permute-done | bytes 65568 | tf_op jit(solution)/shard_map/ppermute | solution.py:400
  14.3 1.4 %collective-permute-start.3 = (bf16[128,128]{1,0:T(8,128)(2,1)S(1)}, bf16[128,128]{1,0:T(8,128)(2,1)S(1)}, u32[]{:S(2)}, u32[]{:S(2)}) collective-permute-start(bf16[128,128]{1,0:T(8,128)(2,1)S(1)} %get-tuple-element.23.mine_ref), channel_id=1, source_target_pairs={{0,5},{1,4},{2,7},{3,6},{4,1},{5,0},{6,3},{7,2},{8,13},{9,12},{10,... | collective-permute-start | bytes 98312 | tf_op jit(solution)/shard_map/ppermute | solution.py:400
  15.7 2.5 %collective-permute-start.5 = (bf16[128,128]{1,0:T(8,128)(2,1)S(1)}, bf16[128,128]{1,0:T(8,128)(2,1)S(1)}, u32[]{:S(2)}, u32[]{:S(2)}) collective-permute-start(bf16[128,128]{1,0:T(8,128)(2,1)S(1)} %get-tuple-element.24.mine_ref), channel_id=1, source_target_pairs={{0,9},{1,8},{2,11},{3,10},{4,13},{5,12},{6,15},{7,14},{8,1},{9,0},... | collective-permute-start | bytes 98312 | tf_op jit(solution)/shard_map/ppermute | solution.py:400
  18.3 0.0 collective-permute-done.3.got_ref
  18.3 2.2 %collective-permute-start.4 = (bf16[128,128]{1,0:T(8,128)(2,1)S(1)}, bf16[128,128]{1,0:T(8,128)(2,1)S(1)}, u32[]{:S(2)}, u32[]{:S(2)}) collective-permute-start(bf16[128,128]{1,0:T(8,128)(2,1)S(1)} %add.6.mine_ref), channel_id=1, source_target_pairs={{0,9},{1,8},{2,11},{3,10},{4,13},{5,12},{6,15},{7,14},{8,1},{9,0},... | collective-permute-start | bytes 98312 | tf_op jit(solution)/shard_map/ppermute | solution.py:400
  20.5 0.0 collective-permute-done.5.got_ref
  20.5 1.3 %collective-permute-start.6 = (bf16[128,128]{1,0:T(8,128)(2,1)S(1)}, bf16[128,128]{1,0:T(8,128)(2,1)S(1)}, u32[]{:S(2)}, u32[]{:S(2)}) collective-permute-start(bf16[128,128]{1,0:T(8,128)(2,1)S(1)} %add.8.mine_ref), channel_id=1, source_target_pairs={{0,5},{1,4},{2,7},{3,6},{4,1},{5,0},{6,3},{7,2},{8,13},{9,12},{10,... | collective-permute-start | bytes 98312 | tf_op jit(solution)/shard_map/ppermute | solution.py:400
  21.8 0.8 %collective-permute-done.4.got_ref = bf16[128,128]{1,0:T(8,128)(2,1)S(1)} collective-permute-done((bf16[128,128]{1,0:T(8,128)(2,1)S(1)}, bf16[128,128]{1,0:T(8,128)(2,1)S(1)}, u32[]{:S(2)}, u32[]{:S(2)}) %collective-permute-start.4) | collective-permute-done | bytes 32800 | tf_op jit(solution)/shard_map/ppermute | solution.py:400
  22.6 1.4 %collective-permute-done.6.got_ref = bf16[128,128]{1,0:T(8,128)(2,1)S(1)} collective-permute-done((bf16[128,128]{1,0:T(8,128)(2,1)S(1)}, bf16[128,128]{1,0:T(8,128)(2,1)S(1)}, u32[]{:S(2)}, u32[]{:S(2)}) %collective-permute-start.6) | collective-permute-done | bytes 32800 | tf_op jit(solution)/shard_map/ppermute | solution.py:400
  24.0 0.0 collective-permute-done.1.refs_0_.got_ref
  24.0 0.3 product_terms.1.mine_ref
  24.3 0.3 collective-permute-start.7
  24.6 0.9 %collective-permute-done.7.got_ref = bf16[128,128]{1,0:T(8,128)(2,1)S(1)} collective-permute-done((bf16[128,128]{1,0:T(8,128)(2,1)S(1)}, bf16[128,128]{1,0:T(8,128)(2,1)S(1)}, u32[]{:S(2)}, u32[]{:S(2)}) %collective-permute-start.7) | collective-permute-done | bytes 32800 | tf_op jit(solution)/shard_map/ppermute | solution.py:400
  25.6 2.6 %collective-permute-start.8 = (bf16[128,128]{1,0:T(8,128)(2,1)S(1)}, bf16[128,128]{1,0:T(8,128)(2,1)S(1)}, u32[]{:S(2)}, u32[]{:S(2)}) collective-permute-start(bf16[128,128]{1,0:T(8,128)(2,1)S(1)} %add.10.term_ref), channel_id=1, source_target_pairs={{0,3},{1,2},{2,1},{3,0},{4,7},{5,6},{6,5},{7,4},{8,11},{9,10},{10,... | collective-permute-start | bytes 98312 | tf_op jit(solution)/shard_map/ppermute | solution.py:400
  28.2 1.6 %collective-permute-done.8.got_ref.got_term_ref = bf16[128,128]{1,0:T(8,128)(2,1)S(1)} collective-permute-done((bf16[128,128]{1,0:T(8,128)(2,1)S(1)}, bf16[128,128]{1,0:T(8,128)(2,1)S(1)}, u32[]{:S(2)}, u32[]{:S(2)}) %collective-permute-start.8) | collective-permute-done | bytes 32800 | tf_op jit(solution)/shard_map/ppermute | solution.py:400
  29.8 0.3 local_gram.1.mine_ref
  30.1 0.8 %collective-permute-start.9 = (f32[32,128]{1,0:T(8,128)S(1)}, f32[32,128]{1,0:T(8,128)S(1)}, u32[]{:S(2)}, u32[]{:S(2)}) collective-permute-start(f32[32,128]{1,0:T(8,128)S(1)} %local_gram.1.mine_ref), channel_id=1, source_target_pairs={{0,5},{1,4},{2,7},{3,6},{4,1},{5,0},{6,3},{7,2},{8,13},{9,12},{10,... | collective-permute-start | bytes 49160 | tf_op jit(solution)/shard_map/ppermute | solution.py:400
  31.0 2.3 %collective-permute-done.9.got_ref = f32[32,128]{1,0:T(8,128)S(1)} collective-permute-done((f32[32,128]{1,0:T(8,128)S(1)}, f32[32,128]{1,0:T(8,128)S(1)}, u32[]{:S(2)}, u32[]{:S(2)}) %collective-permute-start.9) | collective-permute-done | bytes 16416 | tf_op jit(solution)/shard_map/ppermute | solution.py:400
  33.3 1.6 %collective-permute-start.10 = (f32[32,128]{1,0:T(8,128)S(1)}, f32[32,128]{1,0:T(8,128)S(1)}, u32[]{:S(2)}, u32[]{:S(2)}) collective-permute-start(f32[32,128]{1,0:T(8,128)S(1)} %add.11.gram_ref), channel_id=1, source_target_pairs={{0,9},{1,8},{2,11},{3,10},{4,13},{5,12},{6,15},{7,14},{8,1},{9,0},... | collective-permute-start | bytes 49160 | tf_op jit(solution)/shard_map/ppermute | solution.py:400
  34.9 2.5 %collective-permute-done.10.got_gram_ref = f32[32,128]{1,0:T(8,128)S(1)} collective-permute-done((f32[32,128]{1,0:T(8,128)S(1)}, f32[32,128]{1,0:T(8,128)S(1)}, u32[]{:S(2)}, u32[]{:S(2)}) %collective-permute-start.10) | collective-permute-done | bytes 16416 | tf_op jit(solution)/shard_map/ppermute | solution.py:400
  37.4 2.8 %finish.1 = f32[64,64]{1,0:T(8,128)} custom-call(bf16[128,128]{1,0:T(8,128)(2,1)S(1)} %add.10.term_ref, bf16[128,128]{1,0:T(8,128)(2,1)S(1)} %collective-permute-done.8.got_ref.got_term_ref, f32[32,128]{1,0:T(8,128)S(1)} %add.11.gram_ref, f32[32,128]{1,0:T(8,128)S(1)} %collective-permute-done.10.got_gram_ref), custom_call_target="tpu_custom_call" | custom-call | tf_op jit(solution)/shard_map/finish/pallas_call | solution.py:381
  (7 shorter events, 0.1 us)
Async XLA Ops:
  0.0 8.9 %copy-start = (bf16[128,64]{0,1:T(8,128)(2,1)S(1)}, bf16[128,64]{0,1:T(8,128)(2,1)}, u32[]{:S(2)}) copy-start(bf16[128,64]{0,1:T(8,128)(2,1)} %param.5) | copy-start | bytes 49156
  4.3 4.6 %collective-permute-start = (bf16[128,1024]{1,0:T(8,128)(2,1)S(1)}, bf16[128,1024]{1,0:T(8,128)(2,1)S(1)}, u32[]{:S(2)}, u32[]{:S(2)}) collective-permute-start(bf16[128,1024]{1,0:T(8,128)(2,1)S(1)} %get-tuple-element.18), channel_id=1, source_target_pairs={{0,1},{1,0},{2,3},{3,2},{4,5},{5,4},{6,7},{7,6},{8,9},{9,8},{10,11... | collective-permute-start | bytes 786440 | tf_op jit(solution)/shard_map/ppermute | solution.py:400
  9.2 5.1 %collective-permute-start.2 = (bf16[256,128]{1,0:T(8,128)(2,1)S(1)}, bf16[256,128]{1,0:T(8,128)(2,1)S(1)}, u32[]{:S(2)}, u32[]{:S(2)}) collective-permute-start(bf16[256,128]{1,0:T(8,128)(2,1)S(1)} %get-tuple-element.22), channel_id=1, source_target_pairs={{0,3},{1,2},{2,1},{3,0},{4,7},{5,6},{6,5},{7,4},{8,11},{9,10},{10,... | collective-permute-start | bytes 196616 | tf_op jit(solution)/shard_map/ppermute | solution.py:400
  11.9 12.1 %collective-permute-start.1 = (bf16[128,512]{1,0:T(8,128)(2,1)S(1)}, bf16[128,512]{1,0:T(8,128)(2,1)S(1)}, u32[]{:S(2)}, u32[]{:S(2)}) collective-permute-start(bf16[128,512]{1,0:T(8,128)(2,1)S(1)} %get-tuple-element.20), channel_id=1, source_target_pairs={{0,3},{1,2},{2,1},{3,0},{4,7},{5,6},{6,5},{7,4},{8,11},{9,10},{10,... | collective-permute-start | bytes 393224 | tf_op jit(solution)/shard_map/ppermute | solution.py:400
  14.3 3.9 %collective-permute-start.3 = (bf16[128,128]{1,0:T(8,128)(2,1)S(1)}, bf16[128,128]{1,0:T(8,128)(2,1)S(1)}, u32[]{:S(2)}, u32[]{:S(2)}) collective-permute-start(bf16[128,128]{1,0:T(8,128)(2,1)S(1)} %get-tuple-element.23.mine_ref), channel_id=1, source_target_pairs={{0,5},{1,4},{2,7},{3,6},{4,1},{5,0},{6,3},{7,2},{8,13},{9,12},{10,... | collective-permute-start | bytes 98312 | tf_op jit(solution)/shard_map/ppermute | solution.py:400
  15.7 4.8 %collective-permute-start.5 = (bf16[128,128]{1,0:T(8,128)(2,1)S(1)}, bf16[128,128]{1,0:T(8,128)(2,1)S(1)}, u32[]{:S(2)}, u32[]{:S(2)}) collective-permute-start(bf16[128,128]{1,0:T(8,128)(2,1)S(1)} %get-tuple-element.24.mine_ref), channel_id=1, source_target_pairs={{0,9},{1,8},{2,11},{3,10},{4,13},{5,12},{6,15},{7,14},{8,1},{9,0},... | collective-permute-start | bytes 98312 | tf_op jit(solution)/shard_map/ppermute | solution.py:400
  18.3 4.3 %collective-permute-start.4 = (bf16[128,128]{1,0:T(8,128)(2,1)S(1)}, bf16[128,128]{1,0:T(8,128)(2,1)S(1)}, u32[]{:S(2)}, u32[]{:S(2)}) collective-permute-start(bf16[128,128]{1,0:T(8,128)(2,1)S(1)} %add.6.mine_ref), channel_id=1, source_target_pairs={{0,9},{1,8},{2,11},{3,10},{4,13},{5,12},{6,15},{7,14},{8,1},{9,0},... | collective-permute-start | bytes 98312 | tf_op jit(solution)/shard_map/ppermute | solution.py:400
  20.5 3.5 %collective-permute-start.6 = (bf16[128,128]{1,0:T(8,128)(2,1)S(1)}, bf16[128,128]{1,0:T(8,128)(2,1)S(1)}, u32[]{:S(2)}, u32[]{:S(2)}) collective-permute-start(bf16[128,128]{1,0:T(8,128)(2,1)S(1)} %add.8.mine_ref), channel_id=1, source_target_pairs={{0,5},{1,4},{2,7},{3,6},{4,1},{5,0},{6,3},{7,2},{8,13},{9,12},{10,... | collective-permute-start | bytes 98312 | tf_op jit(solution)/shard_map/ppermute | solution.py:400
  24.3 1.3 %collective-permute-start.7 = (bf16[128,128]{1,0:T(8,128)(2,1)S(1)}, bf16[128,128]{1,0:T(8,128)(2,1)S(1)}, u32[]{:S(2)}, u32[]{:S(2)}) collective-permute-start(bf16[128,128]{1,0:T(8,128)(2,1)S(1)} %product_terms.1.mine_ref), channel_id=1, source_target_pairs={{0,1},{1,0},{2,3},{3,2},{4,5},{5,4},{6,7},{7,6},{8,9},{9,8},{10,11... | collective-permute-start | bytes 98312 | tf_op jit(solution)/shard_map/ppermute | solution.py:400
  25.6 4.2 %collective-permute-start.8 = (bf16[128,128]{1,0:T(8,128)(2,1)S(1)}, bf16[128,128]{1,0:T(8,128)(2,1)S(1)}, u32[]{:S(2)}, u32[]{:S(2)}) collective-permute-start(bf16[128,128]{1,0:T(8,128)(2,1)S(1)} %add.10.term_ref), channel_id=1, source_target_pairs={{0,3},{1,2},{2,1},{3,0},{4,7},{5,6},{6,5},{7,4},{8,11},{9,10},{10,... | collective-permute-start | bytes 98312 | tf_op jit(solution)/shard_map/ppermute | solution.py:400
  30.1 3.2 %collective-permute-start.9 = (f32[32,128]{1,0:T(8,128)S(1)}, f32[32,128]{1,0:T(8,128)S(1)}, u32[]{:S(2)}, u32[]{:S(2)}) collective-permute-start(f32[32,128]{1,0:T(8,128)S(1)} %local_gram.1.mine_ref), channel_id=1, source_target_pairs={{0,5},{1,4},{2,7},{3,6},{4,1},{5,0},{6,3},{7,2},{8,13},{9,12},{10,... | collective-permute-start | bytes 49160 | tf_op jit(solution)/shard_map/ppermute | solution.py:400
  33.3 4.1 %collective-permute-start.10 = (f32[32,128]{1,0:T(8,128)S(1)}, f32[32,128]{1,0:T(8,128)S(1)}, u32[]{:S(2)}, u32[]{:S(2)}) collective-permute-start(f32[32,128]{1,0:T(8,128)S(1)} %add.11.gram_ref), channel_id=1, source_target_pairs={{0,9},{1,8},{2,11},{3,10},{4,13},{5,12},{6,15},{7,14},{8,1},{9,0},... | collective-permute-start | bytes 49160 | tf_op jit(solution)/shard_map/ppermute | solution.py:400

commit v19 on v18

--- a/solution.py
+++ b/solution.py
@@ -93,7 +93,6 @@
     cells, half, _ = slab_ref.shape
     rank = mode2_ref.shape[0]
     chunks = cells // STEP
-    kept = kept_ref.shape[0]
     flat = (even_ref, odd_ref)
     sends = [
         slab_copies(snapshot_ref, 0, slab_ref, 1 - own_half(), sems.at[chunk])
@@ -103,22 +102,20 @@
 
     small = pltpu.make_async_copy(mode2_ref, small_ref, small_sem)
     small.start()
-    for chunk in range(min(3, chunks)):
+    for chunk in range(chunks):
         sends[chunk][0](chunk * STEP, STEP, 2 if chunk else 4)
     fill_order(order_ref, half)
     small.wait()
     wide_ref[...] = jnp.concatenate([small_ref[...]] * (LANES // rank), axis=0)
     for chunk in range(chunks):
         sends[chunk][1](chunk * STEP, STEP)
-        if chunk + 3 < chunks:
-            sends[chunk + 3][0]((chunk + 3) * STEP, STEP, 2)
-        if chunk * STEP < kept:
-            start_kept(chunk * STEP, STEP, 2)
+        if chunk == 0:
+            start_kept(0, cells, 2 * chunks)
         multiply(slab_ref[pl.ds(chunk * STEP, STEP)], wide_ref, flat[chunk % 2])
         if chunk:
             spread(half, flat[(chunk - 1) % 2], order_ref, core_ref, (chunk - 1) * STEP)
     spread(half, flat[(chunks - 1) % 2], order_ref, core_ref, (chunks - 1) * STEP)
-    wait_kept(0, kept)
+    wait_kept(0, cells)
 
 
 def contract_send(snapshot, mode2_t):
@@ -133,7 +130,7 @@
         in_specs=[pinned, pinned],
         out_shape=[
             jax.ShapeDtypeStruct((cells, half * rank), BF16),
-            jax.ShapeDtypeStruct((cells // 2, half, depth), BF16),
+            jax.ShapeDtypeStruct((cells, half, depth), BF16),
             jax.ShapeDtypeStruct((LANES, depth), BF16),
             jax.ShapeDtypeStruct((block // reps, block * reps), BF16),
         ],
@@ -151,38 +148,27 @@
     )(snapshot, mode2_t)
 
 
-def own_kernel(
-    kept_ref, snapshot_ref, wide_ref, order_ref, core_ref, rest_ref, even_ref, odd_ref, sem
-):
-    kept, half, _ = kept_ref.shape
-    rest = rest_ref.shape[0]
-    start, wait = slab_copies(snapshot_ref, kept, rest_ref, own_half(), sem)
-    start(kept, rest, 4)
-    multiply(kept_ref[...], wide_ref, even_ref)
-    wait(kept, rest)
-    multiply(rest_ref[...], wide_ref, odd_ref)
-    spread(half, even_ref, order_ref, core_ref, 0)
-    spread(half, odd_ref, order_ref, core_ref, kept)
-
-
-def contract_own(kept, snapshot, wide, order):
-    cells = snapshot.shape[0]
-    rows, half, depth = kept.shape
+def own_kernel(slab_ref, wide_ref, order_ref, core_ref, even_ref, odd_ref):
+    cells, half, _ = slab_ref.shape
+    flat = (even_ref, odd_ref)
+    chunks = cells // STEP
+    for chunk in range(chunks):
+        multiply(slab_ref[pl.ds(chunk * STEP, STEP)], wide_ref, flat[chunk % 2])
+        if chunk:
+            spread(half, flat[(chunk - 1) % 2], order_ref, core_ref, (chunk - 1) * STEP)
+    spread(half, flat[(chunks - 1) % 2], order_ref, core_ref, (chunks - 1) * STEP)
+
+
+def contract_own(slab, wide, order):
+    cells, half, _ = slab.shape
     reps = order.shape[1] // (TILE * half)
-    whole = pl.BlockSpec(memory_space=pltpu.VMEM)
     return pl.pallas_call(
         own_kernel,
-        in_specs=[whole, pl.BlockSpec(memory_space=pltpu.HBM), whole, whole],
         out_shape=jax.ShapeDtypeStruct((cells, half // reps * LANES), BF16),
-        scratch_shapes=[
-            pltpu.VMEM((cells - rows, half, depth), BF16),
-            pltpu.VMEM((rows * half, LANES), BF16),
-            pltpu.VMEM(((cells - rows) * half, LANES), BF16),
-            pltpu.SemaphoreType.DMA,
-        ],
+        scratch_shapes=[pltpu.VMEM((STEP * half, LANES), BF16)] * 2,
         compiler_params=params(24),
         name="contract_own",
-    )(kept, snapshot, wide, order)
+    )(slab, wide, order)
 
 
 def is_even():
@@ -403,7 +389,7 @@
     mode2_t = pltpu.with_memory_space_constraint(mode2_factor.T, pltpu.HBM)
     send, kept, wide, order = contract_send(snapshot, mode2_t)
     got = swap(send, 0)
-    own = contract_own(kept, snapshot, wide, order)
+    own = contract_own(kept, wide, order)
 
     keep, send, columns, give = project(own, got, old_factor.T)
     low, high = add_in_halves(keep, swap(send, masks[0]))

time: 40.3 us -> 38.8 us (0.963)
  Pallas kernels: 12.1 us -> 10.5 us
    pallas_call x1, Pallas kernels: 4.07 us -> 1.77 us  [contract_own(): pl.pallas_call(own_kernel, out_shape=jax.ShapeDtypeStruct((cells, half //...]
    pallas_call x1, Pallas kernels: 4.31 us -> 5.08 us  [contract_send(): pl.pallas_call(send_kernel, in_specs=[pinned, pinned], out_shape=[jax.Sha...]
  transfers between devices with their start and end apart: 11 -> 11, of which waited for: 7 -> 7; matrix products, arithmetic and copies ran while one was open for 0% -> 0% of each run, Pallas kernels for 10% -> 5%
where the time goes in v19:
time: 38.8 us; the launch traced here: 38.6 us
  starting transfers between devices  16.1 us (41%)
  waiting for transfers between devices  12 us (31%)
  Pallas kernels  10.5 us (27%)
    ppermute x11, starting transfers between devices, swap(): return lax.ppermute(x, ('row', 'col'), pairs)  16.1 us
    ppermute x11, waiting for transfers between devices, swap(): return lax.ppermute(x, ('row', 'col'), pairs)  12 us
    pallas_call x1, Pallas kernels, contract_send(): pl.pallas_call(send_kernel, in_specs=[pinned, pinned], out_shape=[jax.Sha...  5.08 us
    pallas_call x1, Pallas kernels, finish(): pl.pallas_call(functools.partial(finish_kernel, total_rows), out_shape=ja...  2.76 us
    pallas_call x1, Pallas kernels, contract_own(): pl.pallas_call(own_kernel, out_shape=jax.ShapeDtypeStruct((cells, half //...  1.77 us
  transfers between devices with their start and end apart: 11, of which 7 were waited for; matrix products, arithmetic and copies ran while one was open for 0% of the time, Pallas kernels for 5%

profile of v19, /device:TPU:0, one launch (start us, length us, event | category | flops | bytes accessed | tf_op | source)
XLA Modules:
  0.0 38.6 jit_solution(2145476558289810093)
XLA Ops:
  0.0 0.0 copy-start
  0.0 5.1 %contract_send.1 = (bf16[128,1024]{1,0:T(8,128)(2,1)S(1)}, bf16[128,16,1024]{2,1,0:T(8,128)(2,1)S(1)}, bf16[128,1024]{1,0:T(8,128)(2,1)S(1)}, bf16[64,256]{1,0:T(8,128)(2,1)S(1)}) custom-call(bf16[128,32,1024]{2,1,0:T(8,128)(2,1)} %snapshot_ref.1, bf16[64,1024]{1,0:T(8,128)(2,1)} %bitcast.3), custom_call_target="tpu_custom_call" | custom-call | tf_op jit(solution)/shard_map/contract_send/pallas_call | solution.py:128
  5.1 0.5 %collective-permute-start = (bf16[128,1024]{1,0:T(8,128)(2,1)S(1)}, bf16[128,1024]{1,0:T(8,128)(2,1)S(1)}, u32[]{:S(2)}, u32[]{:S(2)}) collective-permute-start(bf16[128,1024]{1,0:T(8,128)(2,1)S(1)} %get-tuple-element.18), channel_id=1, source_target_pairs={{0,1},{1,0},{2,3},{3,2},{4,5},{5,4},{6,7},{7,6},{8,9},{9,8},{10,11... | collective-permute-start | bytes 786440 | tf_op jit(solution)/shard_map/ppermute | solution.py:386
  5.6 1.8 %contract_own.1.own_ref = bf16[128,1024]{1,0:T(8,128)(2,1)S(1)} custom-call(bf16[128,16,1024]{2,1,0:T(8,128)(2,1)S(1)} %get-tuple-element.15.slab_ref, bf16[128,1024]{1,0:T(8,128)(2,1)S(1)} %get-tuple-element.16.wide_ref, bf16[64,256]{1,0:T(8,128)(2,1)S(1)} %get-tuple-element.17.order_ref), custom_call_target="tpu_custom_call" | custom-call | tf_op jit(solution)/shard_map/contract_own/pallas_call | solution.py:165
  7.4 0.0 collective-permute-done.got_ref
  7.4 0.0 copy-done
  7.4 0.2 project.1
  7.6 2.7 %collective-permute-start.2 = (bf16[256,128]{1,0:T(8,128)(2,1)S(1)}, bf16[256,128]{1,0:T(8,128)(2,1)S(1)}, u32[]{:S(2)}, u32[]{:S(2)}) collective-permute-start(bf16[256,128]{1,0:T(8,128)(2,1)S(1)} %get-tuple-element.22), channel_id=1, source_target_pairs={{0,3},{1,2},{2,1},{3,0},{4,7},{5,6},{6,5},{7,4},{8,11},{9,10},{10,... | collective-permute-start | bytes 196616 | tf_op jit(solution)/shard_map/ppermute | solution.py:386
  10.4 0.1 collective-permute-start.1
  10.4 2.4 %collective-permute-done.2.got_ref = bf16[256,128]{1,0:T(8,128)(2,1)S(1)} collective-permute-done((bf16[256,128]{1,0:T(8,128)(2,1)S(1)}, bf16[256,128]{1,0:T(8,128)(2,1)S(1)}, u32[]{:S(2)}, u32[]{:S(2)}) %collective-permute-start.2) | collective-permute-done | bytes 65568 | tf_op jit(solution)/shard_map/ppermute | solution.py:386
  12.8 1.4 %collective-permute-start.3 = (bf16[128,128]{1,0:T(8,128)(2,1)S(1)}, bf16[128,128]{1,0:T(8,128)(2,1)S(1)}, u32[]{:S(2)}, u32[]{:S(2)}) collective-permute-start(bf16[128,128]{1,0:T(8,128)(2,1)S(1)} %get-tuple-element.23.mine_ref), channel_id=1, source_target_pairs={{0,5},{1,4},{2,7},{3,6},{4,1},{5,0},{6,3},{7,2},{8,13},{9,12},{10,... | collective-permute-start | bytes 98312 | tf_op jit(solution)/shard_map/ppermute | solution.py:386
  14.2 2.5 %collective-permute-start.5 = (bf16[128,128]{1,0:T(8,128)(2,1)S(1)}, bf16[128,128]{1,0:T(8,128)(2,1)S(1)}, u32[]{:S(2)}, u32[]{:S(2)}) collective-permute-start(bf16[128,128]{1,0:T(8,128)(2,1)S(1)} %get-tuple-element.24.mine_ref), channel_id=1, source_target_pairs={{0,9},{1,8},{2,11},{3,10},{4,13},{5,12},{6,15},{7,14},{8,1},{9,0},... | collective-permute-start | bytes 98312 | tf_op jit(solution)/shard_map/ppermute | solution.py:386
  16.7 0.0 collective-permute-done.3.got_ref
  16.8 2.2 %collective-permute-start.4 = (bf16[128,128]{1,0:T(8,128)(2,1)S(1)}, bf16[128,128]{1,0:T(8,128)(2,1)S(1)}, u32[]{:S(2)}, u32[]{:S(2)}) collective-permute-start(bf16[128,128]{1,0:T(8,128)(2,1)S(1)} %add.6.mine_ref), channel_id=1, source_target_pairs={{0,9},{1,8},{2,11},{3,10},{4,13},{5,12},{6,15},{7,14},{8,1},{9,0},... | collective-permute-start | bytes 98312 | tf_op jit(solution)/shard_map/ppermute | solution.py:386
  19.0 0.0 collective-permute-done.5.got_ref
  19.0 1.2 %collective-permute-start.6 = (bf16[128,128]{1,0:T(8,128)(2,1)S(1)}, bf16[128,128]{1,0:T(8,128)(2,1)S(1)}, u32[]{:S(2)}, u32[]{:S(2)}) collective-permute-start(bf16[128,128]{1,0:T(8,128)(2,1)S(1)} %add.8.mine_ref), channel_id=1, source_target_pairs={{0,5},{1,4},{2,7},{3,6},{4,1},{5,0},{6,3},{7,2},{8,13},{9,12},{10,... | collective-permute-start | bytes 98312 | tf_op jit(solution)/shard_map/ppermute | solution.py:386
  20.2 0.8 %collective-permute-done.4.got_ref = bf16[128,128]{1,0:T(8,128)(2,1)S(1)} collective-permute-done((bf16[128,128]{1,0:T(8,128)(2,1)S(1)}, bf16[128,128]{1,0:T(8,128)(2,1)S(1)}, u32[]{:S(2)}, u32[]{:S(2)}) %collective-permute-start.4) | collective-permute-done | bytes 32800 | tf_op jit(solution)/shard_map/ppermute | solution.py:386
  21.1 1.4 %collective-permute-done.6.got_ref = bf16[128,128]{1,0:T(8,128)(2,1)S(1)} collective-permute-done((bf16[128,128]{1,0:T(8,128)(2,1)S(1)}, bf16[128,128]{1,0:T(8,128)(2,1)S(1)}, u32[]{:S(2)}, u32[]{:S(2)}) %collective-permute-start.6) | collective-permute-done | bytes 32800 | tf_op jit(solution)/shard_map/ppermute | solution.py:386
  22.5 0.0 collective-permute-done.1.refs_0_.got_ref
  22.5 0.3 product_terms.1.mine_ref
  22.8 0.3 collective-permute-start.7
  23.1 0.9 %collective-permute-done.7.got_ref = bf16[128,128]{1,0:T(8,128)(2,1)S(1)} collective-permute-done((bf16[128,128]{1,0:T(8,128)(2,1)S(1)}, bf16[128,128]{1,0:T(8,128)(2,1)S(1)}, u32[]{:S(2)}, u32[]{:S(2)}) %collective-permute-start.7) | collective-permute-done | bytes 32800 | tf_op jit(solution)/shard_map/ppermute | solution.py:386
  24.1 2.6 %collective-permute-start.8 = (bf16[128,128]{1,0:T(8,128)(2,1)S(1)}, bf16[128,128]{1,0:T(8,128)(2,1)S(1)}, u32[]{:S(2)}, u32[]{:S(2)}) collective-permute-start(bf16[128,128]{1,0:T(8,128)(2,1)S(1)} %add.10.term_ref), channel_id=1, source_target_pairs={{0,3},{1,2},{2,1},{3,0},{4,7},{5,6},{6,5},{7,4},{8,11},{9,10},{10,... | collective-permute-start | bytes 98312 | tf_op jit(solution)/shard_map/ppermute | solution.py:386
  26.7 1.6 %collective-permute-done.8.got_ref.got_term_ref = bf16[128,128]{1,0:T(8,128)(2,1)S(1)} collective-permute-done((bf16[128,128]{1,0:T(8,128)(2,1)S(1)}, bf16[128,128]{1,0:T(8,128)(2,1)S(1)}, u32[]{:S(2)}, u32[]{:S(2)}) %collective-permute-start.8) | collective-permute-done | bytes 32800 | tf_op jit(solution)/shard_map/ppermute | solution.py:386
  28.3 0.3 local_gram.1.mine_ref
  28.6 0.8 %collective-permute-start.9 = (f32[32,128]{1,0:T(8,128)S(1)}, f32[32,128]{1,0:T(8,128)S(1)}, u32[]{:S(2)}, u32[]{:S(2)}) collective-permute-start(f32[32,128]{1,0:T(8,128)S(1)} %local_gram.1.mine_ref), channel_id=1, source_target_pairs={{0,5},{1,4},{2,7},{3,6},{4,1},{5,0},{6,3},{7,2},{8,13},{9,12},{10,... | collective-permute-start | bytes 49160 | tf_op jit(solution)/shard_map/ppermute | solution.py:386
  29.5 2.3 %collective-permute-done.9.got_ref = f32[32,128]{1,0:T(8,128)S(1)} collective-permute-done((f32[32,128]{1,0:T(8,128)S(1)}, f32[32,128]{1,0:T(8,128)S(1)}, u32[]{:S(2)}, u32[]{:S(2)}) %collective-permute-start.9) | collective-permute-done | bytes 16416 | tf_op jit(solution)/shard_map/ppermute | solution.py:386
  31.8 1.6 %collective-permute-start.10 = (f32[32,128]{1,0:T(8,128)S(1)}, f32[32,128]{1,0:T(8,128)S(1)}, u32[]{:S(2)}, u32[]{:S(2)}) collective-permute-start(f32[32,128]{1,0:T(8,128)S(1)} %add.11.gram_ref), channel_id=1, source_target_pairs={{0,9},{1,8},{2,11},{3,10},{4,13},{5,12},{6,15},{7,14},{8,1},{9,0},... | collective-permute-start | bytes 49160 | tf_op jit(solution)/shard_map/ppermute | solution.py:386
  33.4 2.5 %collective-permute-done.10.got_gram_ref = f32[32,128]{1,0:T(8,128)S(1)} collective-permute-done((f32[32,128]{1,0:T(8,128)S(1)}, f32[32,128]{1,0:T(8,128)S(1)}, u32[]{:S(2)}, u32[]{:S(2)}) %collective-permute-start.10) | collective-permute-done | bytes 16416 | tf_op jit(solution)/shard_map/ppermute | solution.py:386
  35.9 2.8 %finish.1 = f32[64,64]{1,0:T(8,128)} custom-call(bf16[128,128]{1,0:T(8,128)(2,1)S(1)} %add.10.term_ref, bf16[128,128]{1,0:T(8,128)(2,1)S(1)} %collective-permute-done.8.got_ref.got_term_ref, f32[32,128]{1,0:T(8,128)S(1)} %add.11.gram_ref, f32[32,128]{1,0:T(8,128)S(1)} %collective-permute-done.10.got_gram_ref), custom_call_target="tpu_custom_call" | custom-call | tf_op jit(solution)/shard_map/finish/pallas_call | solution.py:367
  (7 shorter events, 0.1 us)
Async XLA Ops:
  0.0 7.4 %copy-start = (bf16[128,64]{0,1:T(8,128)(2,1)S(1)}, bf16[128,64]{0,1:T(8,128)(2,1)}, u32[]{:S(2)}) copy-start(bf16[128,64]{0,1:T(8,128)(2,1)} %param.5) | copy-start | bytes 49156
  5.1 2.3 %collective-permute-start = (bf16[128,1024]{1,0:T(8,128)(2,1)S(1)}, bf16[128,1024]{1,0:T(8,128)(2,1)S(1)}, u32[]{:S(2)}, u32[]{:S(2)}) collective-permute-start(bf16[128,1024]{1,0:T(8,128)(2,1)S(1)} %get-tuple-element.18), channel_id=1, source_target_pairs={{0,1},{1,0},{2,3},{3,2},{4,5},{5,4},{6,7},{7,6},{8,9},{9,8},{10,11... | collective-permute-start | bytes 786440 | tf_op jit(solution)/shard_map/ppermute | solution.py:386
  7.6 5.2 %collective-permute-start.2 = (bf16[256,128]{1,0:T(8,128)(2,1)S(1)}, bf16[256,128]{1,0:T(8,128)(2,1)S(1)}, u32[]{:S(2)}, u32[]{:S(2)}) collective-permute-start(bf16[256,128]{1,0:T(8,128)(2,1)S(1)} %get-tuple-element.22), channel_id=1, source_target_pairs={{0,3},{1,2},{2,1},{3,0},{4,7},{5,6},{6,5},{7,4},{8,11},{9,10},{10,... | collective-permute-start | bytes 196616 | tf_op jit(solution)/shard_map/ppermute | solution.py:386
  10.4 12.1 %collective-permute-start.1 = (bf16[128,512]{1,0:T(8,128)(2,1)S(1)}, bf16[128,512]{1,0:T(8,128)(2,1)S(1)}, u32[]{:S(2)}, u32[]{:S(2)}) collective-permute-start(bf16[128,512]{1,0:T(8,128)(2,1)S(1)} %get-tuple-element.20), channel_id=1, source_target_pairs={{0,3},{1,2},{2,1},{3,0},{4,7},{5,6},{6,5},{7,4},{8,11},{9,10},{10,... | collective-permute-start | bytes 393224 | tf_op jit(solution)/shard_map/ppermute | solution.py:386
  12.8 3.9 %collective-permute-start.3 = (bf16[128,128]{1,0:T(8,128)(2,1)S(1)}, bf16[128,128]{1,0:T(8,128)(2,1)S(1)}, u32[]{:S(2)}, u32[]{:S(2)}) collective-permute-start(bf16[128,128]{1,0:T(8,128)(2,1)S(1)} %get-tuple-element.23.mine_ref), channel_id=1, source_target_pairs={{0,5},{1,4},{2,7},{3,6},{4,1},{5,0},{6,3},{7,2},{8,13},{9,12},{10,... | collective-permute-start | bytes 98312 | tf_op jit(solution)/shard_map/ppermute | solution.py:386
  14.2 4.8 %collective-permute-start.5 = (bf16[128,128]{1,0:T(8,128)(2,1)S(1)}, bf16[128,128]{1,0:T(8,128)(2,1)S(1)}, u32[]{:S(2)}, u32[]{:S(2)}) collective-permute-start(bf16[128,128]{1,0:T(8,128)(2,1)S(1)} %get-tuple-element.24.mine_ref), channel_id=1, source_target_pairs={{0,9},{1,8},{2,11},{3,10},{4,13},{5,12},{6,15},{7,14},{8,1},{9,0},... | collective-permute-start | bytes 98312 | tf_op jit(solution)/shard_map/ppermute | solution.py:386
  16.8 4.3 %collective-permute-start.4 = (bf16[128,128]{1,0:T(8,128)(2,1)S(1)}, bf16[128,128]{1,0:T(8,128)(2,1)S(1)}, u32[]{:S(2)}, u32[]{:S(2)}) collective-permute-start(bf16[128,128]{1,0:T(8,128)(2,1)S(1)} %add.6.mine_ref), channel_id=1, source_target_pairs={{0,9},{1,8},{2,11},{3,10},{4,13},{5,12},{6,15},{7,14},{8,1},{9,0},... | collective-permute-start | bytes 98312 | tf_op jit(solution)/shard_map/ppermute | solution.py:386
  19.0 3.5 %collective-permute-start.6 = (bf16[128,128]{1,0:T(8,128)(2,1)S(1)}, bf16[128,128]{1,0:T(8,128)(2,1)S(1)}, u32[]{:S(2)}, u32[]{:S(2)}) collective-permute-start(bf16[128,128]{1,0:T(8,128)(2,1)S(1)} %add.8.mine_ref), channel_id=1, source_target_pairs={{0,5},{1,4},{2,7},{3,6},{4,1},{5,0},{6,3},{7,2},{8,13},{9,12},{10,... | collective-permute-start | bytes 98312 | tf_op jit(solution)/shard_map/ppermute | solution.py:386
  22.8 1.3 %collective-permute-start.7 = (bf16[128,128]{1,0:T(8,128)(2,1)S(1)}, bf16[128,128]{1,0:T(8,128)(2,1)S(1)}, u32[]{:S(2)}, u32[]{:S(2)}) collective-permute-start(bf16[128,128]{1,0:T(8,128)(2,1)S(1)} %product_terms.1.mine_ref), channel_id=1, source_target_pairs={{0,1},{1,0},{2,3},{3,2},{4,5},{5,4},{6,7},{7,6},{8,9},{9,8},{10,11... | collective-permute-start | bytes 98312 | tf_op jit(solution)/shard_map/ppermute | solution.py:386
  24.1 4.2 %collective-permute-start.8 = (bf16[128,128]{1,0:T(8,128)(2,1)S(1)}, bf16[128,128]{1,0:T(8,128)(2,1)S(1)}, u32[]{:S(2)}, u32[]{:S(2)}) collective-permute-start(bf16[128,128]{1,0:T(8,128)(2,1)S(1)} %add.10.term_ref), channel_id=1, source_target_pairs={{0,3},{1,2},{2,1},{3,0},{4,7},{5,6},{6,5},{7,4},{8,11},{9,10},{10,... | collective-permute-start | bytes 98312 | tf_op jit(solution)/shard_map/ppermute | solution.py:386
  28.6 3.2 %collective-permute-start.9 = (f32[32,128]{1,0:T(8,128)S(1)}, f32[32,128]{1,0:T(8,128)S(1)}, u32[]{:S(2)}, u32[]{:S(2)}) collective-permute-start(f32[32,128]{1,0:T(8,128)S(1)} %local_gram.1.mine_ref), channel_id=1, source_target_pairs={{0,5},{1,4},{2,7},{3,6},{4,1},{5,0},{6,3},{7,2},{8,13},{9,12},{10,... | collective-permute-start | bytes 49160 | tf_op jit(solution)/shard_map/ppermute | solution.py:386
  31.8 4.1 %collective-permute-start.10 = (f32[32,128]{1,0:T(8,128)S(1)}, f32[32,128]{1,0:T(8,128)S(1)}, u32[]{:S(2)}, u32[]{:S(2)}) collective-permute-start(f32[32,128]{1,0:T(8,128)S(1)} %add.11.gram_ref), channel_id=1, source_target_pairs={{0,9},{1,8},{2,11},{3,10},{4,13},{5,12},{6,15},{7,14},{8,1},{9,0},... | collective-permute-start | bytes 49160 | tf_op jit(solution)/shard_map/ppermute | solution.py:386

commit v20 on v19

--- a/solution.py
+++ b/solution.py
@@ -87,8 +87,8 @@
 
 
 def send_kernel(
-    snapshot_ref, mode2_ref, core_ref, kept_ref, wide_ref, order_ref,
-    slab_ref, small_ref, even_ref, odd_ref, sems, kept_sem, small_sem,
+    snapshot_ref, mode2_ref, core_ref, wide_ref, order_ref,
+    slab_ref, small_ref, even_ref, odd_ref, sems, small_sem,
 ):
     cells, half, _ = slab_ref.shape
     rank = mode2_ref.shape[0]
@@ -98,7 +98,6 @@
         slab_copies(snapshot_ref, 0, slab_ref, 1 - own_half(), sems.at[chunk])
         for chunk in range(chunks)
     ]
-    start_kept, wait_kept = slab_copies(snapshot_ref, 0, kept_ref, own_half(), kept_sem)
 
     small = pltpu.make_async_copy(mode2_ref, small_ref, small_sem)
     small.start()
@@ -109,13 +108,10 @@
     wide_ref[...] = jnp.concatenate([small_ref[...]] * (LANES // rank), axis=0)
     for chunk in range(chunks):
         sends[chunk][1](chunk * STEP, STEP)
-        if chunk == 0:
-            start_kept(0, cells, 2 * chunks)
         multiply(slab_ref[pl.ds(chunk * STEP, STEP)], wide_ref, flat[chunk % 2])
         if chunk:
             spread(half, flat[(chunk - 1) % 2], order_ref, core_ref, (chunk - 1) * STEP)
     spread(half, flat[(chunks - 1) % 2], order_ref, core_ref, (chunks - 1) * STEP)
-    wait_kept(0, cells)
 
 
 def contract_send(snapshot, mode2_t):
@@ -130,7 +126,6 @@
         in_specs=[pinned, pinned],
         out_shape=[
             jax.ShapeDtypeStruct((cells, half * rank), BF16),
-            jax.ShapeDtypeStruct((cells, half, depth), BF16),
             jax.ShapeDtypeStruct((LANES, depth), BF16),
             jax.ShapeDtypeStruct((block // reps, block * reps), BF16),
         ],
@@ -141,7 +136,6 @@
             pltpu.VMEM((STEP * half, LANES), BF16),
             pltpu.SemaphoreType.DMA((cells // STEP,)),
             pltpu.SemaphoreType.DMA,
-            pltpu.SemaphoreType.DMA,
         ],
         compiler_params=params(24),
         name="contract_send",
@@ -149,18 +143,21 @@
 
 
 def own_kernel(slab_ref, wide_ref, order_ref, core_ref, even_ref, odd_ref):
-    cells, half, _ = slab_ref.shape
+    cells, fibers, _ = slab_ref.shape
+    half = fibers // 2
+    kept = pl.ds(pl.multiple_of(own_half() * half, half), half)
     flat = (even_ref, odd_ref)
     chunks = cells // STEP
     for chunk in range(chunks):
-        multiply(slab_ref[pl.ds(chunk * STEP, STEP)], wide_ref, flat[chunk % 2])
+        multiply(slab_ref[pl.ds(chunk * STEP, STEP), kept], wide_ref, flat[chunk % 2])
         if chunk:
             spread(half, flat[(chunk - 1) % 2], order_ref, core_ref, (chunk - 1) * STEP)
     spread(half, flat[(chunks - 1) % 2], order_ref, core_ref, (chunks - 1) * STEP)
 
 
 def contract_own(slab, wide, order):
-    cells, half, _ = slab.shape
+    cells, fibers, _ = slab.shape
+    half = fibers // 2
     reps = order.shape[1] // (TILE * half)
     return pl.pallas_call(
         own_kernel,
@@ -385,11 +382,11 @@
         ]
         return lax.ppermute(x, ("row", "col"), pairs)
 
-    snapshot = pltpu.with_memory_space_constraint(snapshot, pltpu.HBM)
+    pinned = pltpu.with_memory_space_constraint(snapshot, pltpu.HBM)
     mode2_t = pltpu.with_memory_space_constraint(mode2_factor.T, pltpu.HBM)
-    send, kept, wide, order = contract_send(snapshot, mode2_t)
+    send, wide, order = contract_send(pinned, mode2_t)
     got = swap(send, 0)
-    own = contract_own(kept, wide, order)
+    own = contract_own(snapshot, wide, order)
 
     keep, send, columns, give = project(own, got, old_factor.T)
     low, high = add_in_halves(keep, swap(send, masks[0]))

time: 38.8 us -> 38.9 us (level)
  no operation moved by 1% of the time
where the time goes in v20:
time: 38.9 us; the launch traced here: 38.8 us
  starting transfers between devices  16.1 us (41%)
  waiting for transfers between devices  11.9 us (31%)
  Pallas kernels  10.7 us (28%)
    ppermute x11, starting transfers between devices, swap(): return lax.ppermute(x, ('row', 'col'), pairs)  16.1 us
    ppermute x11, waiting for transfers between devices, swap(): return lax.ppermute(x, ('row', 'col'), pairs)  11.9 us
    pallas_call x1, Pallas kernels, contract_send(): pl.pallas_call(send_kernel, in_specs=[pinned, pinned], out_shape=[jax.Sha...  5.22 us
    pallas_call x1, Pallas kernels, finish(): pl.pallas_call(functools.partial(finish_kernel, total_rows), out_shape=ja...  2.76 us
    pallas_call x1, Pallas kernels, contract_own(): pl.pallas_call(own_kernel, out_shape=jax.ShapeDtypeStruct((cells, half //...  1.78 us
  transfers between devices with their start and end apart: 11, of which 7 were waited for; matrix products, arithmetic and copies ran while one was open for 0% of the time, Pallas kernels for 5%

profile of v20, /device:TPU:0, one launch (start us, length us, event | category | flops | bytes accessed | tf_op | source)
XLA Modules:
  0.0 38.8 jit_solution(7093677482795554250)
XLA Ops:
  0.0 0.0 copy-start
  0.0 0.0 copy-start.1
  0.0 5.2 %contract_send.1 = (bf16[128,1024]{1,0:T(8,128)(2,1)S(1)}, bf16[128,1024]{1,0:T(8,128)(2,1)S(1)}, bf16[64,256]{1,0:T(8,128)(2,1)S(1)}) custom-call(bf16[128,32,1024]{2,1,0:T(8,128)(2,1)} %slab_ref.1, bf16[64,1024]{1,0:T(8,128)(2,1)} %bitcast.3), custom_call_target="tpu_custom_call" | custom-call | tf_op jit(solution)/shard_map/contract_send/pallas_call | solution.py:124
  5.2 0.5 %collective-permute-start = (bf16[128,1024]{1,0:T(8,128)(2,1)S(1)}, bf16[128,1024]{1,0:T(8,128)(2,1)S(1)}, u32[]{:S(2)}, u32[]{:S(2)}) collective-permute-start(bf16[128,1024]{1,0:T(8,128)(2,1)S(1)} %get-tuple-element.16), channel_id=1, source_target_pairs={{0,1},{1,0},{2,3},{3,2},{4,5},{5,4},{6,7},{7,6},{8,9},{9,8},{10,11... | collective-permute-start | bytes 786440 | tf_op jit(solution)/shard_map/ppermute | solution.py:383
  5.7 0.0 copy-done
  5.8 1.8 %contract_own.1.own_ref = bf16[128,1024]{1,0:T(8,128)(2,1)S(1)} custom-call(bf16[128,32,1024]{2,1,0:T(8,128)(2,1)S(1)} %copy-done, bf16[128,1024]{1,0:T(8,128)(2,1)S(1)} %get-tuple-element.14.wide_ref, bf16[64,256]{1,0:T(8,128)(2,1)S(1)} %get-tuple-element.15.order_ref), custom_call_target="tpu_custom_call" | custom-call | tf_op jit(solution)/shard_map/contract_own/pallas_call | solution.py:162
  7.5 0.0 collective-permute-done.got_ref
  7.5 0.0 copy-done.1
  7.6 0.2 project.1
  7.8 2.7 %collective-permute-start.2 = (bf16[256,128]{1,0:T(8,128)(2,1)S(1)}, bf16[256,128]{1,0:T(8,128)(2,1)S(1)}, u32[]{:S(2)}, u32[]{:S(2)}) collective-permute-start(bf16[256,128]{1,0:T(8,128)(2,1)S(1)} %get-tuple-element.20), channel_id=1, source_target_pairs={{0,3},{1,2},{2,1},{3,0},{4,7},{5,6},{6,5},{7,4},{8,11},{9,10},{10,... | collective-permute-start | bytes 196616 | tf_op jit(solution)/shard_map/ppermute | solution.py:383
  10.5 0.1 collective-permute-start.1
  10.6 2.4 %collective-permute-done.2.got_ref = bf16[256,128]{1,0:T(8,128)(2,1)S(1)} collective-permute-done((bf16[256,128]{1,0:T(8,128)(2,1)S(1)}, bf16[256,128]{1,0:T(8,128)(2,1)S(1)}, u32[]{:S(2)}, u32[]{:S(2)}) %collective-permute-start.2) | collective-permute-done | bytes 65568 | tf_op jit(solution)/shard_map/ppermute | solution.py:383
  13.0 1.4 %collective-permute-start.3 = (bf16[128,128]{1,0:T(8,128)(2,1)S(1)}, bf16[128,128]{1,0:T(8,128)(2,1)S(1)}, u32[]{:S(2)}, u32[]{:S(2)}) collective-permute-start(bf16[128,128]{1,0:T(8,128)(2,1)S(1)} %get-tuple-element.21.mine_ref), channel_id=1, source_target_pairs={{0,5},{1,4},{2,7},{3,6},{4,1},{5,0},{6,3},{7,2},{8,13},{9,12},{10,... | collective-permute-start | bytes 98312 | tf_op jit(solution)/shard_map/ppermute | solution.py:383
  14.4 2.5 %collective-permute-start.5 = (bf16[128,128]{1,0:T(8,128)(2,1)S(1)}, bf16[128,128]{1,0:T(8,128)(2,1)S(1)}, u32[]{:S(2)}, u32[]{:S(2)}) collective-permute-start(bf16[128,128]{1,0:T(8,128)(2,1)S(1)} %get-tuple-element.22.mine_ref), channel_id=1, source_target_pairs={{0,9},{1,8},{2,11},{3,10},{4,13},{5,12},{6,15},{7,14},{8,1},{9,0},... | collective-permute-start | bytes 98312 | tf_op jit(solution)/shard_map/ppermute | solution.py:383
  16.9 0.0 collective-permute-done.3.got_ref
  16.9 2.1 %collective-permute-start.4 = (bf16[128,128]{1,0:T(8,128)(2,1)S(1)}, bf16[128,128]{1,0:T(8,128)(2,1)S(1)}, u32[]{:S(2)}, u32[]{:S(2)}) collective-permute-start(bf16[128,128]{1,0:T(8,128)(2,1)S(1)} %add.6.mine_ref), channel_id=1, source_target_pairs={{0,9},{1,8},{2,11},{3,10},{4,13},{5,12},{6,15},{7,14},{8,1},{9,0},... | collective-permute-start | bytes 98312 | tf_op jit(solution)/shard_map/ppermute | solution.py:383
  19.1 0.0 collective-permute-done.5.got_ref
  19.1 1.3 %collective-permute-start.6 = (bf16[128,128]{1,0:T(8,128)(2,1)S(1)}, bf16[128,128]{1,0:T(8,128)(2,1)S(1)}, u32[]{:S(2)}, u32[]{:S(2)}) collective-permute-start(bf16[128,128]{1,0:T(8,128)(2,1)S(1)} %add.8.mine_ref), channel_id=1, source_target_pairs={{0,5},{1,4},{2,7},{3,6},{4,1},{5,0},{6,3},{7,2},{8,13},{9,12},{10,... | collective-permute-start | bytes 98312 | tf_op jit(solution)/shard_map/ppermute | solution.py:383
  20.4 0.8 %collective-permute-done.4.got_ref = bf16[128,128]{1,0:T(8,128)(2,1)S(1)} collective-permute-done((bf16[128,128]{1,0:T(8,128)(2,1)S(1)}, bf16[128,128]{1,0:T(8,128)(2,1)S(1)}, u32[]{:S(2)}, u32[]{:S(2)}) %collective-permute-start.4) | collective-permute-done | bytes 32800 | tf_op jit(solution)/shard_map/ppermute | solution.py:383
  21.2 1.4 %collective-permute-done.6.got_ref = bf16[128,128]{1,0:T(8,128)(2,1)S(1)} collective-permute-done((bf16[128,128]{1,0:T(8,128)(2,1)S(1)}, bf16[128,128]{1,0:T(8,128)(2,1)S(1)}, u32[]{:S(2)}, u32[]{:S(2)}) %collective-permute-start.6) | collective-permute-done | bytes 32800 | tf_op jit(solution)/shard_map/ppermute | solution.py:383
  22.6 0.0 collective-permute-done.1.refs_0_.got_ref
  22.6 0.3 product_terms.1.mine_ref
  22.9 0.4 collective-permute-start.7
  23.3 0.9 %collective-permute-done.7.got_ref = bf16[128,128]{1,0:T(8,128)(2,1)S(1)} collective-permute-done((bf16[128,128]{1,0:T(8,128)(2,1)S(1)}, bf16[128,128]{1,0:T(8,128)(2,1)S(1)}, u32[]{:S(2)}, u32[]{:S(2)}) %collective-permute-start.7) | collective-permute-done | bytes 32800 | tf_op jit(solution)/shard_map/ppermute | solution.py:383
  24.2 2.6 %collective-permute-start.8 = (bf16[128,128]{1,0:T(8,128)(2,1)S(1)}, bf16[128,128]{1,0:T(8,128)(2,1)S(1)}, u32[]{:S(2)}, u32[]{:S(2)}) collective-permute-start(bf16[128,128]{1,0:T(8,128)(2,1)S(1)} %add.10.term_ref), channel_id=1, source_target_pairs={{0,3},{1,2},{2,1},{3,0},{4,7},{5,6},{6,5},{7,4},{8,11},{9,10},{10,... | collective-permute-start | bytes 98312 | tf_op jit(solution)/shard_map/ppermute | solution.py:383
  26.8 1.6 %collective-permute-done.8.got_ref.got_term_ref = bf16[128,128]{1,0:T(8,128)(2,1)S(1)} collective-permute-done((bf16[128,128]{1,0:T(8,128)(2,1)S(1)}, bf16[128,128]{1,0:T(8,128)(2,1)S(1)}, u32[]{:S(2)}, u32[]{:S(2)}) %collective-permute-start.8) | collective-permute-done | bytes 32800 | tf_op jit(solution)/shard_map/ppermute | solution.py:383
  28.4 0.3 local_gram.1.mine_ref
  28.8 0.8 %collective-permute-start.9 = (f32[32,128]{1,0:T(8,128)S(1)}, f32[32,128]{1,0:T(8,128)S(1)}, u32[]{:S(2)}, u32[]{:S(2)}) collective-permute-start(f32[32,128]{1,0:T(8,128)S(1)} %local_gram.1.mine_ref), channel_id=1, source_target_pairs={{0,5},{1,4},{2,7},{3,6},{4,1},{5,0},{6,3},{7,2},{8,13},{9,12},{10,... | collective-permute-start | bytes 49160 | tf_op jit(solution)/shard_map/ppermute | solution.py:383
  29.6 2.3 %collective-permute-done.9.got_ref = f32[32,128]{1,0:T(8,128)S(1)} collective-permute-done((f32[32,128]{1,0:T(8,128)S(1)}, f32[32,128]{1,0:T(8,128)S(1)}, u32[]{:S(2)}, u32[]{:S(2)}) %collective-permute-start.9) | collective-permute-done | bytes 16416 | tf_op jit(solution)/shard_map/ppermute | solution.py:383
  32.0 1.6 %collective-permute-start.10 = (f32[32,128]{1,0:T(8,128)S(1)}, f32[32,128]{1,0:T(8,128)S(1)}, u32[]{:S(2)}, u32[]{:S(2)}) collective-permute-start(f32[32,128]{1,0:T(8,128)S(1)} %add.11.gram_ref), channel_id=1, source_target_pairs={{0,9},{1,8},{2,11},{3,10},{4,13},{5,12},{6,15},{7,14},{8,1},{9,0},... | collective-permute-start | bytes 49160 | tf_op jit(solution)/shard_map/ppermute | solution.py:383
  33.5 2.5 %collective-permute-done.10.got_gram_ref = f32[32,128]{1,0:T(8,128)S(1)} collective-permute-done((f32[32,128]{1,0:T(8,128)S(1)}, f32[32,128]{1,0:T(8,128)S(1)}, u32[]{:S(2)}, u32[]{:S(2)}) %collective-permute-start.10) | collective-permute-done | bytes 16416 | tf_op jit(solution)/shard_map/ppermute | solution.py:383
  36.0 2.8 %finish.1 = f32[64,64]{1,0:T(8,128)} custom-call(bf16[128,128]{1,0:T(8,128)(2,1)S(1)} %add.10.term_ref, bf16[128,128]{1,0:T(8,128)(2,1)S(1)} %collective-permute-done.8.got_ref.got_term_ref, f32[32,128]{1,0:T(8,128)S(1)} %add.11.gram_ref, f32[32,128]{1,0:T(8,128)S(1)} %collective-permute-done.10.got_gram_ref), custom_call_target="tpu_custom_call" | custom-call | tf_op jit(solution)/shard_map/finish/pallas_call | solution.py:364
  (7 shorter events, 0.1 us)
Async XLA Ops:
  0.0 5.8 %copy-start = (bf16[128,32,1024]{2,1,0:T(8,128)(2,1)S(1)}, bf16[128,32,1024]{2,1,0:T(8,128)(2,1)}, u32[]{:S(2)}) copy-start(bf16[128,32,1024]{2,1,0:T(8,128)(2,1)} %slab_ref.1) | copy-start | bytes 25165828
  0.0 7.5 %copy-start.1 = (bf16[128,64]{0,1:T(8,128)(2,1)S(1)}, bf16[128,64]{0,1:T(8,128)(2,1)}, u32[]{:S(2)}) copy-start(bf16[128,64]{0,1:T(8,128)(2,1)} %param.5) | copy-start | bytes 49156
  5.2 2.3 %collective-permute-start = (bf16[128,1024]{1,0:T(8,128)(2,1)S(1)}, bf16[128,1024]{1,0:T(8,128)(2,1)S(1)}, u32[]{:S(2)}, u32[]{:S(2)}) collective-permute-start(bf16[128,1024]{1,0:T(8,128)(2,1)S(1)} %get-tuple-element.16), channel_id=1, source_target_pairs={{0,1},{1,0},{2,3},{3,2},{4,5},{5,4},{6,7},{7,6},{8,9},{9,8},{10,11... | collective-permute-start | bytes 786440 | tf_op jit(solution)/shard_map/ppermute | solution.py:383
  7.8 5.2 %collective-permute-start.2 = (bf16[256,128]{1,0:T(8,128)(2,1)S(1)}, bf16[256,128]{1,0:T(8,128)(2,1)S(1)}, u32[]{:S(2)}, u32[]{:S(2)}) collective-permute-start(bf16[256,128]{1,0:T(8,128)(2,1)S(1)} %get-tuple-element.20), channel_id=1, source_target_pairs={{0,3},{1,2},{2,1},{3,0},{4,7},{5,6},{6,5},{7,4},{8,11},{9,10},{10,... | collective-permute-start | bytes 196616 | tf_op jit(solution)/shard_map/ppermute | solution.py:383
  10.5 12.1 %collective-permute-start.1 = (bf16[128,512]{1,0:T(8,128)(2,1)S(1)}, bf16[128,512]{1,0:T(8,128)(2,1)S(1)}, u32[]{:S(2)}, u32[]{:S(2)}) collective-permute-start(bf16[128,512]{1,0:T(8,128)(2,1)S(1)} %get-tuple-element.18), channel_id=1, source_target_pairs={{0,3},{1,2},{2,1},{3,0},{4,7},{5,6},{6,5},{7,4},{8,11},{9,10},{10,... | collective-permute-start | bytes 393224 | tf_op jit(solution)/shard_map/ppermute | solution.py:383
  13.0 3.9 %collective-permute-start.3 = (bf16[128,128]{1,0:T(8,128)(2,1)S(1)}, bf16[128,128]{1,0:T(8,128)(2,1)S(1)}, u32[]{:S(2)}, u32[]{:S(2)}) collective-permute-start(bf16[128,128]{1,0:T(8,128)(2,1)S(1)} %get-tuple-element.21.mine_ref), channel_id=1, source_target_pairs={{0,5},{1,4},{2,7},{3,6},{4,1},{5,0},{6,3},{7,2},{8,13},{9,12},{10,... | collective-permute-start | bytes 98312 | tf_op jit(solution)/shard_map/ppermute | solution.py:383
  14.4 4.7 %collective-permute-start.5 = (bf16[128,128]{1,0:T(8,128)(2,1)S(1)}, bf16[128,128]{1,0:T(8,128)(2,1)S(1)}, u32[]{:S(2)}, u32[]{:S(2)}) collective-permute-start(bf16[128,128]{1,0:T(8,128)(2,1)S(1)} %get-tuple-element.22.mine_ref), channel_id=1, source_target_pairs={{0,9},{1,8},{2,11},{3,10},{4,13},{5,12},{6,15},{7,14},{8,1},{9,0},... | collective-permute-start | bytes 98312 | tf_op jit(solution)/shard_map/ppermute | solution.py:383
  16.9 4.3 %collective-permute-start.4 = (bf16[128,128]{1,0:T(8,128)(2,1)S(1)}, bf16[128,128]{1,0:T(8,128)(2,1)S(1)}, u32[]{:S(2)}, u32[]{:S(2)}) collective-permute-start(bf16[128,128]{1,0:T(8,128)(2,1)S(1)} %add.6.mine_ref), channel_id=1, source_target_pairs={{0,9},{1,8},{2,11},{3,10},{4,13},{5,12},{6,15},{7,14},{8,1},{9,0},... | collective-permute-start | bytes 98312 | tf_op jit(solution)/shard_map/ppermute | solution.py:383
  19.1 3.5 %collective-permute-start.6 = (bf16[128,128]{1,0:T(8,128)(2,1)S(1)}, bf16[128,128]{1,0:T(8,128)(2,1)S(1)}, u32[]{:S(2)}, u32[]{:S(2)}) collective-permute-start(bf16[128,128]{1,0:T(8,128)(2,1)S(1)} %add.8.mine_ref), channel_id=1, source_target_pairs={{0,5},{1,4},{2,7},{3,6},{4,1},{5,0},{6,3},{7,2},{8,13},{9,12},{10,... | collective-permute-start | bytes 98312 | tf_op jit(solution)/shard_map/ppermute | solution.py:383
  22.9 1.3 %collective-permute-start.7 = (bf16[128,128]{1,0:T(8,128)(2,1)S(1)}, bf16[128,128]{1,0:T(8,128)(2,1)S(1)}, u32[]{:S(2)}, u32[]{:S(2)}) collective-permute-start(bf16[128,128]{1,0:T(8,128)(2,1)S(1)} %product_terms.1.mine_ref), channel_id=1, source_target_pairs={{0,1},{1,0},{2,3},{3,2},{4,5},{5,4},{6,7},{7,6},{8,9},{9,8},{10,11... | collective-permute-start | bytes 98312 | tf_op jit(solution)/shard_map/ppermute | solution.py:383
  24.2 4.2 %collective-permute-start.8 = (bf16[128,128]{1,0:T(8,128)(2,1)S(1)}, bf16[128,128]{1,0:T(8,128)(2,1)S(1)}, u32[]{:S(2)}, u32[]{:S(2)}) collective-permute-start(bf16[128,128]{1,0:T(8,128)(2,1)S(1)} %add.10.term_ref), channel_id=1, source_target_pairs={{0,3},{1,2},{2,1},{3,0},{4,7},{5,6},{6,5},{7,4},{8,11},{9,10},{10,... | collective-permute-start | bytes 98312 | tf_op jit(solution)/shard_map/ppermute | solution.py:383
  28.8 3.2 %collective-permute-start.9 = (f32[32,128]{1,0:T(8,128)S(1)}, f32[32,128]{1,0:T(8,128)S(1)}, u32[]{:S(2)}, u32[]{:S(2)}) collective-permute-start(f32[32,128]{1,0:T(8,128)S(1)} %local_gram.1.mine_ref), channel_id=1, source_target_pairs={{0,5},{1,4},{2,7},{3,6},{4,1},{5,0},{6,3},{7,2},{8,13},{9,12},{10,... | collective-permute-start | bytes 49160 | tf_op jit(solution)/shard_map/ppermute | solution.py:383
  32.0 4.1 %collective-permute-start.10 = (f32[32,128]{1,0:T(8,128)S(1)}, f32[32,128]{1,0:T(8,128)S(1)}, u32[]{:S(2)}, u32[]{:S(2)}) collective-permute-start(f32[32,128]{1,0:T(8,128)S(1)} %add.11.gram_ref), channel_id=1, source_target_pairs={{0,9},{1,8},{2,11},{3,10},{4,13},{5,12},{6,15},{7,14},{8,1},{9,0},... | collective-permute-start | bytes 49160 | tf_op jit(solution)/shard_map/ppermute | solution.py:383

commit v21 on v19

--- a/solution.py
+++ b/solution.py
@@ -277,21 +277,24 @@
     return term_ref[...].astype(F32) + got_ref[...].astype(F32)
 
 
-def gram_kernel(term_ref, got_ref, out_ref):
-    product = pair_product(term_ref, got_ref)
+def gram_kernel(*refs):
+    out_ref = refs[-1]
     rank = LANES // 2
+    product = jnp.concatenate(
+        [pair_product(refs[k], refs[k + 1]) for k in range(0, len(refs) - 1, 2)], axis=0
+    )
     wide = dot_parts(product, product, 0)
     gram = wide[:rank, :rank] + wide[rank:, rank:]
     out_ref[...] = jnp.concatenate([gram[:rank // 2], gram[rank // 2:]], axis=1)
 
 
-def local_gram(term, got):
+def local_gram(*terms):
     return pl.pallas_call(
         gram_kernel,
         out_shape=jax.ShapeDtypeStruct((LANES // 4, LANES), F32),
         compiler_params=params(4),
         name="local_gram",
-    )(term, got)
+    )(*terms)
 
 
 def parts(x):
@@ -402,9 +405,10 @@
 
     term = product_terms(columns, got_columns, low, high)
     term = add(term, swap(term, 0))
-    got_term = swap(term, masks[0])
-    gram = local_gram(term, got_term)
-    for mask in masks[1:-1]:
+    pair, next_pair = masks[:2]
+    got_term = swap(term, pair)
+    gram = local_gram(term, got_term, swap(term, next_pair), swap(term, pair | next_pair))
+    for mask in masks[2:-1]:
         gram = add(gram, swap(gram, mask))
     return finish(total_rows, term, got_term, gram, swap(gram, masks[-1]))
 

time: 38.8 us -> 38.8 us (level)
  waiting for transfers between devices: 12 us -> 11.5 us
  starting transfers between devices: 16.1 us -> 16.5 us
    ppermute x11 -> x12, waiting for transfers between devices: 12 us -> 11.5 us  [swap(): return lax.ppermute(x, ('row', 'col'), pairs)]
    ppermute x11 -> x12, starting transfers between devices: 16.1 us -> 16.5 us  [swap(): return lax.ppermute(x, ('row', 'col'), pairs)]
  transfers between devices with their start and end apart: 11 -> 12, of which waited for: 7 -> 8; matrix products, arithmetic and copies ran while one was open for 0% -> 0% of each run, Pallas kernels for 5% -> 5%
where the time goes in v21:
time: 38.8 us; the launch traced here: 38.7 us
  starting transfers between devices  16.5 us (43%)
  waiting for transfers between devices  11.5 us (30%)
  Pallas kernels  10.6 us (27%)
    ppermute x12, starting transfers between devices, swap(): return lax.ppermute(x, ('row', 'col'), pairs)  16.5 us
    ppermute x12, waiting for transfers between devices, swap(): return lax.ppermute(x, ('row', 'col'), pairs)  11.5 us
    pallas_call x1, Pallas kernels, contract_send(): pl.pallas_call(send_kernel, in_specs=[pinned, pinned], out_shape=[jax.Sha...  5.08 us
    pallas_call x1, Pallas kernels, finish(): pl.pallas_call(functools.partial(finish_kernel, total_rows), out_shape=ja...  2.76 us
    pallas_call x1, Pallas kernels, contract_own(): pl.pallas_call(own_kernel, out_shape=jax.ShapeDtypeStruct((cells, half //...  1.77 us
  transfers between devices with their start and end apart: 12, of which 8 were waited for; matrix products, arithmetic and copies ran while one was open for 0% of the time, Pallas kernels for 5%

profile of v21, /device:TPU:0, one launch (start us, length us, event | category | flops | bytes accessed | tf_op | source)
XLA Modules:
  0.0 38.7 jit_solution(6697479637306364877)
XLA Ops:
  0.0 0.0 copy-start
  0.0 5.1 %contract_send.1 = (bf16[128,1024]{1,0:T(8,128)(2,1)S(1)}, bf16[128,16,1024]{2,1,0:T(8,128)(2,1)S(1)}, bf16[128,1024]{1,0:T(8,128)(2,1)S(1)}, bf16[64,256]{1,0:T(8,128)(2,1)S(1)}) custom-call(bf16[128,32,1024]{2,1,0:T(8,128)(2,1)} %snapshot_ref.1, bf16[64,1024]{1,0:T(8,128)(2,1)} %bitcast.3), custom_call_target="tpu_custom_call" | custom-call | tf_op jit(solution)/shard_map/contract_send/pallas_call | solution.py:128
  5.1 0.5 %collective-permute-start = (bf16[128,1024]{1,0:T(8,128)(2,1)S(1)}, bf16[128,1024]{1,0:T(8,128)(2,1)S(1)}, u32[]{:S(2)}, u32[]{:S(2)}) collective-permute-start(bf16[128,1024]{1,0:T(8,128)(2,1)S(1)} %get-tuple-element.18), channel_id=1, source_target_pairs={{0,1},{1,0},{2,3},{3,2},{4,5},{5,4},{6,7},{7,6},{8,9},{9,8},{10,11... | collective-permute-start | bytes 786440 | tf_op jit(solution)/shard_map/ppermute | solution.py:389
  5.6 1.8 %contract_own.1.own_ref = bf16[128,1024]{1,0:T(8,128)(2,1)S(1)} custom-call(bf16[128,16,1024]{2,1,0:T(8,128)(2,1)S(1)} %get-tuple-element.15.slab_ref, bf16[128,1024]{1,0:T(8,128)(2,1)S(1)} %get-tuple-element.16.wide_ref, bf16[64,256]{1,0:T(8,128)(2,1)S(1)} %get-tuple-element.17.order_ref), custom_call_target="tpu_custom_call" | custom-call | tf_op jit(solution)/shard_map/contract_own/pallas_call | solution.py:165
  7.4 0.0 collective-permute-done.got_ref
  7.4 0.0 copy-done
  7.4 0.2 project.1
  7.6 2.7 %collective-permute-start.2 = (bf16[256,128]{1,0:T(8,128)(2,1)S(1)}, bf16[256,128]{1,0:T(8,128)(2,1)S(1)}, u32[]{:S(2)}, u32[]{:S(2)}) collective-permute-start(bf16[256,128]{1,0:T(8,128)(2,1)S(1)} %get-tuple-element.22), channel_id=1, source_target_pairs={{0,3},{1,2},{2,1},{3,0},{4,7},{5,6},{6,5},{7,4},{8,11},{9,10},{10,... | collective-permute-start | bytes 196616 | tf_op jit(solution)/shard_map/ppermute | solution.py:389
  10.4 0.1 collective-permute-start.1
  10.4 2.4 %collective-permute-done.2.got_ref = bf16[256,128]{1,0:T(8,128)(2,1)S(1)} collective-permute-done((bf16[256,128]{1,0:T(8,128)(2,1)S(1)}, bf16[256,128]{1,0:T(8,128)(2,1)S(1)}, u32[]{:S(2)}, u32[]{:S(2)}) %collective-permute-start.2) | collective-permute-done | bytes 65568 | tf_op jit(solution)/shard_map/ppermute | solution.py:389
  12.8 1.4 %collective-permute-start.3 = (bf16[128,128]{1,0:T(8,128)(2,1)S(1)}, bf16[128,128]{1,0:T(8,128)(2,1)S(1)}, u32[]{:S(2)}, u32[]{:S(2)}) collective-permute-start(bf16[128,128]{1,0:T(8,128)(2,1)S(1)} %get-tuple-element.23.mine_ref), channel_id=1, source_target_pairs={{0,5},{1,4},{2,7},{3,6},{4,1},{5,0},{6,3},{7,2},{8,13},{9,12},{10,... | collective-permute-start | bytes 98312 | tf_op jit(solution)/shard_map/ppermute | solution.py:389
  14.2 2.5 %collective-permute-start.5 = (bf16[128,128]{1,0:T(8,128)(2,1)S(1)}, bf16[128,128]{1,0:T(8,128)(2,1)S(1)}, u32[]{:S(2)}, u32[]{:S(2)}) collective-permute-start(bf16[128,128]{1,0:T(8,128)(2,1)S(1)} %get-tuple-element.24.mine_ref), channel_id=1, source_target_pairs={{0,9},{1,8},{2,11},{3,10},{4,13},{5,12},{6,15},{7,14},{8,1},{9,0},... | collective-permute-start | bytes 98312 | tf_op jit(solution)/shard_map/ppermute | solution.py:389
  16.7 0.0 collective-permute-done.3.got_ref
  16.8 2.2 %collective-permute-start.4 = (bf16[128,128]{1,0:T(8,128)(2,1)S(1)}, bf16[128,128]{1,0:T(8,128)(2,1)S(1)}, u32[]{:S(2)}, u32[]{:S(2)}) collective-permute-start(bf16[128,128]{1,0:T(8,128)(2,1)S(1)} %add.5.mine_ref), channel_id=1, source_target_pairs={{0,9},{1,8},{2,11},{3,10},{4,13},{5,12},{6,15},{7,14},{8,1},{9,0},... | collective-permute-start | bytes 98312 | tf_op jit(solution)/shard_map/ppermute | solution.py:389
  19.0 0.0 collective-permute-done.5.got_ref
  19.0 1.2 %collective-permute-start.6 = (bf16[128,128]{1,0:T(8,128)(2,1)S(1)}, bf16[128,128]{1,0:T(8,128)(2,1)S(1)}, u32[]{:S(2)}, u32[]{:S(2)}) collective-permute-start(bf16[128,128]{1,0:T(8,128)(2,1)S(1)} %add.7.mine_ref), channel_id=1, source_target_pairs={{0,5},{1,4},{2,7},{3,6},{4,1},{5,0},{6,3},{7,2},{8,13},{9,12},{10,... | collective-permute-start | bytes 98312 | tf_op jit(solution)/shard_map/ppermute | solution.py:389
  20.2 0.8 %collective-permute-done.4.got_ref = bf16[128,128]{1,0:T(8,128)(2,1)S(1)} collective-permute-done((bf16[128,128]{1,0:T(8,128)(2,1)S(1)}, bf16[128,128]{1,0:T(8,128)(2,1)S(1)}, u32[]{:S(2)}, u32[]{:S(2)}) %collective-permute-start.4) | collective-permute-done | bytes 32800 | tf_op jit(solution)/shard_map/ppermute | solution.py:389
  21.1 1.4 %collective-permute-done.6.got_ref = bf16[128,128]{1,0:T(8,128)(2,1)S(1)} collective-permute-done((bf16[128,128]{1,0:T(8,128)(2,1)S(1)}, bf16[128,128]{1,0:T(8,128)(2,1)S(1)}, u32[]{:S(2)}, u32[]{:S(2)}) %collective-permute-start.6) | collective-permute-done | bytes 32800 | tf_op jit(solution)/shard_map/ppermute | solution.py:389
  22.5 0.0 collective-permute-done.1.refs_0_.got_ref
  22.5 0.3 product_terms.1.mine_ref
  22.8 0.3 collective-permute-start.7
  23.1 0.9 %collective-permute-done.7.got_ref = bf16[128,128]{1,0:T(8,128)(2,1)S(1)} collective-permute-done((bf16[128,128]{1,0:T(8,128)(2,1)S(1)}, bf16[128,128]{1,0:T(8,128)(2,1)S(1)}, u32[]{:S(2)}, u32[]{:S(2)}) %collective-permute-start.7) | collective-permute-done | bytes 32800 | tf_op jit(solution)/shard_map/ppermute | solution.py:389
  24.1 2.9 %collective-permute-start.10 = (bf16[128,128]{1,0:T(8,128)(2,1)S(1)}, bf16[128,128]{1,0:T(8,128)(2,1)S(1)}, u32[]{:S(2)}, u32[]{:S(2)}) collective-permute-start(bf16[128,128]{1,0:T(8,128)(2,1)S(1)} %add.9.refs_0_.term_ref), channel_id=1, source_target_pairs={{0,7},{1,6},{2,5},{3,4},{4,3},{5,2},{6,1},{7,0},{8,15},{9,14},{10,... | collective-permute-start | bytes 98312 | tf_op jit(solution)/shard_map/ppermute | solution.py:389
  27.0 1.1 %collective-permute-start.9 = (bf16[128,128]{1,0:T(8,128)(2,1)S(1)}, bf16[128,128]{1,0:T(8,128)(2,1)S(1)}, u32[]{:S(2)}, u32[]{:S(2)}) collective-permute-start(bf16[128,128]{1,0:T(8,128)(2,1)S(1)} %add.9.refs_0_.term_ref), channel_id=1, source_target_pairs={{0,5},{1,4},{2,7},{3,6},{4,1},{5,0},{6,3},{7,2},{8,13},{9,12},{10,... | collective-permute-start | bytes 98312 | tf_op jit(solution)/shard_map/ppermute | solution.py:389
  28.1 0.0 collective-permute-start.8
  28.1 0.5 %collective-permute-done.10.refs_3_ = bf16[128,128]{1,0:T(8,128)(2,1)S(1)} collective-permute-done((bf16[128,128]{1,0:T(8,128)(2,1)S(1)}, bf16[128,128]{1,0:T(8,128)(2,1)S(1)}, u32[]{:S(2)}, u32[]{:S(2)}) %collective-permute-start.10) | collective-permute-done | bytes 32800 | tf_op jit(solution)/shard_map/ppermute | solution.py:389
  28.6 1.8 %collective-permute-done.9.refs_2_ = bf16[128,128]{1,0:T(8,128)(2,1)S(1)} collective-permute-done((bf16[128,128]{1,0:T(8,128)(2,1)S(1)}, bf16[128,128]{1,0:T(8,128)(2,1)S(1)}, u32[]{:S(2)}, u32[]{:S(2)}) %collective-permute-start.9) | collective-permute-done | bytes 32800 | tf_op jit(solution)/shard_map/ppermute | solution.py:389
  30.4 1.0 %collective-permute-done.8.refs_1_.got_term_ref = bf16[128,128]{1,0:T(8,128)(2,1)S(1)} collective-permute-done((bf16[128,128]{1,0:T(8,128)(2,1)S(1)}, bf16[128,128]{1,0:T(8,128)(2,1)S(1)}, u32[]{:S(2)}, u32[]{:S(2)}) %collective-permute-start.8) | collective-permute-done | bytes 32800 | tf_op jit(solution)/shard_map/ppermute | solution.py:389
  31.4 0.4 local_gram.1.gram_ref
  31.8 1.4 %collective-permute-start.11 = (f32[32,128]{1,0:T(8,128)S(1)}, f32[32,128]{1,0:T(8,128)S(1)}, u32[]{:S(2)}, u32[]{:S(2)}) collective-permute-start(f32[32,128]{1,0:T(8,128)S(1)} %local_gram.1.gram_ref), channel_id=1, source_target_pairs={{0,9},{1,8},{2,11},{3,10},{4,13},{5,12},{6,15},{7,14},{8,1},{9,0},... | collective-permute-start | bytes 49160 | tf_op jit(solution)/shard_map/ppermute | solution.py:389
  33.2 2.7 %collective-permute-done.11.got_gram_ref = f32[32,128]{1,0:T(8,128)S(1)} collective-permute-done((f32[32,128]{1,0:T(8,128)S(1)}, f32[32,128]{1,0:T(8,128)S(1)}, u32[]{:S(2)}, u32[]{:S(2)}) %collective-permute-start.11) | collective-permute-done | bytes 16416 | tf_op jit(solution)/shard_map/ppermute | solution.py:389
  35.9 2.8 %finish.1 = f32[64,64]{1,0:T(8,128)} custom-call(bf16[128,128]{1,0:T(8,128)(2,1)S(1)} %add.9.refs_0_.term_ref, bf16[128,128]{1,0:T(8,128)(2,1)S(1)} %collective-permute-done.8.refs_1_.got_term_ref, f32[32,128]{1,0:T(8,128)S(1)} %local_gram.1.gram_ref, f32[32,128]{1,0:T(8,128)S(1)} %collective-permute-done.11.got_gram_ref), custom_call_target="tpu_custom_call" | custom-call | tf_op jit(solution)/shard_map/finish/pallas_call | solution.py:370
  (6 shorter events, 0.1 us)
Async XLA Ops:
  0.0 7.4 %copy-start = (bf16[128,64]{0,1:T(8,128)(2,1)S(1)}, bf16[128,64]{0,1:T(8,128)(2,1)}, u32[]{:S(2)}) copy-start(bf16[128,64]{0,1:T(8,128)(2,1)} %param.5) | copy-start | bytes 49156
  5.1 2.3 %collective-permute-start = (bf16[128,1024]{1,0:T(8,128)(2,1)S(1)}, bf16[128,1024]{1,0:T(8,128)(2,1)S(1)}, u32[]{:S(2)}, u32[]{:S(2)}) collective-permute-start(bf16[128,1024]{1,0:T(8,128)(2,1)S(1)} %get-tuple-element.18), channel_id=1, source_target_pairs={{0,1},{1,0},{2,3},{3,2},{4,5},{5,4},{6,7},{7,6},{8,9},{9,8},{10,11... | collective-permute-start | bytes 786440 | tf_op jit(solution)/shard_map/ppermute | solution.py:389
  7.6 5.2 %collective-permute-start.2 = (bf16[256,128]{1,0:T(8,128)(2,1)S(1)}, bf16[256,128]{1,0:T(8,128)(2,1)S(1)}, u32[]{:S(2)}, u32[]{:S(2)}) collective-permute-start(bf16[256,128]{1,0:T(8,128)(2,1)S(1)} %get-tuple-element.22), channel_id=1, source_target_pairs={{0,3},{1,2},{2,1},{3,0},{4,7},{5,6},{6,5},{7,4},{8,11},{9,10},{10,... | collective-permute-start | bytes 196616 | tf_op jit(solution)/shard_map/ppermute | solution.py:389
  10.4 12.1 %collective-permute-start.1 = (bf16[128,512]{1,0:T(8,128)(2,1)S(1)}, bf16[128,512]{1,0:T(8,128)(2,1)S(1)}, u32[]{:S(2)}, u32[]{:S(2)}) collective-permute-start(bf16[128,512]{1,0:T(8,128)(2,1)S(1)} %get-tuple-element.20), channel_id=1, source_target_pairs={{0,3},{1,2},{2,1},{3,0},{4,7},{5,6},{6,5},{7,4},{8,11},{9,10},{10,... | collective-permute-start | bytes 393224 | tf_op jit(solution)/shard_map/ppermute | solution.py:389
  12.8 3.9 %collective-permute-start.3 = (bf16[128,128]{1,0:T(8,128)(2,1)S(1)}, bf16[128,128]{1,0:T(8,128)(2,1)S(1)}, u32[]{:S(2)}, u32[]{:S(2)}) collective-permute-start(bf16[128,128]{1,0:T(8,128)(2,1)S(1)} %get-tuple-element.23.mine_ref), channel_id=1, source_target_pairs={{0,5},{1,4},{2,7},{3,6},{4,1},{5,0},{6,3},{7,2},{8,13},{9,12},{10,... | collective-permute-start | bytes 98312 | tf_op jit(solution)/shard_map/ppermute | solution.py:389
  14.2 4.8 %collective-permute-start.5 = (bf16[128,128]{1,0:T(8,128)(2,1)S(1)}, bf16[128,128]{1,0:T(8,128)(2,1)S(1)}, u32[]{:S(2)}, u32[]{:S(2)}) collective-permute-start(bf16[128,128]{1,0:T(8,128)(2,1)S(1)} %get-tuple-element.24.mine_ref), channel_id=1, source_target_pairs={{0,9},{1,8},{2,11},{3,10},{4,13},{5,12},{6,15},{7,14},{8,1},{9,0},... | collective-permute-start | bytes 98312 | tf_op jit(solution)/shard_map/ppermute | solution.py:389
  16.8 4.3 %collective-permute-start.4 = (bf16[128,128]{1,0:T(8,128)(2,1)S(1)}, bf16[128,128]{1,0:T(8,128)(2,1)S(1)}, u32[]{:S(2)}, u32[]{:S(2)}) collective-permute-start(bf16[128,128]{1,0:T(8,128)(2,1)S(1)} %add.5.mine_ref), channel_id=1, source_target_pairs={{0,9},{1,8},{2,11},{3,10},{4,13},{5,12},{6,15},{7,14},{8,1},{9,0},... | collective-permute-start | bytes 98312 | tf_op jit(solution)/shard_map/ppermute | solution.py:389
  19.0 3.5 %collective-permute-start.6 = (bf16[128,128]{1,0:T(8,128)(2,1)S(1)}, bf16[128,128]{1,0:T(8,128)(2,1)S(1)}, u32[]{:S(2)}, u32[]{:S(2)}) collective-permute-start(bf16[128,128]{1,0:T(8,128)(2,1)S(1)} %add.7.mine_ref), channel_id=1, source_target_pairs={{0,5},{1,4},{2,7},{3,6},{4,1},{5,0},{6,3},{7,2},{8,13},{9,12},{10,... | collective-permute-start | bytes 98312 | tf_op jit(solution)/shard_map/ppermute | solution.py:389
  22.8 1.3 %collective-permute-start.7 = (bf16[128,128]{1,0:T(8,128)(2,1)S(1)}, bf16[128,128]{1,0:T(8,128)(2,1)S(1)}, u32[]{:S(2)}, u32[]{:S(2)}) collective-permute-start(bf16[128,128]{1,0:T(8,128)(2,1)S(1)} %product_terms.1.mine_ref), channel_id=1, source_target_pairs={{0,1},{1,0},{2,3},{3,2},{4,5},{5,4},{6,7},{7,6},{8,9},{9,8},{10,11... | collective-permute-start | bytes 98312 | tf_op jit(solution)/shard_map/ppermute | solution.py:389
  24.1 4.5 %collective-permute-start.10 = (bf16[128,128]{1,0:T(8,128)(2,1)S(1)}, bf16[128,128]{1,0:T(8,128)(2,1)S(1)}, u32[]{:S(2)}, u32[]{:S(2)}) collective-permute-start(bf16[128,128]{1,0:T(8,128)(2,1)S(1)} %add.9.refs_0_.term_ref), channel_id=1, source_target_pairs={{0,7},{1,6},{2,5},{3,4},{4,3},{5,2},{6,1},{7,0},{8,15},{9,14},{10,... | collective-permute-start | bytes 98312 | tf_op jit(solution)/shard_map/ppermute | solution.py:389
  27.0 3.4 %collective-permute-start.9 = (bf16[128,128]{1,0:T(8,128)(2,1)S(1)}, bf16[128,128]{1,0:T(8,128)(2,1)S(1)}, u32[]{:S(2)}, u32[]{:S(2)}) collective-permute-start(bf16[128,128]{1,0:T(8,128)(2,1)S(1)} %add.9.refs_0_.term_ref), channel_id=1, source_target_pairs={{0,5},{1,4},{2,7},{3,6},{4,1},{5,0},{6,3},{7,2},{8,13},{9,12},{10,... | collective-permute-start | bytes 98312 | tf_op jit(solution)/shard_map/ppermute | solution.py:389
  28.1 3.3 %collective-permute-start.8 = (bf16[128,128]{1,0:T(8,128)(2,1)S(1)}, bf16[128,128]{1,0:T(8,128)(2,1)S(1)}, u32[]{:S(2)}, u32[]{:S(2)}) collective-permute-start(bf16[128,128]{1,0:T(8,128)(2,1)S(1)} %add.9.refs_0_.term_ref), channel_id=1, source_target_pairs={{0,3},{1,2},{2,1},{3,0},{4,7},{5,6},{6,5},{7,4},{8,11},{9,10},{10,... | collective-permute-start | bytes 98312 | tf_op jit(solution)/shard_map/ppermute | solution.py:389
  31.8 4.1 %collective-permute-start.11 = (f32[32,128]{1,0:T(8,128)S(1)}, f32[32,128]{1,0:T(8,128)S(1)}, u32[]{:S(2)}, u32[]{:S(2)}) collective-permute-start(f32[32,128]{1,0:T(8,128)S(1)} %local_gram.1.gram_ref), channel_id=1, source_target_pairs={{0,9},{1,8},{2,11},{3,10},{4,13},{5,12},{6,15},{7,14},{8,1},{9,0},... | collective-permute-start | bytes 49160 | tf_op jit(solution)/shard_map/ppermute | solution.py:389

commit v22 on v21

--- a/solution.py
+++ b/solution.py
@@ -229,33 +229,11 @@
     )(mine, got, *after)
 
 
-def halves_kernel(mine_ref, got_ref, low_ref, high_ref):
-    size = low_ref.shape[0]
-    for start, ref in ((0, low_ref), (size, high_ref)):
-        rows = pl.ds(start, size)
-        ref[...] = (mine_ref[rows, :] + got_ref[rows, :].astype(F32)).astype(BF16)
-
-
-def add_in_halves(mine, got):
-    out = jax.ShapeDtypeStruct((got.shape[0] // 2, LANES), BF16)
-    return pl.pallas_call(
-        halves_kernel,
-        out_shape=[out, out],
-        compiler_params=params(4),
-        name="add_in_halves",
-    )(mine, got)
-
-
-def product_kernel(mine_ref, got_ref, low_ref, high_ref, out_ref):
-    blocks = mine_ref.shape[1] // LANES // 2
-    rank = low_ref.shape[0] // blocks
+def product_kernel(mine_ref, got_ref, projected_ref, out_ref):
+    blocks = mine_ref.shape[1] // LANES
+    rank = projected_ref.shape[0] // blocks
     projected = jnp.concatenate(
-        [
-            ref[pl.ds(block * rank, rank), :]
-            for ref in (low_ref, high_ref)
-            for block in range(blocks)
-        ],
-        axis=1,
+        [projected_ref[pl.ds(block * rank, rank), :] for block in range(blocks)], axis=1
     )
     terms = [dot_f32(ref[...], projected, ((1,), (1,))) for ref in (mine_ref, got_ref)]
     even = is_even()
@@ -264,13 +242,13 @@
     out_ref[...] = jnp.concatenate([low, high], axis=1).astype(BF16)
 
 
-def product_terms(mine, got, low, high):
+def product_terms(mine, got, projected):
     return pl.pallas_call(
         product_kernel,
         out_shape=jax.ShapeDtypeStruct((mine.shape[0], LANES), BF16),
         compiler_params=params(4),
         name="product_terms",
-    )(mine, got, low, high)
+    )(mine, got, projected)
 
 
 def pair_product(term_ref, got_ref):
@@ -380,12 +358,13 @@
     masks = [1 << bit for bit in range(n_rows.bit_length() - 1)]
     total_rows = snapshot.shape[0] * n_rows
 
-    def swap(x, mask):
-        pairs = [
-            (r * n_cols + c, (r ^ mask) * n_cols + (c + 1) % n_cols)
-            for r in range(n_rows)
-            for c in range(n_cols)
-        ]
+    def swap(x, mask, other=None):
+        pairs = []
+        for r in range(n_rows):
+            for c in range(n_cols):
+                second = (c + r.bit_count()) % 2 and other is not None
+                to = r ^ (other if second else mask)
+                pairs.append((r * n_cols + c, to * n_cols + (c + 1) % n_cols))
         return lax.ppermute(x, ("row", "col"), pairs)
 
     snapshot = pltpu.with_memory_space_constraint(snapshot, pltpu.HBM)
@@ -395,15 +374,15 @@
     own = contract_own(kept, wide, order)
 
     keep, send, columns, give = project(own, got, old_factor.T)
-    low, high = add_in_halves(keep, swap(send, masks[0]))
+    mine = add(keep, swap(send, masks[0]))
     got_columns = swap(give, masks[0])
     others = masks[1:]
-    for step, (mask, turned) in enumerate(zip(others, others[1:] + others[:1])):
+    turned = others[len(others) // 2:] + others[:len(others) // 2]
+    for step, (mask, other) in enumerate(zip(others, turned)):
         after = [got_columns] if step == 1 else []
-        got_low, got_high = swap(low, mask), swap(high, turned)
-        low, high = add(low, got_low), add(high, got_high, *after)
-
-    term = product_terms(columns, got_columns, low, high)
+        mine = add(mine, swap(mine, mask, other), *after)
+
+    term = product_terms(columns, got_columns, mine)
     term = add(term, swap(term, 0))
     pair, next_pair = masks[:2]
     got_term = swap(term, pair)

time: 38.8 us -> 37.6 us (0.969)
  starting transfers between devices: 16.5 us -> 14.5 us
  waiting for transfers between devices: 11.5 us -> 12.2 us
    ppermute x12 -> x10, starting transfers between devices: 16.5 us -> 14.5 us  [swap(): return lax.ppermute(x, ('row', 'col'), pairs)]
    ppermute x12 -> x10, waiting for transfers between devices: 11.5 us -> 12.2 us  [swap(): return lax.ppermute(x, ('row', 'col'), pairs)]
  transfers between devices with their start and end apart: 12 -> 10, of which waited for: 8 -> 8; matrix products, arithmetic and copies ran while one was open for 0% -> 0% of each run, Pallas kernels for 5% -> 5%
where the time goes in v22:
time: 37.6 us; the launch traced here: 37.4 us
  starting transfers between devices  14.5 us (39%)
  waiting for transfers between devices  12.2 us (32%)
  Pallas kernels  10.6 us (28%)
    ppermute x10, starting transfers between devices, swap(): return lax.ppermute(x, ('row', 'col'), pairs)  14.5 us
    ppermute x10, waiting for transfers between devices, swap(): return lax.ppermute(x, ('row', 'col'), pairs)  12.2 us
    pallas_call x1, Pallas kernels, contract_send(): pl.pallas_call(send_kernel, in_specs=[pinned, pinned], out_shape=[jax.Sha...  5.08 us
    pallas_call x1, Pallas kernels, finish(): pl.pallas_call(functools.partial(finish_kernel, total_rows), out_shape=ja...  2.76 us
    pallas_call x1, Pallas kernels, contract_own(): pl.pallas_call(own_kernel, out_shape=jax.ShapeDtypeStruct((cells, half //...  1.77 us
  transfers between devices with their start and end apart: 10, of which 8 were waited for; matrix products, arithmetic and copies ran while one was open for 0% of the time, Pallas kernels for 5%

profile of v22, /device:TPU:0, one launch (start us, length us, event | category | flops | bytes accessed | tf_op | source)
XLA Modules:
  0.0 37.4 jit_solution(10128557199645412440)
XLA Ops:
  0.0 0.0 copy-start
  0.0 5.1 %contract_send.1 = (bf16[128,1024]{1,0:T(8,128)(2,1)S(1)}, bf16[128,16,1024]{2,1,0:T(8,128)(2,1)S(1)}, bf16[128,1024]{1,0:T(8,128)(2,1)S(1)}, bf16[64,256]{1,0:T(8,128)(2,1)S(1)}) custom-call(bf16[128,32,1024]{2,1,0:T(8,128)(2,1)} %snapshot_ref.1, bf16[64,1024]{1,0:T(8,128)(2,1)} %bitcast.3), custom_call_target="tpu_custom_call" | custom-call | tf_op jit(solution)/shard_map/contract_send/pallas_call | solution.py:128
  5.1 0.5 %collective-permute-start = (bf16[128,1024]{1,0:T(8,128)(2,1)S(1)}, bf16[128,1024]{1,0:T(8,128)(2,1)S(1)}, u32[]{:S(2)}, u32[]{:S(2)}) collective-permute-start(bf16[128,1024]{1,0:T(8,128)(2,1)S(1)} %get-tuple-element.16), channel_id=1, source_target_pairs={{0,1},{1,0},{2,3},{3,2},{4,5},{5,4},{6,7},{7,6},{8,9},{9,8},{10,11... | collective-permute-start | bytes 786440 | tf_op jit(solution)/shard_map/ppermute | solution.py:368
  5.6 1.8 %contract_own.1.own_ref = bf16[128,1024]{1,0:T(8,128)(2,1)S(1)} custom-call(bf16[128,16,1024]{2,1,0:T(8,128)(2,1)S(1)} %get-tuple-element.13.slab_ref, bf16[128,1024]{1,0:T(8,128)(2,1)S(1)} %get-tuple-element.14.wide_ref, bf16[64,256]{1,0:T(8,128)(2,1)S(1)} %get-tuple-element.15.order_ref), custom_call_target="tpu_custom_call" | custom-call | tf_op jit(solution)/shard_map/contract_own/pallas_call | solution.py:165
  7.4 0.0 collective-permute-done.got_ref
  7.4 0.0 copy-done
  7.4 0.2 project.1
  7.6 2.7 %collective-permute-start.2 = (bf16[256,128]{1,0:T(8,128)(2,1)S(1)}, bf16[256,128]{1,0:T(8,128)(2,1)S(1)}, u32[]{:S(2)}, u32[]{:S(2)}) collective-permute-start(bf16[256,128]{1,0:T(8,128)(2,1)S(1)} %get-tuple-element.20), channel_id=1, source_target_pairs={{0,3},{1,2},{2,1},{3,0},{4,7},{5,6},{6,5},{7,4},{8,11},{9,10},{10,... | collective-permute-start | bytes 196616 | tf_op jit(solution)/shard_map/ppermute | solution.py:368
  10.3 2.5 %collective-permute-done.2.got_ref = bf16[256,128]{1,0:T(8,128)(2,1)S(1)} collective-permute-done((bf16[256,128]{1,0:T(8,128)(2,1)S(1)}, bf16[256,128]{1,0:T(8,128)(2,1)S(1)}, u32[]{:S(2)}, u32[]{:S(2)}) %collective-permute-start.2) | collective-permute-done | bytes 65568 | tf_op jit(solution)/shard_map/ppermute | solution.py:368
  12.8 1.4 %collective-permute-start.3 = (bf16[256,128]{1,0:T(8,128)(2,1)S(1)}, bf16[256,128]{1,0:T(8,128)(2,1)S(1)}, u32[]{:S(2)}, u32[]{:S(2)}) collective-permute-start(bf16[256,128]{1,0:T(8,128)(2,1)S(1)} %add.4.mine_ref), channel_id=1, source_target_pairs={{0,5},{1,8},{2,11},{3,6},{4,13},{5,0},{6,3},{7,14},{8,1},{9,12},{1... | collective-permute-start | bytes 196616 | tf_op jit(solution)/shard_map/ppermute | solution.py:368
  14.2 1.2 %collective-permute-start.1 = (bf16[128,512]{1,0:T(8,128)(2,1)S(1)}, bf16[128,512]{1,0:T(8,128)(2,1)S(1)}, u32[]{:S(2)}, u32[]{:S(2)}) collective-permute-start(bf16[128,512]{1,0:T(8,128)(2,1)S(1)} %get-tuple-element.18), channel_id=1, source_target_pairs={{0,3},{1,2},{2,1},{3,0},{4,7},{5,6},{6,5},{7,4},{8,11},{9,10},{10,... | collective-permute-start | bytes 393224 | tf_op jit(solution)/shard_map/ppermute | solution.py:368
  15.4 1.2 %collective-permute-done.3.got_ref = bf16[256,128]{1,0:T(8,128)(2,1)S(1)} collective-permute-done((bf16[256,128]{1,0:T(8,128)(2,1)S(1)}, bf16[256,128]{1,0:T(8,128)(2,1)S(1)}, u32[]{:S(2)}, u32[]{:S(2)}) %collective-permute-start.3) | collective-permute-done | bytes 65568 | tf_op jit(solution)/shard_map/ppermute | solution.py:368
  16.6 2.7 %collective-permute-start.4 = (bf16[256,128]{1,0:T(8,128)(2,1)S(1)}, bf16[256,128]{1,0:T(8,128)(2,1)S(1)}, u32[]{:S(2)}, u32[]{:S(2)}) collective-permute-start(bf16[256,128]{1,0:T(8,128)(2,1)S(1)} %add.5.mine_ref), channel_id=1, source_target_pairs={{0,9},{1,4},{2,7},{3,10},{4,1},{5,12},{6,15},{7,2},{8,13},{9,0},{1... | collective-permute-start | bytes 196616 | tf_op jit(solution)/shard_map/ppermute | solution.py:368
  19.3 0.0 collective-permute-done.1.refs_0_.got_ref
  19.3 2.0 %collective-permute-done.4.got_ref = bf16[256,128]{1,0:T(8,128)(2,1)S(1)} collective-permute-done((bf16[256,128]{1,0:T(8,128)(2,1)S(1)}, bf16[256,128]{1,0:T(8,128)(2,1)S(1)}, u32[]{:S(2)}, u32[]{:S(2)}) %collective-permute-start.4) | collective-permute-done | bytes 65568 | tf_op jit(solution)/shard_map/ppermute | solution.py:368
  21.3 0.3 product_terms.1.mine_ref
  21.6 0.9 %collective-permute-start.5 = (bf16[128,128]{1,0:T(8,128)(2,1)S(1)}, bf16[128,128]{1,0:T(8,128)(2,1)S(1)}, u32[]{:S(2)}, u32[]{:S(2)}) collective-permute-start(bf16[128,128]{1,0:T(8,128)(2,1)S(1)} %product_terms.1.mine_ref), channel_id=1, source_target_pairs={{0,1},{1,0},{2,3},{3,2},{4,5},{5,4},{6,7},{7,6},{8,9},{9,8},{10,11... | collective-permute-start | bytes 98312 | tf_op jit(solution)/shard_map/ppermute | solution.py:368
  22.4 0.9 %collective-permute-done.5.got_ref = bf16[128,128]{1,0:T(8,128)(2,1)S(1)} collective-permute-done((bf16[128,128]{1,0:T(8,128)(2,1)S(1)}, bf16[128,128]{1,0:T(8,128)(2,1)S(1)}, u32[]{:S(2)}, u32[]{:S(2)}) %collective-permute-start.5) | collective-permute-done | bytes 32800 | tf_op jit(solution)/shard_map/ppermute | solution.py:368
  23.3 2.6 %collective-permute-start.8 = (bf16[128,128]{1,0:T(8,128)(2,1)S(1)}, bf16[128,128]{1,0:T(8,128)(2,1)S(1)}, u32[]{:S(2)}, u32[]{:S(2)}) collective-permute-start(bf16[128,128]{1,0:T(8,128)(2,1)S(1)} %add.7.refs_0_.term_ref), channel_id=1, source_target_pairs={{0,7},{1,6},{2,5},{3,4},{4,3},{5,2},{6,1},{7,0},{8,15},{9,14},{10,... | collective-permute-start | bytes 98312 | tf_op jit(solution)/shard_map/ppermute | solution.py:368
  25.9 0.9 %collective-permute-start.7 = (bf16[128,128]{1,0:T(8,128)(2,1)S(1)}, bf16[128,128]{1,0:T(8,128)(2,1)S(1)}, u32[]{:S(2)}, u32[]{:S(2)}) collective-permute-start(bf16[128,128]{1,0:T(8,128)(2,1)S(1)} %add.7.refs_0_.term_ref), channel_id=1, source_target_pairs={{0,5},{1,4},{2,7},{3,6},{4,1},{5,0},{6,3},{7,2},{8,13},{9,12},{10,... | collective-permute-start | bytes 98312 | tf_op jit(solution)/shard_map/ppermute | solution.py:368
  26.8 0.0 collective-permute-start.6
  26.8 0.8 %collective-permute-done.8.refs_3_ = bf16[128,128]{1,0:T(8,128)(2,1)S(1)} collective-permute-done((bf16[128,128]{1,0:T(8,128)(2,1)S(1)}, bf16[128,128]{1,0:T(8,128)(2,1)S(1)}, u32[]{:S(2)}, u32[]{:S(2)}) %collective-permute-start.8) | collective-permute-done | bytes 32800 | tf_op jit(solution)/shard_map/ppermute | solution.py:368
  27.6 1.7 %collective-permute-done.7.refs_2_ = bf16[128,128]{1,0:T(8,128)(2,1)S(1)} collective-permute-done((bf16[128,128]{1,0:T(8,128)(2,1)S(1)}, bf16[128,128]{1,0:T(8,128)(2,1)S(1)}, u32[]{:S(2)}, u32[]{:S(2)}) %collective-permute-start.7) | collective-permute-done | bytes 32800 | tf_op jit(solution)/shard_map/ppermute | solution.py:368
  29.3 0.9 %collective-permute-done.6.refs_1_.got_term_ref = bf16[128,128]{1,0:T(8,128)(2,1)S(1)} collective-permute-done((bf16[128,128]{1,0:T(8,128)(2,1)S(1)}, bf16[128,128]{1,0:T(8,128)(2,1)S(1)}, u32[]{:S(2)}, u32[]{:S(2)}) %collective-permute-start.6) | collective-permute-done | bytes 32800 | tf_op jit(solution)/shard_map/ppermute | solution.py:368
  30.1 0.4 %local_gram.1.gram_ref = f32[32,128]{1,0:T(8,128)S(1)} custom-call(bf16[128,128]{1,0:T(8,128)(2,1)S(1)} %add.7.refs_0_.term_ref, bf16[128,128]{1,0:T(8,128)(2,1)S(1)} %collective-permute-done.6.refs_1_.got_term_ref, bf16[128,128]{1,0:T(8,128)(2,1)S(1)} %collective-permute-done.7.refs_2_, bf16[128,128]{1,0:T(8,128)(2,1)S(1)} %collective-permute-done.8.refs_3_), custom_call_target="tpu_custom_call" | custom-call | tf_op jit(solution)/shard_map/local_gram/pallas_call | solution.py:270
  30.5 1.7 %collective-permute-start.9 = (f32[32,128]{1,0:T(8,128)S(1)}, f32[32,128]{1,0:T(8,128)S(1)}, u32[]{:S(2)}, u32[]{:S(2)}) collective-permute-start(f32[32,128]{1,0:T(8,128)S(1)} %local_gram.1.gram_ref), channel_id=1, source_target_pairs={{0,9},{1,8},{2,11},{3,10},{4,13},{5,12},{6,15},{7,14},{8,1},{9,0},... | collective-permute-start | bytes 49160 | tf_op jit(solution)/shard_map/ppermute | solution.py:368
  32.2 2.4 %collective-permute-done.9.got_gram_ref = f32[32,128]{1,0:T(8,128)S(1)} collective-permute-done((f32[32,128]{1,0:T(8,128)S(1)}, f32[32,128]{1,0:T(8,128)S(1)}, u32[]{:S(2)}, u32[]{:S(2)}) %collective-permute-start.9) | collective-permute-done | bytes 16416 | tf_op jit(solution)/shard_map/ppermute | solution.py:368
  34.6 2.8 %finish.1 = f32[64,64]{1,0:T(8,128)} custom-call(bf16[128,128]{1,0:T(8,128)(2,1)S(1)} %add.7.refs_0_.term_ref, bf16[128,128]{1,0:T(8,128)(2,1)S(1)} %collective-permute-done.6.refs_1_.got_term_ref, f32[32,128]{1,0:T(8,128)S(1)} %local_gram.1.gram_ref, f32[32,128]{1,0:T(8,128)S(1)} %collective-permute-done.9.got_gram_ref), custom_call_target="tpu_custom_call" | custom-call | tf_op jit(solution)/shard_map/finish/pallas_call | solution.py:348
  (4 shorter events, 0.1 us)
Async XLA Ops:
  0.0 7.4 %copy-start = (bf16[128,64]{0,1:T(8,128)(2,1)S(1)}, bf16[128,64]{0,1:T(8,128)(2,1)}, u32[]{:S(2)}) copy-start(bf16[128,64]{0,1:T(8,128)(2,1)} %param.5) | copy-start | bytes 49156
  5.1 2.3 %collective-permute-start = (bf16[128,1024]{1,0:T(8,128)(2,1)S(1)}, bf16[128,1024]{1,0:T(8,128)(2,1)S(1)}, u32[]{:S(2)}, u32[]{:S(2)}) collective-permute-start(bf16[128,1024]{1,0:T(8,128)(2,1)S(1)} %get-tuple-element.16), channel_id=1, source_target_pairs={{0,1},{1,0},{2,3},{3,2},{4,5},{5,4},{6,7},{7,6},{8,9},{9,8},{10,11... | collective-permute-start | bytes 786440 | tf_op jit(solution)/shard_map/ppermute | solution.py:368
  7.6 5.2 %collective-permute-start.2 = (bf16[256,128]{1,0:T(8,128)(2,1)S(1)}, bf16[256,128]{1,0:T(8,128)(2,1)S(1)}, u32[]{:S(2)}, u32[]{:S(2)}) collective-permute-start(bf16[256,128]{1,0:T(8,128)(2,1)S(1)} %get-tuple-element.20), channel_id=1, source_target_pairs={{0,3},{1,2},{2,1},{3,0},{4,7},{5,6},{6,5},{7,4},{8,11},{9,10},{10,... | collective-permute-start | bytes 196616 | tf_op jit(solution)/shard_map/ppermute | solution.py:368
  12.8 3.8 %collective-permute-start.3 = (bf16[256,128]{1,0:T(8,128)(2,1)S(1)}, bf16[256,128]{1,0:T(8,128)(2,1)S(1)}, u32[]{:S(2)}, u32[]{:S(2)}) collective-permute-start(bf16[256,128]{1,0:T(8,128)(2,1)S(1)} %add.4.mine_ref), channel_id=1, source_target_pairs={{0,5},{1,8},{2,11},{3,6},{4,13},{5,0},{6,3},{7,14},{8,1},{9,12},{1... | collective-permute-start | bytes 196616 | tf_op jit(solution)/shard_map/ppermute | solution.py:368
  14.2 5.1 %collective-permute-start.1 = (bf16[128,512]{1,0:T(8,128)(2,1)S(1)}, bf16[128,512]{1,0:T(8,128)(2,1)S(1)}, u32[]{:S(2)}, u32[]{:S(2)}) collective-permute-start(bf16[128,512]{1,0:T(8,128)(2,1)S(1)} %get-tuple-element.18), channel_id=1, source_target_pairs={{0,3},{1,2},{2,1},{3,0},{4,7},{5,6},{6,5},{7,4},{8,11},{9,10},{10,... | collective-permute-start | bytes 393224 | tf_op jit(solution)/shard_map/ppermute | solution.py:368
  16.6 4.7 %collective-permute-start.4 = (bf16[256,128]{1,0:T(8,128)(2,1)S(1)}, bf16[256,128]{1,0:T(8,128)(2,1)S(1)}, u32[]{:S(2)}, u32[]{:S(2)}) collective-permute-start(bf16[256,128]{1,0:T(8,128)(2,1)S(1)} %add.5.mine_ref), channel_id=1, source_target_pairs={{0,9},{1,4},{2,7},{3,10},{4,1},{5,12},{6,15},{7,2},{8,13},{9,0},{1... | collective-permute-start | bytes 196616 | tf_op jit(solution)/shard_map/ppermute | solution.py:368
  21.6 1.7 %collective-permute-start.5 = (bf16[128,128]{1,0:T(8,128)(2,1)S(1)}, bf16[128,128]{1,0:T(8,128)(2,1)S(1)}, u32[]{:S(2)}, u32[]{:S(2)}) collective-permute-start(bf16[128,128]{1,0:T(8,128)(2,1)S(1)} %product_terms.1.mine_ref), channel_id=1, source_target_pairs={{0,1},{1,0},{2,3},{3,2},{4,5},{5,4},{6,7},{7,6},{8,9},{9,8},{10,11... | collective-permute-start | bytes 98312 | tf_op jit(solution)/shard_map/ppermute | solution.py:368
  23.3 4.3 %collective-permute-start.8 = (bf16[128,128]{1,0:T(8,128)(2,1)S(1)}, bf16[128,128]{1,0:T(8,128)(2,1)S(1)}, u32[]{:S(2)}, u32[]{:S(2)}) collective-permute-start(bf16[128,128]{1,0:T(8,128)(2,1)S(1)} %add.7.refs_0_.term_ref), channel_id=1, source_target_pairs={{0,7},{1,6},{2,5},{3,4},{4,3},{5,2},{6,1},{7,0},{8,15},{9,14},{10,... | collective-permute-start | bytes 98312 | tf_op jit(solution)/shard_map/ppermute | solution.py:368
  25.9 3.4 %collective-permute-start.7 = (bf16[128,128]{1,0:T(8,128)(2,1)S(1)}, bf16[128,128]{1,0:T(8,128)(2,1)S(1)}, u32[]{:S(2)}, u32[]{:S(2)}) collective-permute-start(bf16[128,128]{1,0:T(8,128)(2,1)S(1)} %add.7.refs_0_.term_ref), channel_id=1, source_target_pairs={{0,5},{1,4},{2,7},{3,6},{4,1},{5,0},{6,3},{7,2},{8,13},{9,12},{10,... | collective-permute-start | bytes 98312 | tf_op jit(solution)/shard_map/ppermute | solution.py:368
  26.8 3.3 %collective-permute-start.6 = (bf16[128,128]{1,0:T(8,128)(2,1)S(1)}, bf16[128,128]{1,0:T(8,128)(2,1)S(1)}, u32[]{:S(2)}, u32[]{:S(2)}) collective-permute-start(bf16[128,128]{1,0:T(8,128)(2,1)S(1)} %add.7.refs_0_.term_ref), channel_id=1, source_target_pairs={{0,3},{1,2},{2,1},{3,0},{4,7},{5,6},{6,5},{7,4},{8,11},{9,10},{10,... | collective-permute-start | bytes 98312 | tf_op jit(solution)/shard_map/ppermute | solution.py:368
  30.5 4.1 %collective-permute-start.9 = (f32[32,128]{1,0:T(8,128)S(1)}, f32[32,128]{1,0:T(8,128)S(1)}, u32[]{:S(2)}, u32[]{:S(2)}) collective-permute-start(f32[32,128]{1,0:T(8,128)S(1)} %local_gram.1.gram_ref), channel_id=1, source_target_pairs={{0,9},{1,8},{2,11},{3,10},{4,13},{5,12},{6,15},{7,14},{8,1},{9,0},... | collective-permute-start | bytes 49160 | tf_op jit(solution)/shard_map/ppermute | solution.py:368

commit v23 on v22

--- a/solution.py
+++ b/solution.py
@@ -379,7 +379,7 @@
     others = masks[1:]
     turned = others[len(others) // 2:] + others[:len(others) // 2]
     for step, (mask, other) in enumerate(zip(others, turned)):
-        after = [got_columns] if step == 1 else []
+        after = [got_columns] if step == 0 else []
         mine = add(mine, swap(mine, mask, other), *after)
 
     term = product_terms(columns, got_columns, mine)

time: 37.6 us -> 38.3 us (1.019)
  waiting for transfers between devices: 12.2 us -> 13.8 us
  starting transfers between devices: 14.5 us -> 13.8 us
    ppermute x10, waiting for transfers between devices: 12.2 us -> 13.8 us  [swap(): return lax.ppermute(x, ('row', 'col'), pairs)]
    ppermute x10, starting transfers between devices: 14.5 us -> 13.8 us  [swap(): return lax.ppermute(x, ('row', 'col'), pairs)]
  transfers between devices with their start and end apart: 10 -> 10, of which waited for: 8 -> 9; matrix products, arithmetic and copies ran while one was open for 0% -> 0% of each run, Pallas kernels for 5% -> 5%
where the time goes in v23:
time: 38.3 us; the launch traced here: 38.2 us
  starting transfers between devices  13.8 us (36%)
  waiting for transfers between devices  13.8 us (36%)
  Pallas kernels  10.6 us (28%)
    ppermute x10, waiting for transfers between devices, swap(): return lax.ppermute(x, ('row', 'col'), pairs)  13.8 us
    ppermute x10, starting transfers between devices, swap(): return lax.ppermute(x, ('row', 'col'), pairs)  13.8 us
    pallas_call x1, Pallas kernels, contract_send(): pl.pallas_call(send_kernel, in_specs=[pinned, pinned], out_shape=[jax.Sha...  5.08 us
    pallas_call x1, Pallas kernels, finish(): pl.pallas_call(functools.partial(finish_kernel, total_rows), out_shape=ja...  2.76 us
    pallas_call x1, Pallas kernels, contract_own(): pl.pallas_call(own_kernel, out_shape=jax.ShapeDtypeStruct((cells, half //...  1.77 us
  transfers between devices with their start and end apart: 10, of which 9 were waited for; matrix products, arithmetic and copies ran while one was open for 0% of the time, Pallas kernels for 5%

profile of v23, /device:TPU:0, one launch (start us, length us, event | category | flops | bytes accessed | tf_op | source)
XLA Modules:
  0.0 38.2 jit_solution(456703627097235895)
XLA Ops:
  0.0 0.0 copy-start
  0.0 5.1 %contract_send.1 = (bf16[128,1024]{1,0:T(8,128)(2,1)S(1)}, bf16[128,16,1024]{2,1,0:T(8,128)(2,1)S(1)}, bf16[128,1024]{1,0:T(8,128)(2,1)S(1)}, bf16[64,256]{1,0:T(8,128)(2,1)S(1)}) custom-call(bf16[128,32,1024]{2,1,0:T(8,128)(2,1)} %snapshot_ref.1, bf16[64,1024]{1,0:T(8,128)(2,1)} %bitcast.3), custom_call_target="tpu_custom_call" | custom-call | tf_op jit(solution)/shard_map/contract_send/pallas_call | solution.py:128
  5.1 0.5 %collective-permute-start = (bf16[128,1024]{1,0:T(8,128)(2,1)S(1)}, bf16[128,1024]{1,0:T(8,128)(2,1)S(1)}, u32[]{:S(2)}, u32[]{:S(2)}) collective-permute-start(bf16[128,1024]{1,0:T(8,128)(2,1)S(1)} %get-tuple-element.16), channel_id=1, source_target_pairs={{0,1},{1,0},{2,3},{3,2},{4,5},{5,4},{6,7},{7,6},{8,9},{9,8},{10,11... | collective-permute-start | bytes 786440 | tf_op jit(solution)/shard_map/ppermute | solution.py:368
  5.6 1.8 %contract_own.1.own_ref = bf16[128,1024]{1,0:T(8,128)(2,1)S(1)} custom-call(bf16[128,16,1024]{2,1,0:T(8,128)(2,1)S(1)} %get-tuple-element.13.slab_ref, bf16[128,1024]{1,0:T(8,128)(2,1)S(1)} %get-tuple-element.14.wide_ref, bf16[64,256]{1,0:T(8,128)(2,1)S(1)} %get-tuple-element.15.order_ref), custom_call_target="tpu_custom_call" | custom-call | tf_op jit(solution)/shard_map/contract_own/pallas_call | solution.py:165
  7.4 0.0 collective-permute-done.got_ref
  7.4 0.0 copy-done
  7.4 0.2 project.1
  7.6 2.7 %collective-permute-start.2 = (bf16[256,128]{1,0:T(8,128)(2,1)S(1)}, bf16[256,128]{1,0:T(8,128)(2,1)S(1)}, u32[]{:S(2)}, u32[]{:S(2)}) collective-permute-start(bf16[256,128]{1,0:T(8,128)(2,1)S(1)} %get-tuple-element.20), channel_id=1, source_target_pairs={{0,3},{1,2},{2,1},{3,0},{4,7},{5,6},{6,5},{7,4},{8,11},{9,10},{10,... | collective-permute-start | bytes 196616 | tf_op jit(solution)/shard_map/ppermute | solution.py:368
  10.4 0.1 collective-permute-start.1
  10.4 2.4 %collective-permute-done.2.got_ref = bf16[256,128]{1,0:T(8,128)(2,1)S(1)} collective-permute-done((bf16[256,128]{1,0:T(8,128)(2,1)S(1)}, bf16[256,128]{1,0:T(8,128)(2,1)S(1)}, u32[]{:S(2)}, u32[]{:S(2)}) %collective-permute-start.2) | collective-permute-done | bytes 65568 | tf_op jit(solution)/shard_map/ppermute | solution.py:368
  12.8 1.4 %collective-permute-start.3 = (bf16[256,128]{1,0:T(8,128)(2,1)S(1)}, bf16[256,128]{1,0:T(8,128)(2,1)S(1)}, u32[]{:S(2)}, u32[]{:S(2)}) collective-permute-start(bf16[256,128]{1,0:T(8,128)(2,1)S(1)} %add.4.mine_ref), channel_id=1, source_target_pairs={{0,5},{1,8},{2,11},{3,6},{4,13},{5,0},{6,3},{7,14},{8,1},{9,12},{1... | collective-permute-start | bytes 196616 | tf_op jit(solution)/shard_map/ppermute | solution.py:368
  14.2 1.8 %collective-permute-done.1.refs_0_.got_ref = bf16[128,512]{1,0:T(8,128)(2,1)S(1)} collective-permute-done((bf16[128,512]{1,0:T(8,128)(2,1)S(1)}, bf16[128,512]{1,0:T(8,128)(2,1)S(1)}, u32[]{:S(2)}, u32[]{:S(2)}) %collective-permute-start.1) | collective-permute-done | bytes 131104 | tf_op jit(solution)/shard_map/ppermute | solution.py:368
  16.0 0.6 %collective-permute-done.3.got_ref = bf16[256,128]{1,0:T(8,128)(2,1)S(1)} collective-permute-done((bf16[256,128]{1,0:T(8,128)(2,1)S(1)}, bf16[256,128]{1,0:T(8,128)(2,1)S(1)}, u32[]{:S(2)}, u32[]{:S(2)}) %collective-permute-start.3) | collective-permute-done | bytes 65568 | tf_op jit(solution)/shard_map/ppermute | solution.py:368
  16.6 2.9 %collective-permute-start.4 = (bf16[256,128]{1,0:T(8,128)(2,1)S(1)}, bf16[256,128]{1,0:T(8,128)(2,1)S(1)}, u32[]{:S(2)}, u32[]{:S(2)}) collective-permute-start(bf16[256,128]{1,0:T(8,128)(2,1)S(1)} %add.5.mine_ref), channel_id=1, source_target_pairs={{0,9},{1,4},{2,7},{3,10},{4,1},{5,12},{6,15},{7,2},{8,13},{9,0},{1... | collective-permute-start | bytes 196616 | tf_op jit(solution)/shard_map/ppermute | solution.py:368
  19.5 2.0 %collective-permute-done.4.got_ref = bf16[256,128]{1,0:T(8,128)(2,1)S(1)} collective-permute-done((bf16[256,128]{1,0:T(8,128)(2,1)S(1)}, bf16[256,128]{1,0:T(8,128)(2,1)S(1)}, u32[]{:S(2)}, u32[]{:S(2)}) %collective-permute-start.4) | collective-permute-done | bytes 65568 | tf_op jit(solution)/shard_map/ppermute | solution.py:368
  21.6 0.3 product_terms.1.mine_ref
  21.8 0.5 %collective-permute-start.5 = (bf16[128,128]{1,0:T(8,128)(2,1)S(1)}, bf16[128,128]{1,0:T(8,128)(2,1)S(1)}, u32[]{:S(2)}, u32[]{:S(2)}) collective-permute-start(bf16[128,128]{1,0:T(8,128)(2,1)S(1)} %product_terms.1.mine_ref), channel_id=1, source_target_pairs={{0,1},{1,0},{2,3},{3,2},{4,5},{5,4},{6,7},{7,6},{8,9},{9,8},{10,11... | collective-permute-start | bytes 98312 | tf_op jit(solution)/shard_map/ppermute | solution.py:368
  22.4 0.9 %collective-permute-done.5.got_ref = bf16[128,128]{1,0:T(8,128)(2,1)S(1)} collective-permute-done((bf16[128,128]{1,0:T(8,128)(2,1)S(1)}, bf16[128,128]{1,0:T(8,128)(2,1)S(1)}, u32[]{:S(2)}, u32[]{:S(2)}) %collective-permute-start.5) | collective-permute-done | bytes 32800 | tf_op jit(solution)/shard_map/ppermute | solution.py:368
  23.3 3.0 %collective-permute-start.8 = (bf16[128,128]{1,0:T(8,128)(2,1)S(1)}, bf16[128,128]{1,0:T(8,128)(2,1)S(1)}, u32[]{:S(2)}, u32[]{:S(2)}) collective-permute-start(bf16[128,128]{1,0:T(8,128)(2,1)S(1)} %add.7.refs_0_.term_ref), channel_id=1, source_target_pairs={{0,7},{1,6},{2,5},{3,4},{4,3},{5,2},{6,1},{7,0},{8,15},{9,14},{10,... | collective-permute-start | bytes 98312 | tf_op jit(solution)/shard_map/ppermute | solution.py:368
  26.3 1.2 %collective-permute-start.7 = (bf16[128,128]{1,0:T(8,128)(2,1)S(1)}, bf16[128,128]{1,0:T(8,128)(2,1)S(1)}, u32[]{:S(2)}, u32[]{:S(2)}) collective-permute-start(bf16[128,128]{1,0:T(8,128)(2,1)S(1)} %add.7.refs_0_.term_ref), channel_id=1, source_target_pairs={{0,5},{1,4},{2,7},{3,6},{4,1},{5,0},{6,3},{7,2},{8,13},{9,12},{10,... | collective-permute-start | bytes 98312 | tf_op jit(solution)/shard_map/ppermute | solution.py:368
  27.5 0.0 collective-permute-start.6
  27.5 0.4 %collective-permute-done.8.refs_3_ = bf16[128,128]{1,0:T(8,128)(2,1)S(1)} collective-permute-done((bf16[128,128]{1,0:T(8,128)(2,1)S(1)}, bf16[128,128]{1,0:T(8,128)(2,1)S(1)}, u32[]{:S(2)}, u32[]{:S(2)}) %collective-permute-start.8) | collective-permute-done | bytes 32800 | tf_op jit(solution)/shard_map/ppermute | solution.py:368
  27.9 2.1 %collective-permute-done.7.refs_2_ = bf16[128,128]{1,0:T(8,128)(2,1)S(1)} collective-permute-done((bf16[128,128]{1,0:T(8,128)(2,1)S(1)}, bf16[128,128]{1,0:T(8,128)(2,1)S(1)}, u32[]{:S(2)}, u32[]{:S(2)}) %collective-permute-start.7) | collective-permute-done | bytes 32800 | tf_op jit(solution)/shard_map/ppermute | solution.py:368
  30.0 0.8 %collective-permute-done.6.refs_1_.got_term_ref = bf16[128,128]{1,0:T(8,128)(2,1)S(1)} collective-permute-done((bf16[128,128]{1,0:T(8,128)(2,1)S(1)}, bf16[128,128]{1,0:T(8,128)(2,1)S(1)}, u32[]{:S(2)}, u32[]{:S(2)}) %collective-permute-start.6) | collective-permute-done | bytes 32800 | tf_op jit(solution)/shard_map/ppermute | solution.py:368
  30.8 0.4 local_gram.1.gram_ref
  31.2 1.4 %collective-permute-start.9 = (f32[32,128]{1,0:T(8,128)S(1)}, f32[32,128]{1,0:T(8,128)S(1)}, u32[]{:S(2)}, u32[]{:S(2)}) collective-permute-start(f32[32,128]{1,0:T(8,128)S(1)} %local_gram.1.gram_ref), channel_id=1, source_target_pairs={{0,9},{1,8},{2,11},{3,10},{4,13},{5,12},{6,15},{7,14},{8,1},{9,0},... | collective-permute-start | bytes 49160 | tf_op jit(solution)/shard_map/ppermute | solution.py:368
  32.6 2.8 %collective-permute-done.9.got_gram_ref = f32[32,128]{1,0:T(8,128)S(1)} collective-permute-done((f32[32,128]{1,0:T(8,128)S(1)}, f32[32,128]{1,0:T(8,128)S(1)}, u32[]{:S(2)}, u32[]{:S(2)}) %collective-permute-start.9) | collective-permute-done | bytes 16416 | tf_op jit(solution)/shard_map/ppermute | solution.py:368
  35.4 2.8 %finish.1 = f32[64,64]{1,0:T(8,128)} custom-call(bf16[128,128]{1,0:T(8,128)(2,1)S(1)} %add.7.refs_0_.term_ref, bf16[128,128]{1,0:T(8,128)(2,1)S(1)} %collective-permute-done.6.refs_1_.got_term_ref, f32[32,128]{1,0:T(8,128)S(1)} %local_gram.1.gram_ref, f32[32,128]{1,0:T(8,128)S(1)} %collective-permute-done.9.got_gram_ref), custom_call_target="tpu_custom_call" | custom-call | tf_op jit(solution)/shard_map/finish/pallas_call | solution.py:348
  (4 shorter events, 0.1 us)
Async XLA Ops:
  0.0 7.4 %copy-start = (bf16[128,64]{0,1:T(8,128)(2,1)S(1)}, bf16[128,64]{0,1:T(8,128)(2,1)}, u32[]{:S(2)}) copy-start(bf16[128,64]{0,1:T(8,128)(2,1)} %param.5) | copy-start | bytes 49156
  5.1 2.3 %collective-permute-start = (bf16[128,1024]{1,0:T(8,128)(2,1)S(1)}, bf16[128,1024]{1,0:T(8,128)(2,1)S(1)}, u32[]{:S(2)}, u32[]{:S(2)}) collective-permute-start(bf16[128,1024]{1,0:T(8,128)(2,1)S(1)} %get-tuple-element.16), channel_id=1, source_target_pairs={{0,1},{1,0},{2,3},{3,2},{4,5},{5,4},{6,7},{7,6},{8,9},{9,8},{10,11... | collective-permute-start | bytes 786440 | tf_op jit(solution)/shard_map/ppermute | solution.py:368
  7.6 5.2 %collective-permute-start.2 = (bf16[256,128]{1,0:T(8,128)(2,1)S(1)}, bf16[256,128]{1,0:T(8,128)(2,1)S(1)}, u32[]{:S(2)}, u32[]{:S(2)}) collective-permute-start(bf16[256,128]{1,0:T(8,128)(2,1)S(1)} %get-tuple-element.20), channel_id=1, source_target_pairs={{0,3},{1,2},{2,1},{3,0},{4,7},{5,6},{6,5},{7,4},{8,11},{9,10},{10,... | collective-permute-start | bytes 196616 | tf_op jit(solution)/shard_map/ppermute | solution.py:368
  10.4 5.6 %collective-permute-start.1 = (bf16[128,512]{1,0:T(8,128)(2,1)S(1)}, bf16[128,512]{1,0:T(8,128)(2,1)S(1)}, u32[]{:S(2)}, u32[]{:S(2)}) collective-permute-start(bf16[128,512]{1,0:T(8,128)(2,1)S(1)} %get-tuple-element.18), channel_id=1, source_target_pairs={{0,3},{1,2},{2,1},{3,0},{4,7},{5,6},{6,5},{7,4},{8,11},{9,10},{10,... | collective-permute-start | bytes 393224 | tf_op jit(solution)/shard_map/ppermute | solution.py:368
  12.8 3.8 %collective-permute-start.3 = (bf16[256,128]{1,0:T(8,128)(2,1)S(1)}, bf16[256,128]{1,0:T(8,128)(2,1)S(1)}, u32[]{:S(2)}, u32[]{:S(2)}) collective-permute-start(bf16[256,128]{1,0:T(8,128)(2,1)S(1)} %add.4.mine_ref), channel_id=1, source_target_pairs={{0,5},{1,8},{2,11},{3,6},{4,13},{5,0},{6,3},{7,14},{8,1},{9,12},{1... | collective-permute-start | bytes 196616 | tf_op jit(solution)/shard_map/ppermute | solution.py:368
  16.6 4.9 %collective-permute-start.4 = (bf16[256,128]{1,0:T(8,128)(2,1)S(1)}, bf16[256,128]{1,0:T(8,128)(2,1)S(1)}, u32[]{:S(2)}, u32[]{:S(2)}) collective-permute-start(bf16[256,128]{1,0:T(8,128)(2,1)S(1)} %add.5.mine_ref), channel_id=1, source_target_pairs={{0,9},{1,4},{2,7},{3,10},{4,1},{5,12},{6,15},{7,2},{8,13},{9,0},{1... | collective-permute-start | bytes 196616 | tf_op jit(solution)/shard_map/ppermute | solution.py:368
  21.8 1.4 %collective-permute-start.5 = (bf16[128,128]{1,0:T(8,128)(2,1)S(1)}, bf16[128,128]{1,0:T(8,128)(2,1)S(1)}, u32[]{:S(2)}, u32[]{:S(2)}) collective-permute-start(bf16[128,128]{1,0:T(8,128)(2,1)S(1)} %product_terms.1.mine_ref), channel_id=1, source_target_pairs={{0,1},{1,0},{2,3},{3,2},{4,5},{5,4},{6,7},{7,6},{8,9},{9,8},{10,11... | collective-permute-start | bytes 98312 | tf_op jit(solution)/shard_map/ppermute | solution.py:368
  23.3 4.6 %collective-permute-start.8 = (bf16[128,128]{1,0:T(8,128)(2,1)S(1)}, bf16[128,128]{1,0:T(8,128)(2,1)S(1)}, u32[]{:S(2)}, u32[]{:S(2)}) collective-permute-start(bf16[128,128]{1,0:T(8,128)(2,1)S(1)} %add.7.refs_0_.term_ref), channel_id=1, source_target_pairs={{0,7},{1,6},{2,5},{3,4},{4,3},{5,2},{6,1},{7,0},{8,15},{9,14},{10,... | collective-permute-start | bytes 98312 | tf_op jit(solution)/shard_map/ppermute | solution.py:368
  26.3 3.7 %collective-permute-start.7 = (bf16[128,128]{1,0:T(8,128)(2,1)S(1)}, bf16[128,128]{1,0:T(8,128)(2,1)S(1)}, u32[]{:S(2)}, u32[]{:S(2)}) collective-permute-start(bf16[128,128]{1,0:T(8,128)(2,1)S(1)} %add.7.refs_0_.term_ref), channel_id=1, source_target_pairs={{0,5},{1,4},{2,7},{3,6},{4,1},{5,0},{6,3},{7,2},{8,13},{9,12},{10,... | collective-permute-start | bytes 98312 | tf_op jit(solution)/shard_map/ppermute | solution.py:368
  27.5 3.3 %collective-permute-start.6 = (bf16[128,128]{1,0:T(8,128)(2,1)S(1)}, bf16[128,128]{1,0:T(8,128)(2,1)S(1)}, u32[]{:S(2)}, u32[]{:S(2)}) collective-permute-start(bf16[128,128]{1,0:T(8,128)(2,1)S(1)} %add.7.refs_0_.term_ref), channel_id=1, source_target_pairs={{0,3},{1,2},{2,1},{3,0},{4,7},{5,6},{6,5},{7,4},{8,11},{9,10},{10,... | collective-permute-start | bytes 98312 | tf_op jit(solution)/shard_map/ppermute | solution.py:368
  31.2 4.3 %collective-permute-start.9 = (f32[32,128]{1,0:T(8,128)S(1)}, f32[32,128]{1,0:T(8,128)S(1)}, u32[]{:S(2)}, u32[]{:S(2)}) collective-permute-start(f32[32,128]{1,0:T(8,128)S(1)} %local_gram.1.gram_ref), channel_id=1, source_target_pairs={{0,9},{1,8},{2,11},{3,10},{4,13},{5,12},{6,15},{7,14},{8,1},{9,0},... | collective-permute-start | bytes 49160 | tf_op jit(solution)/shard_map/ppermute | solution.py:368

commit v24 on v22

--- a/solution.py
+++ b/solution.py
@@ -103,14 +103,14 @@
     small = pltpu.make_async_copy(mode2_ref, small_ref, small_sem)
     small.start()
     for chunk in range(chunks):
-        sends[chunk][0](chunk * STEP, STEP, 2 if chunk else 4)
+        sends[chunk][0](chunk * STEP, STEP, 4)
     fill_order(order_ref, half)
     small.wait()
     wide_ref[...] = jnp.concatenate([small_ref[...]] * (LANES // rank), axis=0)
     for chunk in range(chunks):
         sends[chunk][1](chunk * STEP, STEP)
-        if chunk == 0:
-            start_kept(0, cells, 2 * chunks)
+        if chunk < 2:
+            start_kept(chunk * (cells // 2), cells // 2, 2 * chunks)
         multiply(slab_ref[pl.ds(chunk * STEP, STEP)], wide_ref, flat[chunk % 2])
         if chunk:
             spread(half, flat[(chunk - 1) % 2], order_ref, core_ref, (chunk - 1) * STEP)
@@ -251,15 +251,19 @@
     )(mine, got, projected)
 
 
-def pair_product(term_ref, got_ref):
-    return term_ref[...].astype(F32) + got_ref[...].astype(F32)
-
-
-def gram_kernel(*refs):
-    out_ref = refs[-1]
+def pair_product(term_ref, first_ref, second_ref):
+    got = jnp.where(own_half() == 0, first_ref[...].astype(F32), second_ref[...].astype(F32))
+    return term_ref[...].astype(F32) + got
+
+
+def gram_kernel(term_ref, first_ref, second_ref, last_ref, out_ref):
     rank = LANES // 2
     product = jnp.concatenate(
-        [pair_product(refs[k], refs[k + 1]) for k in range(0, len(refs) - 1, 2)], axis=0
+        [
+            pair_product(term_ref, first_ref, second_ref),
+            pair_product(last_ref, second_ref, first_ref),
+        ],
+        axis=0,
     )
     wide = dot_parts(product, product, 0)
     gram = wide[:rank, :rank] + wide[rank:, rank:]
@@ -329,7 +333,9 @@
     return both, pivots
 
 
-def finish_kernel(total_rows, term_ref, got_term_ref, gram_ref, got_gram_ref, out_ref):
+def finish_kernel(
+    total_rows, term_ref, first_ref, second_ref, gram_ref, got_gram_ref, out_ref
+):
     rank = LANES // 2
     packed = gram_ref[...] + got_gram_ref[...]
     gram = jnp.concatenate([packed[:, :rank], packed[:, rank:]], axis=0)
@@ -338,19 +344,19 @@
     inverse = jnp.concatenate([b * (lax.rsqrt(p) * scale) for b, p in zip(both, pivots)], axis=0)
     inverse = inverse[:, rank:]
     half = term_ref.shape[0] // 2
-    product = pair_product(term_ref, got_term_ref)
+    product = pair_product(term_ref, first_ref, second_ref)
     product = jnp.where(lax.axis_index("col") == 0, product[:half], product[half:])
     mine = jnp.where(is_even(), product[:, :rank], product[:, rank:])
     out_ref[...] = dot_parts(mine, inverse, 1)
 
 
-def finish(total_rows, term, got_term, gram, got_gram):
+def finish(total_rows, term, first, second, gram, got_gram):
     return pl.pallas_call(
         functools.partial(finish_kernel, total_rows),
         out_shape=jax.ShapeDtypeStruct((term.shape[0] // 2, LANES // 2), F32),
         compiler_params=params(4),
         name="finish",
-    )(term, got_term, gram, got_gram)
+    )(term, first, second, gram, got_gram)
 
 
 def per_device(snapshot, mode2_factor, old_factor):
@@ -385,11 +391,11 @@
     term = product_terms(columns, got_columns, mine)
     term = add(term, swap(term, 0))
     pair, next_pair = masks[:2]
-    got_term = swap(term, pair)
-    gram = local_gram(term, got_term, swap(term, next_pair), swap(term, pair | next_pair))
+    first, second = swap(term, pair, next_pair), swap(term, next_pair, pair)
+    gram = local_gram(term, first, second, swap(term, pair | next_pair))
     for mask in masks[2:-1]:
         gram = add(gram, swap(gram, mask))
-    return finish(total_rows, term, got_term, gram, swap(gram, masks[-1]))
+    return finish(total_rows, term, first, second, gram, swap(gram, masks[-1]))
 
 
 def solution(mesh):

time: 37.6 us -> 37.7 us (level)
  no operation moved by 1% of the time
where the time goes in v24:
time: 37.7 us; the launch traced here: 37.5 us
  starting transfers between devices  14.6 us (39%)
  waiting for transfers between devices  12.2 us (32%)
  Pallas kernels  10.6 us (28%)
    ppermute x10, starting transfers between devices, swap(): return lax.ppermute(x, ('row', 'col'), pairs)  14.6 us
    ppermute x10, waiting for transfers between devices, swap(): return lax.ppermute(x, ('row', 'col'), pairs)  12.2 us
    pallas_call x1, Pallas kernels, contract_send(): pl.pallas_call(send_kernel, in_specs=[pinned, pinned], out_shape=[jax.Sha...  5.16 us
    pallas_call x1, Pallas kernels, finish(): pl.pallas_call(functools.partial(finish_kernel, total_rows), out_shape=ja...  2.76 us
    pallas_call x1, Pallas kernels, contract_own(): pl.pallas_call(own_kernel, out_shape=jax.ShapeDtypeStruct((cells, half //...  1.77 us
  transfers between devices with their start and end apart: 10, of which 8 were waited for; matrix products, arithmetic and copies ran while one was open for 0% of the time, Pallas kernels for 5%

profile of v24, /device:TPU:0, one launch (start us, length us, event | category | flops | bytes accessed | tf_op | source)
XLA Modules:
  0.0 37.5 jit_solution(4154567354496455581)
XLA Ops:
  0.0 0.0 copy-start
  0.0 5.2 %contract_send.1 = (bf16[128,1024]{1,0:T(8,128)(2,1)S(1)}, bf16[128,16,1024]{2,1,0:T(8,128)(2,1)S(1)}, bf16[128,1024]{1,0:T(8,128)(2,1)S(1)}, bf16[64,256]{1,0:T(8,128)(2,1)S(1)}) custom-call(bf16[128,32,1024]{2,1,0:T(8,128)(2,1)} %snapshot_ref.1, bf16[64,1024]{1,0:T(8,128)(2,1)} %bitcast.3), custom_call_target="tpu_custom_call" | custom-call | tf_op jit(solution)/shard_map/contract_send/pallas_call | solution.py:128
  5.2 0.5 %collective-permute-start = (bf16[128,1024]{1,0:T(8,128)(2,1)S(1)}, bf16[128,1024]{1,0:T(8,128)(2,1)S(1)}, u32[]{:S(2)}, u32[]{:S(2)}) collective-permute-start(bf16[128,1024]{1,0:T(8,128)(2,1)S(1)} %get-tuple-element.16), channel_id=1, source_target_pairs={{0,1},{1,0},{2,3},{3,2},{4,5},{5,4},{6,7},{7,6},{8,9},{9,8},{10,11... | collective-permute-start | bytes 786440 | tf_op jit(solution)/shard_map/ppermute | solution.py:374
  5.7 1.8 %contract_own.1.own_ref = bf16[128,1024]{1,0:T(8,128)(2,1)S(1)} custom-call(bf16[128,16,1024]{2,1,0:T(8,128)(2,1)S(1)} %get-tuple-element.13.slab_ref, bf16[128,1024]{1,0:T(8,128)(2,1)S(1)} %get-tuple-element.14.wide_ref, bf16[64,256]{1,0:T(8,128)(2,1)S(1)} %get-tuple-element.15.order_ref), custom_call_target="tpu_custom_call" | custom-call | tf_op jit(solution)/shard_map/contract_own/pallas_call | solution.py:165
  7.5 0.0 collective-permute-done.got_ref
  7.5 0.0 copy-done
  7.5 0.2 project.1
  7.7 2.7 %collective-permute-start.2 = (bf16[256,128]{1,0:T(8,128)(2,1)S(1)}, bf16[256,128]{1,0:T(8,128)(2,1)S(1)}, u32[]{:S(2)}, u32[]{:S(2)}) collective-permute-start(bf16[256,128]{1,0:T(8,128)(2,1)S(1)} %get-tuple-element.20), channel_id=1, source_target_pairs={{0,3},{1,2},{2,1},{3,0},{4,7},{5,6},{6,5},{7,4},{8,11},{9,10},{10,... | collective-permute-start | bytes 196616 | tf_op jit(solution)/shard_map/ppermute | solution.py:374
  10.4 2.5 %collective-permute-done.2.got_ref = bf16[256,128]{1,0:T(8,128)(2,1)S(1)} collective-permute-done((bf16[256,128]{1,0:T(8,128)(2,1)S(1)}, bf16[256,128]{1,0:T(8,128)(2,1)S(1)}, u32[]{:S(2)}, u32[]{:S(2)}) %collective-permute-start.2) | collective-permute-done | bytes 65568 | tf_op jit(solution)/shard_map/ppermute | solution.py:374
  12.9 1.4 %collective-permute-start.3 = (bf16[256,128]{1,0:T(8,128)(2,1)S(1)}, bf16[256,128]{1,0:T(8,128)(2,1)S(1)}, u32[]{:S(2)}, u32[]{:S(2)}) collective-permute-start(bf16[256,128]{1,0:T(8,128)(2,1)S(1)} %add.4.mine_ref), channel_id=1, source_target_pairs={{0,5},{1,8},{2,11},{3,6},{4,13},{5,0},{6,3},{7,14},{8,1},{9,12},{1... | collective-permute-start | bytes 196616 | tf_op jit(solution)/shard_map/ppermute | solution.py:374
  14.3 1.2 %collective-permute-start.1 = (bf16[128,512]{1,0:T(8,128)(2,1)S(1)}, bf16[128,512]{1,0:T(8,128)(2,1)S(1)}, u32[]{:S(2)}, u32[]{:S(2)}) collective-permute-start(bf16[128,512]{1,0:T(8,128)(2,1)S(1)} %get-tuple-element.18), channel_id=1, source_target_pairs={{0,3},{1,2},{2,1},{3,0},{4,7},{5,6},{6,5},{7,4},{8,11},{9,10},{10,... | collective-permute-start | bytes 393224 | tf_op jit(solution)/shard_map/ppermute | solution.py:374
  15.5 1.2 %collective-permute-done.3.got_ref = bf16[256,128]{1,0:T(8,128)(2,1)S(1)} collective-permute-done((bf16[256,128]{1,0:T(8,128)(2,1)S(1)}, bf16[256,128]{1,0:T(8,128)(2,1)S(1)}, u32[]{:S(2)}, u32[]{:S(2)}) %collective-permute-start.3) | collective-permute-done | bytes 65568 | tf_op jit(solution)/shard_map/ppermute | solution.py:374
  16.7 2.7 %collective-permute-start.4 = (bf16[256,128]{1,0:T(8,128)(2,1)S(1)}, bf16[256,128]{1,0:T(8,128)(2,1)S(1)}, u32[]{:S(2)}, u32[]{:S(2)}) collective-permute-start(bf16[256,128]{1,0:T(8,128)(2,1)S(1)} %add.5.mine_ref), channel_id=1, source_target_pairs={{0,9},{1,4},{2,7},{3,10},{4,1},{5,12},{6,15},{7,2},{8,13},{9,0},{1... | collective-permute-start | bytes 196616 | tf_op jit(solution)/shard_map/ppermute | solution.py:374
  19.4 0.0 collective-permute-done.1.refs_0_.got_ref
  19.4 2.0 %collective-permute-done.4.got_ref = bf16[256,128]{1,0:T(8,128)(2,1)S(1)} collective-permute-done((bf16[256,128]{1,0:T(8,128)(2,1)S(1)}, bf16[256,128]{1,0:T(8,128)(2,1)S(1)}, u32[]{:S(2)}, u32[]{:S(2)}) %collective-permute-start.4) | collective-permute-done | bytes 65568 | tf_op jit(solution)/shard_map/ppermute | solution.py:374
  21.3 0.3 product_terms.1.mine_ref
  21.6 0.9 %collective-permute-start.5 = (bf16[128,128]{1,0:T(8,128)(2,1)S(1)}, bf16[128,128]{1,0:T(8,128)(2,1)S(1)}, u32[]{:S(2)}, u32[]{:S(2)}) collective-permute-start(bf16[128,128]{1,0:T(8,128)(2,1)S(1)} %product_terms.1.mine_ref), channel_id=1, source_target_pairs={{0,1},{1,0},{2,3},{3,2},{4,5},{5,4},{6,7},{7,6},{8,9},{9,8},{10,11... | collective-permute-start | bytes 98312 | tf_op jit(solution)/shard_map/ppermute | solution.py:374
  22.5 0.9 %collective-permute-done.5.got_ref = bf16[128,128]{1,0:T(8,128)(2,1)S(1)} collective-permute-done((bf16[128,128]{1,0:T(8,128)(2,1)S(1)}, bf16[128,128]{1,0:T(8,128)(2,1)S(1)}, u32[]{:S(2)}, u32[]{:S(2)}) %collective-permute-start.5) | collective-permute-done | bytes 32800 | tf_op jit(solution)/shard_map/ppermute | solution.py:374
  23.4 2.6 %collective-permute-start.8 = (bf16[128,128]{1,0:T(8,128)(2,1)S(1)}, bf16[128,128]{1,0:T(8,128)(2,1)S(1)}, u32[]{:S(2)}, u32[]{:S(2)}) collective-permute-start(bf16[128,128]{1,0:T(8,128)(2,1)S(1)} %add.7.term_ref), channel_id=1, source_target_pairs={{0,7},{1,6},{2,5},{3,4},{4,3},{5,2},{6,1},{7,0},{8,15},{9,14},{10,... | collective-permute-start | bytes 98312 | tf_op jit(solution)/shard_map/ppermute | solution.py:374
  26.0 0.9 %collective-permute-start.7 = (bf16[128,128]{1,0:T(8,128)(2,1)S(1)}, bf16[128,128]{1,0:T(8,128)(2,1)S(1)}, u32[]{:S(2)}, u32[]{:S(2)}) collective-permute-start(bf16[128,128]{1,0:T(8,128)(2,1)S(1)} %add.7.term_ref), channel_id=1, source_target_pairs={{0,5},{1,2},{2,1},{3,6},{4,7},{5,0},{6,3},{7,4},{8,11},{9,12},{10,... | collective-permute-start | bytes 98312 | tf_op jit(solution)/shard_map/ppermute | solution.py:374
  26.9 0.0 collective-permute-start.6
  26.9 0.8 %collective-permute-done.8.last_ref = bf16[128,128]{1,0:T(8,128)(2,1)S(1)} collective-permute-done((bf16[128,128]{1,0:T(8,128)(2,1)S(1)}, bf16[128,128]{1,0:T(8,128)(2,1)S(1)}, u32[]{:S(2)}, u32[]{:S(2)}) %collective-permute-start.8) | collective-permute-done | bytes 32800 | tf_op jit(solution)/shard_map/ppermute | solution.py:374
  27.7 1.7 %collective-permute-done.7.second_ref = bf16[128,128]{1,0:T(8,128)(2,1)S(1)} collective-permute-done((bf16[128,128]{1,0:T(8,128)(2,1)S(1)}, bf16[128,128]{1,0:T(8,128)(2,1)S(1)}, u32[]{:S(2)}, u32[]{:S(2)}) %collective-permute-start.7) | collective-permute-done | bytes 32800 | tf_op jit(solution)/shard_map/ppermute | solution.py:374
  29.3 0.9 %collective-permute-done.6.first_ref = bf16[128,128]{1,0:T(8,128)(2,1)S(1)} collective-permute-done((bf16[128,128]{1,0:T(8,128)(2,1)S(1)}, bf16[128,128]{1,0:T(8,128)(2,1)S(1)}, u32[]{:S(2)}, u32[]{:S(2)}) %collective-permute-start.6) | collective-permute-done | bytes 32800 | tf_op jit(solution)/shard_map/ppermute | solution.py:374
  30.2 0.4 %local_gram.1.gram_ref = f32[32,128]{1,0:T(8,128)S(1)} custom-call(bf16[128,128]{1,0:T(8,128)(2,1)S(1)} %add.7.term_ref, bf16[128,128]{1,0:T(8,128)(2,1)S(1)} %collective-permute-done.6.first_ref, bf16[128,128]{1,0:T(8,128)(2,1)S(1)} %collective-permute-done.7.second_ref, bf16[128,128]{1,0:T(8,128)(2,1)S(1)} %collective-permute-done.8.last_ref), custom_call_target="tpu_custom_call" | custom-call | tf_op jit(solution)/shard_map/local_gram/pallas_call | solution.py:274
  30.6 1.7 %collective-permute-start.9 = (f32[32,128]{1,0:T(8,128)S(1)}, f32[32,128]{1,0:T(8,128)S(1)}, u32[]{:S(2)}, u32[]{:S(2)}) collective-permute-start(f32[32,128]{1,0:T(8,128)S(1)} %local_gram.1.gram_ref), channel_id=1, source_target_pairs={{0,9},{1,8},{2,11},{3,10},{4,13},{5,12},{6,15},{7,14},{8,1},{9,0},... | collective-permute-start | bytes 49160 | tf_op jit(solution)/shard_map/ppermute | solution.py:374
  32.3 2.5 %collective-permute-done.9.got_gram_ref = f32[32,128]{1,0:T(8,128)S(1)} collective-permute-done((f32[32,128]{1,0:T(8,128)S(1)}, f32[32,128]{1,0:T(8,128)S(1)}, u32[]{:S(2)}, u32[]{:S(2)}) %collective-permute-start.9) | collective-permute-done | bytes 16416 | tf_op jit(solution)/shard_map/ppermute | solution.py:374
  34.8 2.8 %finish.1 = f32[64,64]{1,0:T(8,128)} custom-call(bf16[128,128]{1,0:T(8,128)(2,1)S(1)} %add.7.term_ref, bf16[128,128]{1,0:T(8,128)(2,1)S(1)} %collective-permute-done.6.first_ref, bf16[128,128]{1,0:T(8,128)(2,1)S(1)} %collective-permute-done.7.second_ref, f32[32,128]{1,0:T(8,128)S(1)} %local_gram.1.gram_ref, f32[32,128]{1,0:T(8,128)S(1)} %collective-permute-done.9.got_gram_ref), custom_call_target="tpu_custom_call" | custom-call | tf_op jit(solution)/shard_map/finish/pallas_call | solution.py:354
  (4 shorter events, 0.1 us)
Async XLA Ops:
  0.0 7.5 %copy-start = (bf16[128,64]{0,1:T(8,128)(2,1)S(1)}, bf16[128,64]{0,1:T(8,128)(2,1)}, u32[]{:S(2)}) copy-start(bf16[128,64]{0,1:T(8,128)(2,1)} %param.5) | copy-start | bytes 49156
  5.2 2.3 %collective-permute-start = (bf16[128,1024]{1,0:T(8,128)(2,1)S(1)}, bf16[128,1024]{1,0:T(8,128)(2,1)S(1)}, u32[]{:S(2)}, u32[]{:S(2)}) collective-permute-start(bf16[128,1024]{1,0:T(8,128)(2,1)S(1)} %get-tuple-element.16), channel_id=1, source_target_pairs={{0,1},{1,0},{2,3},{3,2},{4,5},{5,4},{6,7},{7,6},{8,9},{9,8},{10,11... | collective-permute-start | bytes 786440 | tf_op jit(solution)/shard_map/ppermute | solution.py:374
  7.7 5.2 %collective-permute-start.2 = (bf16[256,128]{1,0:T(8,128)(2,1)S(1)}, bf16[256,128]{1,0:T(8,128)(2,1)S(1)}, u32[]{:S(2)}, u32[]{:S(2)}) collective-permute-start(bf16[256,128]{1,0:T(8,128)(2,1)S(1)} %get-tuple-element.20), channel_id=1, source_target_pairs={{0,3},{1,2},{2,1},{3,0},{4,7},{5,6},{6,5},{7,4},{8,11},{9,10},{10,... | collective-permute-start | bytes 196616 | tf_op jit(solution)/shard_map/ppermute | solution.py:374
  12.9 3.8 %collective-permute-start.3 = (bf16[256,128]{1,0:T(8,128)(2,1)S(1)}, bf16[256,128]{1,0:T(8,128)(2,1)S(1)}, u32[]{:S(2)}, u32[]{:S(2)}) collective-permute-start(bf16[256,128]{1,0:T(8,128)(2,1)S(1)} %add.4.mine_ref), channel_id=1, source_target_pairs={{0,5},{1,8},{2,11},{3,6},{4,13},{5,0},{6,3},{7,14},{8,1},{9,12},{1... | collective-permute-start | bytes 196616 | tf_op jit(solution)/shard_map/ppermute | solution.py:374
  14.3 5.1 %collective-permute-start.1 = (bf16[128,512]{1,0:T(8,128)(2,1)S(1)}, bf16[128,512]{1,0:T(8,128)(2,1)S(1)}, u32[]{:S(2)}, u32[]{:S(2)}) collective-permute-start(bf16[128,512]{1,0:T(8,128)(2,1)S(1)} %get-tuple-element.18), channel_id=1, source_target_pairs={{0,3},{1,2},{2,1},{3,0},{4,7},{5,6},{6,5},{7,4},{8,11},{9,10},{10,... | collective-permute-start | bytes 393224 | tf_op jit(solution)/shard_map/ppermute | solution.py:374
  16.7 4.7 %collective-permute-start.4 = (bf16[256,128]{1,0:T(8,128)(2,1)S(1)}, bf16[256,128]{1,0:T(8,128)(2,1)S(1)}, u32[]{:S(2)}, u32[]{:S(2)}) collective-permute-start(bf16[256,128]{1,0:T(8,128)(2,1)S(1)} %add.5.mine_ref), channel_id=1, source_target_pairs={{0,9},{1,4},{2,7},{3,10},{4,1},{5,12},{6,15},{7,2},{8,13},{9,0},{1... | collective-permute-start | bytes 196616 | tf_op jit(solution)/shard_map/ppermute | solution.py:374
  21.6 1.7 %collective-permute-start.5 = (bf16[128,128]{1,0:T(8,128)(2,1)S(1)}, bf16[128,128]{1,0:T(8,128)(2,1)S(1)}, u32[]{:S(2)}, u32[]{:S(2)}) collective-permute-start(bf16[128,128]{1,0:T(8,128)(2,1)S(1)} %product_terms.1.mine_ref), channel_id=1, source_target_pairs={{0,1},{1,0},{2,3},{3,2},{4,5},{5,4},{6,7},{7,6},{8,9},{9,8},{10,11... | collective-permute-start | bytes 98312 | tf_op jit(solution)/shard_map/ppermute | solution.py:374
  23.4 4.3 %collective-permute-start.8 = (bf16[128,128]{1,0:T(8,128)(2,1)S(1)}, bf16[128,128]{1,0:T(8,128)(2,1)S(1)}, u32[]{:S(2)}, u32[]{:S(2)}) collective-permute-start(bf16[128,128]{1,0:T(8,128)(2,1)S(1)} %add.7.term_ref), channel_id=1, source_target_pairs={{0,7},{1,6},{2,5},{3,4},{4,3},{5,2},{6,1},{7,0},{8,15},{9,14},{10,... | collective-permute-start | bytes 98312 | tf_op jit(solution)/shard_map/ppermute | solution.py:374
  26.0 3.4 %collective-permute-start.7 = (bf16[128,128]{1,0:T(8,128)(2,1)S(1)}, bf16[128,128]{1,0:T(8,128)(2,1)S(1)}, u32[]{:S(2)}, u32[]{:S(2)}) collective-permute-start(bf16[128,128]{1,0:T(8,128)(2,1)S(1)} %add.7.term_ref), channel_id=1, source_target_pairs={{0,5},{1,2},{2,1},{3,6},{4,7},{5,0},{6,3},{7,4},{8,11},{9,12},{10,... | collective-permute-start | bytes 98312 | tf_op jit(solution)/shard_map/ppermute | solution.py:374
  26.9 3.3 %collective-permute-start.6 = (bf16[128,128]{1,0:T(8,128)(2,1)S(1)}, bf16[128,128]{1,0:T(8,128)(2,1)S(1)}, u32[]{:S(2)}, u32[]{:S(2)}) collective-permute-start(bf16[128,128]{1,0:T(8,128)(2,1)S(1)} %add.7.term_ref), channel_id=1, source_target_pairs={{0,3},{1,4},{2,7},{3,0},{4,1},{5,6},{6,5},{7,2},{8,13},{9,10},{10,... | collective-permute-start | bytes 98312 | tf_op jit(solution)/shard_map/ppermute | solution.py:374
  30.6 4.1 %collective-permute-start.9 = (f32[32,128]{1,0:T(8,128)S(1)}, f32[32,128]{1,0:T(8,128)S(1)}, u32[]{:S(2)}, u32[]{:S(2)}) collective-permute-start(f32[32,128]{1,0:T(8,128)S(1)} %local_gram.1.gram_ref), channel_id=1, source_target_pairs={{0,9},{1,8},{2,11},{3,10},{4,13},{5,12},{6,15},{7,14},{8,1},{9,0},... | collective-permute-start | bytes 49160 | tf_op jit(solution)/shard_map/ppermute | solution.py:374

commit v25 on v22

--- a/solution.py
+++ b/solution.py
@@ -178,13 +178,14 @@
 def project_kernel(own_ref, got_ref, factor_ref, keep_ref, send_ref, mine_ref, give_ref):
     rank = factor_ref.shape[0]
     width = mine_ref.shape[1]
-    even = is_even()
-    halves = []
-    for start in (0, width):
-        where = slice(start, start + width)
-        halves.append(own_ref[:, where].astype(F32) + got_ref[:, where].astype(F32))
-    mine = jnp.where(even, halves[0], halves[1]).astype(BF16)
-    give = jnp.where(even, halves[1], halves[0]).astype(BF16)
+    odd = lax.rem(lax.axis_index("row"), 2)
+
+    def columns(start):
+        where = pl.ds(pl.multiple_of(start, width), width)
+        return (own_ref[:, where].astype(F32) + got_ref[:, where].astype(F32)).astype(BF16)
+
+    mine = columns(odd * width)
+    give = columns((1 - odd) * width)
     mine_ref[...] = mine
     give_ref[...] = give
     keep = dot_f32(factor_ref[...], mine, ((1,), (0,)))
@@ -235,17 +236,17 @@
     projected = jnp.concatenate(
         [projected_ref[pl.ds(block * rank, rank), :] for block in range(blocks)], axis=1
     )
-    terms = [dot_f32(ref[...], projected, ((1,), (1,))) for ref in (mine_ref, got_ref)]
+    terms = [dot_f32(projected, ref[...], ((1,), (1,))) for ref in (mine_ref, got_ref)]
     even = is_even()
     low = jnp.where(even, terms[0], terms[1])
     high = jnp.where(even, terms[1], terms[0])
-    out_ref[...] = jnp.concatenate([low, high], axis=1).astype(BF16)
+    out_ref[...] = jnp.concatenate([low, high], axis=0).astype(BF16)
 
 
 def product_terms(mine, got, projected):
     return pl.pallas_call(
         product_kernel,
-        out_shape=jax.ShapeDtypeStruct((mine.shape[0], LANES), BF16),
+        out_shape=jax.ShapeDtypeStruct((LANES, mine.shape[0]), BF16),
         compiler_params=params(4),
         name="product_terms",
     )(mine, got, projected)
@@ -258,11 +259,9 @@
 def gram_kernel(*refs):
     out_ref = refs[-1]
     rank = LANES // 2
-    product = jnp.concatenate(
-        [pair_product(refs[k], refs[k + 1]) for k in range(0, len(refs) - 1, 2)], axis=0
-    )
-    wide = dot_parts(product, product, 0)
-    gram = wide[:rank, :rank] + wide[rank:, rank:]
+    pairs = [pair_product(refs[k], refs[k + 1]) for k in range(0, len(refs) - 1, 2)]
+    product = jnp.concatenate([x[k:k + rank] for x in pairs for k in (0, rank)], axis=1)
+    gram = dot_parts(product, product, 1)
     out_ref[...] = jnp.concatenate([gram[:rank // 2], gram[rank // 2:]], axis=1)
 
 
@@ -287,8 +286,8 @@
     return dot_f32(left, right, ((axis,), (axis,)))
 
 
-def eliminate(gram):
-    rank = gram.shape[0]
+def eliminate(packed):
+    rank = packed.shape[1] // 2
     tile = 8
     count = rank // tile
     wide = 2 * rank
@@ -297,9 +296,11 @@
     full = lambda x: jnp.broadcast_to(x, (tile, wide))
     both = []
     for v in range(count):
-        mine = gram[v * tile:(v + 1) * tile]
-        both.append(jnp.where(lane < rank, jnp.concatenate([mine, mine], axis=1),
-                              (lane - rank == sublane + v * tile).astype(F32)))
+        at = v % (count // 2) * tile
+        mine = packed[at:at + tile]
+        if v >= count // 2:
+            mine = jnp.concatenate([mine[:, rank:], mine[:, :rank]], axis=1)
+        both.append(jnp.where(lane < rank, mine, (lane - rank == sublane + v * tile).astype(F32)))
     pivots = []
     for p in range(count):
         cols = [
@@ -331,23 +332,21 @@
 
 def finish_kernel(total_rows, term_ref, got_term_ref, gram_ref, got_gram_ref, out_ref):
     rank = LANES // 2
-    packed = gram_ref[...] + got_gram_ref[...]
-    gram = jnp.concatenate([packed[:, :rank], packed[:, rank:]], axis=0)
-    both, pivots = eliminate(gram)
+    both, pivots = eliminate(gram_ref[...] + got_gram_ref[...])
     scale = total_rows ** 0.5
     inverse = jnp.concatenate([b * (lax.rsqrt(p) * scale) for b, p in zip(both, pivots)], axis=0)
     inverse = inverse[:, rank:]
-    half = term_ref.shape[0] // 2
+    half = term_ref.shape[1] // 2
     product = pair_product(term_ref, got_term_ref)
-    product = jnp.where(lax.axis_index("col") == 0, product[:half], product[half:])
-    mine = jnp.where(is_even(), product[:, :rank], product[:, rank:])
+    product = jnp.where(is_even(), product[:rank], product[rank:])
+    mine = jnp.where(lax.axis_index("col") == 0, product[:, :half], product[:, half:]).T
     out_ref[...] = dot_parts(mine, inverse, 1)
 
 
 def finish(total_rows, term, got_term, gram, got_gram):
     return pl.pallas_call(
         functools.partial(finish_kernel, total_rows),
-        out_shape=jax.ShapeDtypeStruct((term.shape[0] // 2, LANES // 2), F32),
+        out_shape=jax.ShapeDtypeStruct((term.shape[1] // 2, LANES // 2), F32),
         compiler_params=params(4),
         name="finish",
     )(term, got_term, gram, got_gram)

time: 37.6 us -> 37.3 us (level)
  no operation moved by 1% of the time
where the time goes in v25:
time: 37.3 us; the launch traced here: 37.1 us
  starting transfers between devices  14.5 us (39%)
  waiting for transfers between devices  12.2 us (33%)
  Pallas kernels  10.3 us (28%)
    ppermute x10, starting transfers between devices, swap(): return lax.ppermute(x, ('row', 'col'), pairs)  14.5 us
    ppermute x10, waiting for transfers between devices, swap(): return lax.ppermute(x, ('row', 'col'), pairs)  12.2 us
    pallas_call x1, Pallas kernels, contract_send(): pl.pallas_call(send_kernel, in_specs=[pinned, pinned], out_shape=[jax.Sha...  5.08 us
    pallas_call x1, Pallas kernels, finish(): pl.pallas_call(functools.partial(finish_kernel, total_rows), out_shape=ja...  2.69 us
    pallas_call x1, Pallas kernels, contract_own(): pl.pallas_call(own_kernel, out_shape=jax.ShapeDtypeStruct((cells, half //...  1.77 us
  transfers between devices with their start and end apart: 10, of which 8 were waited for; matrix products, arithmetic and copies ran while one was open for 0% of the time, Pallas kernels for 5%

profile of v25, /device:TPU:0, one launch (start us, length us, event | category | flops | bytes accessed | tf_op | source)
XLA Modules:
  0.0 37.1 jit_solution(15700675862915108741)
XLA Ops:
  0.0 0.0 copy-start
  0.0 5.1 %contract_send.1 = (bf16[128,1024]{1,0:T(8,128)(2,1)S(1)}, bf16[128,16,1024]{2,1,0:T(8,128)(2,1)S(1)}, bf16[128,1024]{1,0:T(8,128)(2,1)S(1)}, bf16[64,256]{1,0:T(8,128)(2,1)S(1)}) custom-call(bf16[128,32,1024]{2,1,0:T(8,128)(2,1)} %snapshot_ref.1, bf16[64,1024]{1,0:T(8,128)(2,1)} %bitcast.3), custom_call_target="tpu_custom_call" | custom-call | tf_op jit(solution)/shard_map/contract_send/pallas_call | solution.py:128
  5.1 0.5 %collective-permute-start = (bf16[128,1024]{1,0:T(8,128)(2,1)S(1)}, bf16[128,1024]{1,0:T(8,128)(2,1)S(1)}, u32[]{:S(2)}, u32[]{:S(2)}) collective-permute-start(bf16[128,1024]{1,0:T(8,128)(2,1)S(1)} %get-tuple-element.16), channel_id=1, source_target_pairs={{0,1},{1,0},{2,3},{3,2},{4,5},{5,4},{6,7},{7,6},{8,9},{9,8},{10,11... | collective-permute-start | bytes 786440 | tf_op jit(solution)/shard_map/ppermute | solution.py:367
  5.6 1.8 %contract_own.1.own_ref = bf16[128,1024]{1,0:T(8,128)(2,1)S(1)} custom-call(bf16[128,16,1024]{2,1,0:T(8,128)(2,1)S(1)} %get-tuple-element.13.slab_ref, bf16[128,1024]{1,0:T(8,128)(2,1)S(1)} %get-tuple-element.14.wide_ref, bf16[64,256]{1,0:T(8,128)(2,1)S(1)} %get-tuple-element.15.order_ref), custom_call_target="tpu_custom_call" | custom-call | tf_op jit(solution)/shard_map/contract_own/pallas_call | solution.py:165
  7.4 0.0 collective-permute-done.got_ref
  7.4 0.0 copy-done
  7.4 0.2 project.1
  7.6 2.7 %collective-permute-start.2 = (bf16[256,128]{1,0:T(8,128)(2,1)S(1)}, bf16[256,128]{1,0:T(8,128)(2,1)S(1)}, u32[]{:S(2)}, u32[]{:S(2)}) collective-permute-start(bf16[256,128]{1,0:T(8,128)(2,1)S(1)} %get-tuple-element.20), channel_id=1, source_target_pairs={{0,3},{1,2},{2,1},{3,0},{4,7},{5,6},{6,5},{7,4},{8,11},{9,10},{10,... | collective-permute-start | bytes 196616 | tf_op jit(solution)/shard_map/ppermute | solution.py:367
  10.3 2.5 %collective-permute-done.2.got_ref = bf16[256,128]{1,0:T(8,128)(2,1)S(1)} collective-permute-done((bf16[256,128]{1,0:T(8,128)(2,1)S(1)}, bf16[256,128]{1,0:T(8,128)(2,1)S(1)}, u32[]{:S(2)}, u32[]{:S(2)}) %collective-permute-start.2) | collective-permute-done | bytes 65568 | tf_op jit(solution)/shard_map/ppermute | solution.py:367
  12.8 1.4 %collective-permute-start.3 = (bf16[256,128]{1,0:T(8,128)(2,1)S(1)}, bf16[256,128]{1,0:T(8,128)(2,1)S(1)}, u32[]{:S(2)}, u32[]{:S(2)}) collective-permute-start(bf16[256,128]{1,0:T(8,128)(2,1)S(1)} %add.4.mine_ref), channel_id=1, source_target_pairs={{0,5},{1,8},{2,11},{3,6},{4,13},{5,0},{6,3},{7,14},{8,1},{9,12},{1... | collective-permute-start | bytes 196616 | tf_op jit(solution)/shard_map/ppermute | solution.py:367
  14.2 1.2 %collective-permute-start.1 = (bf16[128,512]{1,0:T(8,128)(2,1)S(1)}, bf16[128,512]{1,0:T(8,128)(2,1)S(1)}, u32[]{:S(2)}, u32[]{:S(2)}) collective-permute-start(bf16[128,512]{1,0:T(8,128)(2,1)S(1)} %get-tuple-element.18), channel_id=1, source_target_pairs={{0,3},{1,2},{2,1},{3,0},{4,7},{5,6},{6,5},{7,4},{8,11},{9,10},{10,... | collective-permute-start | bytes 393224 | tf_op jit(solution)/shard_map/ppermute | solution.py:367
  15.4 1.2 %collective-permute-done.3.got_ref = bf16[256,128]{1,0:T(8,128)(2,1)S(1)} collective-permute-done((bf16[256,128]{1,0:T(8,128)(2,1)S(1)}, bf16[256,128]{1,0:T(8,128)(2,1)S(1)}, u32[]{:S(2)}, u32[]{:S(2)}) %collective-permute-start.3) | collective-permute-done | bytes 65568 | tf_op jit(solution)/shard_map/ppermute | solution.py:367
  16.6 2.7 %collective-permute-start.4 = (bf16[256,128]{1,0:T(8,128)(2,1)S(1)}, bf16[256,128]{1,0:T(8,128)(2,1)S(1)}, u32[]{:S(2)}, u32[]{:S(2)}) collective-permute-start(bf16[256,128]{1,0:T(8,128)(2,1)S(1)} %add.5.mine_ref), channel_id=1, source_target_pairs={{0,9},{1,4},{2,7},{3,10},{4,1},{5,12},{6,15},{7,2},{8,13},{9,0},{1... | collective-permute-start | bytes 196616 | tf_op jit(solution)/shard_map/ppermute | solution.py:367
  19.3 0.0 collective-permute-done.1.refs_0_.got_ref
  19.3 2.0 %collective-permute-done.4.got_ref = bf16[256,128]{1,0:T(8,128)(2,1)S(1)} collective-permute-done((bf16[256,128]{1,0:T(8,128)(2,1)S(1)}, bf16[256,128]{1,0:T(8,128)(2,1)S(1)}, u32[]{:S(2)}, u32[]{:S(2)}) %collective-permute-start.4) | collective-permute-done | bytes 65568 | tf_op jit(solution)/shard_map/ppermute | solution.py:367
  21.3 0.2 product_terms.1.mine_ref
  21.5 0.9 %collective-permute-start.5 = (bf16[128,128]{1,0:T(8,128)(2,1)S(1)}, bf16[128,128]{1,0:T(8,128)(2,1)S(1)}, u32[]{:S(2)}, u32[]{:S(2)}) collective-permute-start(bf16[128,128]{1,0:T(8,128)(2,1)S(1)} %product_terms.1.mine_ref), channel_id=1, source_target_pairs={{0,1},{1,0},{2,3},{3,2},{4,5},{5,4},{6,7},{7,6},{8,9},{9,8},{10,11... | collective-permute-start | bytes 98312 | tf_op jit(solution)/shard_map/ppermute | solution.py:367
  22.4 0.9 %collective-permute-done.5.got_ref = bf16[128,128]{1,0:T(8,128)(2,1)S(1)} collective-permute-done((bf16[128,128]{1,0:T(8,128)(2,1)S(1)}, bf16[128,128]{1,0:T(8,128)(2,1)S(1)}, u32[]{:S(2)}, u32[]{:S(2)}) %collective-permute-start.5) | collective-permute-done | bytes 32800 | tf_op jit(solution)/shard_map/ppermute | solution.py:367
  23.2 2.6 %collective-permute-start.8 = (bf16[128,128]{1,0:T(8,128)(2,1)S(1)}, bf16[128,128]{1,0:T(8,128)(2,1)S(1)}, u32[]{:S(2)}, u32[]{:S(2)}) collective-permute-start(bf16[128,128]{1,0:T(8,128)(2,1)S(1)} %add.7.refs_0_.term_ref), channel_id=1, source_target_pairs={{0,7},{1,6},{2,5},{3,4},{4,3},{5,2},{6,1},{7,0},{8,15},{9,14},{10,... | collective-permute-start | bytes 98312 | tf_op jit(solution)/shard_map/ppermute | solution.py:367
  25.8 0.9 %collective-permute-start.7 = (bf16[128,128]{1,0:T(8,128)(2,1)S(1)}, bf16[128,128]{1,0:T(8,128)(2,1)S(1)}, u32[]{:S(2)}, u32[]{:S(2)}) collective-permute-start(bf16[128,128]{1,0:T(8,128)(2,1)S(1)} %add.7.refs_0_.term_ref), channel_id=1, source_target_pairs={{0,5},{1,4},{2,7},{3,6},{4,1},{5,0},{6,3},{7,2},{8,13},{9,12},{10,... | collective-permute-start | bytes 98312 | tf_op jit(solution)/shard_map/ppermute | solution.py:367
  26.7 0.0 collective-permute-start.6
  26.7 0.8 %collective-permute-done.8.refs_3_ = bf16[128,128]{1,0:T(8,128)(2,1)S(1)} collective-permute-done((bf16[128,128]{1,0:T(8,128)(2,1)S(1)}, bf16[128,128]{1,0:T(8,128)(2,1)S(1)}, u32[]{:S(2)}, u32[]{:S(2)}) %collective-permute-start.8) | collective-permute-done | bytes 32800 | tf_op jit(solution)/shard_map/ppermute | solution.py:367
  27.5 1.7 %collective-permute-done.7.refs_2_ = bf16[128,128]{1,0:T(8,128)(2,1)S(1)} collective-permute-done((bf16[128,128]{1,0:T(8,128)(2,1)S(1)}, bf16[128,128]{1,0:T(8,128)(2,1)S(1)}, u32[]{:S(2)}, u32[]{:S(2)}) %collective-permute-start.7) | collective-permute-done | bytes 32800 | tf_op jit(solution)/shard_map/ppermute | solution.py:367
  29.2 0.9 %collective-permute-done.6.refs_1_.got_term_ref = bf16[128,128]{1,0:T(8,128)(2,1)S(1)} collective-permute-done((bf16[128,128]{1,0:T(8,128)(2,1)S(1)}, bf16[128,128]{1,0:T(8,128)(2,1)S(1)}, u32[]{:S(2)}, u32[]{:S(2)}) %collective-permute-start.6) | collective-permute-done | bytes 32800 | tf_op jit(solution)/shard_map/ppermute | solution.py:367
  30.1 0.3 local_gram.1.gram_ref
  30.3 1.7 %collective-permute-start.9 = (f32[32,128]{1,0:T(8,128)S(1)}, f32[32,128]{1,0:T(8,128)S(1)}, u32[]{:S(2)}, u32[]{:S(2)}) collective-permute-start(f32[32,128]{1,0:T(8,128)S(1)} %local_gram.1.gram_ref), channel_id=1, source_target_pairs={{0,9},{1,8},{2,11},{3,10},{4,13},{5,12},{6,15},{7,14},{8,1},{9,0},... | collective-permute-start | bytes 49160 | tf_op jit(solution)/shard_map/ppermute | solution.py:367
  32.0 2.4 %collective-permute-done.9.got_gram_ref = f32[32,128]{1,0:T(8,128)S(1)} collective-permute-done((f32[32,128]{1,0:T(8,128)S(1)}, f32[32,128]{1,0:T(8,128)S(1)}, u32[]{:S(2)}, u32[]{:S(2)}) %collective-permute-start.9) | collective-permute-done | bytes 16416 | tf_op jit(solution)/shard_map/ppermute | solution.py:367
  34.4 2.7 %finish.1 = f32[64,64]{1,0:T(8,128)} custom-call(bf16[128,128]{1,0:T(8,128)(2,1)S(1)} %add.7.refs_0_.term_ref, bf16[128,128]{1,0:T(8,128)(2,1)S(1)} %collective-permute-done.6.refs_1_.got_term_ref, f32[32,128]{1,0:T(8,128)S(1)} %local_gram.1.gram_ref, f32[32,128]{1,0:T(8,128)S(1)} %collective-permute-done.9.got_gram_ref), custom_call_target="tpu_custom_call" | custom-call | tf_op jit(solution)/shard_map/finish/pallas_call | solution.py:347
  (4 shorter events, 0.1 us)
Async XLA Ops:
  0.0 7.4 %copy-start = (bf16[128,64]{0,1:T(8,128)(2,1)S(1)}, bf16[128,64]{0,1:T(8,128)(2,1)}, u32[]{:S(2)}) copy-start(bf16[128,64]{0,1:T(8,128)(2,1)} %param.5) | copy-start | bytes 49156
  5.1 2.3 %collective-permute-start = (bf16[128,1024]{1,0:T(8,128)(2,1)S(1)}, bf16[128,1024]{1,0:T(8,128)(2,1)S(1)}, u32[]{:S(2)}, u32[]{:S(2)}) collective-permute-start(bf16[128,1024]{1,0:T(8,128)(2,1)S(1)} %get-tuple-element.16), channel_id=1, source_target_pairs={{0,1},{1,0},{2,3},{3,2},{4,5},{5,4},{6,7},{7,6},{8,9},{9,8},{10,11... | collective-permute-start | bytes 786440 | tf_op jit(solution)/shard_map/ppermute | solution.py:367
  7.6 5.2 %collective-permute-start.2 = (bf16[256,128]{1,0:T(8,128)(2,1)S(1)}, bf16[256,128]{1,0:T(8,128)(2,1)S(1)}, u32[]{:S(2)}, u32[]{:S(2)}) collective-permute-start(bf16[256,128]{1,0:T(8,128)(2,1)S(1)} %get-tuple-element.20), channel_id=1, source_target_pairs={{0,3},{1,2},{2,1},{3,0},{4,7},{5,6},{6,5},{7,4},{8,11},{9,10},{10,... | collective-permute-start | bytes 196616 | tf_op jit(solution)/shard_map/ppermute | solution.py:367
  12.8 3.8 %collective-permute-start.3 = (bf16[256,128]{1,0:T(8,128)(2,1)S(1)}, bf16[256,128]{1,0:T(8,128)(2,1)S(1)}, u32[]{:S(2)}, u32[]{:S(2)}) collective-permute-start(bf16[256,128]{1,0:T(8,128)(2,1)S(1)} %add.4.mine_ref), channel_id=1, source_target_pairs={{0,5},{1,8},{2,11},{3,6},{4,13},{5,0},{6,3},{7,14},{8,1},{9,12},{1... | collective-permute-start | bytes 196616 | tf_op jit(solution)/shard_map/ppermute | solution.py:367
  14.2 5.1 %collective-permute-start.1 = (bf16[128,512]{1,0:T(8,128)(2,1)S(1)}, bf16[128,512]{1,0:T(8,128)(2,1)S(1)}, u32[]{:S(2)}, u32[]{:S(2)}) collective-permute-start(bf16[128,512]{1,0:T(8,128)(2,1)S(1)} %get-tuple-element.18), channel_id=1, source_target_pairs={{0,3},{1,2},{2,1},{3,0},{4,7},{5,6},{6,5},{7,4},{8,11},{9,10},{10,... | collective-permute-start | bytes 393224 | tf_op jit(solution)/shard_map/ppermute | solution.py:367
  16.6 4.7 %collective-permute-start.4 = (bf16[256,128]{1,0:T(8,128)(2,1)S(1)}, bf16[256,128]{1,0:T(8,128)(2,1)S(1)}, u32[]{:S(2)}, u32[]{:S(2)}) collective-permute-start(bf16[256,128]{1,0:T(8,128)(2,1)S(1)} %add.5.mine_ref), channel_id=1, source_target_pairs={{0,9},{1,4},{2,7},{3,10},{4,1},{5,12},{6,15},{7,2},{8,13},{9,0},{1... | collective-permute-start | bytes 196616 | tf_op jit(solution)/shard_map/ppermute | solution.py:367
  21.5 1.7 %collective-permute-start.5 = (bf16[128,128]{1,0:T(8,128)(2,1)S(1)}, bf16[128,128]{1,0:T(8,128)(2,1)S(1)}, u32[]{:S(2)}, u32[]{:S(2)}) collective-permute-start(bf16[128,128]{1,0:T(8,128)(2,1)S(1)} %product_terms.1.mine_ref), channel_id=1, source_target_pairs={{0,1},{1,0},{2,3},{3,2},{4,5},{5,4},{6,7},{7,6},{8,9},{9,8},{10,11... | collective-permute-start | bytes 98312 | tf_op jit(solution)/shard_map/ppermute | solution.py:367
  23.2 4.3 %collective-permute-start.8 = (bf16[128,128]{1,0:T(8,128)(2,1)S(1)}, bf16[128,128]{1,0:T(8,128)(2,1)S(1)}, u32[]{:S(2)}, u32[]{:S(2)}) collective-permute-start(bf16[128,128]{1,0:T(8,128)(2,1)S(1)} %add.7.refs_0_.term_ref), channel_id=1, source_target_pairs={{0,7},{1,6},{2,5},{3,4},{4,3},{5,2},{6,1},{7,0},{8,15},{9,14},{10,... | collective-permute-start | bytes 98312 | tf_op jit(solution)/shard_map/ppermute | solution.py:367
  25.8 3.4 %collective-permute-start.7 = (bf16[128,128]{1,0:T(8,128)(2,1)S(1)}, bf16[128,128]{1,0:T(8,128)(2,1)S(1)}, u32[]{:S(2)}, u32[]{:S(2)}) collective-permute-start(bf16[128,128]{1,0:T(8,128)(2,1)S(1)} %add.7.refs_0_.term_ref), channel_id=1, source_target_pairs={{0,5},{1,4},{2,7},{3,6},{4,1},{5,0},{6,3},{7,2},{8,13},{9,12},{10,... | collective-permute-start | bytes 98312 | tf_op jit(solution)/shard_map/ppermute | solution.py:367
  26.7 3.3 %collective-permute-start.6 = (bf16[128,128]{1,0:T(8,128)(2,1)S(1)}, bf16[128,128]{1,0:T(8,128)(2,1)S(1)}, u32[]{:S(2)}, u32[]{:S(2)}) collective-permute-start(bf16[128,128]{1,0:T(8,128)(2,1)S(1)} %add.7.refs_0_.term_ref), channel_id=1, source_target_pairs={{0,3},{1,2},{2,1},{3,0},{4,7},{5,6},{6,5},{7,4},{8,11},{9,10},{10,... | collective-permute-start | bytes 98312 | tf_op jit(solution)/shard_map/ppermute | solution.py:367
  30.3 4.1 %collective-permute-start.9 = (f32[32,128]{1,0:T(8,128)S(1)}, f32[32,128]{1,0:T(8,128)S(1)}, u32[]{:S(2)}, u32[]{:S(2)}) collective-permute-start(f32[32,128]{1,0:T(8,128)S(1)} %local_gram.1.gram_ref), channel_id=1, source_target_pairs={{0,9},{1,8},{2,11},{3,10},{4,13},{5,12},{6,15},{7,14},{8,1},{9,0},... | collective-permute-start | bytes 49160 | tf_op jit(solution)/shard_map/ppermute | solution.py:367

commit v26 on v25

--- a/solution.py
+++ b/solution.py
@@ -68,7 +68,7 @@
 STEP = 32
 
 
-def slab_copies(snapshot_ref, first, slab_ref, half_index, sem):
+def slab_copies(snapshot_ref, first, slab_ref, half_index, sem, priority):
     half = slab_ref.shape[1]
     fibers = pl.ds(pl.multiple_of(half_index * half, half), half)
 
@@ -81,7 +81,7 @@
 
     def start(begin, size, count):
         for part in range(count):
-            copy(begin + part * (size // count), size // count).start()
+            copy(begin + part * (size // count), size // count).start(priority=priority)
 
     return start, lambda begin, size: copy(begin, size).wait()
 
@@ -95,22 +95,21 @@
     chunks = cells // STEP
     flat = (even_ref, odd_ref)
     sends = [
-        slab_copies(snapshot_ref, 0, slab_ref, 1 - own_half(), sems.at[chunk])
+        slab_copies(snapshot_ref, 0, slab_ref, 1 - own_half(), sems.at[chunk], 1)
         for chunk in range(chunks)
     ]
-    start_kept, wait_kept = slab_copies(snapshot_ref, 0, kept_ref, own_half(), kept_sem)
+    start_kept, wait_kept = slab_copies(snapshot_ref, 0, kept_ref, own_half(), kept_sem, 0)
 
     small = pltpu.make_async_copy(mode2_ref, small_ref, small_sem)
     small.start()
     for chunk in range(chunks):
         sends[chunk][0](chunk * STEP, STEP, 2 if chunk else 4)
+    start_kept(0, cells, 2 * chunks)
     fill_order(order_ref, half)
     small.wait()
     wide_ref[...] = jnp.concatenate([small_ref[...]] * (LANES // rank), axis=0)
     for chunk in range(chunks):
         sends[chunk][1](chunk * STEP, STEP)
-        if chunk == 0:
-            start_kept(0, cells, 2 * chunks)
         multiply(slab_ref[pl.ds(chunk * STEP, STEP)], wide_ref, flat[chunk % 2])
         if chunk:
             spread(half, flat[(chunk - 1) % 2], order_ref, core_ref, (chunk - 1) * STEP)
@@ -175,42 +174,31 @@
     return lax.rem(lax.axis_index("row"), 2) == 0
 
 
-def project_kernel(own_ref, got_ref, factor_ref, keep_ref, send_ref, mine_ref, give_ref):
+def project_kernel(kept, own_ref, got_ref, factor_ref, projected_ref, core_ref):
     rank = factor_ref.shape[0]
-    width = mine_ref.shape[1]
+    width = core_ref.shape[1]
     odd = lax.rem(lax.axis_index("row"), 2)
-
-    def columns(start):
-        where = pl.ds(pl.multiple_of(start, width), width)
-        return (own_ref[:, where].astype(F32) + got_ref[:, where].astype(F32)).astype(BF16)
-
-    mine = columns(odd * width)
-    give = columns((1 - odd) * width)
-    mine_ref[...] = mine
-    give_ref[...] = give
-    keep = dot_f32(factor_ref[...], mine, ((1,), (0,)))
-    send = dot_f32(factor_ref[...], give, ((1,), (0,)))
+    start = odd * width if kept else (1 - odd) * width
+    where = pl.ds(pl.multiple_of(start, width), width)
+    core = (own_ref[:, where].astype(F32) + got_ref[:, where].astype(F32)).astype(BF16)
+    core_ref[...] = core
+    projected = dot_f32(factor_ref[...], core, ((1,), (0,)))
     for block in range(width // LANES):
-        where = slice(block * LANES, (block + 1) * LANES)
-        rows = pl.ds(block * rank, rank)
-        keep_ref[rows, :] = keep[:, where]
-        send_ref[rows, :] = send[:, where].astype(BF16)
-
-
-def project(own, got, factor_t):
+        part = projected[:, block * LANES:(block + 1) * LANES]
+        projected_ref[pl.ds(block * rank, rank), :] = part.astype(projected_ref.dtype)
+
+
+def project(own, got, factor_t, kept):
     cells, width = own.shape
     rows = factor_t.shape[0] * width // LANES // 2
-    columns = jax.ShapeDtypeStruct((cells, width // 2), BF16)
-    return pl.pallas_call(
-        project_kernel,
+    return pl.pallas_call(
+        functools.partial(project_kernel, kept),
         out_shape=[
-            jax.ShapeDtypeStruct((rows, LANES), F32),
-            jax.ShapeDtypeStruct((rows, LANES), BF16),
-            columns,
-            columns,
+            jax.ShapeDtypeStruct((rows, LANES), F32 if kept else BF16),
+            jax.ShapeDtypeStruct((cells, width // 2), BF16),
         ],
         compiler_params=params(8),
-        name="project",
+        name="project_kept" if kept else "project_sent",
     )(own, got, factor_t)
 
 
@@ -372,7 +360,8 @@
     got = swap(send, 0)
     own = contract_own(kept, wide, order)
 
-    keep, send, columns, give = project(own, got, old_factor.T)
+    send, give = project(own, got, old_factor.T, False)
+    keep, columns = project(own, got, old_factor.T, True)
     mine = add(keep, swap(send, masks[0]))
     got_columns = swap(give, masks[0])
     others = masks[1:]

time: 37.3 us -> 37.9 us (1.016)
  Pallas kernels: 10.3 us -> 10.9 us
    pallas_call x1, Pallas kernels: 5.08 us -> 5.54 us  [contract_send(): pl.pallas_call(send_kernel, in_specs=[pinned, pinned], out_shape=[jax.Sha...]
where the time goes in v26:
time: 37.9 us; the launch traced here: 37.5 us
  starting transfers between devices  14.5 us (38%)
  waiting for transfers between devices  12 us (32%)
  Pallas kernels  10.9 us (29%)
    ppermute x10, starting transfers between devices, swap(): return lax.ppermute(x, ('row', 'col'), pairs)  14.5 us
    ppermute x10, waiting for transfers between devices, swap(): return lax.ppermute(x, ('row', 'col'), pairs)  12 us
    pallas_call x1, Pallas kernels, contract_send(): pl.pallas_call(send_kernel, in_specs=[pinned, pinned], out_shape=[jax.Sha...  5.54 us
    pallas_call x1, Pallas kernels, finish(): pl.pallas_call(functools.partial(finish_kernel, total_rows), out_shape=ja...  2.69 us
    pallas_call x1, Pallas kernels, contract_own(): pl.pallas_call(own_kernel, out_shape=jax.ShapeDtypeStruct((cells, half //...  1.77 us
  transfers between devices with their start and end apart: 10, of which 8 were waited for; matrix products, arithmetic and copies ran while one was open for 0% of the time, Pallas kernels for 5%

profile of v26, /device:TPU:0, one launch (start us, length us, event | category | flops | bytes accessed | tf_op | source)
XLA Modules:
  0.0 37.5 jit_solution(5490934416922381621)
XLA Ops:
  0.0 0.0 copy-start
  0.0 5.5 %contract_send.1 = (bf16[128,1024]{1,0:T(8,128)(2,1)S(1)}, bf16[128,16,1024]{2,1,0:T(8,128)(2,1)S(1)}, bf16[128,1024]{1,0:T(8,128)(2,1)S(1)}, bf16[64,256]{1,0:T(8,128)(2,1)S(1)}) custom-call(bf16[128,32,1024]{2,1,0:T(8,128)(2,1)} %snapshot_ref.1, bf16[64,1024]{1,0:T(8,128)(2,1)} %bitcast.4), custom_call_target="tpu_custom_call" | custom-call | tf_op jit(solution)/shard_map/contract_send/pallas_call | solution.py:127
  5.5 0.5 %collective-permute-start = (bf16[128,1024]{1,0:T(8,128)(2,1)S(1)}, bf16[128,1024]{1,0:T(8,128)(2,1)S(1)}, u32[]{:S(2)}, u32[]{:S(2)}) collective-permute-start(bf16[128,1024]{1,0:T(8,128)(2,1)S(1)} %get-tuple-element.16), channel_id=1, source_target_pairs={{0,1},{1,0},{2,3},{3,2},{4,5},{5,4},{6,7},{7,6},{8,9},{9,8},{10,11... | collective-permute-start | bytes 786440 | tf_op jit(solution)/shard_map/ppermute | solution.py:355
  6.1 1.8 %contract_own.1.own_ref = bf16[128,1024]{1,0:T(8,128)(2,1)S(1)} custom-call(bf16[128,16,1024]{2,1,0:T(8,128)(2,1)S(1)} %get-tuple-element.13.slab_ref, bf16[128,1024]{1,0:T(8,128)(2,1)S(1)} %get-tuple-element.14.wide_ref, bf16[64,256]{1,0:T(8,128)(2,1)S(1)} %get-tuple-element.15.order_ref), custom_call_target="tpu_custom_call" | custom-call | tf_op jit(solution)/shard_map/contract_own/pallas_call | solution.py:164
  7.8 0.0 collective-permute-done.got_ref
  7.9 0.0 copy-done
  7.9 0.2 project_sent.1
  8.1 2.7 %collective-permute-start.2 = (bf16[256,128]{1,0:T(8,128)(2,1)S(1)}, bf16[256,128]{1,0:T(8,128)(2,1)S(1)}, u32[]{:S(2)}, u32[]{:S(2)}) collective-permute-start(bf16[256,128]{1,0:T(8,128)(2,1)S(1)} %get-tuple-element.20), channel_id=1, source_target_pairs={{0,3},{1,2},{2,1},{3,0},{4,7},{5,6},{6,5},{7,4},{8,11},{9,10},{10,... | collective-permute-start | bytes 196616 | tf_op jit(solution)/shard_map/ppermute | solution.py:355
  10.7 0.2 project_kept.1
  10.9 2.3 %collective-permute-done.2.got_ref = bf16[256,128]{1,0:T(8,128)(2,1)S(1)} collective-permute-done((bf16[256,128]{1,0:T(8,128)(2,1)S(1)}, bf16[256,128]{1,0:T(8,128)(2,1)S(1)}, u32[]{:S(2)}, u32[]{:S(2)}) %collective-permute-start.2) | collective-permute-done | bytes 65568 | tf_op jit(solution)/shard_map/ppermute | solution.py:355
  13.2 1.4 %collective-permute-start.3 = (bf16[256,128]{1,0:T(8,128)(2,1)S(1)}, bf16[256,128]{1,0:T(8,128)(2,1)S(1)}, u32[]{:S(2)}, u32[]{:S(2)}) collective-permute-start(bf16[256,128]{1,0:T(8,128)(2,1)S(1)} %add.4.mine_ref), channel_id=1, source_target_pairs={{0,5},{1,8},{2,11},{3,6},{4,13},{5,0},{6,3},{7,14},{8,1},{9,12},{1... | collective-permute-start | bytes 196616 | tf_op jit(solution)/shard_map/ppermute | solution.py:355
  14.6 1.2 %collective-permute-start.1 = (bf16[128,512]{1,0:T(8,128)(2,1)S(1)}, bf16[128,512]{1,0:T(8,128)(2,1)S(1)}, u32[]{:S(2)}, u32[]{:S(2)}) collective-permute-start(bf16[128,512]{1,0:T(8,128)(2,1)S(1)} %get-tuple-element.18), channel_id=1, source_target_pairs={{0,3},{1,2},{2,1},{3,0},{4,7},{5,6},{6,5},{7,4},{8,11},{9,10},{10,... | collective-permute-start | bytes 393224 | tf_op jit(solution)/shard_map/ppermute | solution.py:355
  15.8 1.2 %collective-permute-done.3.got_ref = bf16[256,128]{1,0:T(8,128)(2,1)S(1)} collective-permute-done((bf16[256,128]{1,0:T(8,128)(2,1)S(1)}, bf16[256,128]{1,0:T(8,128)(2,1)S(1)}, u32[]{:S(2)}, u32[]{:S(2)}) %collective-permute-start.3) | collective-permute-done | bytes 65568 | tf_op jit(solution)/shard_map/ppermute | solution.py:355
  17.0 2.7 %collective-permute-start.4 = (bf16[256,128]{1,0:T(8,128)(2,1)S(1)}, bf16[256,128]{1,0:T(8,128)(2,1)S(1)}, u32[]{:S(2)}, u32[]{:S(2)}) collective-permute-start(bf16[256,128]{1,0:T(8,128)(2,1)S(1)} %add.5.mine_ref), channel_id=1, source_target_pairs={{0,9},{1,4},{2,7},{3,10},{4,1},{5,12},{6,15},{7,2},{8,13},{9,0},{1... | collective-permute-start | bytes 196616 | tf_op jit(solution)/shard_map/ppermute | solution.py:355
  19.7 0.0 collective-permute-done.1.refs_0_.got_ref
  19.7 2.0 %collective-permute-done.4.got_ref = bf16[256,128]{1,0:T(8,128)(2,1)S(1)} collective-permute-done((bf16[256,128]{1,0:T(8,128)(2,1)S(1)}, bf16[256,128]{1,0:T(8,128)(2,1)S(1)}, u32[]{:S(2)}, u32[]{:S(2)}) %collective-permute-start.4) | collective-permute-done | bytes 65568 | tf_op jit(solution)/shard_map/ppermute | solution.py:355
  21.7 0.2 product_terms.1.mine_ref
  21.9 0.9 %collective-permute-start.5 = (bf16[128,128]{1,0:T(8,128)(2,1)S(1)}, bf16[128,128]{1,0:T(8,128)(2,1)S(1)}, u32[]{:S(2)}, u32[]{:S(2)}) collective-permute-start(bf16[128,128]{1,0:T(8,128)(2,1)S(1)} %product_terms.1.mine_ref), channel_id=1, source_target_pairs={{0,1},{1,0},{2,3},{3,2},{4,5},{5,4},{6,7},{7,6},{8,9},{9,8},{10,11... | collective-permute-start | bytes 98312 | tf_op jit(solution)/shard_map/ppermute | solution.py:355
  22.8 0.9 %collective-permute-done.5.got_ref = bf16[128,128]{1,0:T(8,128)(2,1)S(1)} collective-permute-done((bf16[128,128]{1,0:T(8,128)(2,1)S(1)}, bf16[128,128]{1,0:T(8,128)(2,1)S(1)}, u32[]{:S(2)}, u32[]{:S(2)}) %collective-permute-start.5) | collective-permute-done | bytes 32800 | tf_op jit(solution)/shard_map/ppermute | solution.py:355
  23.6 2.6 %collective-permute-start.8 = (bf16[128,128]{1,0:T(8,128)(2,1)S(1)}, bf16[128,128]{1,0:T(8,128)(2,1)S(1)}, u32[]{:S(2)}, u32[]{:S(2)}) collective-permute-start(bf16[128,128]{1,0:T(8,128)(2,1)S(1)} %add.7.refs_0_.term_ref), channel_id=1, source_target_pairs={{0,7},{1,6},{2,5},{3,4},{4,3},{5,2},{6,1},{7,0},{8,15},{9,14},{10,... | collective-permute-start | bytes 98312 | tf_op jit(solution)/shard_map/ppermute | solution.py:355
  26.2 0.9 %collective-permute-start.7 = (bf16[128,128]{1,0:T(8,128)(2,1)S(1)}, bf16[128,128]{1,0:T(8,128)(2,1)S(1)}, u32[]{:S(2)}, u32[]{:S(2)}) collective-permute-start(bf16[128,128]{1,0:T(8,128)(2,1)S(1)} %add.7.refs_0_.term_ref), channel_id=1, source_target_pairs={{0,5},{1,4},{2,7},{3,6},{4,1},{5,0},{6,3},{7,2},{8,13},{9,12},{10,... | collective-permute-start | bytes 98312 | tf_op jit(solution)/shard_map/ppermute | solution.py:355
  27.1 0.0 collective-permute-start.6
  27.1 0.8 %collective-permute-done.8.refs_3_ = bf16[128,128]{1,0:T(8,128)(2,1)S(1)} collective-permute-done((bf16[128,128]{1,0:T(8,128)(2,1)S(1)}, bf16[128,128]{1,0:T(8,128)(2,1)S(1)}, u32[]{:S(2)}, u32[]{:S(2)}) %collective-permute-start.8) | collective-permute-done | bytes 32800 | tf_op jit(solution)/shard_map/ppermute | solution.py:355
  27.9 1.7 %collective-permute-done.7.refs_2_ = bf16[128,128]{1,0:T(8,128)(2,1)S(1)} collective-permute-done((bf16[128,128]{1,0:T(8,128)(2,1)S(1)}, bf16[128,128]{1,0:T(8,128)(2,1)S(1)}, u32[]{:S(2)}, u32[]{:S(2)}) %collective-permute-start.7) | collective-permute-done | bytes 32800 | tf_op jit(solution)/shard_map/ppermute | solution.py:355
  29.6 0.9 %collective-permute-done.6.refs_1_.got_term_ref = bf16[128,128]{1,0:T(8,128)(2,1)S(1)} collective-permute-done((bf16[128,128]{1,0:T(8,128)(2,1)S(1)}, bf16[128,128]{1,0:T(8,128)(2,1)S(1)}, u32[]{:S(2)}, u32[]{:S(2)}) %collective-permute-start.6) | collective-permute-done | bytes 32800 | tf_op jit(solution)/shard_map/ppermute | solution.py:355
  30.5 0.3 local_gram.1.gram_ref
  30.7 1.7 %collective-permute-start.9 = (f32[32,128]{1,0:T(8,128)S(1)}, f32[32,128]{1,0:T(8,128)S(1)}, u32[]{:S(2)}, u32[]{:S(2)}) collective-permute-start(f32[32,128]{1,0:T(8,128)S(1)} %local_gram.1.gram_ref), channel_id=1, source_target_pairs={{0,9},{1,8},{2,11},{3,10},{4,13},{5,12},{6,15},{7,14},{8,1},{9,0},... | collective-permute-start | bytes 49160 | tf_op jit(solution)/shard_map/ppermute | solution.py:355
  32.4 2.4 %collective-permute-done.9.got_gram_ref = f32[32,128]{1,0:T(8,128)S(1)} collective-permute-done((f32[32,128]{1,0:T(8,128)S(1)}, f32[32,128]{1,0:T(8,128)S(1)}, u32[]{:S(2)}, u32[]{:S(2)}) %collective-permute-start.9) | collective-permute-done | bytes 16416 | tf_op jit(solution)/shard_map/ppermute | solution.py:355
  34.8 2.7 %finish.1 = f32[64,64]{1,0:T(8,128)} custom-call(bf16[128,128]{1,0:T(8,128)(2,1)S(1)} %add.7.refs_0_.term_ref, bf16[128,128]{1,0:T(8,128)(2,1)S(1)} %collective-permute-done.6.refs_1_.got_term_ref, f32[32,128]{1,0:T(8,128)S(1)} %local_gram.1.gram_ref, f32[32,128]{1,0:T(8,128)S(1)} %collective-permute-done.9.got_gram_ref), custom_call_target="tpu_custom_call" | custom-call | tf_op jit(solution)/shard_map/finish/pallas_call | solution.py:335
  (4 shorter events, 0.1 us)
Async XLA Ops:
  0.0 7.9 %copy-start = (bf16[128,64]{0,1:T(8,128)(2,1)S(1)}, bf16[128,64]{0,1:T(8,128)(2,1)}, u32[]{:S(2)}) copy-start(bf16[128,64]{0,1:T(8,128)(2,1)} %param.5) | copy-start | bytes 49156
  5.5 2.3 %collective-permute-start = (bf16[128,1024]{1,0:T(8,128)(2,1)S(1)}, bf16[128,1024]{1,0:T(8,128)(2,1)S(1)}, u32[]{:S(2)}, u32[]{:S(2)}) collective-permute-start(bf16[128,1024]{1,0:T(8,128)(2,1)S(1)} %get-tuple-element.16), channel_id=1, source_target_pairs={{0,1},{1,0},{2,3},{3,2},{4,5},{5,4},{6,7},{7,6},{8,9},{9,8},{10,11... | collective-permute-start | bytes 786440 | tf_op jit(solution)/shard_map/ppermute | solution.py:355
  8.1 5.1 %collective-permute-start.2 = (bf16[256,128]{1,0:T(8,128)(2,1)S(1)}, bf16[256,128]{1,0:T(8,128)(2,1)S(1)}, u32[]{:S(2)}, u32[]{:S(2)}) collective-permute-start(bf16[256,128]{1,0:T(8,128)(2,1)S(1)} %get-tuple-element.20), channel_id=1, source_target_pairs={{0,3},{1,2},{2,1},{3,0},{4,7},{5,6},{6,5},{7,4},{8,11},{9,10},{10,... | collective-permute-start | bytes 196616 | tf_op jit(solution)/shard_map/ppermute | solution.py:355
  13.2 3.8 %collective-permute-start.3 = (bf16[256,128]{1,0:T(8,128)(2,1)S(1)}, bf16[256,128]{1,0:T(8,128)(2,1)S(1)}, u32[]{:S(2)}, u32[]{:S(2)}) collective-permute-start(bf16[256,128]{1,0:T(8,128)(2,1)S(1)} %add.4.mine_ref), channel_id=1, source_target_pairs={{0,5},{1,8},{2,11},{3,6},{4,13},{5,0},{6,3},{7,14},{8,1},{9,12},{1... | collective-permute-start | bytes 196616 | tf_op jit(solution)/shard_map/ppermute | solution.py:355
  14.6 5.1 %collective-permute-start.1 = (bf16[128,512]{1,0:T(8,128)(2,1)S(1)}, bf16[128,512]{1,0:T(8,128)(2,1)S(1)}, u32[]{:S(2)}, u32[]{:S(2)}) collective-permute-start(bf16[128,512]{1,0:T(8,128)(2,1)S(1)} %get-tuple-element.18), channel_id=1, source_target_pairs={{0,3},{1,2},{2,1},{3,0},{4,7},{5,6},{6,5},{7,4},{8,11},{9,10},{10,... | collective-permute-start | bytes 393224 | tf_op jit(solution)/shard_map/ppermute | solution.py:355
  17.0 4.7 %collective-permute-start.4 = (bf16[256,128]{1,0:T(8,128)(2,1)S(1)}, bf16[256,128]{1,0:T(8,128)(2,1)S(1)}, u32[]{:S(2)}, u32[]{:S(2)}) collective-permute-start(bf16[256,128]{1,0:T(8,128)(2,1)S(1)} %add.5.mine_ref), channel_id=1, source_target_pairs={{0,9},{1,4},{2,7},{3,10},{4,1},{5,12},{6,15},{7,2},{8,13},{9,0},{1... | collective-permute-start | bytes 196616 | tf_op jit(solution)/shard_map/ppermute | solution.py:355
  21.9 1.7 %collective-permute-start.5 = (bf16[128,128]{1,0:T(8,128)(2,1)S(1)}, bf16[128,128]{1,0:T(8,128)(2,1)S(1)}, u32[]{:S(2)}, u32[]{:S(2)}) collective-permute-start(bf16[128,128]{1,0:T(8,128)(2,1)S(1)} %product_terms.1.mine_ref), channel_id=1, source_target_pairs={{0,1},{1,0},{2,3},{3,2},{4,5},{5,4},{6,7},{7,6},{8,9},{9,8},{10,11... | collective-permute-start | bytes 98312 | tf_op jit(solution)/shard_map/ppermute | solution.py:355
  23.6 4.3 %collective-permute-start.8 = (bf16[128,128]{1,0:T(8,128)(2,1)S(1)}, bf16[128,128]{1,0:T(8,128)(2,1)S(1)}, u32[]{:S(2)}, u32[]{:S(2)}) collective-permute-start(bf16[128,128]{1,0:T(8,128)(2,1)S(1)} %add.7.refs_0_.term_ref), channel_id=1, source_target_pairs={{0,7},{1,6},{2,5},{3,4},{4,3},{5,2},{6,1},{7,0},{8,15},{9,14},{10,... | collective-permute-start | bytes 98312 | tf_op jit(solution)/shard_map/ppermute | solution.py:355
  26.2 3.4 %collective-permute-start.7 = (bf16[128,128]{1,0:T(8,128)(2,1)S(1)}, bf16[128,128]{1,0:T(8,128)(2,1)S(1)}, u32[]{:S(2)}, u32[]{:S(2)}) collective-permute-start(bf16[128,128]{1,0:T(8,128)(2,1)S(1)} %add.7.refs_0_.term_ref), channel_id=1, source_target_pairs={{0,5},{1,4},{2,7},{3,6},{4,1},{5,0},{6,3},{7,2},{8,13},{9,12},{10,... | collective-permute-start | bytes 98312 | tf_op jit(solution)/shard_map/ppermute | solution.py:355
  27.1 3.3 %collective-permute-start.6 = (bf16[128,128]{1,0:T(8,128)(2,1)S(1)}, bf16[128,128]{1,0:T(8,128)(2,1)S(1)}, u32[]{:S(2)}, u32[]{:S(2)}) collective-permute-start(bf16[128,128]{1,0:T(8,128)(2,1)S(1)} %add.7.refs_0_.term_ref), channel_id=1, source_target_pairs={{0,3},{1,2},{2,1},{3,0},{4,7},{5,6},{6,5},{7,4},{8,11},{9,10},{10,... | collective-permute-start | bytes 98312 | tf_op jit(solution)/shard_map/ppermute | solution.py:355
  30.7 4.1 %collective-permute-start.9 = (f32[32,128]{1,0:T(8,128)S(1)}, f32[32,128]{1,0:T(8,128)S(1)}, u32[]{:S(2)}, u32[]{:S(2)}) collective-permute-start(f32[32,128]{1,0:T(8,128)S(1)} %local_gram.1.gram_ref), channel_id=1, source_target_pairs={{0,9},{1,8},{2,11},{3,10},{4,13},{5,12},{6,15},{7,14},{8,1},{9,0},... | collective-permute-start | bytes 49160 | tf_op jit(solution)/shard_map/ppermute | solution.py:355

commit v27 on v25

--- a/solution.py
+++ b/solution.py
@@ -21,12 +21,18 @@
     return pltpu.CompilerParams(vmem_limit_bytes=mib * MIB)
 
 
+def row_masks(n_rows):
+    masks = [1 << bit for bit in range(n_rows.bit_length() - 1)]
+    return masks[:-1] + [masks[-1] | masks[-2]]
+
+
+def half_of(row, col, n_rows):
+    bits = n_rows.bit_length() - 2
+    return (col + sum((row // (1 << bit)) % 2 for bit in range(bits))) % 2
+
+
 def own_half():
-    row = lax.axis_index("row")
-    half = lax.axis_index("col")
-    for bit in range(lax.axis_size("row").bit_length() - 1):
-        half += lax.rem(lax.div(row, 1 << bit), 2)
-    return lax.rem(half, 2)
+    return half_of(lax.axis_index("row"), lax.axis_index("col"), lax.axis_size("row"))
 
 
 TILE = 8
@@ -354,14 +360,14 @@
 
 def per_device(snapshot, mode2_factor, old_factor):
     n_rows, n_cols = lax.axis_size("row"), lax.axis_size("col")
-    masks = [1 << bit for bit in range(n_rows.bit_length() - 1)]
+    masks = row_masks(n_rows)
     total_rows = snapshot.shape[0] * n_rows
 
     def swap(x, mask, other=None):
         pairs = []
         for r in range(n_rows):
             for c in range(n_cols):
-                second = (c + r.bit_count()) % 2 and other is not None
+                second = half_of(r, c, n_rows) and other is not None
                 to = r ^ (other if second else mask)
                 pairs.append((r * n_cols + c, to * n_cols + (c + 1) % n_cols))
         return lax.ppermute(x, ("row", "col"), pairs)

time: 37.3 us -> 37.7 us (1.011)
  starting transfers between devices: 14.5 us -> 16.3 us
  Pallas kernels: 10.3 us -> 9.54 us
  waiting for transfers between devices: 12.2 us -> 11.7 us
    ppermute x10, starting transfers between devices: 14.5 us -> 16.3 us  [swap(): return lax.ppermute(x, ('row', 'col'), pairs)]
    pallas_call x1, Pallas kernels: 5.08 us -> 4.31 us  [contract_send(): pl.pallas_call(send_kernel, in_specs=[pinned, pinned], out_shape=[jax.Sha...]
    ppermute x10, waiting for transfers between devices: 12.2 us -> 11.7 us  [swap(): return lax.ppermute(x, ('row', 'col'), pairs)]
where the time goes in v27:
time: 37.7 us; the launch traced here: 37.6 us
  starting transfers between devices  16.3 us (43%)
  waiting for transfers between devices  11.7 us (31%)
  Pallas kernels  9.54 us (25%)
    ppermute x10, starting transfers between devices, swap(): return lax.ppermute(x, ('row', 'col'), pairs)  16.3 us
    ppermute x10, waiting for transfers between devices, swap(): return lax.ppermute(x, ('row', 'col'), pairs)  11.7 us
    pallas_call x1, Pallas kernels, contract_send(): pl.pallas_call(send_kernel, in_specs=[pinned, pinned], out_shape=[jax.Sha...  4.31 us
    pallas_call x1, Pallas kernels, finish(): pl.pallas_call(functools.partial(finish_kernel, total_rows), out_shape=ja...  2.69 us
    pallas_call x1, Pallas kernels, contract_own(): pl.pallas_call(own_kernel, out_shape=jax.ShapeDtypeStruct((cells, half //...  1.77 us
  transfers between devices with their start and end apart: 10, of which 8 were waited for; matrix products, arithmetic and copies ran while one was open for 0% of the time, Pallas kernels for 5%

profile of v27, /device:TPU:0, one launch (start us, length us, event | category | flops | bytes accessed | tf_op | source)
XLA Modules:
  0.0 37.6 jit_solution(5796344066049388503)
XLA Ops:
  0.0 0.0 copy-start
  0.0 4.3 %contract_send.1 = (bf16[128,1024]{1,0:T(8,128)(2,1)S(1)}, bf16[128,16,1024]{2,1,0:T(8,128)(2,1)S(1)}, bf16[128,1024]{1,0:T(8,128)(2,1)S(1)}, bf16[64,256]{1,0:T(8,128)(2,1)S(1)}) custom-call(bf16[128,32,1024]{2,1,0:T(8,128)(2,1)} %snapshot_ref.1, bf16[64,1024]{1,0:T(8,128)(2,1)} %bitcast.3), custom_call_target="tpu_custom_call" | custom-call | tf_op jit(solution)/shard_map/contract_send/pallas_call | solution.py:134
  4.3 0.5 %collective-permute-start = (bf16[128,1024]{1,0:T(8,128)(2,1)S(1)}, bf16[128,1024]{1,0:T(8,128)(2,1)S(1)}, u32[]{:S(2)}, u32[]{:S(2)}) collective-permute-start(bf16[128,1024]{1,0:T(8,128)(2,1)S(1)} %get-tuple-element.16), channel_id=1, source_target_pairs={{0,1},{1,0},{2,3},{3,2},{4,5},{5,4},{6,7},{7,6},{8,9},{9,8},{10,11... | collective-permute-start | bytes 786440 | tf_op jit(solution)/shard_map/ppermute | solution.py:373
  4.8 1.8 %contract_own.1.own_ref = bf16[128,1024]{1,0:T(8,128)(2,1)S(1)} custom-call(bf16[128,16,1024]{2,1,0:T(8,128)(2,1)S(1)} %get-tuple-element.13.slab_ref, bf16[128,1024]{1,0:T(8,128)(2,1)S(1)} %get-tuple-element.14.wide_ref, bf16[64,256]{1,0:T(8,128)(2,1)S(1)} %get-tuple-element.15.order_ref), custom_call_target="tpu_custom_call" | custom-call | tf_op jit(solution)/shard_map/contract_own/pallas_call | solution.py:171
  6.6 0.0 collective-permute-done.got_ref
  6.6 0.0 copy-done
  6.6 0.2 project.1
  6.9 2.7 %collective-permute-start.2 = (bf16[256,128]{1,0:T(8,128)(2,1)S(1)}, bf16[256,128]{1,0:T(8,128)(2,1)S(1)}, u32[]{:S(2)}, u32[]{:S(2)}) collective-permute-start(bf16[256,128]{1,0:T(8,128)(2,1)S(1)} %get-tuple-element.20), channel_id=1, source_target_pairs={{0,3},{1,2},{2,1},{3,0},{4,7},{5,6},{6,5},{7,4},{8,11},{9,10},{10,... | collective-permute-start | bytes 196616 | tf_op jit(solution)/shard_map/ppermute | solution.py:373
  9.6 2.5 %collective-permute-done.2.got_ref = bf16[256,128]{1,0:T(8,128)(2,1)S(1)} collective-permute-done((bf16[256,128]{1,0:T(8,128)(2,1)S(1)}, bf16[256,128]{1,0:T(8,128)(2,1)S(1)}, u32[]{:S(2)}, u32[]{:S(2)}) %collective-permute-start.2) | collective-permute-done | bytes 65568 | tf_op jit(solution)/shard_map/ppermute | solution.py:373
  12.0 1.4 %collective-permute-start.3 = (bf16[256,128]{1,0:T(8,128)(2,1)S(1)}, bf16[256,128]{1,0:T(8,128)(2,1)S(1)}, u32[]{:S(2)}, u32[]{:S(2)}) collective-permute-start(bf16[256,128]{1,0:T(8,128)(2,1)S(1)} %add.4.mine_ref), channel_id=1, source_target_pairs={{0,5},{1,12},{2,15},{3,6},{4,9},{5,0},{6,3},{7,10},{8,13},{9,4},{1... | collective-permute-start | bytes 196616 | tf_op jit(solution)/shard_map/ppermute | solution.py:373
  13.4 1.2 %collective-permute-start.1 = (bf16[128,512]{1,0:T(8,128)(2,1)S(1)}, bf16[128,512]{1,0:T(8,128)(2,1)S(1)}, u32[]{:S(2)}, u32[]{:S(2)}) collective-permute-start(bf16[128,512]{1,0:T(8,128)(2,1)S(1)} %get-tuple-element.18), channel_id=1, source_target_pairs={{0,3},{1,2},{2,1},{3,0},{4,7},{5,6},{6,5},{7,4},{8,11},{9,10},{10,... | collective-permute-start | bytes 393224 | tf_op jit(solution)/shard_map/ppermute | solution.py:373
  14.6 1.2 %collective-permute-done.3.got_ref = bf16[256,128]{1,0:T(8,128)(2,1)S(1)} collective-permute-done((bf16[256,128]{1,0:T(8,128)(2,1)S(1)}, bf16[256,128]{1,0:T(8,128)(2,1)S(1)}, u32[]{:S(2)}, u32[]{:S(2)}) %collective-permute-start.3) | collective-permute-done | bytes 65568 | tf_op jit(solution)/shard_map/ppermute | solution.py:373
  15.8 3.7 %collective-permute-start.4 = (bf16[256,128]{1,0:T(8,128)(2,1)S(1)}, bf16[256,128]{1,0:T(8,128)(2,1)S(1)}, u32[]{:S(2)}, u32[]{:S(2)}) collective-permute-start(bf16[256,128]{1,0:T(8,128)(2,1)S(1)} %add.5.mine_ref), channel_id=1, source_target_pairs={{0,13},{1,4},{2,7},{3,14},{4,1},{5,8},{6,11},{7,2},{8,5},{9,12},{1... | collective-permute-start | bytes 196616 | tf_op jit(solution)/shard_map/ppermute | solution.py:373
  19.5 0.0 collective-permute-done.1.refs_0_.got_ref
  19.5 2.1 %collective-permute-done.4.got_ref = bf16[256,128]{1,0:T(8,128)(2,1)S(1)} collective-permute-done((bf16[256,128]{1,0:T(8,128)(2,1)S(1)}, bf16[256,128]{1,0:T(8,128)(2,1)S(1)}, u32[]{:S(2)}, u32[]{:S(2)}) %collective-permute-start.4) | collective-permute-done | bytes 65568 | tf_op jit(solution)/shard_map/ppermute | solution.py:373
  21.6 0.2 product_terms.1.mine_ref
  21.8 0.6 %collective-permute-start.5 = (bf16[128,128]{1,0:T(8,128)(2,1)S(1)}, bf16[128,128]{1,0:T(8,128)(2,1)S(1)}, u32[]{:S(2)}, u32[]{:S(2)}) collective-permute-start(bf16[128,128]{1,0:T(8,128)(2,1)S(1)} %product_terms.1.mine_ref), channel_id=1, source_target_pairs={{0,1},{1,0},{2,3},{3,2},{4,5},{5,4},{6,7},{7,6},{8,9},{9,8},{10,11... | collective-permute-start | bytes 98312 | tf_op jit(solution)/shard_map/ppermute | solution.py:373
  22.4 0.9 %collective-permute-done.5.got_ref = bf16[128,128]{1,0:T(8,128)(2,1)S(1)} collective-permute-done((bf16[128,128]{1,0:T(8,128)(2,1)S(1)}, bf16[128,128]{1,0:T(8,128)(2,1)S(1)}, u32[]{:S(2)}, u32[]{:S(2)}) %collective-permute-start.5) | collective-permute-done | bytes 32800 | tf_op jit(solution)/shard_map/ppermute | solution.py:373
  23.3 1.3 %collective-permute-start.8 = (bf16[128,128]{1,0:T(8,128)(2,1)S(1)}, bf16[128,128]{1,0:T(8,128)(2,1)S(1)}, u32[]{:S(2)}, u32[]{:S(2)}) collective-permute-start(bf16[128,128]{1,0:T(8,128)(2,1)S(1)} %add.7.refs_0_.term_ref), channel_id=1, source_target_pairs={{0,7},{1,6},{2,5},{3,4},{4,3},{5,2},{6,1},{7,0},{8,15},{9,14},{10,... | collective-permute-start | bytes 98312 | tf_op jit(solution)/shard_map/ppermute | solution.py:373
  24.6 1.7 %collective-permute-start.7 = (bf16[128,128]{1,0:T(8,128)(2,1)S(1)}, bf16[128,128]{1,0:T(8,128)(2,1)S(1)}, u32[]{:S(2)}, u32[]{:S(2)}) collective-permute-start(bf16[128,128]{1,0:T(8,128)(2,1)S(1)} %add.7.refs_0_.term_ref), channel_id=1, source_target_pairs={{0,5},{1,4},{2,7},{3,6},{4,1},{5,0},{6,3},{7,2},{8,13},{9,12},{10,... | collective-permute-start | bytes 98312 | tf_op jit(solution)/shard_map/ppermute | solution.py:373
  26.3 0.2 collective-permute-start.6
  26.5 1.1 %collective-permute-done.8.refs_3_ = bf16[128,128]{1,0:T(8,128)(2,1)S(1)} collective-permute-done((bf16[128,128]{1,0:T(8,128)(2,1)S(1)}, bf16[128,128]{1,0:T(8,128)(2,1)S(1)}, u32[]{:S(2)}, u32[]{:S(2)}) %collective-permute-start.8) | collective-permute-done | bytes 32800 | tf_op jit(solution)/shard_map/ppermute | solution.py:373
  27.6 1.0 %collective-permute-done.7.refs_2_ = bf16[128,128]{1,0:T(8,128)(2,1)S(1)} collective-permute-done((bf16[128,128]{1,0:T(8,128)(2,1)S(1)}, bf16[128,128]{1,0:T(8,128)(2,1)S(1)}, u32[]{:S(2)}, u32[]{:S(2)}) %collective-permute-start.7) | collective-permute-done | bytes 32800 | tf_op jit(solution)/shard_map/ppermute | solution.py:373
  28.6 1.0 %collective-permute-done.6.refs_1_.got_term_ref = bf16[128,128]{1,0:T(8,128)(2,1)S(1)} collective-permute-done((bf16[128,128]{1,0:T(8,128)(2,1)S(1)}, bf16[128,128]{1,0:T(8,128)(2,1)S(1)}, u32[]{:S(2)}, u32[]{:S(2)}) %collective-permute-start.6) | collective-permute-done | bytes 32800 | tf_op jit(solution)/shard_map/ppermute | solution.py:373
  29.6 0.3 local_gram.1.gram_ref
  29.9 3.0 %collective-permute-start.9 = (f32[32,128]{1,0:T(8,128)S(1)}, f32[32,128]{1,0:T(8,128)S(1)}, u32[]{:S(2)}, u32[]{:S(2)}) collective-permute-start(f32[32,128]{1,0:T(8,128)S(1)} %local_gram.1.gram_ref), channel_id=1, source_target_pairs={{0,13},{1,12},{2,15},{3,14},{4,9},{5,8},{6,11},{7,10},{8,5},{9,4},... | collective-permute-start | bytes 49160 | tf_op jit(solution)/shard_map/ppermute | solution.py:373
  32.9 2.0 %collective-permute-done.9.got_gram_ref = f32[32,128]{1,0:T(8,128)S(1)} collective-permute-done((f32[32,128]{1,0:T(8,128)S(1)}, f32[32,128]{1,0:T(8,128)S(1)}, u32[]{:S(2)}, u32[]{:S(2)}) %collective-permute-start.9) | collective-permute-done | bytes 16416 | tf_op jit(solution)/shard_map/ppermute | solution.py:373
  34.9 2.7 %finish.1 = f32[64,64]{1,0:T(8,128)} custom-call(bf16[128,128]{1,0:T(8,128)(2,1)S(1)} %add.7.refs_0_.term_ref, bf16[128,128]{1,0:T(8,128)(2,1)S(1)} %collective-permute-done.6.refs_1_.got_term_ref, f32[32,128]{1,0:T(8,128)S(1)} %local_gram.1.gram_ref, f32[32,128]{1,0:T(8,128)S(1)} %collective-permute-done.9.got_gram_ref), custom_call_target="tpu_custom_call" | custom-call | tf_op jit(solution)/shard_map/finish/pallas_call | solution.py:353
  (4 shorter events, 0.1 us)
Async XLA Ops:
  0.0 6.6 %copy-start = (bf16[128,64]{0,1:T(8,128)(2,1)S(1)}, bf16[128,64]{0,1:T(8,128)(2,1)}, u32[]{:S(2)}) copy-start(bf16[128,64]{0,1:T(8,128)(2,1)} %param.5) | copy-start | bytes 49156
  4.3 2.3 %collective-permute-start = (bf16[128,1024]{1,0:T(8,128)(2,1)S(1)}, bf16[128,1024]{1,0:T(8,128)(2,1)S(1)}, u32[]{:S(2)}, u32[]{:S(2)}) collective-permute-start(bf16[128,1024]{1,0:T(8,128)(2,1)S(1)} %get-tuple-element.16), channel_id=1, source_target_pairs={{0,1},{1,0},{2,3},{3,2},{4,5},{5,4},{6,7},{7,6},{8,9},{9,8},{10,11... | collective-permute-start | bytes 786440 | tf_op jit(solution)/shard_map/ppermute | solution.py:373
  6.9 5.2 %collective-permute-start.2 = (bf16[256,128]{1,0:T(8,128)(2,1)S(1)}, bf16[256,128]{1,0:T(8,128)(2,1)S(1)}, u32[]{:S(2)}, u32[]{:S(2)}) collective-permute-start(bf16[256,128]{1,0:T(8,128)(2,1)S(1)} %get-tuple-element.20), channel_id=1, source_target_pairs={{0,3},{1,2},{2,1},{3,0},{4,7},{5,6},{6,5},{7,4},{8,11},{9,10},{10,... | collective-permute-start | bytes 196616 | tf_op jit(solution)/shard_map/ppermute | solution.py:373
  12.0 3.8 %collective-permute-start.3 = (bf16[256,128]{1,0:T(8,128)(2,1)S(1)}, bf16[256,128]{1,0:T(8,128)(2,1)S(1)}, u32[]{:S(2)}, u32[]{:S(2)}) collective-permute-start(bf16[256,128]{1,0:T(8,128)(2,1)S(1)} %add.4.mine_ref), channel_id=1, source_target_pairs={{0,5},{1,12},{2,15},{3,6},{4,9},{5,0},{6,3},{7,10},{8,13},{9,4},{1... | collective-permute-start | bytes 196616 | tf_op jit(solution)/shard_map/ppermute | solution.py:373
  13.4 6.1 %collective-permute-start.1 = (bf16[128,512]{1,0:T(8,128)(2,1)S(1)}, bf16[128,512]{1,0:T(8,128)(2,1)S(1)}, u32[]{:S(2)}, u32[]{:S(2)}) collective-permute-start(bf16[128,512]{1,0:T(8,128)(2,1)S(1)} %get-tuple-element.18), channel_id=1, source_target_pairs={{0,3},{1,2},{2,1},{3,0},{4,7},{5,6},{6,5},{7,4},{8,11},{9,10},{10,... | collective-permute-start | bytes 393224 | tf_op jit(solution)/shard_map/ppermute | solution.py:373
  15.8 5.8 %collective-permute-start.4 = (bf16[256,128]{1,0:T(8,128)(2,1)S(1)}, bf16[256,128]{1,0:T(8,128)(2,1)S(1)}, u32[]{:S(2)}, u32[]{:S(2)}) collective-permute-start(bf16[256,128]{1,0:T(8,128)(2,1)S(1)} %add.5.mine_ref), channel_id=1, source_target_pairs={{0,13},{1,4},{2,7},{3,14},{4,1},{5,8},{6,11},{7,2},{8,5},{9,12},{1... | collective-permute-start | bytes 196616 | tf_op jit(solution)/shard_map/ppermute | solution.py:373
  21.8 1.4 %collective-permute-start.5 = (bf16[128,128]{1,0:T(8,128)(2,1)S(1)}, bf16[128,128]{1,0:T(8,128)(2,1)S(1)}, u32[]{:S(2)}, u32[]{:S(2)}) collective-permute-start(bf16[128,128]{1,0:T(8,128)(2,1)S(1)} %product_terms.1.mine_ref), channel_id=1, source_target_pairs={{0,1},{1,0},{2,3},{3,2},{4,5},{5,4},{6,7},{7,6},{8,9},{9,8},{10,11... | collective-permute-start | bytes 98312 | tf_op jit(solution)/shard_map/ppermute | solution.py:373
  23.3 4.3 %collective-permute-start.8 = (bf16[128,128]{1,0:T(8,128)(2,1)S(1)}, bf16[128,128]{1,0:T(8,128)(2,1)S(1)}, u32[]{:S(2)}, u32[]{:S(2)}) collective-permute-start(bf16[128,128]{1,0:T(8,128)(2,1)S(1)} %add.7.refs_0_.term_ref), channel_id=1, source_target_pairs={{0,7},{1,6},{2,5},{3,4},{4,3},{5,2},{6,1},{7,0},{8,15},{9,14},{10,... | collective-permute-start | bytes 98312 | tf_op jit(solution)/shard_map/ppermute | solution.py:373
  24.6 4.0 %collective-permute-start.7 = (bf16[128,128]{1,0:T(8,128)(2,1)S(1)}, bf16[128,128]{1,0:T(8,128)(2,1)S(1)}, u32[]{:S(2)}, u32[]{:S(2)}) collective-permute-start(bf16[128,128]{1,0:T(8,128)(2,1)S(1)} %add.7.refs_0_.term_ref), channel_id=1, source_target_pairs={{0,5},{1,4},{2,7},{3,6},{4,1},{5,0},{6,3},{7,2},{8,13},{9,12},{10,... | collective-permute-start | bytes 98312 | tf_op jit(solution)/shard_map/ppermute | solution.py:373
  26.3 3.3 %collective-permute-start.6 = (bf16[128,128]{1,0:T(8,128)(2,1)S(1)}, bf16[128,128]{1,0:T(8,128)(2,1)S(1)}, u32[]{:S(2)}, u32[]{:S(2)}) collective-permute-start(bf16[128,128]{1,0:T(8,128)(2,1)S(1)} %add.7.refs_0_.term_ref), channel_id=1, source_target_pairs={{0,3},{1,2},{2,1},{3,0},{4,7},{5,6},{6,5},{7,4},{8,11},{9,10},{10,... | collective-permute-start | bytes 98312 | tf_op jit(solution)/shard_map/ppermute | solution.py:373
  29.9 5.0 %collective-permute-start.9 = (f32[32,128]{1,0:T(8,128)S(1)}, f32[32,128]{1,0:T(8,128)S(1)}, u32[]{:S(2)}, u32[]{:S(2)}) collective-permute-start(f32[32,128]{1,0:T(8,128)S(1)} %local_gram.1.gram_ref), channel_id=1, source_target_pairs={{0,13},{1,12},{2,15},{3,14},{4,9},{5,8},{6,11},{7,10},{8,5},{9,4},... | collective-permute-start | bytes 49160 | tf_op jit(solution)/shard_map/ppermute | solution.py:373

commit v28 on v25

--- a/solution.py
+++ b/solution.py
@@ -286,7 +286,7 @@
     return dot_f32(left, right, ((axis,), (axis,)))
 
 
-def eliminate(packed):
+def eliminate(packed, spread_ref):
     rank = packed.shape[1] // 2
     tile = 8
     count = rank // tile
@@ -307,8 +307,15 @@
             {v: full(both[v][:, p * tile + j:p * tile + j + 1]) for v in range(p, count)}
             for j in range(tile)
         ]
-        rows = [full(both[p][j:j + 1]) for j in range(tile)]
-        block = [[full(cols[k][p][j:j + 1]) for k in range(j + 1)] for j in range(tile)]
+        base = p * (tile + 1) * tile
+        spread_ref[pl.ds(base, tile), :] = both[p]
+        for k in range(tile):
+            spread_ref[pl.ds(base + (k + 1) * tile, tile), :] = cols[k][p]
+        rows = [full(spread_ref[pl.ds(base + j, 1), :]) for j in range(tile)]
+        block = [
+            [full(spread_ref[pl.ds(base + (k + 1) * tile + j, 1), :]) for k in range(j + 1)]
+            for j in range(tile)
+        ]
         found, kept = block[0][0], rows[0]
         for j in range(tile):
             if j:
@@ -330,9 +337,11 @@
     return both, pivots
 
 
-def finish_kernel(total_rows, term_ref, got_term_ref, gram_ref, got_gram_ref, out_ref):
+def finish_kernel(
+    total_rows, term_ref, got_term_ref, gram_ref, got_gram_ref, out_ref, spread_ref
+):
     rank = LANES // 2
-    both, pivots = eliminate(gram_ref[...] + got_gram_ref[...])
+    both, pivots = eliminate(gram_ref[...] + got_gram_ref[...], spread_ref)
     scale = total_rows ** 0.5
     inverse = jnp.concatenate([b * (lax.rsqrt(p) * scale) for b, p in zip(both, pivots)], axis=0)
     inverse = inverse[:, rank:]
@@ -347,6 +356,7 @@
     return pl.pallas_call(
         functools.partial(finish_kernel, total_rows),
         out_shape=jax.ShapeDtypeStruct((term.shape[1] // 2, LANES // 2), F32),
+        scratch_shapes=[pltpu.VMEM((LANES // 2 * 9, LANES), F32)],
         compiler_params=params(4),
         name="finish",
     )(term, got_term, gram, got_gram)

time: 37.3 us -> 37 us (level)
  no operation moved by 1% of the time
where the time goes in v28:
time: 37 us; the launch traced here: 36.8 us
  starting transfers between devices  14.5 us (39%)
  waiting for transfers between devices  12.2 us (33%)
  Pallas kernels  9.95 us (27%)
    ppermute x10, starting transfers between devices, swap(): return lax.ppermute(x, ('row', 'col'), pairs)  14.5 us
    ppermute x10, waiting for transfers between devices, swap(): return lax.ppermute(x, ('row', 'col'), pairs)  12.2 us
    pallas_call x1, Pallas kernels, contract_send(): pl.pallas_call(send_kernel, in_specs=[pinned, pinned], out_shape=[jax.Sha...  5.08 us
    pallas_call x1, Pallas kernels, finish(): pl.pallas_call(functools.partial(finish_kernel, total_rows), out_shape=ja...  2.34 us
    pallas_call x1, Pallas kernels, contract_own(): pl.pallas_call(own_kernel, out_shape=jax.ShapeDtypeStruct((cells, half //...  1.77 us
  transfers between devices with their start and end apart: 10, of which 8 were waited for; matrix products, arithmetic and copies ran while one was open for 0% of the time, Pallas kernels for 5%

profile of v28, /device:TPU:0, one launch (start us, length us, event | category | flops | bytes accessed | tf_op | source)
XLA Modules:
  0.0 36.8 jit_solution(684368076175873460)
XLA Ops:
  0.0 0.0 copy-start
  0.0 5.1 %contract_send.1 = (bf16[128,1024]{1,0:T(8,128)(2,1)S(1)}, bf16[128,16,1024]{2,1,0:T(8,128)(2,1)S(1)}, bf16[128,1024]{1,0:T(8,128)(2,1)S(1)}, bf16[64,256]{1,0:T(8,128)(2,1)S(1)}) custom-call(bf16[128,32,1024]{2,1,0:T(8,128)(2,1)} %snapshot_ref.1, bf16[64,1024]{1,0:T(8,128)(2,1)} %bitcast.3), custom_call_target="tpu_custom_call" | custom-call | tf_op jit(solution)/shard_map/contract_send/pallas_call | solution.py:128
  5.1 0.5 %collective-permute-start = (bf16[128,1024]{1,0:T(8,128)(2,1)S(1)}, bf16[128,1024]{1,0:T(8,128)(2,1)S(1)}, u32[]{:S(2)}, u32[]{:S(2)}) collective-permute-start(bf16[128,1024]{1,0:T(8,128)(2,1)S(1)} %get-tuple-element.16), channel_id=1, source_target_pairs={{0,1},{1,0},{2,3},{3,2},{4,5},{5,4},{6,7},{7,6},{8,9},{9,8},{10,11... | collective-permute-start | bytes 786440 | tf_op jit(solution)/shard_map/ppermute | solution.py:377
  5.6 1.8 %contract_own.1.own_ref = bf16[128,1024]{1,0:T(8,128)(2,1)S(1)} custom-call(bf16[128,16,1024]{2,1,0:T(8,128)(2,1)S(1)} %get-tuple-element.13.slab_ref, bf16[128,1024]{1,0:T(8,128)(2,1)S(1)} %get-tuple-element.14.wide_ref, bf16[64,256]{1,0:T(8,128)(2,1)S(1)} %get-tuple-element.15.order_ref), custom_call_target="tpu_custom_call" | custom-call | tf_op jit(solution)/shard_map/contract_own/pallas_call | solution.py:165
  7.4 0.0 collective-permute-done.got_ref
  7.4 0.0 copy-done
  7.4 0.2 project.1
  7.6 2.7 %collective-permute-start.2 = (bf16[256,128]{1,0:T(8,128)(2,1)S(1)}, bf16[256,128]{1,0:T(8,128)(2,1)S(1)}, u32[]{:S(2)}, u32[]{:S(2)}) collective-permute-start(bf16[256,128]{1,0:T(8,128)(2,1)S(1)} %get-tuple-element.20), channel_id=1, source_target_pairs={{0,3},{1,2},{2,1},{3,0},{4,7},{5,6},{6,5},{7,4},{8,11},{9,10},{10,... | collective-permute-start | bytes 196616 | tf_op jit(solution)/shard_map/ppermute | solution.py:377
  10.3 2.5 %collective-permute-done.2.got_ref = bf16[256,128]{1,0:T(8,128)(2,1)S(1)} collective-permute-done((bf16[256,128]{1,0:T(8,128)(2,1)S(1)}, bf16[256,128]{1,0:T(8,128)(2,1)S(1)}, u32[]{:S(2)}, u32[]{:S(2)}) %collective-permute-start.2) | collective-permute-done | bytes 65568 | tf_op jit(solution)/shard_map/ppermute | solution.py:377
  12.8 1.4 %collective-permute-start.3 = (bf16[256,128]{1,0:T(8,128)(2,1)S(1)}, bf16[256,128]{1,0:T(8,128)(2,1)S(1)}, u32[]{:S(2)}, u32[]{:S(2)}) collective-permute-start(bf16[256,128]{1,0:T(8,128)(2,1)S(1)} %add.4.mine_ref), channel_id=1, source_target_pairs={{0,5},{1,8},{2,11},{3,6},{4,13},{5,0},{6,3},{7,14},{8,1},{9,12},{1... | collective-permute-start | bytes 196616 | tf_op jit(solution)/shard_map/ppermute | solution.py:377
  14.2 1.2 %collective-permute-start.1 = (bf16[128,512]{1,0:T(8,128)(2,1)S(1)}, bf16[128,512]{1,0:T(8,128)(2,1)S(1)}, u32[]{:S(2)}, u32[]{:S(2)}) collective-permute-start(bf16[128,512]{1,0:T(8,128)(2,1)S(1)} %get-tuple-element.18), channel_id=1, source_target_pairs={{0,3},{1,2},{2,1},{3,0},{4,7},{5,6},{6,5},{7,4},{8,11},{9,10},{10,... | collective-permute-start | bytes 393224 | tf_op jit(solution)/shard_map/ppermute | solution.py:377
  15.4 1.2 %collective-permute-done.3.got_ref = bf16[256,128]{1,0:T(8,128)(2,1)S(1)} collective-permute-done((bf16[256,128]{1,0:T(8,128)(2,1)S(1)}, bf16[256,128]{1,0:T(8,128)(2,1)S(1)}, u32[]{:S(2)}, u32[]{:S(2)}) %collective-permute-start.3) | collective-permute-done | bytes 65568 | tf_op jit(solution)/shard_map/ppermute | solution.py:377
  16.6 2.7 %collective-permute-start.4 = (bf16[256,128]{1,0:T(8,128)(2,1)S(1)}, bf16[256,128]{1,0:T(8,128)(2,1)S(1)}, u32[]{:S(2)}, u32[]{:S(2)}) collective-permute-start(bf16[256,128]{1,0:T(8,128)(2,1)S(1)} %add.5.mine_ref), channel_id=1, source_target_pairs={{0,9},{1,4},{2,7},{3,10},{4,1},{5,12},{6,15},{7,2},{8,13},{9,0},{1... | collective-permute-start | bytes 196616 | tf_op jit(solution)/shard_map/ppermute | solution.py:377
  19.3 0.0 collective-permute-done.1.refs_0_.got_ref
  19.3 2.0 %collective-permute-done.4.got_ref = bf16[256,128]{1,0:T(8,128)(2,1)S(1)} collective-permute-done((bf16[256,128]{1,0:T(8,128)(2,1)S(1)}, bf16[256,128]{1,0:T(8,128)(2,1)S(1)}, u32[]{:S(2)}, u32[]{:S(2)}) %collective-permute-start.4) | collective-permute-done | bytes 65568 | tf_op jit(solution)/shard_map/ppermute | solution.py:377
  21.3 0.2 product_terms.1.mine_ref
  21.5 0.9 %collective-permute-start.5 = (bf16[128,128]{1,0:T(8,128)(2,1)S(1)}, bf16[128,128]{1,0:T(8,128)(2,1)S(1)}, u32[]{:S(2)}, u32[]{:S(2)}) collective-permute-start(bf16[128,128]{1,0:T(8,128)(2,1)S(1)} %product_terms.1.mine_ref), channel_id=1, source_target_pairs={{0,1},{1,0},{2,3},{3,2},{4,5},{5,4},{6,7},{7,6},{8,9},{9,8},{10,11... | collective-permute-start | bytes 98312 | tf_op jit(solution)/shard_map/ppermute | solution.py:377
  22.4 0.9 %collective-permute-done.5.got_ref = bf16[128,128]{1,0:T(8,128)(2,1)S(1)} collective-permute-done((bf16[128,128]{1,0:T(8,128)(2,1)S(1)}, bf16[128,128]{1,0:T(8,128)(2,1)S(1)}, u32[]{:S(2)}, u32[]{:S(2)}) %collective-permute-start.5) | collective-permute-done | bytes 32800 | tf_op jit(solution)/shard_map/ppermute | solution.py:377
  23.2 2.6 %collective-permute-start.8 = (bf16[128,128]{1,0:T(8,128)(2,1)S(1)}, bf16[128,128]{1,0:T(8,128)(2,1)S(1)}, u32[]{:S(2)}, u32[]{:S(2)}) collective-permute-start(bf16[128,128]{1,0:T(8,128)(2,1)S(1)} %add.7.refs_0_.term_ref), channel_id=1, source_target_pairs={{0,7},{1,6},{2,5},{3,4},{4,3},{5,2},{6,1},{7,0},{8,15},{9,14},{10,... | collective-permute-start | bytes 98312 | tf_op jit(solution)/shard_map/ppermute | solution.py:377
  25.8 0.9 %collective-permute-start.7 = (bf16[128,128]{1,0:T(8,128)(2,1)S(1)}, bf16[128,128]{1,0:T(8,128)(2,1)S(1)}, u32[]{:S(2)}, u32[]{:S(2)}) collective-permute-start(bf16[128,128]{1,0:T(8,128)(2,1)S(1)} %add.7.refs_0_.term_ref), channel_id=1, source_target_pairs={{0,5},{1,4},{2,7},{3,6},{4,1},{5,0},{6,3},{7,2},{8,13},{9,12},{10,... | collective-permute-start | bytes 98312 | tf_op jit(solution)/shard_map/ppermute | solution.py:377
  26.7 0.0 collective-permute-start.6
  26.7 0.8 %collective-permute-done.8.refs_3_ = bf16[128,128]{1,0:T(8,128)(2,1)S(1)} collective-permute-done((bf16[128,128]{1,0:T(8,128)(2,1)S(1)}, bf16[128,128]{1,0:T(8,128)(2,1)S(1)}, u32[]{:S(2)}, u32[]{:S(2)}) %collective-permute-start.8) | collective-permute-done | bytes 32800 | tf_op jit(solution)/shard_map/ppermute | solution.py:377
  27.5 1.7 %collective-permute-done.7.refs_2_ = bf16[128,128]{1,0:T(8,128)(2,1)S(1)} collective-permute-done((bf16[128,128]{1,0:T(8,128)(2,1)S(1)}, bf16[128,128]{1,0:T(8,128)(2,1)S(1)}, u32[]{:S(2)}, u32[]{:S(2)}) %collective-permute-start.7) | collective-permute-done | bytes 32800 | tf_op jit(solution)/shard_map/ppermute | solution.py:377
  29.2 0.9 %collective-permute-done.6.refs_1_.got_term_ref = bf16[128,128]{1,0:T(8,128)(2,1)S(1)} collective-permute-done((bf16[128,128]{1,0:T(8,128)(2,1)S(1)}, bf16[128,128]{1,0:T(8,128)(2,1)S(1)}, u32[]{:S(2)}, u32[]{:S(2)}) %collective-permute-start.6) | collective-permute-done | bytes 32800 | tf_op jit(solution)/shard_map/ppermute | solution.py:377
  30.1 0.3 local_gram.1.gram_ref
  30.3 1.7 %collective-permute-start.9 = (f32[32,128]{1,0:T(8,128)S(1)}, f32[32,128]{1,0:T(8,128)S(1)}, u32[]{:S(2)}, u32[]{:S(2)}) collective-permute-start(f32[32,128]{1,0:T(8,128)S(1)} %local_gram.1.gram_ref), channel_id=1, source_target_pairs={{0,9},{1,8},{2,11},{3,10},{4,13},{5,12},{6,15},{7,14},{8,1},{9,0},... | collective-permute-start | bytes 49160 | tf_op jit(solution)/shard_map/ppermute | solution.py:377
  32.0 2.4 %collective-permute-done.9.got_gram_ref = f32[32,128]{1,0:T(8,128)S(1)} collective-permute-done((f32[32,128]{1,0:T(8,128)S(1)}, f32[32,128]{1,0:T(8,128)S(1)}, u32[]{:S(2)}, u32[]{:S(2)}) %collective-permute-start.9) | collective-permute-done | bytes 16416 | tf_op jit(solution)/shard_map/ppermute | solution.py:377
  34.4 2.3 %finish.1 = f32[64,64]{1,0:T(8,128)} custom-call(bf16[128,128]{1,0:T(8,128)(2,1)S(1)} %add.7.refs_0_.term_ref, bf16[128,128]{1,0:T(8,128)(2,1)S(1)} %collective-permute-done.6.refs_1_.got_term_ref, f32[32,128]{1,0:T(8,128)S(1)} %local_gram.1.gram_ref, f32[32,128]{1,0:T(8,128)S(1)} %collective-permute-done.9.got_gram_ref), custom_call_target="tpu_custom_call" | custom-call | tf_op jit(solution)/shard_map/finish/pallas_call | solution.py:356
  (4 shorter events, 0.1 us)
Async XLA Ops:
  0.0 7.4 %copy-start = (bf16[128,64]{0,1:T(8,128)(2,1)S(1)}, bf16[128,64]{0,1:T(8,128)(2,1)}, u32[]{:S(2)}) copy-start(bf16[128,64]{0,1:T(8,128)(2,1)} %param.5) | copy-start | bytes 49156
  5.1 2.3 %collective-permute-start = (bf16[128,1024]{1,0:T(8,128)(2,1)S(1)}, bf16[128,1024]{1,0:T(8,128)(2,1)S(1)}, u32[]{:S(2)}, u32[]{:S(2)}) collective-permute-start(bf16[128,1024]{1,0:T(8,128)(2,1)S(1)} %get-tuple-element.16), channel_id=1, source_target_pairs={{0,1},{1,0},{2,3},{3,2},{4,5},{5,4},{6,7},{7,6},{8,9},{9,8},{10,11... | collective-permute-start | bytes 786440 | tf_op jit(solution)/shard_map/ppermute | solution.py:377
  7.6 5.2 %collective-permute-start.2 = (bf16[256,128]{1,0:T(8,128)(2,1)S(1)}, bf16[256,128]{1,0:T(8,128)(2,1)S(1)}, u32[]{:S(2)}, u32[]{:S(2)}) collective-permute-start(bf16[256,128]{1,0:T(8,128)(2,1)S(1)} %get-tuple-element.20), channel_id=1, source_target_pairs={{0,3},{1,2},{2,1},{3,0},{4,7},{5,6},{6,5},{7,4},{8,11},{9,10},{10,... | collective-permute-start | bytes 196616 | tf_op jit(solution)/shard_map/ppermute | solution.py:377
  12.8 3.8 %collective-permute-start.3 = (bf16[256,128]{1,0:T(8,128)(2,1)S(1)}, bf16[256,128]{1,0:T(8,128)(2,1)S(1)}, u32[]{:S(2)}, u32[]{:S(2)}) collective-permute-start(bf16[256,128]{1,0:T(8,128)(2,1)S(1)} %add.4.mine_ref), channel_id=1, source_target_pairs={{0,5},{1,8},{2,11},{3,6},{4,13},{5,0},{6,3},{7,14},{8,1},{9,12},{1... | collective-permute-start | bytes 196616 | tf_op jit(solution)/shard_map/ppermute | solution.py:377
  14.2 5.1 %collective-permute-start.1 = (bf16[128,512]{1,0:T(8,128)(2,1)S(1)}, bf16[128,512]{1,0:T(8,128)(2,1)S(1)}, u32[]{:S(2)}, u32[]{:S(2)}) collective-permute-start(bf16[128,512]{1,0:T(8,128)(2,1)S(1)} %get-tuple-element.18), channel_id=1, source_target_pairs={{0,3},{1,2},{2,1},{3,0},{4,7},{5,6},{6,5},{7,4},{8,11},{9,10},{10,... | collective-permute-start | bytes 393224 | tf_op jit(solution)/shard_map/ppermute | solution.py:377
  16.6 4.7 %collective-permute-start.4 = (bf16[256,128]{1,0:T(8,128)(2,1)S(1)}, bf16[256,128]{1,0:T(8,128)(2,1)S(1)}, u32[]{:S(2)}, u32[]{:S(2)}) collective-permute-start(bf16[256,128]{1,0:T(8,128)(2,1)S(1)} %add.5.mine_ref), channel_id=1, source_target_pairs={{0,9},{1,4},{2,7},{3,10},{4,1},{5,12},{6,15},{7,2},{8,13},{9,0},{1... | collective-permute-start | bytes 196616 | tf_op jit(solution)/shard_map/ppermute | solution.py:377
  21.5 1.7 %collective-permute-start.5 = (bf16[128,128]{1,0:T(8,128)(2,1)S(1)}, bf16[128,128]{1,0:T(8,128)(2,1)S(1)}, u32[]{:S(2)}, u32[]{:S(2)}) collective-permute-start(bf16[128,128]{1,0:T(8,128)(2,1)S(1)} %product_terms.1.mine_ref), channel_id=1, source_target_pairs={{0,1},{1,0},{2,3},{3,2},{4,5},{5,4},{6,7},{7,6},{8,9},{9,8},{10,11... | collective-permute-start | bytes 98312 | tf_op jit(solution)/shard_map/ppermute | solution.py:377
  23.2 4.3 %collective-permute-start.8 = (bf16[128,128]{1,0:T(8,128)(2,1)S(1)}, bf16[128,128]{1,0:T(8,128)(2,1)S(1)}, u32[]{:S(2)}, u32[]{:S(2)}) collective-permute-start(bf16[128,128]{1,0:T(8,128)(2,1)S(1)} %add.7.refs_0_.term_ref), channel_id=1, source_target_pairs={{0,7},{1,6},{2,5},{3,4},{4,3},{5,2},{6,1},{7,0},{8,15},{9,14},{10,... | collective-permute-start | bytes 98312 | tf_op jit(solution)/shard_map/ppermute | solution.py:377
  25.8 3.4 %collective-permute-start.7 = (bf16[128,128]{1,0:T(8,128)(2,1)S(1)}, bf16[128,128]{1,0:T(8,128)(2,1)S(1)}, u32[]{:S(2)}, u32[]{:S(2)}) collective-permute-start(bf16[128,128]{1,0:T(8,128)(2,1)S(1)} %add.7.refs_0_.term_ref), channel_id=1, source_target_pairs={{0,5},{1,4},{2,7},{3,6},{4,1},{5,0},{6,3},{7,2},{8,13},{9,12},{10,... | collective-permute-start | bytes 98312 | tf_op jit(solution)/shard_map/ppermute | solution.py:377
  26.7 3.3 %collective-permute-start.6 = (bf16[128,128]{1,0:T(8,128)(2,1)S(1)}, bf16[128,128]{1,0:T(8,128)(2,1)S(1)}, u32[]{:S(2)}, u32[]{:S(2)}) collective-permute-start(bf16[128,128]{1,0:T(8,128)(2,1)S(1)} %add.7.refs_0_.term_ref), channel_id=1, source_target_pairs={{0,3},{1,2},{2,1},{3,0},{4,7},{5,6},{6,5},{7,4},{8,11},{9,10},{10,... | collective-permute-start | bytes 98312 | tf_op jit(solution)/shard_map/ppermute | solution.py:377
  30.3 4.1 %collective-permute-start.9 = (f32[32,128]{1,0:T(8,128)S(1)}, f32[32,128]{1,0:T(8,128)S(1)}, u32[]{:S(2)}, u32[]{:S(2)}) collective-permute-start(f32[32,128]{1,0:T(8,128)S(1)} %local_gram.1.gram_ref), channel_id=1, source_target_pairs={{0,9},{1,8},{2,11},{3,10},{4,13},{5,12},{6,15},{7,14},{8,1},{9,0},... | collective-permute-start | bytes 49160 | tf_op jit(solution)/shard_map/ppermute | solution.py:377

commit v29 on v26

--- a/solution.py
+++ b/solution.py
@@ -68,7 +68,7 @@
 STEP = 32
 
 
-def slab_copies(snapshot_ref, first, slab_ref, half_index, sem, priority):
+def slab_copies(snapshot_ref, first, slab_ref, half_index, sem):
     half = slab_ref.shape[1]
     fibers = pl.ds(pl.multiple_of(half_index * half, half), half)
 
@@ -81,7 +81,7 @@
 
     def start(begin, size, count):
         for part in range(count):
-            copy(begin + part * (size // count), size // count).start(priority=priority)
+            copy(begin + part * (size // count), size // count).start()
 
     return start, lambda begin, size: copy(begin, size).wait()
 
@@ -95,21 +95,22 @@
     chunks = cells // STEP
     flat = (even_ref, odd_ref)
     sends = [
-        slab_copies(snapshot_ref, 0, slab_ref, 1 - own_half(), sems.at[chunk], 1)
+        slab_copies(snapshot_ref, 0, slab_ref, 1 - own_half(), sems.at[chunk])
         for chunk in range(chunks)
     ]
-    start_kept, wait_kept = slab_copies(snapshot_ref, 0, kept_ref, own_half(), kept_sem, 0)
+    start_kept, wait_kept = slab_copies(snapshot_ref, 0, kept_ref, own_half(), kept_sem)
 
     small = pltpu.make_async_copy(mode2_ref, small_ref, small_sem)
     small.start()
     for chunk in range(chunks):
         sends[chunk][0](chunk * STEP, STEP, 2 if chunk else 4)
-    start_kept(0, cells, 2 * chunks)
     fill_order(order_ref, half)
     small.wait()
     wide_ref[...] = jnp.concatenate([small_ref[...]] * (LANES // rank), axis=0)
     for chunk in range(chunks):
         sends[chunk][1](chunk * STEP, STEP)
+        if chunk == 0:
+            start_kept(0, cells, 2 * chunks)
         multiply(slab_ref[pl.ds(chunk * STEP, STEP)], wide_ref, flat[chunk % 2])
         if chunk:
             spread(half, flat[(chunk - 1) % 2], order_ref, core_ref, (chunk - 1) * STEP)
@@ -240,14 +241,17 @@
     )(mine, got, projected)
 
 
-def pair_product(term_ref, got_ref):
-    return term_ref[...].astype(F32) + got_ref[...].astype(F32)
-
-
-def gram_kernel(*refs):
-    out_ref = refs[-1]
+def pair_product(term_ref, first_ref, second_ref):
+    got = jnp.where(own_half() == 0, first_ref[...].astype(F32), second_ref[...].astype(F32))
+    return term_ref[...].astype(F32) + got
+
+
+def gram_kernel(term_ref, first_ref, second_ref, last_ref, out_ref):
     rank = LANES // 2
-    pairs = [pair_product(refs[k], refs[k + 1]) for k in range(0, len(refs) - 1, 2)]
+    pairs = [
+        pair_product(term_ref, first_ref, second_ref),
+        pair_product(last_ref, second_ref, first_ref),
+    ]
     product = jnp.concatenate([x[k:k + rank] for x in pairs for k in (0, rank)], axis=1)
     gram = dot_parts(product, product, 1)
     out_ref[...] = jnp.concatenate([gram[:rank // 2], gram[rank // 2:]], axis=1)
@@ -274,7 +278,7 @@
     return dot_f32(left, right, ((axis,), (axis,)))
 
 
-def eliminate(packed):
+def eliminate(packed, spread_ref):
     rank = packed.shape[1] // 2
     tile = 8
     count = rank // tile
@@ -295,8 +299,15 @@
             {v: full(both[v][:, p * tile + j:p * tile + j + 1]) for v in range(p, count)}
             for j in range(tile)
         ]
-        rows = [full(both[p][j:j + 1]) for j in range(tile)]
-        block = [[full(cols[k][p][j:j + 1]) for k in range(j + 1)] for j in range(tile)]
+        base = p * (tile + 1) * tile
+        spread_ref[pl.ds(base, tile), :] = both[p]
+        for k in range(tile):
+            spread_ref[pl.ds(base + (k + 1) * tile, tile), :] = cols[k][p]
+        rows = [full(spread_ref[pl.ds(base + j, 1), :]) for j in range(tile)]
+        block = [
+            [full(spread_ref[pl.ds(base + (k + 1) * tile + j, 1), :]) for k in range(j + 1)]
+            for j in range(tile)
+        ]
         found, kept = block[0][0], rows[0]
         for j in range(tile):
             if j:
@@ -318,26 +329,29 @@
     return both, pivots
 
 
-def finish_kernel(total_rows, term_ref, got_term_ref, gram_ref, got_gram_ref, out_ref):
+def finish_kernel(
+    total_rows, term_ref, first_ref, second_ref, gram_ref, got_gram_ref, out_ref, spread_ref
+):
     rank = LANES // 2
-    both, pivots = eliminate(gram_ref[...] + got_gram_ref[...])
+    both, pivots = eliminate(gram_ref[...] + got_gram_ref[...], spread_ref)
     scale = total_rows ** 0.5
     inverse = jnp.concatenate([b * (lax.rsqrt(p) * scale) for b, p in zip(both, pivots)], axis=0)
     inverse = inverse[:, rank:]
     half = term_ref.shape[1] // 2
-    product = pair_product(term_ref, got_term_ref)
+    product = pair_product(term_ref, first_ref, second_ref)
     product = jnp.where(is_even(), product[:rank], product[rank:])
     mine = jnp.where(lax.axis_index("col") == 0, product[:, :half], product[:, half:]).T
     out_ref[...] = dot_parts(mine, inverse, 1)
 
 
-def finish(total_rows, term, got_term, gram, got_gram):
+def finish(total_rows, term, first, second, gram, got_gram):
     return pl.pallas_call(
         functools.partial(finish_kernel, total_rows),
         out_shape=jax.ShapeDtypeStruct((term.shape[1] // 2, LANES // 2), F32),
+        scratch_shapes=[pltpu.VMEM((LANES // 2 * 9, LANES), F32)],
         compiler_params=params(4),
         name="finish",
-    )(term, got_term, gram, got_gram)
+    )(term, first, second, gram, got_gram)
 
 
 def per_device(snapshot, mode2_factor, old_factor):
@@ -373,11 +387,11 @@
     term = product_terms(columns, got_columns, mine)
     term = add(term, swap(term, 0))
     pair, next_pair = masks[:2]
-    got_term = swap(term, pair)
-    gram = local_gram(term, got_term, swap(term, next_pair), swap(term, pair | next_pair))
+    first, second = swap(term, pair, next_pair), swap(term, next_pair, pair)
+    gram = local_gram(term, first, second, swap(term, pair | next_pair))
     for mask in masks[2:-1]:
         gram = add(gram, swap(gram, mask))
-    return finish(total_rows, term, got_term, gram, swap(gram, masks[-1]))
+    return finish(total_rows, term, first, second, gram, swap(gram, masks[-1]))
 
 
 def solution(mesh):

time: 37.9 us -> 36.9 us (0.974)
  Pallas kernels: 10.9 us -> 10.1 us
    pallas_call x1, Pallas kernels: 5.54 us -> 5.08 us  [contract_send(): pl.pallas_call(send_kernel, in_specs=[pinned, pinned], out_shape=[jax.Sha...]
where the time goes in v29:
time: 36.9 us; the launch traced here: 36.8 us
  starting transfers between devices  14.5 us (39%)
  waiting for transfers between devices  12.1 us (33%)
  Pallas kernels  10.1 us (27%)
    ppermute x10, starting transfers between devices, swap(): return lax.ppermute(x, ('row', 'col'), pairs)  14.5 us
    ppermute x10, waiting for transfers between devices, swap(): return lax.ppermute(x, ('row', 'col'), pairs)  12.1 us
    pallas_call x1, Pallas kernels, contract_send(): pl.pallas_call(send_kernel, in_specs=[pinned, pinned], out_shape=[jax.Sha...  5.08 us
    pallas_call x1, Pallas kernels, finish(): pl.pallas_call(functools.partial(finish_kernel, total_rows), out_shape=ja...  2.34 us
    pallas_call x1, Pallas kernels, contract_own(): pl.pallas_call(own_kernel, out_shape=jax.ShapeDtypeStruct((cells, half //...  1.77 us
  transfers between devices with their start and end apart: 10, of which 8 were waited for; matrix products, arithmetic and copies ran while one was open for 0% of the time, Pallas kernels for 5%

profile of v29, /device:TPU:0, one launch (start us, length us, event | category | flops | bytes accessed | tf_op | source)
XLA Modules:
  0.0 36.8 jit_solution(9545213498564841874)
XLA Ops:
  0.0 0.0 copy-start
  0.0 5.1 %contract_send.1 = (bf16[128,1024]{1,0:T(8,128)(2,1)S(1)}, bf16[128,16,1024]{2,1,0:T(8,128)(2,1)S(1)}, bf16[128,1024]{1,0:T(8,128)(2,1)S(1)}, bf16[64,256]{1,0:T(8,128)(2,1)S(1)}) custom-call(bf16[128,32,1024]{2,1,0:T(8,128)(2,1)} %snapshot_ref.1, bf16[64,1024]{1,0:T(8,128)(2,1)} %bitcast.4), custom_call_target="tpu_custom_call" | custom-call | tf_op jit(solution)/shard_map/contract_send/pallas_call | solution.py:128
  5.1 0.5 %collective-permute-start = (bf16[128,1024]{1,0:T(8,128)(2,1)S(1)}, bf16[128,1024]{1,0:T(8,128)(2,1)S(1)}, u32[]{:S(2)}, u32[]{:S(2)}) collective-permute-start(bf16[128,1024]{1,0:T(8,128)(2,1)S(1)} %get-tuple-element.16), channel_id=1, source_target_pairs={{0,1},{1,0},{2,3},{3,2},{4,5},{5,4},{6,7},{7,6},{8,9},{9,8},{10,11... | collective-permute-start | bytes 786440 | tf_op jit(solution)/shard_map/ppermute | solution.py:369
  5.6 1.8 %contract_own.1.own_ref = bf16[128,1024]{1,0:T(8,128)(2,1)S(1)} custom-call(bf16[128,16,1024]{2,1,0:T(8,128)(2,1)S(1)} %get-tuple-element.13.slab_ref, bf16[128,1024]{1,0:T(8,128)(2,1)S(1)} %get-tuple-element.14.wide_ref, bf16[64,256]{1,0:T(8,128)(2,1)S(1)} %get-tuple-element.15.order_ref), custom_call_target="tpu_custom_call" | custom-call | tf_op jit(solution)/shard_map/contract_own/pallas_call | solution.py:165
  7.4 0.0 collective-permute-done.got_ref
  7.4 0.0 copy-done
  7.4 0.2 project_sent.1
  7.6 2.7 %collective-permute-start.2 = (bf16[256,128]{1,0:T(8,128)(2,1)S(1)}, bf16[256,128]{1,0:T(8,128)(2,1)S(1)}, u32[]{:S(2)}, u32[]{:S(2)}) collective-permute-start(bf16[256,128]{1,0:T(8,128)(2,1)S(1)} %get-tuple-element.20), channel_id=1, source_target_pairs={{0,3},{1,2},{2,1},{3,0},{4,7},{5,6},{6,5},{7,4},{8,11},{9,10},{10,... | collective-permute-start | bytes 196616 | tf_op jit(solution)/shard_map/ppermute | solution.py:369
  10.3 0.2 project_kept.1
  10.5 2.3 %collective-permute-done.2.got_ref = bf16[256,128]{1,0:T(8,128)(2,1)S(1)} collective-permute-done((bf16[256,128]{1,0:T(8,128)(2,1)S(1)}, bf16[256,128]{1,0:T(8,128)(2,1)S(1)}, u32[]{:S(2)}, u32[]{:S(2)}) %collective-permute-start.2) | collective-permute-done | bytes 65568 | tf_op jit(solution)/shard_map/ppermute | solution.py:369
  12.8 1.4 %collective-permute-start.3 = (bf16[256,128]{1,0:T(8,128)(2,1)S(1)}, bf16[256,128]{1,0:T(8,128)(2,1)S(1)}, u32[]{:S(2)}, u32[]{:S(2)}) collective-permute-start(bf16[256,128]{1,0:T(8,128)(2,1)S(1)} %add.4.mine_ref), channel_id=1, source_target_pairs={{0,5},{1,8},{2,11},{3,6},{4,13},{5,0},{6,3},{7,14},{8,1},{9,12},{1... | collective-permute-start | bytes 196616 | tf_op jit(solution)/shard_map/ppermute | solution.py:369
  14.2 1.2 %collective-permute-start.1 = (bf16[128,512]{1,0:T(8,128)(2,1)S(1)}, bf16[128,512]{1,0:T(8,128)(2,1)S(1)}, u32[]{:S(2)}, u32[]{:S(2)}) collective-permute-start(bf16[128,512]{1,0:T(8,128)(2,1)S(1)} %get-tuple-element.18), channel_id=1, source_target_pairs={{0,3},{1,2},{2,1},{3,0},{4,7},{5,6},{6,5},{7,4},{8,11},{9,10},{10,... | collective-permute-start | bytes 393224 | tf_op jit(solution)/shard_map/ppermute | solution.py:369
  15.3 1.2 %collective-permute-done.3.got_ref = bf16[256,128]{1,0:T(8,128)(2,1)S(1)} collective-permute-done((bf16[256,128]{1,0:T(8,128)(2,1)S(1)}, bf16[256,128]{1,0:T(8,128)(2,1)S(1)}, u32[]{:S(2)}, u32[]{:S(2)}) %collective-permute-start.3) | collective-permute-done | bytes 65568 | tf_op jit(solution)/shard_map/ppermute | solution.py:369
  16.5 2.7 %collective-permute-start.4 = (bf16[256,128]{1,0:T(8,128)(2,1)S(1)}, bf16[256,128]{1,0:T(8,128)(2,1)S(1)}, u32[]{:S(2)}, u32[]{:S(2)}) collective-permute-start(bf16[256,128]{1,0:T(8,128)(2,1)S(1)} %add.5.mine_ref), channel_id=1, source_target_pairs={{0,9},{1,4},{2,7},{3,10},{4,1},{5,12},{6,15},{7,2},{8,13},{9,0},{1... | collective-permute-start | bytes 196616 | tf_op jit(solution)/shard_map/ppermute | solution.py:369
  19.2 0.0 collective-permute-done.1.refs_0_.got_ref
  19.2 2.0 %collective-permute-done.4.got_ref = bf16[256,128]{1,0:T(8,128)(2,1)S(1)} collective-permute-done((bf16[256,128]{1,0:T(8,128)(2,1)S(1)}, bf16[256,128]{1,0:T(8,128)(2,1)S(1)}, u32[]{:S(2)}, u32[]{:S(2)}) %collective-permute-start.4) | collective-permute-done | bytes 65568 | tf_op jit(solution)/shard_map/ppermute | solution.py:369
  21.2 0.2 product_terms.1.mine_ref
  21.4 0.9 %collective-permute-start.5 = (bf16[128,128]{1,0:T(8,128)(2,1)S(1)}, bf16[128,128]{1,0:T(8,128)(2,1)S(1)}, u32[]{:S(2)}, u32[]{:S(2)}) collective-permute-start(bf16[128,128]{1,0:T(8,128)(2,1)S(1)} %product_terms.1.mine_ref), channel_id=1, source_target_pairs={{0,1},{1,0},{2,3},{3,2},{4,5},{5,4},{6,7},{7,6},{8,9},{9,8},{10,11... | collective-permute-start | bytes 98312 | tf_op jit(solution)/shard_map/ppermute | solution.py:369
  22.3 0.9 %collective-permute-done.5.got_ref = bf16[128,128]{1,0:T(8,128)(2,1)S(1)} collective-permute-done((bf16[128,128]{1,0:T(8,128)(2,1)S(1)}, bf16[128,128]{1,0:T(8,128)(2,1)S(1)}, u32[]{:S(2)}, u32[]{:S(2)}) %collective-permute-start.5) | collective-permute-done | bytes 32800 | tf_op jit(solution)/shard_map/ppermute | solution.py:369
  23.2 2.6 %collective-permute-start.8 = (bf16[128,128]{1,0:T(8,128)(2,1)S(1)}, bf16[128,128]{1,0:T(8,128)(2,1)S(1)}, u32[]{:S(2)}, u32[]{:S(2)}) collective-permute-start(bf16[128,128]{1,0:T(8,128)(2,1)S(1)} %add.7.term_ref), channel_id=1, source_target_pairs={{0,7},{1,6},{2,5},{3,4},{4,3},{5,2},{6,1},{7,0},{8,15},{9,14},{10,... | collective-permute-start | bytes 98312 | tf_op jit(solution)/shard_map/ppermute | solution.py:369
  25.8 0.9 %collective-permute-start.7 = (bf16[128,128]{1,0:T(8,128)(2,1)S(1)}, bf16[128,128]{1,0:T(8,128)(2,1)S(1)}, u32[]{:S(2)}, u32[]{:S(2)}) collective-permute-start(bf16[128,128]{1,0:T(8,128)(2,1)S(1)} %add.7.term_ref), channel_id=1, source_target_pairs={{0,5},{1,2},{2,1},{3,6},{4,7},{5,0},{6,3},{7,4},{8,11},{9,12},{10,... | collective-permute-start | bytes 98312 | tf_op jit(solution)/shard_map/ppermute | solution.py:369
  26.7 0.0 collective-permute-start.6
  26.7 0.8 %collective-permute-done.8.last_ref = bf16[128,128]{1,0:T(8,128)(2,1)S(1)} collective-permute-done((bf16[128,128]{1,0:T(8,128)(2,1)S(1)}, bf16[128,128]{1,0:T(8,128)(2,1)S(1)}, u32[]{:S(2)}, u32[]{:S(2)}) %collective-permute-start.8) | collective-permute-done | bytes 32800 | tf_op jit(solution)/shard_map/ppermute | solution.py:369
  27.5 1.7 %collective-permute-done.7.second_ref = bf16[128,128]{1,0:T(8,128)(2,1)S(1)} collective-permute-done((bf16[128,128]{1,0:T(8,128)(2,1)S(1)}, bf16[128,128]{1,0:T(8,128)(2,1)S(1)}, u32[]{:S(2)}, u32[]{:S(2)}) %collective-permute-start.7) | collective-permute-done | bytes 32800 | tf_op jit(solution)/shard_map/ppermute | solution.py:369
  29.2 0.9 %collective-permute-done.6.first_ref = bf16[128,128]{1,0:T(8,128)(2,1)S(1)} collective-permute-done((bf16[128,128]{1,0:T(8,128)(2,1)S(1)}, bf16[128,128]{1,0:T(8,128)(2,1)S(1)}, u32[]{:S(2)}, u32[]{:S(2)}) %collective-permute-start.6) | collective-permute-done | bytes 32800 | tf_op jit(solution)/shard_map/ppermute | solution.py:369
  30.0 0.3 local_gram.1.gram_ref
  30.3 1.7 %collective-permute-start.9 = (f32[32,128]{1,0:T(8,128)S(1)}, f32[32,128]{1,0:T(8,128)S(1)}, u32[]{:S(2)}, u32[]{:S(2)}) collective-permute-start(f32[32,128]{1,0:T(8,128)S(1)} %local_gram.1.gram_ref), channel_id=1, source_target_pairs={{0,9},{1,8},{2,11},{3,10},{4,13},{5,12},{6,15},{7,14},{8,1},{9,0},... | collective-permute-start | bytes 49160 | tf_op jit(solution)/shard_map/ppermute | solution.py:369
  32.0 2.5 %collective-permute-done.9.got_gram_ref = f32[32,128]{1,0:T(8,128)S(1)} collective-permute-done((f32[32,128]{1,0:T(8,128)S(1)}, f32[32,128]{1,0:T(8,128)S(1)}, u32[]{:S(2)}, u32[]{:S(2)}) %collective-permute-start.9) | collective-permute-done | bytes 16416 | tf_op jit(solution)/shard_map/ppermute | solution.py:369
  34.4 2.3 %finish.1 = f32[64,64]{1,0:T(8,128)} custom-call(bf16[128,128]{1,0:T(8,128)(2,1)S(1)} %add.7.term_ref, bf16[128,128]{1,0:T(8,128)(2,1)S(1)} %collective-permute-done.6.first_ref, bf16[128,128]{1,0:T(8,128)(2,1)S(1)} %collective-permute-done.7.second_ref, f32[32,128]{1,0:T(8,128)S(1)} %local_gram.1.gram_ref, f32[32,128]{1,0:T(8,128)S(1)} %collective-permute-done.9.got_gram_ref), custom_call_target="tpu_custom_call" | custom-call | tf_op jit(solution)/shard_map/finish/pallas_call | solution.py:348
  (4 shorter events, 0.1 us)
Async XLA Ops:
  0.0 7.4 %copy-start = (bf16[128,64]{0,1:T(8,128)(2,1)S(1)}, bf16[128,64]{0,1:T(8,128)(2,1)}, u32[]{:S(2)}) copy-start(bf16[128,64]{0,1:T(8,128)(2,1)} %param.5) | copy-start | bytes 49156
  5.1 2.3 %collective-permute-start = (bf16[128,1024]{1,0:T(8,128)(2,1)S(1)}, bf16[128,1024]{1,0:T(8,128)(2,1)S(1)}, u32[]{:S(2)}, u32[]{:S(2)}) collective-permute-start(bf16[128,1024]{1,0:T(8,128)(2,1)S(1)} %get-tuple-element.16), channel_id=1, source_target_pairs={{0,1},{1,0},{2,3},{3,2},{4,5},{5,4},{6,7},{7,6},{8,9},{9,8},{10,11... | collective-permute-start | bytes 786440 | tf_op jit(solution)/shard_map/ppermute | solution.py:369
  7.6 5.2 %collective-permute-start.2 = (bf16[256,128]{1,0:T(8,128)(2,1)S(1)}, bf16[256,128]{1,0:T(8,128)(2,1)S(1)}, u32[]{:S(2)}, u32[]{:S(2)}) collective-permute-start(bf16[256,128]{1,0:T(8,128)(2,1)S(1)} %get-tuple-element.20), channel_id=1, source_target_pairs={{0,3},{1,2},{2,1},{3,0},{4,7},{5,6},{6,5},{7,4},{8,11},{9,10},{10,... | collective-permute-start | bytes 196616 | tf_op jit(solution)/shard_map/ppermute | solution.py:369
  12.8 3.8 %collective-permute-start.3 = (bf16[256,128]{1,0:T(8,128)(2,1)S(1)}, bf16[256,128]{1,0:T(8,128)(2,1)S(1)}, u32[]{:S(2)}, u32[]{:S(2)}) collective-permute-start(bf16[256,128]{1,0:T(8,128)(2,1)S(1)} %add.4.mine_ref), channel_id=1, source_target_pairs={{0,5},{1,8},{2,11},{3,6},{4,13},{5,0},{6,3},{7,14},{8,1},{9,12},{1... | collective-permute-start | bytes 196616 | tf_op jit(solution)/shard_map/ppermute | solution.py:369
  14.2 5.1 %collective-permute-start.1 = (bf16[128,512]{1,0:T(8,128)(2,1)S(1)}, bf16[128,512]{1,0:T(8,128)(2,1)S(1)}, u32[]{:S(2)}, u32[]{:S(2)}) collective-permute-start(bf16[128,512]{1,0:T(8,128)(2,1)S(1)} %get-tuple-element.18), channel_id=1, source_target_pairs={{0,3},{1,2},{2,1},{3,0},{4,7},{5,6},{6,5},{7,4},{8,11},{9,10},{10,... | collective-permute-start | bytes 393224 | tf_op jit(solution)/shard_map/ppermute | solution.py:369
  16.5 4.7 %collective-permute-start.4 = (bf16[256,128]{1,0:T(8,128)(2,1)S(1)}, bf16[256,128]{1,0:T(8,128)(2,1)S(1)}, u32[]{:S(2)}, u32[]{:S(2)}) collective-permute-start(bf16[256,128]{1,0:T(8,128)(2,1)S(1)} %add.5.mine_ref), channel_id=1, source_target_pairs={{0,9},{1,4},{2,7},{3,10},{4,1},{5,12},{6,15},{7,2},{8,13},{9,0},{1... | collective-permute-start | bytes 196616 | tf_op jit(solution)/shard_map/ppermute | solution.py:369
  21.4 1.7 %collective-permute-start.5 = (bf16[128,128]{1,0:T(8,128)(2,1)S(1)}, bf16[128,128]{1,0:T(8,128)(2,1)S(1)}, u32[]{:S(2)}, u32[]{:S(2)}) collective-permute-start(bf16[128,128]{1,0:T(8,128)(2,1)S(1)} %product_terms.1.mine_ref), channel_id=1, source_target_pairs={{0,1},{1,0},{2,3},{3,2},{4,5},{5,4},{6,7},{7,6},{8,9},{9,8},{10,11... | collective-permute-start | bytes 98312 | tf_op jit(solution)/shard_map/ppermute | solution.py:369
  23.2 4.3 %collective-permute-start.8 = (bf16[128,128]{1,0:T(8,128)(2,1)S(1)}, bf16[128,128]{1,0:T(8,128)(2,1)S(1)}, u32[]{:S(2)}, u32[]{:S(2)}) collective-permute-start(bf16[128,128]{1,0:T(8,128)(2,1)S(1)} %add.7.term_ref), channel_id=1, source_target_pairs={{0,7},{1,6},{2,5},{3,4},{4,3},{5,2},{6,1},{7,0},{8,15},{9,14},{10,... | collective-permute-start | bytes 98312 | tf_op jit(solution)/shard_map/ppermute | solution.py:369
  25.8 3.4 %collective-permute-start.7 = (bf16[128,128]{1,0:T(8,128)(2,1)S(1)}, bf16[128,128]{1,0:T(8,128)(2,1)S(1)}, u32[]{:S(2)}, u32[]{:S(2)}) collective-permute-start(bf16[128,128]{1,0:T(8,128)(2,1)S(1)} %add.7.term_ref), channel_id=1, source_target_pairs={{0,5},{1,2},{2,1},{3,6},{4,7},{5,0},{6,3},{7,4},{8,11},{9,12},{10,... | collective-permute-start | bytes 98312 | tf_op jit(solution)/shard_map/ppermute | solution.py:369
  26.7 3.3 %collective-permute-start.6 = (bf16[128,128]{1,0:T(8,128)(2,1)S(1)}, bf16[128,128]{1,0:T(8,128)(2,1)S(1)}, u32[]{:S(2)}, u32[]{:S(2)}) collective-permute-start(bf16[128,128]{1,0:T(8,128)(2,1)S(1)} %add.7.term_ref), channel_id=1, source_target_pairs={{0,3},{1,4},{2,7},{3,0},{4,1},{5,6},{6,5},{7,2},{8,13},{9,10},{10,... | collective-permute-start | bytes 98312 | tf_op jit(solution)/shard_map/ppermute | solution.py:369
  30.3 4.1 %collective-permute-start.9 = (f32[32,128]{1,0:T(8,128)S(1)}, f32[32,128]{1,0:T(8,128)S(1)}, u32[]{:S(2)}, u32[]{:S(2)}) collective-permute-start(f32[32,128]{1,0:T(8,128)S(1)} %local_gram.1.gram_ref), channel_id=1, source_target_pairs={{0,9},{1,8},{2,11},{3,10},{4,13},{5,12},{6,15},{7,14},{8,1},{9,0},... | collective-permute-start | bytes 49160 | tf_op jit(solution)/shard_map/ppermute | solution.py:369

commit v30 on v29

--- a/solution.py
+++ b/solution.py
@@ -293,21 +293,26 @@
         if v >= count // 2:
             mine = jnp.concatenate([mine[:, rank:], mine[:, :rank]], axis=1)
         both.append(jnp.where(lane < rank, mine, (lane - rank == sublane + v * tile).astype(F32)))
+    def lanes(v, p):
+        return [full(both[v][:, p * tile + k:p * tile + k + 1]) for k in range(tile)]
+
+    slots = [0]
+
+    def spread(x, count):
+        at = slots[0] * tile
+        slots[0] += 1
+        spread_ref[pl.ds(at, tile), :] = x
+        return [full(spread_ref[pl.ds(at + j, 1), :]) for j in range(count)]
+
     pivots = []
+    diagonal = lanes(0, 0)
     for p in range(count):
-        cols = [
-            {v: full(both[v][:, p * tile + j:p * tile + j + 1]) for v in range(p, count)}
-            for j in range(tile)
-        ]
-        base = p * (tile + 1) * tile
-        spread_ref[pl.ds(base, tile), :] = both[p]
-        for k in range(tile):
-            spread_ref[pl.ds(base + (k + 1) * tile, tile), :] = cols[k][p]
-        rows = [full(spread_ref[pl.ds(base + j, 1), :]) for j in range(tile)]
-        block = [
-            [full(spread_ref[pl.ds(base + (k + 1) * tile + j, 1), :]) for k in range(j + 1)]
-            for j in range(tile)
-        ]
+        columns = [spread(diagonal[k], tile) for k in range(tile)]
+        block = [[columns[k][j] for k in range(j + 1)] for j in range(tile)]
+        rows = spread(both[p], tile)
+        below = range(p + 1, count)
+        cols = {v: lanes(v, p) for v in below}
+        diagonal = lanes(p + 1, p + 1) if below else []
         found, kept = block[0][0], rows[0]
         for j in range(tile):
             if j:
@@ -319,11 +324,15 @@
                 for k in range(j + 1, i + 1):
                     block[i][k] = block[i][k] - factor * block[k][j]
                 rows[i] = rows[i] - factor * rows[j]
+            if below:
+                column = cols[p + 1][j]
+                entries = spread(column, tile)
+                diagonal = [x - column * (e * inverse) for x, e in zip(diagonal, entries)]
             row = rows[j] * inverse
-            for v in range(p + 1, count):
+            for v in below:
                 for i, factor in scaled.items():
-                    cols[i][v] = cols[i][v] - factor * cols[j][v]
-                both[v] = both[v] - cols[j][v] * row
+                    cols[v][i] = cols[v][i] - factor * cols[v][j]
+                both[v] = both[v] - cols[v][j] * row
         both[p] = kept
         pivots.append(found)
     return both, pivots
@@ -348,7 +357,7 @@
     return pl.pallas_call(
         functools.partial(finish_kernel, total_rows),
         out_shape=jax.ShapeDtypeStruct((term.shape[1] // 2, LANES // 2), F32),
-        scratch_shapes=[pltpu.VMEM((LANES // 2 * 9, LANES), F32)],
+        scratch_shapes=[pltpu.VMEM((LANES // 2 * 17, LANES), F32)],
         compiler_params=params(4),
         name="finish",
     )(term, first, second, gram, got_gram)

time: 36.9 us -> 36.5 us (0.989)
  Pallas kernels: 10.1 us -> 9.69 us
    pallas_call x1, Pallas kernels: 2.34 us -> 1.92 us  [finish(): pl.pallas_call(functools.partial(finish_kernel, total_rows), out_shape=ja...]
where the time goes in v30:
time: 36.5 us; the launch traced here: 36.4 us
  starting transfers between devices  14.5 us (40%)
  waiting for transfers between devices  12.1 us (33%)
  Pallas kernels  9.69 us (27%)
    ppermute x10, starting transfers between devices, swap(): return lax.ppermute(x, ('row', 'col'), pairs)  14.5 us
    ppermute x10, waiting for transfers between devices, swap(): return lax.ppermute(x, ('row', 'col'), pairs)  12.1 us
    pallas_call x1, Pallas kernels, contract_send(): pl.pallas_call(send_kernel, in_specs=[pinned, pinned], out_shape=[jax.Sha...  5.08 us
    pallas_call x1, Pallas kernels, finish(): pl.pallas_call(functools.partial(finish_kernel, total_rows), out_shape=ja...  1.92 us
    pallas_call x1, Pallas kernels, contract_own(): pl.pallas_call(own_kernel, out_shape=jax.ShapeDtypeStruct((cells, half //...  1.77 us
  transfers between devices with their start and end apart: 10, of which 8 were waited for; matrix products, arithmetic and copies ran while one was open for 0% of the time, Pallas kernels for 5%

profile of v30, /device:TPU:0, one launch (start us, length us, event | category | flops | bytes accessed | tf_op | source)
XLA Modules:
  0.0 36.4 jit_solution(17061081973701227160)
XLA Ops:
  0.0 0.0 copy-start
  0.0 5.1 %contract_send.1 = (bf16[128,1024]{1,0:T(8,128)(2,1)S(1)}, bf16[128,16,1024]{2,1,0:T(8,128)(2,1)S(1)}, bf16[128,1024]{1,0:T(8,128)(2,1)S(1)}, bf16[64,256]{1,0:T(8,128)(2,1)S(1)}) custom-call(bf16[128,32,1024]{2,1,0:T(8,128)(2,1)} %snapshot_ref.1, bf16[64,1024]{1,0:T(8,128)(2,1)} %bitcast.4), custom_call_target="tpu_custom_call" | custom-call | tf_op jit(solution)/shard_map/contract_send/pallas_call | solution.py:128
  5.1 0.5 %collective-permute-start = (bf16[128,1024]{1,0:T(8,128)(2,1)S(1)}, bf16[128,1024]{1,0:T(8,128)(2,1)S(1)}, u32[]{:S(2)}, u32[]{:S(2)}) collective-permute-start(bf16[128,1024]{1,0:T(8,128)(2,1)S(1)} %get-tuple-element.16), channel_id=1, source_target_pairs={{0,1},{1,0},{2,3},{3,2},{4,5},{5,4},{6,7},{7,6},{8,9},{9,8},{10,11... | collective-permute-start | bytes 786440 | tf_op jit(solution)/shard_map/ppermute | solution.py:378
  5.6 1.8 %contract_own.1.own_ref = bf16[128,1024]{1,0:T(8,128)(2,1)S(1)} custom-call(bf16[128,16,1024]{2,1,0:T(8,128)(2,1)S(1)} %get-tuple-element.13.slab_ref, bf16[128,1024]{1,0:T(8,128)(2,1)S(1)} %get-tuple-element.14.wide_ref, bf16[64,256]{1,0:T(8,128)(2,1)S(1)} %get-tuple-element.15.order_ref), custom_call_target="tpu_custom_call" | custom-call | tf_op jit(solution)/shard_map/contract_own/pallas_call | solution.py:165
  7.4 0.0 collective-permute-done.got_ref
  7.4 0.0 copy-done
  7.4 0.2 project_sent.1
  7.6 2.7 %collective-permute-start.2 = (bf16[256,128]{1,0:T(8,128)(2,1)S(1)}, bf16[256,128]{1,0:T(8,128)(2,1)S(1)}, u32[]{:S(2)}, u32[]{:S(2)}) collective-permute-start(bf16[256,128]{1,0:T(8,128)(2,1)S(1)} %get-tuple-element.20), channel_id=1, source_target_pairs={{0,3},{1,2},{2,1},{3,0},{4,7},{5,6},{6,5},{7,4},{8,11},{9,10},{10,... | collective-permute-start | bytes 196616 | tf_op jit(solution)/shard_map/ppermute | solution.py:378
  10.3 0.2 project_kept.1
  10.5 2.3 %collective-permute-done.2.got_ref = bf16[256,128]{1,0:T(8,128)(2,1)S(1)} collective-permute-done((bf16[256,128]{1,0:T(8,128)(2,1)S(1)}, bf16[256,128]{1,0:T(8,128)(2,1)S(1)}, u32[]{:S(2)}, u32[]{:S(2)}) %collective-permute-start.2) | collective-permute-done | bytes 65568 | tf_op jit(solution)/shard_map/ppermute | solution.py:378
  12.8 1.4 %collective-permute-start.3 = (bf16[256,128]{1,0:T(8,128)(2,1)S(1)}, bf16[256,128]{1,0:T(8,128)(2,1)S(1)}, u32[]{:S(2)}, u32[]{:S(2)}) collective-permute-start(bf16[256,128]{1,0:T(8,128)(2,1)S(1)} %add.4.mine_ref), channel_id=1, source_target_pairs={{0,5},{1,8},{2,11},{3,6},{4,13},{5,0},{6,3},{7,14},{8,1},{9,12},{1... | collective-permute-start | bytes 196616 | tf_op jit(solution)/shard_map/ppermute | solution.py:378
  14.2 1.2 %collective-permute-start.1 = (bf16[128,512]{1,0:T(8,128)(2,1)S(1)}, bf16[128,512]{1,0:T(8,128)(2,1)S(1)}, u32[]{:S(2)}, u32[]{:S(2)}) collective-permute-start(bf16[128,512]{1,0:T(8,128)(2,1)S(1)} %get-tuple-element.18), channel_id=1, source_target_pairs={{0,3},{1,2},{2,1},{3,0},{4,7},{5,6},{6,5},{7,4},{8,11},{9,10},{10,... | collective-permute-start | bytes 393224 | tf_op jit(solution)/shard_map/ppermute | solution.py:378
  15.3 1.2 %collective-permute-done.3.got_ref = bf16[256,128]{1,0:T(8,128)(2,1)S(1)} collective-permute-done((bf16[256,128]{1,0:T(8,128)(2,1)S(1)}, bf16[256,128]{1,0:T(8,128)(2,1)S(1)}, u32[]{:S(2)}, u32[]{:S(2)}) %collective-permute-start.3) | collective-permute-done | bytes 65568 | tf_op jit(solution)/shard_map/ppermute | solution.py:378
  16.5 2.7 %collective-permute-start.4 = (bf16[256,128]{1,0:T(8,128)(2,1)S(1)}, bf16[256,128]{1,0:T(8,128)(2,1)S(1)}, u32[]{:S(2)}, u32[]{:S(2)}) collective-permute-start(bf16[256,128]{1,0:T(8,128)(2,1)S(1)} %add.5.mine_ref), channel_id=1, source_target_pairs={{0,9},{1,4},{2,7},{3,10},{4,1},{5,12},{6,15},{7,2},{8,13},{9,0},{1... | collective-permute-start | bytes 196616 | tf_op jit(solution)/shard_map/ppermute | solution.py:378
  19.2 0.0 collective-permute-done.1.refs_0_.got_ref
  19.2 2.0 %collective-permute-done.4.got_ref = bf16[256,128]{1,0:T(8,128)(2,1)S(1)} collective-permute-done((bf16[256,128]{1,0:T(8,128)(2,1)S(1)}, bf16[256,128]{1,0:T(8,128)(2,1)S(1)}, u32[]{:S(2)}, u32[]{:S(2)}) %collective-permute-start.4) | collective-permute-done | bytes 65568 | tf_op jit(solution)/shard_map/ppermute | solution.py:378
  21.2 0.2 product_terms.1.mine_ref
  21.4 0.9 %collective-permute-start.5 = (bf16[128,128]{1,0:T(8,128)(2,1)S(1)}, bf16[128,128]{1,0:T(8,128)(2,1)S(1)}, u32[]{:S(2)}, u32[]{:S(2)}) collective-permute-start(bf16[128,128]{1,0:T(8,128)(2,1)S(1)} %product_terms.1.mine_ref), channel_id=1, source_target_pairs={{0,1},{1,0},{2,3},{3,2},{4,5},{5,4},{6,7},{7,6},{8,9},{9,8},{10,11... | collective-permute-start | bytes 98312 | tf_op jit(solution)/shard_map/ppermute | solution.py:378
  22.3 0.9 %collective-permute-done.5.got_ref = bf16[128,128]{1,0:T(8,128)(2,1)S(1)} collective-permute-done((bf16[128,128]{1,0:T(8,128)(2,1)S(1)}, bf16[128,128]{1,0:T(8,128)(2,1)S(1)}, u32[]{:S(2)}, u32[]{:S(2)}) %collective-permute-start.5) | collective-permute-done | bytes 32800 | tf_op jit(solution)/shard_map/ppermute | solution.py:378
  23.2 2.6 %collective-permute-start.8 = (bf16[128,128]{1,0:T(8,128)(2,1)S(1)}, bf16[128,128]{1,0:T(8,128)(2,1)S(1)}, u32[]{:S(2)}, u32[]{:S(2)}) collective-permute-start(bf16[128,128]{1,0:T(8,128)(2,1)S(1)} %add.7.term_ref), channel_id=1, source_target_pairs={{0,7},{1,6},{2,5},{3,4},{4,3},{5,2},{6,1},{7,0},{8,15},{9,14},{10,... | collective-permute-start | bytes 98312 | tf_op jit(solution)/shard_map/ppermute | solution.py:378
  25.8 0.9 %collective-permute-start.7 = (bf16[128,128]{1,0:T(8,128)(2,1)S(1)}, bf16[128,128]{1,0:T(8,128)(2,1)S(1)}, u32[]{:S(2)}, u32[]{:S(2)}) collective-permute-start(bf16[128,128]{1,0:T(8,128)(2,1)S(1)} %add.7.term_ref), channel_id=1, source_target_pairs={{0,5},{1,2},{2,1},{3,6},{4,7},{5,0},{6,3},{7,4},{8,11},{9,12},{10,... | collective-permute-start | bytes 98312 | tf_op jit(solution)/shard_map/ppermute | solution.py:378
  26.7 0.0 collective-permute-start.6
  26.7 0.8 %collective-permute-done.8.last_ref = bf16[128,128]{1,0:T(8,128)(2,1)S(1)} collective-permute-done((bf16[128,128]{1,0:T(8,128)(2,1)S(1)}, bf16[128,128]{1,0:T(8,128)(2,1)S(1)}, u32[]{:S(2)}, u32[]{:S(2)}) %collective-permute-start.8) | collective-permute-done | bytes 32800 | tf_op jit(solution)/shard_map/ppermute | solution.py:378
  27.5 1.7 %collective-permute-done.7.second_ref = bf16[128,128]{1,0:T(8,128)(2,1)S(1)} collective-permute-done((bf16[128,128]{1,0:T(8,128)(2,1)S(1)}, bf16[128,128]{1,0:T(8,128)(2,1)S(1)}, u32[]{:S(2)}, u32[]{:S(2)}) %collective-permute-start.7) | collective-permute-done | bytes 32800 | tf_op jit(solution)/shard_map/ppermute | solution.py:378
  29.2 0.9 %collective-permute-done.6.first_ref = bf16[128,128]{1,0:T(8,128)(2,1)S(1)} collective-permute-done((bf16[128,128]{1,0:T(8,128)(2,1)S(1)}, bf16[128,128]{1,0:T(8,128)(2,1)S(1)}, u32[]{:S(2)}, u32[]{:S(2)}) %collective-permute-start.6) | collective-permute-done | bytes 32800 | tf_op jit(solution)/shard_map/ppermute | solution.py:378
  30.0 0.3 local_gram.1.gram_ref
  30.3 1.7 %collective-permute-start.9 = (f32[32,128]{1,0:T(8,128)S(1)}, f32[32,128]{1,0:T(8,128)S(1)}, u32[]{:S(2)}, u32[]{:S(2)}) collective-permute-start(f32[32,128]{1,0:T(8,128)S(1)} %local_gram.1.gram_ref), channel_id=1, source_target_pairs={{0,9},{1,8},{2,11},{3,10},{4,13},{5,12},{6,15},{7,14},{8,1},{9,0},... | collective-permute-start | bytes 49160 | tf_op jit(solution)/shard_map/ppermute | solution.py:378
  32.0 2.5 %collective-permute-done.9.got_gram_ref = f32[32,128]{1,0:T(8,128)S(1)} collective-permute-done((f32[32,128]{1,0:T(8,128)S(1)}, f32[32,128]{1,0:T(8,128)S(1)}, u32[]{:S(2)}, u32[]{:S(2)}) %collective-permute-start.9) | collective-permute-done | bytes 16416 | tf_op jit(solution)/shard_map/ppermute | solution.py:378
  34.4 1.9 %finish.1 = f32[64,64]{1,0:T(8,128)} custom-call(bf16[128,128]{1,0:T(8,128)(2,1)S(1)} %add.7.term_ref, bf16[128,128]{1,0:T(8,128)(2,1)S(1)} %collective-permute-done.6.first_ref, bf16[128,128]{1,0:T(8,128)(2,1)S(1)} %collective-permute-done.7.second_ref, f32[32,128]{1,0:T(8,128)S(1)} %local_gram.1.gram_ref, f32[32,128]{1,0:T(8,128)S(1)} %collective-permute-done.9.got_gram_ref), custom_call_target="tpu_custom_call" | custom-call | tf_op jit(solution)/shard_map/finish/pallas_call | solution.py:357
  (4 shorter events, 0.1 us)
Async XLA Ops:
  0.0 7.4 %copy-start = (bf16[128,64]{0,1:T(8,128)(2,1)S(1)}, bf16[128,64]{0,1:T(8,128)(2,1)}, u32[]{:S(2)}) copy-start(bf16[128,64]{0,1:T(8,128)(2,1)} %param.5) | copy-start | bytes 49156
  5.1 2.3 %collective-permute-start = (bf16[128,1024]{1,0:T(8,128)(2,1)S(1)}, bf16[128,1024]{1,0:T(8,128)(2,1)S(1)}, u32[]{:S(2)}, u32[]{:S(2)}) collective-permute-start(bf16[128,1024]{1,0:T(8,128)(2,1)S(1)} %get-tuple-element.16), channel_id=1, source_target_pairs={{0,1},{1,0},{2,3},{3,2},{4,5},{5,4},{6,7},{7,6},{8,9},{9,8},{10,11... | collective-permute-start | bytes 786440 | tf_op jit(solution)/shard_map/ppermute | solution.py:378
  7.6 5.2 %collective-permute-start.2 = (bf16[256,128]{1,0:T(8,128)(2,1)S(1)}, bf16[256,128]{1,0:T(8,128)(2,1)S(1)}, u32[]{:S(2)}, u32[]{:S(2)}) collective-permute-start(bf16[256,128]{1,0:T(8,128)(2,1)S(1)} %get-tuple-element.20), channel_id=1, source_target_pairs={{0,3},{1,2},{2,1},{3,0},{4,7},{5,6},{6,5},{7,4},{8,11},{9,10},{10,... | collective-permute-start | bytes 196616 | tf_op jit(solution)/shard_map/ppermute | solution.py:378
  12.8 3.8 %collective-permute-start.3 = (bf16[256,128]{1,0:T(8,128)(2,1)S(1)}, bf16[256,128]{1,0:T(8,128)(2,1)S(1)}, u32[]{:S(2)}, u32[]{:S(2)}) collective-permute-start(bf16[256,128]{1,0:T(8,128)(2,1)S(1)} %add.4.mine_ref), channel_id=1, source_target_pairs={{0,5},{1,8},{2,11},{3,6},{4,13},{5,0},{6,3},{7,14},{8,1},{9,12},{1... | collective-permute-start | bytes 196616 | tf_op jit(solution)/shard_map/ppermute | solution.py:378
  14.2 5.1 %collective-permute-start.1 = (bf16[128,512]{1,0:T(8,128)(2,1)S(1)}, bf16[128,512]{1,0:T(8,128)(2,1)S(1)}, u32[]{:S(2)}, u32[]{:S(2)}) collective-permute-start(bf16[128,512]{1,0:T(8,128)(2,1)S(1)} %get-tuple-element.18), channel_id=1, source_target_pairs={{0,3},{1,2},{2,1},{3,0},{4,7},{5,6},{6,5},{7,4},{8,11},{9,10},{10,... | collective-permute-start | bytes 393224 | tf_op jit(solution)/shard_map/ppermute | solution.py:378
  16.5 4.7 %collective-permute-start.4 = (bf16[256,128]{1,0:T(8,128)(2,1)S(1)}, bf16[256,128]{1,0:T(8,128)(2,1)S(1)}, u32[]{:S(2)}, u32[]{:S(2)}) collective-permute-start(bf16[256,128]{1,0:T(8,128)(2,1)S(1)} %add.5.mine_ref), channel_id=1, source_target_pairs={{0,9},{1,4},{2,7},{3,10},{4,1},{5,12},{6,15},{7,2},{8,13},{9,0},{1... | collective-permute-start | bytes 196616 | tf_op jit(solution)/shard_map/ppermute | solution.py:378
  21.4 1.7 %collective-permute-start.5 = (bf16[128,128]{1,0:T(8,128)(2,1)S(1)}, bf16[128,128]{1,0:T(8,128)(2,1)S(1)}, u32[]{:S(2)}, u32[]{:S(2)}) collective-permute-start(bf16[128,128]{1,0:T(8,128)(2,1)S(1)} %product_terms.1.mine_ref), channel_id=1, source_target_pairs={{0,1},{1,0},{2,3},{3,2},{4,5},{5,4},{6,7},{7,6},{8,9},{9,8},{10,11... | collective-permute-start | bytes 98312 | tf_op jit(solution)/shard_map/ppermute | solution.py:378
  23.2 4.3 %collective-permute-start.8 = (bf16[128,128]{1,0:T(8,128)(2,1)S(1)}, bf16[128,128]{1,0:T(8,128)(2,1)S(1)}, u32[]{:S(2)}, u32[]{:S(2)}) collective-permute-start(bf16[128,128]{1,0:T(8,128)(2,1)S(1)} %add.7.term_ref), channel_id=1, source_target_pairs={{0,7},{1,6},{2,5},{3,4},{4,3},{5,2},{6,1},{7,0},{8,15},{9,14},{10,... | collective-permute-start | bytes 98312 | tf_op jit(solution)/shard_map/ppermute | solution.py:378
  25.8 3.4 %collective-permute-start.7 = (bf16[128,128]{1,0:T(8,128)(2,1)S(1)}, bf16[128,128]{1,0:T(8,128)(2,1)S(1)}, u32[]{:S(2)}, u32[]{:S(2)}) collective-permute-start(bf16[128,128]{1,0:T(8,128)(2,1)S(1)} %add.7.term_ref), channel_id=1, source_target_pairs={{0,5},{1,2},{2,1},{3,6},{4,7},{5,0},{6,3},{7,4},{8,11},{9,12},{10,... | collective-permute-start | bytes 98312 | tf_op jit(solution)/shard_map/ppermute | solution.py:378
  26.7 3.3 %collective-permute-start.6 = (bf16[128,128]{1,0:T(8,128)(2,1)S(1)}, bf16[128,128]{1,0:T(8,128)(2,1)S(1)}, u32[]{:S(2)}, u32[]{:S(2)}) collective-permute-start(bf16[128,128]{1,0:T(8,128)(2,1)S(1)} %add.7.term_ref), channel_id=1, source_target_pairs={{0,3},{1,4},{2,7},{3,0},{4,1},{5,6},{6,5},{7,2},{8,13},{9,10},{10,... | collective-permute-start | bytes 98312 | tf_op jit(solution)/shard_map/ppermute | solution.py:378
  30.3 4.1 %collective-permute-start.9 = (f32[32,128]{1,0:T(8,128)S(1)}, f32[32,128]{1,0:T(8,128)S(1)}, u32[]{:S(2)}, u32[]{:S(2)}) collective-permute-start(f32[32,128]{1,0:T(8,128)S(1)} %local_gram.1.gram_ref), channel_id=1, source_target_pairs={{0,9},{1,8},{2,11},{3,10},{4,13},{5,12},{6,15},{7,14},{8,1},{9,0},... | collective-permute-start | bytes 49160 | tf_op jit(solution)/shard_map/ppermute | solution.py:378

commit v31 on v30

--- a/solution.py
+++ b/solution.py
@@ -322,12 +322,16 @@
             scaled = {i: block[i][j] * inverse for i in range(j + 1, tile)}
             for i, factor in scaled.items():
                 for k in range(j + 1, i + 1):
-                    block[i][k] = block[i][k] - factor * block[k][j]
+                    if i == j + 1:
+                        update = block[i][j] * block[k][j] * inverse
+                    else:
+                        update = factor * block[k][j]
+                    block[i][k] = block[i][k] - update
                 rows[i] = rows[i] - factor * rows[j]
             if below:
                 column = cols[p + 1][j]
                 entries = spread(column, tile)
-                diagonal = [x - column * (e * inverse) for x, e in zip(diagonal, entries)]
+                diagonal = [x - column * e * inverse for x, e in zip(diagonal, entries)]
             row = rows[j] * inverse
             for v in below:
                 for i, factor in scaled.items():

time: 36.5 us -> 36.5 us (level)
  no operation moved by 1% of the time
where the time goes in v31:
time: 36.5 us; the launch traced here: 36.3 us
  starting transfers between devices  14.5 us (40%)
  waiting for transfers between devices  12.1 us (33%)
  Pallas kernels  9.64 us (26%)
    ppermute x10, starting transfers between devices, swap(): return lax.ppermute(x, ('row', 'col'), pairs)  14.5 us
    ppermute x10, waiting for transfers between devices, swap(): return lax.ppermute(x, ('row', 'col'), pairs)  12.1 us
    pallas_call x1, Pallas kernels, contract_send(): pl.pallas_call(send_kernel, in_specs=[pinned, pinned], out_shape=[jax.Sha...  5.08 us
    pallas_call x1, Pallas kernels, finish(): pl.pallas_call(functools.partial(finish_kernel, total_rows), out_shape=ja...  1.87 us
    pallas_call x1, Pallas kernels, contract_own(): pl.pallas_call(own_kernel, out_shape=jax.ShapeDtypeStruct((cells, half //...  1.77 us
  transfers between devices with their start and end apart: 10, of which 8 were waited for; matrix products, arithmetic and copies ran while one was open for 0% of the time, Pallas kernels for 5%

profile of v31, /device:TPU:0, one launch (start us, length us, event | category | flops | bytes accessed | tf_op | source)
XLA Modules:
  0.0 36.3 jit_solution(15251369960542332340)
XLA Ops:
  0.0 0.0 copy-start
  0.0 5.1 %contract_send.1 = (bf16[128,1024]{1,0:T(8,128)(2,1)S(1)}, bf16[128,16,1024]{2,1,0:T(8,128)(2,1)S(1)}, bf16[128,1024]{1,0:T(8,128)(2,1)S(1)}, bf16[64,256]{1,0:T(8,128)(2,1)S(1)}) custom-call(bf16[128,32,1024]{2,1,0:T(8,128)(2,1)} %snapshot_ref.1, bf16[64,1024]{1,0:T(8,128)(2,1)} %bitcast.4), custom_call_target="tpu_custom_call" | custom-call | tf_op jit(solution)/shard_map/contract_send/pallas_call | solution.py:128
  5.1 0.5 %collective-permute-start = (bf16[128,1024]{1,0:T(8,128)(2,1)S(1)}, bf16[128,1024]{1,0:T(8,128)(2,1)S(1)}, u32[]{:S(2)}, u32[]{:S(2)}) collective-permute-start(bf16[128,1024]{1,0:T(8,128)(2,1)S(1)} %get-tuple-element.16), channel_id=1, source_target_pairs={{0,1},{1,0},{2,3},{3,2},{4,5},{5,4},{6,7},{7,6},{8,9},{9,8},{10,11... | collective-permute-start | bytes 786440 | tf_op jit(solution)/shard_map/ppermute | solution.py:382
  5.6 1.8 %contract_own.1.own_ref = bf16[128,1024]{1,0:T(8,128)(2,1)S(1)} custom-call(bf16[128,16,1024]{2,1,0:T(8,128)(2,1)S(1)} %get-tuple-element.13.slab_ref, bf16[128,1024]{1,0:T(8,128)(2,1)S(1)} %get-tuple-element.14.wide_ref, bf16[64,256]{1,0:T(8,128)(2,1)S(1)} %get-tuple-element.15.order_ref), custom_call_target="tpu_custom_call" | custom-call | tf_op jit(solution)/shard_map/contract_own/pallas_call | solution.py:165
  7.4 0.0 collective-permute-done.got_ref
  7.4 0.0 copy-done
  7.4 0.2 project_sent.1
  7.6 2.7 %collective-permute-start.2 = (bf16[256,128]{1,0:T(8,128)(2,1)S(1)}, bf16[256,128]{1,0:T(8,128)(2,1)S(1)}, u32[]{:S(2)}, u32[]{:S(2)}) collective-permute-start(bf16[256,128]{1,0:T(8,128)(2,1)S(1)} %get-tuple-element.20), channel_id=1, source_target_pairs={{0,3},{1,2},{2,1},{3,0},{4,7},{5,6},{6,5},{7,4},{8,11},{9,10},{10,... | collective-permute-start | bytes 196616 | tf_op jit(solution)/shard_map/ppermute | solution.py:382
  10.3 0.2 project_kept.1
  10.5 2.3 %collective-permute-done.2.got_ref = bf16[256,128]{1,0:T(8,128)(2,1)S(1)} collective-permute-done((bf16[256,128]{1,0:T(8,128)(2,1)S(1)}, bf16[256,128]{1,0:T(8,128)(2,1)S(1)}, u32[]{:S(2)}, u32[]{:S(2)}) %collective-permute-start.2) | collective-permute-done | bytes 65568 | tf_op jit(solution)/shard_map/ppermute | solution.py:382
  12.8 1.4 %collective-permute-start.3 = (bf16[256,128]{1,0:T(8,128)(2,1)S(1)}, bf16[256,128]{1,0:T(8,128)(2,1)S(1)}, u32[]{:S(2)}, u32[]{:S(2)}) collective-permute-start(bf16[256,128]{1,0:T(8,128)(2,1)S(1)} %add.4.mine_ref), channel_id=1, source_target_pairs={{0,5},{1,8},{2,11},{3,6},{4,13},{5,0},{6,3},{7,14},{8,1},{9,12},{1... | collective-permute-start | bytes 196616 | tf_op jit(solution)/shard_map/ppermute | solution.py:382
  14.2 1.2 %collective-permute-start.1 = (bf16[128,512]{1,0:T(8,128)(2,1)S(1)}, bf16[128,512]{1,0:T(8,128)(2,1)S(1)}, u32[]{:S(2)}, u32[]{:S(2)}) collective-permute-start(bf16[128,512]{1,0:T(8,128)(2,1)S(1)} %get-tuple-element.18), channel_id=1, source_target_pairs={{0,3},{1,2},{2,1},{3,0},{4,7},{5,6},{6,5},{7,4},{8,11},{9,10},{10,... | collective-permute-start | bytes 393224 | tf_op jit(solution)/shard_map/ppermute | solution.py:382
  15.3 1.2 %collective-permute-done.3.got_ref = bf16[256,128]{1,0:T(8,128)(2,1)S(1)} collective-permute-done((bf16[256,128]{1,0:T(8,128)(2,1)S(1)}, bf16[256,128]{1,0:T(8,128)(2,1)S(1)}, u32[]{:S(2)}, u32[]{:S(2)}) %collective-permute-start.3) | collective-permute-done | bytes 65568 | tf_op jit(solution)/shard_map/ppermute | solution.py:382
  16.5 2.7 %collective-permute-start.4 = (bf16[256,128]{1,0:T(8,128)(2,1)S(1)}, bf16[256,128]{1,0:T(8,128)(2,1)S(1)}, u32[]{:S(2)}, u32[]{:S(2)}) collective-permute-start(bf16[256,128]{1,0:T(8,128)(2,1)S(1)} %add.5.mine_ref), channel_id=1, source_target_pairs={{0,9},{1,4},{2,7},{3,10},{4,1},{5,12},{6,15},{7,2},{8,13},{9,0},{1... | collective-permute-start | bytes 196616 | tf_op jit(solution)/shard_map/ppermute | solution.py:382
  19.2 0.0 collective-permute-done.1.refs_0_.got_ref
  19.2 2.0 %collective-permute-done.4.got_ref = bf16[256,128]{1,0:T(8,128)(2,1)S(1)} collective-permute-done((bf16[256,128]{1,0:T(8,128)(2,1)S(1)}, bf16[256,128]{1,0:T(8,128)(2,1)S(1)}, u32[]{:S(2)}, u32[]{:S(2)}) %collective-permute-start.4) | collective-permute-done | bytes 65568 | tf_op jit(solution)/shard_map/ppermute | solution.py:382
  21.2 0.2 product_terms.1.mine_ref
  21.4 0.9 %collective-permute-start.5 = (bf16[128,128]{1,0:T(8,128)(2,1)S(1)}, bf16[128,128]{1,0:T(8,128)(2,1)S(1)}, u32[]{:S(2)}, u32[]{:S(2)}) collective-permute-start(bf16[128,128]{1,0:T(8,128)(2,1)S(1)} %product_terms.1.mine_ref), channel_id=1, source_target_pairs={{0,1},{1,0},{2,3},{3,2},{4,5},{5,4},{6,7},{7,6},{8,9},{9,8},{10,11... | collective-permute-start | bytes 98312 | tf_op jit(solution)/shard_map/ppermute | solution.py:382
  22.3 0.9 %collective-permute-done.5.got_ref = bf16[128,128]{1,0:T(8,128)(2,1)S(1)} collective-permute-done((bf16[128,128]{1,0:T(8,128)(2,1)S(1)}, bf16[128,128]{1,0:T(8,128)(2,1)S(1)}, u32[]{:S(2)}, u32[]{:S(2)}) %collective-permute-start.5) | collective-permute-done | bytes 32800 | tf_op jit(solution)/shard_map/ppermute | solution.py:382
  23.2 2.6 %collective-permute-start.8 = (bf16[128,128]{1,0:T(8,128)(2,1)S(1)}, bf16[128,128]{1,0:T(8,128)(2,1)S(1)}, u32[]{:S(2)}, u32[]{:S(2)}) collective-permute-start(bf16[128,128]{1,0:T(8,128)(2,1)S(1)} %add.7.term_ref), channel_id=1, source_target_pairs={{0,7},{1,6},{2,5},{3,4},{4,3},{5,2},{6,1},{7,0},{8,15},{9,14},{10,... | collective-permute-start | bytes 98312 | tf_op jit(solution)/shard_map/ppermute | solution.py:382
  25.8 0.9 %collective-permute-start.7 = (bf16[128,128]{1,0:T(8,128)(2,1)S(1)}, bf16[128,128]{1,0:T(8,128)(2,1)S(1)}, u32[]{:S(2)}, u32[]{:S(2)}) collective-permute-start(bf16[128,128]{1,0:T(8,128)(2,1)S(1)} %add.7.term_ref), channel_id=1, source_target_pairs={{0,5},{1,2},{2,1},{3,6},{4,7},{5,0},{6,3},{7,4},{8,11},{9,12},{10,... | collective-permute-start | bytes 98312 | tf_op jit(solution)/shard_map/ppermute | solution.py:382
  26.7 0.0 collective-permute-start.6
  26.7 0.8 %collective-permute-done.8.last_ref = bf16[128,128]{1,0:T(8,128)(2,1)S(1)} collective-permute-done((bf16[128,128]{1,0:T(8,128)(2,1)S(1)}, bf16[128,128]{1,0:T(8,128)(2,1)S(1)}, u32[]{:S(2)}, u32[]{:S(2)}) %collective-permute-start.8) | collective-permute-done | bytes 32800 | tf_op jit(solution)/shard_map/ppermute | solution.py:382
  27.5 1.7 %collective-permute-done.7.second_ref = bf16[128,128]{1,0:T(8,128)(2,1)S(1)} collective-permute-done((bf16[128,128]{1,0:T(8,128)(2,1)S(1)}, bf16[128,128]{1,0:T(8,128)(2,1)S(1)}, u32[]{:S(2)}, u32[]{:S(2)}) %collective-permute-start.7) | collective-permute-done | bytes 32800 | tf_op jit(solution)/shard_map/ppermute | solution.py:382
  29.2 0.9 %collective-permute-done.6.first_ref = bf16[128,128]{1,0:T(8,128)(2,1)S(1)} collective-permute-done((bf16[128,128]{1,0:T(8,128)(2,1)S(1)}, bf16[128,128]{1,0:T(8,128)(2,1)S(1)}, u32[]{:S(2)}, u32[]{:S(2)}) %collective-permute-start.6) | collective-permute-done | bytes 32800 | tf_op jit(solution)/shard_map/ppermute | solution.py:382
  30.0 0.3 local_gram.1.gram_ref
  30.3 1.7 %collective-permute-start.9 = (f32[32,128]{1,0:T(8,128)S(1)}, f32[32,128]{1,0:T(8,128)S(1)}, u32[]{:S(2)}, u32[]{:S(2)}) collective-permute-start(f32[32,128]{1,0:T(8,128)S(1)} %local_gram.1.gram_ref), channel_id=1, source_target_pairs={{0,9},{1,8},{2,11},{3,10},{4,13},{5,12},{6,15},{7,14},{8,1},{9,0},... | collective-permute-start | bytes 49160 | tf_op jit(solution)/shard_map/ppermute | solution.py:382
  32.0 2.5 %collective-permute-done.9.got_gram_ref = f32[32,128]{1,0:T(8,128)S(1)} collective-permute-done((f32[32,128]{1,0:T(8,128)S(1)}, f32[32,128]{1,0:T(8,128)S(1)}, u32[]{:S(2)}, u32[]{:S(2)}) %collective-permute-start.9) | collective-permute-done | bytes 16416 | tf_op jit(solution)/shard_map/ppermute | solution.py:382
  34.4 1.9 %finish.1 = f32[64,64]{1,0:T(8,128)} custom-call(bf16[128,128]{1,0:T(8,128)(2,1)S(1)} %add.7.term_ref, bf16[128,128]{1,0:T(8,128)(2,1)S(1)} %collective-permute-done.6.first_ref, bf16[128,128]{1,0:T(8,128)(2,1)S(1)} %collective-permute-done.7.second_ref, f32[32,128]{1,0:T(8,128)S(1)} %local_gram.1.gram_ref, f32[32,128]{1,0:T(8,128)S(1)} %collective-permute-done.9.got_gram_ref), custom_call_target="tpu_custom_call" | custom-call | tf_op jit(solution)/shard_map/finish/pallas_call | solution.py:361
  (4 shorter events, 0.1 us)
Async XLA Ops:
  0.0 7.4 %copy-start = (bf16[128,64]{0,1:T(8,128)(2,1)S(1)}, bf16[128,64]{0,1:T(8,128)(2,1)}, u32[]{:S(2)}) copy-start(bf16[128,64]{0,1:T(8,128)(2,1)} %param.5) | copy-start | bytes 49156
  5.1 2.3 %collective-permute-start = (bf16[128,1024]{1,0:T(8,128)(2,1)S(1)}, bf16[128,1024]{1,0:T(8,128)(2,1)S(1)}, u32[]{:S(2)}, u32[]{:S(2)}) collective-permute-start(bf16[128,1024]{1,0:T(8,128)(2,1)S(1)} %get-tuple-element.16), channel_id=1, source_target_pairs={{0,1},{1,0},{2,3},{3,2},{4,5},{5,4},{6,7},{7,6},{8,9},{9,8},{10,11... | collective-permute-start | bytes 786440 | tf_op jit(solution)/shard_map/ppermute | solution.py:382
  7.6 5.2 %collective-permute-start.2 = (bf16[256,128]{1,0:T(8,128)(2,1)S(1)}, bf16[256,128]{1,0:T(8,128)(2,1)S(1)}, u32[]{:S(2)}, u32[]{:S(2)}) collective-permute-start(bf16[256,128]{1,0:T(8,128)(2,1)S(1)} %get-tuple-element.20), channel_id=1, source_target_pairs={{0,3},{1,2},{2,1},{3,0},{4,7},{5,6},{6,5},{7,4},{8,11},{9,10},{10,... | collective-permute-start | bytes 196616 | tf_op jit(solution)/shard_map/ppermute | solution.py:382
  12.8 3.8 %collective-permute-start.3 = (bf16[256,128]{1,0:T(8,128)(2,1)S(1)}, bf16[256,128]{1,0:T(8,128)(2,1)S(1)}, u32[]{:S(2)}, u32[]{:S(2)}) collective-permute-start(bf16[256,128]{1,0:T(8,128)(2,1)S(1)} %add.4.mine_ref), channel_id=1, source_target_pairs={{0,5},{1,8},{2,11},{3,6},{4,13},{5,0},{6,3},{7,14},{8,1},{9,12},{1... | collective-permute-start | bytes 196616 | tf_op jit(solution)/shard_map/ppermute | solution.py:382
  14.2 5.1 %collective-permute-start.1 = (bf16[128,512]{1,0:T(8,128)(2,1)S(1)}, bf16[128,512]{1,0:T(8,128)(2,1)S(1)}, u32[]{:S(2)}, u32[]{:S(2)}) collective-permute-start(bf16[128,512]{1,0:T(8,128)(2,1)S(1)} %get-tuple-element.18), channel_id=1, source_target_pairs={{0,3},{1,2},{2,1},{3,0},{4,7},{5,6},{6,5},{7,4},{8,11},{9,10},{10,... | collective-permute-start | bytes 393224 | tf_op jit(solution)/shard_map/ppermute | solution.py:382
  16.5 4.7 %collective-permute-start.4 = (bf16[256,128]{1,0:T(8,128)(2,1)S(1)}, bf16[256,128]{1,0:T(8,128)(2,1)S(1)}, u32[]{:S(2)}, u32[]{:S(2)}) collective-permute-start(bf16[256,128]{1,0:T(8,128)(2,1)S(1)} %add.5.mine_ref), channel_id=1, source_target_pairs={{0,9},{1,4},{2,7},{3,10},{4,1},{5,12},{6,15},{7,2},{8,13},{9,0},{1... | collective-permute-start | bytes 196616 | tf_op jit(solution)/shard_map/ppermute | solution.py:382
  21.4 1.7 %collective-permute-start.5 = (bf16[128,128]{1,0:T(8,128)(2,1)S(1)}, bf16[128,128]{1,0:T(8,128)(2,1)S(1)}, u32[]{:S(2)}, u32[]{:S(2)}) collective-permute-start(bf16[128,128]{1,0:T(8,128)(2,1)S(1)} %product_terms.1.mine_ref), channel_id=1, source_target_pairs={{0,1},{1,0},{2,3},{3,2},{4,5},{5,4},{6,7},{7,6},{8,9},{9,8},{10,11... | collective-permute-start | bytes 98312 | tf_op jit(solution)/shard_map/ppermute | solution.py:382
  23.2 4.3 %collective-permute-start.8 = (bf16[128,128]{1,0:T(8,128)(2,1)S(1)}, bf16[128,128]{1,0:T(8,128)(2,1)S(1)}, u32[]{:S(2)}, u32[]{:S(2)}) collective-permute-start(bf16[128,128]{1,0:T(8,128)(2,1)S(1)} %add.7.term_ref), channel_id=1, source_target_pairs={{0,7},{1,6},{2,5},{3,4},{4,3},{5,2},{6,1},{7,0},{8,15},{9,14},{10,... | collective-permute-start | bytes 98312 | tf_op jit(solution)/shard_map/ppermute | solution.py:382
  25.8 3.4 %collective-permute-start.7 = (bf16[128,128]{1,0:T(8,128)(2,1)S(1)}, bf16[128,128]{1,0:T(8,128)(2,1)S(1)}, u32[]{:S(2)}, u32[]{:S(2)}) collective-permute-start(bf16[128,128]{1,0:T(8,128)(2,1)S(1)} %add.7.term_ref), channel_id=1, source_target_pairs={{0,5},{1,2},{2,1},{3,6},{4,7},{5,0},{6,3},{7,4},{8,11},{9,12},{10,... | collective-permute-start | bytes 98312 | tf_op jit(solution)/shard_map/ppermute | solution.py:382
  26.7 3.3 %collective-permute-start.6 = (bf16[128,128]{1,0:T(8,128)(2,1)S(1)}, bf16[128,128]{1,0:T(8,128)(2,1)S(1)}, u32[]{:S(2)}, u32[]{:S(2)}) collective-permute-start(bf16[128,128]{1,0:T(8,128)(2,1)S(1)} %add.7.term_ref), channel_id=1, source_target_pairs={{0,3},{1,4},{2,7},{3,0},{4,1},{5,6},{6,5},{7,2},{8,13},{9,10},{10,... | collective-permute-start | bytes 98312 | tf_op jit(solution)/shard_map/ppermute | solution.py:382
  30.3 4.1 %collective-permute-start.9 = (f32[32,128]{1,0:T(8,128)S(1)}, f32[32,128]{1,0:T(8,128)S(1)}, u32[]{:S(2)}, u32[]{:S(2)}) collective-permute-start(f32[32,128]{1,0:T(8,128)S(1)} %local_gram.1.gram_ref), channel_id=1, source_target_pairs={{0,9},{1,8},{2,11},{3,10},{4,13},{5,12},{6,15},{7,14},{8,1},{9,0},... | collective-permute-start | bytes 49160 | tf_op jit(solution)/shard_map/ppermute | solution.py:382

commit v32 on v30

--- a/solution.py
+++ b/solution.py
@@ -87,8 +87,8 @@
 
 
 def send_kernel(
-    snapshot_ref, mode2_ref, core_ref, kept_ref, wide_ref, order_ref,
-    slab_ref, small_ref, even_ref, odd_ref, sems, kept_sem, small_sem,
+    snapshot_ref, mode2_ref, core_ref, kept_ref, part_ref, wide_ref, order_ref,
+    slab_ref, small_ref, even_ref, odd_ref, sems, kept_sems, small_sem,
 ):
     cells, half, _ = slab_ref.shape
     rank = mode2_ref.shape[0]
@@ -98,7 +98,9 @@
         slab_copies(snapshot_ref, 0, slab_ref, 1 - own_half(), sems.at[chunk])
         for chunk in range(chunks)
     ]
-    start_kept, wait_kept = slab_copies(snapshot_ref, 0, kept_ref, own_half(), kept_sem)
+    (start_first, wait_first), (start_rest, wait_rest) = (
+        slab_copies(snapshot_ref, 0, kept_ref, own_half(), kept_sems.at[k]) for k in range(2)
+    )
 
     small = pltpu.make_async_copy(mode2_ref, small_ref, small_sem)
     small.start()
@@ -110,12 +112,16 @@
     for chunk in range(chunks):
         sends[chunk][1](chunk * STEP, STEP)
         if chunk == 0:
-            start_kept(0, cells, 2 * chunks)
+            start_first(0, STEP, 4)
+            start_rest(STEP, cells - STEP, 2 * (chunks - 1))
         multiply(slab_ref[pl.ds(chunk * STEP, STEP)], wide_ref, flat[chunk % 2])
         if chunk:
             spread(half, flat[(chunk - 1) % 2], order_ref, core_ref, (chunk - 1) * STEP)
     spread(half, flat[(chunks - 1) % 2], order_ref, core_ref, (chunks - 1) * STEP)
-    wait_kept(0, cells)
+    wait_first(0, STEP)
+    multiply(kept_ref[pl.ds(0, STEP)], wide_ref, flat[chunks % 2])
+    spread(half, flat[chunks % 2], order_ref, part_ref, 0)
+    wait_rest(STEP, cells - STEP)
 
 
 def contract_send(snapshot, mode2_t):
@@ -131,6 +137,7 @@
         out_shape=[
             jax.ShapeDtypeStruct((cells, half * rank), BF16),
             jax.ShapeDtypeStruct((cells, half, depth), BF16),
+            jax.ShapeDtypeStruct((STEP, half * rank), BF16),
             jax.ShapeDtypeStruct((LANES, depth), BF16),
             jax.ShapeDtypeStruct((block // reps, block * reps), BF16),
         ],
@@ -140,7 +147,7 @@
             pltpu.VMEM((STEP * half, LANES), BF16),
             pltpu.VMEM((STEP * half, LANES), BF16),
             pltpu.SemaphoreType.DMA((cells // STEP,)),
-            pltpu.SemaphoreType.DMA,
+            pltpu.SemaphoreType.DMA((2,)),
             pltpu.SemaphoreType.DMA,
         ],
         compiler_params=params(24),
@@ -148,18 +155,19 @@
     )(snapshot, mode2_t)
 
 
-def own_kernel(slab_ref, wide_ref, order_ref, core_ref, even_ref, odd_ref):
+def own_kernel(slab_ref, part_ref, wide_ref, order_ref, core_ref, even_ref, odd_ref):
     cells, half, _ = slab_ref.shape
     flat = (even_ref, odd_ref)
     chunks = cells // STEP
-    for chunk in range(chunks):
+    core_ref[pl.ds(0, STEP), :] = part_ref[...]
+    for chunk in range(1, chunks):
         multiply(slab_ref[pl.ds(chunk * STEP, STEP)], wide_ref, flat[chunk % 2])
-        if chunk:
+        if chunk > 1:
             spread(half, flat[(chunk - 1) % 2], order_ref, core_ref, (chunk - 1) * STEP)
     spread(half, flat[(chunks - 1) % 2], order_ref, core_ref, (chunks - 1) * STEP)
 
 
-def contract_own(slab, wide, order):
+def contract_own(slab, part, wide, order):
     cells, half, _ = slab.shape
     reps = order.shape[1] // (TILE * half)
     return pl.pallas_call(
@@ -168,7 +176,7 @@
         scratch_shapes=[pltpu.VMEM((STEP * half, LANES), BF16)] * 2,
         compiler_params=params(24),
         name="contract_own",
-    )(slab, wide, order)
+    )(slab, part, wide, order)
 
 
 def is_even():
@@ -379,9 +387,9 @@
 
     snapshot = pltpu.with_memory_space_constraint(snapshot, pltpu.HBM)
     mode2_t = pltpu.with_memory_space_constraint(mode2_factor.T, pltpu.HBM)
-    send, kept, wide, order = contract_send(snapshot, mode2_t)
+    send, kept, part, wide, order = contract_send(snapshot, mode2_t)
     got = swap(send, 0)
-    own = contract_own(kept, wide, order)
+    own = contract_own(kept, part, wide, order)
 
     send, give = project(own, got, old_factor.T, False)
     keep, columns = project(own, got, old_factor.T, True)

time: 36.5 us -> 36.9 us (1.011)
    pallas_call x1, Pallas kernels: 5.08 us -> 5.74 us  [contract_send(): pl.pallas_call(send_kernel, in_specs=[pinned, pinned], out_shape=[jax.Sha...]
  transfers between devices with their start and end apart: 10 -> 10, of which waited for: 8 -> 8; matrix products, arithmetic and copies ran while one was open for 0% -> 0% of each run, Pallas kernels for 5% -> 4%
where the time goes in v32:
time: 36.9 us; the launch traced here: 36.8 us
  starting transfers between devices  14.8 us (40%)
  waiting for transfers between devices  11.9 us (32%)
  Pallas kernels  10 us (27%)
    ppermute x10, starting transfers between devices, swap(): return lax.ppermute(x, ('row', 'col'), pairs)  14.8 us
    ppermute x10, waiting for transfers between devices, swap(): return lax.ppermute(x, ('row', 'col'), pairs)  11.9 us
    pallas_call x1, Pallas kernels, contract_send(): pl.pallas_call(send_kernel, in_specs=[pinned, pinned], out_shape=[jax.Sha...  5.74 us
    pallas_call x1, Pallas kernels, finish(): pl.pallas_call(functools.partial(finish_kernel, total_rows), out_shape=ja...  1.92 us
    pallas_call x1, Pallas kernels, contract_own(): pl.pallas_call(own_kernel, out_shape=jax.ShapeDtypeStruct((cells, half //...  1.43 us
  transfers between devices with their start and end apart: 10, of which 8 were waited for; matrix products, arithmetic and copies ran while one was open for 0% of the time, Pallas kernels for 4%

profile of v32, /device:TPU:0, one launch (start us, length us, event | category | flops | bytes accessed | tf_op | source)
XLA Modules:
  0.0 36.8 jit_solution(10272459550489518239)
XLA Ops:
  0.0 0.0 copy-start
  0.0 5.7 %contract_send.1 = (bf16[128,1024]{1,0:T(8,128)(2,1)S(1)}, bf16[128,16,1024]{2,1,0:T(8,128)(2,1)S(1)}, bf16[32,1024]{1,0:T(8,128)(2,1)S(1)}, bf16[128,1024]{1,0:T(8,128)(2,1)S(1)}, bf16[64,256]{1,0:T(8,128)(2,1)S(1)}) custom-call(bf16[128,32,1024]{2,1,0:T(8,128)(2,1)} %snapshot_ref.1, bf16[64,1024]{1,0:T(8,128)(2,1)} %bitcast.4), custom_call_target="tpu_custom_call" | custom-call | tf_op jit(solution)/shard_map/contract_send/pallas_call | solution.py:134
  5.7 0.5 %collective-permute-start = (bf16[128,1024]{1,0:T(8,128)(2,1)S(1)}, bf16[128,1024]{1,0:T(8,128)(2,1)S(1)}, u32[]{:S(2)}, u32[]{:S(2)}) collective-permute-start(bf16[128,1024]{1,0:T(8,128)(2,1)S(1)} %get-tuple-element.18), channel_id=1, source_target_pairs={{0,1},{1,0},{2,3},{3,2},{4,5},{5,4},{6,7},{7,6},{8,9},{9,8},{10,11... | collective-permute-start | bytes 786440 | tf_op jit(solution)/shard_map/ppermute | solution.py:386
  6.3 1.4 %contract_own.1.own_ref = bf16[128,1024]{1,0:T(8,128)(2,1)S(1)} custom-call(bf16[128,16,1024]{2,1,0:T(8,128)(2,1)S(1)} %get-tuple-element.14.slab_ref, bf16[32,1024]{1,0:T(8,128)(2,1)S(1)} %get-tuple-element.15.part_ref, bf16[128,1024]{1,0:T(8,128)(2,1)S(1)} %get-tuple-element.16.wide_ref, bf16[64,256]{1,0:T(8,128)(2,1)S(1)} %get-tuple-element.17.order_ref), custom_call_target="tpu_custom_call" | custom-call | tf_op jit(solution)/shard_map/contract_own/pallas_call | solution.py:173
  7.7 0.0 collective-permute-done.got_ref
  7.7 0.0 copy-done
  7.7 0.2 project_sent.1
  7.9 2.7 %collective-permute-start.2 = (bf16[256,128]{1,0:T(8,128)(2,1)S(1)}, bf16[256,128]{1,0:T(8,128)(2,1)S(1)}, u32[]{:S(2)}, u32[]{:S(2)}) collective-permute-start(bf16[256,128]{1,0:T(8,128)(2,1)S(1)} %get-tuple-element.22), channel_id=1, source_target_pairs={{0,3},{1,2},{2,1},{3,0},{4,7},{5,6},{6,5},{7,4},{8,11},{9,10},{10,... | collective-permute-start | bytes 196616 | tf_op jit(solution)/shard_map/ppermute | solution.py:386
  10.6 0.2 project_kept.1
  10.8 2.2 %collective-permute-done.2.got_ref = bf16[256,128]{1,0:T(8,128)(2,1)S(1)} collective-permute-done((bf16[256,128]{1,0:T(8,128)(2,1)S(1)}, bf16[256,128]{1,0:T(8,128)(2,1)S(1)}, u32[]{:S(2)}, u32[]{:S(2)}) %collective-permute-start.2) | collective-permute-done | bytes 65568 | tf_op jit(solution)/shard_map/ppermute | solution.py:386
  13.0 1.5 %collective-permute-start.3 = (bf16[256,128]{1,0:T(8,128)(2,1)S(1)}, bf16[256,128]{1,0:T(8,128)(2,1)S(1)}, u32[]{:S(2)}, u32[]{:S(2)}) collective-permute-start(bf16[256,128]{1,0:T(8,128)(2,1)S(1)} %add.4.mine_ref), channel_id=1, source_target_pairs={{0,5},{1,8},{2,11},{3,6},{4,13},{5,0},{6,3},{7,14},{8,1},{9,12},{1... | collective-permute-start | bytes 196616 | tf_op jit(solution)/shard_map/ppermute | solution.py:386
  14.5 1.2 %collective-permute-start.1 = (bf16[128,512]{1,0:T(8,128)(2,1)S(1)}, bf16[128,512]{1,0:T(8,128)(2,1)S(1)}, u32[]{:S(2)}, u32[]{:S(2)}) collective-permute-start(bf16[128,512]{1,0:T(8,128)(2,1)S(1)} %get-tuple-element.20), channel_id=1, source_target_pairs={{0,3},{1,2},{2,1},{3,0},{4,7},{5,6},{6,5},{7,4},{8,11},{9,10},{10,... | collective-permute-start | bytes 393224 | tf_op jit(solution)/shard_map/ppermute | solution.py:386
  15.8 1.0 %collective-permute-done.3.got_ref = bf16[256,128]{1,0:T(8,128)(2,1)S(1)} collective-permute-done((bf16[256,128]{1,0:T(8,128)(2,1)S(1)}, bf16[256,128]{1,0:T(8,128)(2,1)S(1)}, u32[]{:S(2)}, u32[]{:S(2)}) %collective-permute-start.3) | collective-permute-done | bytes 65568 | tf_op jit(solution)/shard_map/ppermute | solution.py:386
  16.8 2.8 %collective-permute-start.4 = (bf16[256,128]{1,0:T(8,128)(2,1)S(1)}, bf16[256,128]{1,0:T(8,128)(2,1)S(1)}, u32[]{:S(2)}, u32[]{:S(2)}) collective-permute-start(bf16[256,128]{1,0:T(8,128)(2,1)S(1)} %add.5.mine_ref), channel_id=1, source_target_pairs={{0,9},{1,4},{2,7},{3,10},{4,1},{5,12},{6,15},{7,2},{8,13},{9,0},{1... | collective-permute-start | bytes 196616 | tf_op jit(solution)/shard_map/ppermute | solution.py:386
  19.6 0.0 collective-permute-done.1.refs_0_.got_ref
  19.6 1.9 %collective-permute-done.4.got_ref = bf16[256,128]{1,0:T(8,128)(2,1)S(1)} collective-permute-done((bf16[256,128]{1,0:T(8,128)(2,1)S(1)}, bf16[256,128]{1,0:T(8,128)(2,1)S(1)}, u32[]{:S(2)}, u32[]{:S(2)}) %collective-permute-start.4) | collective-permute-done | bytes 65568 | tf_op jit(solution)/shard_map/ppermute | solution.py:386
  21.6 0.2 product_terms.1.mine_ref
  21.8 0.8 %collective-permute-start.5 = (bf16[128,128]{1,0:T(8,128)(2,1)S(1)}, bf16[128,128]{1,0:T(8,128)(2,1)S(1)}, u32[]{:S(2)}, u32[]{:S(2)}) collective-permute-start(bf16[128,128]{1,0:T(8,128)(2,1)S(1)} %product_terms.1.mine_ref), channel_id=1, source_target_pairs={{0,1},{1,0},{2,3},{3,2},{4,5},{5,4},{6,7},{7,6},{8,9},{9,8},{10,11... | collective-permute-start | bytes 98312 | tf_op jit(solution)/shard_map/ppermute | solution.py:386
  22.6 0.9 %collective-permute-done.5.got_ref = bf16[128,128]{1,0:T(8,128)(2,1)S(1)} collective-permute-done((bf16[128,128]{1,0:T(8,128)(2,1)S(1)}, bf16[128,128]{1,0:T(8,128)(2,1)S(1)}, u32[]{:S(2)}, u32[]{:S(2)}) %collective-permute-start.5) | collective-permute-done | bytes 32800 | tf_op jit(solution)/shard_map/ppermute | solution.py:386
  23.4 2.7 %collective-permute-start.8 = (bf16[128,128]{1,0:T(8,128)(2,1)S(1)}, bf16[128,128]{1,0:T(8,128)(2,1)S(1)}, u32[]{:S(2)}, u32[]{:S(2)}) collective-permute-start(bf16[128,128]{1,0:T(8,128)(2,1)S(1)} %add.7.term_ref), channel_id=1, source_target_pairs={{0,7},{1,6},{2,5},{3,4},{4,3},{5,2},{6,1},{7,0},{8,15},{9,14},{10,... | collective-permute-start | bytes 98312 | tf_op jit(solution)/shard_map/ppermute | solution.py:386
  26.1 1.0 %collective-permute-start.7 = (bf16[128,128]{1,0:T(8,128)(2,1)S(1)}, bf16[128,128]{1,0:T(8,128)(2,1)S(1)}, u32[]{:S(2)}, u32[]{:S(2)}) collective-permute-start(bf16[128,128]{1,0:T(8,128)(2,1)S(1)} %add.7.term_ref), channel_id=1, source_target_pairs={{0,5},{1,2},{2,1},{3,6},{4,7},{5,0},{6,3},{7,4},{8,11},{9,12},{10,... | collective-permute-start | bytes 98312 | tf_op jit(solution)/shard_map/ppermute | solution.py:386
  27.0 0.0 collective-permute-start.6
  27.1 0.7 %collective-permute-done.8.last_ref = bf16[128,128]{1,0:T(8,128)(2,1)S(1)} collective-permute-done((bf16[128,128]{1,0:T(8,128)(2,1)S(1)}, bf16[128,128]{1,0:T(8,128)(2,1)S(1)}, u32[]{:S(2)}, u32[]{:S(2)}) %collective-permute-start.8) | collective-permute-done | bytes 32800 | tf_op jit(solution)/shard_map/ppermute | solution.py:386
  27.7 1.8 %collective-permute-done.7.second_ref = bf16[128,128]{1,0:T(8,128)(2,1)S(1)} collective-permute-done((bf16[128,128]{1,0:T(8,128)(2,1)S(1)}, bf16[128,128]{1,0:T(8,128)(2,1)S(1)}, u32[]{:S(2)}, u32[]{:S(2)}) %collective-permute-start.7) | collective-permute-done | bytes 32800 | tf_op jit(solution)/shard_map/ppermute | solution.py:386
  29.5 0.9 %collective-permute-done.6.first_ref = bf16[128,128]{1,0:T(8,128)(2,1)S(1)} collective-permute-done((bf16[128,128]{1,0:T(8,128)(2,1)S(1)}, bf16[128,128]{1,0:T(8,128)(2,1)S(1)}, u32[]{:S(2)}, u32[]{:S(2)}) %collective-permute-start.6) | collective-permute-done | bytes 32800 | tf_op jit(solution)/shard_map/ppermute | solution.py:386
  30.4 0.3 local_gram.1.gram_ref
  30.7 1.6 %collective-permute-start.9 = (f32[32,128]{1,0:T(8,128)S(1)}, f32[32,128]{1,0:T(8,128)S(1)}, u32[]{:S(2)}, u32[]{:S(2)}) collective-permute-start(f32[32,128]{1,0:T(8,128)S(1)} %local_gram.1.gram_ref), channel_id=1, source_target_pairs={{0,9},{1,8},{2,11},{3,10},{4,13},{5,12},{6,15},{7,14},{8,1},{9,0},... | collective-permute-start | bytes 49160 | tf_op jit(solution)/shard_map/ppermute | solution.py:386
  32.3 2.6 %collective-permute-done.9.got_gram_ref = f32[32,128]{1,0:T(8,128)S(1)} collective-permute-done((f32[32,128]{1,0:T(8,128)S(1)}, f32[32,128]{1,0:T(8,128)S(1)}, u32[]{:S(2)}, u32[]{:S(2)}) %collective-permute-start.9) | collective-permute-done | bytes 16416 | tf_op jit(solution)/shard_map/ppermute | solution.py:386
  34.9 1.9 %finish.1 = f32[64,64]{1,0:T(8,128)} custom-call(bf16[128,128]{1,0:T(8,128)(2,1)S(1)} %add.7.term_ref, bf16[128,128]{1,0:T(8,128)(2,1)S(1)} %collective-permute-done.6.first_ref, bf16[128,128]{1,0:T(8,128)(2,1)S(1)} %collective-permute-done.7.second_ref, f32[32,128]{1,0:T(8,128)S(1)} %local_gram.1.gram_ref, f32[32,128]{1,0:T(8,128)S(1)} %collective-permute-done.9.got_gram_ref), custom_call_target="tpu_custom_call" | custom-call | tf_op jit(solution)/shard_map/finish/pallas_call | solution.py:365
  (4 shorter events, 0.1 us)
Async XLA Ops:
  0.0 7.7 %copy-start = (bf16[128,64]{0,1:T(8,128)(2,1)S(1)}, bf16[128,64]{0,1:T(8,128)(2,1)}, u32[]{:S(2)}) copy-start(bf16[128,64]{0,1:T(8,128)(2,1)} %param.5) | copy-start | bytes 49156
  5.7 2.0 %collective-permute-start = (bf16[128,1024]{1,0:T(8,128)(2,1)S(1)}, bf16[128,1024]{1,0:T(8,128)(2,1)S(1)}, u32[]{:S(2)}, u32[]{:S(2)}) collective-permute-start(bf16[128,1024]{1,0:T(8,128)(2,1)S(1)} %get-tuple-element.18), channel_id=1, source_target_pairs={{0,1},{1,0},{2,3},{3,2},{4,5},{5,4},{6,7},{7,6},{8,9},{9,8},{10,11... | collective-permute-start | bytes 786440 | tf_op jit(solution)/shard_map/ppermute | solution.py:386
  7.9 5.1 %collective-permute-start.2 = (bf16[256,128]{1,0:T(8,128)(2,1)S(1)}, bf16[256,128]{1,0:T(8,128)(2,1)S(1)}, u32[]{:S(2)}, u32[]{:S(2)}) collective-permute-start(bf16[256,128]{1,0:T(8,128)(2,1)S(1)} %get-tuple-element.22), channel_id=1, source_target_pairs={{0,3},{1,2},{2,1},{3,0},{4,7},{5,6},{6,5},{7,4},{8,11},{9,10},{10,... | collective-permute-start | bytes 196616 | tf_op jit(solution)/shard_map/ppermute | solution.py:386
  13.0 3.8 %collective-permute-start.3 = (bf16[256,128]{1,0:T(8,128)(2,1)S(1)}, bf16[256,128]{1,0:T(8,128)(2,1)S(1)}, u32[]{:S(2)}, u32[]{:S(2)}) collective-permute-start(bf16[256,128]{1,0:T(8,128)(2,1)S(1)} %add.4.mine_ref), channel_id=1, source_target_pairs={{0,5},{1,8},{2,11},{3,6},{4,13},{5,0},{6,3},{7,14},{8,1},{9,12},{1... | collective-permute-start | bytes 196616 | tf_op jit(solution)/shard_map/ppermute | solution.py:386
  14.5 5.1 %collective-permute-start.1 = (bf16[128,512]{1,0:T(8,128)(2,1)S(1)}, bf16[128,512]{1,0:T(8,128)(2,1)S(1)}, u32[]{:S(2)}, u32[]{:S(2)}) collective-permute-start(bf16[128,512]{1,0:T(8,128)(2,1)S(1)} %get-tuple-element.20), channel_id=1, source_target_pairs={{0,3},{1,2},{2,1},{3,0},{4,7},{5,6},{6,5},{7,4},{8,11},{9,10},{10,... | collective-permute-start | bytes 393224 | tf_op jit(solution)/shard_map/ppermute | solution.py:386
  16.8 4.8 %collective-permute-start.4 = (bf16[256,128]{1,0:T(8,128)(2,1)S(1)}, bf16[256,128]{1,0:T(8,128)(2,1)S(1)}, u32[]{:S(2)}, u32[]{:S(2)}) collective-permute-start(bf16[256,128]{1,0:T(8,128)(2,1)S(1)} %add.5.mine_ref), channel_id=1, source_target_pairs={{0,9},{1,4},{2,7},{3,10},{4,1},{5,12},{6,15},{7,2},{8,13},{9,0},{1... | collective-permute-start | bytes 196616 | tf_op jit(solution)/shard_map/ppermute | solution.py:386
  21.8 1.6 %collective-permute-start.5 = (bf16[128,128]{1,0:T(8,128)(2,1)S(1)}, bf16[128,128]{1,0:T(8,128)(2,1)S(1)}, u32[]{:S(2)}, u32[]{:S(2)}) collective-permute-start(bf16[128,128]{1,0:T(8,128)(2,1)S(1)} %product_terms.1.mine_ref), channel_id=1, source_target_pairs={{0,1},{1,0},{2,3},{3,2},{4,5},{5,4},{6,7},{7,6},{8,9},{9,8},{10,11... | collective-permute-start | bytes 98312 | tf_op jit(solution)/shard_map/ppermute | solution.py:386
  23.4 4.3 %collective-permute-start.8 = (bf16[128,128]{1,0:T(8,128)(2,1)S(1)}, bf16[128,128]{1,0:T(8,128)(2,1)S(1)}, u32[]{:S(2)}, u32[]{:S(2)}) collective-permute-start(bf16[128,128]{1,0:T(8,128)(2,1)S(1)} %add.7.term_ref), channel_id=1, source_target_pairs={{0,7},{1,6},{2,5},{3,4},{4,3},{5,2},{6,1},{7,0},{8,15},{9,14},{10,... | collective-permute-start | bytes 98312 | tf_op jit(solution)/shard_map/ppermute | solution.py:386
  26.1 3.4 %collective-permute-start.7 = (bf16[128,128]{1,0:T(8,128)(2,1)S(1)}, bf16[128,128]{1,0:T(8,128)(2,1)S(1)}, u32[]{:S(2)}, u32[]{:S(2)}) collective-permute-start(bf16[128,128]{1,0:T(8,128)(2,1)S(1)} %add.7.term_ref), channel_id=1, source_target_pairs={{0,5},{1,2},{2,1},{3,6},{4,7},{5,0},{6,3},{7,4},{8,11},{9,12},{10,... | collective-permute-start | bytes 98312 | tf_op jit(solution)/shard_map/ppermute | solution.py:386
  27.0 3.3 %collective-permute-start.6 = (bf16[128,128]{1,0:T(8,128)(2,1)S(1)}, bf16[128,128]{1,0:T(8,128)(2,1)S(1)}, u32[]{:S(2)}, u32[]{:S(2)}) collective-permute-start(bf16[128,128]{1,0:T(8,128)(2,1)S(1)} %add.7.term_ref), channel_id=1, source_target_pairs={{0,3},{1,4},{2,7},{3,0},{4,1},{5,6},{6,5},{7,2},{8,13},{9,10},{10,... | collective-permute-start | bytes 98312 | tf_op jit(solution)/shard_map/ppermute | solution.py:386
  30.7 4.2 %collective-permute-start.9 = (f32[32,128]{1,0:T(8,128)S(1)}, f32[32,128]{1,0:T(8,128)S(1)}, u32[]{:S(2)}, u32[]{:S(2)}) collective-permute-start(f32[32,128]{1,0:T(8,128)S(1)} %local_gram.1.gram_ref), channel_id=1, source_target_pairs={{0,9},{1,8},{2,11},{3,10},{4,13},{5,12},{6,15},{7,14},{8,1},{9,0},... | collective-permute-start | bytes 49160 | tf_op jit(solution)/shard_map/ppermute | solution.py:386

commit v33 on v30

--- a/solution.py
+++ b/solution.py
@@ -102,15 +102,18 @@
 
     small = pltpu.make_async_copy(mode2_ref, small_ref, small_sem)
     small.start()
-    for chunk in range(chunks):
-        sends[chunk][0](chunk * STEP, STEP, 2 if chunk else 4)
+    sends[0][0](0, STEP, 8)
+    sends[1][0](STEP, STEP, 2)
     fill_order(order_ref, half)
     small.wait()
     wide_ref[...] = jnp.concatenate([small_ref[...]] * (LANES // rank), axis=0)
     for chunk in range(chunks):
         sends[chunk][1](chunk * STEP, STEP)
         if chunk == 0:
-            start_kept(0, cells, 2 * chunks)
+            for later in range(2, chunks):
+                sends[later][0](later * STEP, STEP, 2)
+        if chunk < 2:
+            start_kept(chunk * (cells // 2), cells // 2, chunks)
         multiply(slab_ref[pl.ds(chunk * STEP, STEP)], wide_ref, flat[chunk % 2])
         if chunk:
             spread(half, flat[(chunk - 1) % 2], order_ref, core_ref, (chunk - 1) * STEP)

time: 36.5 us -> 36 us (0.986)
  Pallas kernels: 9.69 us -> 9.16 us
    pallas_call x1, Pallas kernels: 5.08 us -> 4.55 us  [contract_send(): pl.pallas_call(send_kernel, in_specs=[pinned, pinned], out_shape=[jax.Sha...]
where the time goes in v33:
time: 36 us; the launch traced here: 35.8 us
  starting transfers between devices  14.5 us (40%)
  waiting for transfers between devices  12.1 us (34%)
  Pallas kernels  9.16 us (25%)
    ppermute x10, starting transfers between devices, swap(): return lax.ppermute(x, ('row', 'col'), pairs)  14.5 us
    ppermute x10, waiting for transfers between devices, swap(): return lax.ppermute(x, ('row', 'col'), pairs)  12.1 us
    pallas_call x1, Pallas kernels, contract_send(): pl.pallas_call(send_kernel, in_specs=[pinned, pinned], out_shape=[jax.Sha...  4.55 us
    pallas_call x1, Pallas kernels, finish(): pl.pallas_call(functools.partial(finish_kernel, total_rows), out_shape=ja...  1.92 us
    pallas_call x1, Pallas kernels, contract_own(): pl.pallas_call(own_kernel, out_shape=jax.ShapeDtypeStruct((cells, half //...  1.77 us
  transfers between devices with their start and end apart: 10, of which 8 were waited for; matrix products, arithmetic and copies ran while one was open for 0% of the time, Pallas kernels for 5%

profile of v33, /device:TPU:0, one launch (start us, length us, event | category | flops | bytes accessed | tf_op | source)
XLA Modules:
  0.0 35.8 jit_solution(12625394273665246754)
XLA Ops:
  0.0 0.0 copy-start
  0.0 4.6 %contract_send.1 = (bf16[128,1024]{1,0:T(8,128)(2,1)S(1)}, bf16[128,16,1024]{2,1,0:T(8,128)(2,1)S(1)}, bf16[128,1024]{1,0:T(8,128)(2,1)S(1)}, bf16[64,256]{1,0:T(8,128)(2,1)S(1)}) custom-call(bf16[128,32,1024]{2,1,0:T(8,128)(2,1)} %snapshot_ref.1, bf16[64,1024]{1,0:T(8,128)(2,1)} %bitcast.4), custom_call_target="tpu_custom_call" | custom-call | tf_op jit(solution)/shard_map/contract_send/pallas_call | solution.py:131
  4.6 0.5 %collective-permute-start = (bf16[128,1024]{1,0:T(8,128)(2,1)S(1)}, bf16[128,1024]{1,0:T(8,128)(2,1)S(1)}, u32[]{:S(2)}, u32[]{:S(2)}) collective-permute-start(bf16[128,1024]{1,0:T(8,128)(2,1)S(1)} %get-tuple-element.16), channel_id=1, source_target_pairs={{0,1},{1,0},{2,3},{3,2},{4,5},{5,4},{6,7},{7,6},{8,9},{9,8},{10,11... | collective-permute-start | bytes 786440 | tf_op jit(solution)/shard_map/ppermute | solution.py:381
  5.1 1.8 %contract_own.1.own_ref = bf16[128,1024]{1,0:T(8,128)(2,1)S(1)} custom-call(bf16[128,16,1024]{2,1,0:T(8,128)(2,1)S(1)} %get-tuple-element.13.slab_ref, bf16[128,1024]{1,0:T(8,128)(2,1)S(1)} %get-tuple-element.14.wide_ref, bf16[64,256]{1,0:T(8,128)(2,1)S(1)} %get-tuple-element.15.order_ref), custom_call_target="tpu_custom_call" | custom-call | tf_op jit(solution)/shard_map/contract_own/pallas_call | solution.py:168
  6.9 0.0 collective-permute-done.got_ref
  6.9 0.0 copy-done
  6.9 0.2 project_sent.1
  7.1 2.7 %collective-permute-start.2 = (bf16[256,128]{1,0:T(8,128)(2,1)S(1)}, bf16[256,128]{1,0:T(8,128)(2,1)S(1)}, u32[]{:S(2)}, u32[]{:S(2)}) collective-permute-start(bf16[256,128]{1,0:T(8,128)(2,1)S(1)} %get-tuple-element.20), channel_id=1, source_target_pairs={{0,3},{1,2},{2,1},{3,0},{4,7},{5,6},{6,5},{7,4},{8,11},{9,10},{10,... | collective-permute-start | bytes 196616 | tf_op jit(solution)/shard_map/ppermute | solution.py:381
  9.8 0.2 project_kept.1
  9.9 2.3 %collective-permute-done.2.got_ref = bf16[256,128]{1,0:T(8,128)(2,1)S(1)} collective-permute-done((bf16[256,128]{1,0:T(8,128)(2,1)S(1)}, bf16[256,128]{1,0:T(8,128)(2,1)S(1)}, u32[]{:S(2)}, u32[]{:S(2)}) %collective-permute-start.2) | collective-permute-done | bytes 65568 | tf_op jit(solution)/shard_map/ppermute | solution.py:381
  12.2 1.4 %collective-permute-start.3 = (bf16[256,128]{1,0:T(8,128)(2,1)S(1)}, bf16[256,128]{1,0:T(8,128)(2,1)S(1)}, u32[]{:S(2)}, u32[]{:S(2)}) collective-permute-start(bf16[256,128]{1,0:T(8,128)(2,1)S(1)} %add.4.mine_ref), channel_id=1, source_target_pairs={{0,5},{1,8},{2,11},{3,6},{4,13},{5,0},{6,3},{7,14},{8,1},{9,12},{1... | collective-permute-start | bytes 196616 | tf_op jit(solution)/shard_map/ppermute | solution.py:381
  13.6 1.2 %collective-permute-start.1 = (bf16[128,512]{1,0:T(8,128)(2,1)S(1)}, bf16[128,512]{1,0:T(8,128)(2,1)S(1)}, u32[]{:S(2)}, u32[]{:S(2)}) collective-permute-start(bf16[128,512]{1,0:T(8,128)(2,1)S(1)} %get-tuple-element.18), channel_id=1, source_target_pairs={{0,3},{1,2},{2,1},{3,0},{4,7},{5,6},{6,5},{7,4},{8,11},{9,10},{10,... | collective-permute-start | bytes 393224 | tf_op jit(solution)/shard_map/ppermute | solution.py:381
  14.8 1.2 %collective-permute-done.3.got_ref = bf16[256,128]{1,0:T(8,128)(2,1)S(1)} collective-permute-done((bf16[256,128]{1,0:T(8,128)(2,1)S(1)}, bf16[256,128]{1,0:T(8,128)(2,1)S(1)}, u32[]{:S(2)}, u32[]{:S(2)}) %collective-permute-start.3) | collective-permute-done | bytes 65568 | tf_op jit(solution)/shard_map/ppermute | solution.py:381
  16.0 2.7 %collective-permute-start.4 = (bf16[256,128]{1,0:T(8,128)(2,1)S(1)}, bf16[256,128]{1,0:T(8,128)(2,1)S(1)}, u32[]{:S(2)}, u32[]{:S(2)}) collective-permute-start(bf16[256,128]{1,0:T(8,128)(2,1)S(1)} %add.5.mine_ref), channel_id=1, source_target_pairs={{0,9},{1,4},{2,7},{3,10},{4,1},{5,12},{6,15},{7,2},{8,13},{9,0},{1... | collective-permute-start | bytes 196616 | tf_op jit(solution)/shard_map/ppermute | solution.py:381
  18.7 0.0 collective-permute-done.1.refs_0_.got_ref
  18.7 2.0 %collective-permute-done.4.got_ref = bf16[256,128]{1,0:T(8,128)(2,1)S(1)} collective-permute-done((bf16[256,128]{1,0:T(8,128)(2,1)S(1)}, bf16[256,128]{1,0:T(8,128)(2,1)S(1)}, u32[]{:S(2)}, u32[]{:S(2)}) %collective-permute-start.4) | collective-permute-done | bytes 65568 | tf_op jit(solution)/shard_map/ppermute | solution.py:381
  20.7 0.2 product_terms.1.mine_ref
  20.9 0.9 %collective-permute-start.5 = (bf16[128,128]{1,0:T(8,128)(2,1)S(1)}, bf16[128,128]{1,0:T(8,128)(2,1)S(1)}, u32[]{:S(2)}, u32[]{:S(2)}) collective-permute-start(bf16[128,128]{1,0:T(8,128)(2,1)S(1)} %product_terms.1.mine_ref), channel_id=1, source_target_pairs={{0,1},{1,0},{2,3},{3,2},{4,5},{5,4},{6,7},{7,6},{8,9},{9,8},{10,11... | collective-permute-start | bytes 98312 | tf_op jit(solution)/shard_map/ppermute | solution.py:381
  21.8 0.9 %collective-permute-done.5.got_ref = bf16[128,128]{1,0:T(8,128)(2,1)S(1)} collective-permute-done((bf16[128,128]{1,0:T(8,128)(2,1)S(1)}, bf16[128,128]{1,0:T(8,128)(2,1)S(1)}, u32[]{:S(2)}, u32[]{:S(2)}) %collective-permute-start.5) | collective-permute-done | bytes 32800 | tf_op jit(solution)/shard_map/ppermute | solution.py:381
  22.7 2.6 %collective-permute-start.8 = (bf16[128,128]{1,0:T(8,128)(2,1)S(1)}, bf16[128,128]{1,0:T(8,128)(2,1)S(1)}, u32[]{:S(2)}, u32[]{:S(2)}) collective-permute-start(bf16[128,128]{1,0:T(8,128)(2,1)S(1)} %add.7.term_ref), channel_id=1, source_target_pairs={{0,7},{1,6},{2,5},{3,4},{4,3},{5,2},{6,1},{7,0},{8,15},{9,14},{10,... | collective-permute-start | bytes 98312 | tf_op jit(solution)/shard_map/ppermute | solution.py:381
  25.3 0.9 %collective-permute-start.7 = (bf16[128,128]{1,0:T(8,128)(2,1)S(1)}, bf16[128,128]{1,0:T(8,128)(2,1)S(1)}, u32[]{:S(2)}, u32[]{:S(2)}) collective-permute-start(bf16[128,128]{1,0:T(8,128)(2,1)S(1)} %add.7.term_ref), channel_id=1, source_target_pairs={{0,5},{1,2},{2,1},{3,6},{4,7},{5,0},{6,3},{7,4},{8,11},{9,12},{10,... | collective-permute-start | bytes 98312 | tf_op jit(solution)/shard_map/ppermute | solution.py:381
  26.1 0.0 collective-permute-start.6
  26.2 0.8 %collective-permute-done.8.last_ref = bf16[128,128]{1,0:T(8,128)(2,1)S(1)} collective-permute-done((bf16[128,128]{1,0:T(8,128)(2,1)S(1)}, bf16[128,128]{1,0:T(8,128)(2,1)S(1)}, u32[]{:S(2)}, u32[]{:S(2)}) %collective-permute-start.8) | collective-permute-done | bytes 32800 | tf_op jit(solution)/shard_map/ppermute | solution.py:381
  27.0 1.7 %collective-permute-done.7.second_ref = bf16[128,128]{1,0:T(8,128)(2,1)S(1)} collective-permute-done((bf16[128,128]{1,0:T(8,128)(2,1)S(1)}, bf16[128,128]{1,0:T(8,128)(2,1)S(1)}, u32[]{:S(2)}, u32[]{:S(2)}) %collective-permute-start.7) | collective-permute-done | bytes 32800 | tf_op jit(solution)/shard_map/ppermute | solution.py:381
  28.6 0.9 %collective-permute-done.6.first_ref = bf16[128,128]{1,0:T(8,128)(2,1)S(1)} collective-permute-done((bf16[128,128]{1,0:T(8,128)(2,1)S(1)}, bf16[128,128]{1,0:T(8,128)(2,1)S(1)}, u32[]{:S(2)}, u32[]{:S(2)}) %collective-permute-start.6) | collective-permute-done | bytes 32800 | tf_op jit(solution)/shard_map/ppermute | solution.py:381
  29.5 0.3 local_gram.1.gram_ref
  29.8 1.7 %collective-permute-start.9 = (f32[32,128]{1,0:T(8,128)S(1)}, f32[32,128]{1,0:T(8,128)S(1)}, u32[]{:S(2)}, u32[]{:S(2)}) collective-permute-start(f32[32,128]{1,0:T(8,128)S(1)} %local_gram.1.gram_ref), channel_id=1, source_target_pairs={{0,9},{1,8},{2,11},{3,10},{4,13},{5,12},{6,15},{7,14},{8,1},{9,0},... | collective-permute-start | bytes 49160 | tf_op jit(solution)/shard_map/ppermute | solution.py:381
  31.5 2.5 %collective-permute-done.9.got_gram_ref = f32[32,128]{1,0:T(8,128)S(1)} collective-permute-done((f32[32,128]{1,0:T(8,128)S(1)}, f32[32,128]{1,0:T(8,128)S(1)}, u32[]{:S(2)}, u32[]{:S(2)}) %collective-permute-start.9) | collective-permute-done | bytes 16416 | tf_op jit(solution)/shard_map/ppermute | solution.py:381
  33.9 1.9 %finish.1 = f32[64,64]{1,0:T(8,128)} custom-call(bf16[128,128]{1,0:T(8,128)(2,1)S(1)} %add.7.term_ref, bf16[128,128]{1,0:T(8,128)(2,1)S(1)} %collective-permute-done.6.first_ref, bf16[128,128]{1,0:T(8,128)(2,1)S(1)} %collective-permute-done.7.second_ref, f32[32,128]{1,0:T(8,128)S(1)} %local_gram.1.gram_ref, f32[32,128]{1,0:T(8,128)S(1)} %collective-permute-done.9.got_gram_ref), custom_call_target="tpu_custom_call" | custom-call | tf_op jit(solution)/shard_map/finish/pallas_call | solution.py:360
  (4 shorter events, 0.1 us)
Async XLA Ops:
  0.0 6.9 %copy-start = (bf16[128,64]{0,1:T(8,128)(2,1)S(1)}, bf16[128,64]{0,1:T(8,128)(2,1)}, u32[]{:S(2)}) copy-start(bf16[128,64]{0,1:T(8,128)(2,1)} %param.5) | copy-start | bytes 49156
  4.6 2.3 %collective-permute-start = (bf16[128,1024]{1,0:T(8,128)(2,1)S(1)}, bf16[128,1024]{1,0:T(8,128)(2,1)S(1)}, u32[]{:S(2)}, u32[]{:S(2)}) collective-permute-start(bf16[128,1024]{1,0:T(8,128)(2,1)S(1)} %get-tuple-element.16), channel_id=1, source_target_pairs={{0,1},{1,0},{2,3},{3,2},{4,5},{5,4},{6,7},{7,6},{8,9},{9,8},{10,11... | collective-permute-start | bytes 786440 | tf_op jit(solution)/shard_map/ppermute | solution.py:381
  7.1 5.2 %collective-permute-start.2 = (bf16[256,128]{1,0:T(8,128)(2,1)S(1)}, bf16[256,128]{1,0:T(8,128)(2,1)S(1)}, u32[]{:S(2)}, u32[]{:S(2)}) collective-permute-start(bf16[256,128]{1,0:T(8,128)(2,1)S(1)} %get-tuple-element.20), channel_id=1, source_target_pairs={{0,3},{1,2},{2,1},{3,0},{4,7},{5,6},{6,5},{7,4},{8,11},{9,10},{10,... | collective-permute-start | bytes 196616 | tf_op jit(solution)/shard_map/ppermute | solution.py:381
  12.2 3.8 %collective-permute-start.3 = (bf16[256,128]{1,0:T(8,128)(2,1)S(1)}, bf16[256,128]{1,0:T(8,128)(2,1)S(1)}, u32[]{:S(2)}, u32[]{:S(2)}) collective-permute-start(bf16[256,128]{1,0:T(8,128)(2,1)S(1)} %add.4.mine_ref), channel_id=1, source_target_pairs={{0,5},{1,8},{2,11},{3,6},{4,13},{5,0},{6,3},{7,14},{8,1},{9,12},{1... | collective-permute-start | bytes 196616 | tf_op jit(solution)/shard_map/ppermute | solution.py:381
  13.6 5.1 %collective-permute-start.1 = (bf16[128,512]{1,0:T(8,128)(2,1)S(1)}, bf16[128,512]{1,0:T(8,128)(2,1)S(1)}, u32[]{:S(2)}, u32[]{:S(2)}) collective-permute-start(bf16[128,512]{1,0:T(8,128)(2,1)S(1)} %get-tuple-element.18), channel_id=1, source_target_pairs={{0,3},{1,2},{2,1},{3,0},{4,7},{5,6},{6,5},{7,4},{8,11},{9,10},{10,... | collective-permute-start | bytes 393224 | tf_op jit(solution)/shard_map/ppermute | solution.py:381
  16.0 4.7 %collective-permute-start.4 = (bf16[256,128]{1,0:T(8,128)(2,1)S(1)}, bf16[256,128]{1,0:T(8,128)(2,1)S(1)}, u32[]{:S(2)}, u32[]{:S(2)}) collective-permute-start(bf16[256,128]{1,0:T(8,128)(2,1)S(1)} %add.5.mine_ref), channel_id=1, source_target_pairs={{0,9},{1,4},{2,7},{3,10},{4,1},{5,12},{6,15},{7,2},{8,13},{9,0},{1... | collective-permute-start | bytes 196616 | tf_op jit(solution)/shard_map/ppermute | solution.py:381
  20.9 1.7 %collective-permute-start.5 = (bf16[128,128]{1,0:T(8,128)(2,1)S(1)}, bf16[128,128]{1,0:T(8,128)(2,1)S(1)}, u32[]{:S(2)}, u32[]{:S(2)}) collective-permute-start(bf16[128,128]{1,0:T(8,128)(2,1)S(1)} %product_terms.1.mine_ref), channel_id=1, source_target_pairs={{0,1},{1,0},{2,3},{3,2},{4,5},{5,4},{6,7},{7,6},{8,9},{9,8},{10,11... | collective-permute-start | bytes 98312 | tf_op jit(solution)/shard_map/ppermute | solution.py:381
  22.7 4.3 %collective-permute-start.8 = (bf16[128,128]{1,0:T(8,128)(2,1)S(1)}, bf16[128,128]{1,0:T(8,128)(2,1)S(1)}, u32[]{:S(2)}, u32[]{:S(2)}) collective-permute-start(bf16[128,128]{1,0:T(8,128)(2,1)S(1)} %add.7.term_ref), channel_id=1, source_target_pairs={{0,7},{1,6},{2,5},{3,4},{4,3},{5,2},{6,1},{7,0},{8,15},{9,14},{10,... | collective-permute-start | bytes 98312 | tf_op jit(solution)/shard_map/ppermute | solution.py:381
  25.3 3.4 %collective-permute-start.7 = (bf16[128,128]{1,0:T(8,128)(2,1)S(1)}, bf16[128,128]{1,0:T(8,128)(2,1)S(1)}, u32[]{:S(2)}, u32[]{:S(2)}) collective-permute-start(bf16[128,128]{1,0:T(8,128)(2,1)S(1)} %add.7.term_ref), channel_id=1, source_target_pairs={{0,5},{1,2},{2,1},{3,6},{4,7},{5,0},{6,3},{7,4},{8,11},{9,12},{10,... | collective-permute-start | bytes 98312 | tf_op jit(solution)/shard_map/ppermute | solution.py:381
  26.1 3.3 %collective-permute-start.6 = (bf16[128,128]{1,0:T(8,128)(2,1)S(1)}, bf16[128,128]{1,0:T(8,128)(2,1)S(1)}, u32[]{:S(2)}, u32[]{:S(2)}) collective-permute-start(bf16[128,128]{1,0:T(8,128)(2,1)S(1)} %add.7.term_ref), channel_id=1, source_target_pairs={{0,3},{1,4},{2,7},{3,0},{4,1},{5,6},{6,5},{7,2},{8,13},{9,10},{10,... | collective-permute-start | bytes 98312 | tf_op jit(solution)/shard_map/ppermute | solution.py:381
  29.8 4.1 %collective-permute-start.9 = (f32[32,128]{1,0:T(8,128)S(1)}, f32[32,128]{1,0:T(8,128)S(1)}, u32[]{:S(2)}, u32[]{:S(2)}) collective-permute-start(f32[32,128]{1,0:T(8,128)S(1)} %local_gram.1.gram_ref), channel_id=1, source_target_pairs={{0,9},{1,8},{2,11},{3,10},{4,13},{5,12},{6,15},{7,14},{8,1},{9,0},... | collective-permute-start | bytes 49160 | tf_op jit(solution)/shard_map/ppermute | solution.py:381

commit v34 on v32

--- a/solution.py
+++ b/solution.py
@@ -104,16 +104,20 @@
 
     small = pltpu.make_async_copy(mode2_ref, small_ref, small_sem)
     small.start()
-    for chunk in range(chunks):
-        sends[chunk][0](chunk * STEP, STEP, 2 if chunk else 4)
+    sends[0][0](0, STEP, 8)
+    sends[1][0](STEP, STEP, 2)
     fill_order(order_ref, half)
     small.wait()
     wide_ref[...] = jnp.concatenate([small_ref[...]] * (LANES // rank), axis=0)
     for chunk in range(chunks):
         sends[chunk][1](chunk * STEP, STEP)
         if chunk == 0:
-            start_first(0, STEP, 4)
-            start_rest(STEP, cells - STEP, 2 * (chunks - 1))
+            for later in range(2, chunks):
+                sends[later][0](later * STEP, STEP, 2)
+            start_first(0, STEP, 2)
+            start_rest(STEP, STEP, 2)
+        if chunk == 1:
+            start_rest(2 * STEP, cells - 2 * STEP, chunks)
         multiply(slab_ref[pl.ds(chunk * STEP, STEP)], wide_ref, flat[chunk % 2])
         if chunk:
             spread(half, flat[(chunk - 1) % 2], order_ref, core_ref, (chunk - 1) * STEP)

time: 36.9 us -> 36.5 us (0.989)
  Pallas kernels: 10 us -> 9.52 us
    pallas_call x1, Pallas kernels: 5.74 us -> 5.26 us  [contract_send(): pl.pallas_call(send_kernel, in_specs=[pinned, pinned], out_shape=[jax.Sha...]
where the time goes in v34:
time: 36.5 us; the launch traced here: 36.3 us
  starting transfers between devices  14.8 us (41%)
  waiting for transfers between devices  11.9 us (33%)
  Pallas kernels  9.52 us (26%)
    ppermute x10, starting transfers between devices, swap(): return lax.ppermute(x, ('row', 'col'), pairs)  14.8 us
    ppermute x10, waiting for transfers between devices, swap(): return lax.ppermute(x, ('row', 'col'), pairs)  11.9 us
    pallas_call x1, Pallas kernels, contract_send(): pl.pallas_call(send_kernel, in_specs=[pinned, pinned], out_shape=[jax.Sha...  5.26 us
    pallas_call x1, Pallas kernels, finish(): pl.pallas_call(functools.partial(finish_kernel, total_rows), out_shape=ja...  1.92 us
    pallas_call x1, Pallas kernels, contract_own(): pl.pallas_call(own_kernel, out_shape=jax.ShapeDtypeStruct((cells, half //...  1.43 us
  transfers between devices with their start and end apart: 10, of which 8 were waited for; matrix products, arithmetic and copies ran while one was open for 0% of the time, Pallas kernels for 4%

profile of v34, /device:TPU:0, one launch (start us, length us, event | category | flops | bytes accessed | tf_op | source)
XLA Modules:
  0.0 36.3 jit_solution(10507180999054224291)
XLA Ops:
  0.0 0.0 copy-start
  0.0 5.3 %contract_send.1 = (bf16[128,1024]{1,0:T(8,128)(2,1)S(1)}, bf16[128,16,1024]{2,1,0:T(8,128)(2,1)S(1)}, bf16[32,1024]{1,0:T(8,128)(2,1)S(1)}, bf16[128,1024]{1,0:T(8,128)(2,1)S(1)}, bf16[64,256]{1,0:T(8,128)(2,1)S(1)}) custom-call(bf16[128,32,1024]{2,1,0:T(8,128)(2,1)} %snapshot_ref.1, bf16[64,1024]{1,0:T(8,128)(2,1)} %bitcast.4), custom_call_target="tpu_custom_call" | custom-call | tf_op jit(solution)/shard_map/contract_send/pallas_call | solution.py:138
  5.3 0.5 %collective-permute-start = (bf16[128,1024]{1,0:T(8,128)(2,1)S(1)}, bf16[128,1024]{1,0:T(8,128)(2,1)S(1)}, u32[]{:S(2)}, u32[]{:S(2)}) collective-permute-start(bf16[128,1024]{1,0:T(8,128)(2,1)S(1)} %get-tuple-element.18), channel_id=1, source_target_pairs={{0,1},{1,0},{2,3},{3,2},{4,5},{5,4},{6,7},{7,6},{8,9},{9,8},{10,11... | collective-permute-start | bytes 786440 | tf_op jit(solution)/shard_map/ppermute | solution.py:390
  5.8 1.4 %contract_own.1.own_ref = bf16[128,1024]{1,0:T(8,128)(2,1)S(1)} custom-call(bf16[128,16,1024]{2,1,0:T(8,128)(2,1)S(1)} %get-tuple-element.14.slab_ref, bf16[32,1024]{1,0:T(8,128)(2,1)S(1)} %get-tuple-element.15.part_ref, bf16[128,1024]{1,0:T(8,128)(2,1)S(1)} %get-tuple-element.16.wide_ref, bf16[64,256]{1,0:T(8,128)(2,1)S(1)} %get-tuple-element.17.order_ref), custom_call_target="tpu_custom_call" | custom-call | tf_op jit(solution)/shard_map/contract_own/pallas_call | solution.py:177
  7.2 0.0 collective-permute-done.got_ref
  7.2 0.0 copy-done
  7.2 0.2 project_sent.1
  7.4 2.7 %collective-permute-start.2 = (bf16[256,128]{1,0:T(8,128)(2,1)S(1)}, bf16[256,128]{1,0:T(8,128)(2,1)S(1)}, u32[]{:S(2)}, u32[]{:S(2)}) collective-permute-start(bf16[256,128]{1,0:T(8,128)(2,1)S(1)} %get-tuple-element.22), channel_id=1, source_target_pairs={{0,3},{1,2},{2,1},{3,0},{4,7},{5,6},{6,5},{7,4},{8,11},{9,10},{10,... | collective-permute-start | bytes 196616 | tf_op jit(solution)/shard_map/ppermute | solution.py:390
  10.1 0.2 project_kept.1
  10.3 2.2 %collective-permute-done.2.got_ref = bf16[256,128]{1,0:T(8,128)(2,1)S(1)} collective-permute-done((bf16[256,128]{1,0:T(8,128)(2,1)S(1)}, bf16[256,128]{1,0:T(8,128)(2,1)S(1)}, u32[]{:S(2)}, u32[]{:S(2)}) %collective-permute-start.2) | collective-permute-done | bytes 65568 | tf_op jit(solution)/shard_map/ppermute | solution.py:390
  12.5 1.5 %collective-permute-start.3 = (bf16[256,128]{1,0:T(8,128)(2,1)S(1)}, bf16[256,128]{1,0:T(8,128)(2,1)S(1)}, u32[]{:S(2)}, u32[]{:S(2)}) collective-permute-start(bf16[256,128]{1,0:T(8,128)(2,1)S(1)} %add.4.mine_ref), channel_id=1, source_target_pairs={{0,5},{1,8},{2,11},{3,6},{4,13},{5,0},{6,3},{7,14},{8,1},{9,12},{1... | collective-permute-start | bytes 196616 | tf_op jit(solution)/shard_map/ppermute | solution.py:390
  14.0 1.2 %collective-permute-start.1 = (bf16[128,512]{1,0:T(8,128)(2,1)S(1)}, bf16[128,512]{1,0:T(8,128)(2,1)S(1)}, u32[]{:S(2)}, u32[]{:S(2)}) collective-permute-start(bf16[128,512]{1,0:T(8,128)(2,1)S(1)} %get-tuple-element.20), channel_id=1, source_target_pairs={{0,3},{1,2},{2,1},{3,0},{4,7},{5,6},{6,5},{7,4},{8,11},{9,10},{10,... | collective-permute-start | bytes 393224 | tf_op jit(solution)/shard_map/ppermute | solution.py:390
  15.3 1.0 %collective-permute-done.3.got_ref = bf16[256,128]{1,0:T(8,128)(2,1)S(1)} collective-permute-done((bf16[256,128]{1,0:T(8,128)(2,1)S(1)}, bf16[256,128]{1,0:T(8,128)(2,1)S(1)}, u32[]{:S(2)}, u32[]{:S(2)}) %collective-permute-start.3) | collective-permute-done | bytes 65568 | tf_op jit(solution)/shard_map/ppermute | solution.py:390
  16.3 2.8 %collective-permute-start.4 = (bf16[256,128]{1,0:T(8,128)(2,1)S(1)}, bf16[256,128]{1,0:T(8,128)(2,1)S(1)}, u32[]{:S(2)}, u32[]{:S(2)}) collective-permute-start(bf16[256,128]{1,0:T(8,128)(2,1)S(1)} %add.5.mine_ref), channel_id=1, source_target_pairs={{0,9},{1,4},{2,7},{3,10},{4,1},{5,12},{6,15},{7,2},{8,13},{9,0},{1... | collective-permute-start | bytes 196616 | tf_op jit(solution)/shard_map/ppermute | solution.py:390
  19.1 0.0 collective-permute-done.1.refs_0_.got_ref
  19.1 1.9 %collective-permute-done.4.got_ref = bf16[256,128]{1,0:T(8,128)(2,1)S(1)} collective-permute-done((bf16[256,128]{1,0:T(8,128)(2,1)S(1)}, bf16[256,128]{1,0:T(8,128)(2,1)S(1)}, u32[]{:S(2)}, u32[]{:S(2)}) %collective-permute-start.4) | collective-permute-done | bytes 65568 | tf_op jit(solution)/shard_map/ppermute | solution.py:390
  21.1 0.2 product_terms.1.mine_ref
  21.3 0.8 %collective-permute-start.5 = (bf16[128,128]{1,0:T(8,128)(2,1)S(1)}, bf16[128,128]{1,0:T(8,128)(2,1)S(1)}, u32[]{:S(2)}, u32[]{:S(2)}) collective-permute-start(bf16[128,128]{1,0:T(8,128)(2,1)S(1)} %product_terms.1.mine_ref), channel_id=1, source_target_pairs={{0,1},{1,0},{2,3},{3,2},{4,5},{5,4},{6,7},{7,6},{8,9},{9,8},{10,11... | collective-permute-start | bytes 98312 | tf_op jit(solution)/shard_map/ppermute | solution.py:390
  22.1 0.9 %collective-permute-done.5.got_ref = bf16[128,128]{1,0:T(8,128)(2,1)S(1)} collective-permute-done((bf16[128,128]{1,0:T(8,128)(2,1)S(1)}, bf16[128,128]{1,0:T(8,128)(2,1)S(1)}, u32[]{:S(2)}, u32[]{:S(2)}) %collective-permute-start.5) | collective-permute-done | bytes 32800 | tf_op jit(solution)/shard_map/ppermute | solution.py:390
  23.0 2.7 %collective-permute-start.8 = (bf16[128,128]{1,0:T(8,128)(2,1)S(1)}, bf16[128,128]{1,0:T(8,128)(2,1)S(1)}, u32[]{:S(2)}, u32[]{:S(2)}) collective-permute-start(bf16[128,128]{1,0:T(8,128)(2,1)S(1)} %add.7.term_ref), channel_id=1, source_target_pairs={{0,7},{1,6},{2,5},{3,4},{4,3},{5,2},{6,1},{7,0},{8,15},{9,14},{10,... | collective-permute-start | bytes 98312 | tf_op jit(solution)/shard_map/ppermute | solution.py:390
  25.6 0.9 %collective-permute-start.7 = (bf16[128,128]{1,0:T(8,128)(2,1)S(1)}, bf16[128,128]{1,0:T(8,128)(2,1)S(1)}, u32[]{:S(2)}, u32[]{:S(2)}) collective-permute-start(bf16[128,128]{1,0:T(8,128)(2,1)S(1)} %add.7.term_ref), channel_id=1, source_target_pairs={{0,5},{1,2},{2,1},{3,6},{4,7},{5,0},{6,3},{7,4},{8,11},{9,12},{10,... | collective-permute-start | bytes 98312 | tf_op jit(solution)/shard_map/ppermute | solution.py:390
  26.6 0.0 collective-permute-start.6
  26.6 0.7 %collective-permute-done.8.last_ref = bf16[128,128]{1,0:T(8,128)(2,1)S(1)} collective-permute-done((bf16[128,128]{1,0:T(8,128)(2,1)S(1)}, bf16[128,128]{1,0:T(8,128)(2,1)S(1)}, u32[]{:S(2)}, u32[]{:S(2)}) %collective-permute-start.8) | collective-permute-done | bytes 32800 | tf_op jit(solution)/shard_map/ppermute | solution.py:390
  27.3 1.8 %collective-permute-done.7.second_ref = bf16[128,128]{1,0:T(8,128)(2,1)S(1)} collective-permute-done((bf16[128,128]{1,0:T(8,128)(2,1)S(1)}, bf16[128,128]{1,0:T(8,128)(2,1)S(1)}, u32[]{:S(2)}, u32[]{:S(2)}) %collective-permute-start.7) | collective-permute-done | bytes 32800 | tf_op jit(solution)/shard_map/ppermute | solution.py:390
  29.0 0.9 %collective-permute-done.6.first_ref = bf16[128,128]{1,0:T(8,128)(2,1)S(1)} collective-permute-done((bf16[128,128]{1,0:T(8,128)(2,1)S(1)}, bf16[128,128]{1,0:T(8,128)(2,1)S(1)}, u32[]{:S(2)}, u32[]{:S(2)}) %collective-permute-start.6) | collective-permute-done | bytes 32800 | tf_op jit(solution)/shard_map/ppermute | solution.py:390
  29.9 0.3 local_gram.1.gram_ref
  30.2 1.6 %collective-permute-start.9 = (f32[32,128]{1,0:T(8,128)S(1)}, f32[32,128]{1,0:T(8,128)S(1)}, u32[]{:S(2)}, u32[]{:S(2)}) collective-permute-start(f32[32,128]{1,0:T(8,128)S(1)} %local_gram.1.gram_ref), channel_id=1, source_target_pairs={{0,9},{1,8},{2,11},{3,10},{4,13},{5,12},{6,15},{7,14},{8,1},{9,0},... | collective-permute-start | bytes 49160 | tf_op jit(solution)/shard_map/ppermute | solution.py:390
  31.8 2.6 %collective-permute-done.9.got_gram_ref = f32[32,128]{1,0:T(8,128)S(1)} collective-permute-done((f32[32,128]{1,0:T(8,128)S(1)}, f32[32,128]{1,0:T(8,128)S(1)}, u32[]{:S(2)}, u32[]{:S(2)}) %collective-permute-start.9) | collective-permute-done | bytes 16416 | tf_op jit(solution)/shard_map/ppermute | solution.py:390
  34.4 1.9 %finish.1 = f32[64,64]{1,0:T(8,128)} custom-call(bf16[128,128]{1,0:T(8,128)(2,1)S(1)} %add.7.term_ref, bf16[128,128]{1,0:T(8,128)(2,1)S(1)} %collective-permute-done.6.first_ref, bf16[128,128]{1,0:T(8,128)(2,1)S(1)} %collective-permute-done.7.second_ref, f32[32,128]{1,0:T(8,128)S(1)} %local_gram.1.gram_ref, f32[32,128]{1,0:T(8,128)S(1)} %collective-permute-done.9.got_gram_ref), custom_call_target="tpu_custom_call" | custom-call | tf_op jit(solution)/shard_map/finish/pallas_call | solution.py:369
  (4 shorter events, 0.1 us)
Async XLA Ops:
  0.0 7.2 %copy-start = (bf16[128,64]{0,1:T(8,128)(2,1)S(1)}, bf16[128,64]{0,1:T(8,128)(2,1)}, u32[]{:S(2)}) copy-start(bf16[128,64]{0,1:T(8,128)(2,1)} %param.5) | copy-start | bytes 49156
  5.3 2.0 %collective-permute-start = (bf16[128,1024]{1,0:T(8,128)(2,1)S(1)}, bf16[128,1024]{1,0:T(8,128)(2,1)S(1)}, u32[]{:S(2)}, u32[]{:S(2)}) collective-permute-start(bf16[128,1024]{1,0:T(8,128)(2,1)S(1)} %get-tuple-element.18), channel_id=1, source_target_pairs={{0,1},{1,0},{2,3},{3,2},{4,5},{5,4},{6,7},{7,6},{8,9},{9,8},{10,11... | collective-permute-start | bytes 786440 | tf_op jit(solution)/shard_map/ppermute | solution.py:390
  7.4 5.1 %collective-permute-start.2 = (bf16[256,128]{1,0:T(8,128)(2,1)S(1)}, bf16[256,128]{1,0:T(8,128)(2,1)S(1)}, u32[]{:S(2)}, u32[]{:S(2)}) collective-permute-start(bf16[256,128]{1,0:T(8,128)(2,1)S(1)} %get-tuple-element.22), channel_id=1, source_target_pairs={{0,3},{1,2},{2,1},{3,0},{4,7},{5,6},{6,5},{7,4},{8,11},{9,10},{10,... | collective-permute-start | bytes 196616 | tf_op jit(solution)/shard_map/ppermute | solution.py:390
  12.5 3.8 %collective-permute-start.3 = (bf16[256,128]{1,0:T(8,128)(2,1)S(1)}, bf16[256,128]{1,0:T(8,128)(2,1)S(1)}, u32[]{:S(2)}, u32[]{:S(2)}) collective-permute-start(bf16[256,128]{1,0:T(8,128)(2,1)S(1)} %add.4.mine_ref), channel_id=1, source_target_pairs={{0,5},{1,8},{2,11},{3,6},{4,13},{5,0},{6,3},{7,14},{8,1},{9,12},{1... | collective-permute-start | bytes 196616 | tf_op jit(solution)/shard_map/ppermute | solution.py:390
  14.0 5.1 %collective-permute-start.1 = (bf16[128,512]{1,0:T(8,128)(2,1)S(1)}, bf16[128,512]{1,0:T(8,128)(2,1)S(1)}, u32[]{:S(2)}, u32[]{:S(2)}) collective-permute-start(bf16[128,512]{1,0:T(8,128)(2,1)S(1)} %get-tuple-element.20), channel_id=1, source_target_pairs={{0,3},{1,2},{2,1},{3,0},{4,7},{5,6},{6,5},{7,4},{8,11},{9,10},{10,... | collective-permute-start | bytes 393224 | tf_op jit(solution)/shard_map/ppermute | solution.py:390
  16.3 4.8 %collective-permute-start.4 = (bf16[256,128]{1,0:T(8,128)(2,1)S(1)}, bf16[256,128]{1,0:T(8,128)(2,1)S(1)}, u32[]{:S(2)}, u32[]{:S(2)}) collective-permute-start(bf16[256,128]{1,0:T(8,128)(2,1)S(1)} %add.5.mine_ref), channel_id=1, source_target_pairs={{0,9},{1,4},{2,7},{3,10},{4,1},{5,12},{6,15},{7,2},{8,13},{9,0},{1... | collective-permute-start | bytes 196616 | tf_op jit(solution)/shard_map/ppermute | solution.py:390
  21.3 1.6 %collective-permute-start.5 = (bf16[128,128]{1,0:T(8,128)(2,1)S(1)}, bf16[128,128]{1,0:T(8,128)(2,1)S(1)}, u32[]{:S(2)}, u32[]{:S(2)}) collective-permute-start(bf16[128,128]{1,0:T(8,128)(2,1)S(1)} %product_terms.1.mine_ref), channel_id=1, source_target_pairs={{0,1},{1,0},{2,3},{3,2},{4,5},{5,4},{6,7},{7,6},{8,9},{9,8},{10,11... | collective-permute-start | bytes 98312 | tf_op jit(solution)/shard_map/ppermute | solution.py:390
  23.0 4.3 %collective-permute-start.8 = (bf16[128,128]{1,0:T(8,128)(2,1)S(1)}, bf16[128,128]{1,0:T(8,128)(2,1)S(1)}, u32[]{:S(2)}, u32[]{:S(2)}) collective-permute-start(bf16[128,128]{1,0:T(8,128)(2,1)S(1)} %add.7.term_ref), channel_id=1, source_target_pairs={{0,7},{1,6},{2,5},{3,4},{4,3},{5,2},{6,1},{7,0},{8,15},{9,14},{10,... | collective-permute-start | bytes 98312 | tf_op jit(solution)/shard_map/ppermute | solution.py:390
  25.6 3.4 %collective-permute-start.7 = (bf16[128,128]{1,0:T(8,128)(2,1)S(1)}, bf16[128,128]{1,0:T(8,128)(2,1)S(1)}, u32[]{:S(2)}, u32[]{:S(2)}) collective-permute-start(bf16[128,128]{1,0:T(8,128)(2,1)S(1)} %add.7.term_ref), channel_id=1, source_target_pairs={{0,5},{1,2},{2,1},{3,6},{4,7},{5,0},{6,3},{7,4},{8,11},{9,12},{10,... | collective-permute-start | bytes 98312 | tf_op jit(solution)/shard_map/ppermute | solution.py:390
  26.6 3.3 %collective-permute-start.6 = (bf16[128,128]{1,0:T(8,128)(2,1)S(1)}, bf16[128,128]{1,0:T(8,128)(2,1)S(1)}, u32[]{:S(2)}, u32[]{:S(2)}) collective-permute-start(bf16[128,128]{1,0:T(8,128)(2,1)S(1)} %add.7.term_ref), channel_id=1, source_target_pairs={{0,3},{1,4},{2,7},{3,0},{4,1},{5,6},{6,5},{7,2},{8,13},{9,10},{10,... | collective-permute-start | bytes 98312 | tf_op jit(solution)/shard_map/ppermute | solution.py:390
  30.2 4.2 %collective-permute-start.9 = (f32[32,128]{1,0:T(8,128)S(1)}, f32[32,128]{1,0:T(8,128)S(1)}, u32[]{:S(2)}, u32[]{:S(2)}) collective-permute-start(f32[32,128]{1,0:T(8,128)S(1)} %local_gram.1.gram_ref), channel_id=1, source_target_pairs={{0,9},{1,8},{2,11},{3,10},{4,13},{5,12},{6,15},{7,14},{8,1},{9,0},... | collective-permute-start | bytes 49160 | tf_op jit(solution)/shard_map/ppermute | solution.py:390
